TPU v7x, 32 devices: a whole 2x2x4 slice. The times are simulated.
32 devices in a mesh: seq: 8 (over z, y), dp: 4 (over x, core).
Axes of the slice: x: 2, y: 2, z: 4, core: 2. Of those that a mesh axis runs over, the one named last changes fastest.
Arguments:
- queries: bfloat16 [4, 1024, 2048], P('dp', 'seq'), may hold values from -48 to 48
- keys: bfloat16 [4, 1024, 2048], P('dp', 'seq'), may hold values from -8 to 8
- values: bfloat16 [4, 1024, 2048], P('dp', 'seq'), may hold values from -6 to 6
- shifts: float32 [4, 2048], P('dp'), may hold values from -1.2 to 1.2
- scales: float32 [4, 2048], P('dp'), may hold values from -0.9 to 0.9
- proj_out: bfloat16 [2048, 64], replicated, may hold values from -0.125 to 0.125
- patch_embed: bfloat16 [16, 64, 1280], P(None, 'seq'), may hold values from -0.1875 to 0.1875
- pos_embed: bfloat16 [64, 1280], replicated, may hold values from -1.796875 to 1.796875
- pre_gain: float32 [1280], replicated, may hold values from 0.25 to 1.75
- post_gain: float32 [1280], replicated, may hold values from 0.25 to 1.75
- prompt: float32 [4, 1280], P('dp'), may hold values from -6 to 6
- cotangent: float32 [4], P('dp'), may hold values from 2 to 20
Outputs:
- rewards: float32 [4], P('dp')
- attn_grad: bfloat16 [4, 16, 1024, 128], P('dp', 'seq')
- proj_grad: float32 [2048, 64], replicated
All inputs are finite; a program needn't handle non-finite values.
Results may differ from a plain program's by a relative error of at most 0.0065.
Values may be sent and summed in bfloat16 or wider, within the bound.
No kernel may reach another device: no remote copies, remote signals or barrier semaphores. Data moves between devices by JAX's collectives and lax.ppermute only.
A program may use at most 64 MiB of HBM per device.

v0:
```python
import math

import jax
import jax.numpy as jnp
from jax import lax
from jax.sharding import PartitionSpec as P

HEADS = 16
HD = 128
CH = 64
GW = 64
VW = 1280


epsilon = 1e-05


def layer_norm(features):
    center = features - jnp.mean(features, axis=-1, keepdims=True)
    variance = jnp.mean(center * center, axis=-1, keepdims=True)
    return center * lax.rsqrt(variance + epsilon)


def pooled_reward(pooled, post_gain, prompt):
    final = layer_norm(pooled) * post_gain
    cosine = jnp.sum(final * prompt) / (
        jnp.sqrt(jnp.sum(final * final)) * jnp.sqrt(jnp.sum(prompt * prompt))
    )
    return 100.0 * cosine


def send_copies(query_send, key_groups, value_groups, query_parts):
    key_send = jnp.repeat(key_groups, query_parts, axis=0)
    value_send = jnp.repeat(value_groups, query_parts, axis=0)
    query_in, key_in, value_in = (
        lax.all_to_all(query_send, "seq", split_axis=0, concat_axis=1, tiled=True),
        lax.all_to_all(key_send, "seq", split_axis=0, concat_axis=1, tiled=True),
        lax.all_to_all(value_send, "seq", split_axis=0, concat_axis=1, tiled=True),
    )
    return (query_in[0], key_in[0], value_in[0])


def on_device(
    queries,
    keys,
    values,
    shifts,
    scales,
    proj_out,
    patch_embed,
    pos_embed,
    pre_gain,
    post_gain,
    prompt,
    cotangent,
):
    seq_count = lax.axis_size("seq")
    data_count = lax.axis_size("dp")
    tok_rows = queries.shape[1]
    query_parts = max(1, seq_count // HEADS)
    head_count = max(1, HEADS // seq_count)
    group_count = HEADS // head_count
    head_width = head_count * HD
    seq_index = lax.axis_index("seq")
    head_group = seq_index // query_parts
    query_part = seq_index % query_parts
    part_rows = tok_rows // query_parts
    lat_rows = seq_count * tok_rows
    grid_rows = lat_rows // GW
    query_send = queries[0].reshape(query_parts, part_rows, group_count, head_width)
    query_send = query_send.transpose(2, 0, 1, 3).reshape(seq_count, part_rows, head_width)
    key_groups = keys[0].reshape(tok_rows, group_count, head_width).transpose(1, 0, 2)
    value_groups = values[0].reshape(tok_rows, group_count, head_width).transpose(1, 0, 2)
    query_mine, key_all, value_all = send_copies(query_send, key_groups, value_groups, query_parts)
    query_rows = query_mine.shape[0]
    block_rows = math.gcd(query_rows, 512)
    key_heads = key_all.reshape(lat_rows, head_count, HD)
    value_heads = value_all.reshape(lat_rows, head_count, HD)

    def block_attend(query_block):
        logits = jnp.einsum(
            "qhd,khd->hqk", query_block, key_heads, preferred_element_type=jnp.float32
        ) * HD ** (-0.5)
        row_max = jnp.max(logits, axis=-1, keepdims=True)
        weights = jnp.exp(logits - row_max)
        totals = jnp.sum(weights, axis=-1, keepdims=True)
        mixed = jnp.einsum(
            "hqk,khd->qhd",
            weights.astype(jnp.bfloat16),
            value_heads,
            preferred_element_type=jnp.float32,
        )
        return mixed / jnp.transpose(totals, (1, 0, 2))

    query_blocks = query_mine.reshape(query_rows // block_rows, block_rows, head_count, HD)
    attended = lax.map(block_attend, query_blocks).reshape(query_rows, head_width)
    scale_mine = lax.dynamic_slice_in_dim(scales[0], head_group * head_width, head_width, 0)
    shift_mine = lax.dynamic_slice_in_dim(shifts[0], head_group * head_width, head_width, 0)
    modulated = (attended * (1.0 + scale_mine) + shift_mine).astype(jnp.bfloat16)
    proj_mine = lax.dynamic_slice_in_dim(proj_out, head_group * head_width, head_width, 0)
    latent_part = jnp.dot(modulated, proj_mine, preferred_element_type=jnp.float32)
    picker = (jnp.arange(query_parts) == query_part).astype(jnp.float32)
    spread_rows = latent_part.reshape(seq_count, 1, part_rows, CH) * picker[None, :, None, None]
    patch_major = spread_rows.reshape(grid_rows // 4, 4, GW // 4, 4, CH).transpose(0, 2, 1, 3, 4)
    patch_major = patch_major.reshape(lat_rows // 16, 16 * CH)
    patch_total = lat_rows // 16
    patch_local = patch_total // seq_count
    patch_mine = lax.psum_scatter(
        patch_major.astype(jnp.bfloat16), "seq", scatter_dimension=0, tiled=True
    )
    embed_full = lax.all_gather(patch_embed, "seq", axis=1, tiled=True).reshape(16 * CH, VW)
    pos_mine = lax.dynamic_slice_in_dim(pos_embed, seq_index * patch_local, patch_local, 0).astype(
        jnp.float32
    )
    embedded_mine = jnp.dot(patch_mine, embed_full, preferred_element_type=jnp.float32) + pos_mine

    def norm_fn(embed_in):
        return layer_norm(embed_in) * pre_gain

    normed, norm_pull = jax.vjp(norm_fn, embedded_mine)
    pooled = lax.psum(jnp.sum(normed, axis=0), "seq") * (1.0 / patch_total)

    def head_fn(pooled_in):
        return pooled_reward(pooled_in, post_gain, prompt[0])

    reward, head_pull = jax.vjp(head_fn, pooled)
    pooled_grad = head_pull(cotangent[0])[0] * (1.0 / patch_total)
    embed_grad = norm_pull(jnp.broadcast_to(pooled_grad, normed.shape))[0]
    patch_grad = jnp.dot(
        embed_grad, embed_full.astype(jnp.float32).T, precision=lax.Precision.HIGHEST
    )
    patch_grad = patch_grad.astype(jnp.bfloat16)
    grad_all = lax.all_gather(patch_grad, "seq", axis=0, tiled=True)
    token_grad = grad_all.reshape(grid_rows // 4, GW // 4, 4, 4, CH).transpose(0, 2, 1, 3, 4)
    token_grad = token_grad.reshape(seq_count, query_parts, part_rows, CH)
    selected = lax.dynamic_index_in_dim(token_grad, query_part, 1, keepdims=False).reshape(
        query_rows, CH
    )
    modulated_grad = jnp.dot(selected, proj_mine.T, preferred_element_type=jnp.float32)
    weight_grad = jnp.dot(modulated.T, selected, preferred_element_type=jnp.float32)
    attn_grad = (modulated_grad * (1.0 + scale_mine)).astype(jnp.bfloat16)
    attn_grad = attn_grad.reshape(query_rows, head_count, HD).transpose(1, 0, 2)[None]
    weight_full = jnp.zeros((HEADS * HD, CH), jnp.float32)
    weight_full = lax.dynamic_update_slice_in_dim(
        weight_full, weight_grad, head_group * head_width, 0
    )
    proj_grad = lax.psum(weight_full, ("seq", "dp")) * (1.0 / math.sqrt(data_count * lat_rows))
    return (reward[None], attn_grad, proj_grad)


def solution(mesh):
    return jax.shard_map(
        on_device,
        mesh=mesh,
        in_specs=(
            P("dp", "seq", None),
            P("dp", "seq", None),
            P("dp", "seq", None),
            P("dp", None),
            P("dp", None),
            P(),
            P(None, "seq", None),
            P(),
            P(),
            P(),
            P("dp", None),
            P("dp"),
        ),
        out_specs=(P("dp"), P("dp", "seq", None, None), P()),
        check_vma=False,
    )
```

profile of v0, /device:TPU:0, one launch (start us, length us, event | category | flops | bytes accessed | tf_op | source)
XLA Modules:
  0.0 394.5 jit_solution(497045108283261852)
XLA Ops:
  7.2 2.1 copy.29
  9.3 7.3 %all-to-all-start.1 = ((bf16[8,128,256]{1,2,0:T(8,128)(2,1)}), bf16[8,128,256]{1,2,0:T(8,128)(2,1)S(1)}, u32[]{:S(2)}, u32[]{:S(2)}) async-start(bf16[8,128,256]{1,2,0:T(8,128)(2,1)} %bitcast.9), calls=%async_computation.1 | async-start | bytes 1048576 | tf_op jit(solution)/shard_map/all_to_all | solution.py:37
  16.6 2.0 copy.31
  18.6 12.4 %all-to-all-done.1 = bf16[8,128,256]{1,2,0:T(8,128)(2,1)S(1)} async-done(((bf16[8,128,256]{1,2,0:T(8,128)(2,1)}), bf16[8,128,256]{1,2,0:T(8,128)(2,1)S(1)}, u32[]{:S(2)}, u32[]{:S(2)}) %all-to-all-start.1) | async-done | bytes 524320 | tf_op jit(solution)/shard_map/all_to_all | solution.py:37
  31.1 3.6 all-to-all-start.2
  35.5 13.8 %all-to-all-done.2 = bf16[8,128,256]{1,2,0:T(8,128)(2,1)S(1)} async-done(((bf16[8,128,256]{1,2,0:T(8,128)(2,1)}), bf16[8,128,256]{1,2,0:T(8,128)(2,1)S(1)}, u32[]{:S(2)}, u32[]{:S(2)}) %all-to-all-start.2) | async-done | bytes 524320 | tf_op jit(solution)/shard_map/all_to_all | solution.py:38
  49.4 3.6 all-to-all-start
  54.1 1.0 reshape_squeeze.21
  55.1 1.3 copy.34
  57.3 10.4 %all-to-all-done = bf16[8,128,256]{2,1,0:T(8,128)(2,1)S(1)} async-done(((bf16[8,128,256]{2,1,0:T(8,128)(2,1)}), bf16[8,128,256]{2,1,0:T(8,128)(2,1)S(1)}, u32[]{:S(2)}, u32[]{:S(2)}) %all-to-all-start) | async-done | bytes 524320 | tf_op jit(solution)/shard_map/all_to_all | solution.py:36
  67.8 6.1 %while.10 = (s32[]{:T(128)}, f32[2,512,2,128]{3,1,2,0:T(8,128)S(1)}, bf16[2,512,2,128]{3,2,1,0:T(2,128)(2,1)S(1)}, bf16[1024,2,128]{2,0,1:T(8,128)(2,1)S(1)}, bf16[1024,2,128]{2,0,1:T(8,128)(2,1)S(1)}, /*index=5*/s32[]{:T(128)}) while((s32[]{:T(128)}, f32[2,512,2,128]{3,1,2,0:T(8,128)S(1)}, bf16[2,512,2,128]{3,2,1,0:T(2,128)(2,1)S(1)}, ...), condition=%wide.region_3.4_spmd, body=%wide.region_0.3_spmd.sunk | while | flops 545388544 | bytes 14962773 | solution.py:96
  68.8 0.9 fusion.57
  69.8 1.1 fusion.58
  72.8 1.1 fusion.58
  74.7 1.0 reshape.122
  79.6 57.9 %reduce-scatter.2.cloned.1.call-done = bf16[8,1024]{1,0:T(8,128)(2,1)} async-done(((bf16[64,1024]{1,0:T(8,128)(2,1)}), bf16[8,1024]{1,0:T(8,128)(2,1)}) %reduce-scatter.2.cloned.1.call-update) | async-done | bytes 16400 | tf_op jit(solution)/shard_map/reduce_scatter | solution.py:108
  137.5 56.3 %all-gather.2.cloned.1.call-done = bf16[16,64,1280]{2,1,0:T(8,128)(2,1)} async-done(((bf16[16,8,1280]{2,1,0:T(8,128)(2,1)}), bf16[16,64,1280]{2,1,0:T(8,128)(2,1)}) %all-gather.2.cloned.1.call-update) | async-done | bytes 2621456 | tf_op jit(solution)/shard_map/all_gather | solution.py:111
  193.7 2.3 fusion.41
  196.3 19.2 %psum.14 = f32[1280]{0:T(1024)S(1)} all-reduce(f32[1280]{0:T(1024)S(1)} %multiply_reduce_fusion.2), channel_id=1, replica_groups=mesh['seq'=8,'dp'=4] {'seq'}, use_global_device_ids=true, to_apply=%region_8.9 | all-reduce | flops 1280 | bytes 10240 | tf_op jit(solution)/shard_map/psum | solution.py:121
  223.8 3.9 convolution_convert_fusion.1
  227.7 30.6 %all_gather.7 = bf16[64,1024]{1,0:T(8,128)(2,1)S(1)} all-gather(bf16[8,1024]{1,0:T(8,128)(2,1)S(1)} %convolution_convert_fusion.1), channel_id=1, replica_groups=mesh['seq'=8,'dp'=4] {'seq'}, dimensions={0}, use_global_device_ids=true | all-gather | bytes 147456 | tf_op jit(solution)/shard_map/all_gather | solution.py:133
  260.7 1.0 copy.40
  261.7 123.2 %all-reduce.2.cloned.1.call-done = f32[2048,64]{0,1:T(8,128)} async-done(((f32[2048,64]{0,1:T(8,128)}), f32[2048,64]{0,1:T(8,128)}) %all-reduce.2.cloned.1.call-update) | async-done | bytes 524304 | tf_op jit(solution)/shard_map/psum | solution.py:147
  385.0 1.9 broadcast_multiply_fusion
  (58 shorter events, 15.2 us)
Async XLA Ops:
  7.2 68.9 %copy-start = (bf16[2048,64]{0,1:T(8,128)(2,1)S(1)}, bf16[2048,64]{0,1:T(8,128)(2,1)}, u32[]{:S(2)}) copy-start(bf16[2048,64]{0,1:T(8,128)(2,1)} %param.19) | copy-start | bytes 786436
  7.2 27.5 %copy-start.2 = (bf16[1,128,2048]{2,1,0:T(8,128)(2,1)S(1)}, bf16[1,128,2048]{2,1,0:T(8,128)(2,1)}, u32[]{:S(2)}) copy-start(bf16[1,128,2048]{2,1,0:T(8,128)(2,1)} %param.14) | copy-start | bytes 1572868
  9.3 21.8 %all-to-all-start.1 = ((bf16[8,128,256]{1,2,0:T(8,128)(2,1)}), bf16[8,128,256]{1,2,0:T(8,128)(2,1)S(1)}, u32[]{:S(2)}, u32[]{:S(2)}) async-start(bf16[8,128,256]{1,2,0:T(8,128)(2,1)} %bitcast.9), calls=%async_computation.1 | async-start | bytes 1048576 | tf_op jit(solution)/shard_map/all_to_all | solution.py:37
  31.1 18.3 %all-to-all-start.2 = ((bf16[8,128,256]{1,2,0:T(8,128)(2,1)}), bf16[8,128,256]{1,2,0:T(8,128)(2,1)S(1)}, u32[]{:S(2)}, u32[]{:S(2)}) async-start(bf16[8,128,256]{1,2,0:T(8,128)(2,1)} %bitcast.11), calls=%async_computation.2 | async-start | bytes 1048576 | tf_op jit(solution)/shard_map/all_to_all | solution.py:38
  49.4 18.3 %all-to-all-start = ((bf16[8,128,256]{2,1,0:T(8,128)(2,1)}), bf16[8,128,256]{2,1,0:T(8,128)(2,1)S(1)}, u32[]{:S(2)}, u32[]{:S(2)}) async-start(bf16[8,128,256]{2,1,0:T(8,128)(2,1)} %bitcast.77), calls=%async_computation | async-start | bytes 1048576 | tf_op jit(solution)/shard_map/all_to_all | solution.py:36
  53.0 84.4 %reduce-scatter.2.cloned.1.call-start = ((), (), s32[]{:S(2)}) async-start(), calls=%async_computation.4 | async-start | bytes 147456 | tf_op jit(solution)/shard_map/reduce_scatter | solution.py:108
  73.9 4.9 %copy-start.5 = (f32[1,1280]{1,0:T(1,128)S(1)}, f32[1,1280]{1,0:T(1,128)}, u32[]{:S(2)}) copy-start(f32[1,1280]{1,0:T(1,128)} %param.24) | copy-start | bytes 15364
  76.1 120.1 %copy-start.4 = (f32[1280]{0:T(1024)S(1)}, f32[1280]{0:T(1024)}, u32[]{:S(2)}) copy-start(f32[1280]{0:T(1024)} %param.22) | copy-start | bytes 15364
  76.1 142.0 %copy-start.3 = (f32[1280]{0:T(1024)S(1)}, f32[1280]{0:T(1024)}, u32[]{:S(2)}) copy-start(f32[1280]{0:T(1024)} %param.23) | copy-start | bytes 15364
  77.4 116.3 %all-gather.2.cloned.1.call-start = ((), (), s32[]{:S(2)}) async-start(), calls=%async_computation.5 | async-start | bytes 2949120 | tf_op jit(solution)/shard_map/all_gather | solution.py:111
  78.2 306.8 %all-reduce.2.cloned.1.call-start = ((), (), s32[]{:S(2)}) async-start(), calls=%async_computation.6 | async-start | bytes 1048576 | tf_op jit(solution)/shard_map/psum | solution.py:147
  258.9 0.8 copy-start.1
Sparse Core Ops, SparseCore 0:
  77.5 59.8 reduce-scatter.1
  139.7 53.9 all-gather.1
  259.8 125.0 all-reduce.1
where the time goes:
time: 395 us; the launch traced here: 394 us
  waiting for transfers between devices  275 us (70%)
  blocking collectives  49.8 us (13%)
  between operations  21.2 us (5%)
  starting transfers between devices  14.7 us (4%)
  local copies, waits for them, and re-layouts  14.5 us (4%)
  matrix products  10.8 us (3%)
  other arithmetic  8.67 us (2%)
    psum x1, waiting for transfers between devices, on_device(): lax.psum(weight_full, ('seq', 'dp'))  123 us
    reduce_scatter x1, waiting for transfers between devices, on_device(): lax.psum_scatter(patch_major.astype(jnp.bfloat16), 'seq', scatter_dimensi...  57.9 us
    all_gather x1, waiting for transfers between devices, on_device(): lax.all_gather(patch_embed, 'seq', axis=1, tiled=True).reshape(16 * CH, VW)  56.3 us
    all_gather x1, blocking collectives, on_device(): grad_all = lax.all_gather(patch_grad, 'seq', axis=0, tiled=True)  30.6 us
    psum x1, blocking collectives, on_device(): pooled = lax.psum(jnp.sum(normed, axis=0), 'seq') * (1.0 / patch_total)  19.2 us
    all_to_all x1, waiting for transfers between devices, send_copies(): lax.all_to_all(value_send, 'seq', split_axis=0, concat_axis=1, tiled=True)  13.8 us
    all_to_all x1, waiting for transfers between devices, send_copies(): lax.all_to_all(key_send, 'seq', split_axis=0, concat_axis=1, tiled=True)  12.4 us
    all_to_all x1, waiting for transfers between devices, send_copies(): lax.all_to_all(query_send, 'seq', split_axis=0, concat_axis=1, tiled=True)  10.4 us
  transfers between devices with their start and end apart: 6, of which 6 were waited for; matrix products, arithmetic and copies ran while one was open for 2% of the time, Pallas kernels for 0%

commit v1 on v0

v1 whole, which is shorter than its diff:
```python
import functools
import math

import jax
import jax.numpy as jnp
from jax import lax
from jax.experimental import pallas as pl
from jax.experimental.pallas import tpu as pltpu
from jax.sharding import PartitionSpec as P

HEADS = 16
HD = 128
CH = 64
GW = 64
VW = 1280
EPS = 1e-05
BF16 = jnp.bfloat16
F32 = jnp.float32
VMEM_LIMIT = 48 * 1024 * 1024


def mm(a, b):
    return jnp.dot(a, b, preferred_element_type=F32)


def mm_nt(a, b):
    return lax.dot_general(a, b, (((1,), (1,)), ((), ())), preferred_element_type=F32)


def mm_tn(a, b):
    return lax.dot_general(a, b, (((0,), (0,)), ((), ())), preferred_element_type=F32)


def pack_kernel(seq_count, query_parts, part_rows, tok_rows, width, q_ref, k_ref, v_ref, out_ref, sems):
    copies = []
    for dest in range(seq_count):
        group, part = dest // query_parts, dest % query_parts
        cols = pl.ds(group * width, width)
        copies.append(
            pltpu.make_async_copy(
                q_ref.at[0, pl.ds(part * part_rows, part_rows), cols],
                out_ref.at[dest, pl.ds(0, part_rows)],
                sems.at[0, dest],
            )
        )
        copies.append(
            pltpu.make_async_copy(
                k_ref.at[0, :, cols], out_ref.at[dest, pl.ds(part_rows, tok_rows)], sems.at[1, dest]
            )
        )
        copies.append(
            pltpu.make_async_copy(
                v_ref.at[0, :, cols],
                out_ref.at[dest, pl.ds(part_rows + tok_rows, tok_rows)],
                sems.at[2, dest],
            )
        )
    for copy in copies:
        copy.start()
    for copy in copies:
        copy.wait()


def pack(queries, keys, values, seq_count, query_parts, part_rows, tok_rows, width):
    rows = part_rows + 2 * tok_rows
    return pl.pallas_call(
        functools.partial(pack_kernel, seq_count, query_parts, part_rows, tok_rows, width),
        out_shape=jax.ShapeDtypeStruct((seq_count, rows, width), BF16),
        in_specs=[pl.BlockSpec(memory_space=pl.ANY)] * 3,
        out_specs=pl.BlockSpec(memory_space=pl.ANY),
        scratch_shapes=[pltpu.SemaphoreType.DMA((3, seq_count))],
        cost_estimate=pl.CostEstimate(
            flops=0, bytes_accessed=4 * seq_count * rows * width, transcendentals=0
        ),
    )(queries, keys, values)


def attend_kernel(
    seq_count, part_rows, tok_rows, heads,
    in_ref, scale_ref, shift_ref, proj_ref, mod_ref, lat_ref, key_scr, value_scr,
):
    half = part_rows // 2
    width = heads * HD
    factor = HD ** (-0.5) * math.log2(math.e)
    for src in range(seq_count):
        key_scr[pl.ds(src * tok_rows, tok_rows), :] = in_ref[src, pl.ds(part_rows, tok_rows), :]
        value_scr[pl.ds(src * tok_rows, tok_rows), :] = in_ref[
            src, pl.ds(part_rows + tok_rows, tok_rows), :
        ]
    gain = 1.0 + scale_ref[...]
    shift = shift_ref[...]
    proj = proj_ref[...]
    zero = jnp.zeros_like(proj)
    proj_pair = jnp.concatenate(
        [jnp.concatenate([proj, zero], axis=1), jnp.concatenate([zero, proj], axis=1)], axis=0
    )

    def body(src, carry):
        mixed = []
        for head in range(heads):
            cols = pl.ds(head * HD, HD)
            query = in_ref[src, pl.ds(0, part_rows), cols]
            logits = mm_nt(query, key_scr[:, cols])
            top = jnp.max(logits, axis=-1, keepdims=True)
            weights = jnp.exp2((logits - top) * factor)
            total = jnp.sum(weights, axis=-1, keepdims=True)
            mixed.append(mm(weights.astype(BF16), value_scr[:, cols]) / total)
        attended = jnp.concatenate(mixed, axis=1) if heads > 1 else mixed[0]
        modulated = (attended * gain + shift).astype(BF16)
        mod_ref[src] = modulated
        pair = jnp.concatenate([modulated[:half], modulated[half:]], axis=1)
        lat_ref[src] = mm(pair, proj_pair).astype(BF16)
        return carry

    lax.fori_loop(0, seq_count, body, 0)


def attend(received, scale, shift, proj, seq_count, part_rows, tok_rows, heads):
    width = heads * HD
    lat_rows = seq_count * tok_rows
    query_rows = seq_count * part_rows
    vmem = pl.BlockSpec(memory_space=pltpu.VMEM)
    return pl.pallas_call(
        functools.partial(attend_kernel, seq_count, part_rows, tok_rows, heads),
        out_shape=(
            jax.ShapeDtypeStruct((seq_count, part_rows, width), BF16),
            jax.ShapeDtypeStruct((seq_count, part_rows // 2, 2 * CH), BF16),
        ),
        in_specs=[vmem] * 4,
        out_specs=(vmem, vmem),
        scratch_shapes=[pltpu.VMEM((lat_rows, width), BF16), pltpu.VMEM((lat_rows, width), BF16)],
        compiler_params=pltpu.CompilerParams(vmem_limit_bytes=VMEM_LIMIT),
        cost_estimate=pl.CostEstimate(
            flops=4 * query_rows * lat_rows * width,
            bytes_accessed=2 * (query_rows * 2 + lat_rows * 2) * width,
            transcendentals=query_rows * lat_rows * heads,
        ),
    )(received, scale, shift, proj)


def lane_mean(x, count):
    return jnp.sum(x, axis=-1, keepdims=True) * (1.0 / count)


def head_kernel(
    grid_rows, fused,
    lat_ref, embed_ref, pos_ref, pre_ref, post_ref, prompt_ref, cot_ref, mod_ref,
    reward_ref, grad_ref, weight_ref, lat_scr, grad_scr,
):
    patch_rows = grid_rows // 4
    patch_cols = GW // 4
    patches = patch_rows * patch_cols
    lat_scr[...] = lat_ref[...].astype(F32)

    def embed_block(hi, tx):
        first = 4 * (2 * hi) + tx
        second = 4 * (2 * hi + 1) + tx
        return jnp.concatenate(
            [embed_ref[pl.ds(first * CH, CH), :], embed_ref[pl.ds(second * CH, CH), :]], axis=0
        )

    embedded = pos_ref[...].astype(F32)
    for hi in range(2):
        for tx in range(4):
            rows = [
                lat_scr[pl.ds((2 * pr + hi) * GW + tx, patch_cols, stride=4), :]
                for pr in range(patch_rows)
            ]
            block = jnp.concatenate(rows, axis=0).astype(BF16)
            embedded = embedded + mm(block, embed_block(hi, tx))
    pre = pre_ref[...]
    post = post_ref[...]
    prompt = prompt_ref[...]
    center = embedded - lane_mean(embedded, VW)
    rstd = lax.rsqrt(lane_mean(center * center, VW) + EPS)
    unit = center * rstd
    pooled = jnp.sum(unit, axis=0, keepdims=True) * (1.0 / patches) * pre
    pooled_center = pooled - lane_mean(pooled, VW)
    pooled_rstd = lax.rsqrt(lane_mean(pooled_center * pooled_center, VW) + EPS)
    pooled_unit = pooled_center * pooled_rstd
    final = pooled_unit * post
    dot = jnp.sum(final * prompt, axis=-1, keepdims=True)
    final_sq = jnp.sum(final * final, axis=-1, keepdims=True)
    prompt_sq = jnp.sum(prompt * prompt, axis=-1, keepdims=True)
    final_len = jnp.sqrt(final_sq)
    prompt_len = jnp.sqrt(prompt_sq)
    cosine = dot / (final_len * prompt_len)
    reward_ref[...] = jnp.broadcast_to(100.0 * cosine, reward_ref.shape)
    cot = cot_ref[...]
    final_grad = (100.0 * cot) * (prompt / (final_len * prompt_len) - final * (cosine / final_sq))
    unit_grad = final_grad * post
    pooled_grad = pooled_rstd * (
        unit_grad
        - lane_mean(unit_grad, VW)
        - pooled_unit * lane_mean(unit_grad * pooled_unit, VW)
    )
    flow = pooled_grad * pre * (1.0 / patches)
    embed_grad = rstd * (flow - lane_mean(flow, VW) - unit * lane_mean(flow * unit, VW))
    high = embed_grad.astype(BF16)
    low = (embed_grad - high.astype(F32)).astype(BF16)
    stacked = jnp.concatenate([high, low], axis=0)
    for hi in range(2):
        for tx in range(4):
            both = mm_nt(stacked, embed_block(hi, tx))
            piece = both[:patches] + both[patches:]
            for pr in range(patch_rows):
                grad_scr[pl.ds((2 * pr + hi) * GW + tx, patch_cols, stride=4), :] = piece[
                    pr * patch_cols : (pr + 1) * patch_cols
                ]
    grad = grad_scr[...].astype(BF16)
    grad_ref[...] = grad
    if fused:
        weight_ref[...] = readout_grad(grad, mod_ref)
    else:
        weight_ref[...] = jnp.zeros_like(weight_ref)


def readout_grad(grad, mod_ref):
    count, rows, width = mod_ref.shape
    half = rows // 2
    first = mod_ref[:, :half, :].reshape(count * half, width)
    second = mod_ref[:, half:, :].reshape(count * half, width)
    return mm_tn(grad, first)[:CH] + mm_tn(grad, second)[CH:]


def reward_head(latent, embed, pos, pre, post, prompt, cot, modulated, grid_rows, fused):
    patches = grid_rows * GW // 16
    rows = grid_rows * GW // 2
    width = modulated.shape[2]
    vmem = pl.BlockSpec(memory_space=pltpu.VMEM)
    return pl.pallas_call(
        functools.partial(head_kernel, grid_rows, fused),
        out_shape=(
            jax.ShapeDtypeStruct((1, 128), F32),
            jax.ShapeDtypeStruct((rows, 2 * CH), BF16),
            jax.ShapeDtypeStruct((CH, width), F32),
        ),
        in_specs=[vmem] * 8,
        out_specs=(vmem, vmem, vmem),
        scratch_shapes=[pltpu.VMEM((rows, 2 * CH), F32), pltpu.VMEM((rows, 2 * CH), F32)],
        compiler_params=pltpu.CompilerParams(vmem_limit_bytes=VMEM_LIMIT),
        cost_estimate=pl.CostEstimate(
            flops=6 * patches * 16 * CH * VW,
            bytes_accessed=2 * 16 * CH * VW + 2 * patches * VW,
            transcendentals=0,
        ),
    )(latent, embed, pos, pre, post, prompt, cot, modulated)


def spread_kernel(count, half, heads, grad_ref, scale_ref, proj_ref, out_ref):
    gain = 1.0 + scale_ref[...]
    proj = proj_ref[...]
    zero = jnp.zeros_like(proj)
    sides = (jnp.concatenate([proj, zero], axis=1), jnp.concatenate([zero, proj], axis=1))
    for src in range(count):
        grad = grad_ref[pl.ds(src * half, half), :]
        for side in range(2):
            rows = (mm_nt(grad, sides[side]) * gain).astype(BF16)
            for head in range(heads):
                out_ref[0, head, pl.ds((2 * src + side) * half, half), :] = rows[
                    :, head * HD : (head + 1) * HD
                ]


def spread(grad, scale, proj, count, half, heads):
    vmem = pl.BlockSpec(memory_space=pltpu.VMEM)
    return pl.pallas_call(
        functools.partial(spread_kernel, count, half, heads),
        out_shape=jax.ShapeDtypeStruct((1, heads, 2 * count * half, HD), BF16),
        in_specs=[vmem] * 3,
        out_specs=vmem,
        compiler_params=pltpu.CompilerParams(vmem_limit_bytes=VMEM_LIMIT),
        cost_estimate=pl.CostEstimate(
            flops=8 * count * half * CH * heads * HD,
            bytes_accessed=4 * count * half * heads * HD,
            transcendentals=0,
        ),
    )(grad, scale, proj)


def weight_kernel(grad_ref, mod_ref, out_ref):
    out_ref[...] = readout_grad(grad_ref[...], mod_ref)


def weight_call(grad, modulated):
    vmem = pl.BlockSpec(memory_space=pltpu.VMEM)
    return pl.pallas_call(
        weight_kernel,
        out_shape=jax.ShapeDtypeStruct((CH, modulated.shape[2]), F32),
        in_specs=[vmem] * 2,
        out_specs=vmem,
        compiler_params=pltpu.CompilerParams(vmem_limit_bytes=VMEM_LIMIT),
    )(grad, modulated)


def swap(x, axis, bit):
    count = lax.axis_size(axis)
    return lax.ppermute(x, axis, [(i, i ^ bit) for i in range(count)])


def gather_doubling(x, axis):
    count = lax.axis_size(axis)
    index = lax.axis_index(axis)
    steps = count.bit_length() - 1
    x = x.reshape((1,) * steps + x.shape)
    for step in range(steps):
        bit = count >> (step + 1)
        other = swap(x, axis, bit)
        mine_first = (index & bit) == 0
        x = jnp.concatenate(
            [jnp.where(mine_first, x, other), jnp.where(mine_first, other, x)], axis=step
        )
    return x.reshape((count,) + x.shape[steps:])


def gather_direct(x, axis):
    count = lax.axis_size(axis)
    index = lax.axis_index(axis)
    parts = [x] + [swap(x, axis, k) for k in range(1, count)]
    stacked = jnp.stack(parts)
    order = jnp.arange(count) ^ index
    return stacked[order]


def sum_direct(x, axis):
    count = lax.axis_size(axis)
    parts = [x] + [swap(x, axis, k) for k in range(1, count)]
    parts = [part.astype(F32) for part in parts]
    while len(parts) > 1:
        parts = [parts[i] + parts[i + 1] for i in range(0, len(parts), 2)]
    return parts[0]


def gather_embed(patch_embed):
    seq_count = lax.axis_size("seq")
    data_count = lax.axis_size("dp")
    positions, local, width = patch_embed.shape
    share = positions // data_count if positions % data_count == 0 else 0
    if share:
        mine = lax.dynamic_slice_in_dim(patch_embed, lax.axis_index("dp") * share, share, 0)
    else:
        mine = patch_embed
    gathered = gather_doubling(mine, "seq")
    full = gathered.transpose(1, 0, 2, 3).reshape(mine.shape[0], seq_count * local, width)
    if share:
        full = gather_doubling(full, "dp")
    return full.reshape(positions * seq_count * local, width)


def on_device(
    queries,
    keys,
    values,
    shifts,
    scales,
    proj_out,
    patch_embed,
    pos_embed,
    pre_gain,
    post_gain,
    prompt,
    cotangent,
):
    seq_count = lax.axis_size("seq")
    data_count = lax.axis_size("dp")
    tok_rows = queries.shape[1]
    query_parts = max(1, seq_count // HEADS)
    head_count = max(1, HEADS // seq_count)
    group_count = HEADS // head_count
    width = head_count * HD
    seq_index = lax.axis_index("seq")
    head_group = seq_index // query_parts
    query_part = seq_index % query_parts
    part_rows = tok_rows // query_parts
    half = part_rows // 2
    lat_rows = seq_count * tok_rows
    grid_rows = lat_rows // GW
    canonical = part_rows == 2 * GW

    scale_mine = lax.dynamic_slice_in_dim(scales, head_group * width, width, 1)
    shift_mine = lax.dynamic_slice_in_dim(shifts, head_group * width, width, 1)
    proj_mine = lax.dynamic_slice_in_dim(proj_out, head_group * width, width, 0)

    send = pack(queries, keys, values, seq_count, query_parts, part_rows, tok_rows, width)
    received = lax.all_to_all(send, "seq", split_axis=0, concat_axis=0, tiled=True)
    embed_full = gather_embed(patch_embed)

    modulated, latent_part = attend(
        received, scale_mine, shift_mine, proj_mine, seq_count, part_rows, tok_rows, head_count
    )

    shares = latent_part.reshape(group_count, seq_count // group_count * half, 2 * CH)
    groups = [[g * query_parts + r for g in range(group_count)] for r in range(query_parts)]
    pieces = lax.all_to_all(
        shares, "seq", split_axis=0, concat_axis=0, tiled=True,
        axis_index_groups=groups if query_parts > 1 else None,
    )
    summed = jnp.sum(pieces.astype(F32), axis=0).astype(BF16)
    latent = gather_direct(summed, "seq")
    per_share = seq_count // group_count
    if canonical:
        latent = latent.reshape(lat_rows // 2, 2 * CH)
    else:
        latent = latent.reshape(group_count, query_parts, per_share, half, 2, CH)
        latent = latent.transpose(0, 2, 1, 4, 3, 5).reshape(grid_rows // 2, 2, GW, CH)
        latent = latent.transpose(0, 2, 1, 3).reshape(lat_rows // 2, 2 * CH)

    reward, grad, weight = reward_head(
        latent, embed_full, pos_embed, pre_gain[None], post_gain[None], prompt,
        cotangent[None], modulated, grid_rows, canonical,
    )
    if not canonical:
        tokens = grad.reshape(grid_rows // 2, GW, 2, CH).transpose(0, 2, 1, 3)
        tokens = tokens.reshape(seq_count, query_parts, 2, half, CH)
        tokens = lax.dynamic_index_in_dim(tokens, query_part, 1, keepdims=False)
        grad = tokens.transpose(0, 2, 1, 3).reshape(seq_count * half, 2 * CH)
        weight = weight_call(grad, modulated)

    weight = weight * (1.0 / math.sqrt(data_count * lat_rows))
    total = sum_direct(weight.astype(BF16), "dp")
    attn_grad = spread(grad, scale_mine, proj_mine, seq_count, half, head_count)
    for part in range(1, query_parts):
        total = total + swap(total, "seq", part)
    weight_all = gather_direct(total.astype(BF16), "seq")
    weight_all = weight_all.reshape(group_count, query_parts, CH, width)[:, 0]
    proj_grad = weight_all.transpose(0, 2, 1).reshape(HEADS * HD, CH).astype(F32)
    return (reward[0, :1], attn_grad, proj_grad)


def solution(mesh):
    return jax.shard_map(
        on_device,
        mesh=mesh,
        in_specs=(
            P("dp", "seq", None),
            P("dp", "seq", None),
            P("dp", "seq", None),
            P("dp", None),
            P("dp", None),
            P(),
            P(None, "seq", None),
            P(),
            P(),
            P(),
            P("dp", None),
            P("dp"),
        ),
        out_specs=(P("dp"), P("dp", "seq", None, None), P()),
        check_vma=False,
    )
```

time: 395 us -> 185 us (0.47)
  waiting for transfers between devices: 275 us -> 54.7 us
  Pallas kernels: 0 us -> 61.7 us
  blocking collectives: 49.8 us -> 0 us
  starting transfers between devices: 14.7 us -> 43.2 us
  between operations: 21.2 us -> 1.55 us
  matrix products: 10.8 us -> 0 us
    psum x1 -> x0, waiting for transfers between devices: 123 us -> none  [on_device(): lax.psum(weight_full, ('seq', 'dp'))]
    pallas_call x0 -> x4, Pallas kernels: none -> 61.7 us  [the longest x1 49 us: pack(): pl.pallas_call(functools.partial(pack_kernel, seq_count, query_parts, par...]
    reduce_scatter x1 -> x0, waiting for transfers between devices: 57.9 us -> none  [on_device(): lax.psum_scatter(patch_major.astype(jnp.bfloat16), 'seq', scatter_dimensi...]
    all_gather x1 -> x0, waiting for transfers between devices: 56.3 us -> none  [on_device(): lax.all_gather(patch_embed, 'seq', axis=1, tiled=True).reshape(16 * CH, VW)]
    ppermute x0 -> x22, starting transfers between devices: none -> 32.3 us  [swap(): return lax.ppermute(x, axis, [(i, i ^ bit) for i in range(count)])]
    all_gather x1 -> x0, blocking collectives: 30.6 us -> none  [on_device(): grad_all = lax.all_gather(patch_grad, 'seq', axis=0, tiled=True)]
    ppermute x0 -> x22, waiting for transfers between devices: none -> 23.7 us  [swap(): return lax.ppermute(x, axis, [(i, i ^ bit) for i in range(count)])]
    psum x1 -> x0, blocking collectives: 19.2 us -> none  [on_device(): pooled = lax.psum(jnp.sum(normed, axis=0), 'seq') * (1.0 / patch_total)]
  transfers between devices with their start and end apart: 6 -> 24, of which waited for: 6 -> 10; matrix products, arithmetic and copies ran while one was open for 2% -> 8% of each run, Pallas kernels for 0% -> 27%
where the time goes in v1:
time: 185 us
  Pallas kernels  61.7 us (33%)
  waiting for transfers between devices  54.7 us (30%)
  starting transfers between devices  43.2 us (23%)
  local copies, waits for them, and re-layouts  13.2 us (7%)
  other arithmetic  10.3 us (6%)
    pallas_call x1, Pallas kernels, pack(): pl.pallas_call(functools.partial(pack_kernel, seq_count, query_parts, par...  49 us
    ppermute x22, starting transfers between devices, swap(): return lax.ppermute(x, axis, [(i, i ^ bit) for i in range(count)])  32.3 us
    all_to_all x1, waiting for transfers between devices, on_device(): lax.all_to_all(send, 'seq', split_axis=0, concat_axis=0, tiled=True)  25.6 us
    ppermute x22, waiting for transfers between devices, swap(): return lax.ppermute(x, axis, [(i, i ^ bit) for i in range(count)])  23.7 us
    pallas_call x1, Pallas kernels, attend(): pl.pallas_call(functools.partial(attend_kernel, seq_count, part_rows, tok...  8.68 us
    all_to_all x1, starting transfers between devices, on_device(): lax.all_to_all(send, 'seq', split_axis=0, concat_axis=0, tiled=True)  7.54 us
    unnamed x36, local copies, waits for them, and re-layouts  6.9 us
    select_n x5, other arithmetic, gather_doubling(): jnp.where(mine_first, x, other)  5.64 us
  transfers between devices with their start and end apart: 24, of which 10 were waited for; matrix products, arithmetic and copies ran while one was open for 8% of the time, Pallas kernels for 27%

profile of v1, /device:TPU:0, one launch (start us, length us, event | category | flops | bytes accessed | tf_op | source)
XLA Modules:
  0.0 184.8 jit_solution(6832656079872519652)
XLA Ops:
  1.6 4.0 %collective-permute-start.7 = (bf16[1,1,1,4,8,1280]{5,4,3,2,1,0:T(8,128)(2,1)S(1)}, bf16[1,1,1,4,8,1280]{5,4,3,2,1,0:T(8,128)(2,1)S(1)}, u32[]{:S(2)}, u32[]{:S(2)}) collective-permute-start(bf16[1,1,1,4,8,1280]{5,4,3,2,1,0:T(8,128)(2,1)S(1)} %dynamic-slice_bitcast_fusion), channel_id=1, source_target_pairs={{0,16},{4,20},{8,24},{12,28},{16,0},{20,4},{24,8},{28,12},{1,17},{... | collective-permute-start | bytes 245768 | tf_op jit(solution)/shard_map/ppermute | solution.py:298
  5.6 4.2 %collective-permute-done.7 = bf16[1,1,1,4,8,1280]{5,4,3,2,1,0:T(8,128)(2,1)S(1)} collective-permute-done((bf16[1,1,1,4,8,1280]{5,4,3,2,1,0:T(8,128)(2,1)S(1)}, bf16[1,1,1,4,8,1280]{5,4,3,2,1,0:T(8,128)(2,1)S(1)}, u32[]{:S(2)}, u32[]{:S(2)}) %collective-permute-start.7) | collective-permute-done | bytes 81952 | tf_op jit(solution)/shard_map/ppermute | solution.py:298
  11.5 4.6 %collective-permute-done.8 = bf16[2,1,1,4,8,1280]{5,4,3,2,1,0:T(8,128)(2,1)S(1)} collective-permute-done((bf16[2,1,1,4,8,1280]{5,4,3,2,1,0:T(8,128)(2,1)S(1)}, bf16[2,1,1,4,8,1280]{5,4,3,2,1,0:T(8,128)(2,1)S(1)}, u32[]{:S(2)}, u32[]{:S(2)}) %collective-permute-start.8) | collective-permute-done | bytes 163872 | tf_op jit(solution)/shard_map/ppermute | solution.py:298
  16.2 1.8 collective-permute-start.9
  18.0 5.8 %collective-permute-done.9 = bf16[2,2,1,4,8,1280]{5,4,3,2,1,0:T(8,128)(2,1)S(1)} collective-permute-done((bf16[2,2,1,4,8,1280]{5,4,3,2,1,0:T(8,128)(2,1)S(1)}, bf16[2,2,1,4,8,1280]{5,4,3,2,1,0:T(8,128)(2,1)S(1)}, u32[]{:S(2)}, u32[]{:S(2)}) %collective-permute-start.9) | collective-permute-done | bytes 327712 | tf_op jit(solution)/shard_map/ppermute | solution.py:298
  24.8 1.5 collective-permute-start.10
  26.3 49.0 %shard_map.139 = bf16[8,384,256]{2,1,0:T(8,128)(2,1)} custom-call(bf16[1,128,2048]{2,1,0:T(8,128)(2,1)} %q_ref.1, bf16[1,128,2048]{2,1,0:T(8,128)(2,1)} %k_ref.1, bf16[1,128,2048]{2,1,0:T(8,128)(2,1)} %v_ref.1), custom_call_target="tpu_custom_call" | custom-call | bytes 3145728 | tf_op jit(solution)/shard_map/pallas_call | solution.py:66
  75.3 7.5 %all-to-all-start = ((bf16[8,384,256]{2,1,0:T(8,128)(2,1)}), bf16[8,384,256]{2,1,0:T(8,128)(2,1)S(1)}, u32[]{:S(2)}, u32[]{:S(2)}) async-start(bf16[8,384,256]{2,1,0:T(8,128)(2,1)} %shard_map.139), calls=%async_computation | async-start | bytes 3145728 | tf_op jit(solution)/shard_map/all_to_all | solution.py:385
  89.0 3.4 %broadcast_select_fusion.1 = (bf16[2,1,4,64,1280]{4,3,2,1,0:T(8,128)(2,1)}, bf16[2,1,4,64,1280]{4,3,2,1,0:T(8,128)(2,1)}) fusion(bf16[2,1,4,64,1280]{4,3,2,1,0:T(8,128)(2,1)} %collective-permute-done.11, pred[]{:T(512)S(6)} %eq.15, bf16[1,1,4,64,1280]{4,3,2,1,0:T(8,128)(2,1)} %copy-done.8, bf16[1,1,4,64,1280]{4,3,2,1,0:T(8,128)(2,1)} %copy-done.7), kind=kLoop, calls=%fused_computation.5 | loop fusion | flops 1966080 | bytes 5242881 | tf_op jit(solution)/shard_map/jit(_where)/select_n | solution.py:311
  92.4 25.6 %all-to-all-done.in_ref = bf16[8,384,256]{2,1,0:T(8,128)(2,1)S(1)} async-done(((bf16[8,384,256]{2,1,0:T(8,128)(2,1)}), bf16[8,384,256]{2,1,0:T(8,128)(2,1)S(1)}, u32[]{:S(2)}, u32[]{:S(2)}) %all-to-all-start) | async-done | bytes 1572896 | tf_op jit(solution)/shard_map/all_to_all | solution.py:385
  118.0 8.7 %shard_map.140 = (bf16[8,128,256]{2,1,0:T(8,128)(2,1)S(1)}, bf16[8,64,128]{2,1,0:T(8,128)(2,1)}) custom-call(bf16[8,384,256]{2,1,0:T(8,128)(2,1)S(1)} %all-to-all-done.in_ref, f32[1,256]{1,0:T(1,128)S(1)} %get-tuple-element.26.scale_ref, f32[1,256]{1,0:T(1,128)S(1)} %get-tuple-element.25.shift_ref, bf16[256,64]{1,0:T(8,128)(2,1)S(1)} %copy.21.proj_ref), custom_call_target="tpu_custom_call" | custom-call | flops 1073741824 | bytes 2097152 | tf_op jit(solution)/shard_map/pallas_call | solution.py:123
  126.7 3.4 %all-to-all-start.1 = ((bf16[8,64,128]{2,1,0:T(8,128)(2,1)}), bf16[8,64,128]{2,1,0:T(8,128)(2,1)S(1)}, u32[]{:S(2)}, u32[]{:S(2)}) async-start(bf16[8,64,128]{2,1,0:T(8,128)(2,1)} %get-tuple-element.8), calls=%async_computation.1 | async-start | bytes 262144 | tf_op jit(solution)/shard_map/all_to_all | solution.py:394
  130.1 2.0 %pad_maximum_fusion = bf16[2,2,4,64,1280]{4,3,2,1,0:T(8,128)(2,1)S(1)} fusion(bf16[2,1,4,64,1280]{4,3,2,1,0:T(8,128)(2,1)} %get-tuple-element.16, bf16[2,1,4,64,1280]{4,3,2,1,0:T(8,128)(2,1)} %get-tuple-element.15), kind=kLoop, calls=%fused_computation.2 | loop fusion | flops 1310720 | bytes 5242880 | tf_op jit(solution)/shard_map/concatenate | solution.py:310
  132.1 5.4 %all-to-all-done.1 = bf16[8,64,128]{2,1,0:T(8,128)(2,1)S(1)} async-done(((bf16[8,64,128]{2,1,0:T(8,128)(2,1)}), bf16[8,64,128]{2,1,0:T(8,128)(2,1)S(1)}, u32[]{:S(2)}, u32[]{:S(2)}) %all-to-all-start.1) | async-done | bytes 131104 | tf_op jit(solution)/shard_map/all_to_all | solution.py:394
  140.7 2.2 %collective-permute-start.2 = (bf16[64,128]{1,0:T(8,128)(2,1)}, bf16[64,128]{1,0:T(8,128)(2,1)S(1)}, u32[]{:S(2)}, u32[]{:S(2)}) collective-permute-start(bf16[64,128]{1,0:T(8,128)(2,1)} %reduce_sum.12), channel_id=1, source_target_pairs={{0,12},{4,8},{8,4},{12,0},{16,28},{20,24},{24,20},{28,16},{1,13},{... | collective-permute-start | bytes 49160 | tf_op jit(solution)/shard_map/ppermute | solution.py:298
  143.3 2.3 %collective-permute-start.4 = (bf16[64,128]{1,0:T(8,128)(2,1)}, bf16[64,128]{1,0:T(8,128)(2,1)S(1)}, u32[]{:S(2)}, u32[]{:S(2)}) collective-permute-start(bf16[64,128]{1,0:T(8,128)(2,1)} %reduce_sum.12), channel_id=1, source_target_pairs={{0,20},{4,16},{8,28},{12,24},{16,4},{20,0},{24,12},{28,8},{1,21},{... | collective-permute-start | bytes 49160 | tf_op jit(solution)/shard_map/ppermute | solution.py:298
  147.7 3.5 %collective-permute-start.6 = (bf16[64,128]{1,0:T(8,128)(2,1)}, bf16[64,128]{1,0:T(8,128)(2,1)S(1)}, u32[]{:S(2)}, u32[]{:S(2)}) collective-permute-start(bf16[64,128]{1,0:T(8,128)(2,1)} %reduce_sum.12), channel_id=1, source_target_pairs={{0,28},{4,24},{8,20},{12,16},{16,12},{20,8},{24,4},{28,0},{1,29},{... | collective-permute-start | bytes 49160 | tf_op jit(solution)/shard_map/ppermute | solution.py:298
  155.0 1.6 gather_fusion
  158.2 2.8 %shard_map.141 = (f32[1,128]{1,0:T(1,128)}, bf16[512,128]{1,0:T(8,128)(2,1)S(1)}, f32[64,256]{1,0:T(8,128)S(1)}) custom-call(bf16[512,128]{1,0:T(8,128)(2,1)S(1)} %bitcast.62, bf16[1024,1280]{1,0:T(8,128)(2,1)S(1)} %bitcast.61, bf16[64,1280]{1,0:T(8,128)(2,1)S(1)} %copy-done.3, f32[1,1280]{1,0:T(1,128)S(1)} %broadcast_in_dim.11.pre_ref, ...), custom_call_target="tpu_custom_call" | custom-call | flops 503316480 | bytes 2785280 | tf_op jit(solution)/shard_map/pallas_call | solution.py:231
  162.8 2.4 %collective-permute-done.13 = bf16[64,256]{1,0:T(8,128)(2,1)S(1)} collective-permute-done((bf16[64,256]{1,0:T(8,128)(2,1)S(1)}, bf16[64,256]{1,0:T(8,128)(2,1)S(1)}, u32[]{:S(2)}, u32[]{:S(2)}) %collective-permute-start.13) | collective-permute-done | bytes 32800 | tf_op jit(solution)/shard_map/ppermute | solution.py:298
  167.6 2.5 %collective-permute-start.17 = (bf16[64,256]{1,0:T(8,128)(2,1)S(1)}, bf16[64,256]{1,0:T(8,128)(2,1)S(1)}, u32[]{:S(2)}, u32[]{:S(2)}) collective-permute-start(bf16[64,256]{1,0:T(8,128)(2,1)S(1)} %get-tuple-element.14), channel_id=1, source_target_pairs={{0,12},{4,8},{8,4},{12,0},{16,28},{20,24},{24,20},{28,16},{1,13},{... | collective-permute-start | bytes 98312 | tf_op jit(solution)/shard_map/ppermute | solution.py:298
  171.3 2.2 %collective-permute-start.19 = (bf16[64,256]{1,0:T(8,128)(2,1)S(1)}, bf16[64,256]{1,0:T(8,128)(2,1)S(1)}, u32[]{:S(2)}, u32[]{:S(2)}) collective-permute-start(bf16[64,256]{1,0:T(8,128)(2,1)S(1)} %get-tuple-element.14), channel_id=1, source_target_pairs={{0,20},{4,16},{8,28},{12,24},{16,4},{20,0},{24,12},{28,8},{1,21},{... | collective-permute-start | bytes 98312 | tf_op jit(solution)/shard_map/ppermute | solution.py:298
  173.5 3.1 %collective-permute-start.20 = (bf16[64,256]{1,0:T(8,128)(2,1)S(1)}, bf16[64,256]{1,0:T(8,128)(2,1)S(1)}, u32[]{:S(2)}, u32[]{:S(2)}) collective-permute-start(bf16[64,256]{1,0:T(8,128)(2,1)S(1)} %get-tuple-element.14), channel_id=1, source_target_pairs={{0,24},{4,28},{8,16},{12,20},{16,8},{20,12},{24,0},{28,4},{1,25},{... | collective-permute-start | bytes 98312 | tf_op jit(solution)/shard_map/ppermute | solution.py:298
  179.3 3.9 %collective-permute-done.21 = bf16[64,256]{1,0:T(8,128)(2,1)S(1)} collective-permute-done((bf16[64,256]{1,0:T(8,128)(2,1)S(1)}, bf16[64,256]{1,0:T(8,128)(2,1)S(1)}, u32[]{:S(2)}, u32[]{:S(2)}) %collective-permute-start.21) | collective-permute-done | bytes 32800 | tf_op jit(solution)/shard_map/ppermute | solution.py:298
  (91 shorter events, 29.9 us)
Async XLA Ops:
  1.6 8.2 %collective-permute-start.7 = (bf16[1,1,1,4,8,1280]{5,4,3,2,1,0:T(8,128)(2,1)S(1)}, bf16[1,1,1,4,8,1280]{5,4,3,2,1,0:T(8,128)(2,1)S(1)}, u32[]{:S(2)}, u32[]{:S(2)}) collective-permute-start(bf16[1,1,1,4,8,1280]{5,4,3,2,1,0:T(8,128)(2,1)S(1)} %dynamic-slice_bitcast_fusion), channel_id=1, source_target_pairs={{0,16},{4,20},{8,24},{12,28},{16,0},{20,4},{24,8},{28,12},{1,17},{... | collective-permute-start | bytes 245768 | tf_op jit(solution)/shard_map/ppermute | solution.py:298
  10.8 5.4 %collective-permute-start.8 = (bf16[2,1,1,4,8,1280]{5,4,3,2,1,0:T(8,128)(2,1)S(1)}, bf16[2,1,1,4,8,1280]{5,4,3,2,1,0:T(8,128)(2,1)S(1)}, u32[]{:S(2)}, u32[]{:S(2)}) collective-permute-start(bf16[2,1,1,4,8,1280]{5,4,3,2,1,0:T(8,128)(2,1)S(1)} %pad_maximum_fusion.4), channel_id=1, source_target_pairs={{0,8},{4,12},{8,0},{12,4},{16,24},{20,28},{24,16},{28,20},{1,9},{5... | collective-permute-start | bytes 491528 | tf_op jit(solution)/shard_map/ppermute | solution.py:298
  16.2 7.6 %collective-permute-start.9 = (bf16[2,2,1,4,8,1280]{5,4,3,2,1,0:T(8,128)(2,1)S(1)}, bf16[2,2,1,4,8,1280]{5,4,3,2,1,0:T(8,128)(2,1)S(1)}, u32[]{:S(2)}, u32[]{:S(2)}) collective-permute-start(bf16[2,2,1,4,8,1280]{5,4,3,2,1,0:T(8,128)(2,1)S(1)} %pad_maximum_fusion.3), channel_id=1, source_target_pairs={{0,4},{4,0},{8,12},{12,8},{16,20},{20,16},{24,28},{28,24},{1,5},{5... | collective-permute-start | bytes 983048 | tf_op jit(solution)/shard_map/ppermute | solution.py:298
  24.8 58.0 %collective-permute-start.10 = (bf16[1,1,4,64,1280]{4,3,2,1,0:T(8,128)(2,1)}, bf16[1,1,4,64,1280]{4,3,2,1,0:T(8,128)(2,1)}, u32[]{:S(2)}, u32[]{:S(2)}) collective-permute-start(bf16[1,1,4,64,1280]{4,3,2,1,0:T(8,128)(2,1)} %copy_bitcast_fusion), channel_id=1, source_target_pairs={{0,2},{1,3},{2,0},{3,1},{4,6},{5,7},{6,4},{7,5},{8,10},{9,11},{10,... | collective-permute-start | bytes 1966088 | tf_op jit(solution)/shard_map/ppermute | solution.py:298
  75.3 42.7 %all-to-all-start = ((bf16[8,384,256]{2,1,0:T(8,128)(2,1)}), bf16[8,384,256]{2,1,0:T(8,128)(2,1)S(1)}, u32[]{:S(2)}, u32[]{:S(2)}) async-start(bf16[8,384,256]{2,1,0:T(8,128)(2,1)} %shard_map.139), calls=%async_computation | async-start | bytes 3145728 | tf_op jit(solution)/shard_map/all_to_all | solution.py:385
  85.6 3.4 %collective-permute-start.11 = (bf16[2,1,4,64,1280]{4,3,2,1,0:T(8,128)(2,1)}, bf16[2,1,4,64,1280]{4,3,2,1,0:T(8,128)(2,1)}, u32[]{:S(2)}, u32[]{:S(2)}) collective-permute-start(bf16[2,1,4,64,1280]{4,3,2,1,0:T(8,128)(2,1)} %pad_maximum_fusion.1), channel_id=1, source_target_pairs={{0,1},{1,0},{2,3},{3,2},{4,5},{5,4},{6,7},{7,6},{8,9},{9,8},{10,11... | collective-permute-start | bytes 3932168 | tf_op jit(solution)/shard_map/ppermute | solution.py:298
  126.7 10.8 %all-to-all-start.1 = ((bf16[8,64,128]{2,1,0:T(8,128)(2,1)}), bf16[8,64,128]{2,1,0:T(8,128)(2,1)S(1)}, u32[]{:S(2)}, u32[]{:S(2)}) async-start(bf16[8,64,128]{2,1,0:T(8,128)(2,1)} %get-tuple-element.8), calls=%async_computation.1 | async-start | bytes 262144 | tf_op jit(solution)/shard_map/all_to_all | solution.py:394
  138.1 7.6 %collective-permute-start = (bf16[64,128]{1,0:T(8,128)(2,1)}, bf16[64,128]{1,0:T(8,128)(2,1)S(1)}, u32[]{:S(2)}, u32[]{:S(2)}) collective-permute-start(bf16[64,128]{1,0:T(8,128)(2,1)} %reduce_sum.12), channel_id=1, source_target_pairs={{0,4},{4,0},{8,12},{12,8},{16,20},{20,16},{24,28},{28,24},{1,5},{5... | collective-permute-start | bytes 49160 | tf_op jit(solution)/shard_map/ppermute | solution.py:298
  139.8 7.9 %collective-permute-start.1 = (bf16[64,128]{1,0:T(8,128)(2,1)}, bf16[64,128]{1,0:T(8,128)(2,1)S(1)}, u32[]{:S(2)}, u32[]{:S(2)}) collective-permute-start(bf16[64,128]{1,0:T(8,128)(2,1)} %reduce_sum.12), channel_id=1, source_target_pairs={{0,8},{4,12},{8,0},{12,4},{16,24},{20,28},{24,16},{28,20},{1,9},{5... | collective-permute-start | bytes 49160 | tf_op jit(solution)/shard_map/ppermute | solution.py:298
  140.7 11.1 %collective-permute-start.2 = (bf16[64,128]{1,0:T(8,128)(2,1)}, bf16[64,128]{1,0:T(8,128)(2,1)S(1)}, u32[]{:S(2)}, u32[]{:S(2)}) collective-permute-start(bf16[64,128]{1,0:T(8,128)(2,1)} %reduce_sum.12), channel_id=1, source_target_pairs={{0,12},{4,8},{8,4},{12,0},{16,28},{20,24},{24,20},{28,16},{1,13},{... | collective-permute-start | bytes 49160 | tf_op jit(solution)/shard_map/ppermute | solution.py:298
  142.9 9.5 %collective-permute-start.3 = (bf16[64,128]{1,0:T(8,128)(2,1)}, bf16[64,128]{1,0:T(8,128)(2,1)S(1)}, u32[]{:S(2)}, u32[]{:S(2)}) collective-permute-start(bf16[64,128]{1,0:T(8,128)(2,1)} %reduce_sum.12), channel_id=1, source_target_pairs={{0,16},{4,20},{8,24},{12,28},{16,0},{20,4},{24,8},{28,12},{1,17},{... | collective-permute-start | bytes 49160 | tf_op jit(solution)/shard_map/ppermute | solution.py:298
  143.3 9.7 %collective-permute-start.4 = (bf16[64,128]{1,0:T(8,128)(2,1)}, bf16[64,128]{1,0:T(8,128)(2,1)S(1)}, u32[]{:S(2)}, u32[]{:S(2)}) collective-permute-start(bf16[64,128]{1,0:T(8,128)(2,1)} %reduce_sum.12), channel_id=1, source_target_pairs={{0,20},{4,16},{8,28},{12,24},{16,4},{20,0},{24,12},{28,8},{1,21},{... | collective-permute-start | bytes 49160 | tf_op jit(solution)/shard_map/ppermute | solution.py:298
  145.7 8.0 %collective-permute-start.5 = (bf16[64,128]{1,0:T(8,128)(2,1)}, bf16[64,128]{1,0:T(8,128)(2,1)S(1)}, u32[]{:S(2)}, u32[]{:S(2)}) collective-permute-start(bf16[64,128]{1,0:T(8,128)(2,1)} %reduce_sum.12), channel_id=1, source_target_pairs={{0,24},{4,28},{8,16},{12,20},{16,8},{20,12},{24,0},{28,4},{1,25},{... | collective-permute-start | bytes 49160 | tf_op jit(solution)/shard_map/ppermute | solution.py:298
  147.7 6.6 %collective-permute-start.6 = (bf16[64,128]{1,0:T(8,128)(2,1)}, bf16[64,128]{1,0:T(8,128)(2,1)S(1)}, u32[]{:S(2)}, u32[]{:S(2)}) collective-permute-start(bf16[64,128]{1,0:T(8,128)(2,1)} %reduce_sum.12), channel_id=1, source_target_pairs={{0,28},{4,24},{8,20},{12,16},{16,12},{20,8},{24,4},{28,0},{1,29},{... | collective-permute-start | bytes 49160 | tf_op jit(solution)/shard_map/ppermute | solution.py:298
  161.0 1.9 %collective-permute-start.12 = (bf16[64,256]{1,0:T(8,128)(2,1)S(1)}, bf16[64,256]{1,0:T(8,128)(2,1)S(1)}, u32[]{:S(2)}, u32[]{:S(2)}) collective-permute-start(bf16[64,256]{1,0:T(8,128)(2,1)S(1)} %multiply_convert_fusion), channel_id=1, source_target_pairs={{0,1},{1,0},{2,3},{3,2},{4,5},{5,4},{6,7},{7,6},{8,9},{9,8},{10,11... | collective-permute-start | bytes 98312 | tf_op jit(solution)/shard_map/ppermute | solution.py:298
  161.0 4.3 %collective-permute-start.13 = (bf16[64,256]{1,0:T(8,128)(2,1)S(1)}, bf16[64,256]{1,0:T(8,128)(2,1)S(1)}, u32[]{:S(2)}, u32[]{:S(2)}) collective-permute-start(bf16[64,256]{1,0:T(8,128)(2,1)S(1)} %multiply_convert_fusion), channel_id=1, source_target_pairs={{0,2},{1,3},{2,0},{3,1},{4,6},{5,7},{6,4},{7,5},{8,10},{9,11},{10,... | collective-permute-start | bytes 98312 | tf_op jit(solution)/shard_map/ppermute | solution.py:298
  161.6 3.7 %collective-permute-start.14 = (bf16[64,256]{1,0:T(8,128)(2,1)S(1)}, bf16[64,256]{1,0:T(8,128)(2,1)S(1)}, u32[]{:S(2)}, u32[]{:S(2)}) collective-permute-start(bf16[64,256]{1,0:T(8,128)(2,1)S(1)} %multiply_convert_fusion), channel_id=1, source_target_pairs={{0,3},{1,2},{2,1},{3,0},{4,7},{5,6},{6,5},{7,4},{8,11},{9,10},{10,... | collective-permute-start | bytes 98312 | tf_op jit(solution)/shard_map/ppermute | solution.py:298
  165.3 8.2 %collective-permute-start.15 = (bf16[64,256]{1,0:T(8,128)(2,1)S(1)}, bf16[64,256]{1,0:T(8,128)(2,1)S(1)}, u32[]{:S(2)}, u32[]{:S(2)}) collective-permute-start(bf16[64,256]{1,0:T(8,128)(2,1)S(1)} %get-tuple-element.14), channel_id=1, source_target_pairs={{0,4},{4,0},{8,12},{12,8},{16,20},{20,16},{24,28},{28,24},{1,5},{5... | collective-permute-start | bytes 98312 | tf_op jit(solution)/shard_map/ppermute | solution.py:298
  167.6 9.0 %collective-permute-start.16 = (bf16[64,256]{1,0:T(8,128)(2,1)S(1)}, bf16[64,256]{1,0:T(8,128)(2,1)S(1)}, u32[]{:S(2)}, u32[]{:S(2)}) collective-permute-start(bf16[64,256]{1,0:T(8,128)(2,1)S(1)} %get-tuple-element.14), channel_id=1, source_target_pairs={{0,8},{4,12},{8,0},{12,4},{16,24},{20,28},{24,16},{28,20},{1,9},{5... | collective-permute-start | bytes 98312 | tf_op jit(solution)/shard_map/ppermute | solution.py:298
  167.6 10.2 %collective-permute-start.17 = (bf16[64,256]{1,0:T(8,128)(2,1)S(1)}, bf16[64,256]{1,0:T(8,128)(2,1)S(1)}, u32[]{:S(2)}, u32[]{:S(2)}) collective-permute-start(bf16[64,256]{1,0:T(8,128)(2,1)S(1)} %get-tuple-element.14), channel_id=1, source_target_pairs={{0,12},{4,8},{8,4},{12,0},{16,28},{20,24},{24,20},{28,16},{1,13},{... | collective-permute-start | bytes 98312 | tf_op jit(solution)/shard_map/ppermute | solution.py:298
  170.1 7.7 %collective-permute-start.18 = (bf16[64,256]{1,0:T(8,128)(2,1)S(1)}, bf16[64,256]{1,0:T(8,128)(2,1)S(1)}, u32[]{:S(2)}, u32[]{:S(2)}) collective-permute-start(bf16[64,256]{1,0:T(8,128)(2,1)S(1)} %get-tuple-element.14), channel_id=1, source_target_pairs={{0,16},{4,20},{8,24},{12,28},{16,0},{20,4},{24,8},{28,12},{1,17},{... | collective-permute-start | bytes 98312 | tf_op jit(solution)/shard_map/ppermute | solution.py:298
  171.3 6.6 %collective-permute-start.19 = (bf16[64,256]{1,0:T(8,128)(2,1)S(1)}, bf16[64,256]{1,0:T(8,128)(2,1)S(1)}, u32[]{:S(2)}, u32[]{:S(2)}) collective-permute-start(bf16[64,256]{1,0:T(8,128)(2,1)S(1)} %get-tuple-element.14), channel_id=1, source_target_pairs={{0,20},{4,16},{8,28},{12,24},{16,4},{20,0},{24,12},{28,8},{1,21},{... | collective-permute-start | bytes 98312 | tf_op jit(solution)/shard_map/ppermute | solution.py:298
  173.5 5.8 %collective-permute-start.20 = (bf16[64,256]{1,0:T(8,128)(2,1)S(1)}, bf16[64,256]{1,0:T(8,128)(2,1)S(1)}, u32[]{:S(2)}, u32[]{:S(2)}) collective-permute-start(bf16[64,256]{1,0:T(8,128)(2,1)S(1)} %get-tuple-element.14), channel_id=1, source_target_pairs={{0,24},{4,28},{8,16},{12,20},{16,8},{20,12},{24,0},{28,4},{1,25},{... | collective-permute-start | bytes 98312 | tf_op jit(solution)/shard_map/ppermute | solution.py:298
  176.6 6.6 %collective-permute-start.21 = (bf16[64,256]{1,0:T(8,128)(2,1)S(1)}, bf16[64,256]{1,0:T(8,128)(2,1)S(1)}, u32[]{:S(2)}, u32[]{:S(2)}) collective-permute-start(bf16[64,256]{1,0:T(8,128)(2,1)S(1)} %get-tuple-element.14), channel_id=1, source_target_pairs={{0,28},{4,24},{8,20},{12,16},{16,12},{20,8},{24,4},{28,0},{1,29},{... | collective-permute-start | bytes 98312 | tf_op jit(solution)/shard_map/ppermute | solution.py:298
  (11 other events, 172.0 us)

commit v2 on v1

v2 whole, which is shorter than its diff:
```python
import functools
import math

import jax
import jax.numpy as jnp
from jax import lax
from jax.experimental import pallas as pl
from jax.experimental.pallas import tpu as pltpu
from jax.sharding import PartitionSpec as P

HEADS = 16
HD = 128
CH = 64
GW = 64
VW = 1280
EPS = 1e-05
BF16 = jnp.bfloat16
F32 = jnp.float32
VMEM_LIMIT = 48 * 1024 * 1024


def mm(a, b):
    return jnp.dot(a, b, preferred_element_type=F32)


def mm_nt(a, b):
    return lax.dot_general(a, b, (((1,), (1,)), ((), ())), preferred_element_type=F32)


def mm_tn(a, b):
    return lax.dot_general(a, b, (((0,), (0,)), ((), ())), preferred_element_type=F32)


def pack_kernel(count, query_parts, part_rows, tok_rows, width, place_ref, q_ref, k_ref, v_ref, *out_refs):
    me = place_ref[0]
    for mask in range(count):
        dest = jnp.bitwise_xor(me, mask)
        group, part = dest // query_parts, dest % query_parts
        cols = pl.ds(pl.multiple_of(group * width, HD), width)
        first = pl.multiple_of(part * part_rows, part_rows)
        out = out_refs[mask]
        out[pl.ds(0, part_rows), :] = q_ref[0, pl.ds(first, part_rows), cols]
        out[pl.ds(part_rows, tok_rows), :] = k_ref[0, :, cols]
        out[pl.ds(part_rows + tok_rows, tok_rows), :] = v_ref[0, :, cols]


def pack(place, queries, keys, values, count, query_parts, part_rows, tok_rows, width):
    rows = part_rows + 2 * tok_rows
    vmem = pl.BlockSpec(memory_space=pltpu.VMEM)
    return pl.pallas_call(
        functools.partial(pack_kernel, count, query_parts, part_rows, tok_rows, width),
        out_shape=[jax.ShapeDtypeStruct((rows, width), BF16)] * count,
        in_specs=[pl.BlockSpec(memory_space=pltpu.SMEM)] + [vmem] * 3,
        out_specs=[vmem] * count,
        compiler_params=pltpu.CompilerParams(vmem_limit_bytes=VMEM_LIMIT),
        cost_estimate=pl.CostEstimate(
            flops=0, bytes_accessed=4 * count * rows * width, transcendentals=0
        ),
    )(place, queries, keys, values)


def attend_kernel(count, query_parts, part_rows, tok_rows, heads, *refs):
    in_refs = refs[:count]
    scale_ref, shift_ref, proj_ref, mod_ref, keep_ref, send_ref, key_scr, value_scr = refs[count:]
    half = part_rows // 2
    factor = HD ** (-0.5) * math.log2(math.e)
    ones = jnp.ones((tok_rows, HD), BF16)
    for src in range(count):
        rows = pl.ds(src * tok_rows, tok_rows)
        key_scr[rows, :] = in_refs[src][pl.ds(part_rows, tok_rows), :]
        for head in range(heads):
            value_scr[rows, pl.ds(2 * head * HD, HD)] = in_refs[src][
                pl.ds(part_rows + tok_rows, tok_rows), pl.ds(head * HD, HD)
            ]
            value_scr[rows, pl.ds((2 * head + 1) * HD, HD)] = ones
    gain = 1.0 + scale_ref[...]
    shift = shift_ref[...]
    proj = proj_ref[...]
    zero = jnp.zeros_like(proj)
    proj_pair = jnp.concatenate(
        [jnp.concatenate([proj, zero], axis=1), jnp.concatenate([zero, proj], axis=1)], axis=0
    )
    for src in range(count):
        mixed = []
        for head in range(heads):
            cols = pl.ds(head * HD, HD)
            query = in_refs[src][pl.ds(0, part_rows), cols]
            logits = mm_nt(query, key_scr[:, cols])
            top = jnp.max(logits, axis=-1, keepdims=True)
            weights = jnp.exp2((logits - top) * factor).astype(BF16)
            both = mm(weights, value_scr[:, pl.ds(2 * head * HD, 2 * HD)])
            mixed.append(both[:, :HD] / both[:, HD:])
        attended = jnp.concatenate(mixed, axis=1) if heads > 1 else mixed[0]
        modulated = (attended * gain + shift).astype(BF16)
        mod_ref[src] = modulated
        pair = jnp.concatenate([modulated[:half], modulated[half:]], axis=1)
        group, inner = src // query_parts, src % query_parts
        out_ref = send_ref if group % 2 else keep_ref
        out_ref[(group // 2) * query_parts + inner] = mm(pair, proj_pair).astype(BF16)


def attend(received, scale, shift, proj, query_parts, part_rows, tok_rows, heads):
    count = len(received)
    width = heads * HD
    lat_rows = count * tok_rows
    query_rows = count * part_rows
    vmem = pl.BlockSpec(memory_space=pltpu.VMEM)
    blocks = jax.ShapeDtypeStruct((count // 2, part_rows // 2, 2 * CH), BF16)
    return pl.pallas_call(
        functools.partial(attend_kernel, count, query_parts, part_rows, tok_rows, heads),
        out_shape=(jax.ShapeDtypeStruct((count, part_rows, width), BF16), blocks, blocks),
        in_specs=[vmem] * (count + 3),
        out_specs=(vmem, vmem, vmem),
        scratch_shapes=[
            pltpu.VMEM((lat_rows, width), BF16),
            pltpu.VMEM((lat_rows, 2 * width), BF16),
        ],
        compiler_params=pltpu.CompilerParams(vmem_limit_bytes=VMEM_LIMIT),
        cost_estimate=pl.CostEstimate(
            flops=4 * query_rows * lat_rows * width,
            bytes_accessed=2 * (query_rows * 2 + lat_rows * 2) * width,
            transcendentals=query_rows * lat_rows * heads,
        ),
    )(*received, scale, shift, proj)


def add_split_kernel(ways, keep_ref, got_ref, *out_refs):
    for way in range(ways):
        for slot in range(keep_ref.shape[0] // ways):
            block = slot * ways + way
            total = keep_ref[block].astype(F32) + got_ref[block].astype(F32)
            out_refs[way][slot] = total.astype(BF16)


def add_split(keep, got, ways):
    vmem = pl.BlockSpec(memory_space=pltpu.VMEM)
    shape = (keep.shape[0] // ways,) + keep.shape[1:]
    return pl.pallas_call(
        functools.partial(add_split_kernel, ways),
        out_shape=[jax.ShapeDtypeStruct(shape, BF16)] * ways,
        in_specs=[vmem] * 2,
        out_specs=[vmem] * ways,
    )(keep, got)


def lane_mean(x, count):
    return jnp.sum(x, axis=-1, keepdims=True) * (1.0 / count)


def head_kernel(grid_rows, fused, lat_masks, embed_masks, place_ref, *refs):
    lat_refs, refs = refs[: len(lat_masks)], refs[len(lat_masks) :]
    embed_refs, refs = refs[: len(embed_masks)], refs[len(embed_masks) :]
    pos_ref, pre_ref, post_ref, prompt_ref, cot_ref, mod_ref, *refs = refs
    reward_ref, grad_ref, weight_ref, lat_scr, grad_scr, embed_ref, sems = refs
    patch_rows = grid_rows // 4
    patch_cols = GW // 4
    patches = patch_rows * patch_cols
    me = place_ref[0]
    copies = []
    for slot, mask in enumerate(embed_masks):
        rows = embed_refs[slot].shape[0]
        first = pl.multiple_of(jnp.bitwise_xor(place_ref[1], mask) * rows, rows)
        copies.append(
            pltpu.make_async_copy(embed_refs[slot], embed_ref.at[pl.ds(first, rows)], sems.at[slot])
        )
        copies[-1].start()
    for ref, masks in zip(lat_refs, lat_masks):
        for slot, mask in enumerate(masks):
            first = pl.multiple_of(jnp.bitwise_xor(me, mask) * GW, GW)
            lat_scr[pl.ds(first, GW), :] = ref[slot].astype(F32)
    for copy in copies:
        copy.wait()

    def embed_block(hi, tx):
        first = 4 * (2 * hi) + tx
        second = 4 * (2 * hi + 1) + tx
        return jnp.concatenate(
            [embed_ref[pl.ds(first * CH, CH), :], embed_ref[pl.ds(second * CH, CH), :]], axis=0
        )

    embedded = pos_ref[...].astype(F32)
    for hi in range(2):
        for tx in range(4):
            rows = [
                lat_scr[pl.ds((2 * pr + hi) * GW + tx, patch_cols, stride=4), :]
                for pr in range(patch_rows)
            ]
            block = jnp.concatenate(rows, axis=0).astype(BF16)
            embedded = embedded + mm(block, embed_block(hi, tx))
    pre = pre_ref[...]
    post = post_ref[...]
    prompt = prompt_ref[...]
    center = embedded - lane_mean(embedded, VW)
    rstd = lax.rsqrt(lane_mean(center * center, VW) + EPS)
    unit = center * rstd
    pooled = jnp.sum(unit, axis=0, keepdims=True) * (1.0 / patches) * pre
    pooled_center = pooled - lane_mean(pooled, VW)
    pooled_rstd = lax.rsqrt(lane_mean(pooled_center * pooled_center, VW) + EPS)
    pooled_unit = pooled_center * pooled_rstd
    final = pooled_unit * post
    dot = jnp.sum(final * prompt, axis=-1, keepdims=True)
    final_sq = jnp.sum(final * final, axis=-1, keepdims=True)
    prompt_sq = jnp.sum(prompt * prompt, axis=-1, keepdims=True)
    final_len = jnp.sqrt(final_sq)
    prompt_len = jnp.sqrt(prompt_sq)
    cosine = dot / (final_len * prompt_len)
    reward_ref[...] = jnp.broadcast_to(100.0 * cosine, reward_ref.shape)
    cot = cot_ref[...]
    final_grad = (100.0 * cot) * (prompt / (final_len * prompt_len) - final * (cosine / final_sq))
    unit_grad = final_grad * post
    pooled_grad = pooled_rstd * (
        unit_grad
        - lane_mean(unit_grad, VW)
        - pooled_unit * lane_mean(unit_grad * pooled_unit, VW)
    )
    flow = pooled_grad * pre * (1.0 / patches)
    embed_grad = rstd * (flow - lane_mean(flow, VW) - unit * lane_mean(flow * unit, VW))
    high = embed_grad.astype(BF16)
    low = (embed_grad - high.astype(F32)).astype(BF16)
    stacked = jnp.concatenate([high, low], axis=0)
    for hi in range(2):
        for tx in range(4):
            both = mm_nt(stacked, embed_block(hi, tx))
            piece = both[:patches] + both[patches:]
            for pr in range(patch_rows):
                grad_scr[pl.ds((2 * pr + hi) * GW + tx, patch_cols, stride=4), :] = piece[
                    pr * patch_cols : (pr + 1) * patch_cols
                ]
    grad = grad_scr[...].astype(BF16)
    grad_ref[...] = grad
    if fused:
        blocks = [
            grad_scr[pl.ds(pl.multiple_of(jnp.bitwise_xor(me, mask) * GW, GW), GW), :].astype(BF16)
            for mask in range(grid_rows // 2)
        ]
        weight_ref[...] = readout_grad(jnp.concatenate(blocks, axis=0), mod_ref)
    else:
        weight_ref[...] = jnp.zeros_like(weight_ref)


def readout_grad(grad, mod_ref):
    count, rows, width = mod_ref.shape
    half = rows // 2
    first = mod_ref[:, :half, :].reshape(count * half, width)
    second = mod_ref[:, half:, :].reshape(count * half, width)
    return mm_tn(grad, first)[:CH] + mm_tn(grad, second)[CH:]


def reward_head(place, latent, embed, pos, pre, post, prompt, cot, modulated, grid_rows, fused):
    patches = grid_rows * GW // 16
    rows = grid_rows * GW // 2
    width = modulated.shape[2]
    lat_arrays, lat_masks = [x for x, _ in latent], [masks for _, masks in latent]
    embed_arrays, embed_masks = [x for x, _ in embed], [mask for _, mask in embed]
    vmem = pl.BlockSpec(memory_space=pltpu.VMEM)
    anywhere = pl.BlockSpec(memory_space=pl.ANY)
    return pl.pallas_call(
        functools.partial(head_kernel, grid_rows, fused, lat_masks, embed_masks),
        out_shape=(
            jax.ShapeDtypeStruct((1, 128), F32),
            jax.ShapeDtypeStruct((rows, 2 * CH), BF16),
            jax.ShapeDtypeStruct((CH, width), F32),
        ),
        in_specs=[pl.BlockSpec(memory_space=pltpu.SMEM)]
        + [vmem] * len(lat_arrays)
        + [anywhere] * len(embed_arrays)
        + [vmem] * 6,
        out_specs=(vmem, vmem, vmem),
        scratch_shapes=[
            pltpu.VMEM((rows, 2 * CH), F32),
            pltpu.VMEM((rows, 2 * CH), F32),
            pltpu.VMEM((16 * CH, VW), BF16),
            pltpu.SemaphoreType.DMA((len(embed_arrays),)),
        ],
        compiler_params=pltpu.CompilerParams(vmem_limit_bytes=VMEM_LIMIT),
        cost_estimate=pl.CostEstimate(
            flops=6 * patches * 16 * CH * VW,
            bytes_accessed=2 * 16 * CH * VW + 2 * patches * VW,
            transcendentals=0,
        ),
    )(place, *lat_arrays, *embed_arrays, pos, pre, post, prompt, cot, modulated)


def spread_kernel(count, half, heads, grad_ref, scale_ref, proj_ref, out_ref):
    gain = 1.0 + scale_ref[...]
    proj = proj_ref[...]
    zero = jnp.zeros_like(proj)
    sides = (jnp.concatenate([proj, zero], axis=1), jnp.concatenate([zero, proj], axis=1))
    for src in range(count):
        grad = grad_ref[pl.ds(src * half, half), :]
        for side in range(2):
            rows = (mm_nt(grad, sides[side]) * gain).astype(BF16)
            for head in range(heads):
                out_ref[0, head, pl.ds((2 * src + side) * half, half), :] = rows[
                    :, head * HD : (head + 1) * HD
                ]


def spread(grad, scale, proj, count, half, heads):
    vmem = pl.BlockSpec(memory_space=pltpu.VMEM)
    return pl.pallas_call(
        functools.partial(spread_kernel, count, half, heads),
        out_shape=jax.ShapeDtypeStruct((1, heads, 2 * count * half, HD), BF16),
        in_specs=[vmem] * 3,
        out_specs=vmem,
        compiler_params=pltpu.CompilerParams(vmem_limit_bytes=VMEM_LIMIT),
        cost_estimate=pl.CostEstimate(
            flops=8 * count * half * CH * heads * HD,
            bytes_accessed=4 * count * half * heads * HD,
            transcendentals=0,
        ),
    )(grad, scale, proj)


def weight_kernel(grad_ref, mod_ref, out_ref):
    out_ref[...] = readout_grad(grad_ref[...], mod_ref)


def weight_call(grad, modulated):
    vmem = pl.BlockSpec(memory_space=pltpu.VMEM)
    return pl.pallas_call(
        weight_kernel,
        out_shape=jax.ShapeDtypeStruct((CH, modulated.shape[2]), F32),
        in_specs=[vmem] * 2,
        out_specs=vmem,
        compiler_params=pltpu.CompilerParams(vmem_limit_bytes=VMEM_LIMIT),
    )(grad, modulated)


def finish_kernel(masks, width, place_ref, *refs):
    group = place_ref[2]
    out_ref = refs[-1]
    for ref, some in zip(refs[:-1], masks):
        for slot, mask in enumerate(some):
            first = pl.multiple_of(jnp.bitwise_xor(group, mask) * width, width)
            out_ref[pl.ds(first, width), :] = ref[slot].astype(F32).T


def finish(place, parts, width):
    vmem = pl.BlockSpec(memory_space=pltpu.VMEM)
    return pl.pallas_call(
        functools.partial(finish_kernel, [masks for _, masks in parts], width),
        out_shape=jax.ShapeDtypeStruct((HEADS * HD, CH), F32),
        in_specs=[pl.BlockSpec(memory_space=pltpu.SMEM)] + [vmem] * len(parts),
        out_specs=vmem,
        compiler_params=pltpu.CompilerParams(vmem_limit_bytes=VMEM_LIMIT),
    )(place, *[x for x, _ in parts])


def swap(x, axis, mask):
    count = lax.axis_size(axis)
    return lax.ppermute(x, axis, [(i, i ^ mask) for i in range(count)])


def stages_of(count):
    bits = [1 << b for b in range(1, count.bit_length() - 1)]
    pairs = [bits[i : i + 2] for i in range(0, len(bits), 2)]
    return [[p[0], p[1], p[0] | p[1]] if len(p) == 2 else p for p in pairs]


def gather_relative(x, axis, unit, count):
    held, masks = x[None], [0]
    for stage in stages_of(count):
        held = jnp.concatenate([held] + [swap(held, axis, unit * m) for m in stage], axis=0)
        masks = masks + [m ^ other for m in stage for other in masks]
    return [(held, masks), (swap(held, axis, unit), [m ^ 1 for m in masks])]


def scatter_relative(keep, send, axis, unit, count, inner):
    got = swap(send, axis, unit)
    stages = stages_of(count)
    shape = keep.shape[1:]
    for stage in stages:
        ways = len(stage) + 1
        if inner > 1:
            keep = keep.reshape((-1, inner * shape[0]) + shape[1:])
            got = got.reshape(keep.shape)
        parts = add_split(keep, got, ways)
        got = [swap(parts[way], axis, unit * mask) for way, mask in enumerate(stage, 1)]
        got = sum(part.astype(F32) for part in got)
        keep = parts[0]
        if stage is not stages[-1]:
            got = got.astype(BF16)
    total = (keep.astype(F32) + got.astype(F32)).astype(BF16)
    return total.reshape((inner,) + shape)


def gather_doubling(x, axis):
    count = lax.axis_size(axis)
    held, masks = x[None], [0]
    bit = count >> 1
    while bit:
        held = jnp.concatenate([held, swap(held, axis, bit)], axis=0)
        masks = masks + [m ^ bit for m in masks]
        bit >>= 1
    where = [masks.index(m) for m in range(count)]
    return held[jnp.asarray(where)[jnp.arange(count) ^ lax.axis_index(axis)]]


def sum_direct(x, axis):
    count = lax.axis_size(axis)
    parts = [x] + [swap(x, axis, k) for k in range(1, count)]
    parts = [part.astype(F32) for part in parts]
    while len(parts) > 1:
        parts = [parts[i] + parts[i + 1] for i in range(0, len(parts), 2)]
    return parts[0]


def gather_embed(patch_embed):
    seq_count = lax.axis_size("seq")
    data_count = lax.axis_size("dp")
    positions, local, width = patch_embed.shape
    share = positions // data_count if positions % data_count == 0 else 0
    if share:
        mine = lax.dynamic_slice_in_dim(patch_embed, lax.axis_index("dp") * share, share, 0)
    else:
        mine = patch_embed
    gathered = gather_doubling(mine, "seq")
    full = gathered.transpose(1, 0, 2, 3).reshape(-1, width)
    if not share:
        return [(full, 0)]
    held = [(full, 0)]
    bit = data_count >> 1
    while bit:
        held = held + [(swap(x, "dp", bit), m ^ bit) for x, m in held]
        bit >>= 1
    return held


def on_device(
    queries,
    keys,
    values,
    shifts,
    scales,
    proj_out,
    patch_embed,
    pos_embed,
    pre_gain,
    post_gain,
    prompt,
    cotangent,
):
    seq_count = lax.axis_size("seq")
    data_count = lax.axis_size("dp")
    tok_rows = queries.shape[1]
    query_parts = max(1, seq_count // HEADS)
    head_count = max(1, HEADS // seq_count)
    group_count = HEADS // head_count
    width = head_count * HD
    seq_index = lax.axis_index("seq")
    head_group = seq_index // query_parts
    query_part = seq_index % query_parts
    part_rows = tok_rows // query_parts
    half = part_rows // 2
    lat_rows = seq_count * tok_rows
    grid_rows = lat_rows // GW
    canonical = part_rows == 2 * GW
    place = jnp.stack([seq_index, lax.axis_index("dp"), head_group]).astype(jnp.int32)

    scale_mine = lax.dynamic_slice_in_dim(scales, head_group * width, width, 1)
    shift_mine = lax.dynamic_slice_in_dim(shifts, head_group * width, width, 1)
    proj_mine = lax.dynamic_slice_in_dim(proj_out, head_group * width, width, 0)

    send = pack(place, queries, keys, values, seq_count, query_parts, part_rows, tok_rows, width)
    received = {0: send[0]}
    for mask in reversed(range(1, seq_count)):
        received[mask] = swap(send[mask], "seq", mask)
    received = [received[mask] for mask in range(seq_count)]
    embed = gather_embed(patch_embed)

    modulated, keep, away = attend(
        received, scale_mine, shift_mine, proj_mine, query_parts, part_rows, tok_rows, head_count
    )

    summed = scatter_relative(keep, away, "seq", query_parts, group_count, query_parts)
    if canonical:
        latent = gather_relative(summed[0], "seq", 1, seq_count)
    else:
        blocks = gather_doubling(summed, "seq").reshape(
            group_count, query_parts, query_parts, half, 2, CH
        )
        order = [[inner ^ part for inner in range(query_parts)] for part in range(query_parts)]
        blocks = jnp.stack([blocks[:, part][:, jnp.asarray(order[part])] for part in range(query_parts)], axis=2)
        blocks = blocks.transpose(0, 1, 2, 4, 3, 5).reshape(grid_rows // 2, 2, GW, CH)
        blocks = blocks.transpose(0, 2, 1, 3).reshape(grid_rows // 2, GW, 2 * CH)
        latent = [(blocks, list(range(grid_rows // 2)))]

    reward, grad, weight = reward_head(
        place if canonical else place * jnp.asarray([0, 1, 1], jnp.int32),
        latent, embed, pos_embed, pre_gain[None], post_gain[None], prompt,
        cotangent[None], modulated, grid_rows, canonical,
    )
    if not canonical:
        tokens = grad.reshape(grid_rows // 2, GW, 2, CH).transpose(0, 2, 1, 3)
        tokens = tokens.reshape(seq_count, query_parts, 2, half, CH)
        tokens = lax.dynamic_index_in_dim(tokens, query_part, 1, keepdims=False)
        tokens = tokens.transpose(0, 2, 1, 3)
        grad = tokens.reshape(seq_count * half, 2 * CH)
        relative = tokens[jnp.arange(seq_count) ^ seq_index].reshape(seq_count * half, 2 * CH)
        weight = weight_call(relative, modulated)

    total = sum_direct((weight * (1.0 / math.sqrt(data_count * lat_rows))).astype(BF16), "dp")
    attn_grad = spread(grad, scale_mine, proj_mine, seq_count, half, head_count)
    for part in range(1, query_parts):
        total = total + swap(total, "seq", part)
    parts = gather_relative(total.astype(BF16), "seq", query_parts, group_count)
    proj_grad = finish(place, parts, width)
    return (reward[0, :1], attn_grad, proj_grad)


def solution(mesh):
    return jax.shard_map(
        on_device,
        mesh=mesh,
        in_specs=(
            P("dp", "seq", None),
            P("dp", "seq", None),
            P("dp", "seq", None),
            P("dp", None),
            P("dp", None),
            P(),
            P(None, "seq", None),
            P(),
            P(),
            P(),
            P("dp", None),
            P("dp"),
        ),
        out_specs=(P("dp"), P("dp", "seq", None, None), P()),
        check_vma=False,
    )
```

time: 185 us -> 134 us (0.72)
  Pallas kernels: 61.7 us -> 16.4 us
  other arithmetic: 10.3 us -> 1.01 us
  waiting for transfers between devices: 54.7 us -> 45.9 us
  starting transfers between devices: 43.2 us -> 50.2 us
  local copies, waits for them, and re-layouts: 13.2 us -> 18.6 us
    pallas_call x3 -> x5, Pallas kernels: 60.4 us -> 15.1 us  [the longest x1 7.1 us: attend(): pl.pallas_call(functools.partial(attend_kernel, count, query_parts, part_...]
    all_to_all x2 -> x0, waiting for transfers between devices: 31 us -> none  [the longest x1 25.6 us: on_device(): lax.all_to_all(send, 'seq', split_axis=0, concat_axis=0, tiled=True)]
    ppermute x22 -> x28, waiting for transfers between devices: 23.7 us -> 45.9 us  [swap(): return lax.ppermute(x, axis, [(i, i ^ mask) for i in range(count)])]
    ppermute x22 -> x28, starting transfers between devices: 32.3 us -> 50.2 us  [swap(): return lax.ppermute(x, axis, [(i, i ^ mask) for i in range(count)])]
    all_to_all x2 -> x0, starting transfers between devices: 11 us -> none  [the longest x1 7.54 us: on_device(): lax.all_to_all(send, 'seq', split_axis=0, concat_axis=0, tiled=True)]
    unnamed x36 -> x48, local copies, waits for them, and re-layouts: 6.9 us -> 14.6 us
    select_n x6 -> x2, other arithmetic: 5.64 us -> 0.01 us  [gather_doubling(): return held[jnp.asarray(where)[jnp.arange(count) ^ lax.axis_index(axis)]]]
    concatenate x5, other arithmetic: 3.39 us -> 0.15 us  [the longest x3 0.12 us: gather_doubling(): held = jnp.concatenate([held, swap(held, axis, bit)], axis=0)]
  transfers between devices with their start and end apart: 24 -> 28, of which waited for: 10 -> 15; matrix products, arithmetic and copies ran while one was open for 8% -> 4% of each run, Pallas kernels for 27% -> 9%
where the time goes in v2:
time: 134 us
  starting transfers between devices  50.2 us (37%)
  waiting for transfers between devices  45.9 us (34%)
  local copies, waits for them, and re-layouts  18.6 us (14%)
  Pallas kernels  16.4 us (12%)
  between operations  1.52 us (1%)
    ppermute x28, starting transfers between devices, swap(): return lax.ppermute(x, axis, [(i, i ^ mask) for i in range(count)])  50.2 us
    ppermute x28, waiting for transfers between devices, swap(): return lax.ppermute(x, axis, [(i, i ^ mask) for i in range(count)])  45.9 us
    unnamed x48, local copies, waits for them, and re-layouts  14.6 us
    pallas_call x1, Pallas kernels, attend(): pl.pallas_call(functools.partial(attend_kernel, count, query_parts, part_...  7.1 us
    pallas_call x1, Pallas kernels, reward_head(): pl.pallas_call(functools.partial(head_kernel, grid_rows, fused, lat_masks...  4.22 us
  transfers between devices with their start and end apart: 28, of which 15 were waited for; matrix products, arithmetic and copies ran while one was open for 4% of the time, Pallas kernels for 9%

profile of v2, /device:TPU:0, one launch (start us, length us, event | category | flops | bytes accessed | tf_op | source)
XLA Modules:
  0.0 133.7 jit_solution(7821454215089221624)
XLA Ops:
  1.6 4.0 %collective-permute-start.15 = (bf16[1,4,8,1280]{3,2,1,0:T(8,128)(2,1)S(1)}, bf16[1,4,8,1280]{3,2,1,0:T(8,128)(2,1)S(1)}, u32[]{:S(2)}, u32[]{:S(2)}) collective-permute-start(bf16[1,4,8,1280]{3,2,1,0:T(8,128)(2,1)S(1)} %dynamic-slice_bitcast_fusion), channel_id=1, source_target_pairs={{0,16},{4,20},{8,24},{12,28},{16,0},{20,4},{24,8},{28,12},{1,17},{... | collective-permute-start | bytes 245768 | tf_op jit(solution)/shard_map/ppermute | solution.py:352
  5.7 4.2 %collective-permute-done.15 = bf16[1,4,8,1280]{3,2,1,0:T(8,128)(2,1)S(1)} collective-permute-done((bf16[1,4,8,1280]{3,2,1,0:T(8,128)(2,1)S(1)}, bf16[1,4,8,1280]{3,2,1,0:T(8,128)(2,1)S(1)}, u32[]{:S(2)}, u32[]{:S(2)}) %collective-permute-start.15) | collective-permute-done | bytes 81952 | tf_op jit(solution)/shard_map/ppermute | solution.py:352
  12.0 3.3 %collective-permute-done.16 = bf16[2,4,8,1280]{3,2,1,0:T(8,128)(2,1)S(1)} collective-permute-done((bf16[2,4,8,1280]{3,2,1,0:T(8,128)(2,1)S(1)}, bf16[2,4,8,1280]{3,2,1,0:T(8,128)(2,1)S(1)}, u32[]{:S(2)}, u32[]{:S(2)}) %collective-permute-start.16) | collective-permute-done | bytes 163872 | tf_op jit(solution)/shard_map/ppermute | solution.py:352
  17.1 5.8 %collective-permute-done.17 = bf16[4,4,8,1280]{3,2,1,0:T(8,128)(2,1)S(1)} collective-permute-done((bf16[4,4,8,1280]{3,2,1,0:T(8,128)(2,1)S(1)}, bf16[4,4,8,1280]{3,2,1,0:T(8,128)(2,1)S(1)}, u32[]{:S(2)}, u32[]{:S(2)}) %collective-permute-start.17) | collective-permute-done | bytes 327712 | tf_op jit(solution)/shard_map/ppermute | solution.py:352
  29.0 2.5 %collective-permute-start.1 = (bf16[384,256]{1,0:T(8,128)(2,1)S(1)}, bf16[384,256]{1,0:T(8,128)(2,1)S(1)}, u32[]{:S(2)}, u32[]{:S(2)}) collective-permute-start(bf16[384,256]{1,0:T(8,128)(2,1)S(1)} %get-tuple-element.23), channel_id=1, source_target_pairs={{0,8},{4,12},{8,0},{12,4},{16,24},{20,28},{24,16},{28,20},{1,9},{5... | collective-permute-start | bytes 589832 | tf_op jit(solution)/shard_map/ppermute | solution.py:352
  31.4 3.9 %collective-permute-start.3 = (bf16[384,256]{1,0:T(8,128)(2,1)S(1)}, bf16[384,256]{1,0:T(8,128)(2,1)S(1)}, u32[]{:S(2)}, u32[]{:S(2)}) collective-permute-start(bf16[384,256]{1,0:T(8,128)(2,1)S(1)} %get-tuple-element.25), channel_id=1, source_target_pairs={{0,16},{4,20},{8,24},{12,28},{16,0},{20,4},{24,8},{28,12},{1,17},{... | collective-permute-start | bytes 589832 | tf_op jit(solution)/shard_map/ppermute | solution.py:352
  37.4 3.9 %collective-permute-start.4 = (bf16[384,256]{1,0:T(8,128)(2,1)}, bf16[384,256]{1,0:T(8,128)(2,1)}, u32[]{:S(2)}, u32[]{:S(2)}) collective-permute-start(bf16[384,256]{1,0:T(8,128)(2,1)} %get-tuple-element.26), channel_id=1, source_target_pairs={{0,20},{4,16},{8,28},{12,24},{16,4},{20,0},{24,12},{28,8},{1,21},{... | collective-permute-start | bytes 589832 | tf_op jit(solution)/shard_map/ppermute | solution.py:352
  42.0 3.6 %collective-permute-start.5 = (bf16[384,256]{1,0:T(8,128)(2,1)}, bf16[384,256]{1,0:T(8,128)(2,1)}, u32[]{:S(2)}, u32[]{:S(2)}) collective-permute-start(bf16[384,256]{1,0:T(8,128)(2,1)} %get-tuple-element.27), channel_id=1, source_target_pairs={{0,24},{4,28},{8,16},{12,20},{16,8},{20,12},{24,0},{28,4},{1,25},{... | collective-permute-start | bytes 589832 | tf_op jit(solution)/shard_map/ppermute | solution.py:352
  46.3 3.1 %collective-permute-start.6 = (bf16[384,256]{1,0:T(8,128)(2,1)S(1)}, bf16[384,256]{1,0:T(8,128)(2,1)S(1)}, u32[]{:S(2)}, u32[]{:S(2)}) collective-permute-start(bf16[384,256]{1,0:T(8,128)(2,1)S(1)} %get-tuple-element.28), channel_id=1, source_target_pairs={{0,28},{4,24},{8,20},{12,16},{16,12},{20,8},{24,4},{28,0},{1,29},{... | collective-permute-start | bytes 589832 | tf_op jit(solution)/shard_map/ppermute | solution.py:352
  52.8 9.5 %collective-permute-done.4.refs_5_ = bf16[384,256]{1,0:T(8,128)(2,1)} collective-permute-done((bf16[384,256]{1,0:T(8,128)(2,1)}, bf16[384,256]{1,0:T(8,128)(2,1)}, u32[]{:S(2)}, u32[]{:S(2)}) %collective-permute-start.4) | collective-permute-done | bytes 196640 | tf_op jit(solution)/shard_map/ppermute | solution.py:352
  68.6 7.1 %shard_map.149 = (bf16[8,128,256]{2,1,0:T(8,128)(2,1)S(1)}, bf16[4,64,128]{2,1,0:T(8,128)(2,1)S(1)}, bf16[4,64,128]{2,1,0:T(8,128)(2,1)S(1)}) custom-call(bf16[384,256]{1,0:T(8,128)(2,1)S(1)} %copy-done.8, bf16[384,256]{1,0:T(8,128)(2,1)S(1)} %copy-done.10, bf16[384,256]{1,0:T(8,128)(2,1)S(1)} %copy-done.12, bf16[384,256]{1,0:T(8,128)(2,1)S(1)} %copy-done.14, ...), custom_call_target="tpu_custom_call" | custom-call | flops 1073741824 | bytes 2097152 | tf_op jit(solution)/shard_map/pallas_call | solution.py:109
  77.5 3.1 %collective-permute-done.7.got_ref = bf16[4,64,128]{2,1,0:T(8,128)(2,1)S(1)} collective-permute-done((bf16[4,64,128]{2,1,0:T(8,128)(2,1)S(1)}, bf16[4,64,128]{2,1,0:T(8,128)(2,1)S(1)}, u32[]{:S(2)}, u32[]{:S(2)}) %collective-permute-start.7) | collective-permute-done | bytes 65568 | tf_op jit(solution)/shard_map/ppermute | solution.py:352
  82.7 3.1 %collective-permute-start.10 = (bf16[1,64,128]{2,1,0:T(8,128)(2,1)}, bf16[1,64,128]{2,1,0:T(8,128)(2,1)S(1)}, u32[]{:S(2)}, u32[]{:S(2)}) collective-permute-start(bf16[1,64,128]{2,1,0:T(8,128)(2,1)} %get-tuple-element.34), channel_id=1, source_target_pairs={{0,24},{4,28},{8,16},{12,20},{16,8},{20,12},{24,0},{28,4},{1,25},{... | collective-permute-start | bytes 49160 | tf_op jit(solution)/shard_map/ppermute | solution.py:352
  85.8 5.6 %collective-permute-start.8 = (bf16[1,64,128]{2,1,0:T(8,128)(2,1)}, bf16[1,64,128]{2,1,0:T(8,128)(2,1)S(1)}, u32[]{:S(2)}, u32[]{:S(2)}) collective-permute-start(bf16[1,64,128]{2,1,0:T(8,128)(2,1)} %get-tuple-element.32), channel_id=1, source_target_pairs={{0,8},{4,12},{8,0},{12,4},{16,24},{20,28},{24,16},{28,20},{1,9},{5... | collective-permute-start | bytes 49160 | tf_op jit(solution)/shard_map/ppermute | solution.py:352
  93.3 2.9 %collective-permute-done.9 = bf16[1,64,128]{2,1,0:T(8,128)(2,1)S(1)} collective-permute-done((bf16[1,64,128]{2,1,0:T(8,128)(2,1)}, bf16[1,64,128]{2,1,0:T(8,128)(2,1)S(1)}, u32[]{:S(2)}, u32[]{:S(2)}) %collective-permute-start.9) | collective-permute-done | bytes 16416 | tf_op jit(solution)/shard_map/ppermute | solution.py:352
  97.0 2.5 %collective-permute-start.12 = (bf16[1,64,128]{2,1,0:T(8,128)(2,1)S(1)}, bf16[1,64,128]{2,1,0:T(8,128)(2,1)S(1)}, u32[]{:S(2)}, u32[]{:S(2)}) collective-permute-start(bf16[1,64,128]{2,1,0:T(8,128)(2,1)S(1)} %add_convert_fusion.1), channel_id=1, source_target_pairs={{0,16},{4,20},{8,24},{12,28},{16,0},{20,4},{24,8},{28,12},{1,17},{... | collective-permute-start | bytes 49160 | tf_op jit(solution)/shard_map/ppermute | solution.py:352
  99.6 1.9 %collective-permute-start.13 = (bf16[1,64,128]{2,1,0:T(8,128)(2,1)S(1)}, bf16[1,64,128]{2,1,0:T(8,128)(2,1)S(1)}, u32[]{:S(2)}, u32[]{:S(2)}) collective-permute-start(bf16[1,64,128]{2,1,0:T(8,128)(2,1)S(1)} %add_convert_fusion.1), channel_id=1, source_target_pairs={{0,24},{4,28},{8,16},{12,20},{16,8},{20,12},{24,0},{28,4},{1,25},{... | collective-permute-start | bytes 49160 | tf_op jit(solution)/shard_map/ppermute | solution.py:352
  101.7 3.3 %collective-permute-done.13 = bf16[1,64,128]{2,1,0:T(8,128)(2,1)S(1)} collective-permute-done((bf16[1,64,128]{2,1,0:T(8,128)(2,1)S(1)}, bf16[1,64,128]{2,1,0:T(8,128)(2,1)S(1)}, u32[]{:S(2)}, u32[]{:S(2)}) %collective-permute-start.13) | collective-permute-done | bytes 16416 | tf_op jit(solution)/shard_map/ppermute | solution.py:352
  106.5 3.0 %collective-permute-done.14.refs_1_ = bf16[4,64,128]{2,1,0:T(8,128)(2,1)S(1)} collective-permute-done((bf16[4,64,128]{2,1,0:T(8,128)(2,1)S(1)}, bf16[4,64,128]{2,1,0:T(8,128)(2,1)S(1)}, u32[]{:S(2)}, u32[]{:S(2)}) %collective-permute-start.14) | collective-permute-done | bytes 65568 | tf_op jit(solution)/shard_map/ppermute | solution.py:352
  109.5 4.2 %shard_map.151 = (f32[1,128]{1,0:T(1,128)}, bf16[512,128]{1,0:T(8,128)(2,1)S(1)}, f32[64,256]{1,0:T(8,128)S(1)}) custom-call(s32[3]{0:T(128)S(1)} %pad_add_fusion.place_ref, bf16[4,64,128]{2,1,0:T(8,128)(2,1)S(1)} %pad_maximum_fusion.4.refs_0_, bf16[4,64,128]{2,1,0:T(8,128)(2,1)S(1)} %collective-permute-done.14.refs_1_, bf16[256,1280]{1,0:T(8,128)(2,1)S(1)} %bitcast.20, ...), custom_call_target="tpu_custom_call" | custom-call | flops 503316480 | bytes 2785280 | tf_op jit(solution)/shard_map/pallas_call | solution.py:257
  115.7 2.1 %collective-permute-done.22 = bf16[64,256]{1,0:T(8,128)(2,1)S(1)} collective-permute-done((bf16[64,256]{1,0:T(8,128)(2,1)S(1)}, bf16[64,256]{1,0:T(8,128)(2,1)S(1)}, u32[]{:S(2)}, u32[]{:S(2)}) %collective-permute-start.22) | collective-permute-done | bytes 32800 | tf_op jit(solution)/shard_map/ppermute | solution.py:352
  118.4 2.7 %collective-permute-start.25 = (bf16[1,64,256]{2,1,0:T(8,128)(2,1)S(1)}, bf16[1,64,256]{2,1,0:T(8,128)(2,1)S(1)}, u32[]{:S(2)}, u32[]{:S(2)}) collective-permute-start(bf16[1,64,256]{2,1,0:T(8,128)(2,1)S(1)} %fusion), channel_id=1, source_target_pairs={{0,16},{4,20},{8,24},{12,28},{16,0},{20,4},{24,8},{28,12},{1,17},{... | collective-permute-start | bytes 98312 | tf_op jit(solution)/shard_map/ppermute | solution.py:352
  123.8 2.9 %collective-permute-done.26 = bf16[1,64,256]{2,1,0:T(8,128)(2,1)S(1)} collective-permute-done((bf16[1,64,256]{2,1,0:T(8,128)(2,1)S(1)}, bf16[1,64,256]{2,1,0:T(8,128)(2,1)S(1)}, u32[]{:S(2)}, u32[]{:S(2)}) %collective-permute-start.26) | collective-permute-done | bytes 32800 | tf_op jit(solution)/shard_map/ppermute | solution.py:352
  129.4 2.4 %collective-permute-done.27.refs_1_ = bf16[4,64,256]{2,1,0:T(8,128)(2,1)S(1)} collective-permute-done((bf16[4,64,256]{2,1,0:T(8,128)(2,1)S(1)}, bf16[4,64,256]{2,1,0:T(8,128)(2,1)S(1)}, u32[]{:S(2)}, u32[]{:S(2)}) %collective-permute-start.27) | collective-permute-done | bytes 131104 | tf_op jit(solution)/shard_map/ppermute | solution.py:352
  (108 shorter events, 41.6 us)
Async XLA Ops:
  1.6 8.2 %collective-permute-start.15 = (bf16[1,4,8,1280]{3,2,1,0:T(8,128)(2,1)S(1)}, bf16[1,4,8,1280]{3,2,1,0:T(8,128)(2,1)S(1)}, u32[]{:S(2)}, u32[]{:S(2)}) collective-permute-start(bf16[1,4,8,1280]{3,2,1,0:T(8,128)(2,1)S(1)} %dynamic-slice_bitcast_fusion), channel_id=1, source_target_pairs={{0,16},{4,20},{8,24},{12,28},{16,0},{20,4},{24,8},{28,12},{1,17},{... | collective-permute-start | bytes 245768 | tf_op jit(solution)/shard_map/ppermute | solution.py:352
  9.9 5.4 %collective-permute-start.16 = (bf16[2,4,8,1280]{3,2,1,0:T(8,128)(2,1)S(1)}, bf16[2,4,8,1280]{3,2,1,0:T(8,128)(2,1)S(1)}, u32[]{:S(2)}, u32[]{:S(2)}) collective-permute-start(bf16[2,4,8,1280]{3,2,1,0:T(8,128)(2,1)S(1)} %pad_maximum_fusion.2), channel_id=1, source_target_pairs={{0,8},{4,12},{8,0},{12,4},{16,24},{20,28},{24,16},{28,20},{1,9},{5... | collective-permute-start | bytes 491528 | tf_op jit(solution)/shard_map/ppermute | solution.py:352
  15.3 7.6 %collective-permute-start.17 = (bf16[4,4,8,1280]{3,2,1,0:T(8,128)(2,1)S(1)}, bf16[4,4,8,1280]{3,2,1,0:T(8,128)(2,1)S(1)}, u32[]{:S(2)}, u32[]{:S(2)}) collective-permute-start(bf16[4,4,8,1280]{3,2,1,0:T(8,128)(2,1)S(1)} %pad_maximum_fusion.1), channel_id=1, source_target_pairs={{0,4},{4,0},{8,12},{12,8},{16,20},{20,16},{24,28},{28,24},{1,5},{5... | collective-permute-start | bytes 983048 | tf_op jit(solution)/shard_map/ppermute | solution.py:352
  23.6 27.1 %collective-permute-start.18 = (bf16[256,1280]{1,0:T(8,128)(2,1)S(1)}, bf16[256,1280]{1,0:T(8,128)(2,1)S(1)}, u32[]{:S(2)}, u32[]{:S(2)}) collective-permute-start(bf16[256,1280]{1,0:T(8,128)(2,1)S(1)} %bitcast.18), channel_id=1, source_target_pairs={{0,2},{1,3},{2,0},{3,1},{4,6},{5,7},{6,4},{7,5},{8,10},{9,11},{10,... | collective-permute-start | bytes 1966088 | tf_op jit(solution)/shard_map/ppermute | solution.py:352
  27.4 9.3 %collective-permute-start = (bf16[384,256]{1,0:T(8,128)(2,1)S(1)}, bf16[384,256]{1,0:T(8,128)(2,1)S(1)}, u32[]{:S(2)}, u32[]{:S(2)}) collective-permute-start(bf16[384,256]{1,0:T(8,128)(2,1)S(1)} %get-tuple-element.22), channel_id=1, source_target_pairs={{0,4},{4,0},{8,12},{12,8},{16,20},{20,16},{24,28},{28,24},{1,5},{5... | collective-permute-start | bytes 589832 | tf_op jit(solution)/shard_map/ppermute | solution.py:352
  29.0 12.3 %collective-permute-start.1 = (bf16[384,256]{1,0:T(8,128)(2,1)S(1)}, bf16[384,256]{1,0:T(8,128)(2,1)S(1)}, u32[]{:S(2)}, u32[]{:S(2)}) collective-permute-start(bf16[384,256]{1,0:T(8,128)(2,1)S(1)} %get-tuple-element.23), channel_id=1, source_target_pairs={{0,8},{4,12},{8,0},{12,4},{16,24},{20,28},{24,16},{28,20},{1,9},{5... | collective-permute-start | bytes 589832 | tf_op jit(solution)/shard_map/ppermute | solution.py:352
  31.4 14.1 %collective-permute-start.2 = (bf16[384,256]{1,0:T(8,128)(2,1)S(1)}, bf16[384,256]{1,0:T(8,128)(2,1)S(1)}, u32[]{:S(2)}, u32[]{:S(2)}) collective-permute-start(bf16[384,256]{1,0:T(8,128)(2,1)S(1)} %get-tuple-element.24), channel_id=1, source_target_pairs={{0,12},{4,8},{8,4},{12,0},{16,28},{20,24},{24,20},{28,16},{1,13},{... | collective-permute-start | bytes 589832 | tf_op jit(solution)/shard_map/ppermute | solution.py:352
  31.4 18.6 %collective-permute-start.3 = (bf16[384,256]{1,0:T(8,128)(2,1)S(1)}, bf16[384,256]{1,0:T(8,128)(2,1)S(1)}, u32[]{:S(2)}, u32[]{:S(2)}) collective-permute-start(bf16[384,256]{1,0:T(8,128)(2,1)S(1)} %get-tuple-element.25), channel_id=1, source_target_pairs={{0,16},{4,20},{8,24},{12,28},{16,0},{20,4},{24,8},{28,12},{1,17},{... | collective-permute-start | bytes 589832 | tf_op jit(solution)/shard_map/ppermute | solution.py:352
  37.4 24.9 %collective-permute-start.4 = (bf16[384,256]{1,0:T(8,128)(2,1)}, bf16[384,256]{1,0:T(8,128)(2,1)}, u32[]{:S(2)}, u32[]{:S(2)}) collective-permute-start(bf16[384,256]{1,0:T(8,128)(2,1)} %get-tuple-element.26), channel_id=1, source_target_pairs={{0,20},{4,16},{8,28},{12,24},{16,4},{20,0},{24,12},{28,8},{1,21},{... | collective-permute-start | bytes 589832 | tf_op jit(solution)/shard_map/ppermute | solution.py:352
  42.0 20.4 %collective-permute-start.5 = (bf16[384,256]{1,0:T(8,128)(2,1)}, bf16[384,256]{1,0:T(8,128)(2,1)}, u32[]{:S(2)}, u32[]{:S(2)}) collective-permute-start(bf16[384,256]{1,0:T(8,128)(2,1)} %get-tuple-element.27), channel_id=1, source_target_pairs={{0,24},{4,28},{8,16},{12,20},{16,8},{20,12},{24,0},{28,4},{1,25},{... | collective-permute-start | bytes 589832 | tf_op jit(solution)/shard_map/ppermute | solution.py:352
  46.3 16.1 %collective-permute-start.6 = (bf16[384,256]{1,0:T(8,128)(2,1)S(1)}, bf16[384,256]{1,0:T(8,128)(2,1)S(1)}, u32[]{:S(2)}, u32[]{:S(2)}) collective-permute-start(bf16[384,256]{1,0:T(8,128)(2,1)S(1)} %get-tuple-element.28), channel_id=1, source_target_pairs={{0,28},{4,24},{8,20},{12,16},{16,12},{20,8},{24,4},{28,0},{1,29},{... | collective-permute-start | bytes 589832 | tf_op jit(solution)/shard_map/ppermute | solution.py:352
  50.7 58.7 %collective-permute-start.19 = (bf16[256,1280]{1,0:T(8,128)(2,1)S(1)}, bf16[256,1280]{1,0:T(8,128)(2,1)S(1)}, u32[]{:S(2)}, u32[]{:S(2)}) collective-permute-start(bf16[256,1280]{1,0:T(8,128)(2,1)S(1)} %bitcast.19), channel_id=1, source_target_pairs={{0,1},{1,0},{2,3},{3,2},{4,5},{5,4},{6,7},{7,6},{8,9},{9,8},{10,11... | collective-permute-start | bytes 1966088 | tf_op jit(solution)/shard_map/ppermute | solution.py:352
  50.7 58.7 %collective-permute-start.20 = (bf16[256,1280]{1,0:T(8,128)(2,1)S(1)}, bf16[256,1280]{1,0:T(8,128)(2,1)S(1)}, u32[]{:S(2)}, u32[]{:S(2)}) collective-permute-start(bf16[256,1280]{1,0:T(8,128)(2,1)S(1)} %collective-permute-done.18.refs_3_), channel_id=1, source_target_pairs={{0,1},{1,0},{2,3},{3,2},{4,5},{5,4},{6,7},{7,6},{8,9},{9,8},{10,11... | collective-permute-start | bytes 1966088 | tf_op jit(solution)/shard_map/ppermute | solution.py:352
  82.7 9.2 %collective-permute-start.10 = (bf16[1,64,128]{2,1,0:T(8,128)(2,1)}, bf16[1,64,128]{2,1,0:T(8,128)(2,1)S(1)}, u32[]{:S(2)}, u32[]{:S(2)}) collective-permute-start(bf16[1,64,128]{2,1,0:T(8,128)(2,1)} %get-tuple-element.34), channel_id=1, source_target_pairs={{0,24},{4,28},{8,16},{12,20},{16,8},{20,12},{24,0},{28,4},{1,25},{... | collective-permute-start | bytes 49160 | tf_op jit(solution)/shard_map/ppermute | solution.py:352
  85.8 7.5 %collective-permute-start.8 = (bf16[1,64,128]{2,1,0:T(8,128)(2,1)}, bf16[1,64,128]{2,1,0:T(8,128)(2,1)S(1)}, u32[]{:S(2)}, u32[]{:S(2)}) collective-permute-start(bf16[1,64,128]{2,1,0:T(8,128)(2,1)} %get-tuple-element.32), channel_id=1, source_target_pairs={{0,8},{4,12},{8,0},{12,4},{16,24},{20,28},{24,16},{28,20},{1,9},{5... | collective-permute-start | bytes 49160 | tf_op jit(solution)/shard_map/ppermute | solution.py:352
  91.4 4.8 %collective-permute-start.9 = (bf16[1,64,128]{2,1,0:T(8,128)(2,1)}, bf16[1,64,128]{2,1,0:T(8,128)(2,1)S(1)}, u32[]{:S(2)}, u32[]{:S(2)}) collective-permute-start(bf16[1,64,128]{2,1,0:T(8,128)(2,1)} %get-tuple-element.33), channel_id=1, source_target_pairs={{0,16},{4,20},{8,24},{12,28},{16,0},{20,4},{24,8},{28,12},{1,17},{... | collective-permute-start | bytes 49160 | tf_op jit(solution)/shard_map/ppermute | solution.py:352
  97.0 4.5 %collective-permute-start.11 = (bf16[1,64,128]{2,1,0:T(8,128)(2,1)S(1)}, bf16[1,64,128]{2,1,0:T(8,128)(2,1)S(1)}, u32[]{:S(2)}, u32[]{:S(2)}) collective-permute-start(bf16[1,64,128]{2,1,0:T(8,128)(2,1)S(1)} %add_convert_fusion.1), channel_id=1, source_target_pairs={{0,8},{4,12},{8,0},{12,4},{16,24},{20,28},{24,16},{28,20},{1,9},{5... | collective-permute-start | bytes 49160 | tf_op jit(solution)/shard_map/ppermute | solution.py:352
  97.0 4.7 %collective-permute-start.12 = (bf16[1,64,128]{2,1,0:T(8,128)(2,1)S(1)}, bf16[1,64,128]{2,1,0:T(8,128)(2,1)S(1)}, u32[]{:S(2)}, u32[]{:S(2)}) collective-permute-start(bf16[1,64,128]{2,1,0:T(8,128)(2,1)S(1)} %add_convert_fusion.1), channel_id=1, source_target_pairs={{0,16},{4,20},{8,24},{12,28},{16,0},{20,4},{24,8},{28,12},{1,17},{... | collective-permute-start | bytes 49160 | tf_op jit(solution)/shard_map/ppermute | solution.py:352
  99.6 5.5 %collective-permute-start.13 = (bf16[1,64,128]{2,1,0:T(8,128)(2,1)S(1)}, bf16[1,64,128]{2,1,0:T(8,128)(2,1)S(1)}, u32[]{:S(2)}, u32[]{:S(2)}) collective-permute-start(bf16[1,64,128]{2,1,0:T(8,128)(2,1)S(1)} %add_convert_fusion.1), channel_id=1, source_target_pairs={{0,24},{4,28},{8,16},{12,20},{16,8},{20,12},{24,0},{28,4},{1,25},{... | collective-permute-start | bytes 49160 | tf_op jit(solution)/shard_map/ppermute | solution.py:352
  105.1 4.3 %collective-permute-start.14 = (bf16[4,64,128]{2,1,0:T(8,128)(2,1)S(1)}, bf16[4,64,128]{2,1,0:T(8,128)(2,1)S(1)}, u32[]{:S(2)}, u32[]{:S(2)}) collective-permute-start(bf16[4,64,128]{2,1,0:T(8,128)(2,1)S(1)} %pad_maximum_fusion.4.refs_0_), channel_id=1, source_target_pairs={{0,4},{4,0},{8,12},{12,8},{16,20},{20,16},{24,28},{28,24},{1,5},{5... | collective-permute-start | bytes 196616 | tf_op jit(solution)/shard_map/ppermute | solution.py:352
  118.3 4.5 %collective-permute-start.24 = (bf16[1,64,256]{2,1,0:T(8,128)(2,1)S(1)}, bf16[1,64,256]{2,1,0:T(8,128)(2,1)S(1)}, u32[]{:S(2)}, u32[]{:S(2)}) collective-permute-start(bf16[1,64,256]{2,1,0:T(8,128)(2,1)S(1)} %fusion), channel_id=1, source_target_pairs={{0,8},{4,12},{8,0},{12,4},{16,24},{20,28},{24,16},{28,20},{1,9},{5... | collective-permute-start | bytes 98312 | tf_op jit(solution)/shard_map/ppermute | solution.py:352
  118.4 5.5 %collective-permute-start.25 = (bf16[1,64,256]{2,1,0:T(8,128)(2,1)S(1)}, bf16[1,64,256]{2,1,0:T(8,128)(2,1)S(1)}, u32[]{:S(2)}, u32[]{:S(2)}) collective-permute-start(bf16[1,64,256]{2,1,0:T(8,128)(2,1)S(1)} %fusion), channel_id=1, source_target_pairs={{0,16},{4,20},{8,24},{12,28},{16,0},{20,4},{24,8},{28,12},{1,17},{... | collective-permute-start | bytes 98312 | tf_op jit(solution)/shard_map/ppermute | solution.py:352
  121.0 5.7 %collective-permute-start.26 = (bf16[1,64,256]{2,1,0:T(8,128)(2,1)S(1)}, bf16[1,64,256]{2,1,0:T(8,128)(2,1)S(1)}, u32[]{:S(2)}, u32[]{:S(2)}) collective-permute-start(bf16[1,64,256]{2,1,0:T(8,128)(2,1)S(1)} %fusion), channel_id=1, source_target_pairs={{0,24},{4,28},{8,16},{12,20},{16,8},{20,12},{24,0},{28,4},{1,25},{... | collective-permute-start | bytes 98312 | tf_op jit(solution)/shard_map/ppermute | solution.py:352
  126.8 5.0 %collective-permute-start.27 = (bf16[4,64,256]{2,1,0:T(8,128)(2,1)S(1)}, bf16[4,64,256]{2,1,0:T(8,128)(2,1)S(1)}, u32[]{:S(2)}, u32[]{:S(2)}) collective-permute-start(bf16[4,64,256]{2,1,0:T(8,128)(2,1)S(1)} %pad_maximum_fusion.3.refs_0_), channel_id=1, source_target_pairs={{0,4},{4,0},{8,12},{12,8},{16,20},{20,16},{24,28},{28,24},{1,5},{5... | collective-permute-start | bytes 393224 | tf_op jit(solution)/shard_map/ppermute | solution.py:352
  (27 other events, 71.7 us)

commit v3 on v2

v3 whole, which is shorter than its diff:
```python
import functools
import math

import jax
import jax.numpy as jnp
from jax import lax
from jax.experimental import pallas as pl
from jax.experimental.pallas import tpu as pltpu
from jax.sharding import PartitionSpec as P

HEADS = 16
HD = 128
CH = 64
GW = 64
VW = 1280
EPS = 1e-05
BF16 = jnp.bfloat16
F32 = jnp.float32
VMEM_LIMIT = 20 * 1024 * 1024


def mm(a, b):
    return jnp.dot(a, b, preferred_element_type=F32)


def mm_nt(a, b):
    return lax.dot_general(a, b, (((1,), (1,)), ((), ())), preferred_element_type=F32)


def mm_tn(a, b):
    return lax.dot_general(a, b, (((0,), (0,)), ((), ())), preferred_element_type=F32)


def pack_piece(sizes, me, mask, q_ref, k_ref, v_ref, out):
    query_parts, part_rows, tok_rows, width = sizes
    dest = jnp.bitwise_xor(me, mask)
    group, part = dest // query_parts, dest % query_parts
    cols = pl.ds(pl.multiple_of(group * width, HD), width)
    first = pl.multiple_of(part * part_rows, part_rows)
    out[pl.ds(0, part_rows), :] = q_ref[0, pl.ds(first, part_rows), cols]
    out[pl.ds(part_rows, tok_rows), :] = k_ref[0, :, cols]
    out[pl.ds(part_rows + tok_rows, tok_rows), :] = v_ref[0, :, cols]


def pack_kernel(sizes, masks, share, place_ref, q_ref, k_ref, v_ref, embed_ref, share_ref, *out_refs):
    me = place_ref[0]
    share_ref[...] = embed_ref[pl.ds(place_ref[1] * share, share)] if share else embed_ref[...]
    for mask, out in zip(masks, out_refs):
        pack_piece(sizes, me, mask, q_ref, k_ref, v_ref, out)


def pack_call(kernel, sizes, masks, extra_shape, place, arrays):
    _, part_rows, tok_rows, width = sizes
    rows = part_rows + 2 * tok_rows
    vmem = pl.BlockSpec(memory_space=pltpu.VMEM)
    return pl.pallas_call(
        kernel,
        out_shape=[jax.ShapeDtypeStruct(extra_shape, BF16)]
        + [jax.ShapeDtypeStruct((rows, width), BF16)] * len(masks),
        in_specs=[pl.BlockSpec(memory_space=pltpu.SMEM)] + [vmem] * len(arrays),
        out_specs=[vmem] * (len(masks) + 1),
        compiler_params=pltpu.CompilerParams(vmem_limit_bytes=VMEM_LIMIT),
        cost_estimate=pl.CostEstimate(
            flops=0, bytes_accessed=4 * len(masks) * rows * width, transcendentals=0
        ),
    )(place, *arrays)


def attend_kernel(masks, query_parts, part_rows, tok_rows, heads, place_ref, *refs):
    count = len(masks)
    in_refs = refs[:count]
    scale_ref, shift_ref, proj_ref, mod_ref, lat_ref, key_scr, value_scr = refs[count:]
    half = part_rows // 2
    width = heads * HD
    factor = HD ** (-0.5) * math.log2(math.e)
    me = place_ref[0]
    mine = pl.ds(pl.multiple_of(place_ref[2] * width, HD), width)
    ones = jnp.ones((tok_rows, HD), BF16)
    for src in range(count):
        rows = pl.ds(src * tok_rows, tok_rows)
        key_scr[rows, :] = in_refs[src][pl.ds(part_rows, tok_rows), :]
        for head in range(heads):
            value_scr[rows, pl.ds(2 * head * HD, HD)] = in_refs[src][
                pl.ds(part_rows + tok_rows, tok_rows), pl.ds(head * HD, HD)
            ]
            value_scr[rows, pl.ds((2 * head + 1) * HD, HD)] = ones
    gain = 1.0 + scale_ref[:, mine]
    shift = shift_ref[:, mine]
    proj = proj_ref[:, mine]
    zero = jnp.zeros_like(proj)
    proj_pair = jnp.concatenate(
        [jnp.concatenate([proj, zero], axis=1), jnp.concatenate([zero, proj], axis=1)], axis=0
    )
    for src in range(count):
        mixed = []
        for head in range(heads):
            cols = pl.ds(head * HD, HD)
            query = in_refs[src][pl.ds(0, part_rows), cols]
            logits = mm_nt(query, key_scr[:, cols])
            top = jnp.max(logits, axis=-1, keepdims=True)
            weights = jnp.exp2((logits - top) * factor).astype(BF16)
            both = mm(weights, value_scr[:, pl.ds(2 * head * HD, 2 * HD)])
            mixed.append(both[:, :HD] / both[:, HD:])
        attended = jnp.concatenate(mixed, axis=1) if heads > 1 else mixed[0]
        modulated = (attended * gain + shift).astype(BF16)
        place = jnp.bitwise_xor(me, masks[src])
        mod_ref[place] = modulated
        pair = jnp.concatenate([modulated[:half], modulated[half:]], axis=1)
        lat_ref[place] = mm_nt(pair, proj_pair).astype(BF16)


def attend(place, masks, received, scales, shifts, proj, query_parts, part_rows, tok_rows, heads):
    count = len(received)
    width = heads * HD
    lat_rows = count * tok_rows
    query_rows = count * part_rows
    vmem = pl.BlockSpec(memory_space=pltpu.VMEM)
    return pl.pallas_call(
        functools.partial(attend_kernel, masks, query_parts, part_rows, tok_rows, heads),
        out_shape=(
            jax.ShapeDtypeStruct((count, part_rows, width), BF16),
            jax.ShapeDtypeStruct((count, part_rows // 2, 2 * CH), BF16),
        ),
        in_specs=[pl.BlockSpec(memory_space=pltpu.SMEM)] + [vmem] * (count + 3),
        out_specs=(vmem, vmem),
        scratch_shapes=[
            pltpu.VMEM((lat_rows, width), BF16),
            pltpu.VMEM((lat_rows, 2 * width), BF16),
        ],
        compiler_params=pltpu.CompilerParams(vmem_limit_bytes=VMEM_LIMIT),
        cost_estimate=pl.CostEstimate(
            flops=4 * query_rows * lat_rows * width,
            bytes_accessed=2 * (query_rows * 2 + lat_rows * 2) * width,
            transcendentals=query_rows * lat_rows * heads,
        ),
    )(place, *received, scales, shifts, proj)


def total_kernel(copies, *refs):
    out_ref = refs[-1]
    if len(refs) == 2:
        parts = [refs[0][i].astype(F32) for i in range(refs[0].shape[0])]
    else:
        parts = [ref[...].astype(F32) for ref in refs[:-1]]
    while len(parts) > 1:
        parts = [parts[i] + parts[i + 1] for i in range(0, len(parts), 2)]
    for copy in range(copies):
        out_ref[copy] = parts[0].astype(BF16)


def total_copies(arrays, copies):
    vmem = pl.BlockSpec(memory_space=pltpu.VMEM)
    return pl.pallas_call(
        functools.partial(total_kernel, copies),
        out_shape=jax.ShapeDtypeStruct((copies,) + arrays[0].shape[-2:], BF16),
        in_specs=[vmem] * len(arrays),
        out_specs=vmem,
        compiler_params=pltpu.CompilerParams(vmem_limit_bytes=VMEM_LIMIT),
    )(*arrays)


def lane_mean(x, count):
    return jnp.sum(x, axis=-1, keepdims=True) * (1.0 / count)


def head_kernel(grid_rows, fused, embed_masks, out_factor, place_ref, lat_ref, *refs):
    embed_refs, refs = refs[: len(embed_masks)], refs[len(embed_masks) :]
    pos_ref, pre_ref, post_ref, prompt_ref, cot_ref, mod_ref, *refs = refs
    reward_ref, grad_ref, weight_ref, lat_scr, grad_scr, embed_ref, sems = refs
    patch_rows = grid_rows // 4
    patch_cols = GW // 4
    patches = patch_rows * patch_cols
    copies = []
    for slot, mask in enumerate(embed_masks):
        rows = embed_refs[slot].shape[0]
        first = pl.multiple_of(jnp.bitwise_xor(place_ref[1], mask) * rows, rows)
        copies.append(
            pltpu.make_async_copy(embed_refs[slot], embed_ref.at[pl.ds(first, rows)], sems.at[slot])
        )
        copies[-1].start()
    lat_scr[...] = lat_ref[...].astype(F32)
    for copy in copies:
        copy.wait()

    def embed_block(hi, tx):
        first = 4 * (2 * hi) + tx
        second = 4 * (2 * hi + 1) + tx
        return jnp.concatenate(
            [embed_ref[pl.ds(first * CH, CH), :], embed_ref[pl.ds(second * CH, CH), :]], axis=0
        )

    embedded = pos_ref[...].astype(F32)
    for hi in range(2):
        for tx in range(4):
            rows = [
                lat_scr[pl.ds((2 * pr + hi) * GW + tx, patch_cols, stride=4), :]
                for pr in range(patch_rows)
            ]
            block = jnp.concatenate(rows, axis=0).astype(BF16)
            embedded = embedded + mm(block, embed_block(hi, tx))
    pre = pre_ref[...]
    post = post_ref[...]
    prompt = prompt_ref[...]
    center = embedded - lane_mean(embedded, VW)
    rstd = lax.rsqrt(lane_mean(center * center, VW) + EPS)
    unit = center * rstd
    pooled = jnp.sum(unit, axis=0, keepdims=True) * (1.0 / patches) * pre
    pooled_center = pooled - lane_mean(pooled, VW)
    pooled_rstd = lax.rsqrt(lane_mean(pooled_center * pooled_center, VW) + EPS)
    pooled_unit = pooled_center * pooled_rstd
    final = pooled_unit * post
    dot = jnp.sum(final * prompt, axis=-1, keepdims=True)
    final_sq = jnp.sum(final * final, axis=-1, keepdims=True)
    prompt_sq = jnp.sum(prompt * prompt, axis=-1, keepdims=True)
    final_len = jnp.sqrt(final_sq)
    prompt_len = jnp.sqrt(prompt_sq)
    cosine = dot / (final_len * prompt_len)
    reward_ref[...] = jnp.broadcast_to(100.0 * cosine, reward_ref.shape)
    cot = cot_ref[...]
    final_grad = (100.0 * cot) * (prompt / (final_len * prompt_len) - final * (cosine / final_sq))
    unit_grad = final_grad * post
    pooled_grad = pooled_rstd * (
        unit_grad
        - lane_mean(unit_grad, VW)
        - pooled_unit * lane_mean(unit_grad * pooled_unit, VW)
    )
    flow = pooled_grad * pre * (1.0 / patches)
    embed_grad = rstd * (flow - lane_mean(flow, VW) - unit * lane_mean(flow * unit, VW))
    high = embed_grad.astype(BF16)
    low = (embed_grad - high.astype(F32)).astype(BF16)
    stacked = jnp.concatenate([high, low], axis=0)
    for hi in range(2):
        for tx in range(4):
            both = mm_nt(stacked, embed_block(hi, tx))
            piece = both[:patches] + both[patches:]
            for pr in range(patch_rows):
                grad_scr[pl.ds((2 * pr + hi) * GW + tx, patch_cols, stride=4), :] = piece[
                    pr * patch_cols : (pr + 1) * patch_cols
                ]
    grad = grad_scr[...].astype(BF16)
    grad_ref[...] = grad
    if fused:
        weight_ref[...] = (readout_grad(grad, mod_ref) * out_factor).astype(BF16)
    else:
        weight_ref[...] = jnp.zeros_like(weight_ref)


def readout_grad(grad, mod_ref):
    count, rows, width = mod_ref.shape
    half = rows // 2
    first = mod_ref[:, :half, :].reshape(count * half, width)
    second = mod_ref[:, half:, :].reshape(count * half, width)
    return mm_tn(grad, first)[:CH] + mm_tn(grad, second)[CH:]


def reward_head(
    place, latent, embed, pos, pre, post, prompt, cot, modulated, grid_rows, fused, out_factor
):
    patches = grid_rows * GW // 16
    rows = grid_rows * GW // 2
    width = modulated.shape[2]
    embed_arrays, embed_masks = [x for x, _ in embed], [mask for _, mask in embed]
    vmem = pl.BlockSpec(memory_space=pltpu.VMEM)
    anywhere = pl.BlockSpec(memory_space=pl.ANY)
    return pl.pallas_call(
        functools.partial(head_kernel, grid_rows, fused, embed_masks, out_factor),
        out_shape=(
            jax.ShapeDtypeStruct((1, 128), F32),
            jax.ShapeDtypeStruct((rows, 2 * CH), BF16),
            jax.ShapeDtypeStruct((CH, width), BF16),
        ),
        in_specs=[pl.BlockSpec(memory_space=pltpu.SMEM), vmem]
        + [anywhere] * len(embed_arrays)
        + [vmem] * 6,
        out_specs=(vmem, vmem, vmem),
        scratch_shapes=[
            pltpu.VMEM((rows, 2 * CH), F32),
            pltpu.VMEM((rows, 2 * CH), F32),
            pltpu.VMEM((16 * CH, VW), BF16),
            pltpu.SemaphoreType.DMA((len(embed_arrays),)),
        ],
        compiler_params=pltpu.CompilerParams(vmem_limit_bytes=VMEM_LIMIT),
        cost_estimate=pl.CostEstimate(
            flops=6 * patches * 16 * CH * VW,
            bytes_accessed=2 * 16 * CH * VW + 2 * patches * VW,
            transcendentals=0,
        ),
    )(place, latent, *embed_arrays, pos, pre, post, prompt, cot, modulated)


def spread_kernel(count, half, heads, place_ref, grad_ref, scale_ref, proj_ref, out_ref):
    width = heads * HD
    mine = pl.ds(pl.multiple_of(place_ref[2] * width, HD), width)
    gain = 1.0 + scale_ref[:, mine]
    proj = proj_ref[:, mine]
    zero = jnp.zeros_like(proj)
    sides = (jnp.concatenate([proj, zero], axis=0), jnp.concatenate([zero, proj], axis=0))
    for src in range(count):
        grad = grad_ref[pl.ds(src * half, half), :]
        for side in range(2):
            rows = (mm(grad, sides[side]) * gain).astype(BF16)
            for head in range(heads):
                out_ref[0, head, pl.ds((2 * src + side) * half, half), :] = rows[
                    :, head * HD : (head + 1) * HD
                ]


def spread(place, grad, scales, proj, count, half, heads):
    vmem = pl.BlockSpec(memory_space=pltpu.VMEM)
    return pl.pallas_call(
        functools.partial(spread_kernel, count, half, heads),
        out_shape=jax.ShapeDtypeStruct((1, heads, 2 * count * half, HD), BF16),
        in_specs=[pl.BlockSpec(memory_space=pltpu.SMEM)] + [vmem] * 3,
        out_specs=vmem,
        compiler_params=pltpu.CompilerParams(vmem_limit_bytes=VMEM_LIMIT),
        cost_estimate=pl.CostEstimate(
            flops=8 * count * half * CH * heads * HD,
            bytes_accessed=4 * count * half * heads * HD,
            transcendentals=0,
        ),
    )(place, grad, scales, proj)


def weight_kernel(out_factor, grad_ref, mod_ref, out_ref):
    out_ref[...] = (readout_grad(grad_ref[...], mod_ref) * out_factor).astype(BF16)


def weight_call(grad, modulated, out_factor):
    vmem = pl.BlockSpec(memory_space=pltpu.VMEM)
    return pl.pallas_call(
        functools.partial(weight_kernel, out_factor),
        out_shape=jax.ShapeDtypeStruct((CH, modulated.shape[2]), BF16),
        in_specs=[vmem] * 2,
        out_specs=vmem,
        compiler_params=pltpu.CompilerParams(vmem_limit_bytes=VMEM_LIMIT),
    )(grad, modulated)


def finish_kernel(in_ref, out_ref):
    count, _, width = in_ref.shape
    for group in range(count):
        out_ref[:, pl.ds(group * width, width)] = in_ref[group].astype(F32)


def finish(blocks):
    vmem = pl.BlockSpec(memory_space=pltpu.VMEM)
    return pl.pallas_call(
        finish_kernel,
        out_shape=jax.ShapeDtypeStruct((CH, HEADS * HD), F32),
        in_specs=[vmem],
        out_specs=vmem,
        compiler_params=pltpu.CompilerParams(vmem_limit_bytes=VMEM_LIMIT),
    )(blocks)


def swap(x, axis, mask):
    count = lax.axis_size(axis)
    return lax.ppermute(x, axis, [(i, i ^ mask) for i in range(count)])


def all_to_all(x, groups=None):
    return lax.all_to_all(
        x, "seq", split_axis=0, concat_axis=0, tiled=True, axis_index_groups=groups
    )


def ring_gather(block):
    count = lax.axis_size("seq")
    me = lax.axis_index("seq")
    order = list(range(0, count, 2)) + list(range(count - 1, 0, -2))
    ahead = [(order[i], order[(i + 1) % count]) for i in range(count)]
    behind = [(b, a) for a, b in ahead]
    spot = jnp.where(me % 2 == 0, me // 2, count - 1 - me // 2)

    def place_of(at):
        at = (at + count) % count
        return jnp.where(at < count // 2, 2 * at, 2 * (count - 1 - at) + 1)

    def put(held, piece, at):
        return lax.dynamic_update_slice_in_dim(held, piece[:, None], place_of(at), 1)

    def step(t, carry):
        up, down, held = carry
        up = lax.ppermute(up, "seq", ahead)
        down = lax.ppermute(down, "seq", behind)
        held = put(held, up, spot - t - 1)
        held = put(held, down, spot + t + 1)
        return up, down, held

    held = jnp.zeros((block.shape[0], count) + block.shape[1:], block.dtype)
    held = put(held, block, spot)
    held = lax.fori_loop(0, count // 2, step, (block, block, held))[2]
    return held.reshape(-1, block.shape[2])


def after_kernel(*refs):
    del refs


def after(x, others):
    anywhere = pl.BlockSpec(memory_space=pl.ANY)
    return pl.pallas_call(
        after_kernel,
        out_shape=jax.ShapeDtypeStruct(x.shape, x.dtype),
        in_specs=[anywhere] * (1 + len(others)),
        out_specs=anywhere,
        input_output_aliases={0: 0},
    )(x, *others)


def on_device(
    queries,
    keys,
    values,
    shifts,
    scales,
    proj_out,
    patch_embed,
    pos_embed,
    pre_gain,
    post_gain,
    prompt,
    cotangent,
):
    seq_count = lax.axis_size("seq")
    data_count = lax.axis_size("dp")
    tok_rows = queries.shape[1]
    query_parts = max(1, seq_count // HEADS)
    head_count = max(1, HEADS // seq_count)
    group_count = HEADS // head_count
    width = head_count * HD
    seq_index = lax.axis_index("seq")
    head_group = seq_index // query_parts
    query_part = seq_index % query_parts
    part_rows = tok_rows // query_parts
    half = part_rows // 2
    lat_rows = seq_count * tok_rows
    grid_rows = lat_rows // GW
    canonical = part_rows == 2 * GW
    place = jnp.stack([seq_index, lax.axis_index("dp"), head_group]).astype(jnp.int32)
    proj_turned = proj_out.T
    out_factor = 1.0 / math.sqrt(data_count * lat_rows)

    sizes = (query_parts, part_rows, tok_rows, width)
    positions = patch_embed.shape[0]
    share = positions // data_count if positions % data_count == 0 else 0
    share_shape = (share or positions,) + patch_embed.shape[1:]
    masks = list(range(seq_count - 1, -1, -1))
    embed_share, *pieces = pack_call(
        functools.partial(pack_kernel, sizes, masks, share),
        sizes, masks, share_shape, place, (queries, keys, values, patch_embed),
    )
    received = [swap(piece, "seq", mask) if mask else piece for mask, piece in zip(masks, pieces)]
    embed_mine = after(ring_gather(embed_share), received[:-1])
    embed_bits = [1 << b for b in reversed(range(data_count.bit_length() - 1))] if share else []
    embed = [(embed_mine, 0)]
    for bit in embed_bits[:1]:
        embed = embed + [(swap(x, "dp", bit), m ^ bit) for x, m in embed]

    modulated, latent_part = attend(
        place, masks, received, scales, shifts, proj_turned,
        query_parts, part_rows, tok_rows, head_count,
    )

    groups = None
    if query_parts > 1:
        groups = [[g * query_parts + r for g in range(group_count)] for r in range(query_parts)]
    per_share = seq_count // group_count
    pieces = all_to_all(latent_part.reshape(group_count, per_share * half, 2 * CH), groups)
    embed = [embed[0]] + [(after(x, [pieces]), m) for x, m in embed[1:]]
    for bit in embed_bits[1:]:
        embed = embed + [(swap(x, "dp", bit), m ^ bit) for x, m in embed]
    latent = all_to_all(total_copies([pieces], seq_count))
    if canonical:
        latent = latent.reshape(lat_rows // 2, 2 * CH)
    else:
        latent = latent.reshape(group_count, query_parts, per_share, half, 2, CH)
        latent = latent.transpose(0, 2, 1, 4, 3, 5).reshape(grid_rows // 2, 2, GW, CH)
        latent = latent.transpose(0, 2, 1, 3).reshape(lat_rows // 2, 2 * CH)

    reward, grad, weight = reward_head(
        place, latent, embed, pos_embed, pre_gain[None], post_gain[None], prompt,
        cotangent[None], modulated, grid_rows, canonical, out_factor,
    )
    if not canonical:
        tokens = grad.reshape(grid_rows // 2, GW, 2, CH).transpose(0, 2, 1, 3)
        tokens = tokens.reshape(seq_count, query_parts, 2, half, CH)
        tokens = lax.dynamic_index_in_dim(tokens, query_part, 1, keepdims=False)
        grad = tokens.transpose(0, 2, 1, 3).reshape(seq_count * half, 2 * CH)
        weight = weight_call(grad, modulated, out_factor)

    parts = [weight] + [swap(weight, "dp", mask) for mask in range(1, data_count)]
    attn_grad = spread(place, grad, scales, proj_turned, seq_count, half, head_count)
    if query_parts > 1:
        total = total_copies(parts, 1)[0]
        parts = [total] + [swap(total, "seq", mask) for mask in range(1, query_parts)]
    blocks = all_to_all(total_copies(parts, group_count), groups)
    return (reward[0, :1], attn_grad, finish(blocks).T)


def solution(mesh):
    return jax.shard_map(
        on_device,
        mesh=mesh,
        in_specs=(
            P("dp", "seq", None),
            P("dp", "seq", None),
            P("dp", "seq", None),
            P("dp", None),
            P("dp", None),
            P(),
            P(None, "seq", None),
            P(),
            P(),
            P(),
            P("dp", None),
            P("dp"),
        ),
        out_specs=(P("dp"), P("dp", "seq", None, None), P()),
        check_vma=False,
    )
```

time: 134 us -> 135 us (level)
  waiting for transfers between devices: 45.9 us -> 53.6 us
  starting transfers between devices: 50.2 us -> 46.7 us
  local copies, waits for them, and re-layouts: 18.6 us -> 15.7 us
    ppermute x28 -> x13, waiting for transfers between devices: 45.9 us -> 8.57 us  [swap(): return lax.ppermute(x, axis, [(i, i ^ mask) for i in range(count)])]
    ppermute x28 -> x13, starting transfers between devices: 50.2 us -> 15.6 us  [swap(): return lax.ppermute(x, axis, [(i, i ^ mask) for i in range(count)])]
    ppermute x0 -> x8, waiting for transfers between devices: none -> 22.9 us  [the longest x4 13.6 us: step(): down = lax.ppermute(down, 'seq', behind)]
    all_to_all x0 -> x3, waiting for transfers between devices: none -> 22.1 us  [all_to_all(): lax.all_to_all(x, 'seq', split_axis=0, concat_axis=0, tiled=True, axis_in...]
    ppermute x0 -> x8, starting transfers between devices: none -> 20.8 us  [the longest x4 14.8 us: step(): up = lax.ppermute(up, 'seq', ahead)]
    all_to_all x0 -> x3, starting transfers between devices: none -> 10.3 us  [all_to_all(): lax.all_to_all(x, 'seq', split_axis=0, concat_axis=0, tiled=True, axis_in...]
    dynamic_slice x3 -> x0, local copies, waits for them, and re-layouts: 2.73 us -> none  [the longest x1 1.37 us: on_device(): proj_mine = lax.dynamic_slice_in_dim(proj_out, head_group * width, width, 0)]
    pallas_call x5 -> x8, Pallas kernels: 15.1 us -> 14.5 us  [the longest x1 7.33 us: attend(): pl.pallas_call(functools.partial(attend_kernel, masks, query_parts, part_...]
  transfers between devices with their start and end apart: 28 -> 24, of which waited for: 15 -> 16; matrix products, arithmetic and copies ran while one was open for 4% -> 1% of each run, Pallas kernels for 9% -> 7%
where the time goes in v3:
time: 135 us; the launch traced here: 134 us
  waiting for transfers between devices  53.6 us (40%)
  starting transfers between devices  46.7 us (35%)
  Pallas kernels  16.1 us (12%)
  local copies, waits for them, and re-layouts  15.7 us (12%)
  between operations  1.56 us (1%)
    all_to_all x3, waiting for transfers between devices, all_to_all(): lax.all_to_all(x, 'seq', split_axis=0, concat_axis=0, tiled=True, axis_in...  22.1 us
    ppermute x13, starting transfers between devices, swap(): return lax.ppermute(x, axis, [(i, i ^ mask) for i in range(count)])  15.6 us
    ppermute x4, starting transfers between devices, step(): up = lax.ppermute(up, 'seq', ahead)  14.8 us
    unnamed x65, local copies, waits for them, and re-layouts  14.6 us
    ppermute x4, waiting for transfers between devices, step(): down = lax.ppermute(down, 'seq', behind)  13.6 us
    all_to_all x3, starting transfers between devices, all_to_all(): lax.all_to_all(x, 'seq', split_axis=0, concat_axis=0, tiled=True, axis_in...  10.3 us
    ppermute x4, waiting for transfers between devices, step(): up = lax.ppermute(up, 'seq', ahead)  9.33 us
    ppermute x13, waiting for transfers between devices, swap(): return lax.ppermute(x, axis, [(i, i ^ mask) for i in range(count)])  8.57 us
  transfers between devices with their start and end apart: 24, of which 16 were waited for; matrix products, arithmetic and copies ran while one was open for 1% of the time, Pallas kernels for 7%

profile of v3, /device:TPU:0, one launch (start us, length us, event | category | flops | bytes accessed | tf_op | source)
XLA Modules:
  0.0 133.9 jit_solution(14694075499163983094)
XLA Ops:
  6.3 6.0 %collective-permute-start.2 = (bf16[384,256]{1,0:T(8,128)(2,1)S(1)}, bf16[384,256]{1,0:T(8,128)(2,1)S(1)}, u32[]{:S(2)}, u32[]{:S(2)}) collective-permute-start(bf16[384,256]{1,0:T(8,128)(2,1)S(1)} %get-tuple-element.190), channel_id=1, source_target_pairs={{0,28},{4,24},{8,20},{12,16},{16,12},{20,8},{24,4},{28,0},{1,29},{... | collective-permute-start | bytes 589832 | tf_op jit(solution)/shard_map/ppermute | solution.py:358
  13.3 43.9 %while.21 = (s32[]{:T(128)}, bf16[4,8,1280]{2,1,0:T(8,128)(2,1)S(1)}, bf16[4,8,1280]{2,1,0:T(8,128)(2,1)S(1)}, bf16[4,8,8,1280]{3,2,0,1:T(8,128)(2,1)S(1)}, s32[...) while((s32[]{:T(128)}, ...), condition=%wide.region_1.2_spmd, body=%wide.region_0.1_spmd.sunk | while | flops 46 | bytes 1311407 | solution.py:392
  14.9 1.9 %collective-permute-start = (bf16[4,8,1280]{2,1,0:T(8,128)(2,1)S(1)}, bf16[4,8,1280]{2,1,0:T(8,128)(2,1)S(1)}, u32[]{:S(2)}, u32[]{:S(2)}) collective-permute-start(bf16[4,8,1280]{2,1,0:T(8,128)(2,1)S(1)} %get-tuple-element.259), channel_id=1, source_target_pairs={{0,8},{8,16},{16,24},{24,28},{28,20},{20,12},{12,4},{4,0},{1,9},{9... | collective-permute-start | bytes 245768 | tf_op jit(solution)/shard_map/while/body/eval_jaxpr/ppermute | solution.py:384
  16.8 6.4 %collective-permute-done.1 = bf16[4,8,1280]{2,1,0:T(8,128)(2,1)S(1)} collective-permute-done((bf16[4,8,1280]{2,1,0:T(8,128)(2,1)S(1)}, bf16[4,8,1280]{2,1,0:T(8,128)(2,1)S(1)}, u32[]{:S(2)}, u32[]{:S(2)}) %collective-permute-start.1) | collective-permute-done | bytes 81952 | tf_op jit(solution)/shard_map/while/body/eval_jaxpr/ppermute | solution.py:385
  23.2 3.5 %collective-permute-done = bf16[4,8,1280]{2,1,0:T(8,128)(2,1)S(1)} collective-permute-done((bf16[4,8,1280]{2,1,0:T(8,128)(2,1)S(1)}, bf16[4,8,1280]{2,1,0:T(8,128)(2,1)S(1)}, u32[]{:S(2)}, u32[]{:S(2)}) %collective-permute-start) | collective-permute-done | bytes 81952 | tf_op jit(solution)/shard_map/while/body/eval_jaxpr/ppermute | solution.py:384
  27.3 12.6 %collective-permute-start = (bf16[4,8,1280]{2,1,0:T(8,128)(2,1)S(1)}, bf16[4,8,1280]{2,1,0:T(8,128)(2,1)S(1)}, u32[]{:S(2)}, u32[]{:S(2)}) collective-permute-start(bf16[4,8,1280]{2,1,0:T(8,128)(2,1)S(1)} %get-tuple-element.259), channel_id=1, source_target_pairs={{0,8},{8,16},{16,24},{24,28},{28,20},{20,12},{12,4},{4,0},{1,9},{9... | collective-permute-start | bytes 245768 | tf_op jit(solution)/shard_map/while/body/eval_jaxpr/ppermute | solution.py:384
  39.9 2.4 %collective-permute-done.1 = bf16[4,8,1280]{2,1,0:T(8,128)(2,1)S(1)} collective-permute-done((bf16[4,8,1280]{2,1,0:T(8,128)(2,1)S(1)}, bf16[4,8,1280]{2,1,0:T(8,128)(2,1)S(1)}, u32[]{:S(2)}, u32[]{:S(2)}) %collective-permute-start.1) | collective-permute-done | bytes 81952 | tf_op jit(solution)/shard_map/while/body/eval_jaxpr/ppermute | solution.py:385
  42.8 2.1 %collective-permute-start.1 = (bf16[4,8,1280]{2,1,0:T(8,128)(2,1)S(1)}, bf16[4,8,1280]{2,1,0:T(8,128)(2,1)S(1)}, u32[]{:S(2)}, u32[]{:S(2)}) collective-permute-start(bf16[4,8,1280]{2,1,0:T(8,128)(2,1)S(1)} %get-tuple-element.260), channel_id=1, source_target_pairs={{8,0},{16,8},{24,16},{28,24},{20,28},{12,20},{4,12},{0,4},{9,1},{1... | collective-permute-start | bytes 245768 | tf_op jit(solution)/shard_map/while/body/eval_jaxpr/ppermute | solution.py:385
  44.9 2.4 %collective-permute-done.1 = bf16[4,8,1280]{2,1,0:T(8,128)(2,1)S(1)} collective-permute-done((bf16[4,8,1280]{2,1,0:T(8,128)(2,1)S(1)}, bf16[4,8,1280]{2,1,0:T(8,128)(2,1)S(1)}, u32[]{:S(2)}, u32[]{:S(2)}) %collective-permute-start.1) | collective-permute-done | bytes 81952 | tf_op jit(solution)/shard_map/while/body/eval_jaxpr/ppermute | solution.py:385
  47.3 2.2 %collective-permute-done = bf16[4,8,1280]{2,1,0:T(8,128)(2,1)S(1)} collective-permute-done((bf16[4,8,1280]{2,1,0:T(8,128)(2,1)S(1)}, bf16[4,8,1280]{2,1,0:T(8,128)(2,1)S(1)}, u32[]{:S(2)}, u32[]{:S(2)}) %collective-permute-start) | collective-permute-done | bytes 81952 | tf_op jit(solution)/shard_map/while/body/eval_jaxpr/ppermute | solution.py:384
  49.6 1.8 %collective-permute-start.1 = (bf16[4,8,1280]{2,1,0:T(8,128)(2,1)S(1)}, bf16[4,8,1280]{2,1,0:T(8,128)(2,1)S(1)}, u32[]{:S(2)}, u32[]{:S(2)}) collective-permute-start(bf16[4,8,1280]{2,1,0:T(8,128)(2,1)S(1)} %get-tuple-element.260), channel_id=1, source_target_pairs={{8,0},{16,8},{24,16},{28,24},{20,28},{12,20},{4,12},{0,4},{9,1},{1... | collective-permute-start | bytes 245768 | tf_op jit(solution)/shard_map/while/body/eval_jaxpr/ppermute | solution.py:385
  51.7 2.4 %collective-permute-done.1 = bf16[4,8,1280]{2,1,0:T(8,128)(2,1)S(1)} collective-permute-done((bf16[4,8,1280]{2,1,0:T(8,128)(2,1)S(1)}, bf16[4,8,1280]{2,1,0:T(8,128)(2,1)S(1)}, u32[]{:S(2)}, u32[]{:S(2)}) %collective-permute-start.1) | collective-permute-done | bytes 81952 | tf_op jit(solution)/shard_map/while/body/eval_jaxpr/ppermute | solution.py:385
  54.1 3.1 %collective-permute-done = bf16[4,8,1280]{2,1,0:T(8,128)(2,1)S(1)} collective-permute-done((bf16[4,8,1280]{2,1,0:T(8,128)(2,1)S(1)}, bf16[4,8,1280]{2,1,0:T(8,128)(2,1)S(1)}, u32[]{:S(2)}, u32[]{:S(2)}) %collective-permute-start) | collective-permute-done | bytes 81952 | tf_op jit(solution)/shard_map/while/body/eval_jaxpr/ppermute | solution.py:384
  58.9 2.6 %collective-permute-start.6 = (bf16[384,256]{1,0:T(8,128)(2,1)S(1)}, bf16[384,256]{1,0:T(8,128)(2,1)S(1)}, u32[]{:S(2)}, u32[]{:S(2)}) collective-permute-start(bf16[384,256]{1,0:T(8,128)(2,1)S(1)} %get-tuple-element.194), channel_id=1, source_target_pairs={{0,12},{4,8},{8,4},{12,0},{16,28},{20,24},{24,20},{28,16},{1,13},{... | collective-permute-start | bytes 589832 | tf_op jit(solution)/shard_map/ppermute | solution.py:358
  63.3 2.0 %collective-permute-done.5.refs_3_.refs_4_ = bf16[384,256]{1,0:T(8,128)(2,1)S(1)} collective-permute-done((bf16[384,256]{1,0:T(8,128)(2,1)S(1)}, bf16[384,256]{1,0:T(8,128)(2,1)S(1)}, u32[]{:S(2)}, u32[]{:S(2)}) %collective-permute-start.5) | collective-permute-done | bytes 196640 | tf_op jit(solution)/shard_map/ppermute | solution.py:358
  65.7 3.8 %collective-permute-done.7.refs_5_.refs_6_ = bf16[384,256]{1,0:T(8,128)(2,1)S(1)} collective-permute-done((bf16[384,256]{1,0:T(8,128)(2,1)S(1)}, bf16[384,256]{1,0:T(8,128)(2,1)S(1)}, u32[]{:S(2)}, u32[]{:S(2)}) %collective-permute-start.7) | collective-permute-done | bytes 196640 | tf_op jit(solution)/shard_map/ppermute | solution.py:358
  77.4 7.3 %shard_map.140 = (bf16[8,128,256]{2,1,0:T(8,128)(2,1)S(1)}, bf16[8,64,128]{2,1,0:T(8,128)(2,1)}) custom-call(s32[3]{0:T(128)S(1)} %pad_add_fusion.place_ref, bf16[384,256]{1,0:T(8,128)(2,1)S(1)} %copy-done.11, bf16[384,256]{1,0:T(8,128)(2,1)S(1)} %copy-done.13, bf16[384,256]{1,0:T(8,128)(2,1)S(1)} %copy-done.15, bf16[384,256]{1,0:T(8,128)(2,1)S(1)} %copy-done.17, ...), custom_call_target="tpu_custom_call" | custom-call | flops 1073741824 | bytes 2097152 | tf_op jit(solution)/shard_map/pallas_call | solution.py:118
  84.7 3.4 %all-to-all-start = ((bf16[8,64,128]{2,1,0:T(8,128)(2,1)}), bf16[8,64,128]{2,1,0:T(8,128)(2,1)S(1)}, u32[]{:S(2)}, u32[]{:S(2)}) async-start(bf16[8,64,128]{2,1,0:T(8,128)(2,1)} %get-tuple-element.198), calls=%async_computation | async-start | bytes 262144 | tf_op jit(solution)/shard_map/all_to_all | solution.py:362
  88.2 7.2 %all-to-all-done.refs_0_.refs_1_ = bf16[8,64,128]{2,1,0:T(8,128)(2,1)S(1)} async-done(((bf16[8,64,128]{2,1,0:T(8,128)(2,1)}), bf16[8,64,128]{2,1,0:T(8,128)(2,1)S(1)}, u32[]{:S(2)}, u32[]{:S(2)}) %all-to-all-start) | async-done | bytes 131104 | tf_op jit(solution)/shard_map/all_to_all | solution.py:362
  98.5 3.5 %all-to-all-start.1 = ((bf16[8,64,128]{2,1,0:T(8,128)(2,1)}), bf16[8,64,128]{2,1,0:T(8,128)(2,1)S(1)}, u32[]{:S(2)}, u32[]{:S(2)}) async-start(bf16[8,64,128]{2,1,0:T(8,128)(2,1)} %shard_map.141), calls=%async_computation.1 | async-start | bytes 262144 | tf_op jit(solution)/shard_map/all_to_all | solution.py:362
  102.7 7.1 %all-to-all-done.1 = bf16[8,64,128]{2,1,0:T(8,128)(2,1)S(1)} async-done(((bf16[8,64,128]{2,1,0:T(8,128)(2,1)}), bf16[8,64,128]{2,1,0:T(8,128)(2,1)S(1)}, u32[]{:S(2)}, u32[]{:S(2)}) %all-to-all-start.1) | async-done | bytes 131104 | tf_op jit(solution)/shard_map/all_to_all | solution.py:362
  111.0 4.2 %shard_map.144 = (f32[1,128]{1,0:T(1,128)}, bf16[512,128]{1,0:T(8,128)(2,1)S(1)}, bf16[64,256]{1,0:T(8,128)(2,1)S(1)}) custom-call(s32[3]{0:T(128)S(1)} %pad_add_fusion.place_ref, bf16[512,128]{1,0:T(8,128)(2,1)S(1)} %bitcast.21, bf16[256,1280]{1,0:T(8,128)(2,1)S(1)} %copy-done, bf16[256,1280]{1,0:T(8,128)(2,1)S(1)} %copy-done.2, ...), custom_call_target="tpu_custom_call" | custom-call | flops 503316480 | bytes 2785280 | tf_op jit(solution)/shard_map/pallas_call | solution.py:265
  120.3 3.4 %all-to-all-start.2 = ((bf16[8,64,256]{2,1,0:T(8,128)(2,1)}), bf16[8,64,256]{2,1,0:T(8,128)(2,1)S(1)}, u32[]{:S(2)}, u32[]{:S(2)}) async-start(bf16[8,64,256]{2,1,0:T(8,128)(2,1)} %shard_map.146), calls=%async_computation.2 | async-start | bytes 524288 | tf_op jit(solution)/shard_map/all_to_all | solution.py:362
  125.3 7.8 %all-to-all-done.2.in_ref = bf16[8,64,256]{2,1,0:T(8,128)(2,1)S(1)} async-done(((bf16[8,64,256]{2,1,0:T(8,128)(2,1)}), bf16[8,64,256]{2,1,0:T(8,128)(2,1)S(1)}, u32[]{:S(2)}, u32[]{:S(2)}) %all-to-all-start.2) | async-done | bytes 262176 | tf_op jit(solution)/shard_map/all_to_all | solution.py:362
  (121 shorter events, 33.3 us)
Async XLA Ops:
  6.3 55.2 %collective-permute-start.2 = (bf16[384,256]{1,0:T(8,128)(2,1)S(1)}, bf16[384,256]{1,0:T(8,128)(2,1)S(1)}, u32[]{:S(2)}, u32[]{:S(2)}) collective-permute-start(bf16[384,256]{1,0:T(8,128)(2,1)S(1)} %get-tuple-element.190), channel_id=1, source_target_pairs={{0,28},{4,24},{8,20},{12,16},{16,12},{20,8},{24,4},{28,0},{1,29},{... | collective-permute-start | bytes 589832 | tf_op jit(solution)/shard_map/ppermute | solution.py:358
  12.3 49.4 %collective-permute-start.3 = (bf16[384,256]{1,0:T(8,128)(2,1)S(1)}, bf16[384,256]{1,0:T(8,128)(2,1)S(1)}, u32[]{:S(2)}, u32[]{:S(2)}) collective-permute-start(bf16[384,256]{1,0:T(8,128)(2,1)S(1)} %get-tuple-element.191), channel_id=1, source_target_pairs={{0,24},{4,28},{8,16},{12,20},{16,8},{20,12},{24,0},{28,4},{1,25},{... | collective-permute-start | bytes 589832 | tf_op jit(solution)/shard_map/ppermute | solution.py:358
  12.5 50.8 %collective-permute-start.4 = (bf16[384,256]{1,0:T(8,128)(2,1)S(1)}, bf16[384,256]{1,0:T(8,128)(2,1)S(1)}, u32[]{:S(2)}, u32[]{:S(2)}) collective-permute-start(bf16[384,256]{1,0:T(8,128)(2,1)S(1)} %get-tuple-element.192), channel_id=1, source_target_pairs={{0,20},{4,16},{8,28},{12,24},{16,4},{20,0},{24,12},{28,8},{1,21},{... | collective-permute-start | bytes 589832 | tf_op jit(solution)/shard_map/ppermute | solution.py:358
  13.3 9.9 %collective-permute-start.1 = (bf16[4,8,1280]{2,1,0:T(8,128)(2,1)S(1)}, bf16[4,8,1280]{2,1,0:T(8,128)(2,1)S(1)}, u32[]{:S(2)}, u32[]{:S(2)}) collective-permute-start(bf16[4,8,1280]{2,1,0:T(8,128)(2,1)S(1)} %get-tuple-element.260), channel_id=1, source_target_pairs={{8,0},{16,8},{24,16},{28,24},{20,28},{12,20},{4,12},{0,4},{9,1},{1... | collective-permute-start | bytes 245768 | tf_op jit(solution)/shard_map/while/body/eval_jaxpr/ppermute | solution.py:385
  14.9 11.8 %collective-permute-start = (bf16[4,8,1280]{2,1,0:T(8,128)(2,1)S(1)}, bf16[4,8,1280]{2,1,0:T(8,128)(2,1)S(1)}, u32[]{:S(2)}, u32[]{:S(2)}) collective-permute-start(bf16[4,8,1280]{2,1,0:T(8,128)(2,1)S(1)} %get-tuple-element.259), channel_id=1, source_target_pairs={{0,8},{8,16},{16,24},{24,28},{28,20},{20,12},{12,4},{4,0},{1,9},{9... | collective-permute-start | bytes 245768 | tf_op jit(solution)/shard_map/while/body/eval_jaxpr/ppermute | solution.py:384
  26.8 15.5 %collective-permute-start.1 = (bf16[4,8,1280]{2,1,0:T(8,128)(2,1)S(1)}, bf16[4,8,1280]{2,1,0:T(8,128)(2,1)S(1)}, u32[]{:S(2)}, u32[]{:S(2)}) collective-permute-start(bf16[4,8,1280]{2,1,0:T(8,128)(2,1)S(1)} %get-tuple-element.260), channel_id=1, source_target_pairs={{8,0},{16,8},{24,16},{28,24},{20,28},{12,20},{4,12},{0,4},{9,1},{1... | collective-permute-start | bytes 245768 | tf_op jit(solution)/shard_map/while/body/eval_jaxpr/ppermute | solution.py:385
  27.3 15.4 %collective-permute-start = (bf16[4,8,1280]{2,1,0:T(8,128)(2,1)S(1)}, bf16[4,8,1280]{2,1,0:T(8,128)(2,1)S(1)}, u32[]{:S(2)}, u32[]{:S(2)}) collective-permute-start(bf16[4,8,1280]{2,1,0:T(8,128)(2,1)S(1)} %get-tuple-element.259), channel_id=1, source_target_pairs={{0,8},{8,16},{16,24},{24,28},{28,20},{20,12},{12,4},{4,0},{1,9},{9... | collective-permute-start | bytes 245768 | tf_op jit(solution)/shard_map/while/body/eval_jaxpr/ppermute | solution.py:384
  42.8 4.5 %collective-permute-start.1 = (bf16[4,8,1280]{2,1,0:T(8,128)(2,1)S(1)}, bf16[4,8,1280]{2,1,0:T(8,128)(2,1)S(1)}, u32[]{:S(2)}, u32[]{:S(2)}) collective-permute-start(bf16[4,8,1280]{2,1,0:T(8,128)(2,1)S(1)} %get-tuple-element.260), channel_id=1, source_target_pairs={{8,0},{16,8},{24,16},{28,24},{20,28},{12,20},{4,12},{0,4},{9,1},{1... | collective-permute-start | bytes 245768 | tf_op jit(solution)/shard_map/while/body/eval_jaxpr/ppermute | solution.py:385
  44.9 4.6 %collective-permute-start = (bf16[4,8,1280]{2,1,0:T(8,128)(2,1)S(1)}, bf16[4,8,1280]{2,1,0:T(8,128)(2,1)S(1)}, u32[]{:S(2)}, u32[]{:S(2)}) collective-permute-start(bf16[4,8,1280]{2,1,0:T(8,128)(2,1)S(1)} %get-tuple-element.259), channel_id=1, source_target_pairs={{0,8},{8,16},{16,24},{24,28},{28,20},{20,12},{12,4},{4,0},{1,9},{9... | collective-permute-start | bytes 245768 | tf_op jit(solution)/shard_map/while/body/eval_jaxpr/ppermute | solution.py:384
  49.6 4.5 %collective-permute-start.1 = (bf16[4,8,1280]{2,1,0:T(8,128)(2,1)S(1)}, bf16[4,8,1280]{2,1,0:T(8,128)(2,1)S(1)}, u32[]{:S(2)}, u32[]{:S(2)}) collective-permute-start(bf16[4,8,1280]{2,1,0:T(8,128)(2,1)S(1)} %get-tuple-element.260), channel_id=1, source_target_pairs={{8,0},{16,8},{24,16},{28,24},{20,28},{12,20},{4,12},{0,4},{9,1},{1... | collective-permute-start | bytes 245768 | tf_op jit(solution)/shard_map/while/body/eval_jaxpr/ppermute | solution.py:385
  51.4 5.8 %collective-permute-start = (bf16[4,8,1280]{2,1,0:T(8,128)(2,1)S(1)}, bf16[4,8,1280]{2,1,0:T(8,128)(2,1)S(1)}, u32[]{:S(2)}, u32[]{:S(2)}) collective-permute-start(bf16[4,8,1280]{2,1,0:T(8,128)(2,1)S(1)} %get-tuple-element.259), channel_id=1, source_target_pairs={{0,8},{8,16},{16,24},{24,28},{28,20},{20,12},{12,4},{4,0},{1,9},{9... | collective-permute-start | bytes 245768 | tf_op jit(solution)/shard_map/while/body/eval_jaxpr/ppermute | solution.py:384
  57.3 8.1 %collective-permute-start.5 = (bf16[384,256]{1,0:T(8,128)(2,1)S(1)}, bf16[384,256]{1,0:T(8,128)(2,1)S(1)}, u32[]{:S(2)}, u32[]{:S(2)}) collective-permute-start(bf16[384,256]{1,0:T(8,128)(2,1)S(1)} %get-tuple-element.193), channel_id=1, source_target_pairs={{0,16},{4,20},{8,24},{12,28},{16,0},{20,4},{24,8},{28,12},{1,17},{... | collective-permute-start | bytes 589832 | tf_op jit(solution)/shard_map/ppermute | solution.py:358
  58.9 6.8 %collective-permute-start.6 = (bf16[384,256]{1,0:T(8,128)(2,1)S(1)}, bf16[384,256]{1,0:T(8,128)(2,1)S(1)}, u32[]{:S(2)}, u32[]{:S(2)}) collective-permute-start(bf16[384,256]{1,0:T(8,128)(2,1)S(1)} %get-tuple-element.194), channel_id=1, source_target_pairs={{0,12},{4,8},{8,4},{12,0},{16,28},{20,24},{24,20},{28,16},{1,13},{... | collective-permute-start | bytes 589832 | tf_op jit(solution)/shard_map/ppermute | solution.py:358
  61.5 8.0 %collective-permute-start.7 = (bf16[384,256]{1,0:T(8,128)(2,1)S(1)}, bf16[384,256]{1,0:T(8,128)(2,1)S(1)}, u32[]{:S(2)}, u32[]{:S(2)}) collective-permute-start(bf16[384,256]{1,0:T(8,128)(2,1)S(1)} %get-tuple-element.195), channel_id=1, source_target_pairs={{0,8},{4,12},{8,0},{12,4},{16,24},{20,28},{24,16},{28,20},{1,9},{5... | collective-permute-start | bytes 589832 | tf_op jit(solution)/shard_map/ppermute | solution.py:358
  61.7 7.8 %collective-permute-start.8 = (bf16[384,256]{1,0:T(8,128)(2,1)S(1)}, bf16[384,256]{1,0:T(8,128)(2,1)S(1)}, u32[]{:S(2)}, u32[]{:S(2)}) collective-permute-start(bf16[384,256]{1,0:T(8,128)(2,1)S(1)} %get-tuple-element.196), channel_id=1, source_target_pairs={{0,4},{4,0},{8,12},{12,8},{16,20},{20,16},{24,28},{28,24},{1,5},{5... | collective-permute-start | bytes 589832 | tf_op jit(solution)/shard_map/ppermute | solution.py:358
  70.2 25.1 %collective-permute-start.9 = (bf16[256,1280]{1,0:T(8,128)(2,1)}, bf16[256,1280]{1,0:T(8,128)(2,1)S(1)}, u32[]{:S(2)}, u32[]{:S(2)}) collective-permute-start(bf16[256,1280]{1,0:T(8,128)(2,1)} %shard_map.142.refs_0_), channel_id=1, source_target_pairs={{0,2},{1,3},{2,0},{3,1},{4,6},{5,7},{6,4},{7,5},{8,10},{9,11},{10,... | collective-permute-start | bytes 1966088 | tf_op jit(solution)/shard_map/ppermute | solution.py:358
  84.7 10.7 %all-to-all-start = ((bf16[8,64,128]{2,1,0:T(8,128)(2,1)}), bf16[8,64,128]{2,1,0:T(8,128)(2,1)S(1)}, u32[]{:S(2)}, u32[]{:S(2)}) async-start(bf16[8,64,128]{2,1,0:T(8,128)(2,1)} %get-tuple-element.198), calls=%async_computation | async-start | bytes 262144 | tf_op jit(solution)/shard_map/all_to_all | solution.py:362
  88.1 21.8 %collective-permute-start.10 = (bf16[256,1280]{1,0:T(8,128)(2,1)S(1)}, bf16[256,1280]{1,0:T(8,128)(2,1)S(1)}, u32[]{:S(2)}, u32[]{:S(2)}) collective-permute-start(bf16[256,1280]{1,0:T(8,128)(2,1)S(1)} %copy-done), channel_id=1, source_target_pairs={{0,1},{1,0},{2,3},{3,2},{4,5},{5,4},{6,7},{7,6},{8,9},{9,8},{10,11... | collective-permute-start | bytes 1966088 | tf_op jit(solution)/shard_map/ppermute | solution.py:358
  96.9 13.0 %collective-permute-start.11 = (bf16[256,1280]{1,0:T(8,128)(2,1)}, bf16[256,1280]{1,0:T(8,128)(2,1)S(1)}, u32[]{:S(2)}, u32[]{:S(2)}) collective-permute-start(bf16[256,1280]{1,0:T(8,128)(2,1)} %shard_map.143.refs_1_), channel_id=1, source_target_pairs={{0,1},{1,0},{2,3},{3,2},{4,5},{5,4},{6,7},{7,6},{8,9},{9,8},{10,11... | collective-permute-start | bytes 1966088 | tf_op jit(solution)/shard_map/ppermute | solution.py:358
  98.5 11.4 %all-to-all-start.1 = ((bf16[8,64,128]{2,1,0:T(8,128)(2,1)}), bf16[8,64,128]{2,1,0:T(8,128)(2,1)S(1)}, u32[]{:S(2)}, u32[]{:S(2)}) async-start(bf16[8,64,128]{2,1,0:T(8,128)(2,1)} %shard_map.141), calls=%async_computation.1 | async-start | bytes 262144 | tf_op jit(solution)/shard_map/all_to_all | solution.py:362
  115.2 3.4 %collective-permute-start.14 = (bf16[64,256]{1,0:T(8,128)(2,1)S(1)}, bf16[64,256]{1,0:T(8,128)(2,1)S(1)}, u32[]{:S(2)}, u32[]{:S(2)}) collective-permute-start(bf16[64,256]{1,0:T(8,128)(2,1)S(1)} %get-tuple-element.204.refs_0_), channel_id=1, source_target_pairs={{0,3},{1,2},{2,1},{3,0},{4,7},{5,6},{6,5},{7,4},{8,11},{9,10},{10,... | collective-permute-start | bytes 98312 | tf_op jit(solution)/shard_map/ppermute | solution.py:358
  115.3 4.3 %collective-permute-start.13 = (bf16[64,256]{1,0:T(8,128)(2,1)S(1)}, bf16[64,256]{1,0:T(8,128)(2,1)S(1)}, u32[]{:S(2)}, u32[]{:S(2)}) collective-permute-start(bf16[64,256]{1,0:T(8,128)(2,1)S(1)} %get-tuple-element.204.refs_0_), channel_id=1, source_target_pairs={{0,2},{1,3},{2,0},{3,1},{4,6},{5,7},{6,4},{7,5},{8,10},{9,11},{10,... | collective-permute-start | bytes 98312 | tf_op jit(solution)/shard_map/ppermute | solution.py:358
  116.3 3.2 %collective-permute-start.12 = (bf16[64,256]{1,0:T(8,128)(2,1)S(1)}, bf16[64,256]{1,0:T(8,128)(2,1)S(1)}, u32[]{:S(2)}, u32[]{:S(2)}) collective-permute-start(bf16[64,256]{1,0:T(8,128)(2,1)S(1)} %get-tuple-element.204.refs_0_), channel_id=1, source_target_pairs={{0,1},{1,0},{2,3},{3,2},{4,5},{5,4},{6,7},{7,6},{8,9},{9,8},{10,11... | collective-permute-start | bytes 98312 | tf_op jit(solution)/shard_map/ppermute | solution.py:358
  120.3 12.8 %all-to-all-start.2 = ((bf16[8,64,256]{2,1,0:T(8,128)(2,1)}), bf16[8,64,256]{2,1,0:T(8,128)(2,1)S(1)}, u32[]{:S(2)}, u32[]{:S(2)}) async-start(bf16[8,64,256]{2,1,0:T(8,128)(2,1)} %shard_map.146), calls=%async_computation.2 | async-start | bytes 524288 | tf_op jit(solution)/shard_map/all_to_all | solution.py:362
  (32 other events, 75.0 us)

commit v4 on v3

--- a/solution.py
+++ b/solution.py
@@ -31,62 +31,214 @@
     return lax.dot_general(a, b, (((0,), (0,)), ((), ())), preferred_element_type=F32)
 
 
-def pack_piece(sizes, me, mask, q_ref, k_ref, v_ref, out):
-    query_parts, part_rows, tok_rows, width = sizes
-    dest = jnp.bitwise_xor(me, mask)
-    group, part = dest // query_parts, dest % query_parts
-    cols = pl.ds(pl.multiple_of(group * width, HD), width)
-    first = pl.multiple_of(part * part_rows, part_rows)
-    out[pl.ds(0, part_rows), :] = q_ref[0, pl.ds(first, part_rows), cols]
-    out[pl.ds(part_rows, tok_rows), :] = k_ref[0, :, cols]
-    out[pl.ds(part_rows + tok_rows, tok_rows), :] = v_ref[0, :, cols]
-
-
-def pack_kernel(sizes, masks, share, place_ref, q_ref, k_ref, v_ref, embed_ref, share_ref, *out_refs):
+SMEM_SPEC = pl.BlockSpec(memory_space=pltpu.SMEM)
+VMEM_SPEC = pl.BlockSpec(memory_space=pltpu.VMEM)
+HBM_SPEC = pl.BlockSpec(memory_space=pltpu.HBM)
+ANY_SPEC = pl.BlockSpec(memory_space=pl.ANY)
+
+
+def in_hbm(x):
+    return pltpu.with_memory_space_constraint(x, pltpu.HBM)
+
+
+def limits():
+    return pltpu.CompilerParams(vmem_limit_bytes=VMEM_LIMIT)
+
+
+class Sizes:
+    def __init__(self, seq_count, data_count, tok_rows, patch_embed):
+        self.count = seq_count
+        self.query_parts = max(1, seq_count // HEADS)
+        self.heads = max(1, HEADS // seq_count)
+        self.width = self.heads * HD
+        self.tok_rows = tok_rows
+        self.part_rows = tok_rows // self.query_parts
+        positions, self.local, _ = patch_embed.shape
+        self.share = positions // data_count if positions % data_count == 0 else positions
+        self.rows = self.part_rows + 2 * tok_rows
+        self.share_rows = self.share * self.local
+        self.chunks = VW // self.width
+        self.riding = self.local % 8 == 0 and self.share_rows % 16 == 0 and VW % self.width == 0
+        self.ride_rows = self.chunks * self.share_rows if self.riding else 0
+
+    def piece_rows(self, mask):
+        return self.rows + (self.ride_rows if mask % 2 == 0 else 0)
+
+
+def pack_kernel(sizes, masks, place_ref, q_ref, k_ref, v_ref, embed_ref, *refs):
+    out_refs = refs[: len(masks)]
+    q_scr, k_scr, v_scr, embed_scr, share_scr, in_sems, out_sems = refs[len(masks) :]
     me = place_ref[0]
-    share_ref[...] = embed_ref[pl.ds(place_ref[1] * share, share)] if share else embed_ref[...]
-    for mask, out in zip(masks, out_refs):
-        pack_piece(sizes, me, mask, q_ref, k_ref, v_ref, out)
-
-
-def pack_call(kernel, sizes, masks, extra_shape, place, arrays):
-    _, part_rows, tok_rows, width = sizes
-    rows = part_rows + 2 * tok_rows
-    vmem = pl.BlockSpec(memory_space=pltpu.VMEM)
-    return pl.pallas_call(
-        kernel,
-        out_shape=[jax.ShapeDtypeStruct(extra_shape, BF16)]
-        + [jax.ShapeDtypeStruct((rows, width), BF16)] * len(masks),
-        in_specs=[pl.BlockSpec(memory_space=pltpu.SMEM)] + [vmem] * len(arrays),
-        out_specs=[vmem] * (len(masks) + 1),
-        compiler_params=pltpu.CompilerParams(vmem_limit_bytes=VMEM_LIMIT),
+    tok_rows, part_rows, width = sizes.tok_rows, sizes.part_rows, sizes.width
+    share = pl.ds(place_ref[1] * sizes.share, sizes.share)
+    loads = [
+        pltpu.make_async_copy(embed_ref.at[share], embed_scr, in_sems.at[3]),
+        pltpu.make_async_copy(q_ref.at[0], q_scr, in_sems.at[0]),
+        pltpu.make_async_copy(k_ref.at[0], k_scr, in_sems.at[1]),
+        pltpu.make_async_copy(v_ref.at[0], v_scr, in_sems.at[2]),
+    ]
+    for load in loads:
+        load.start()
+    loads[0].wait()
+    if sizes.riding:
+        for chunk in range(sizes.chunks):
+            cols = embed_scr[:, :, pl.ds(chunk * width, width)].astype(F32)
+            share_scr[pl.ds(chunk * sizes.share_rows, sizes.share_rows), :] = cols.reshape(
+                sizes.share_rows, width
+            ).astype(BF16)
+    for load in loads[1:]:
+        load.wait()
+    stores = []
+    for slot, (mask, out) in enumerate(zip(masks, out_refs)):
+        dest = jnp.bitwise_xor(me, mask)
+        group, part = dest // sizes.query_parts, dest % sizes.query_parts
+        cols = pl.ds(pl.multiple_of(group * width, HD), width)
+        first = pl.ds(pl.multiple_of(part * part_rows, part_rows), part_rows)
+        stores += [
+            pltpu.make_async_copy(
+                q_scr.at[first, cols], out.at[pl.ds(0, part_rows)], out_sems.at[0, slot]
+            ),
+            pltpu.make_async_copy(
+                k_scr.at[:, cols], out.at[pl.ds(part_rows, tok_rows)], out_sems.at[1, slot]
+            ),
+            pltpu.make_async_copy(
+                v_scr.at[:, cols], out.at[pl.ds(part_rows + tok_rows, tok_rows)], out_sems.at[2, slot]
+            ),
+        ]
+        if sizes.riding and mask % 2 == 0:
+            stores.append(
+                pltpu.make_async_copy(
+                    share_scr, out.at[pl.ds(sizes.rows, sizes.ride_rows)], out_sems.at[3, slot]
+                )
+            )
+    for store in stores:
+        store.start()
+    for store in stores:
+        store.wait()
+
+
+def pack(sizes, masks, place, queries, keys, values, patch_embed):
+    tok_rows, full = queries.shape[1:]
+    return pl.pallas_call(
+        functools.partial(pack_kernel, sizes, masks),
+        out_shape=[
+            jax.ShapeDtypeStruct((sizes.piece_rows(mask), sizes.width), BF16) for mask in masks
+        ],
+        in_specs=[SMEM_SPEC] + [HBM_SPEC] * 4,
+        out_specs=[HBM_SPEC] * len(masks),
+        scratch_shapes=[pltpu.VMEM((tok_rows, full), BF16)] * 3
+        + [
+            pltpu.VMEM((sizes.share,) + patch_embed.shape[1:], BF16),
+            pltpu.VMEM((max(16, sizes.ride_rows), sizes.width), BF16),
+            pltpu.SemaphoreType.DMA((4,)),
+            pltpu.SemaphoreType.DMA((4, len(masks))),
+        ],
+        compiler_params=limits(),
         cost_estimate=pl.CostEstimate(
-            flops=0, bytes_accessed=4 * len(masks) * rows * width, transcendentals=0
+            flops=0, bytes_accessed=12 * tok_rows * full, transcendentals=0
         ),
-    )(place, *arrays)
-
-
-def attend_kernel(masks, query_parts, part_rows, tok_rows, heads, place_ref, *refs):
-    count = len(masks)
+    )(place, queries, keys, values, patch_embed)
+
+
+def collect_kernel(sizes, count, *refs):
+    in_refs, out_ref, sems = refs[:count], refs[-2], refs[-1]
+    copies = [
+        pltpu.make_async_copy(
+            ref.at[pl.ds(sizes.rows, sizes.ride_rows)], out_ref.at[slot], sems.at[slot]
+        )
+        for slot, ref in enumerate(in_refs)
+    ]
+    for copy in copies:
+        copy.start()
+    for copy in copies:
+        copy.wait()
+
+
+def collect(sizes, pieces, others):
+    return pl.pallas_call(
+        functools.partial(collect_kernel, sizes, len(pieces)),
+        out_shape=jax.ShapeDtypeStruct((len(pieces), sizes.ride_rows, sizes.width), BF16),
+        in_specs=[HBM_SPEC] * (len(pieces) + len(others)),
+        out_specs=VMEM_SPEC,
+        scratch_shapes=[pltpu.SemaphoreType.DMA((len(pieces),))],
+        compiler_params=limits(),
+    )(*pieces, *others)
+
+
+def arrange_kernel(sizes, masks, place_ref, held_ref, got_ref, wait_ref, out_ref):
+    del wait_ref
+    me = place_ref[0]
+    odd = me % 2 == 1
+    local, width = sizes.local, sizes.width
+    for slot, mask in enumerate(masks):
+        pair = jnp.bitwise_xor(me, mask) // 2
+        for chunk in range(sizes.chunks):
+            rows = pl.ds(chunk * sizes.share_rows, sizes.share_rows)
+            held = held_ref[slot, rows, :].astype(F32)
+            got = got_ref[slot, rows, :].astype(F32)
+            first = jnp.where(odd, got, held)
+            second = jnp.where(odd, held, got)
+            for at in range(sizes.share):
+                part = slice(at * local, (at + 1) * local)
+                both = jnp.concatenate([first[part], second[part]], axis=0).astype(BF16)
+                start = pl.multiple_of(at * sizes.count * local + pair * 2 * local, 2 * local)
+                out_ref[pl.ds(start, 2 * local), pl.ds(chunk * width, width)] = both
+
+
+def arrange(sizes, masks, place, held, got, wait):
+    rows = sizes.share * sizes.count * sizes.local
+    return pl.pallas_call(
+        functools.partial(arrange_kernel, sizes, masks),
+        out_shape=jax.ShapeDtypeStruct((rows, VW), BF16),
+        in_specs=[SMEM_SPEC, VMEM_SPEC, VMEM_SPEC, ANY_SPEC],
+        out_specs=VMEM_SPEC,
+        compiler_params=limits(),
+    )(place, held, got, wait)
+
+
+def attend_kernel(sizes, masks, place_ref, *refs):
+    count, heads, width = sizes.count, sizes.heads, sizes.width
+    tok_rows, part_rows = sizes.tok_rows, sizes.part_rows
     in_refs = refs[:count]
-    scale_ref, shift_ref, proj_ref, mod_ref, lat_ref, key_scr, value_scr = refs[count:]
+    scale_ref, shift_ref, proj_ref, mod_ref, lat_ref, *refs = refs[count:]
+    query_scr, key_scr, value_scr, scale_scr, shift_scr, proj_scr, sems, side_sems = refs
     half = part_rows // 2
-    width = heads * HD
     factor = HD ** (-0.5) * math.log2(math.e)
     me = place_ref[0]
     mine = pl.ds(pl.multiple_of(place_ref[2] * width, HD), width)
+    copies = [
+        pltpu.make_async_copy(scale_ref.at[:, mine], scale_scr, side_sems.at[0]),
+        pltpu.make_async_copy(shift_ref.at[:, mine], shift_scr, side_sems.at[1]),
+        pltpu.make_async_copy(proj_ref.at[:, mine], proj_scr, side_sems.at[2]),
+    ]
+    for src in range(count):
+        ref = in_refs[src]
+        rows = pl.ds(src * tok_rows, tok_rows)
+        copies += [
+            pltpu.make_async_copy(ref.at[pl.ds(0, part_rows)], query_scr.at[src], sems.at[0, src]),
+            pltpu.make_async_copy(
+                ref.at[pl.ds(part_rows, tok_rows)], key_scr.at[rows], sems.at[1, src]
+            ),
+        ]
+        for head in range(heads):
+            copies.append(
+                pltpu.make_async_copy(
+                    ref.at[pl.ds(part_rows + tok_rows, tok_rows), pl.ds(head * HD, HD)],
+                    value_scr.at[rows, pl.ds(2 * head * HD, HD)],
+                    sems.at[2 + head, src],
+                )
+            )
+    for copy in copies:
+        copy.start()
     ones = jnp.ones((tok_rows, HD), BF16)
     for src in range(count):
-        rows = pl.ds(src * tok_rows, tok_rows)
-        key_scr[rows, :] = in_refs[src][pl.ds(part_rows, tok_rows), :]
         for head in range(heads):
-            value_scr[rows, pl.ds(2 * head * HD, HD)] = in_refs[src][
-                pl.ds(part_rows + tok_rows, tok_rows), pl.ds(head * HD, HD)
-            ]
-            value_scr[rows, pl.ds((2 * head + 1) * HD, HD)] = ones
-    gain = 1.0 + scale_ref[:, mine]
-    shift = shift_ref[:, mine]
-    proj = proj_ref[:, mine]
+            value_scr[pl.ds(src * tok_rows, tok_rows), pl.ds((2 * head + 1) * HD, HD)] = ones
+    for copy in copies:
+        copy.wait()
+    gain = 1.0 + scale_scr[...]
+    shift = shift_scr[...]
+    proj = proj_scr[...]
     zero = jnp.zeros_like(proj)
     proj_pair = jnp.concatenate(
         [jnp.concatenate([proj, zero], axis=1), jnp.concatenate([zero, proj], axis=1)], axis=0
@@ -95,8 +247,7 @@
         mixed = []
         for head in range(heads):
             cols = pl.ds(head * HD, HD)
-            query = in_refs[src][pl.ds(0, part_rows), cols]
-            logits = mm_nt(query, key_scr[:, cols])
+            logits = mm_nt(query_scr[src, :, cols], key_scr[:, cols])
             top = jnp.max(logits, axis=-1, keepdims=True)
             weights = jnp.exp2((logits - top) * factor).astype(BF16)
             both = mm(weights, value_scr[:, pl.ds(2 * head * HD, 2 * HD)])
@@ -109,25 +260,29 @@
         lat_ref[place] = mm_nt(pair, proj_pair).astype(BF16)
 
 
-def attend(place, masks, received, scales, shifts, proj, query_parts, part_rows, tok_rows, heads):
-    count = len(received)
-    width = heads * HD
-    lat_rows = count * tok_rows
-    query_rows = count * part_rows
-    vmem = pl.BlockSpec(memory_space=pltpu.VMEM)
-    return pl.pallas_call(
-        functools.partial(attend_kernel, masks, query_parts, part_rows, tok_rows, heads),
+def attend(sizes, masks, place, received, scales, shifts, proj):
+    count, width, heads = sizes.count, sizes.width, sizes.heads
+    lat_rows = count * sizes.tok_rows
+    query_rows = count * sizes.part_rows
+    return pl.pallas_call(
+        functools.partial(attend_kernel, sizes, masks),
         out_shape=(
-            jax.ShapeDtypeStruct((count, part_rows, width), BF16),
-            jax.ShapeDtypeStruct((count, part_rows // 2, 2 * CH), BF16),
+            jax.ShapeDtypeStruct((count, sizes.part_rows, width), BF16),
+            jax.ShapeDtypeStruct((count, sizes.part_rows // 2, 2 * CH), BF16),
         ),
-        in_specs=[pl.BlockSpec(memory_space=pltpu.SMEM)] + [vmem] * (count + 3),
-        out_specs=(vmem, vmem),
+        in_specs=[SMEM_SPEC] + [HBM_SPEC] * (count + 3),
+        out_specs=(VMEM_SPEC, VMEM_SPEC),
         scratch_shapes=[
+            pltpu.VMEM((count, sizes.part_rows, width), BF16),
             pltpu.VMEM((lat_rows, width), BF16),
             pltpu.VMEM((lat_rows, 2 * width), BF16),
+            pltpu.VMEM((1, width), F32),
+            pltpu.VMEM((1, width), F32),
+            pltpu.VMEM((CH, width), BF16),
+            pltpu.SemaphoreType.DMA((2 + heads, count)),
+            pltpu.SemaphoreType.DMA((3,)),
         ],
-        compiler_params=pltpu.CompilerParams(vmem_limit_bytes=VMEM_LIMIT),
+        compiler_params=limits(),
         cost_estimate=pl.CostEstimate(
             flops=4 * query_rows * lat_rows * width,
             bytes_accessed=2 * (query_rows * 2 + lat_rows * 2) * width,
@@ -149,13 +304,12 @@
 
 
 def total_copies(arrays, copies):
-    vmem = pl.BlockSpec(memory_space=pltpu.VMEM)
     return pl.pallas_call(
         functools.partial(total_kernel, copies),
         out_shape=jax.ShapeDtypeStruct((copies,) + arrays[0].shape[-2:], BF16),
-        in_specs=[vmem] * len(arrays),
-        out_specs=vmem,
-        compiler_params=pltpu.CompilerParams(vmem_limit_bytes=VMEM_LIMIT),
+        in_specs=[VMEM_SPEC] * len(arrays),
+        out_specs=VMEM_SPEC,
+        compiler_params=limits(),
     )(*arrays)
 
 
@@ -165,8 +319,9 @@
 
 def head_kernel(grid_rows, fused, embed_masks, out_factor, place_ref, lat_ref, *refs):
     embed_refs, refs = refs[: len(embed_masks)], refs[len(embed_masks) :]
-    pos_ref, pre_ref, post_ref, prompt_ref, cot_ref, mod_ref, *refs = refs
-    reward_ref, grad_ref, weight_ref, lat_scr, grad_scr, embed_ref, sems = refs
+    sides, refs = refs[:4], refs[4:]
+    cot_ref, mod_ref, reward_ref, grad_ref, weight_ref, lat_scr, grad_scr, embed_ref, *refs = refs
+    pos_ref, pre_ref, post_ref, prompt_ref, sems, side_sems = refs
     patch_rows = grid_rows // 4
     patch_cols = GW // 4
     patches = patch_rows * patch_cols
@@ -177,7 +332,10 @@
         copies.append(
             pltpu.make_async_copy(embed_refs[slot], embed_ref.at[pl.ds(first, rows)], sems.at[slot])
         )
-        copies[-1].start()
+    for slot, (side, scr) in enumerate(zip(sides, (pos_ref, pre_ref, post_ref, prompt_ref))):
+        copies.append(pltpu.make_async_copy(side, scr, side_sems.at[slot]))
+    for copy in copies:
+        copy.start()
     lat_scr[...] = lat_ref[...].astype(F32)
     for copy in copies:
         copy.wait()
@@ -216,7 +374,7 @@
     prompt_len = jnp.sqrt(prompt_sq)
     cosine = dot / (final_len * prompt_len)
     reward_ref[...] = jnp.broadcast_to(100.0 * cosine, reward_ref.shape)
-    cot = cot_ref[...]
+    cot = cot_ref[0]
     final_grad = (100.0 * cot) * (prompt / (final_len * prompt_len) - final * (cosine / final_sq))
     unit_grad = final_grad * post
     pooled_grad = pooled_rstd * (
@@ -260,8 +418,6 @@
     rows = grid_rows * GW // 2
     width = modulated.shape[2]
     embed_arrays, embed_masks = [x for x, _ in embed], [mask for _, mask in embed]
-    vmem = pl.BlockSpec(memory_space=pltpu.VMEM)
-    anywhere = pl.BlockSpec(memory_space=pl.ANY)
     return pl.pallas_call(
         functools.partial(head_kernel, grid_rows, fused, embed_masks, out_factor),
         out_shape=(
@@ -269,17 +425,23 @@
             jax.ShapeDtypeStruct((rows, 2 * CH), BF16),
             jax.ShapeDtypeStruct((CH, width), BF16),
         ),
-        in_specs=[pl.BlockSpec(memory_space=pltpu.SMEM), vmem]
-        + [anywhere] * len(embed_arrays)
-        + [vmem] * 6,
-        out_specs=(vmem, vmem, vmem),
+        in_specs=[SMEM_SPEC, VMEM_SPEC]
+        + [ANY_SPEC] * len(embed_arrays)
+        + [HBM_SPEC] * 4
+        + [SMEM_SPEC, VMEM_SPEC],
+        out_specs=(VMEM_SPEC, VMEM_SPEC, VMEM_SPEC),
         scratch_shapes=[
             pltpu.VMEM((rows, 2 * CH), F32),
             pltpu.VMEM((rows, 2 * CH), F32),
             pltpu.VMEM((16 * CH, VW), BF16),
+            pltpu.VMEM((patches, VW), BF16),
+            pltpu.VMEM((1, VW), F32),
+            pltpu.VMEM((1, VW), F32),
+            pltpu.VMEM((1, VW), F32),
             pltpu.SemaphoreType.DMA((len(embed_arrays),)),
+            pltpu.SemaphoreType.DMA((4,)),
         ],
-        compiler_params=pltpu.CompilerParams(vmem_limit_bytes=VMEM_LIMIT),
+        compiler_params=limits(),
         cost_estimate=pl.CostEstimate(
             flops=6 * patches * 16 * CH * VW,
             bytes_accessed=2 * 16 * CH * VW + 2 * patches * VW,
@@ -306,13 +468,12 @@
 
 
 def spread(place, grad, scales, proj, count, half, heads):
-    vmem = pl.BlockSpec(memory_space=pltpu.VMEM)
     return pl.pallas_call(
         functools.partial(spread_kernel, count, half, heads),
         out_shape=jax.ShapeDtypeStruct((1, heads, 2 * count * half, HD), BF16),
-        in_specs=[pl.BlockSpec(memory_space=pltpu.SMEM)] + [vmem] * 3,
-        out_specs=vmem,
-        compiler_params=pltpu.CompilerParams(vmem_limit_bytes=VMEM_LIMIT),
+        in_specs=[SMEM_SPEC] + [VMEM_SPEC] * 3,
+        out_specs=VMEM_SPEC,
+        compiler_params=limits(),
         cost_estimate=pl.CostEstimate(
             flops=8 * count * half * CH * heads * HD,
             bytes_accessed=4 * count * half * heads * HD,
@@ -326,13 +487,12 @@
 
 
 def weight_call(grad, modulated, out_factor):
-    vmem = pl.BlockSpec(memory_space=pltpu.VMEM)
     return pl.pallas_call(
         functools.partial(weight_kernel, out_factor),
         out_shape=jax.ShapeDtypeStruct((CH, modulated.shape[2]), BF16),
-        in_specs=[vmem] * 2,
-        out_specs=vmem,
-        compiler_params=pltpu.CompilerParams(vmem_limit_bytes=VMEM_LIMIT),
+        in_specs=[VMEM_SPEC] * 2,
+        out_specs=VMEM_SPEC,
+        compiler_params=limits(),
     )(grad, modulated)
 
 
@@ -343,13 +503,12 @@
 
 
 def finish(blocks):
-    vmem = pl.BlockSpec(memory_space=pltpu.VMEM)
     return pl.pallas_call(
         finish_kernel,
         out_shape=jax.ShapeDtypeStruct((CH, HEADS * HD), F32),
-        in_specs=[vmem],
-        out_specs=vmem,
-        compiler_params=pltpu.CompilerParams(vmem_limit_bytes=VMEM_LIMIT),
+        in_specs=[VMEM_SPEC],
+        out_specs=VMEM_SPEC,
+        compiler_params=limits(),
     )(blocks)
 
 
@@ -364,46 +523,16 @@
     )
 
 
-def ring_gather(block):
-    count = lax.axis_size("seq")
-    me = lax.axis_index("seq")
-    order = list(range(0, count, 2)) + list(range(count - 1, 0, -2))
-    ahead = [(order[i], order[(i + 1) % count]) for i in range(count)]
-    behind = [(b, a) for a, b in ahead]
-    spot = jnp.where(me % 2 == 0, me // 2, count - 1 - me // 2)
-
-    def place_of(at):
-        at = (at + count) % count
-        return jnp.where(at < count // 2, 2 * at, 2 * (count - 1 - at) + 1)
-
-    def put(held, piece, at):
-        return lax.dynamic_update_slice_in_dim(held, piece[:, None], place_of(at), 1)
-
-    def step(t, carry):
-        up, down, held = carry
-        up = lax.ppermute(up, "seq", ahead)
-        down = lax.ppermute(down, "seq", behind)
-        held = put(held, up, spot - t - 1)
-        held = put(held, down, spot + t + 1)
-        return up, down, held
-
-    held = jnp.zeros((block.shape[0], count) + block.shape[1:], block.dtype)
-    held = put(held, block, spot)
-    held = lax.fori_loop(0, count // 2, step, (block, block, held))[2]
-    return held.reshape(-1, block.shape[2])
-
-
 def after_kernel(*refs):
     del refs
 
 
 def after(x, others):
-    anywhere = pl.BlockSpec(memory_space=pl.ANY)
     return pl.pallas_call(
         after_kernel,
         out_shape=jax.ShapeDtypeStruct(x.shape, x.dtype),
-        in_specs=[anywhere] * (1 + len(others)),
-        out_specs=anywhere,
+        in_specs=[ANY_SPEC] * (1 + len(others)),
+        out_specs=ANY_SPEC,
         input_output_aliases={0: 0},
     )(x, *others)
 
@@ -425,14 +554,12 @@
     seq_count = lax.axis_size("seq")
     data_count = lax.axis_size("dp")
     tok_rows = queries.shape[1]
-    query_parts = max(1, seq_count // HEADS)
-    head_count = max(1, HEADS // seq_count)
+    sizes = Sizes(seq_count, data_count, tok_rows, patch_embed)
+    query_parts, head_count, part_rows = sizes.query_parts, sizes.heads, sizes.part_rows
     group_count = HEADS // head_count
-    width = head_count * HD
     seq_index = lax.axis_index("seq")
     head_group = seq_index // query_parts
     query_part = seq_index % query_parts
-    part_rows = tok_rows // query_parts
     half = part_rows // 2
     lat_rows = seq_count * tok_rows
     grid_rows = lat_rows // GW
@@ -441,34 +568,50 @@
     proj_turned = proj_out.T
     out_factor = 1.0 / math.sqrt(data_count * lat_rows)
 
-    sizes = (query_parts, part_rows, tok_rows, width)
-    positions = patch_embed.shape[0]
-    share = positions // data_count if positions % data_count == 0 else 0
-    share_shape = (share or positions,) + patch_embed.shape[1:]
-    masks = list(range(seq_count - 1, -1, -1))
-    embed_share, *pieces = pack_call(
-        functools.partial(pack_kernel, sizes, masks, share),
-        sizes, masks, share_shape, place, (queries, keys, values, patch_embed),
+    masks = [1, 2] + list(range(seq_count - 1, 2, -1)) + [0]
+    pieces = pack(
+        sizes, masks, place, in_hbm(queries), in_hbm(keys), in_hbm(values), in_hbm(patch_embed)
     )
     received = [swap(piece, "seq", mask) if mask else piece for mask, piece in zip(masks, pieces)]
-    embed_mine = after(ring_gather(embed_share), received[:-1])
-    embed_bits = [1 << b for b in reversed(range(data_count.bit_length() - 1))] if share else []
-    embed = [(embed_mine, 0)]
-    for bit in embed_bits[:1]:
-        embed = embed + [(swap(x, "dp", bit), m ^ bit) for x, m in embed]
+    bits = [1 << b for b in reversed(range(data_count.bit_length() - 1))]
+    shared = sizes.share < patch_embed.shape[0]
+    if sizes.riding:
+        even = [slot for slot, mask in enumerate(masks) if mask % 2 == 0]
+        others = [slot for slot, mask in enumerate(masks) if mask % 2]
+        held = collect(
+            sizes, [received[slot] for slot in even], [received[slot] for slot in others]
+        )
+        got = swap(held, "seq", 1)
+        far_held = swap(held, "dp", bits[0]) if shared else None
 
     modulated, latent_part = attend(
-        place, masks, received, scales, shifts, proj_turned,
-        query_parts, part_rows, tok_rows, head_count,
+        sizes, masks, place, received, in_hbm(scales), in_hbm(shifts), in_hbm(proj_turned)
     )
+
+    if sizes.riding:
+        got = after(got, [modulated])
+        even_masks = [masks[slot] for slot in even]
+        embed = [(arrange(sizes, even_masks, place, held, got, modulated), 0)]
+        far_got = swap(got, "dp", bits[0]) if shared else None
+    else:
+        mine = patch_embed
+        if shared:
+            mine = lax.dynamic_slice_in_dim(
+                patch_embed, lax.axis_index("dp") * sizes.share, sizes.share, 0
+            )
+        mine = lax.all_gather(mine, "seq", axis=1, tiled=True).reshape(-1, VW)
+        embed = [(mine, 0)]
+        if shared:
+            embed = embed + [(swap(mine, "dp", bits[0]), bits[0])]
 
     groups = None
     if query_parts > 1:
         groups = [[g * query_parts + r for g in range(group_count)] for r in range(query_parts)]
     per_share = seq_count // group_count
     pieces = all_to_all(latent_part.reshape(group_count, per_share * half, 2 * CH), groups)
-    embed = [embed[0]] + [(after(x, [pieces]), m) for x, m in embed[1:]]
-    for bit in embed_bits[1:]:
+    if sizes.riding and shared:
+        embed.append((arrange(sizes, even_masks, place, far_held, far_got, pieces), bits[0]))
+    for bit in bits[1:] if shared else []:
         embed = embed + [(swap(x, "dp", bit), m ^ bit) for x, m in embed]
     latent = all_to_all(total_copies([pieces], seq_count))
     if canonical:
@@ -479,8 +622,8 @@
         latent = latent.transpose(0, 2, 1, 3).reshape(lat_rows // 2, 2 * CH)
 
     reward, grad, weight = reward_head(
-        place, latent, embed, pos_embed, pre_gain[None], post_gain[None], prompt,
-        cotangent[None], modulated, grid_rows, canonical, out_factor,
+        place, latent, embed, in_hbm(pos_embed), pre_gain[None], post_gain[None], in_hbm(prompt),
+        cotangent, modulated, grid_rows, canonical, out_factor,
     )
     if not canonical:
         tokens = grad.reshape(grid_rows // 2, GW, 2, CH).transpose(0, 2, 1, 3)

time: 135 us -> 115 us (0.85)
  starting transfers between devices: 46.7 us -> 32.3 us
  local copies, waits for them, and re-layouts: 15.7 us -> 2.52 us
  Pallas kernels: 16.1 us -> 22.9 us
    ppermute x13 -> x15, waiting for transfers between devices: 8.57 us -> 34.4 us  [swap(): return lax.ppermute(x, axis, [(i, i ^ mask) for i in range(count)])]
    ppermute x8 -> x0, waiting for transfers between devices: 22.9 us -> none  [the longest x4 13.6 us: step(): down = lax.ppermute(down, 'seq', behind)]
    ppermute x8 -> x0, starting transfers between devices: 20.8 us -> none  [the longest x4 14.8 us: step(): up = lax.ppermute(up, 'seq', ahead)]
    unnamed x65 -> x16, local copies, waits for them, and re-layouts: 14.6 us -> 2.5 us
    pallas_call x2 -> x5, Pallas kernels: 8.09 us -> 13.9 us  [the longest x1 9.12 us: attend(): pl.pallas_call(functools.partial(attend_kernel, sizes, masks), out_shape=...]
    ppermute x13 -> x15, starting transfers between devices: 15.6 us -> 20.5 us  [swap(): return lax.ppermute(x, axis, [(i, i ^ mask) for i in range(count)])]
    all_to_all x3, waiting for transfers between devices: 22.1 us -> 20.5 us  [all_to_all(): lax.all_to_all(x, 'seq', split_axis=0, concat_axis=0, tiled=True, axis_in...]
    all_to_all x3, starting transfers between devices: 10.3 us -> 11.8 us  [all_to_all(): lax.all_to_all(x, 'seq', split_axis=0, concat_axis=0, tiled=True, axis_in...]
  transfers between devices with their start and end apart: 24 -> 18, of which waited for: 16 -> 7; matrix products, arithmetic and copies ran while one was open for 1% -> 0% of each run, Pallas kernels for 7% -> 11%
where the time goes in v4:
time: 115 us; the launch traced here: 114 us
  waiting for transfers between devices  54.9 us (48%)
  starting transfers between devices  32.3 us (28%)
  Pallas kernels  22.9 us (20%)
  local copies, waits for them, and re-layouts  2.52 us (2%)
  between operations  1.48 us (1%)
    ppermute x15, waiting for transfers between devices, swap(): return lax.ppermute(x, axis, [(i, i ^ mask) for i in range(count)])  34.4 us
    ppermute x15, starting transfers between devices, swap(): return lax.ppermute(x, axis, [(i, i ^ mask) for i in range(count)])  20.5 us
    all_to_all x3, waiting for transfers between devices, all_to_all(): lax.all_to_all(x, 'seq', split_axis=0, concat_axis=0, tiled=True, axis_in...  20.5 us
    all_to_all x3, starting transfers between devices, all_to_all(): lax.all_to_all(x, 'seq', split_axis=0, concat_axis=0, tiled=True, axis_in...  11.8 us
    pallas_call x1, Pallas kernels, attend(): pl.pallas_call(functools.partial(attend_kernel, sizes, masks), out_shape=...  9.12 us
    pallas_call x1, Pallas kernels, reward_head(): pl.pallas_call(functools.partial(head_kernel, grid_rows, fused, embed_mas...  5.11 us
    pallas_call x1, Pallas kernels, pack(): pl.pallas_call(functools.partial(pack_kernel, sizes, masks), out_shape=[j...  2.99 us
    unnamed x16, local copies, waits for them, and re-layouts  2.5 us
  transfers between devices with their start and end apart: 18, of which 7 were waited for; matrix products, arithmetic and copies ran while one was open for 0% of the time, Pallas kernels for 11%

profile of v4, /device:TPU:0, one launch (start us, length us, event | category | flops | bytes accessed | tf_op | source)
XLA Modules:
  0.0 114.2 jit_solution(12607294586585556389)
XLA Ops:
  0.7 3.0 %shard_map.139 = (bf16[384,256]{1,0:T(8,128)(2,1)S(1)}, bf16[544,256]{1,0:T(8,128)(2,1)S(1)}, bf16[384,256]{1,0:T(8,128)(2,1)S(1)}, bf16[544,256]{1,0:T(8,128)(2...) custom-call(s32[3]{0:T(128)S(1)} %pad_add_fusion.place_ref, ...), custom_call_target="tpu_custom_call" | custom-call | bytes 3145728 | tf_op jit(solution)/shard_map/pallas_call | solution.py:122
  3.7 3.0 %collective-permute-start = (bf16[384,256]{1,0:T(8,128)(2,1)S(1)}, bf16[384,256]{1,0:T(8,128)(2,1)S(1)}, u32[]{:S(2)}, u32[]{:S(2)}) collective-permute-start(bf16[384,256]{1,0:T(8,128)(2,1)S(1)} %get-tuple-element.16), channel_id=1, source_target_pairs={{0,4},{4,0},{8,12},{12,8},{16,20},{20,16},{24,28},{28,24},{1,5},{5... | collective-permute-start | bytes 589832 | tf_op jit(solution)/shard_map/ppermute | solution.py:517
  6.7 3.5 %collective-permute-start.2 = (bf16[384,256]{1,0:T(8,128)(2,1)S(1)}, bf16[384,256]{1,0:T(8,128)(2,1)S(1)}, u32[]{:S(2)}, u32[]{:S(2)}) collective-permute-start(bf16[384,256]{1,0:T(8,128)(2,1)S(1)} %get-tuple-element.18), channel_id=1, source_target_pairs={{0,28},{4,24},{8,20},{12,16},{16,12},{20,8},{24,4},{28,0},{1,29},{... | collective-permute-start | bytes 589832 | tf_op jit(solution)/shard_map/ppermute | solution.py:517
  10.3 0.9 collective-permute-start.3
  11.2 2.6 %collective-permute-start.5 = (bf16[544,256]{1,0:T(8,128)(2,1)S(1)}, bf16[544,256]{1,0:T(8,128)(2,1)S(1)}, u32[]{:S(2)}, u32[]{:S(2)}) collective-permute-start(bf16[544,256]{1,0:T(8,128)(2,1)S(1)} %get-tuple-element.21), channel_id=1, source_target_pairs={{0,16},{4,20},{8,24},{12,28},{16,0},{20,4},{24,8},{28,12},{1,17},{... | collective-permute-start | bytes 835592 | tf_op jit(solution)/shard_map/ppermute | solution.py:517
  13.8 1.2 %collective-permute-done.refs_0_.refs_4_ = bf16[384,256]{1,0:T(8,128)(2,1)S(1)} collective-permute-done((bf16[384,256]{1,0:T(8,128)(2,1)S(1)}, bf16[384,256]{1,0:T(8,128)(2,1)S(1)}, u32[]{:S(2)}, u32[]{:S(2)}) %collective-permute-start) | collective-permute-done | bytes 196640 | tf_op jit(solution)/shard_map/ppermute | solution.py:517
  15.0 2.6 %collective-permute-start.4 = (bf16[384,256]{1,0:T(8,128)(2,1)S(1)}, bf16[384,256]{1,0:T(8,128)(2,1)S(1)}, u32[]{:S(2)}, u32[]{:S(2)}) collective-permute-start(bf16[384,256]{1,0:T(8,128)(2,1)S(1)} %get-tuple-element.20), channel_id=1, source_target_pairs={{0,20},{4,16},{8,28},{12,24},{16,4},{20,0},{24,12},{28,8},{1,21},{... | collective-permute-start | bytes 589832 | tf_op jit(solution)/shard_map/ppermute | solution.py:517
  17.6 3.2 %collective-permute-start.6 = (bf16[384,256]{1,0:T(8,128)(2,1)S(1)}, bf16[384,256]{1,0:T(8,128)(2,1)S(1)}, u32[]{:S(2)}, u32[]{:S(2)}) collective-permute-start(bf16[384,256]{1,0:T(8,128)(2,1)S(1)} %get-tuple-element.22), channel_id=1, source_target_pairs={{0,12},{4,8},{8,4},{12,0},{16,28},{20,24},{24,20},{28,16},{1,13},{... | collective-permute-start | bytes 589832 | tf_op jit(solution)/shard_map/ppermute | solution.py:517
  20.8 30.7 %collective-permute-done.4.refs_4_.refs_6_ = bf16[384,256]{1,0:T(8,128)(2,1)S(1)} collective-permute-done((bf16[384,256]{1,0:T(8,128)(2,1)S(1)}, bf16[384,256]{1,0:T(8,128)(2,1)S(1)}, u32[]{:S(2)}, u32[]{:S(2)}) %collective-permute-start.4) | collective-permute-done | bytes 196640 | tf_op jit(solution)/shard_map/ppermute | solution.py:517
  52.6 1.5 %collective-permute-start.8 = (bf16[4,160,256]{2,1,0:T(8,128)(2,1)S(1)}, bf16[4,160,256]{2,1,0:T(8,128)(2,1)S(1)}, u32[]{:S(2)}, u32[]{:S(2)}) collective-permute-start(bf16[4,160,256]{2,1,0:T(8,128)(2,1)S(1)} %shard_map.142.held_ref), channel_id=1, source_target_pairs={{0,2},{1,3},{2,0},{3,1},{4,6},{5,7},{6,4},{7,5},{8,10},{9,11},{10,... | collective-permute-start | bytes 983048 | tf_op jit(solution)/shard_map/ppermute | solution.py:517
  54.1 9.1 %shard_map.140 = (bf16[8,128,256]{2,1,0:T(8,128)(2,1)S(1)}, bf16[8,64,128]{2,1,0:T(8,128)(2,1)}) custom-call(s32[3]{0:T(128)S(1)} %pad_add_fusion.place_ref, bf16[384,256]{1,0:T(8,128)(2,1)S(1)} %collective-permute-done.refs_0_.refs_4_, bf16[544,256]{1,0:T(8,128)(2,1)S(1)} %collective-permute-done.1.refs_1_.refs_0_, ...), custom_call_target="tpu_custom_call" | custom-call | flops 1073741824 | bytes 2097152 | tf_op jit(solution)/shard_map/pallas_call | solution.py:267
  63.2 0.8 copy-done
  65.3 4.7 %all-to-all-start = ((bf16[8,64,128]{2,1,0:T(8,128)(2,1)}), bf16[8,64,128]{2,1,0:T(8,128)(2,1)S(1)}, u32[]{:S(2)}, u32[]{:S(2)}) async-start(bf16[8,64,128]{2,1,0:T(8,128)(2,1)} %get-tuple-element.24), calls=%async_computation | async-start | bytes 262144 | tf_op jit(solution)/shard_map/all_to_all | solution.py:521
  70.1 1.0 copy-done.3
  71.8 5.6 %all-to-all-done.refs_0_.wait_ref = bf16[8,64,128]{2,1,0:T(8,128)(2,1)S(1)} async-done(((bf16[8,64,128]{2,1,0:T(8,128)(2,1)}), bf16[8,64,128]{2,1,0:T(8,128)(2,1)S(1)}, u32[]{:S(2)}, u32[]{:S(2)}) %all-to-all-start) | async-done | bytes 131104 | tf_op jit(solution)/shard_map/all_to_all | solution.py:521
  78.8 3.5 %all-to-all-start.1 = ((bf16[8,64,128]{2,1,0:T(8,128)(2,1)}), bf16[8,64,128]{2,1,0:T(8,128)(2,1)S(1)}, u32[]{:S(2)}, u32[]{:S(2)}) async-start(bf16[8,64,128]{2,1,0:T(8,128)(2,1)} %shard_map.141), calls=%async_computation.1 | async-start | bytes 262144 | tf_op jit(solution)/shard_map/all_to_all | solution.py:521
  83.1 7.1 %all-to-all-done.1 = bf16[8,64,128]{2,1,0:T(8,128)(2,1)S(1)} async-done(((bf16[8,64,128]{2,1,0:T(8,128)(2,1)}), bf16[8,64,128]{2,1,0:T(8,128)(2,1)S(1)}, u32[]{:S(2)}, u32[]{:S(2)}) %all-to-all-start.1) | async-done | bytes 131104 | tf_op jit(solution)/shard_map/all_to_all | solution.py:521
  90.2 5.1 %shard_map.146 = (f32[1,128]{1,0:T(1,128)}, bf16[512,128]{1,0:T(8,128)(2,1)S(1)}, bf16[64,256]{1,0:T(8,128)(2,1)S(1)}) custom-call(s32[3]{0:T(128)S(1)} %pad_add_fusion.place_ref, bf16[512,128]{1,0:T(8,128)(2,1)S(1)} %bitcast.7, bf16[256,1280]{1,0:T(8,128)(2,1)S(1)} %shard_map.144.refs_0_, bf16[256,1280]{1,0:T(8,128)(2,1)S(1)} %shard_map.145.refs_1_, ...), custom_call_target="tpu_custom_call" | custom-call | flops 503316480 | bytes 2785280 | tf_op jit(solution)/shard_map/pallas_call | solution.py:421
  95.7 1.2 %collective-permute-start.13 = (bf16[64,256]{1,0:T(8,128)(2,1)S(1)}, bf16[64,256]{1,0:T(8,128)(2,1)S(1)}, u32[]{:S(2)}, u32[]{:S(2)}) collective-permute-start(bf16[64,256]{1,0:T(8,128)(2,1)S(1)} %get-tuple-element.28.refs_0_), channel_id=1, source_target_pairs={{0,2},{1,3},{2,0},{3,1},{4,6},{5,7},{6,4},{7,5},{8,10},{9,11},{10,... | collective-permute-start | bytes 98312 | tf_op jit(solution)/shard_map/ppermute | solution.py:517
  97.3 1.8 %collective-permute-done.14.refs_3_ = bf16[64,256]{1,0:T(8,128)(2,1)S(1)} collective-permute-done((bf16[64,256]{1,0:T(8,128)(2,1)S(1)}, bf16[64,256]{1,0:T(8,128)(2,1)S(1)}, u32[]{:S(2)}, u32[]{:S(2)}) %collective-permute-start.14) | collective-permute-done | bytes 32800 | tf_op jit(solution)/shard_map/ppermute | solution.py:517
  100.4 3.5 %all-to-all-start.2 = ((bf16[8,64,256]{2,1,0:T(8,128)(2,1)}), bf16[8,64,256]{2,1,0:T(8,128)(2,1)S(1)}, u32[]{:S(2)}, u32[]{:S(2)}) async-start(bf16[8,64,256]{2,1,0:T(8,128)(2,1)} %shard_map.148), calls=%async_computation.2 | async-start | bytes 524288 | tf_op jit(solution)/shard_map/all_to_all | solution.py:521
  104.0 1.6 %shard_map.147 = bf16[1,2,1024,128]{3,2,1,0:T(8,128)(2,1)} custom-call(s32[3]{0:T(128)S(1)} %pad_add_fusion.place_ref, bf16[512,128]{1,0:T(8,128)(2,1)S(1)} %get-tuple-element.27.grad_ref, f32[1,2048]{1,0:T(1,128)S(1)} %copy-done.5, bf16[64,2048]{1,0:T(8,128)(2,1)S(1)} %bitcast.9), custom_call_target="tpu_custom_call" | custom-call | flops 67108864 | bytes 524288 | tf_op jit(solution)/shard_map/pallas_call | solution.py:471
  105.6 7.8 %all-to-all-done.2.in_ref = bf16[8,64,256]{2,1,0:T(8,128)(2,1)S(1)} async-done(((bf16[8,64,256]{2,1,0:T(8,128)(2,1)}), bf16[8,64,256]{2,1,0:T(8,128)(2,1)S(1)}, u32[]{:S(2)}, u32[]{:S(2)}) %all-to-all-start.2) | async-done | bytes 262176 | tf_op jit(solution)/shard_map/all_to_all | solution.py:521
  113.4 0.8 shard_map.149
  (42 shorter events, 6.7 us)
Async XLA Ops:
  3.7 11.3 %collective-permute-start = (bf16[384,256]{1,0:T(8,128)(2,1)S(1)}, bf16[384,256]{1,0:T(8,128)(2,1)S(1)}, u32[]{:S(2)}, u32[]{:S(2)}) collective-permute-start(bf16[384,256]{1,0:T(8,128)(2,1)S(1)} %get-tuple-element.16), channel_id=1, source_target_pairs={{0,4},{4,0},{8,12},{12,8},{16,20},{20,16},{24,28},{28,24},{1,5},{5... | collective-permute-start | bytes 589832 | tf_op jit(solution)/shard_map/ppermute | solution.py:517
  6.7 10.8 %collective-permute-start.2 = (bf16[384,256]{1,0:T(8,128)(2,1)S(1)}, bf16[384,256]{1,0:T(8,128)(2,1)S(1)}, u32[]{:S(2)}, u32[]{:S(2)}) collective-permute-start(bf16[384,256]{1,0:T(8,128)(2,1)S(1)} %get-tuple-element.18), channel_id=1, source_target_pairs={{0,28},{4,24},{8,20},{12,16},{16,12},{20,8},{24,4},{28,0},{1,29},{... | collective-permute-start | bytes 589832 | tf_op jit(solution)/shard_map/ppermute | solution.py:517
  10.3 41.2 %collective-permute-start.1 = (bf16[544,256]{1,0:T(8,128)(2,1)S(1)}, bf16[544,256]{1,0:T(8,128)(2,1)S(1)}, u32[]{:S(2)}, u32[]{:S(2)}) collective-permute-start(bf16[544,256]{1,0:T(8,128)(2,1)S(1)} %get-tuple-element.17), channel_id=1, source_target_pairs={{0,8},{4,12},{8,0},{12,4},{16,24},{20,28},{24,16},{28,20},{1,9},{5... | collective-permute-start | bytes 835592 | tf_op jit(solution)/shard_map/ppermute | solution.py:517
  10.3 41.2 %collective-permute-start.3 = (bf16[544,256]{1,0:T(8,128)(2,1)S(1)}, bf16[544,256]{1,0:T(8,128)(2,1)S(1)}, u32[]{:S(2)}, u32[]{:S(2)}) collective-permute-start(bf16[544,256]{1,0:T(8,128)(2,1)S(1)} %get-tuple-element.19), channel_id=1, source_target_pairs={{0,24},{4,28},{8,16},{12,20},{16,8},{20,12},{24,0},{28,4},{1,25},{... | collective-permute-start | bytes 835592 | tf_op jit(solution)/shard_map/ppermute | solution.py:517
  11.2 40.4 %collective-permute-start.5 = (bf16[544,256]{1,0:T(8,128)(2,1)S(1)}, bf16[544,256]{1,0:T(8,128)(2,1)S(1)}, u32[]{:S(2)}, u32[]{:S(2)}) collective-permute-start(bf16[544,256]{1,0:T(8,128)(2,1)S(1)} %get-tuple-element.21), channel_id=1, source_target_pairs={{0,16},{4,20},{8,24},{12,28},{16,0},{20,4},{24,8},{28,12},{1,17},{... | collective-permute-start | bytes 835592 | tf_op jit(solution)/shard_map/ppermute | solution.py:517
  15.0 36.5 %collective-permute-start.4 = (bf16[384,256]{1,0:T(8,128)(2,1)S(1)}, bf16[384,256]{1,0:T(8,128)(2,1)S(1)}, u32[]{:S(2)}, u32[]{:S(2)}) collective-permute-start(bf16[384,256]{1,0:T(8,128)(2,1)S(1)} %get-tuple-element.20), channel_id=1, source_target_pairs={{0,20},{4,16},{8,28},{12,24},{16,4},{20,0},{24,12},{28,8},{1,21},{... | collective-permute-start | bytes 589832 | tf_op jit(solution)/shard_map/ppermute | solution.py:517
  17.6 34.0 %collective-permute-start.6 = (bf16[384,256]{1,0:T(8,128)(2,1)S(1)}, bf16[384,256]{1,0:T(8,128)(2,1)S(1)}, u32[]{:S(2)}, u32[]{:S(2)}) collective-permute-start(bf16[384,256]{1,0:T(8,128)(2,1)S(1)} %get-tuple-element.22), channel_id=1, source_target_pairs={{0,12},{4,8},{8,4},{12,0},{16,28},{20,24},{24,20},{28,16},{1,13},{... | collective-permute-start | bytes 589832 | tf_op jit(solution)/shard_map/ppermute | solution.py:517
  52.0 12.0 %collective-permute-start.7 = (bf16[4,160,256]{2,1,0:T(8,128)(2,1)S(1)}, bf16[4,160,256]{2,1,0:T(8,128)(2,1)S(1)}, u32[]{:S(2)}, u32[]{:S(2)}) collective-permute-start(bf16[4,160,256]{2,1,0:T(8,128)(2,1)S(1)} %shard_map.142.held_ref), channel_id=1, source_target_pairs={{0,4},{4,0},{8,12},{12,8},{16,20},{20,16},{24,28},{28,24},{1,5},{5... | collective-permute-start | bytes 983048 | tf_op jit(solution)/shard_map/ppermute | solution.py:517
  52.6 24.8 %collective-permute-start.8 = (bf16[4,160,256]{2,1,0:T(8,128)(2,1)S(1)}, bf16[4,160,256]{2,1,0:T(8,128)(2,1)S(1)}, u32[]{:S(2)}, u32[]{:S(2)}) collective-permute-start(bf16[4,160,256]{2,1,0:T(8,128)(2,1)S(1)} %shard_map.142.held_ref), channel_id=1, source_target_pairs={{0,2},{1,3},{2,0},{3,1},{4,6},{5,7},{6,4},{7,5},{8,10},{9,11},{10,... | collective-permute-start | bytes 983048 | tf_op jit(solution)/shard_map/ppermute | solution.py:517
  63.2 0.8 copy-start
  64.7 5.3 %copy-start.1 = (bf16[8,128,256]{2,1,0:T(8,128)(2,1)S(1)}, bf16[8,128,256]{2,1,0:T(8,128)(2,1)}, u32[]{:S(2)}) copy-start(bf16[8,128,256]{2,1,0:T(8,128)(2,1)} %copy-done) | copy-start | bytes 1572868
  64.7 12.6 %collective-permute-start.9 = (bf16[4,160,256]{2,1,0:T(8,128)(2,1)}, bf16[4,160,256]{2,1,0:T(8,128)(2,1)S(1)}, u32[]{:S(2)}, u32[]{:S(2)}) collective-permute-start(bf16[4,160,256]{2,1,0:T(8,128)(2,1)} %shard_map.143.got_ref), channel_id=1, source_target_pairs={{0,2},{1,3},{2,0},{3,1},{4,6},{5,7},{6,4},{7,5},{8,10},{9,11},{10,... | collective-permute-start | bytes 983048 | tf_op jit(solution)/shard_map/ppermute | solution.py:517
  65.3 12.1 %all-to-all-start = ((bf16[8,64,128]{2,1,0:T(8,128)(2,1)}), bf16[8,64,128]{2,1,0:T(8,128)(2,1)S(1)}, u32[]{:S(2)}, u32[]{:S(2)}) async-start(bf16[8,64,128]{2,1,0:T(8,128)(2,1)} %get-tuple-element.24), calls=%async_computation | async-start | bytes 262144 | tf_op jit(solution)/shard_map/all_to_all | solution.py:521
  70.0 1.0 copy-start.3
  71.7 18.5 %collective-permute-start.10 = (bf16[256,1280]{1,0:T(8,128)(2,1)S(1)}, bf16[256,1280]{1,0:T(8,128)(2,1)S(1)}, u32[]{:S(2)}, u32[]{:S(2)}) collective-permute-start(bf16[256,1280]{1,0:T(8,128)(2,1)S(1)} %shard_map.144.refs_0_), channel_id=1, source_target_pairs={{0,1},{1,0},{2,3},{3,2},{4,5},{5,4},{6,7},{7,6},{8,9},{9,8},{10,11... | collective-permute-start | bytes 1966088 | tf_op jit(solution)/shard_map/ppermute | solution.py:517
  78.1 12.1 %collective-permute-start.11 = (bf16[256,1280]{1,0:T(8,128)(2,1)S(1)}, bf16[256,1280]{1,0:T(8,128)(2,1)S(1)}, u32[]{:S(2)}, u32[]{:S(2)}) collective-permute-start(bf16[256,1280]{1,0:T(8,128)(2,1)S(1)} %shard_map.145.refs_1_), channel_id=1, source_target_pairs={{0,1},{1,0},{2,3},{3,2},{4,5},{5,4},{6,7},{7,6},{8,9},{9,8},{10,11... | collective-permute-start | bytes 1966088 | tf_op jit(solution)/shard_map/ppermute | solution.py:517
  78.8 4.2 %copy-start.6 = (f32[1280]{0:T(1024)S(1)}, f32[1280]{0:T(1024)}, u32[]{:S(2)}) copy-start(f32[1280]{0:T(1024)} %param.20) | copy-start | bytes 15364
  78.8 11.4 %all-to-all-start.1 = ((bf16[8,64,128]{2,1,0:T(8,128)(2,1)}), bf16[8,64,128]{2,1,0:T(8,128)(2,1)S(1)}, u32[]{:S(2)}, u32[]{:S(2)}) async-start(bf16[8,64,128]{2,1,0:T(8,128)(2,1)} %shard_map.141), calls=%async_computation.1 | async-start | bytes 262144 | tf_op jit(solution)/shard_map/all_to_all | solution.py:521
  95.3 3.7 %collective-permute-start.14 = (bf16[64,256]{1,0:T(8,128)(2,1)S(1)}, bf16[64,256]{1,0:T(8,128)(2,1)S(1)}, u32[]{:S(2)}, u32[]{:S(2)}) collective-permute-start(bf16[64,256]{1,0:T(8,128)(2,1)S(1)} %get-tuple-element.28.refs_0_), channel_id=1, source_target_pairs={{0,3},{1,2},{2,1},{3,0},{4,7},{5,6},{6,5},{7,4},{8,11},{9,10},{10,... | collective-permute-start | bytes 98312 | tf_op jit(solution)/shard_map/ppermute | solution.py:517
  95.7 4.0 %collective-permute-start.13 = (bf16[64,256]{1,0:T(8,128)(2,1)S(1)}, bf16[64,256]{1,0:T(8,128)(2,1)S(1)}, u32[]{:S(2)}, u32[]{:S(2)}) collective-permute-start(bf16[64,256]{1,0:T(8,128)(2,1)S(1)} %get-tuple-element.28.refs_0_), channel_id=1, source_target_pairs={{0,2},{1,3},{2,0},{3,1},{4,6},{5,7},{6,4},{7,5},{8,10},{9,11},{10,... | collective-permute-start | bytes 98312 | tf_op jit(solution)/shard_map/ppermute | solution.py:517
  97.0 2.7 %collective-permute-start.12 = (bf16[64,256]{1,0:T(8,128)(2,1)S(1)}, bf16[64,256]{1,0:T(8,128)(2,1)S(1)}, u32[]{:S(2)}, u32[]{:S(2)}) collective-permute-start(bf16[64,256]{1,0:T(8,128)(2,1)S(1)} %get-tuple-element.28.refs_0_), channel_id=1, source_target_pairs={{0,1},{1,0},{2,3},{3,2},{4,5},{5,4},{6,7},{7,6},{8,9},{9,8},{10,11... | collective-permute-start | bytes 98312 | tf_op jit(solution)/shard_map/ppermute | solution.py:517
  100.4 3.6 %copy-start.4 = (bf16[2048,64]{0,1:T(8,128)(2,1)S(1)}, bf16[2048,64]{0,1:T(8,128)(2,1)}, u32[]{:S(2)}) copy-start(bf16[2048,64]{0,1:T(8,128)(2,1)} %param.17) | copy-start | bytes 786436
  100.4 3.6 %copy-start.5 = (f32[1,2048]{1,0:T(1,128)S(1)}, f32[1,2048]{1,0:T(1,128)}, u32[]{:S(2)}) copy-start(f32[1,2048]{1,0:T(1,128)} %scale_ref.1) | copy-start | bytes 24580
  100.4 13.0 %all-to-all-start.2 = ((bf16[8,64,256]{2,1,0:T(8,128)(2,1)}), bf16[8,64,256]{2,1,0:T(8,128)(2,1)S(1)}, u32[]{:S(2)}, u32[]{:S(2)}) async-start(bf16[8,64,256]{2,1,0:T(8,128)(2,1)} %shard_map.148), calls=%async_computation.2 | async-start | bytes 524288 | tf_op jit(solution)/shard_map/all_to_all | solution.py:521
  (2 other events, 1.4 us)

commit v5 on v4

v5 whole, which is shorter than its diff:
```python
import functools
import math

import jax
import jax.numpy as jnp
from jax import lax
from jax.experimental import pallas as pl
from jax.experimental.pallas import tpu as pltpu
from jax.sharding import PartitionSpec as P

HEADS = 16
HD = 128
CH = 64
GW = 64
VW = 1280
EPS = 1e-05
BF16 = jnp.bfloat16
F32 = jnp.float32
VMEM_LIMIT = 20 * 1024 * 1024


def mm(a, b):
    return jnp.dot(a, b, preferred_element_type=F32)


def mm_nt(a, b):
    return lax.dot_general(a, b, (((1,), (1,)), ((), ())), preferred_element_type=F32)


def mm_tn(a, b):
    return lax.dot_general(a, b, (((0,), (0,)), ((), ())), preferred_element_type=F32)


SMEM_SPEC = pl.BlockSpec(memory_space=pltpu.SMEM)
VMEM_SPEC = pl.BlockSpec(memory_space=pltpu.VMEM)
HBM_SPEC = pl.BlockSpec(memory_space=pltpu.HBM)
ANY_SPEC = pl.BlockSpec(memory_space=pl.ANY)


def in_hbm(x):
    return pltpu.with_memory_space_constraint(x, pltpu.HBM)


def limits():
    return pltpu.CompilerParams(vmem_limit_bytes=VMEM_LIMIT)


class Sizes:
    def __init__(self, seq_count, data_count, tok_rows, patch_embed):
        self.count = seq_count
        self.query_parts = max(1, seq_count // HEADS)
        self.heads = max(1, HEADS // seq_count)
        self.width = self.heads * HD
        self.tok_rows = tok_rows
        self.part_rows = tok_rows // self.query_parts
        positions, self.local, _ = patch_embed.shape
        self.share = positions // data_count if positions % data_count == 0 else positions
        self.rows = self.part_rows + 2 * tok_rows
        self.share_rows = self.share * self.local
        self.chunks = VW // HD
        self.riding = self.local % 8 == 0 and self.share_rows % 16 == 0 and seq_count >= 4
        self.ride_rows = self.chunks * self.share_rows if self.riding else 0

    def pieces(self):
        middle = self.count // 2
        far, near = range(self.count - 1, middle - 1, -1), range(1, middle)
        every = tuple(range(self.heads))
        listed = [(mask, (0,)) for mask in far] + [(mask, every) for mask in near]
        for head in every[1:]:
            listed += [(mask, (head,)) for mask in far]
        return listed + [(0, every)]

    def rides(self, piece):
        return self.riding and piece[0] % 2 == 0 and 0 in piece[1]

    def piece_shape(self, piece):
        wide = len(piece[1])
        return (self.rows + (self.ride_rows // wide if self.rides(piece) else 0), wide * HD)

    def ride_slices(self, piece):
        wide = len(piece[1])
        deep = self.ride_rows // wide
        return [
            (pl.ds(self.rows, deep), pl.ds(at * HD, HD), pl.ds(at * deep, deep)) for at in range(wide)
        ]


def pack_kernel(sizes, place_ref, q_ref, k_ref, v_ref, embed_ref, *refs):
    pieces = sizes.pieces()
    out_refs = refs[: len(pieces)]
    q_scr, k_scr, v_scr, embed_scr, share_scr, in_sems, out_sems = refs[len(pieces) :]
    me = place_ref[0]
    tok_rows, part_rows, width = sizes.tok_rows, sizes.part_rows, sizes.width
    share = pl.ds(place_ref[1] * sizes.share, sizes.share)
    loads = [
        pltpu.make_async_copy(embed_ref.at[share], embed_scr, in_sems.at[3]),
        pltpu.make_async_copy(q_ref.at[0], q_scr, in_sems.at[0]),
        pltpu.make_async_copy(k_ref.at[0], k_scr, in_sems.at[1]),
        pltpu.make_async_copy(v_ref.at[0], v_scr, in_sems.at[2]),
    ]
    for load in loads:
        load.start()
    stores = []
    sent = [[], [], [], []]
    for slot, (piece, out) in enumerate(zip(pieces, out_refs)):
        mask, some = piece
        dest = jnp.bitwise_xor(me, mask)
        group, part = dest // sizes.query_parts, dest % sizes.query_parts
        cols = pl.ds(pl.multiple_of(group * width + some[0] * HD, HD), len(some) * HD)
        first = pl.ds(pl.multiple_of(part * part_rows, part_rows), part_rows)
        for kind, source, rows in (
            (0, q_scr.at[first, cols], pl.ds(0, part_rows)),
            (1, k_scr.at[:, cols], pl.ds(part_rows, tok_rows)),
            (2, v_scr.at[:, cols], pl.ds(part_rows + tok_rows, tok_rows)),
        ):
            sent[kind].append(pltpu.make_async_copy(source, out.at[rows], out_sems.at[kind, slot]))
        if sizes.rides(piece):
            for at, (rows, place, from_rows) in enumerate(sizes.ride_slices(piece)):
                sent[3].append(
                    pltpu.make_async_copy(
                        share_scr.at[from_rows], out.at[rows, place], out_sems.at[3 + at, slot]
                    )
                )
    loads[0].wait()
    if sizes.riding:
        for chunk in range(sizes.chunks):
            cols = embed_scr[:, :, pl.ds(chunk * HD, HD)].astype(F32)
            share_scr[pl.ds(chunk * sizes.share_rows, sizes.share_rows), :] = cols.reshape(
                sizes.share_rows, HD
            ).astype(BF16)
    for store in sent[3]:
        store.start()
    for kind in range(3):
        loads[kind + 1].wait()
        for store in sent[kind]:
            store.start()
    for stores in sent:
        for store in stores:
            store.wait()


def pack(sizes, place, queries, keys, values, patch_embed):
    tok_rows, full = queries.shape[1:]
    pieces = sizes.pieces()
    return pl.pallas_call(
        functools.partial(pack_kernel, sizes),
        out_shape=[jax.ShapeDtypeStruct(sizes.piece_shape(piece), BF16) for piece in pieces],
        in_specs=[SMEM_SPEC] + [HBM_SPEC] * 4,
        out_specs=[HBM_SPEC] * len(pieces),
        scratch_shapes=[pltpu.VMEM((tok_rows, full), BF16)] * 3
        + [
            pltpu.VMEM((sizes.share,) + patch_embed.shape[1:], BF16),
            pltpu.VMEM((max(16, sizes.ride_rows), HD), BF16),
            pltpu.SemaphoreType.DMA((4,)),
            pltpu.SemaphoreType.DMA((3 + sizes.heads, len(pieces))),
        ],
        compiler_params=limits(),
        cost_estimate=pl.CostEstimate(
            flops=0, bytes_accessed=12 * tok_rows * full, transcendentals=0
        ),
    )(place, queries, keys, values, patch_embed)


def collect_kernel(sizes, pieces, *refs):
    in_refs, out_ref, sems = refs[: len(pieces)], refs[-2], refs[-1]
    copies = []
    for slot, (piece, ref) in enumerate(zip(pieces, in_refs)):
        for at, (rows, cols, to_rows) in enumerate(sizes.ride_slices(piece)):
            copies.append(
                pltpu.make_async_copy(
                    ref.at[rows, cols], out_ref.at[slot, to_rows], sems.at[at, slot]
                )
            )
    for copy in copies:
        copy.start()
    for copy in copies:
        copy.wait()


def collect(sizes, pieces, arrays, others):
    return pl.pallas_call(
        functools.partial(collect_kernel, sizes, pieces),
        out_shape=jax.ShapeDtypeStruct((len(pieces), sizes.ride_rows, HD), BF16),
        in_specs=[ANY_SPEC] * (len(arrays) + len(others)),
        out_specs=VMEM_SPEC,
        scratch_shapes=[pltpu.SemaphoreType.DMA((sizes.heads, len(pieces)))],
        compiler_params=limits(),
    )(*arrays, *others)


def arrange_kernel(sizes, masks, place_ref, held_ref, got_ref, wait_ref, out_ref):
    del wait_ref
    me = place_ref[0]
    odd = me % 2 == 1
    local, width = sizes.local, HD
    for slot, mask in enumerate(masks):
        pair = jnp.bitwise_xor(me, mask) // 2
        for chunk in range(sizes.chunks):
            rows = pl.ds(chunk * sizes.share_rows, sizes.share_rows)
            held = held_ref[slot, rows, :].astype(F32)
            got = got_ref[slot, rows, :].astype(F32)
            first = jnp.where(odd, got, held)
            second = jnp.where(odd, held, got)
            for at in range(sizes.share):
                part = slice(at * local, (at + 1) * local)
                both = jnp.concatenate([first[part], second[part]], axis=0).astype(BF16)
                start = pl.multiple_of(at * sizes.count * local + pair * 2 * local, 2 * local)
                out_ref[pl.ds(start, 2 * local), pl.ds(chunk * width, width)] = both


def arrange(sizes, masks, place, held, got, wait):
    rows = sizes.share * sizes.count * sizes.local
    return pl.pallas_call(
        functools.partial(arrange_kernel, sizes, masks),
        out_shape=jax.ShapeDtypeStruct((rows, VW), BF16),
        in_specs=[SMEM_SPEC, VMEM_SPEC, VMEM_SPEC, ANY_SPEC],
        out_specs=VMEM_SPEC,
        compiler_params=limits(),
    )(place, held, got, wait)


def attend_kernel(sizes, head, pieces, place_ref, *refs):
    count, width = sizes.count, sizes.width
    tok_rows, part_rows = sizes.tok_rows, sizes.part_rows
    in_refs, refs = refs[:count], refs[count:]
    scale_ref, shift_ref, proj_ref, *refs = refs
    before_ref = None
    if head:
        before_ref, *refs = refs
    mod_ref, lat_ref, query_scr, key_scr, value_scr, scale_scr, shift_scr, proj_scr, *refs = refs
    sems, side_sems = refs
    half = part_rows // 2
    lat_rows = count * tok_rows
    factor = HD ** (-0.5) * math.log2(math.e)
    me = place_ref[0]
    mine = pl.ds(pl.multiple_of(place_ref[2] * width + head * HD, HD), HD)
    copies = []
    for src, (piece, ref) in enumerate(zip(pieces, in_refs)):
        cols = pl.ds(piece[1].index(head) * HD, HD)
        for kind, start, rows, scr in (
            (0, 0, part_rows, query_scr),
            (1, part_rows, tok_rows, key_scr),
            (2, part_rows + tok_rows, tok_rows, value_scr),
        ):
            to = scr.at[pl.ds(src * rows, rows)]
            if kind == 2:
                to = scr.at[pl.ds(src * rows, rows), pl.ds(0, HD)]
            copies.append(
                pltpu.make_async_copy(ref.at[pl.ds(start, rows), cols], to, sems.at[kind, src])
            )
    copies += [
        pltpu.make_async_copy(scale_ref.at[:, mine], scale_scr, side_sems.at[0]),
        pltpu.make_async_copy(shift_ref.at[:, mine], shift_scr, side_sems.at[1]),
        pltpu.make_async_copy(proj_ref.at[:, mine], proj_scr, side_sems.at[2]),
    ]
    for copy in copies:
        copy.start()
    value_scr[:, pl.ds(HD, HD)] = jnp.ones((lat_rows, HD), BF16)
    for copy in copies:
        copy.wait()
    gain = 1.0 + scale_scr[...]
    shift = shift_scr[...]
    proj = proj_scr[...]
    zero = jnp.zeros_like(proj)
    proj_pair = jnp.concatenate(
        [jnp.concatenate([proj, zero], axis=1), jnp.concatenate([zero, proj], axis=1)], axis=0
    )
    block = min(count * part_rows, max(part_rows, min(256, (1 << 18) // lat_rows)))
    for first in range(0, count * part_rows, block):
        logits = mm_nt(query_scr[pl.ds(first, block), :], key_scr[...])
        top = jnp.max(logits, axis=-1, keepdims=True)
        weights = jnp.exp2((logits - top) * factor).astype(BF16)
        both = mm(weights, value_scr[...])
        modulated = (both[:, :HD] / both[:, HD:] * gain + shift).astype(BF16)
        for at in range(0, block, part_rows):
            place = jnp.bitwise_xor(me, pieces[(first + at) // part_rows][0])
            mod_ref[place] = modulated[at : at + part_rows]
            pair = jnp.concatenate(
                [modulated[at : at + half], modulated[at + half : at + part_rows]], axis=1
            )
            latent = mm_nt(pair, proj_pair)
            if head:
                latent = latent + before_ref[place]
            lat_ref[place] = latent.astype(lat_ref.dtype)


def attend(sizes, head, place, pieces, received, scales, shifts, proj, before):
    count = sizes.count
    lat_rows = count * sizes.tok_rows
    query_rows = count * sizes.part_rows
    last = head == sizes.heads - 1
    return pl.pallas_call(
        functools.partial(attend_kernel, sizes, head, pieces),
        out_shape=(
            jax.ShapeDtypeStruct((count, sizes.part_rows, HD), BF16),
            jax.ShapeDtypeStruct((count, sizes.part_rows // 2, 2 * CH), BF16 if last else F32),
        ),
        in_specs=[SMEM_SPEC] + [ANY_SPEC] * count + [HBM_SPEC] * 3 + [VMEM_SPEC] * len(before),
        out_specs=(VMEM_SPEC, VMEM_SPEC),
        scratch_shapes=[
            pltpu.VMEM((query_rows, HD), BF16),
            pltpu.VMEM((lat_rows, HD), BF16),
            pltpu.VMEM((lat_rows, 2 * HD), BF16),
            pltpu.VMEM((1, HD), F32),
            pltpu.VMEM((1, HD), F32),
            pltpu.VMEM((CH, HD), BF16),
            pltpu.SemaphoreType.DMA((3, count)),
            pltpu.SemaphoreType.DMA((3,)),
        ],
        compiler_params=limits(),
        cost_estimate=pl.CostEstimate(
            flops=4 * query_rows * lat_rows * HD,
            bytes_accessed=2 * (query_rows * 2 + lat_rows * 2) * HD,
            transcendentals=query_rows * lat_rows,
        ),
    )(place, *received, scales, shifts, proj, *before)


def total_kernel(copies, *refs):
    out_ref = refs[-1]
    if len(refs) == 2:
        parts = [refs[0][i].astype(F32) for i in range(refs[0].shape[0])]
    else:
        parts = [ref[...].astype(F32) for ref in refs[:-1]]
    while len(parts) > 1:
        parts = [parts[i] + parts[i + 1] for i in range(0, len(parts), 2)]
    for copy in range(copies):
        out_ref[copy] = parts[0].astype(BF16)


def total_copies(arrays, copies):
    return pl.pallas_call(
        functools.partial(total_kernel, copies),
        out_shape=jax.ShapeDtypeStruct((copies,) + arrays[0].shape[-2:], BF16),
        in_specs=[VMEM_SPEC] * len(arrays),
        out_specs=VMEM_SPEC,
        compiler_params=limits(),
    )(*arrays)


def lane_mean(x, count):
    return jnp.sum(x, axis=-1, keepdims=True) * (1.0 / count)


def head_kernel(grid_rows, heads, fused, embed_masks, out_factor, place_ref, lat_ref, *refs):
    embed_refs, refs = refs[: len(embed_masks)], refs[len(embed_masks) :]
    sides, refs = refs[:4], refs[4:]
    cot_ref, refs = refs[0], refs[1:]
    mod_refs, refs = refs[:heads], refs[heads:]
    reward_ref, grad_ref, weight_ref, lat_scr, grad_scr, embed_ref, *refs = refs
    pos_ref, pre_ref, post_ref, prompt_ref, sems, side_sems = refs
    patch_rows = grid_rows // 4
    patch_cols = GW // 4
    patches = patch_rows * patch_cols
    copies = []
    for slot, mask in enumerate(embed_masks):
        rows = embed_refs[slot].shape[0]
        first = pl.multiple_of(jnp.bitwise_xor(place_ref[1], mask) * rows, rows)
        copies.append(
            pltpu.make_async_copy(embed_refs[slot], embed_ref.at[pl.ds(first, rows)], sems.at[slot])
        )
    for slot, (side, scr) in enumerate(zip(sides, (pos_ref, pre_ref, post_ref, prompt_ref))):
        copies.append(pltpu.make_async_copy(side, scr, side_sems.at[slot]))
    for copy in copies:
        copy.start()
    lat_scr[...] = lat_ref[...].astype(F32)

    def position_rows(ty):
        return embed_ref[pl.ds(4 * ty * CH, 4 * CH), :]

    blocks = []
    for hi in range(2):
        wide = []
        for tx in range(4):
            rows = [
                lat_scr[pl.ds((2 * pr + hi) * GW + tx, patch_cols, stride=4), :]
                for pr in range(patch_rows)
            ]
            wide.append(jnp.concatenate(rows, axis=0))
        for side in range(2):
            lanes = slice(side * CH, (side + 1) * CH)
            blocks.append(jnp.concatenate([x[:, lanes] for x in wide], axis=1).astype(BF16))
    for copy in copies:
        copy.wait()
    embedded = pos_ref[...].astype(F32)
    for ty in range(4):
        embedded = embedded + mm(blocks[ty], position_rows(ty))
    pre = pre_ref[...].reshape(1, VW)
    post = post_ref[...].reshape(1, VW)
    prompt = prompt_ref[...]
    center = embedded - lane_mean(embedded, VW)
    rstd = lax.rsqrt(lane_mean(center * center, VW) + EPS)
    unit = center * rstd
    pooled = jnp.sum(unit, axis=0, keepdims=True) * (1.0 / patches) * pre
    pooled_center = pooled - lane_mean(pooled, VW)
    pooled_rstd = lax.rsqrt(lane_mean(pooled_center * pooled_center, VW) + EPS)
    pooled_unit = pooled_center * pooled_rstd
    final = pooled_unit * post
    dot = jnp.sum(final * prompt, axis=-1, keepdims=True)
    final_sq = jnp.sum(final * final, axis=-1, keepdims=True)
    prompt_sq = jnp.sum(prompt * prompt, axis=-1, keepdims=True)
    final_len = jnp.sqrt(final_sq)
    prompt_len = jnp.sqrt(prompt_sq)
    cosine = dot / (final_len * prompt_len)
    reward_ref[...] = jnp.broadcast_to(100.0 * cosine, reward_ref.shape)
    cot = cot_ref[0]
    final_grad = (100.0 * cot) * (prompt / (final_len * prompt_len) - final * (cosine / final_sq))
    unit_grad = final_grad * post
    pooled_grad = pooled_rstd * (
        unit_grad
        - lane_mean(unit_grad, VW)
        - pooled_unit * lane_mean(unit_grad * pooled_unit, VW)
    )
    flow = pooled_grad * pre * (1.0 / patches)
    embed_grad = rstd * (flow - lane_mean(flow, VW) - unit * lane_mean(flow * unit, VW))
    high = embed_grad.astype(BF16)
    low = (embed_grad - high.astype(F32)).astype(BF16)
    stacked = jnp.concatenate([high, low], axis=0)
    for hi in range(2):
        sides = []
        for side in range(2):
            both = mm_nt(stacked, position_rows(2 * hi + side))
            sides.append(both[:patches] + both[patches:])
        for tx in range(4):
            lanes = slice(tx * CH, (tx + 1) * CH)
            piece = jnp.concatenate([sides[0][:, lanes], sides[1][:, lanes]], axis=1)
            for pr in range(patch_rows):
                grad_scr[pl.ds((2 * pr + hi) * GW + tx, patch_cols, stride=4), :] = piece[
                    pr * patch_cols : (pr + 1) * patch_cols
                ]
    grad = grad_scr[...].astype(BF16)
    grad_ref[...] = grad
    if fused:
        store_readout_grad(grad, mod_refs, out_factor, weight_ref)
    else:
        weight_ref[...] = jnp.zeros_like(weight_ref)


def store_readout_grad(grad, mod_refs, out_factor, out_ref):
    for head, mod_ref in enumerate(mod_refs):
        count, rows, width = mod_ref.shape
        half = rows // 2
        first = mod_ref[:, :half, :].reshape(count * half, width)
        second = mod_ref[:, half:, :].reshape(count * half, width)
        total = mm_tn(grad, first)[:CH] + mm_tn(grad, second)[CH:]
        out_ref[:, pl.ds(head * width, width)] = (total * out_factor).astype(BF16)


def reward_head(
    place, latent, embed, pos, pre, post, prompt, cot, modulated, grid_rows, fused, out_factor
):
    patches = grid_rows * GW // 16
    rows = grid_rows * GW // 2
    width = HD * len(modulated)
    embed_arrays, embed_masks = [x for x, _ in embed], [mask for _, mask in embed]
    return pl.pallas_call(
        functools.partial(
            head_kernel, grid_rows, len(modulated), fused, embed_masks, out_factor
        ),
        out_shape=(
            jax.ShapeDtypeStruct((1, 128), F32),
            jax.ShapeDtypeStruct((rows, 2 * CH), BF16),
            jax.ShapeDtypeStruct((CH, width), BF16),
        ),
        in_specs=[SMEM_SPEC, VMEM_SPEC]
        + [ANY_SPEC] * len(embed_arrays)
        + [HBM_SPEC] * 4
        + [SMEM_SPEC]
        + [VMEM_SPEC] * len(modulated),
        out_specs=(VMEM_SPEC, VMEM_SPEC, VMEM_SPEC),
        scratch_shapes=[
            pltpu.VMEM((rows, 2 * CH), F32),
            pltpu.VMEM((rows, 2 * CH), F32),
            pltpu.VMEM((16 * CH, VW), BF16),
            pltpu.VMEM((patches, VW), BF16),
            pltpu.VMEM((VW,), F32),
            pltpu.VMEM((VW,), F32),
            pltpu.VMEM((1, VW), F32),
            pltpu.SemaphoreType.DMA((len(embed_arrays),)),
            pltpu.SemaphoreType.DMA((4,)),
        ],
        compiler_params=limits(),
        cost_estimate=pl.CostEstimate(
            flops=6 * patches * 16 * CH * VW,
            bytes_accessed=2 * 16 * CH * VW + 2 * patches * VW,
            transcendentals=0,
        ),
    )(place, latent, *embed_arrays, pos, pre, post, prompt, cot, *modulated)


def spread_kernel(
    count, half, heads, place_ref, grad_ref, scale_ref, proj_ref, out_ref, scale_scr, proj_scr, sems
):
    width = heads * HD
    mine = pl.ds(pl.multiple_of(place_ref[2] * width, HD), width)
    copies = [
        pltpu.make_async_copy(scale_ref.at[:, mine], scale_scr, sems.at[0]),
        pltpu.make_async_copy(proj_ref.at[:, mine], proj_scr, sems.at[1]),
    ]
    for copy in copies:
        copy.start()
    for copy in copies:
        copy.wait()
    gain = 1.0 + scale_scr[...]
    proj = proj_scr[...]
    zero = jnp.zeros_like(proj)
    sides = (jnp.concatenate([proj, zero], axis=0), jnp.concatenate([zero, proj], axis=0))
    for src in range(count):
        grad = grad_ref[pl.ds(src * half, half), :]
        for side in range(2):
            rows = (mm(grad, sides[side]) * gain).astype(BF16)
            for head in range(heads):
                out_ref[0, head, pl.ds((2 * src + side) * half, half), :] = rows[
                    :, head * HD : (head + 1) * HD
                ]


def spread(place, grad, scales, proj, count, half, heads):
    return pl.pallas_call(
        functools.partial(spread_kernel, count, half, heads),
        out_shape=jax.ShapeDtypeStruct((1, heads, 2 * count * half, HD), BF16),
        in_specs=[SMEM_SPEC, VMEM_SPEC, HBM_SPEC, HBM_SPEC],
        out_specs=VMEM_SPEC,
        scratch_shapes=[
            pltpu.VMEM((1, heads * HD), F32),
            pltpu.VMEM((CH, heads * HD), BF16),
            pltpu.SemaphoreType.DMA((2,)),
        ],
        compiler_params=limits(),
        cost_estimate=pl.CostEstimate(
            flops=8 * count * half * CH * heads * HD,
            bytes_accessed=4 * count * half * heads * HD,
            transcendentals=0,
        ),
    )(place, grad, scales, proj)


def weight_kernel(out_factor, grad_ref, *refs):
    store_readout_grad(grad_ref[...], refs[:-1], out_factor, refs[-1])


def weight_call(grad, modulated, out_factor):
    return pl.pallas_call(
        functools.partial(weight_kernel, out_factor),
        out_shape=jax.ShapeDtypeStruct((CH, HD * len(modulated)), BF16),
        in_specs=[VMEM_SPEC] * (1 + len(modulated)),
        out_specs=VMEM_SPEC,
        compiler_params=limits(),
    )(grad, *modulated)


def finish_kernel(in_ref, out_ref):
    count, _, width = in_ref.shape
    for group in range(count):
        out_ref[:, pl.ds(group * width, width)] = in_ref[group].astype(F32)


def finish(blocks):
    return pl.pallas_call(
        finish_kernel,
        out_shape=jax.ShapeDtypeStruct((CH, HEADS * HD), F32),
        in_specs=[VMEM_SPEC],
        out_specs=VMEM_SPEC,
        compiler_params=limits(),
    )(blocks)


def swap(x, axis, mask):
    count = lax.axis_size(axis)
    return lax.ppermute(x, axis, [(i, i ^ mask) for i in range(count)])


def all_to_all(x, groups=None):
    return lax.all_to_all(
        x, "seq", split_axis=0, concat_axis=0, tiled=True, axis_index_groups=groups
    )


def after_kernel(*refs):
    del refs


def after(x, others):
    return pl.pallas_call(
        after_kernel,
        out_shape=jax.ShapeDtypeStruct(x.shape, x.dtype),
        in_specs=[ANY_SPEC] * (1 + len(others)),
        out_specs=ANY_SPEC,
        input_output_aliases={0: 0},
    )(x, *others)


def on_device(
    queries,
    keys,
    values,
    shifts,
    scales,
    proj_out,
    patch_embed,
    pos_embed,
    pre_gain,
    post_gain,
    prompt,
    cotangent,
):
    seq_count = lax.axis_size("seq")
    data_count = lax.axis_size("dp")
    tok_rows = queries.shape[1]
    sizes = Sizes(seq_count, data_count, tok_rows, patch_embed)
    query_parts, head_count, part_rows = sizes.query_parts, sizes.heads, sizes.part_rows
    group_count = HEADS // head_count
    seq_index = lax.axis_index("seq")
    head_group = seq_index // query_parts
    query_part = seq_index % query_parts
    half = part_rows // 2
    lat_rows = seq_count * tok_rows
    grid_rows = lat_rows // GW
    canonical = part_rows == 2 * GW
    place = jnp.stack([seq_index, lax.axis_index("dp"), head_group]).astype(jnp.int32)
    proj_turned = proj_out.T
    out_factor = 1.0 / math.sqrt(data_count * lat_rows)

    pieces = sizes.pieces()
    packed = pack(
        sizes, place, in_hbm(queries), in_hbm(keys), in_hbm(values), in_hbm(patch_embed)
    )
    received = [swap(x, "seq", piece[0]) if piece[0] else x for piece, x in zip(pieces, packed)]
    bits = [1 << b for b in reversed(range(data_count.bit_length() - 1))]
    shared = sizes.share < patch_embed.shape[0]

    modulated, latent_part = [], []
    for head in range(head_count):
        slots = [slot for slot, piece in enumerate(pieces) if head in piece[1]]
        if head == head_count - 1 and sizes.riding:
            even = [slot for slot, piece in enumerate(pieces) if sizes.rides(piece)]
            rest = [x for slot, x in enumerate(received) if slot not in even]
            held = collect(
                sizes, [pieces[slot] for slot in even], [received[slot] for slot in even],
                rest + modulated,
            )
            got = swap(held, "seq", 1)
            far_held = swap(held, "dp", bits[0]) if shared else None
        mod, latent_sum = attend(
            sizes, head, place, [pieces[slot] for slot in slots], [received[slot] for slot in slots],
            in_hbm(scales), in_hbm(shifts), in_hbm(proj_turned), latent_part,
        )
        modulated, latent_part = modulated + [mod], [latent_sum]
    latent_part = latent_part[0]

    if sizes.riding:
        got = after(got, [modulated[-1]])
        even_masks = [pieces[slot][0] for slot in even]
        embed = [(arrange(sizes, even_masks, place, held, got, modulated[-1]), 0)]
        far_got = swap(got, "dp", bits[0]) if shared else None
    else:
        mine = patch_embed
        if shared:
            mine = lax.dynamic_slice_in_dim(
                patch_embed, lax.axis_index("dp") * sizes.share, sizes.share, 0
            )
        mine = lax.all_gather(mine, "seq", axis=1, tiled=True).reshape(-1, VW)
        embed = [(mine, 0)]
        if shared:
            embed = embed + [(swap(mine, "dp", bits[0]), bits[0])]

    groups = None
    if query_parts > 1:
        groups = [[g * query_parts + r for g in range(group_count)] for r in range(query_parts)]
    per_share = seq_count // group_count
    parts = all_to_all(latent_part.reshape(group_count, per_share * half, 2 * CH), groups)
    if sizes.riding and shared:
        embed.append((arrange(sizes, even_masks, place, far_held, far_got, parts), bits[0]))
    for bit in bits[1:] if shared else []:
        embed = embed + [(swap(x, "dp", bit), m ^ bit) for x, m in embed]
    latent = all_to_all(total_copies([parts], seq_count))
    if canonical:
        latent = latent.reshape(lat_rows // 2, 2 * CH)
    else:
        latent = latent.reshape(group_count, query_parts, per_share, half, 2, CH)
        latent = latent.transpose(0, 2, 1, 4, 3, 5).reshape(grid_rows // 2, 2, GW, CH)
        latent = latent.transpose(0, 2, 1, 3).reshape(lat_rows // 2, 2 * CH)

    reward, grad, weight = reward_head(
        place, latent, embed, in_hbm(pos_embed), in_hbm(pre_gain), in_hbm(post_gain), in_hbm(prompt),
        cotangent, modulated, grid_rows, canonical, out_factor,
    )
    if not canonical:
        tokens = grad.reshape(grid_rows // 2, GW, 2, CH).transpose(0, 2, 1, 3)
        tokens = tokens.reshape(seq_count, query_parts, 2, half, CH)
        tokens = lax.dynamic_index_in_dim(tokens, query_part, 1, keepdims=False)
        grad = tokens.transpose(0, 2, 1, 3).reshape(seq_count * half, 2 * CH)
        weight = weight_call(grad, modulated, out_factor)

    parts = [weight] + [swap(weight, "dp", mask) for mask in range(1, data_count)]
    attn_grad = spread(place, grad, in_hbm(scales), in_hbm(proj_turned), seq_count, half, head_count)
    if query_parts > 1:
        total = total_copies(parts, 1)[0]
        parts = [total] + [swap(total, "seq", mask) for mask in range(1, query_parts)]
    blocks = all_to_all(total_copies(parts, group_count), groups)
    return (reward[0, :1], attn_grad, finish(blocks).T)


def solution(mesh):
    return jax.shard_map(
        on_device,
        mesh=mesh,
        in_specs=(
            P("dp", "seq", None),
            P("dp", "seq", None),
            P("dp", "seq", None),
            P("dp", None),
            P("dp", None),
            P(),
            P(None, "seq", None),
            P(),
            P(),
            P(),
            P("dp", None),
            P("dp"),
        ),
        out_specs=(P("dp"), P("dp", "seq", None, None), P()),
        check_vma=False,
    )
```

time: 115 us -> 111 us (0.965)
  waiting for transfers between devices: 54.9 us -> 40.6 us
  starting transfers between devices: 32.3 us -> 39.9 us
  Pallas kernels: 22.9 us -> 25.5 us
    ppermute x15 -> x19, waiting for transfers between devices: 34.4 us -> 20.9 us  [swap(): return lax.ppermute(x, axis, [(i, i ^ mask) for i in range(count)])]
    ppermute x15 -> x19, starting transfers between devices: 20.5 us -> 29.8 us  [swap(): return lax.ppermute(x, axis, [(i, i ^ mask) for i in range(count)])]
    pallas_call x4 -> x5, Pallas kernels: 17.7 us -> 19.4 us  [the longest x2 11.2 us: attend(): pl.pallas_call(functools.partial(attend_kernel, sizes, head, pieces), out...]
    all_to_all x3, starting transfers between devices: 11.8 us -> 10.2 us  [all_to_all(): lax.all_to_all(x, 'seq', split_axis=0, concat_axis=0, tiled=True, axis_in...]
    unnamed x16 -> x8, local copies, waits for them, and re-layouts: 2.5 us -> 2.39 us
  transfers between devices with their start and end apart: 18 -> 22, of which waited for: 7 -> 8; matrix products, arithmetic and copies ran while one was open for 0% -> 0% of each run, Pallas kernels for 11% -> 14%
where the time goes in v5:
time: 111 us; the launch traced here: 110 us
  waiting for transfers between devices  40.6 us (37%)
  starting transfers between devices  39.9 us (36%)
  Pallas kernels  25.5 us (23%)
  local copies, waits for them, and re-layouts  2.39 us (2%)
  between operations  1.47 us (1%)
    ppermute x19, starting transfers between devices, swap(): return lax.ppermute(x, axis, [(i, i ^ mask) for i in range(count)])  29.8 us
    ppermute x19, waiting for transfers between devices, swap(): return lax.ppermute(x, axis, [(i, i ^ mask) for i in range(count)])  20.9 us
    all_to_all x3, waiting for transfers between devices, all_to_all(): lax.all_to_all(x, 'seq', split_axis=0, concat_axis=0, tiled=True, axis_in...  19.7 us
    pallas_call x2, Pallas kernels, attend(): pl.pallas_call(functools.partial(attend_kernel, sizes, head, pieces), out...  11.2 us
    all_to_all x3, starting transfers between devices, all_to_all(): lax.all_to_all(x, 'seq', split_axis=0, concat_axis=0, tiled=True, axis_in...  10.2 us
    pallas_call x1, Pallas kernels, reward_head(): pl.pallas_call(functools.partial(head_kernel, grid_rows, len(modulated),...  5.14 us
    pallas_call x1, Pallas kernels, pack(): pl.pallas_call(functools.partial(pack_kernel, sizes), out_shape=[jax.Shap...  2.71 us
    pallas_call x1, Pallas kernels, spread(): pl.pallas_call(functools.partial(spread_kernel, count, half, heads), out_...  2.41 us
  transfers between devices with their start and end apart: 22, of which 8 were waited for; matrix products, arithmetic and copies ran while one was open for 0% of the time, Pallas kernels for 14%

profile of v5, /device:TPU:0, one launch (start us, length us, event | category | flops | bytes accessed | tf_op | source)
XLA Modules:
  0.0 109.9 jit_solution(12705202333976623744)
XLA Ops:
  0.7 2.7 %shard_map.139 = (bf16[384,128]{1,0:T(8,128)(2,1)S(1)}, bf16[704,128]{1,0:T(8,128)(2,1)S(1)}, bf16[384,128]{1,0:T(8,128)(2,1)S(1)}, bf16[704,128]{1,0:T(8,128)(2...) custom-call(s32[3]{0:T(128)S(1)} %pad_add_fusion.place_ref, ...), custom_call_target="tpu_custom_call" | custom-call | bytes 3145728 | tf_op jit(solution)/shard_map/pallas_call | solution.py:145
  3.4 6.1 %collective-permute-start.7 = (bf16[384,128]{1,0:T(8,128)(2,1)S(1)}, bf16[384,128]{1,0:T(8,128)(2,1)S(1)}, u32[]{:S(2)}, u32[]{:S(2)}) collective-permute-start(bf16[384,128]{1,0:T(8,128)(2,1)S(1)} %get-tuple-element.30), channel_id=1, source_target_pairs={{0,28},{4,24},{8,20},{12,16},{16,12},{20,8},{24,4},{28,0},{1,29},{... | collective-permute-start | bytes 294920 | tf_op jit(solution)/shard_map/ppermute | solution.py:570
  10.1 1.6 %collective-permute-start = (bf16[384,256]{1,0:T(8,128)(2,1)S(1)}, bf16[384,256]{1,0:T(8,128)(2,1)S(1)}, u32[]{:S(2)}, u32[]{:S(2)}) collective-permute-start(bf16[384,256]{1,0:T(8,128)(2,1)S(1)} %get-tuple-element.22), channel_id=1, source_target_pairs={{0,4},{4,0},{8,12},{12,8},{16,20},{20,16},{24,28},{28,24},{1,5},{5... | collective-permute-start | bytes 589832 | tf_op jit(solution)/shard_map/ppermute | solution.py:570
  11.8 1.2 %collective-permute-start.2 = (bf16[384,256]{1,0:T(8,128)(2,1)S(1)}, bf16[384,256]{1,0:T(8,128)(2,1)S(1)}, u32[]{:S(2)}, u32[]{:S(2)}) collective-permute-start(bf16[384,256]{1,0:T(8,128)(2,1)S(1)} %get-tuple-element.24), channel_id=1, source_target_pairs={{0,12},{4,8},{8,4},{12,0},{16,28},{20,24},{24,20},{28,16},{1,13},{... | collective-permute-start | bytes 589832 | tf_op jit(solution)/shard_map/ppermute | solution.py:570
  13.0 4.0 %collective-permute-start.8 = (bf16[704,128]{1,0:T(8,128)(2,1)S(1)}, bf16[704,128]{1,0:T(8,128)(2,1)S(1)}, u32[]{:S(2)}, u32[]{:S(2)}) collective-permute-start(bf16[704,128]{1,0:T(8,128)(2,1)S(1)} %get-tuple-element.31), channel_id=1, source_target_pairs={{0,24},{4,28},{8,16},{12,20},{16,8},{20,12},{24,0},{28,4},{1,25},{... | collective-permute-start | bytes 540680 | tf_op jit(solution)/shard_map/ppermute | solution.py:570
  18.7 11.0 %collective-permute-done.8.refs_1_.refs_0_ = bf16[704,128]{1,0:T(8,128)(2,1)S(1)} collective-permute-done((bf16[704,128]{1,0:T(8,128)(2,1)S(1)}, bf16[704,128]{1,0:T(8,128)(2,1)S(1)}, u32[]{:S(2)}, u32[]{:S(2)}) %collective-permute-start.8) | collective-permute-done | bytes 180256 | tf_op jit(solution)/shard_map/ppermute | solution.py:570
  29.6 3.6 %collective-permute-start.3 = (bf16[384,128]{1,0:T(8,128)(2,1)S(1)}, bf16[384,128]{1,0:T(8,128)(2,1)S(1)}, u32[]{:S(2)}, u32[]{:S(2)}) collective-permute-start(bf16[384,128]{1,0:T(8,128)(2,1)S(1)} %get-tuple-element.25), channel_id=1, source_target_pairs={{0,28},{4,24},{8,20},{12,16},{16,12},{20,8},{24,4},{28,0},{1,29},{... | collective-permute-start | bytes 294920 | tf_op jit(solution)/shard_map/ppermute | solution.py:570
  33.2 6.6 %collective-permute-done.10.refs_3_.refs_1_ = bf16[704,128]{1,0:T(8,128)(2,1)S(1)} collective-permute-done((bf16[704,128]{1,0:T(8,128)(2,1)S(1)}, bf16[704,128]{1,0:T(8,128)(2,1)S(1)}, u32[]{:S(2)}, u32[]{:S(2)}) %collective-permute-start.10) | collective-permute-done | bytes 180256 | tf_op jit(solution)/shard_map/ppermute | solution.py:570
  39.7 1.2 %collective-permute-start.4 = (bf16[384,128]{1,0:T(8,128)(2,1)S(1)}, bf16[384,128]{1,0:T(8,128)(2,1)S(1)}, u32[]{:S(2)}, u32[]{:S(2)}) collective-permute-start(bf16[384,128]{1,0:T(8,128)(2,1)S(1)} %get-tuple-element.26), channel_id=1, source_target_pairs={{0,24},{4,28},{8,16},{12,20},{16,8},{20,12},{24,0},{28,4},{1,25},{... | collective-permute-start | bytes 294920 | tf_op jit(solution)/shard_map/ppermute | solution.py:570
  40.9 2.1 %collective-permute-start.5 = (bf16[384,128]{1,0:T(8,128)(2,1)S(1)}, bf16[384,128]{1,0:T(8,128)(2,1)S(1)}, u32[]{:S(2)}, u32[]{:S(2)}) collective-permute-start(bf16[384,128]{1,0:T(8,128)(2,1)S(1)} %get-tuple-element.27), channel_id=1, source_target_pairs={{0,20},{4,16},{8,28},{12,24},{16,4},{20,0},{24,12},{28,8},{1,21},{... | collective-permute-start | bytes 294920 | tf_op jit(solution)/shard_map/ppermute | solution.py:570
  43.1 4.3 %collective-permute-start.6 = (bf16[384,128]{1,0:T(8,128)(2,1)S(1)}, bf16[384,128]{1,0:T(8,128)(2,1)S(1)}, u32[]{:S(2)}, u32[]{:S(2)}) collective-permute-start(bf16[384,128]{1,0:T(8,128)(2,1)S(1)} %get-tuple-element.28), channel_id=1, source_target_pairs={{0,16},{4,20},{8,24},{12,28},{16,0},{20,4},{24,8},{28,12},{1,17},{... | collective-permute-start | bytes 294920 | tf_op jit(solution)/shard_map/ppermute | solution.py:570
  47.4 5.3 %shard_map.140 = (bf16[8,128,128]{2,1,0:T(8,128)(2,1)S(1)}, f32[8,64,128]{2,1,0:T(8,128)S(1)}) custom-call(s32[3]{0:T(128)S(1)} %pad_add_fusion.place_ref, bf16[384,128]{1,0:T(8,128)(2,1)S(1)} %collective-permute-done.7.refs_0_.refs_4_, bf16[704,128]{1,0:T(8,128)(2,1)S(1)} %collective-permute-done.8.refs_1_.refs_0_, ...), custom_call_target="tpu_custom_call" | custom-call | flops 536870912 | bytes 1048576 | tf_op jit(solution)/shard_map/pallas_call | solution.py:292
  53.1 1.6 %collective-permute-start.12 = (bf16[4,320,128]{2,1,0:T(8,128)(2,1)S(1)}, bf16[4,320,128]{2,1,0:T(8,128)(2,1)S(1)}, u32[]{:S(2)}, u32[]{:S(2)}) collective-permute-start(bf16[4,320,128]{2,1,0:T(8,128)(2,1)S(1)} %shard_map.143.held_ref), channel_id=1, source_target_pairs={{0,2},{1,3},{2,0},{3,1},{4,6},{5,7},{6,4},{7,5},{8,10},{9,11},{10,... | collective-permute-start | bytes 983048 | tf_op jit(solution)/shard_map/ppermute | solution.py:570
  54.7 5.9 %shard_map.141 = (bf16[8,128,128]{2,1,0:T(8,128)(2,1)S(1)}, bf16[8,64,128]{2,1,0:T(8,128)(2,1)}) custom-call(s32[3]{0:T(128)S(1)} %pad_add_fusion.place_ref, bf16[384,256]{1,0:T(8,128)(2,1)S(1)} %collective-permute-done.refs_4_.refs_0_.refs_6_, bf16[544,256]{1,0:T(8,128)(2,1)S(1)} %collective-permute-done.1.refs_5_.refs_1_.refs_2_, ...), custom_call_target="tpu_custom_call" | custom-call | flops 536870912 | bytes 1048576 | tf_op jit(solution)/shard_map/pallas_call | solution.py:292
  62.6 3.4 %all-to-all-start = ((bf16[8,64,128]{2,1,0:T(8,128)(2,1)}), bf16[8,64,128]{2,1,0:T(8,128)(2,1)S(1)}, u32[]{:S(2)}, u32[]{:S(2)}) async-start(bf16[8,64,128]{2,1,0:T(8,128)(2,1)} %get-tuple-element.35), calls=%async_computation | async-start | bytes 262144 | tf_op jit(solution)/shard_map/all_to_all | solution.py:574
  67.7 5.5 %all-to-all-done.refs_0_.wait_ref = bf16[8,64,128]{2,1,0:T(8,128)(2,1)S(1)} async-done(((bf16[8,64,128]{2,1,0:T(8,128)(2,1)}), bf16[8,64,128]{2,1,0:T(8,128)(2,1)S(1)}, u32[]{:S(2)}, u32[]{:S(2)}) %all-to-all-start) | async-done | bytes 131104 | tf_op jit(solution)/shard_map/all_to_all | solution.py:574
  74.7 3.4 %all-to-all-start.1 = ((bf16[8,64,128]{2,1,0:T(8,128)(2,1)}), bf16[8,64,128]{2,1,0:T(8,128)(2,1)S(1)}, u32[]{:S(2)}, u32[]{:S(2)}) async-start(bf16[8,64,128]{2,1,0:T(8,128)(2,1)} %shard_map.142), calls=%async_computation.1 | async-start | bytes 262144 | tf_op jit(solution)/shard_map/all_to_all | solution.py:574
  78.8 7.2 %all-to-all-done.1 = bf16[8,64,128]{2,1,0:T(8,128)(2,1)S(1)} async-done(((bf16[8,64,128]{2,1,0:T(8,128)(2,1)}), bf16[8,64,128]{2,1,0:T(8,128)(2,1)S(1)}, u32[]{:S(2)}, u32[]{:S(2)}) %all-to-all-start.1) | async-done | bytes 131104 | tf_op jit(solution)/shard_map/all_to_all | solution.py:574
  86.0 5.1 %shard_map.147 = (f32[1,128]{1,0:T(1,128)}, bf16[512,128]{1,0:T(8,128)(2,1)S(1)}, bf16[64,256]{1,0:T(8,128)(2,1)S(1)}) custom-call(s32[3]{0:T(128)S(1)} %pad_add_fusion.place_ref, bf16[512,128]{1,0:T(8,128)(2,1)S(1)} %bitcast.7, bf16[256,1280]{1,0:T(8,128)(2,1)S(1)} %shard_map.145.refs_0_, bf16[256,1280]{1,0:T(8,128)(2,1)S(1)} %shard_map.146.refs_1_, ...), custom_call_target="tpu_custom_call" | custom-call | flops 503316480 | bytes 2785280 | tf_op jit(solution)/shard_map/pallas_call | solution.py:456
  91.5 1.2 %collective-permute-start.17 = (bf16[64,256]{1,0:T(8,128)(2,1)S(1)}, bf16[64,256]{1,0:T(8,128)(2,1)S(1)}, u32[]{:S(2)}, u32[]{:S(2)}) collective-permute-start(bf16[64,256]{1,0:T(8,128)(2,1)S(1)} %get-tuple-element.40.refs_0_), channel_id=1, source_target_pairs={{0,2},{1,3},{2,0},{3,1},{4,6},{5,7},{6,4},{7,5},{8,10},{9,11},{10,... | collective-permute-start | bytes 98312 | tf_op jit(solution)/shard_map/ppermute | solution.py:570
  93.1 1.8 %collective-permute-done.18.refs_3_ = bf16[64,256]{1,0:T(8,128)(2,1)S(1)} collective-permute-done((bf16[64,256]{1,0:T(8,128)(2,1)S(1)}, bf16[64,256]{1,0:T(8,128)(2,1)S(1)}, u32[]{:S(2)}, u32[]{:S(2)}) %collective-permute-start.18) | collective-permute-done | bytes 32800 | tf_op jit(solution)/shard_map/ppermute | solution.py:570
  96.2 3.4 %all-to-all-start.2 = ((bf16[8,64,256]{2,1,0:T(8,128)(2,1)}), bf16[8,64,256]{2,1,0:T(8,128)(2,1)S(1)}, u32[]{:S(2)}, u32[]{:S(2)}) async-start(bf16[8,64,256]{2,1,0:T(8,128)(2,1)} %shard_map.149), calls=%async_computation.2 | async-start | bytes 524288 | tf_op jit(solution)/shard_map/all_to_all | solution.py:574
  99.7 2.4 %shard_map.148 = bf16[1,2,1024,128]{3,2,1,0:T(8,128)(2,1)} custom-call(s32[3]{0:T(128)S(1)} %pad_add_fusion.place_ref, bf16[512,128]{1,0:T(8,128)(2,1)S(1)} %get-tuple-element.39.grad_ref, f32[1,2048]{1,0:T(1,128)} %scale_ref.1, bf16[64,2048]{1,0:T(8,128)(2,1)} %bitcast.11), custom_call_target="tpu_custom_call" | custom-call | flops 67108864 | bytes 524288 | tf_op jit(solution)/shard_map/pallas_call | solution.py:519
  102.1 7.0 %all-to-all-done.2.in_ref = bf16[8,64,256]{2,1,0:T(8,128)(2,1)S(1)} async-done(((bf16[8,64,256]{2,1,0:T(8,128)(2,1)}), bf16[8,64,256]{2,1,0:T(8,128)(2,1)S(1)}, u32[]{:S(2)}, u32[]{:S(2)}) %all-to-all-start.2) | async-done | bytes 262176 | tf_op jit(solution)/shard_map/all_to_all | solution.py:574
  (41 shorter events, 10.9 us)
Async XLA Ops:
  3.4 9.6 %collective-permute-start.7 = (bf16[384,128]{1,0:T(8,128)(2,1)S(1)}, bf16[384,128]{1,0:T(8,128)(2,1)S(1)}, u32[]{:S(2)}, u32[]{:S(2)}) collective-permute-start(bf16[384,128]{1,0:T(8,128)(2,1)S(1)} %get-tuple-element.30), channel_id=1, source_target_pairs={{0,28},{4,24},{8,20},{12,16},{16,12},{20,8},{24,4},{28,0},{1,29},{... | collective-permute-start | bytes 294920 | tf_op jit(solution)/shard_map/ppermute | solution.py:570
  9.5 8.4 %collective-permute-start.9 = (bf16[384,128]{1,0:T(8,128)(2,1)S(1)}, bf16[384,128]{1,0:T(8,128)(2,1)S(1)}, u32[]{:S(2)}, u32[]{:S(2)}) collective-permute-start(bf16[384,128]{1,0:T(8,128)(2,1)S(1)} %get-tuple-element.32), channel_id=1, source_target_pairs={{0,20},{4,16},{8,28},{12,24},{16,4},{20,0},{24,12},{28,8},{1,21},{... | collective-permute-start | bytes 294920 | tf_op jit(solution)/shard_map/ppermute | solution.py:570
  9.5 37.9 %collective-permute-start.1 = (bf16[544,256]{1,0:T(8,128)(2,1)S(1)}, bf16[544,256]{1,0:T(8,128)(2,1)S(1)}, u32[]{:S(2)}, u32[]{:S(2)}) collective-permute-start(bf16[544,256]{1,0:T(8,128)(2,1)S(1)} %get-tuple-element.23), channel_id=1, source_target_pairs={{0,8},{4,12},{8,0},{12,4},{16,24},{20,28},{24,16},{28,20},{1,9},{5... | collective-permute-start | bytes 835592 | tf_op jit(solution)/shard_map/ppermute | solution.py:570
  10.1 30.8 %collective-permute-start = (bf16[384,256]{1,0:T(8,128)(2,1)S(1)}, bf16[384,256]{1,0:T(8,128)(2,1)S(1)}, u32[]{:S(2)}, u32[]{:S(2)}) collective-permute-start(bf16[384,256]{1,0:T(8,128)(2,1)S(1)} %get-tuple-element.22), channel_id=1, source_target_pairs={{0,4},{4,0},{8,12},{12,8},{16,20},{20,16},{24,28},{28,24},{1,5},{5... | collective-permute-start | bytes 589832 | tf_op jit(solution)/shard_map/ppermute | solution.py:570
  11.8 31.3 %collective-permute-start.2 = (bf16[384,256]{1,0:T(8,128)(2,1)S(1)}, bf16[384,256]{1,0:T(8,128)(2,1)S(1)}, u32[]{:S(2)}, u32[]{:S(2)}) collective-permute-start(bf16[384,256]{1,0:T(8,128)(2,1)S(1)} %get-tuple-element.24), channel_id=1, source_target_pairs={{0,12},{4,8},{8,4},{12,0},{16,28},{20,24},{24,20},{28,16},{1,13},{... | collective-permute-start | bytes 589832 | tf_op jit(solution)/shard_map/ppermute | solution.py:570
  13.0 16.6 %collective-permute-start.8 = (bf16[704,128]{1,0:T(8,128)(2,1)S(1)}, bf16[704,128]{1,0:T(8,128)(2,1)S(1)}, u32[]{:S(2)}, u32[]{:S(2)}) collective-permute-start(bf16[704,128]{1,0:T(8,128)(2,1)S(1)} %get-tuple-element.31), channel_id=1, source_target_pairs={{0,24},{4,28},{8,16},{12,20},{16,8},{20,12},{24,0},{28,4},{1,25},{... | collective-permute-start | bytes 540680 | tf_op jit(solution)/shard_map/ppermute | solution.py:570
  17.9 21.9 %collective-permute-start.10 = (bf16[704,128]{1,0:T(8,128)(2,1)S(1)}, bf16[704,128]{1,0:T(8,128)(2,1)S(1)}, u32[]{:S(2)}, u32[]{:S(2)}) collective-permute-start(bf16[704,128]{1,0:T(8,128)(2,1)S(1)} %get-tuple-element.33), channel_id=1, source_target_pairs={{0,16},{4,20},{8,24},{12,28},{16,0},{20,4},{24,8},{28,12},{1,17},{... | collective-permute-start | bytes 540680 | tf_op jit(solution)/shard_map/ppermute | solution.py:570
  29.6 23.0 %collective-permute-start.3 = (bf16[384,128]{1,0:T(8,128)(2,1)S(1)}, bf16[384,128]{1,0:T(8,128)(2,1)S(1)}, u32[]{:S(2)}, u32[]{:S(2)}) collective-permute-start(bf16[384,128]{1,0:T(8,128)(2,1)S(1)} %get-tuple-element.25), channel_id=1, source_target_pairs={{0,28},{4,24},{8,20},{12,16},{16,12},{20,8},{24,4},{28,0},{1,29},{... | collective-permute-start | bytes 294920 | tf_op jit(solution)/shard_map/ppermute | solution.py:570
  39.7 12.9 %collective-permute-start.4 = (bf16[384,128]{1,0:T(8,128)(2,1)S(1)}, bf16[384,128]{1,0:T(8,128)(2,1)S(1)}, u32[]{:S(2)}, u32[]{:S(2)}) collective-permute-start(bf16[384,128]{1,0:T(8,128)(2,1)S(1)} %get-tuple-element.26), channel_id=1, source_target_pairs={{0,24},{4,28},{8,16},{12,20},{16,8},{20,12},{24,0},{28,4},{1,25},{... | collective-permute-start | bytes 294920 | tf_op jit(solution)/shard_map/ppermute | solution.py:570
  40.9 11.7 %collective-permute-start.5 = (bf16[384,128]{1,0:T(8,128)(2,1)S(1)}, bf16[384,128]{1,0:T(8,128)(2,1)S(1)}, u32[]{:S(2)}, u32[]{:S(2)}) collective-permute-start(bf16[384,128]{1,0:T(8,128)(2,1)S(1)} %get-tuple-element.27), channel_id=1, source_target_pairs={{0,20},{4,16},{8,28},{12,24},{16,4},{20,0},{24,12},{28,8},{1,21},{... | collective-permute-start | bytes 294920 | tf_op jit(solution)/shard_map/ppermute | solution.py:570
  43.1 9.6 %collective-permute-start.6 = (bf16[384,128]{1,0:T(8,128)(2,1)S(1)}, bf16[384,128]{1,0:T(8,128)(2,1)S(1)}, u32[]{:S(2)}, u32[]{:S(2)}) collective-permute-start(bf16[384,128]{1,0:T(8,128)(2,1)S(1)} %get-tuple-element.28), channel_id=1, source_target_pairs={{0,16},{4,20},{8,24},{12,28},{16,0},{20,4},{24,8},{28,12},{1,17},{... | collective-permute-start | bytes 294920 | tf_op jit(solution)/shard_map/ppermute | solution.py:570
  53.0 8.3 %collective-permute-start.11 = (bf16[4,320,128]{2,1,0:T(8,128)(2,1)S(1)}, bf16[4,320,128]{2,1,0:T(8,128)(2,1)S(1)}, u32[]{:S(2)}, u32[]{:S(2)}) collective-permute-start(bf16[4,320,128]{2,1,0:T(8,128)(2,1)S(1)} %shard_map.143.held_ref), channel_id=1, source_target_pairs={{0,4},{4,0},{8,12},{12,8},{16,20},{20,16},{24,28},{28,24},{1,5},{5... | collective-permute-start | bytes 983048 | tf_op jit(solution)/shard_map/ppermute | solution.py:570
  53.1 20.1 %collective-permute-start.12 = (bf16[4,320,128]{2,1,0:T(8,128)(2,1)S(1)}, bf16[4,320,128]{2,1,0:T(8,128)(2,1)S(1)}, u32[]{:S(2)}, u32[]{:S(2)}) collective-permute-start(bf16[4,320,128]{2,1,0:T(8,128)(2,1)S(1)} %shard_map.143.held_ref), channel_id=1, source_target_pairs={{0,2},{1,3},{2,0},{3,1},{4,6},{5,7},{6,4},{7,5},{8,10},{9,11},{10,... | collective-permute-start | bytes 983048 | tf_op jit(solution)/shard_map/ppermute | solution.py:570
  62.1 3.9 %copy-start.1 = (bf16[8,128,128]{2,1,0:T(8,128)(2,1)S(1)}, bf16[8,128,128]{2,1,0:T(8,128)(2,1)}, u32[]{:S(2)}) copy-start(bf16[8,128,128]{2,1,0:T(8,128)(2,1)} %copy-done) | copy-start | bytes 786436
  62.1 11.2 %collective-permute-start.13 = (bf16[4,320,128]{2,1,0:T(8,128)(2,1)}, bf16[4,320,128]{2,1,0:T(8,128)(2,1)S(1)}, u32[]{:S(2)}, u32[]{:S(2)}) collective-permute-start(bf16[4,320,128]{2,1,0:T(8,128)(2,1)} %shard_map.144.got_ref), channel_id=1, source_target_pairs={{0,2},{1,3},{2,0},{3,1},{4,6},{5,7},{6,4},{7,5},{8,10},{9,11},{10,... | collective-permute-start | bytes 983048 | tf_op jit(solution)/shard_map/ppermute | solution.py:570
  62.6 10.7 %all-to-all-start = ((bf16[8,64,128]{2,1,0:T(8,128)(2,1)}), bf16[8,64,128]{2,1,0:T(8,128)(2,1)S(1)}, u32[]{:S(2)}, u32[]{:S(2)}) async-start(bf16[8,64,128]{2,1,0:T(8,128)(2,1)} %get-tuple-element.35), calls=%async_computation | async-start | bytes 262144 | tf_op jit(solution)/shard_map/all_to_all | solution.py:574
  66.0 1.0 copy-start.3
  67.7 18.3 %collective-permute-start.14 = (bf16[256,1280]{1,0:T(8,128)(2,1)S(1)}, bf16[256,1280]{1,0:T(8,128)(2,1)S(1)}, u32[]{:S(2)}, u32[]{:S(2)}) collective-permute-start(bf16[256,1280]{1,0:T(8,128)(2,1)S(1)} %shard_map.145.refs_0_), channel_id=1, source_target_pairs={{0,1},{1,0},{2,3},{3,2},{4,5},{5,4},{6,7},{7,6},{8,9},{9,8},{10,11... | collective-permute-start | bytes 1966088 | tf_op jit(solution)/shard_map/ppermute | solution.py:570
  74.0 12.0 %collective-permute-start.15 = (bf16[256,1280]{1,0:T(8,128)(2,1)S(1)}, bf16[256,1280]{1,0:T(8,128)(2,1)S(1)}, u32[]{:S(2)}, u32[]{:S(2)}) collective-permute-start(bf16[256,1280]{1,0:T(8,128)(2,1)S(1)} %shard_map.146.refs_1_), channel_id=1, source_target_pairs={{0,1},{1,0},{2,3},{3,2},{4,5},{5,4},{6,7},{7,6},{8,9},{9,8},{10,11... | collective-permute-start | bytes 1966088 | tf_op jit(solution)/shard_map/ppermute | solution.py:570
  74.7 11.2 %all-to-all-start.1 = ((bf16[8,64,128]{2,1,0:T(8,128)(2,1)}), bf16[8,64,128]{2,1,0:T(8,128)(2,1)S(1)}, u32[]{:S(2)}, u32[]{:S(2)}) async-start(bf16[8,64,128]{2,1,0:T(8,128)(2,1)} %shard_map.142), calls=%async_computation.1 | async-start | bytes 262144 | tf_op jit(solution)/shard_map/all_to_all | solution.py:574
  91.1 3.7 %collective-permute-start.18 = (bf16[64,256]{1,0:T(8,128)(2,1)S(1)}, bf16[64,256]{1,0:T(8,128)(2,1)S(1)}, u32[]{:S(2)}, u32[]{:S(2)}) collective-permute-start(bf16[64,256]{1,0:T(8,128)(2,1)S(1)} %get-tuple-element.40.refs_0_), channel_id=1, source_target_pairs={{0,3},{1,2},{2,1},{3,0},{4,7},{5,6},{6,5},{7,4},{8,11},{9,10},{10,... | collective-permute-start | bytes 98312 | tf_op jit(solution)/shard_map/ppermute | solution.py:570
  91.5 4.0 %collective-permute-start.17 = (bf16[64,256]{1,0:T(8,128)(2,1)S(1)}, bf16[64,256]{1,0:T(8,128)(2,1)S(1)}, u32[]{:S(2)}, u32[]{:S(2)}) collective-permute-start(bf16[64,256]{1,0:T(8,128)(2,1)S(1)} %get-tuple-element.40.refs_0_), channel_id=1, source_target_pairs={{0,2},{1,3},{2,0},{3,1},{4,6},{5,7},{6,4},{7,5},{8,10},{9,11},{10,... | collective-permute-start | bytes 98312 | tf_op jit(solution)/shard_map/ppermute | solution.py:570
  92.8 2.7 %collective-permute-start.16 = (bf16[64,256]{1,0:T(8,128)(2,1)S(1)}, bf16[64,256]{1,0:T(8,128)(2,1)S(1)}, u32[]{:S(2)}, u32[]{:S(2)}) collective-permute-start(bf16[64,256]{1,0:T(8,128)(2,1)S(1)} %get-tuple-element.40.refs_0_), channel_id=1, source_target_pairs={{0,1},{1,0},{2,3},{3,2},{4,5},{5,4},{6,7},{7,6},{8,9},{9,8},{10,11... | collective-permute-start | bytes 98312 | tf_op jit(solution)/shard_map/ppermute | solution.py:570
  96.2 12.8 %all-to-all-start.2 = ((bf16[8,64,256]{2,1,0:T(8,128)(2,1)}), bf16[8,64,256]{2,1,0:T(8,128)(2,1)S(1)}, u32[]{:S(2)}, u32[]{:S(2)}) async-start(bf16[8,64,256]{2,1,0:T(8,128)(2,1)} %shard_map.149), calls=%async_computation.2 | async-start | bytes 524288 | tf_op jit(solution)/shard_map/all_to_all | solution.py:574
  (2 other events, 1.4 us)

commit v6 on v5

--- a/solution.py
+++ b/solution.py
@@ -58,7 +58,7 @@
         self.rows = self.part_rows + 2 * tok_rows
         self.share_rows = self.share * self.local
         self.chunks = VW // HD
-        self.riding = self.local % 8 == 0 and self.share_rows % 16 == 0 and seq_count >= 4
+        self.riding = self.local % 8 == 0 and self.share_rows % 16 == 0 and seq_count == 8
         self.ride_rows = self.chunks * self.share_rows if self.riding else 0
 
     def pieces(self):
@@ -71,7 +71,7 @@
         return listed + [(0, every)]
 
     def rides(self, piece):
-        return self.riding and piece[0] % 2 == 0 and 0 in piece[1]
+        return self.riding and piece[0] in (0, 4) and 0 in piece[1]
 
     def piece_shape(self, piece):
         wide = len(piece[1])
@@ -188,6 +188,23 @@
     )(*arrays, *others)
 
 
+def join_kernel(first_ref, second_ref, *refs):
+    out_ref = refs[-1]
+    count = first_ref.shape[0]
+    out_ref[:count] = first_ref[...]
+    out_ref[count:] = second_ref[...]
+
+
+def join(first, second, others):
+    return pl.pallas_call(
+        join_kernel,
+        out_shape=jax.ShapeDtypeStruct((2 * first.shape[0],) + first.shape[1:], BF16),
+        in_specs=[VMEM_SPEC] * 2 + [ANY_SPEC] * len(others),
+        out_specs=VMEM_SPEC,
+        compiler_params=limits(),
+    )(first, second, *others)
+
+
 def arrange_kernel(sizes, masks, place_ref, held_ref, got_ref, wait_ref, out_ref):
     del wait_ref
     me = place_ref[0]
@@ -213,7 +230,7 @@
     return pl.pallas_call(
         functools.partial(arrange_kernel, sizes, masks),
         out_shape=jax.ShapeDtypeStruct((rows, VW), BF16),
-        in_specs=[SMEM_SPEC, VMEM_SPEC, VMEM_SPEC, ANY_SPEC],
+        in_specs=[SMEM_SPEC, VMEM_SPEC, VMEM_SPEC, VMEM_SPEC],
         out_specs=VMEM_SPEC,
         compiler_params=limits(),
     )(place, held, got, wait)
@@ -227,11 +244,11 @@
     before_ref = None
     if head:
         before_ref, *refs = refs
-    mod_ref, lat_ref, query_scr, key_scr, value_scr, scale_scr, shift_scr, proj_scr, *refs = refs
-    sems, side_sems = refs
+    mod_ref, lat_ref, query_scr, key_scr, turned_scr, value_scr, *refs = refs
+    scale_scr, shift_scr, proj_scr, sems, side_sems = refs
     half = part_rows // 2
     lat_rows = count * tok_rows
-    factor = HD ** (-0.5) * math.log2(math.e)
+    factor = HD ** (-0.5)
     me = place_ref[0]
     mine = pl.ds(pl.multiple_of(place_ref[2] * width + head * HD, HD), HD)
     copies = []
@@ -260,16 +277,17 @@
         copy.wait()
     gain = 1.0 + scale_scr[...]
     shift = shift_scr[...]
-    proj = proj_scr[...]
+    turned_scr[...] = key_scr[...].astype(F32).T.astype(BF16)
+    proj = proj_scr[...].astype(F32).T.astype(BF16)
     zero = jnp.zeros_like(proj)
     proj_pair = jnp.concatenate(
         [jnp.concatenate([proj, zero], axis=1), jnp.concatenate([zero, proj], axis=1)], axis=0
     )
-    block = min(count * part_rows, max(part_rows, min(256, (1 << 18) // lat_rows)))
+    block = min(count * part_rows, max(part_rows, min(128, (1 << 18) // lat_rows)))
     for first in range(0, count * part_rows, block):
-        logits = mm_nt(query_scr[pl.ds(first, block), :], key_scr[...])
+        logits = mm(query_scr[pl.ds(first, block), :], turned_scr[...])
         top = jnp.max(logits, axis=-1, keepdims=True)
-        weights = jnp.exp2((logits - top) * factor).astype(BF16)
+        weights = jnp.exp((logits - top) * factor).astype(BF16)
         both = mm(weights, value_scr[...])
         modulated = (both[:, :HD] / both[:, HD:] * gain + shift).astype(BF16)
         for at in range(0, block, part_rows):
@@ -278,7 +296,7 @@
             pair = jnp.concatenate(
                 [modulated[at : at + half], modulated[at + half : at + part_rows]], axis=1
             )
-            latent = mm_nt(pair, proj_pair)
+            latent = mm(pair, proj_pair)
             if head:
                 latent = latent + before_ref[place]
             lat_ref[place] = latent.astype(lat_ref.dtype)
@@ -300,6 +318,7 @@
         scratch_shapes=[
             pltpu.VMEM((query_rows, HD), BF16),
             pltpu.VMEM((lat_rows, HD), BF16),
+            pltpu.VMEM((HD, lat_rows), BF16),
             pltpu.VMEM((lat_rows, 2 * HD), BF16),
             pltpu.VMEM((1, HD), F32),
             pltpu.VMEM((1, HD), F32),
@@ -413,17 +432,18 @@
     )
     flow = pooled_grad * pre * (1.0 / patches)
     embed_grad = rstd * (flow - lane_mean(flow, VW) - unit * lane_mean(flow * unit, VW))
-    high = embed_grad.astype(BF16)
-    low = (embed_grad - high.astype(F32)).astype(BF16)
-    stacked = jnp.concatenate([high, low], axis=0)
+    turned = embed_grad.T
+    high = turned.astype(BF16)
+    low = (turned - high.astype(F32)).astype(BF16)
+    both = mm(embed_ref[...], jnp.concatenate([high, low], axis=1))
+    position_grad = both[:, :patches] + both[:, patches:]
     for hi in range(2):
-        sides = []
-        for side in range(2):
-            both = mm_nt(stacked, position_rows(2 * hi + side))
-            sides.append(both[:patches] + both[patches:])
         for tx in range(4):
-            lanes = slice(tx * CH, (tx + 1) * CH)
-            piece = jnp.concatenate([sides[0][:, lanes], sides[1][:, lanes]], axis=1)
+            first = ((2 * hi) * 4 + tx) * CH
+            second = ((2 * hi + 1) * 4 + tx) * CH
+            piece = jnp.concatenate(
+                [position_grad[first : first + CH], position_grad[second : second + CH]], axis=0
+            ).T
             for pr in range(patch_rows):
                 grad_scr[pl.ds((2 * pr + hi) * GW + tx, patch_cols, stride=4), :] = piece[
                     pr * patch_cols : (pr + 1) * patch_cols
@@ -437,12 +457,13 @@
 
 
 def store_readout_grad(grad, mod_refs, out_factor, out_ref):
+    turned = grad.astype(F32).T.astype(BF16)
     for head, mod_ref in enumerate(mod_refs):
         count, rows, width = mod_ref.shape
         half = rows // 2
         first = mod_ref[:, :half, :].reshape(count * half, width)
         second = mod_ref[:, half:, :].reshape(count * half, width)
-        total = mm_tn(grad, first)[:CH] + mm_tn(grad, second)[CH:]
+        total = mm(turned[:CH], first) + mm(turned[CH:], second)
         out_ref[:, pl.ds(head * width, width)] = (total * out_factor).astype(BF16)
 
 
@@ -577,16 +598,15 @@
 
 
 def after_kernel(*refs):
-    del refs
+    refs[-1][...] = refs[0][...]
 
 
 def after(x, others):
     return pl.pallas_call(
         after_kernel,
         out_shape=jax.ShapeDtypeStruct(x.shape, x.dtype),
-        in_specs=[ANY_SPEC] * (1 + len(others)),
-        out_specs=ANY_SPEC,
-        input_output_aliases={0: 0},
+        in_specs=[VMEM_SPEC] * (1 + len(others)),
+        out_specs=VMEM_SPEC,
     )(x, *others)
 
 
@@ -632,13 +652,15 @@
     modulated, latent_part = [], []
     for head in range(head_count):
         slots = [slot for slot, piece in enumerate(pieces) if head in piece[1]]
+        if head == 0 and sizes.riding:
+            ride = [slot for slot, piece in enumerate(pieces) if sizes.rides(piece)]
+            two = collect(
+                sizes, [pieces[slot] for slot in ride], [received[slot] for slot in ride], []
+            )
+            other_two = swap(two, "seq", 2)
         if head == head_count - 1 and sizes.riding:
-            even = [slot for slot, piece in enumerate(pieces) if sizes.rides(piece)]
-            rest = [x for slot, x in enumerate(received) if slot not in even]
-            held = collect(
-                sizes, [pieces[slot] for slot in even], [received[slot] for slot in even],
-                rest + modulated,
-            )
+            rest = [received[slot] for slot in slots if slot not in ride]
+            held = join(two, other_two, rest + modulated)
             got = swap(held, "seq", 1)
             far_held = swap(held, "dp", bits[0]) if shared else None
         mod, latent_sum = attend(
@@ -650,7 +672,8 @@
 
     if sizes.riding:
         got = after(got, [modulated[-1]])
-        even_masks = [pieces[slot][0] for slot in even]
+        even_masks = [pieces[slot][0] for slot in ride]
+        even_masks = even_masks + [mask ^ 2 for mask in even_masks]
         embed = [(arrange(sizes, even_masks, place, held, got, modulated[-1]), 0)]
         far_got = swap(got, "dp", bits[0]) if shared else None
     else:

time: 111 us -> 115 us (1.036)
  waiting for transfers between devices: 40.6 us -> 33.1 us
  starting transfers between devices: 39.9 us -> 46.8 us
  Pallas kernels: 25.5 us -> 30 us
    ppermute x19 -> x20, waiting for transfers between devices: 20.9 us -> 13.5 us  [swap(): return lax.ppermute(x, axis, [(i, i ^ mask) for i in range(count)])]
    ppermute x19 -> x20, starting transfers between devices: 29.8 us -> 36 us  [swap(): return lax.ppermute(x, axis, [(i, i ^ mask) for i in range(count)])]
    pallas_call x2, Pallas kernels: 11.2 us -> 13.9 us  [attend(): pl.pallas_call(functools.partial(attend_kernel, sizes, head, pieces), out...]
    pallas_call x1, Pallas kernels: 0.01 us -> 1.79 us  [after(): pl.pallas_call(after_kernel, out_shape=jax.ShapeDtypeStruct(x.shape, x.dt...]
  transfers between devices with their start and end apart: 22 -> 23, of which waited for: 8 -> 11; matrix products, arithmetic and copies ran while one was open for 0% -> 0% of each run, Pallas kernels for 14% -> 18%
where the time goes in v6:
time: 115 us; the launch traced here: 114 us
  starting transfers between devices  46.8 us (41%)
  waiting for transfers between devices  33.1 us (29%)
  Pallas kernels  30 us (26%)
  local copies, waits for them, and re-layouts  2.38 us (2%)
  between operations  1.43 us (1%)
    ppermute x20, starting transfers between devices, swap(): return lax.ppermute(x, axis, [(i, i ^ mask) for i in range(count)])  36 us
    all_to_all x3, waiting for transfers between devices, all_to_all(): lax.all_to_all(x, 'seq', split_axis=0, concat_axis=0, tiled=True, axis_in...  19.6 us
    pallas_call x2, Pallas kernels, attend(): pl.pallas_call(functools.partial(attend_kernel, sizes, head, pieces), out...  13.9 us
    ppermute x20, waiting for transfers between devices, swap(): return lax.ppermute(x, axis, [(i, i ^ mask) for i in range(count)])  13.5 us
    all_to_all x3, starting transfers between devices, all_to_all(): lax.all_to_all(x, 'seq', split_axis=0, concat_axis=0, tiled=True, axis_in...  10.8 us
    pallas_call x1, Pallas kernels, reward_head(): pl.pallas_call(functools.partial(head_kernel, grid_rows, len(modulated),...  5.41 us
    pallas_call x1, Pallas kernels, pack(): pl.pallas_call(functools.partial(pack_kernel, sizes), out_shape=[jax.Shap...  2.7 us
    pallas_call x1, Pallas kernels, spread(): pl.pallas_call(functools.partial(spread_kernel, count, half, heads), out_...  2.41 us
  transfers between devices with their start and end apart: 23, of which 11 were waited for; matrix products, arithmetic and copies ran while one was open for 0% of the time, Pallas kernels for 18%

profile of v6, /device:TPU:0, one launch (start us, length us, event | category | flops | bytes accessed | tf_op | source)
XLA Modules:
  0.0 113.8 jit_solution(14011816118170648565)
XLA Ops:
  0.7 2.7 %shard_map.139 = (bf16[384,128]{1,0:T(8,128)(2,1)S(1)}, bf16[384,128]{1,0:T(8,128)(2,1)S(1)}, bf16[384,128]{1,0:T(8,128)(2,1)S(1)}, bf16[704,128]{1,0:T(8,128)(2...) custom-call(s32[3]{0:T(128)S(1)} %pad_add_fusion.place_ref, ...), custom_call_target="tpu_custom_call" | custom-call | bytes 3145728 | tf_op jit(solution)/shard_map/pallas_call | solution.py:145
  3.4 4.1 %collective-permute-start.10 = (bf16[704,128]{1,0:T(8,128)(2,1)S(1)}, bf16[704,128]{1,0:T(8,128)(2,1)S(1)}, u32[]{:S(2)}, u32[]{:S(2)}) collective-permute-start(bf16[704,128]{1,0:T(8,128)(2,1)S(1)} %get-tuple-element.33), channel_id=1, source_target_pairs={{0,16},{4,20},{8,24},{12,28},{16,0},{20,4},{24,8},{28,12},{1,17},{... | collective-permute-start | bytes 540680 | tf_op jit(solution)/shard_map/ppermute | solution.py:591
  7.5 2.3 %collective-permute-start.7 = (bf16[384,128]{1,0:T(8,128)(2,1)S(1)}, bf16[384,128]{1,0:T(8,128)(2,1)S(1)}, u32[]{:S(2)}, u32[]{:S(2)}) collective-permute-start(bf16[384,128]{1,0:T(8,128)(2,1)S(1)} %get-tuple-element.30), channel_id=1, source_target_pairs={{0,28},{4,24},{8,20},{12,16},{16,12},{20,8},{24,4},{28,0},{1,29},{... | collective-permute-start | bytes 294920 | tf_op jit(solution)/shard_map/ppermute | solution.py:591
  10.6 2.7 %collective-permute-start.2 = (bf16[384,256]{1,0:T(8,128)(2,1)S(1)}, bf16[384,256]{1,0:T(8,128)(2,1)S(1)}, u32[]{:S(2)}, u32[]{:S(2)}) collective-permute-start(bf16[384,256]{1,0:T(8,128)(2,1)S(1)} %get-tuple-element.24), channel_id=1, source_target_pairs={{0,12},{4,8},{8,4},{12,0},{16,28},{20,24},{24,20},{28,16},{1,13},{... | collective-permute-start | bytes 589832 | tf_op jit(solution)/shard_map/ppermute | solution.py:591
  13.3 4.1 %collective-permute-done.7.refs_0_ = bf16[384,128]{1,0:T(8,128)(2,1)S(1)} collective-permute-done((bf16[384,128]{1,0:T(8,128)(2,1)S(1)}, bf16[384,128]{1,0:T(8,128)(2,1)S(1)}, u32[]{:S(2)}, u32[]{:S(2)}) %collective-permute-start.7) | collective-permute-done | bytes 98336 | tf_op jit(solution)/shard_map/ppermute | solution.py:591
  17.4 2.5 %collective-permute-start.8 = (bf16[384,128]{1,0:T(8,128)(2,1)S(1)}, bf16[384,128]{1,0:T(8,128)(2,1)S(1)}, u32[]{:S(2)}, u32[]{:S(2)}) collective-permute-start(bf16[384,128]{1,0:T(8,128)(2,1)S(1)} %get-tuple-element.31), channel_id=1, source_target_pairs={{0,24},{4,28},{8,16},{12,20},{16,8},{20,12},{24,0},{28,4},{1,25},{... | collective-permute-start | bytes 294920 | tf_op jit(solution)/shard_map/ppermute | solution.py:591
  19.9 5.9 %collective-permute-start.9 = (bf16[384,128]{1,0:T(8,128)(2,1)S(1)}, bf16[384,128]{1,0:T(8,128)(2,1)S(1)}, u32[]{:S(2)}, u32[]{:S(2)}) collective-permute-start(bf16[384,128]{1,0:T(8,128)(2,1)S(1)} %get-tuple-element.32), channel_id=1, source_target_pairs={{0,20},{4,16},{8,28},{12,24},{16,4},{20,0},{24,12},{28,8},{1,21},{... | collective-permute-start | bytes 294920 | tf_op jit(solution)/shard_map/ppermute | solution.py:591
  25.9 1.8 %collective-permute-done.8.refs_1_ = bf16[384,128]{1,0:T(8,128)(2,1)S(1)} collective-permute-done((bf16[384,128]{1,0:T(8,128)(2,1)S(1)}, bf16[384,128]{1,0:T(8,128)(2,1)S(1)}, u32[]{:S(2)}, u32[]{:S(2)}) %collective-permute-start.8) | collective-permute-done | bytes 98336 | tf_op jit(solution)/shard_map/ppermute | solution.py:591
  27.7 4.8 %collective-permute-start.11 = (bf16[2,320,128]{2,1,0:T(8,128)(2,1)S(1)}, bf16[2,320,128]{2,1,0:T(8,128)(2,1)S(1)}, u32[]{:S(2)}, u32[]{:S(2)}) collective-permute-start(bf16[2,320,128]{2,1,0:T(8,128)(2,1)S(1)} %shard_map.143.first_ref), channel_id=1, source_target_pairs={{0,8},{4,12},{8,0},{12,4},{16,24},{20,28},{24,16},{28,20},{1,9},{5... | collective-permute-start | bytes 491528 | tf_op jit(solution)/shard_map/ppermute | solution.py:591
  34.0 2.0 %collective-permute-start.3 = (bf16[384,128]{1,0:T(8,128)(2,1)S(1)}, bf16[384,128]{1,0:T(8,128)(2,1)S(1)}, u32[]{:S(2)}, u32[]{:S(2)}) collective-permute-start(bf16[384,128]{1,0:T(8,128)(2,1)S(1)} %get-tuple-element.25), channel_id=1, source_target_pairs={{0,28},{4,24},{8,20},{12,16},{16,12},{20,8},{24,4},{28,0},{1,29},{... | collective-permute-start | bytes 294920 | tf_op jit(solution)/shard_map/ppermute | solution.py:591
  36.1 2.6 %collective-permute-start.4 = (bf16[384,128]{1,0:T(8,128)(2,1)S(1)}, bf16[384,128]{1,0:T(8,128)(2,1)S(1)}, u32[]{:S(2)}, u32[]{:S(2)}) collective-permute-start(bf16[384,128]{1,0:T(8,128)(2,1)S(1)} %get-tuple-element.26), channel_id=1, source_target_pairs={{0,24},{4,28},{8,16},{12,20},{16,8},{20,12},{24,0},{28,4},{1,25},{... | collective-permute-start | bytes 294920 | tf_op jit(solution)/shard_map/ppermute | solution.py:591
  38.7 3.0 %collective-permute-start.6 = (bf16[384,128]{1,0:T(8,128)(2,1)S(1)}, bf16[384,128]{1,0:T(8,128)(2,1)S(1)}, u32[]{:S(2)}, u32[]{:S(2)}) collective-permute-start(bf16[384,128]{1,0:T(8,128)(2,1)S(1)} %get-tuple-element.28), channel_id=1, source_target_pairs={{0,16},{4,20},{8,24},{12,28},{16,0},{20,4},{24,8},{28,12},{1,17},{... | collective-permute-start | bytes 294920 | tf_op jit(solution)/shard_map/ppermute | solution.py:591
  41.7 6.6 %shard_map.140 = (bf16[8,128,128]{2,1,0:T(8,128)(2,1)S(1)}, f32[8,64,128]{2,1,0:T(8,128)S(1)}) custom-call(s32[3]{0:T(128)S(1)} %pad_add_fusion.place_ref, bf16[384,128]{1,0:T(8,128)(2,1)S(1)} %collective-permute-done.7.refs_0_, bf16[384,128]{1,0:T(8,128)(2,1)S(1)} %collective-permute-done.8.refs_1_, bf16[384,128]{1,0:T(8,128)(2,1)S(1)} %collective-permute-done.9.refs_2_, ...), custom_call_target="tpu_custom_call" | custom-call | flops 536870912 | bytes 1048576 | tf_op jit(solution)/shard_map/pallas_call | solution.py:310
  48.3 2.6 %collective-permute-done.5.refs_5_ = bf16[384,128]{1,0:T(8,128)(2,1)S(1)} collective-permute-done((bf16[384,128]{1,0:T(8,128)(2,1)S(1)}, bf16[384,128]{1,0:T(8,128)(2,1)S(1)}, u32[]{:S(2)}, u32[]{:S(2)}) %collective-permute-start.5) | collective-permute-done | bytes 98336 | tf_op jit(solution)/shard_map/ppermute | solution.py:591
  53.1 7.3 %shard_map.141 = (bf16[8,128,128]{2,1,0:T(8,128)(2,1)S(1)}, bf16[8,64,128]{2,1,0:T(8,128)(2,1)}) custom-call(s32[3]{0:T(128)S(1)} %pad_add_fusion.place_ref, bf16[384,256]{1,0:T(8,128)(2,1)S(1)} %collective-permute-done.refs_4_.refs_0_, bf16[384,256]{1,0:T(8,128)(2,1)S(1)} %collective-permute-done.1.refs_5_.refs_1_, ...), custom_call_target="tpu_custom_call" | custom-call | flops 536870912 | bytes 1048576 | tf_op jit(solution)/shard_map/pallas_call | solution.py:310
  63.3 1.8 %shard_map.145.got_ref = bf16[4,320,128]{2,1,0:T(8,128)(2,1)} custom-call(bf16[4,320,128]{2,1,0:T(8,128)(2,1)} %copy-done.3, bf16[8,128,128]{2,1,0:T(8,128)(2,1)} %copy-done), custom_call_target="tpu_custom_call" | custom-call | tf_op jit(solution)/shard_map/pallas_call | solution.py:605
  65.6 3.5 %all-to-all-start = ((bf16[8,64,128]{2,1,0:T(8,128)(2,1)}), bf16[8,64,128]{2,1,0:T(8,128)(2,1)S(1)}, u32[]{:S(2)}, u32[]{:S(2)}) async-start(bf16[8,64,128]{2,1,0:T(8,128)(2,1)} %get-tuple-element.35), calls=%async_computation | async-start | bytes 262144 | tf_op jit(solution)/shard_map/all_to_all | solution.py:595
  70.9 5.6 %all-to-all-done.refs_0_.wait_ref = bf16[8,64,128]{2,1,0:T(8,128)(2,1)S(1)} async-done(((bf16[8,64,128]{2,1,0:T(8,128)(2,1)}), bf16[8,64,128]{2,1,0:T(8,128)(2,1)S(1)}, u32[]{:S(2)}, u32[]{:S(2)}) %all-to-all-start) | async-done | bytes 131104 | tf_op jit(solution)/shard_map/all_to_all | solution.py:595
  78.4 3.7 %all-to-all-start.1 = ((bf16[8,64,128]{2,1,0:T(8,128)(2,1)}), bf16[8,64,128]{2,1,0:T(8,128)(2,1)S(1)}, u32[]{:S(2)}, u32[]{:S(2)}) async-start(bf16[8,64,128]{2,1,0:T(8,128)(2,1)} %shard_map.142), calls=%async_computation.1 | async-start | bytes 262144 | tf_op jit(solution)/shard_map/all_to_all | solution.py:595
  82.7 7.0 %all-to-all-done.1 = bf16[8,64,128]{2,1,0:T(8,128)(2,1)S(1)} async-done(((bf16[8,64,128]{2,1,0:T(8,128)(2,1)}), bf16[8,64,128]{2,1,0:T(8,128)(2,1)S(1)}, u32[]{:S(2)}, u32[]{:S(2)}) %all-to-all-start.1) | async-done | bytes 131104 | tf_op jit(solution)/shard_map/all_to_all | solution.py:595
  89.7 5.4 %shard_map.148 = (f32[1,128]{1,0:T(1,128)}, bf16[512,128]{1,0:T(8,128)(2,1)S(1)}, bf16[64,256]{1,0:T(8,128)(2,1)S(1)}) custom-call(s32[3]{0:T(128)S(1)} %pad_add_fusion.place_ref, bf16[512,128]{1,0:T(8,128)(2,1)S(1)} %bitcast.7, bf16[256,1280]{1,0:T(8,128)(2,1)S(1)} %shard_map.146.refs_0_, bf16[256,1280]{1,0:T(8,128)(2,1)S(1)} %shard_map.147.refs_1_, ...), custom_call_target="tpu_custom_call" | custom-call | flops 503316480 | bytes 2785280 | tf_op jit(solution)/shard_map/pallas_call | solution.py:477
  100.0 3.6 %all-to-all-start.2 = ((bf16[8,64,256]{2,1,0:T(8,128)(2,1)}), bf16[8,64,256]{2,1,0:T(8,128)(2,1)S(1)}, u32[]{:S(2)}, u32[]{:S(2)}) async-start(bf16[8,64,256]{2,1,0:T(8,128)(2,1)} %shard_map.150), calls=%async_computation.2 | async-start | bytes 524288 | tf_op jit(solution)/shard_map/all_to_all | solution.py:595
  103.5 2.4 %shard_map.149 = bf16[1,2,1024,128]{3,2,1,0:T(8,128)(2,1)} custom-call(s32[3]{0:T(128)S(1)} %pad_add_fusion.place_ref, bf16[512,128]{1,0:T(8,128)(2,1)S(1)} %get-tuple-element.39.grad_ref, f32[1,2048]{1,0:T(1,128)} %scale_ref.1, bf16[64,2048]{1,0:T(8,128)(2,1)} %bitcast.11), custom_call_target="tpu_custom_call" | custom-call | flops 67108864 | bytes 524288 | tf_op jit(solution)/shard_map/pallas_call | solution.py:540
  105.9 7.1 %all-to-all-done.2.in_ref = bf16[8,64,256]{2,1,0:T(8,128)(2,1)S(1)} async-done(((bf16[8,64,256]{2,1,0:T(8,128)(2,1)}), bf16[8,64,256]{2,1,0:T(8,128)(2,1)S(1)}, u32[]{:S(2)}, u32[]{:S(2)}) %all-to-all-start.2) | async-done | bytes 262176 | tf_op jit(solution)/shard_map/all_to_all | solution.py:595
  (44 shorter events, 17.4 us)
Async XLA Ops:
  3.4 16.5 %collective-permute-start.10 = (bf16[704,128]{1,0:T(8,128)(2,1)S(1)}, bf16[704,128]{1,0:T(8,128)(2,1)S(1)}, u32[]{:S(2)}, u32[]{:S(2)}) collective-permute-start(bf16[704,128]{1,0:T(8,128)(2,1)S(1)} %get-tuple-element.33), channel_id=1, source_target_pairs={{0,16},{4,20},{8,24},{12,28},{16,0},{20,4},{24,8},{28,12},{1,17},{... | collective-permute-start | bytes 540680 | tf_op jit(solution)/shard_map/ppermute | solution.py:591
  7.5 9.9 %collective-permute-start.7 = (bf16[384,128]{1,0:T(8,128)(2,1)S(1)}, bf16[384,128]{1,0:T(8,128)(2,1)S(1)}, u32[]{:S(2)}, u32[]{:S(2)}) collective-permute-start(bf16[384,128]{1,0:T(8,128)(2,1)S(1)} %get-tuple-element.30), channel_id=1, source_target_pairs={{0,28},{4,24},{8,20},{12,16},{16,12},{20,8},{24,4},{28,0},{1,29},{... | collective-permute-start | bytes 294920 | tf_op jit(solution)/shard_map/ppermute | solution.py:591
  9.8 26.2 %collective-permute-start = (bf16[384,256]{1,0:T(8,128)(2,1)S(1)}, bf16[384,256]{1,0:T(8,128)(2,1)S(1)}, u32[]{:S(2)}, u32[]{:S(2)}) collective-permute-start(bf16[384,256]{1,0:T(8,128)(2,1)S(1)} %get-tuple-element.22), channel_id=1, source_target_pairs={{0,4},{4,0},{8,12},{12,8},{16,20},{20,16},{24,28},{28,24},{1,5},{5... | collective-permute-start | bytes 589832 | tf_op jit(solution)/shard_map/ppermute | solution.py:591
  10.3 28.4 %collective-permute-start.1 = (bf16[384,256]{1,0:T(8,128)(2,1)S(1)}, bf16[384,256]{1,0:T(8,128)(2,1)S(1)}, u32[]{:S(2)}, u32[]{:S(2)}) collective-permute-start(bf16[384,256]{1,0:T(8,128)(2,1)S(1)} %get-tuple-element.23), channel_id=1, source_target_pairs={{0,8},{4,12},{8,0},{12,4},{16,24},{20,28},{24,16},{28,20},{1,9},{5... | collective-permute-start | bytes 589832 | tf_op jit(solution)/shard_map/ppermute | solution.py:591
  10.6 28.1 %collective-permute-start.2 = (bf16[384,256]{1,0:T(8,128)(2,1)S(1)}, bf16[384,256]{1,0:T(8,128)(2,1)S(1)}, u32[]{:S(2)}, u32[]{:S(2)}) collective-permute-start(bf16[384,256]{1,0:T(8,128)(2,1)S(1)} %get-tuple-element.24), channel_id=1, source_target_pairs={{0,12},{4,8},{8,4},{12,0},{16,28},{20,24},{24,20},{28,16},{1,13},{... | collective-permute-start | bytes 589832 | tf_op jit(solution)/shard_map/ppermute | solution.py:591
  17.4 10.3 %collective-permute-start.8 = (bf16[384,128]{1,0:T(8,128)(2,1)S(1)}, bf16[384,128]{1,0:T(8,128)(2,1)S(1)}, u32[]{:S(2)}, u32[]{:S(2)}) collective-permute-start(bf16[384,128]{1,0:T(8,128)(2,1)S(1)} %get-tuple-element.31), channel_id=1, source_target_pairs={{0,24},{4,28},{8,16},{12,20},{16,8},{20,12},{24,0},{28,4},{1,25},{... | collective-permute-start | bytes 294920 | tf_op jit(solution)/shard_map/ppermute | solution.py:591
  19.9 14.1 %collective-permute-start.9 = (bf16[384,128]{1,0:T(8,128)(2,1)S(1)}, bf16[384,128]{1,0:T(8,128)(2,1)S(1)}, u32[]{:S(2)}, u32[]{:S(2)}) collective-permute-start(bf16[384,128]{1,0:T(8,128)(2,1)S(1)} %get-tuple-element.32), channel_id=1, source_target_pairs={{0,20},{4,16},{8,28},{12,24},{16,4},{20,0},{24,12},{28,8},{1,21},{... | collective-permute-start | bytes 294920 | tf_op jit(solution)/shard_map/ppermute | solution.py:591
  27.7 24.1 %collective-permute-start.11 = (bf16[2,320,128]{2,1,0:T(8,128)(2,1)S(1)}, bf16[2,320,128]{2,1,0:T(8,128)(2,1)S(1)}, u32[]{:S(2)}, u32[]{:S(2)}) collective-permute-start(bf16[2,320,128]{2,1,0:T(8,128)(2,1)S(1)} %shard_map.143.first_ref), channel_id=1, source_target_pairs={{0,8},{4,12},{8,0},{12,4},{16,24},{20,28},{24,16},{28,20},{1,9},{5... | collective-permute-start | bytes 491528 | tf_op jit(solution)/shard_map/ppermute | solution.py:591
  34.0 14.3 %collective-permute-start.3 = (bf16[384,128]{1,0:T(8,128)(2,1)S(1)}, bf16[384,128]{1,0:T(8,128)(2,1)S(1)}, u32[]{:S(2)}, u32[]{:S(2)}) collective-permute-start(bf16[384,128]{1,0:T(8,128)(2,1)S(1)} %get-tuple-element.25), channel_id=1, source_target_pairs={{0,28},{4,24},{8,20},{12,16},{16,12},{20,8},{24,4},{28,0},{1,29},{... | collective-permute-start | bytes 294920 | tf_op jit(solution)/shard_map/ppermute | solution.py:591
  36.1 12.3 %collective-permute-start.4 = (bf16[384,128]{1,0:T(8,128)(2,1)S(1)}, bf16[384,128]{1,0:T(8,128)(2,1)S(1)}, u32[]{:S(2)}, u32[]{:S(2)}) collective-permute-start(bf16[384,128]{1,0:T(8,128)(2,1)S(1)} %get-tuple-element.26), channel_id=1, source_target_pairs={{0,24},{4,28},{8,16},{12,20},{16,8},{20,12},{24,0},{28,4},{1,25},{... | collective-permute-start | bytes 294920 | tf_op jit(solution)/shard_map/ppermute | solution.py:591
  38.7 12.2 %collective-permute-start.5 = (bf16[384,128]{1,0:T(8,128)(2,1)S(1)}, bf16[384,128]{1,0:T(8,128)(2,1)S(1)}, u32[]{:S(2)}, u32[]{:S(2)}) collective-permute-start(bf16[384,128]{1,0:T(8,128)(2,1)S(1)} %get-tuple-element.27), channel_id=1, source_target_pairs={{0,20},{4,16},{8,28},{12,24},{16,4},{20,0},{24,12},{28,8},{1,21},{... | collective-permute-start | bytes 294920 | tf_op jit(solution)/shard_map/ppermute | solution.py:591
  38.7 13.1 %collective-permute-start.6 = (bf16[384,128]{1,0:T(8,128)(2,1)S(1)}, bf16[384,128]{1,0:T(8,128)(2,1)S(1)}, u32[]{:S(2)}, u32[]{:S(2)}) collective-permute-start(bf16[384,128]{1,0:T(8,128)(2,1)S(1)} %get-tuple-element.28), channel_id=1, source_target_pairs={{0,16},{4,20},{8,24},{12,28},{16,0},{20,4},{24,8},{28,12},{1,17},{... | collective-permute-start | bytes 294920 | tf_op jit(solution)/shard_map/ppermute | solution.py:591
  51.8 10.7 %collective-permute-start.12 = (bf16[4,320,128]{2,1,0:T(8,128)(2,1)S(1)}, bf16[4,320,128]{2,1,0:T(8,128)(2,1)S(1)}, u32[]{:S(2)}, u32[]{:S(2)}) collective-permute-start(bf16[4,320,128]{2,1,0:T(8,128)(2,1)S(1)} %shard_map.144.held_ref), channel_id=1, source_target_pairs={{0,4},{4,0},{8,12},{12,8},{16,20},{20,16},{24,28},{28,24},{1,5},{5... | collective-permute-start | bytes 983048 | tf_op jit(solution)/shard_map/ppermute | solution.py:591
  61.0 15.4 %collective-permute-start.13 = (bf16[4,320,128]{2,1,0:T(8,128)(2,1)S(1)}, bf16[4,320,128]{2,1,0:T(8,128)(2,1)S(1)}, u32[]{:S(2)}, u32[]{:S(2)}) collective-permute-start(bf16[4,320,128]{2,1,0:T(8,128)(2,1)S(1)} %shard_map.144.held_ref), channel_id=1, source_target_pairs={{0,2},{1,3},{2,0},{3,1},{4,6},{5,7},{6,4},{7,5},{8,10},{9,11},{10,... | collective-permute-start | bytes 983048 | tf_op jit(solution)/shard_map/ppermute | solution.py:591
  65.1 4.1 %copy-start.1 = (bf16[8,128,128]{2,1,0:T(8,128)(2,1)S(1)}, bf16[8,128,128]{2,1,0:T(8,128)(2,1)}, u32[]{:S(2)}) copy-start(bf16[8,128,128]{2,1,0:T(8,128)(2,1)} %copy-done) | copy-start | bytes 786436
  65.1 11.8 %collective-permute-start.14 = (bf16[4,320,128]{2,1,0:T(8,128)(2,1)}, bf16[4,320,128]{2,1,0:T(8,128)(2,1)S(1)}, u32[]{:S(2)}, u32[]{:S(2)}) collective-permute-start(bf16[4,320,128]{2,1,0:T(8,128)(2,1)} %shard_map.145.got_ref), channel_id=1, source_target_pairs={{0,2},{1,3},{2,0},{3,1},{4,6},{5,7},{6,4},{7,5},{8,10},{9,11},{10,... | collective-permute-start | bytes 983048 | tf_op jit(solution)/shard_map/ppermute | solution.py:591
  65.6 10.9 %all-to-all-start = ((bf16[8,64,128]{2,1,0:T(8,128)(2,1)}), bf16[8,64,128]{2,1,0:T(8,128)(2,1)S(1)}, u32[]{:S(2)}, u32[]{:S(2)}) async-start(bf16[8,64,128]{2,1,0:T(8,128)(2,1)} %get-tuple-element.35), calls=%async_computation | async-start | bytes 262144 | tf_op jit(solution)/shard_map/all_to_all | solution.py:595
  70.8 18.9 %collective-permute-start.15 = (bf16[256,1280]{1,0:T(8,128)(2,1)S(1)}, bf16[256,1280]{1,0:T(8,128)(2,1)S(1)}, u32[]{:S(2)}, u32[]{:S(2)}) collective-permute-start(bf16[256,1280]{1,0:T(8,128)(2,1)S(1)} %shard_map.146.refs_0_), channel_id=1, source_target_pairs={{0,1},{1,0},{2,3},{3,2},{4,5},{5,4},{6,7},{7,6},{8,9},{9,8},{10,11... | collective-permute-start | bytes 1966088 | tf_op jit(solution)/shard_map/ppermute | solution.py:591
  77.6 12.1 %collective-permute-start.16 = (bf16[256,1280]{1,0:T(8,128)(2,1)S(1)}, bf16[256,1280]{1,0:T(8,128)(2,1)S(1)}, u32[]{:S(2)}, u32[]{:S(2)}) collective-permute-start(bf16[256,1280]{1,0:T(8,128)(2,1)S(1)} %shard_map.147.refs_1_), channel_id=1, source_target_pairs={{0,1},{1,0},{2,3},{3,2},{4,5},{5,4},{6,7},{7,6},{8,9},{9,8},{10,11... | collective-permute-start | bytes 1966088 | tf_op jit(solution)/shard_map/ppermute | solution.py:591
  78.4 11.3 %all-to-all-start.1 = ((bf16[8,64,128]{2,1,0:T(8,128)(2,1)}), bf16[8,64,128]{2,1,0:T(8,128)(2,1)S(1)}, u32[]{:S(2)}, u32[]{:S(2)}) async-start(bf16[8,64,128]{2,1,0:T(8,128)(2,1)} %shard_map.142), calls=%async_computation.1 | async-start | bytes 262144 | tf_op jit(solution)/shard_map/all_to_all | solution.py:595
  95.1 3.7 %collective-permute-start.19 = (bf16[64,256]{1,0:T(8,128)(2,1)S(1)}, bf16[64,256]{1,0:T(8,128)(2,1)S(1)}, u32[]{:S(2)}, u32[]{:S(2)}) collective-permute-start(bf16[64,256]{1,0:T(8,128)(2,1)S(1)} %get-tuple-element.40.refs_0_), channel_id=1, source_target_pairs={{0,3},{1,2},{2,1},{3,0},{4,7},{5,6},{6,5},{7,4},{8,11},{9,10},{10,... | collective-permute-start | bytes 98312 | tf_op jit(solution)/shard_map/ppermute | solution.py:591
  95.2 4.0 %collective-permute-start.18 = (bf16[64,256]{1,0:T(8,128)(2,1)S(1)}, bf16[64,256]{1,0:T(8,128)(2,1)S(1)}, u32[]{:S(2)}, u32[]{:S(2)}) collective-permute-start(bf16[64,256]{1,0:T(8,128)(2,1)S(1)} %get-tuple-element.40.refs_0_), channel_id=1, source_target_pairs={{0,2},{1,3},{2,0},{3,1},{4,6},{5,7},{6,4},{7,5},{8,10},{9,11},{10,... | collective-permute-start | bytes 98312 | tf_op jit(solution)/shard_map/ppermute | solution.py:591
  96.8 2.5 %collective-permute-start.17 = (bf16[64,256]{1,0:T(8,128)(2,1)S(1)}, bf16[64,256]{1,0:T(8,128)(2,1)S(1)}, u32[]{:S(2)}, u32[]{:S(2)}) collective-permute-start(bf16[64,256]{1,0:T(8,128)(2,1)S(1)} %get-tuple-element.40.refs_0_), channel_id=1, source_target_pairs={{0,1},{1,0},{2,3},{3,2},{4,5},{5,4},{6,7},{7,6},{8,9},{9,8},{10,11... | collective-permute-start | bytes 98312 | tf_op jit(solution)/shard_map/ppermute | solution.py:591
  100.0 13.0 %all-to-all-start.2 = ((bf16[8,64,256]{2,1,0:T(8,128)(2,1)}), bf16[8,64,256]{2,1,0:T(8,128)(2,1)S(1)}, u32[]{:S(2)}, u32[]{:S(2)}) async-start(bf16[8,64,256]{2,1,0:T(8,128)(2,1)} %shard_map.150), calls=%async_computation.2 | async-start | bytes 524288 | tf_op jit(solution)/shard_map/all_to_all | solution.py:595
  (3 other events, 2.4 us)

commit v7 on v5

--- a/solution.py
+++ b/solution.py
@@ -16,7 +16,6 @@
 EPS = 1e-05
 BF16 = jnp.bfloat16
 F32 = jnp.float32
-VMEM_LIMIT = 20 * 1024 * 1024
 
 
 def mm(a, b):
@@ -41,8 +40,8 @@
     return pltpu.with_memory_space_constraint(x, pltpu.HBM)
 
 
-def limits():
-    return pltpu.CompilerParams(vmem_limit_bytes=VMEM_LIMIT)
+def limits(mib=4):
+    return pltpu.CompilerParams(vmem_limit_bytes=mib * 1024 * 1024)
 
 
 class Sizes:
@@ -58,30 +57,23 @@
         self.rows = self.part_rows + 2 * tok_rows
         self.share_rows = self.share * self.local
         self.chunks = VW // HD
-        self.riding = self.local % 8 == 0 and self.share_rows % 16 == 0 and seq_count >= 4
+        self.riding = self.local % 8 == 0 and self.share_rows % 16 == 0 and seq_count == 8
         self.ride_rows = self.chunks * self.share_rows if self.riding else 0
 
     def pieces(self):
-        middle = self.count // 2
-        far, near = range(self.count - 1, middle - 1, -1), range(1, middle)
-        every = tuple(range(self.heads))
-        listed = [(mask, (0,)) for mask in far] + [(mask, every) for mask in near]
-        for head in every[1:]:
-            listed += [(mask, (head,)) for mask in far]
-        return listed + [(0, every)]
-
-    def rides(self, piece):
-        return self.riding and piece[0] % 2 == 0 and 0 in piece[1]
-
-    def piece_shape(self, piece):
-        wide = len(piece[1])
-        return (self.rows + (self.ride_rows // wide if self.rides(piece) else 0), wide * HD)
-
-    def ride_slices(self, piece):
-        wide = len(piece[1])
-        deep = self.ride_rows // wide
+        return list(range(1, self.count)) + [0]
+
+    def rides(self, mask):
+        return self.riding and mask in (0, 4)
+
+    def piece_shape(self, mask):
+        return (self.rows + (self.ride_rows // self.heads if self.rides(mask) else 0), self.width)
+
+    def ride_slices(self):
+        deep = self.ride_rows // self.heads
         return [
-            (pl.ds(self.rows, deep), pl.ds(at * HD, HD), pl.ds(at * deep, deep)) for at in range(wide)
+            (pl.ds(self.rows, deep), pl.ds(at * HD, HD), pl.ds(at * deep, deep))
+            for at in range(self.heads)
         ]
 
 
@@ -100,13 +92,11 @@
     ]
     for load in loads:
         load.start()
-    stores = []
     sent = [[], [], [], []]
-    for slot, (piece, out) in enumerate(zip(pieces, out_refs)):
-        mask, some = piece
+    for slot, (mask, out) in enumerate(zip(pieces, out_refs)):
         dest = jnp.bitwise_xor(me, mask)
         group, part = dest // sizes.query_parts, dest % sizes.query_parts
-        cols = pl.ds(pl.multiple_of(group * width + some[0] * HD, HD), len(some) * HD)
+        cols = pl.ds(pl.multiple_of(group * width, HD), width)
         first = pl.ds(pl.multiple_of(part * part_rows, part_rows), part_rows)
         for kind, source, rows in (
             (0, q_scr.at[first, cols], pl.ds(0, part_rows)),
@@ -114,8 +104,8 @@
             (2, v_scr.at[:, cols], pl.ds(part_rows + tok_rows, tok_rows)),
         ):
             sent[kind].append(pltpu.make_async_copy(source, out.at[rows], out_sems.at[kind, slot]))
-        if sizes.rides(piece):
-            for at, (rows, place, from_rows) in enumerate(sizes.ride_slices(piece)):
+        if sizes.rides(mask):
+            for at, (rows, place, from_rows) in enumerate(sizes.ride_slices()):
                 sent[3].append(
                     pltpu.make_async_copy(
                         share_scr.at[from_rows], out.at[rows, place], out_sems.at[3 + at, slot]
@@ -144,7 +134,7 @@
     pieces = sizes.pieces()
     return pl.pallas_call(
         functools.partial(pack_kernel, sizes),
-        out_shape=[jax.ShapeDtypeStruct(sizes.piece_shape(piece), BF16) for piece in pieces],
+        out_shape=[jax.ShapeDtypeStruct(sizes.piece_shape(mask), BF16) for mask in pieces],
         in_specs=[SMEM_SPEC] + [HBM_SPEC] * 4,
         out_specs=[HBM_SPEC] * len(pieces),
         scratch_shapes=[pltpu.VMEM((tok_rows, full), BF16)] * 3
@@ -161,11 +151,11 @@
     )(place, queries, keys, values, patch_embed)
 
 
-def collect_kernel(sizes, pieces, *refs):
-    in_refs, out_ref, sems = refs[: len(pieces)], refs[-2], refs[-1]
+def collect_kernel(sizes, *refs):
+    *in_refs, out_ref, sems = refs
     copies = []
-    for slot, (piece, ref) in enumerate(zip(pieces, in_refs)):
-        for at, (rows, cols, to_rows) in enumerate(sizes.ride_slices(piece)):
+    for slot, ref in enumerate(in_refs):
+        for at, (rows, cols, to_rows) in enumerate(sizes.ride_slices()):
             copies.append(
                 pltpu.make_async_copy(
                     ref.at[rows, cols], out_ref.at[slot, to_rows], sems.at[at, slot]
@@ -177,15 +167,32 @@
         copy.wait()
 
 
-def collect(sizes, pieces, arrays, others):
-    return pl.pallas_call(
-        functools.partial(collect_kernel, sizes, pieces),
-        out_shape=jax.ShapeDtypeStruct((len(pieces), sizes.ride_rows, HD), BF16),
-        in_specs=[ANY_SPEC] * (len(arrays) + len(others)),
+def collect(sizes, arrays):
+    return pl.pallas_call(
+        functools.partial(collect_kernel, sizes),
+        out_shape=jax.ShapeDtypeStruct((len(arrays), sizes.ride_rows, HD), BF16),
+        in_specs=[ANY_SPEC] * len(arrays),
         out_specs=VMEM_SPEC,
-        scratch_shapes=[pltpu.SemaphoreType.DMA((sizes.heads, len(pieces)))],
+        scratch_shapes=[pltpu.SemaphoreType.DMA((sizes.heads, len(arrays)))],
         compiler_params=limits(),
-    )(*arrays, *others)
+    )(*arrays)
+
+
+def join_kernel(first_ref, second_ref, *refs):
+    out_ref = refs[-1]
+    count = first_ref.shape[0]
+    out_ref[:count] = first_ref[...]
+    out_ref[count:] = second_ref[...]
+
+
+def join(first, second, others):
+    return pl.pallas_call(
+        join_kernel,
+        out_shape=jax.ShapeDtypeStruct((2 * first.shape[0],) + first.shape[1:], BF16),
+        in_specs=[VMEM_SPEC] * 2 + [ANY_SPEC] * len(others),
+        out_specs=VMEM_SPEC,
+        compiler_params=limits(),
+    )(first, second, *others)
 
 
 def arrange_kernel(sizes, masks, place_ref, held_ref, got_ref, wait_ref, out_ref):
@@ -213,50 +220,51 @@
     return pl.pallas_call(
         functools.partial(arrange_kernel, sizes, masks),
         out_shape=jax.ShapeDtypeStruct((rows, VW), BF16),
-        in_specs=[SMEM_SPEC, VMEM_SPEC, VMEM_SPEC, ANY_SPEC],
+        in_specs=[SMEM_SPEC, VMEM_SPEC, VMEM_SPEC, VMEM_SPEC],
         out_specs=VMEM_SPEC,
         compiler_params=limits(),
     )(place, held, got, wait)
 
 
-def attend_kernel(sizes, head, pieces, place_ref, *refs):
-    count, width = sizes.count, sizes.width
+def attend_kernel(sizes, masks, place_ref, *refs):
+    count, heads, width = sizes.count, sizes.heads, sizes.width
     tok_rows, part_rows = sizes.tok_rows, sizes.part_rows
     in_refs, refs = refs[:count], refs[count:]
-    scale_ref, shift_ref, proj_ref, *refs = refs
-    before_ref = None
-    if head:
-        before_ref, *refs = refs
-    mod_ref, lat_ref, query_scr, key_scr, value_scr, scale_scr, shift_scr, proj_scr, *refs = refs
-    sems, side_sems = refs
+    scale_ref, shift_ref, proj_ref, mod_ref, lat_ref, token_ref, *refs = refs
+    query_scr, key_scr, value_scr, scale_scr, shift_scr, proj_scr, sems, side_sems = refs
     half = part_rows // 2
-    lat_rows = count * tok_rows
     factor = HD ** (-0.5) * math.log2(math.e)
     me = place_ref[0]
-    mine = pl.ds(pl.multiple_of(place_ref[2] * width + head * HD, HD), HD)
-    copies = []
-    for src, (piece, ref) in enumerate(zip(pieces, in_refs)):
-        cols = pl.ds(piece[1].index(head) * HD, HD)
-        for kind, start, rows, scr in (
-            (0, 0, part_rows, query_scr),
-            (1, part_rows, tok_rows, key_scr),
-            (2, part_rows + tok_rows, tok_rows, value_scr),
-        ):
-            to = scr.at[pl.ds(src * rows, rows)]
-            if kind == 2:
-                to = scr.at[pl.ds(src * rows, rows), pl.ds(0, HD)]
-            copies.append(
-                pltpu.make_async_copy(ref.at[pl.ds(start, rows), cols], to, sems.at[kind, src])
+    mine = pl.ds(pl.multiple_of(place_ref[2] * width, HD), width)
+    logit_copies, value_copies = [], []
+    for src, ref in enumerate(in_refs):
+        rows = pl.ds(src * tok_rows, tok_rows)
+        logit_copies += [
+            pltpu.make_async_copy(ref.at[pl.ds(0, part_rows)], query_scr.at[src], sems.at[0, src]),
+            pltpu.make_async_copy(
+                ref.at[pl.ds(part_rows, tok_rows)], key_scr.at[rows], sems.at[1, src]
+            ),
+        ]
+        for head in range(heads):
+            value_copies.append(
+                pltpu.make_async_copy(
+                    ref.at[pl.ds(part_rows + tok_rows, tok_rows), pl.ds(head * HD, HD)],
+                    value_scr.at[rows, pl.ds(2 * head * HD, HD)],
+                    sems.at[2 + head, src],
+                )
             )
-    copies += [
+    value_copies += [
         pltpu.make_async_copy(scale_ref.at[:, mine], scale_scr, side_sems.at[0]),
         pltpu.make_async_copy(shift_ref.at[:, mine], shift_scr, side_sems.at[1]),
         pltpu.make_async_copy(proj_ref.at[:, mine], proj_scr, side_sems.at[2]),
     ]
-    for copy in copies:
+    for copy in logit_copies + value_copies:
         copy.start()
-    value_scr[:, pl.ds(HD, HD)] = jnp.ones((lat_rows, HD), BF16)
-    for copy in copies:
+    token_ref[...] = jnp.zeros_like(token_ref)
+    ones = jnp.ones((count * tok_rows, HD), BF16)
+    for head in range(heads):
+        value_scr[:, pl.ds((2 * head + 1) * HD, HD)] = ones
+    for copy in logit_copies + value_copies:
         copy.wait()
     gain = 1.0 + scale_scr[...]
     shift = shift_scr[...]
@@ -265,55 +273,58 @@
     proj_pair = jnp.concatenate(
         [jnp.concatenate([proj, zero], axis=1), jnp.concatenate([zero, proj], axis=1)], axis=0
     )
-    block = min(count * part_rows, max(part_rows, min(256, (1 << 18) // lat_rows)))
-    for first in range(0, count * part_rows, block):
-        logits = mm_nt(query_scr[pl.ds(first, block), :], key_scr[...])
-        top = jnp.max(logits, axis=-1, keepdims=True)
-        weights = jnp.exp2((logits - top) * factor).astype(BF16)
-        both = mm(weights, value_scr[...])
-        modulated = (both[:, :HD] / both[:, HD:] * gain + shift).astype(BF16)
-        for at in range(0, block, part_rows):
-            place = jnp.bitwise_xor(me, pieces[(first + at) // part_rows][0])
-            mod_ref[place] = modulated[at : at + part_rows]
-            pair = jnp.concatenate(
-                [modulated[at : at + half], modulated[at + half : at + part_rows]], axis=1
-            )
-            latent = mm_nt(pair, proj_pair)
-            if head:
-                latent = latent + before_ref[place]
-            lat_ref[place] = latent.astype(lat_ref.dtype)
-
-
-def attend(sizes, head, place, pieces, received, scales, shifts, proj, before):
-    count = sizes.count
+    together = 2
+    for first in range(0, count, together):
+        results = []
+        for src in range(first, first + together):
+            mixed = []
+            for head in range(heads):
+                cols = pl.ds(head * HD, HD)
+                logits = mm_nt(query_scr[src, :, cols], key_scr[:, cols])
+                top = jnp.max(logits, axis=-1, keepdims=True)
+                weights = jnp.exp2((logits - top) * factor).astype(BF16)
+                both = mm(weights, value_scr[:, pl.ds(2 * head * HD, 2 * HD)])
+                mixed.append(both[:, :HD] / both[:, HD:])
+            attended = jnp.concatenate(mixed, axis=1) if heads > 1 else mixed[0]
+            modulated = (attended * gain + shift).astype(BF16)
+            pair = jnp.concatenate([modulated[:half], modulated[half:]], axis=1)
+            results.append((modulated, mm_nt(pair, proj_pair).astype(BF16)))
+        for at, (modulated, latent) in enumerate(results):
+            place = jnp.bitwise_xor(me, masks[first + at])
+            mod_ref[place] = modulated
+            lat_ref[place] = latent
+
+
+def attend(sizes, masks, place, received, scales, shifts, proj):
+    count, width, heads = sizes.count, sizes.width, sizes.heads
     lat_rows = count * sizes.tok_rows
     query_rows = count * sizes.part_rows
-    last = head == sizes.heads - 1
-    return pl.pallas_call(
-        functools.partial(attend_kernel, sizes, head, pieces),
+    return pl.pallas_call(
+        functools.partial(attend_kernel, sizes, masks),
         out_shape=(
-            jax.ShapeDtypeStruct((count, sizes.part_rows, HD), BF16),
-            jax.ShapeDtypeStruct((count, sizes.part_rows // 2, 2 * CH), BF16 if last else F32),
+            jax.ShapeDtypeStruct((count, sizes.part_rows, width), BF16),
+            jax.ShapeDtypeStruct((count, sizes.part_rows // 2, 2 * CH), BF16),
+            jax.ShapeDtypeStruct((8, 128), F32),
         ),
-        in_specs=[SMEM_SPEC] + [ANY_SPEC] * count + [HBM_SPEC] * 3 + [VMEM_SPEC] * len(before),
-        out_specs=(VMEM_SPEC, VMEM_SPEC),
+        in_specs=[SMEM_SPEC] + [ANY_SPEC] * count + [HBM_SPEC] * 3,
+        out_specs=(VMEM_SPEC, VMEM_SPEC, VMEM_SPEC),
         scratch_shapes=[
-            pltpu.VMEM((query_rows, HD), BF16),
-            pltpu.VMEM((lat_rows, HD), BF16),
-            pltpu.VMEM((lat_rows, 2 * HD), BF16),
-            pltpu.VMEM((1, HD), F32),
-            pltpu.VMEM((1, HD), F32),
-            pltpu.VMEM((CH, HD), BF16),
-            pltpu.SemaphoreType.DMA((3, count)),
+            pltpu.VMEM((count, sizes.part_rows, width), BF16),
+            pltpu.VMEM((lat_rows, width), BF16),
+            pltpu.VMEM((lat_rows, 2 * width), BF16),
+            pltpu.VMEM((1, width), F32),
+            pltpu.VMEM((1, width), F32),
+            pltpu.VMEM((CH, width), BF16),
+            pltpu.SemaphoreType.DMA((2 + heads, count)),
             pltpu.SemaphoreType.DMA((3,)),
         ],
-        compiler_params=limits(),
+        compiler_params=limits(16),
         cost_estimate=pl.CostEstimate(
-            flops=4 * query_rows * lat_rows * HD,
-            bytes_accessed=2 * (query_rows * 2 + lat_rows * 2) * HD,
-            transcendentals=query_rows * lat_rows,
+            flops=4 * query_rows * lat_rows * width,
+            bytes_accessed=2 * (query_rows * 2 + lat_rows * 2) * width,
+            transcendentals=query_rows * lat_rows * heads,
         ),
-    )(place, *received, scales, shifts, proj, *before)
+    )(place, *received, scales, shifts, proj)
 
 
 def total_kernel(copies, *refs):
@@ -342,11 +353,11 @@
     return jnp.sum(x, axis=-1, keepdims=True) * (1.0 / count)
 
 
-def head_kernel(grid_rows, heads, fused, embed_masks, out_factor, place_ref, lat_ref, *refs):
+def head_kernel(grid_rows, fused, embed_masks, out_factor, place_ref, lat_ref, *refs):
     embed_refs, refs = refs[: len(embed_masks)], refs[len(embed_masks) :]
     sides, refs = refs[:4], refs[4:]
     cot_ref, refs = refs[0], refs[1:]
-    mod_refs, refs = refs[:heads], refs[heads:]
+    mod_ref, refs = refs[0], refs[1:]
     reward_ref, grad_ref, weight_ref, lat_scr, grad_scr, embed_ref, *refs = refs
     pos_ref, pre_ref, post_ref, prompt_ref, sems, side_sems = refs
     patch_rows = grid_rows // 4
@@ -431,19 +442,19 @@
     grad = grad_scr[...].astype(BF16)
     grad_ref[...] = grad
     if fused:
-        store_readout_grad(grad, mod_refs, out_factor, weight_ref)
+        store_readout_grad(grad, mod_ref, out_factor, weight_ref)
     else:
         weight_ref[...] = jnp.zeros_like(weight_ref)
 
 
-def store_readout_grad(grad, mod_refs, out_factor, out_ref):
-    for head, mod_ref in enumerate(mod_refs):
-        count, rows, width = mod_ref.shape
-        half = rows // 2
-        first = mod_ref[:, :half, :].reshape(count * half, width)
-        second = mod_ref[:, half:, :].reshape(count * half, width)
-        total = mm_tn(grad, first)[:CH] + mm_tn(grad, second)[CH:]
-        out_ref[:, pl.ds(head * width, width)] = (total * out_factor).astype(BF16)
+def store_readout_grad(grad, mod_ref, out_factor, out_ref):
+    turned = grad.astype(F32).T.astype(BF16)
+    count, rows, width = mod_ref.shape
+    half = rows // 2
+    first = mod_ref[:, :half, :].reshape(count * half, width)
+    second = mod_ref[:, half:, :].reshape(count * half, width)
+    total = mm(turned[:CH], first) + mm(turned[CH:], second)
+    out_ref[...] = (total * out_factor).astype(BF16)
 
 
 def reward_head(
@@ -451,12 +462,10 @@
 ):
     patches = grid_rows * GW // 16
     rows = grid_rows * GW // 2
-    width = HD * len(modulated)
+    width = modulated.shape[2]
     embed_arrays, embed_masks = [x for x, _ in embed], [mask for _, mask in embed]
     return pl.pallas_call(
-        functools.partial(
-            head_kernel, grid_rows, len(modulated), fused, embed_masks, out_factor
-        ),
+        functools.partial(head_kernel, grid_rows, fused, embed_masks, out_factor),
         out_shape=(
             jax.ShapeDtypeStruct((1, 128), F32),
             jax.ShapeDtypeStruct((rows, 2 * CH), BF16),
@@ -465,8 +474,7 @@
         in_specs=[SMEM_SPEC, VMEM_SPEC]
         + [ANY_SPEC] * len(embed_arrays)
         + [HBM_SPEC] * 4
-        + [SMEM_SPEC]
-        + [VMEM_SPEC] * len(modulated),
+        + [SMEM_SPEC, VMEM_SPEC],
         out_specs=(VMEM_SPEC, VMEM_SPEC, VMEM_SPEC),
         scratch_shapes=[
             pltpu.VMEM((rows, 2 * CH), F32),
@@ -479,13 +487,13 @@
             pltpu.SemaphoreType.DMA((len(embed_arrays),)),
             pltpu.SemaphoreType.DMA((4,)),
         ],
-        compiler_params=limits(),
+        compiler_params=limits(16),
         cost_estimate=pl.CostEstimate(
             flops=6 * patches * 16 * CH * VW,
             bytes_accessed=2 * 16 * CH * VW + 2 * patches * VW,
             transcendentals=0,
         ),
-    )(place, latent, *embed_arrays, pos, pre, post, prompt, cot, *modulated)
+    )(place, latent, *embed_arrays, pos, pre, post, prompt, cot, modulated)
 
 
 def spread_kernel(
@@ -536,17 +544,17 @@
 
 
 def weight_kernel(out_factor, grad_ref, *refs):
-    store_readout_grad(grad_ref[...], refs[:-1], out_factor, refs[-1])
+    store_readout_grad(grad_ref[...], refs[0], out_factor, refs[1])
 
 
 def weight_call(grad, modulated, out_factor):
     return pl.pallas_call(
         functools.partial(weight_kernel, out_factor),
-        out_shape=jax.ShapeDtypeStruct((CH, HD * len(modulated)), BF16),
-        in_specs=[VMEM_SPEC] * (1 + len(modulated)),
+        out_shape=jax.ShapeDtypeStruct((CH, modulated.shape[2]), BF16),
+        in_specs=[VMEM_SPEC] * 2,
         out_specs=VMEM_SPEC,
         compiler_params=limits(),
-    )(grad, *modulated)
+    )(grad, modulated)
 
 
 def finish_kernel(in_ref, out_ref):
@@ -577,16 +585,15 @@
 
 
 def after_kernel(*refs):
-    del refs
+    refs[-1][...] = refs[0][...]
 
 
 def after(x, others):
     return pl.pallas_call(
         after_kernel,
         out_shape=jax.ShapeDtypeStruct(x.shape, x.dtype),
-        in_specs=[ANY_SPEC] * (1 + len(others)),
-        out_specs=ANY_SPEC,
-        input_output_aliases={0: 0},
+        in_specs=[VMEM_SPEC] * (1 + len(others)),
+        out_specs=VMEM_SPEC,
     )(x, *others)
 
 
@@ -621,37 +628,29 @@
     proj_turned = proj_out.T
     out_factor = 1.0 / math.sqrt(data_count * lat_rows)
 
-    pieces = sizes.pieces()
+    masks = sizes.pieces()
     packed = pack(
         sizes, place, in_hbm(queries), in_hbm(keys), in_hbm(values), in_hbm(patch_embed)
     )
-    received = [swap(x, "seq", piece[0]) if piece[0] else x for piece, x in zip(pieces, packed)]
+    received = [swap(x, "seq", mask) if mask else x for mask, x in zip(masks, packed)]
     bits = [1 << b for b in reversed(range(data_count.bit_length() - 1))]
     shared = sizes.share < patch_embed.shape[0]
-
-    modulated, latent_part = [], []
-    for head in range(head_count):
-        slots = [slot for slot, piece in enumerate(pieces) if head in piece[1]]
-        if head == head_count - 1 and sizes.riding:
-            even = [slot for slot, piece in enumerate(pieces) if sizes.rides(piece)]
-            rest = [x for slot, x in enumerate(received) if slot not in even]
-            held = collect(
-                sizes, [pieces[slot] for slot in even], [received[slot] for slot in even],
-                rest + modulated,
-            )
-            got = swap(held, "seq", 1)
-            far_held = swap(held, "dp", bits[0]) if shared else None
-        mod, latent_sum = attend(
-            sizes, head, place, [pieces[slot] for slot in slots], [received[slot] for slot in slots],
-            in_hbm(scales), in_hbm(shifts), in_hbm(proj_turned), latent_part,
-        )
-        modulated, latent_part = modulated + [mod], [latent_sum]
-    latent_part = latent_part[0]
-
     if sizes.riding:
-        got = after(got, [modulated[-1]])
-        even_masks = [pieces[slot][0] for slot in even]
-        embed = [(arrange(sizes, even_masks, place, held, got, modulated[-1]), 0)]
+        ride = [slot for slot, mask in enumerate(masks) if sizes.rides(mask)]
+        two = collect(sizes, [received[slot] for slot in ride])
+        held = join(two, swap(two, "seq", 2), received)
+        ride_masks = [masks[slot] for slot in ride]
+        ride_masks = ride_masks + [mask ^ 2 for mask in ride_masks]
+        got = swap(held, "seq", 1)
+        far_held = swap(held, "dp", bits[0]) if shared else None
+
+    modulated, latent_part, token = attend(
+        sizes, masks, place, received, in_hbm(scales), in_hbm(shifts), in_hbm(proj_turned)
+    )
+
+    if sizes.riding:
+        got = after(got, [token])
+        embed = [(arrange(sizes, ride_masks, place, held, got, token), 0)]
         far_got = swap(got, "dp", bits[0]) if shared else None
     else:
         mine = patch_embed
@@ -670,7 +669,7 @@
     per_share = seq_count // group_count
     parts = all_to_all(latent_part.reshape(group_count, per_share * half, 2 * CH), groups)
     if sizes.riding and shared:
-        embed.append((arrange(sizes, even_masks, place, far_held, far_got, parts), bits[0]))
+        embed.append((arrange(sizes, ride_masks, place, far_held, far_got, parts), bits[0]))
     for bit in bits[1:] if shared else []:
         embed = embed + [(swap(x, "dp", bit), m ^ bit) for x, m in embed]
     latent = all_to_all(total_copies([parts], seq_count))

time: 111 us -> 112 us (level)
  waiting for transfers between devices: 40.6 us -> 44.5 us
  starting transfers between devices: 39.9 us -> 37.9 us
    ppermute x19 -> x16, starting transfers between devices: 29.8 us -> 18.8 us  [swap(): return lax.ppermute(x, axis, [(i, i ^ mask) for i in range(count)])]
    all_to_all x3, starting transfers between devices: 10.2 us -> 19.1 us  [all_to_all(): lax.all_to_all(x, 'seq', split_axis=0, concat_axis=0, tiled=True, axis_in...]
    ppermute x19 -> x16, waiting for transfers between devices: 20.9 us -> 24.9 us  [swap(): return lax.ppermute(x, axis, [(i, i ^ mask) for i in range(count)])]
    pallas_call x4, Pallas kernels: 16.7 us -> 14.9 us  [the longest x1 9.79 us: attend(): pl.pallas_call(functools.partial(attend_kernel, sizes, masks), out_shape=...]
    pallas_call x1, Pallas kernels: 0.01 us -> 1.72 us  [after(): pl.pallas_call(after_kernel, out_shape=jax.ShapeDtypeStruct(x.shape, x.dt...]
  transfers between devices with their start and end apart: 22 -> 19, of which waited for: 8 -> 11; matrix products, arithmetic and copies ran while one was open for 0% -> 0% of each run, Pallas kernels for 14% -> 14%
where the time goes in v7:
time: 112 us; the launch traced here: 111 us
  waiting for transfers between devices  44.5 us (40%)
  starting transfers between devices  37.9 us (34%)
  Pallas kernels  25.2 us (22%)
  local copies, waits for them, and re-layouts  2.28 us (2%)
  between operations  1.4 us (1%)
    ppermute x16, waiting for transfers between devices, swap(): return lax.ppermute(x, axis, [(i, i ^ mask) for i in range(count)])  24.9 us
    all_to_all x3, waiting for transfers between devices, all_to_all(): lax.all_to_all(x, 'seq', split_axis=0, concat_axis=0, tiled=True, axis_in...  19.6 us
    all_to_all x3, starting transfers between devices, all_to_all(): lax.all_to_all(x, 'seq', split_axis=0, concat_axis=0, tiled=True, axis_in...  19.1 us
    ppermute x16, starting transfers between devices, swap(): return lax.ppermute(x, axis, [(i, i ^ mask) for i in range(count)])  18.8 us
    pallas_call x1, Pallas kernels, attend(): pl.pallas_call(functools.partial(attend_kernel, sizes, masks), out_shape=...  9.79 us
    pallas_call x1, Pallas kernels, reward_head(): pl.pallas_call(functools.partial(head_kernel, grid_rows, fused, embed_mas...  5.06 us
    pallas_call x1, Pallas kernels, pack(): pl.pallas_call(functools.partial(pack_kernel, sizes), out_shape=[jax.Shap...  2.47 us
    pallas_call x1, Pallas kernels, spread(): pl.pallas_call(functools.partial(spread_kernel, count, half, heads), out_...  2.41 us
  transfers between devices with their start and end apart: 19, of which 11 were waited for; matrix products, arithmetic and copies ran while one was open for 0% of the time, Pallas kernels for 14%

profile of v7, /device:TPU:0, one launch (start us, length us, event | category | flops | bytes accessed | tf_op | source)
XLA Modules:
  0.0 111.4 jit_solution(15064570899285128673)
XLA Ops:
  0.7 2.5 %shard_map.139 = (bf16[384,256]{1,0:T(8,128)(2,1)S(1)}, bf16[384,256]{1,0:T(8,128)(2,1)S(1)}, bf16[384,256]{1,0:T(8,128)(2,1)S(1)}, bf16[544,256]{1,0:T(8,128)(2...) custom-call(s32[3]{0:T(128)S(1)} %pad_add_fusion.place_ref, ...), custom_call_target="tpu_custom_call" | custom-call | bytes 3145728 | tf_op jit(solution)/shard_map/pallas_call | solution.py:135
  3.2 4.1 %collective-permute-start.3 = (bf16[544,256]{1,0:T(8,128)(2,1)S(1)}, bf16[544,256]{1,0:T(8,128)(2,1)S(1)}, u32[]{:S(2)}, u32[]{:S(2)}) collective-permute-start(bf16[544,256]{1,0:T(8,128)(2,1)S(1)} %get-tuple-element.20), channel_id=1, source_target_pairs={{0,16},{4,20},{8,24},{12,28},{16,0},{20,4},{24,8},{28,12},{1,17},{... | collective-permute-start | bytes 835592 | tf_op jit(solution)/shard_map/ppermute | solution.py:578
  7.3 1.5 %collective-permute-start = (bf16[384,256]{1,0:T(8,128)(2,1)S(1)}, bf16[384,256]{1,0:T(8,128)(2,1)S(1)}, u32[]{:S(2)}, u32[]{:S(2)}) collective-permute-start(bf16[384,256]{1,0:T(8,128)(2,1)S(1)} %get-tuple-element.17), channel_id=1, source_target_pairs={{0,4},{4,0},{8,12},{12,8},{16,20},{20,16},{24,28},{28,24},{1,5},{5... | collective-permute-start | bytes 589832 | tf_op jit(solution)/shard_map/ppermute | solution.py:578
  8.8 1.6 %collective-permute-start.1 = (bf16[384,256]{1,0:T(8,128)(2,1)S(1)}, bf16[384,256]{1,0:T(8,128)(2,1)S(1)}, u32[]{:S(2)}, u32[]{:S(2)}) collective-permute-start(bf16[384,256]{1,0:T(8,128)(2,1)S(1)} %get-tuple-element.18), channel_id=1, source_target_pairs={{0,8},{4,12},{8,0},{12,4},{16,24},{20,28},{24,16},{28,20},{1,9},{5... | collective-permute-start | bytes 589832 | tf_op jit(solution)/shard_map/ppermute | solution.py:578
  10.8 1.3 %collective-permute-start.4 = (bf16[384,256]{1,0:T(8,128)(2,1)S(1)}, bf16[384,256]{1,0:T(8,128)(2,1)S(1)}, u32[]{:S(2)}, u32[]{:S(2)}) collective-permute-start(bf16[384,256]{1,0:T(8,128)(2,1)S(1)} %get-tuple-element.21), channel_id=1, source_target_pairs={{0,20},{4,16},{8,28},{12,24},{16,4},{20,0},{24,12},{28,8},{1,21},{... | collective-permute-start | bytes 589832 | tf_op jit(solution)/shard_map/ppermute | solution.py:578
  12.1 2.2 %collective-permute-done.refs_0_ = bf16[384,256]{1,0:T(8,128)(2,1)S(1)} collective-permute-done((bf16[384,256]{1,0:T(8,128)(2,1)S(1)}, bf16[384,256]{1,0:T(8,128)(2,1)S(1)}, u32[]{:S(2)}, u32[]{:S(2)}) %collective-permute-start) | collective-permute-done | bytes 196640 | tf_op jit(solution)/shard_map/ppermute | solution.py:578
  14.2 1.4 %collective-permute-start.5 = (bf16[384,256]{1,0:T(8,128)(2,1)S(1)}, bf16[384,256]{1,0:T(8,128)(2,1)S(1)}, u32[]{:S(2)}, u32[]{:S(2)}) collective-permute-start(bf16[384,256]{1,0:T(8,128)(2,1)S(1)} %get-tuple-element.22), channel_id=1, source_target_pairs={{0,24},{4,28},{8,16},{12,20},{16,8},{20,12},{24,0},{28,4},{1,25},{... | collective-permute-start | bytes 589832 | tf_op jit(solution)/shard_map/ppermute | solution.py:578
  15.7 5.2 %collective-permute-done.3.refs_3_.refs_0_ = bf16[544,256]{1,0:T(8,128)(2,1)S(1)} collective-permute-done((bf16[544,256]{1,0:T(8,128)(2,1)S(1)}, bf16[544,256]{1,0:T(8,128)(2,1)S(1)}, u32[]{:S(2)}, u32[]{:S(2)}) %collective-permute-start.3) | collective-permute-done | bytes 278560 | tf_op jit(solution)/shard_map/ppermute | solution.py:578
  20.8 3.8 %collective-permute-start.6 = (bf16[384,256]{1,0:T(8,128)(2,1)S(1)}, bf16[384,256]{1,0:T(8,128)(2,1)S(1)}, u32[]{:S(2)}, u32[]{:S(2)}) collective-permute-start(bf16[384,256]{1,0:T(8,128)(2,1)S(1)} %get-tuple-element.23), channel_id=1, source_target_pairs={{0,28},{4,24},{8,20},{12,16},{16,12},{20,8},{24,4},{28,0},{1,29},{... | collective-permute-start | bytes 589832 | tf_op jit(solution)/shard_map/ppermute | solution.py:578
  25.0 2.5 %collective-permute-done.2.refs_2_ = bf16[384,256]{1,0:T(8,128)(2,1)S(1)} collective-permute-done((bf16[384,256]{1,0:T(8,128)(2,1)S(1)}, bf16[384,256]{1,0:T(8,128)(2,1)S(1)}, u32[]{:S(2)}, u32[]{:S(2)}) %collective-permute-start.2) | collective-permute-done | bytes 196640 | tf_op jit(solution)/shard_map/ppermute | solution.py:578
  27.5 11.5 %collective-permute-done.4.refs_4_ = bf16[384,256]{1,0:T(8,128)(2,1)S(1)} collective-permute-done((bf16[384,256]{1,0:T(8,128)(2,1)S(1)}, bf16[384,256]{1,0:T(8,128)(2,1)S(1)}, u32[]{:S(2)}, u32[]{:S(2)}) %collective-permute-start.4) | collective-permute-done | bytes 196640 | tf_op jit(solution)/shard_map/ppermute | solution.py:578
  40.7 9.8 %shard_map.140 = (bf16[8,128,256]{2,1,0:T(8,128)(2,1)S(1)}, bf16[8,64,128]{2,1,0:T(8,128)(2,1)}, f32[8,128]{1,0:T(8,128)S(1)}) custom-call(s32[3]{0:T(128)S(1)} %pad_add_fusion.place_ref, bf16[384,256]{1,0:T(8,128)(2,1)S(1)} %collective-permute-done.refs_0_, bf16[384,256]{1,0:T(8,128)(2,1)S(1)} %collective-permute-done.1.refs_1_, ...), custom_call_target="tpu_custom_call" | custom-call | flops 1073741824 | bytes 2097152 | tf_op jit(solution)/shard_map/pallas_call | solution.py:302
  51.1 1.5 %collective-permute-start.9 = (bf16[4,320,128]{2,1,0:T(8,128)(2,1)S(1)}, bf16[4,320,128]{2,1,0:T(8,128)(2,1)S(1)}, u32[]{:S(2)}, u32[]{:S(2)}) collective-permute-start(bf16[4,320,128]{2,1,0:T(8,128)(2,1)S(1)} %shard_map.143.held_ref), channel_id=1, source_target_pairs={{0,2},{1,3},{2,0},{3,1},{4,6},{5,7},{6,4},{7,5},{8,10},{9,11},{10,... | collective-permute-start | bytes 983048 | tf_op jit(solution)/shard_map/ppermute | solution.py:578
  53.3 1.7 %shard_map.144.got_ref = bf16[4,320,128]{2,1,0:T(8,128)(2,1)} custom-call(bf16[4,320,128]{2,1,0:T(8,128)(2,1)} %copy-done.3, f32[8,128]{1,0:T(8,128)} %copy-done.1), custom_call_target="tpu_custom_call" | custom-call | tf_op jit(solution)/shard_map/pallas_call | solution.py:592
  55.6 11.1 %all-to-all-start = ((bf16[8,64,128]{2,1,0:T(8,128)(2,1)}), bf16[8,64,128]{2,1,0:T(8,128)(2,1)S(1)}, u32[]{:S(2)}, u32[]{:S(2)}) async-start(bf16[8,64,128]{2,1,0:T(8,128)(2,1)} %get-tuple-element.25), calls=%async_computation | async-start | bytes 262144 | tf_op jit(solution)/shard_map/all_to_all | solution.py:582
  68.5 5.6 %all-to-all-done.refs_0_.wait_ref = bf16[8,64,128]{2,1,0:T(8,128)(2,1)S(1)} async-done(((bf16[8,64,128]{2,1,0:T(8,128)(2,1)}), bf16[8,64,128]{2,1,0:T(8,128)(2,1)S(1)}, u32[]{:S(2)}, u32[]{:S(2)}) %all-to-all-start) | async-done | bytes 131104 | tf_op jit(solution)/shard_map/all_to_all | solution.py:582
  75.5 4.4 %all-to-all-start.1 = ((bf16[8,64,128]{2,1,0:T(8,128)(2,1)}), bf16[8,64,128]{2,1,0:T(8,128)(2,1)S(1)}, u32[]{:S(2)}, u32[]{:S(2)}) async-start(bf16[8,64,128]{2,1,0:T(8,128)(2,1)} %shard_map.141), calls=%async_computation.1 | async-start | bytes 262144 | tf_op jit(solution)/shard_map/all_to_all | solution.py:582
  80.6 7.0 %all-to-all-done.1 = bf16[8,64,128]{2,1,0:T(8,128)(2,1)S(1)} async-done(((bf16[8,64,128]{2,1,0:T(8,128)(2,1)}), bf16[8,64,128]{2,1,0:T(8,128)(2,1)S(1)}, u32[]{:S(2)}, u32[]{:S(2)}) %all-to-all-start.1) | async-done | bytes 131104 | tf_op jit(solution)/shard_map/all_to_all | solution.py:582
  87.6 5.1 %shard_map.147 = (f32[1,128]{1,0:T(1,128)}, bf16[512,128]{1,0:T(8,128)(2,1)S(1)}, bf16[64,256]{1,0:T(8,128)(2,1)S(1)}) custom-call(s32[3]{0:T(128)S(1)} %pad_add_fusion.place_ref, bf16[512,128]{1,0:T(8,128)(2,1)S(1)} %bitcast.7, bf16[256,1280]{1,0:T(8,128)(2,1)S(1)} %shard_map.145.refs_0_, bf16[256,1280]{1,0:T(8,128)(2,1)S(1)} %shard_map.146.refs_1_, ...), custom_call_target="tpu_custom_call" | custom-call | flops 503316480 | bytes 2785280 | tf_op jit(solution)/shard_map/pallas_call | solution.py:467
  92.7 1.5 %collective-permute-start.14 = (bf16[64,256]{1,0:T(8,128)(2,1)S(1)}, bf16[64,256]{1,0:T(8,128)(2,1)S(1)}, u32[]{:S(2)}, u32[]{:S(2)}) collective-permute-start(bf16[64,256]{1,0:T(8,128)(2,1)S(1)} %get-tuple-element.30.refs_0_), channel_id=1, source_target_pairs={{0,2},{1,3},{2,0},{3,1},{4,6},{5,7},{6,4},{7,5},{8,10},{9,11},{10,... | collective-permute-start | bytes 98312 | tf_op jit(solution)/shard_map/ppermute | solution.py:578
  94.6 1.8 %collective-permute-done.15.refs_3_ = bf16[64,256]{1,0:T(8,128)(2,1)S(1)} collective-permute-done((bf16[64,256]{1,0:T(8,128)(2,1)S(1)}, bf16[64,256]{1,0:T(8,128)(2,1)S(1)}, u32[]{:S(2)}, u32[]{:S(2)}) %collective-permute-start.15) | collective-permute-done | bytes 32800 | tf_op jit(solution)/shard_map/ppermute | solution.py:578
  97.5 3.6 %all-to-all-start.2 = ((bf16[8,64,256]{2,1,0:T(8,128)(2,1)}), bf16[8,64,256]{2,1,0:T(8,128)(2,1)S(1)}, u32[]{:S(2)}, u32[]{:S(2)}) async-start(bf16[8,64,256]{2,1,0:T(8,128)(2,1)} %shard_map.149), calls=%async_computation.2 | async-start | bytes 524288 | tf_op jit(solution)/shard_map/all_to_all | solution.py:582
  101.1 2.4 %shard_map.148 = bf16[1,2,1024,128]{3,2,1,0:T(8,128)(2,1)} custom-call(s32[3]{0:T(128)S(1)} %pad_add_fusion.place_ref, bf16[512,128]{1,0:T(8,128)(2,1)S(1)} %get-tuple-element.29.grad_ref, f32[1,2048]{1,0:T(1,128)} %scale_ref.1, bf16[64,2048]{1,0:T(8,128)(2,1)} %bitcast.10), custom_call_target="tpu_custom_call" | custom-call | flops 67108864 | bytes 524288 | tf_op jit(solution)/shard_map/pallas_call | solution.py:527
  103.5 7.1 %all-to-all-done.2.in_ref = bf16[8,64,256]{2,1,0:T(8,128)(2,1)S(1)} async-done(((bf16[8,64,256]{2,1,0:T(8,128)(2,1)}), bf16[8,64,256]{2,1,0:T(8,128)(2,1)S(1)}, u32[]{:S(2)}, u32[]{:S(2)}) %all-to-all-start.2) | async-done | bytes 262176 | tf_op jit(solution)/shard_map/all_to_all | solution.py:582
  (35 shorter events, 9.9 us)
Async XLA Ops:
  3.2 17.7 %collective-permute-start.3 = (bf16[544,256]{1,0:T(8,128)(2,1)S(1)}, bf16[544,256]{1,0:T(8,128)(2,1)S(1)}, u32[]{:S(2)}, u32[]{:S(2)}) collective-permute-start(bf16[544,256]{1,0:T(8,128)(2,1)S(1)} %get-tuple-element.20), channel_id=1, source_target_pairs={{0,16},{4,20},{8,24},{12,28},{16,0},{20,4},{24,8},{28,12},{1,17},{... | collective-permute-start | bytes 835592 | tf_op jit(solution)/shard_map/ppermute | solution.py:578
  7.3 6.9 %collective-permute-start = (bf16[384,256]{1,0:T(8,128)(2,1)S(1)}, bf16[384,256]{1,0:T(8,128)(2,1)S(1)}, u32[]{:S(2)}, u32[]{:S(2)}) collective-permute-start(bf16[384,256]{1,0:T(8,128)(2,1)S(1)} %get-tuple-element.17), channel_id=1, source_target_pairs={{0,4},{4,0},{8,12},{12,8},{16,20},{20,16},{24,28},{28,24},{1,5},{5... | collective-permute-start | bytes 589832 | tf_op jit(solution)/shard_map/ppermute | solution.py:578
  8.8 16.1 %collective-permute-start.1 = (bf16[384,256]{1,0:T(8,128)(2,1)S(1)}, bf16[384,256]{1,0:T(8,128)(2,1)S(1)}, u32[]{:S(2)}, u32[]{:S(2)}) collective-permute-start(bf16[384,256]{1,0:T(8,128)(2,1)S(1)} %get-tuple-element.18), channel_id=1, source_target_pairs={{0,8},{4,12},{8,0},{12,4},{16,24},{20,28},{24,16},{28,20},{1,9},{5... | collective-permute-start | bytes 589832 | tf_op jit(solution)/shard_map/ppermute | solution.py:578
  10.4 17.1 %collective-permute-start.2 = (bf16[384,256]{1,0:T(8,128)(2,1)S(1)}, bf16[384,256]{1,0:T(8,128)(2,1)S(1)}, u32[]{:S(2)}, u32[]{:S(2)}) collective-permute-start(bf16[384,256]{1,0:T(8,128)(2,1)S(1)} %get-tuple-element.19), channel_id=1, source_target_pairs={{0,12},{4,8},{8,4},{12,0},{16,28},{20,24},{24,20},{28,16},{1,13},{... | collective-permute-start | bytes 589832 | tf_op jit(solution)/shard_map/ppermute | solution.py:578
  10.8 28.2 %collective-permute-start.4 = (bf16[384,256]{1,0:T(8,128)(2,1)S(1)}, bf16[384,256]{1,0:T(8,128)(2,1)S(1)}, u32[]{:S(2)}, u32[]{:S(2)}) collective-permute-start(bf16[384,256]{1,0:T(8,128)(2,1)S(1)} %get-tuple-element.21), channel_id=1, source_target_pairs={{0,20},{4,16},{8,28},{12,24},{16,4},{20,0},{24,12},{28,8},{1,21},{... | collective-permute-start | bytes 589832 | tf_op jit(solution)/shard_map/ppermute | solution.py:578
  14.2 24.8 %collective-permute-start.5 = (bf16[384,256]{1,0:T(8,128)(2,1)S(1)}, bf16[384,256]{1,0:T(8,128)(2,1)S(1)}, u32[]{:S(2)}, u32[]{:S(2)}) collective-permute-start(bf16[384,256]{1,0:T(8,128)(2,1)S(1)} %get-tuple-element.22), channel_id=1, source_target_pairs={{0,24},{4,28},{8,16},{12,20},{16,8},{20,12},{24,0},{28,4},{1,25},{... | collective-permute-start | bytes 589832 | tf_op jit(solution)/shard_map/ppermute | solution.py:578
  20.8 18.1 %collective-permute-start.6 = (bf16[384,256]{1,0:T(8,128)(2,1)S(1)}, bf16[384,256]{1,0:T(8,128)(2,1)S(1)}, u32[]{:S(2)}, u32[]{:S(2)}) collective-permute-start(bf16[384,256]{1,0:T(8,128)(2,1)S(1)} %get-tuple-element.23), channel_id=1, source_target_pairs={{0,28},{4,24},{8,20},{12,16},{16,12},{20,8},{24,4},{28,0},{1,29},{... | collective-permute-start | bytes 589832 | tf_op jit(solution)/shard_map/ppermute | solution.py:578
  25.0 15.1 %collective-permute-start.7 = (bf16[2,320,128]{2,1,0:T(8,128)(2,1)S(1)}, bf16[2,320,128]{2,1,0:T(8,128)(2,1)S(1)}, u32[]{:S(2)}, u32[]{:S(2)}) collective-permute-start(bf16[2,320,128]{2,1,0:T(8,128)(2,1)S(1)} %shard_map.142.first_ref), channel_id=1, source_target_pairs={{0,8},{4,12},{8,0},{12,4},{16,24},{20,28},{24,16},{28,20},{1,9},{5... | collective-permute-start | bytes 491528 | tf_op jit(solution)/shard_map/ppermute | solution.py:578
  40.1 12.5 %collective-permute-start.8 = (bf16[4,320,128]{2,1,0:T(8,128)(2,1)S(1)}, bf16[4,320,128]{2,1,0:T(8,128)(2,1)S(1)}, u32[]{:S(2)}, u32[]{:S(2)}) collective-permute-start(bf16[4,320,128]{2,1,0:T(8,128)(2,1)S(1)} %shard_map.143.held_ref), channel_id=1, source_target_pairs={{0,4},{4,0},{8,12},{12,8},{16,20},{20,16},{24,28},{28,24},{1,5},{5... | collective-permute-start | bytes 983048 | tf_op jit(solution)/shard_map/ppermute | solution.py:578
  50.5 0.6 copy-start.1
  51.1 23.0 %collective-permute-start.9 = (bf16[4,320,128]{2,1,0:T(8,128)(2,1)S(1)}, bf16[4,320,128]{2,1,0:T(8,128)(2,1)S(1)}, u32[]{:S(2)}, u32[]{:S(2)}) collective-permute-start(bf16[4,320,128]{2,1,0:T(8,128)(2,1)S(1)} %shard_map.143.held_ref), channel_id=1, source_target_pairs={{0,2},{1,3},{2,0},{3,1},{4,6},{5,7},{6,4},{7,5},{8,10},{9,11},{10,... | collective-permute-start | bytes 983048 | tf_op jit(solution)/shard_map/ppermute | solution.py:578
  52.6 0.7 copy-start.3
  55.0 19.0 %collective-permute-start.10 = (bf16[4,320,128]{2,1,0:T(8,128)(2,1)}, bf16[4,320,128]{2,1,0:T(8,128)(2,1)S(1)}, u32[]{:S(2)}, u32[]{:S(2)}) collective-permute-start(bf16[4,320,128]{2,1,0:T(8,128)(2,1)} %shard_map.144.got_ref), channel_id=1, source_target_pairs={{0,2},{1,3},{2,0},{3,1},{4,6},{5,7},{6,4},{7,5},{8,10},{9,11},{10,... | collective-permute-start | bytes 983048 | tf_op jit(solution)/shard_map/ppermute | solution.py:578
  55.6 11.1 %copy-start.2 = (f32[8,128]{1,0:T(8,128)S(1)}, f32[8,128]{1,0:T(8,128)}, u32[]{:S(2)}) copy-start(f32[8,128]{1,0:T(8,128)} %copy-done.1) | copy-start | bytes 12292
  55.6 18.5 %all-to-all-start = ((bf16[8,64,128]{2,1,0:T(8,128)(2,1)}), bf16[8,64,128]{2,1,0:T(8,128)(2,1)S(1)}, u32[]{:S(2)}, u32[]{:S(2)}) async-start(bf16[8,64,128]{2,1,0:T(8,128)(2,1)} %get-tuple-element.25), calls=%async_computation | async-start | bytes 262144 | tf_op jit(solution)/shard_map/all_to_all | solution.py:582
  66.7 1.0 copy-start
  68.4 19.2 %collective-permute-start.11 = (bf16[256,1280]{1,0:T(8,128)(2,1)S(1)}, bf16[256,1280]{1,0:T(8,128)(2,1)S(1)}, u32[]{:S(2)}, u32[]{:S(2)}) collective-permute-start(bf16[256,1280]{1,0:T(8,128)(2,1)S(1)} %shard_map.145.refs_0_), channel_id=1, source_target_pairs={{0,1},{1,0},{2,3},{3,2},{4,5},{5,4},{6,7},{7,6},{8,9},{9,8},{10,11... | collective-permute-start | bytes 1966088 | tf_op jit(solution)/shard_map/ppermute | solution.py:578
  74.8 12.8 %collective-permute-start.12 = (bf16[256,1280]{1,0:T(8,128)(2,1)S(1)}, bf16[256,1280]{1,0:T(8,128)(2,1)S(1)}, u32[]{:S(2)}, u32[]{:S(2)}) collective-permute-start(bf16[256,1280]{1,0:T(8,128)(2,1)S(1)} %shard_map.146.refs_1_), channel_id=1, source_target_pairs={{0,1},{1,0},{2,3},{3,2},{4,5},{5,4},{6,7},{7,6},{8,9},{9,8},{10,11... | collective-permute-start | bytes 1966088 | tf_op jit(solution)/shard_map/ppermute | solution.py:578
  75.5 12.1 %all-to-all-start.1 = ((bf16[8,64,128]{2,1,0:T(8,128)(2,1)}), bf16[8,64,128]{2,1,0:T(8,128)(2,1)S(1)}, u32[]{:S(2)}, u32[]{:S(2)}) async-start(bf16[8,64,128]{2,1,0:T(8,128)(2,1)} %shard_map.141), calls=%async_computation.1 | async-start | bytes 262144 | tf_op jit(solution)/shard_map/all_to_all | solution.py:582
  92.7 3.7 %collective-permute-start.15 = (bf16[64,256]{1,0:T(8,128)(2,1)S(1)}, bf16[64,256]{1,0:T(8,128)(2,1)S(1)}, u32[]{:S(2)}, u32[]{:S(2)}) collective-permute-start(bf16[64,256]{1,0:T(8,128)(2,1)S(1)} %get-tuple-element.30.refs_0_), channel_id=1, source_target_pairs={{0,3},{1,2},{2,1},{3,0},{4,7},{5,6},{6,5},{7,4},{8,11},{9,10},{10,... | collective-permute-start | bytes 98312 | tf_op jit(solution)/shard_map/ppermute | solution.py:578
  92.7 4.0 %collective-permute-start.14 = (bf16[64,256]{1,0:T(8,128)(2,1)S(1)}, bf16[64,256]{1,0:T(8,128)(2,1)S(1)}, u32[]{:S(2)}, u32[]{:S(2)}) collective-permute-start(bf16[64,256]{1,0:T(8,128)(2,1)S(1)} %get-tuple-element.30.refs_0_), channel_id=1, source_target_pairs={{0,2},{1,3},{2,0},{3,1},{4,6},{5,7},{6,4},{7,5},{8,10},{9,11},{10,... | collective-permute-start | bytes 98312 | tf_op jit(solution)/shard_map/ppermute | solution.py:578
  94.3 2.5 %collective-permute-start.13 = (bf16[64,256]{1,0:T(8,128)(2,1)S(1)}, bf16[64,256]{1,0:T(8,128)(2,1)S(1)}, u32[]{:S(2)}, u32[]{:S(2)}) collective-permute-start(bf16[64,256]{1,0:T(8,128)(2,1)S(1)} %get-tuple-element.30.refs_0_), channel_id=1, source_target_pairs={{0,1},{1,0},{2,3},{3,2},{4,5},{5,4},{6,7},{7,6},{8,9},{9,8},{10,11... | collective-permute-start | bytes 98312 | tf_op jit(solution)/shard_map/ppermute | solution.py:578
  97.5 13.0 %all-to-all-start.2 = ((bf16[8,64,256]{2,1,0:T(8,128)(2,1)}), bf16[8,64,256]{2,1,0:T(8,128)(2,1)S(1)}, u32[]{:S(2)}, u32[]{:S(2)}) async-start(bf16[8,64,256]{2,1,0:T(8,128)(2,1)} %shard_map.149), calls=%async_computation.2 | async-start | bytes 524288 | tf_op jit(solution)/shard_map/all_to_all | solution.py:582

commit v8 on v7

--- a/solution.py
+++ b/solution.py
@@ -58,6 +58,7 @@
         self.share_rows = self.share * self.local
         self.chunks = VW // HD
         self.riding = self.local % 8 == 0 and self.share_rows % 16 == 0 and seq_count == 8
+        self.riding = self.riding and 1 < data_count <= positions
         self.ride_rows = self.chunks * self.share_rows if self.riding else 0
 
     def pieces(self):
@@ -195,35 +196,38 @@
     )(first, second, *others)
 
 
-def arrange_kernel(sizes, masks, place_ref, held_ref, got_ref, wait_ref, out_ref):
-    del wait_ref
+def arrange_kernel(sizes, masks, place_ref, *refs):
+    *pair_refs, out_ref = refs[:-2] + refs[-1:]
     me = place_ref[0]
     odd = me % 2 == 1
-    local, width = sizes.local, HD
-    for slot, mask in enumerate(masks):
-        pair = jnp.bitwise_xor(me, mask) // 2
-        for chunk in range(sizes.chunks):
-            rows = pl.ds(chunk * sizes.share_rows, sizes.share_rows)
-            held = held_ref[slot, rows, :].astype(F32)
-            got = got_ref[slot, rows, :].astype(F32)
-            first = jnp.where(odd, got, held)
-            second = jnp.where(odd, held, got)
-            for at in range(sizes.share):
-                part = slice(at * local, (at + 1) * local)
-                both = jnp.concatenate([first[part], second[part]], axis=0).astype(BF16)
-                start = pl.multiple_of(at * sizes.count * local + pair * 2 * local, 2 * local)
-                out_ref[pl.ds(start, 2 * local), pl.ds(chunk * width, width)] = both
-
-
-def arrange(sizes, masks, place, held, got, wait):
+    local = sizes.local
+    for quarter in range(len(pair_refs) // 2):
+        held_ref, got_ref = pair_refs[2 * quarter], pair_refs[2 * quarter + 1]
+        for slot, mask in enumerate(masks):
+            pair = jnp.bitwise_xor(me, mask) // 2
+            for chunk in range(sizes.chunks):
+                rows = pl.ds(chunk * sizes.share_rows, sizes.share_rows)
+                held = held_ref[slot, rows, :].astype(F32)
+                got = got_ref[slot, rows, :].astype(F32)
+                first = jnp.where(odd, got, held)
+                second = jnp.where(odd, held, got)
+                for at in range(sizes.share):
+                    part = slice(at * local, (at + 1) * local)
+                    both = jnp.concatenate([first[part], second[part]], axis=0).astype(BF16)
+                    start = pl.multiple_of(at * sizes.count * local + pair * 2 * local, 2 * local)
+                    out_ref[quarter, pl.ds(start, 2 * local), pl.ds(chunk * HD, HD)] = both
+
+
+def arrange(sizes, masks, place, pairs, wait):
     rows = sizes.share * sizes.count * sizes.local
+    flat = [x for pair in pairs for x in pair]
     return pl.pallas_call(
         functools.partial(arrange_kernel, sizes, masks),
-        out_shape=jax.ShapeDtypeStruct((rows, VW), BF16),
-        in_specs=[SMEM_SPEC, VMEM_SPEC, VMEM_SPEC, VMEM_SPEC],
+        out_shape=jax.ShapeDtypeStruct((len(pairs), rows, VW), BF16),
+        in_specs=[SMEM_SPEC] + [VMEM_SPEC] * (len(flat) + 1),
         out_specs=VMEM_SPEC,
         compiler_params=limits(),
-    )(place, held, got, wait)
+    )(place, *flat, wait)
 
 
 def attend_kernel(sizes, masks, place_ref, *refs):
@@ -364,12 +368,12 @@
     patch_cols = GW // 4
     patches = patch_rows * patch_cols
     copies = []
-    for slot, mask in enumerate(embed_masks):
-        rows = embed_refs[slot].shape[0]
-        first = pl.multiple_of(jnp.bitwise_xor(place_ref[1], mask) * rows, rows)
-        copies.append(
-            pltpu.make_async_copy(embed_refs[slot], embed_ref.at[pl.ds(first, rows)], sems.at[slot])
-        )
+    for ref, masks in zip(embed_refs, embed_masks):
+        for slot, mask in enumerate(masks):
+            rows = ref.shape[1]
+            first = pl.multiple_of(jnp.bitwise_xor(place_ref[1], mask) * rows, rows)
+            to = embed_ref.at[pl.ds(first, rows)]
+            copies.append(pltpu.make_async_copy(ref.at[slot], to, sems.at[len(copies)]))
     for slot, (side, scr) in enumerate(zip(sides, (pos_ref, pre_ref, post_ref, prompt_ref))):
         copies.append(pltpu.make_async_copy(side, scr, side_sems.at[slot]))
     for copy in copies:
@@ -463,7 +467,7 @@
     patches = grid_rows * GW // 16
     rows = grid_rows * GW // 2
     width = modulated.shape[2]
-    embed_arrays, embed_masks = [x for x, _ in embed], [mask for _, mask in embed]
+    embed_arrays, embed_masks = [x for x, _ in embed], [masks for _, masks in embed]
     return pl.pallas_call(
         functools.partial(head_kernel, grid_rows, fused, embed_masks, out_factor),
         out_shape=(
@@ -484,7 +488,7 @@
             pltpu.VMEM((VW,), F32),
             pltpu.VMEM((VW,), F32),
             pltpu.VMEM((1, VW), F32),
-            pltpu.SemaphoreType.DMA((len(embed_arrays),)),
+            pltpu.SemaphoreType.DMA((sum(len(masks) for masks in embed_masks),)),
             pltpu.SemaphoreType.DMA((4,)),
         ],
         compiler_params=limits(16),
@@ -584,17 +588,14 @@
     )
 
 
-def after_kernel(*refs):
-    refs[-1][...] = refs[0][...]
-
-
-def after(x, others):
-    return pl.pallas_call(
-        after_kernel,
-        out_shape=jax.ShapeDtypeStruct(x.shape, x.dtype),
-        in_specs=[VMEM_SPEC] * (1 + len(others)),
-        out_specs=VMEM_SPEC,
-    )(x, *others)
+def swap_both(x, seq_mask, data_mask):
+    seq_count, data_count = lax.axis_size("seq"), lax.axis_size("dp")
+    pairs = [
+        (i * data_count + j, (i ^ seq_mask) * data_count + (j ^ data_mask))
+        for i in range(seq_count)
+        for j in range(data_count)
+    ]
+    return lax.ppermute(x, ("seq", "dp"), pairs)
 
 
 def on_device(
@@ -638,20 +639,20 @@
     if sizes.riding:
         ride = [slot for slot, mask in enumerate(masks) if sizes.rides(mask)]
         two = collect(sizes, [received[slot] for slot in ride])
-        held = join(two, swap(two, "seq", 2), received)
+        held = join(two, swap(two, "seq", 2), received[:-1])
         ride_masks = [masks[slot] for slot in ride]
         ride_masks = ride_masks + [mask ^ 2 for mask in ride_masks]
-        got = swap(held, "seq", 1)
-        far_held = swap(held, "dp", bits[0]) if shared else None
+        pairs = [
+            (held, swap(held, "seq", 1)),
+            (swap(held, "dp", bits[0]), swap_both(held, 1, bits[0])),
+        ]
 
     modulated, latent_part, token = attend(
         sizes, masks, place, received, in_hbm(scales), in_hbm(shifts), in_hbm(proj_turned)
     )
 
     if sizes.riding:
-        got = after(got, [token])
-        embed = [(arrange(sizes, ride_masks, place, held, got, token), 0)]
-        far_got = swap(got, "dp", bits[0]) if shared else None
+        embed = [(arrange(sizes, ride_masks, place, pairs, token), [0, bits[0]])]
     else:
         mine = patch_embed
         if shared:
@@ -659,19 +660,17 @@
                 patch_embed, lax.axis_index("dp") * sizes.share, sizes.share, 0
             )
         mine = lax.all_gather(mine, "seq", axis=1, tiled=True).reshape(-1, VW)
-        embed = [(mine, 0)]
+        embed = [(mine[None], [0])]
         if shared:
-            embed = embed + [(swap(mine, "dp", bits[0]), bits[0])]
+            embed = embed + [(swap(mine[None], "dp", bits[0]), [bits[0]])]
 
     groups = None
     if query_parts > 1:
         groups = [[g * query_parts + r for g in range(group_count)] for r in range(query_parts)]
     per_share = seq_count // group_count
     parts = all_to_all(latent_part.reshape(group_count, per_share * half, 2 * CH), groups)
-    if sizes.riding and shared:
-        embed.append((arrange(sizes, ride_masks, place, far_held, far_got, parts), bits[0]))
     for bit in bits[1:] if shared else []:
-        embed = embed + [(swap(x, "dp", bit), m ^ bit) for x, m in embed]
+        embed = embed + [(swap(x, "dp", bit), [m ^ bit for m in some]) for x, some in embed]
     latent = all_to_all(total_copies([parts], seq_count))
     if canonical:
         latent = latent.reshape(lat_rows // 2, 2 * CH)

time: 112 us -> 112 us (level)
  blocking collectives: 0 us -> 18 us
  starting transfers between devices: 37.9 us -> 26.4 us
  Pallas kernels: 25.2 us -> 22.2 us
  local copies, waits for them, and re-layouts: 2.28 us -> 0 us
  waiting for transfers between devices: 44.5 us -> 43.2 us
    all_to_all x0 -> x1, blocking collectives: none -> 18 us  [all_to_all(): lax.all_to_all(x, 'seq', split_axis=0, concat_axis=0, tiled=True, axis_in...]
    all_to_all x3 -> x2, starting transfers between devices: 19.1 us -> 6.78 us  [all_to_all(): lax.all_to_all(x, 'seq', split_axis=0, concat_axis=0, tiled=True, axis_in...]
    all_to_all x3 -> x2, waiting for transfers between devices: 19.6 us -> 13.8 us  [all_to_all(): lax.all_to_all(x, 'seq', split_axis=0, concat_axis=0, tiled=True, axis_in...]
    ppermute x16 -> x14, waiting for transfers between devices: 24.9 us -> 29.4 us  [swap(): return lax.ppermute(x, axis, [(i, i ^ mask) for i in range(count)])]
    unnamed x8 -> x0, local copies, waits for them, and re-layouts: 2.28 us -> none
    pallas_call x1 -> x0, Pallas kernels: 1.72 us -> none  [after(): pl.pallas_call(after_kernel, out_shape=jax.ShapeDtypeStruct(x.shape, x.dt...]
    ppermute x0 -> x1, starting transfers between devices: none -> 1.55 us  [swap_both(): return lax.ppermute(x, ('seq', 'dp'), pairs)]
    ppermute x16 -> x14, starting transfers between devices: 18.8 us -> 18.1 us  [swap(): return lax.ppermute(x, axis, [(i, i ^ mask) for i in range(count)])]
  transfers between devices with their start and end apart: 19 -> 17, of which waited for: 11 -> 12; matrix products, arithmetic and copies ran while one was open for 0% -> 0% of each run, Pallas kernels for 14% -> 11%
where the time goes in v8:
time: 112 us; the launch traced here: 111 us
  waiting for transfers between devices  43.2 us (39%)
  starting transfers between devices  26.4 us (24%)
  Pallas kernels  22.2 us (20%)
  blocking collectives  18 us (16%)
  between operations  1.38 us (1%)
    ppermute x14, waiting for transfers between devices, swap(): return lax.ppermute(x, axis, [(i, i ^ mask) for i in range(count)])  29.4 us
    ppermute x14, starting transfers between devices, swap(): return lax.ppermute(x, axis, [(i, i ^ mask) for i in range(count)])  18.1 us
    all_to_all x1, blocking collectives, all_to_all(): lax.all_to_all(x, 'seq', split_axis=0, concat_axis=0, tiled=True, axis_in...  18 us
    all_to_all x2, waiting for transfers between devices, all_to_all(): lax.all_to_all(x, 'seq', split_axis=0, concat_axis=0, tiled=True, axis_in...  13.8 us
    pallas_call x1, Pallas kernels, attend(): pl.pallas_call(functools.partial(attend_kernel, sizes, masks), out_shape=...  9.12 us
    all_to_all x2, starting transfers between devices, all_to_all(): lax.all_to_all(x, 'seq', split_axis=0, concat_axis=0, tiled=True, axis_in...  6.78 us
    pallas_call x1, Pallas kernels, reward_head(): pl.pallas_call(functools.partial(head_kernel, grid_rows, fused, embed_mas...  5.04 us
    pallas_call x1, Pallas kernels, pack(): pl.pallas_call(functools.partial(pack_kernel, sizes), out_shape=[jax.Shap...  2.47 us
  transfers between devices with their start and end apart: 17, of which 12 were waited for; matrix products, arithmetic and copies ran while one was open for 0% of the time, Pallas kernels for 11%

profile of v8, /device:TPU:0, one launch (start us, length us, event | category | flops | bytes accessed | tf_op | source)
XLA Modules:
  0.0 111.3 jit_solution(8828974058465253889)
XLA Ops:
  0.7 2.5 %shard_map.139 = (bf16[384,256]{1,0:T(8,128)(2,1)S(1)}, bf16[384,256]{1,0:T(8,128)(2,1)S(1)}, bf16[384,256]{1,0:T(8,128)(2,1)S(1)}, bf16[544,256]{1,0:T(8,128)(2...) custom-call(s32[3]{0:T(128)S(1)} %pad_add_fusion.place_ref, ...), custom_call_target="tpu_custom_call" | custom-call | bytes 3145728 | tf_op jit(solution)/shard_map/pallas_call | solution.py:136
  3.2 4.1 %collective-permute-start.3 = (bf16[544,256]{1,0:T(8,128)(2,1)S(1)}, bf16[544,256]{1,0:T(8,128)(2,1)S(1)}, u32[]{:S(2)}, u32[]{:S(2)}) collective-permute-start(bf16[544,256]{1,0:T(8,128)(2,1)S(1)} %get-tuple-element.20), channel_id=1, source_target_pairs={{0,16},{4,20},{8,24},{12,28},{16,0},{20,4},{24,8},{28,12},{1,17},{... | collective-permute-start | bytes 835592 | tf_op jit(solution)/shard_map/ppermute | solution.py:582
  7.3 1.5 %collective-permute-start = (bf16[384,256]{1,0:T(8,128)(2,1)S(1)}, bf16[384,256]{1,0:T(8,128)(2,1)S(1)}, u32[]{:S(2)}, u32[]{:S(2)}) collective-permute-start(bf16[384,256]{1,0:T(8,128)(2,1)S(1)} %get-tuple-element.17), channel_id=1, source_target_pairs={{0,4},{4,0},{8,12},{12,8},{16,20},{20,16},{24,28},{28,24},{1,5},{5... | collective-permute-start | bytes 589832 | tf_op jit(solution)/shard_map/ppermute | solution.py:582
  8.8 1.6 %collective-permute-start.1 = (bf16[384,256]{1,0:T(8,128)(2,1)S(1)}, bf16[384,256]{1,0:T(8,128)(2,1)S(1)}, u32[]{:S(2)}, u32[]{:S(2)}) collective-permute-start(bf16[384,256]{1,0:T(8,128)(2,1)S(1)} %get-tuple-element.18), channel_id=1, source_target_pairs={{0,8},{4,12},{8,0},{12,4},{16,24},{20,28},{24,16},{28,20},{1,9},{5... | collective-permute-start | bytes 589832 | tf_op jit(solution)/shard_map/ppermute | solution.py:582
  10.8 1.3 %collective-permute-start.4 = (bf16[384,256]{1,0:T(8,128)(2,1)S(1)}, bf16[384,256]{1,0:T(8,128)(2,1)S(1)}, u32[]{:S(2)}, u32[]{:S(2)}) collective-permute-start(bf16[384,256]{1,0:T(8,128)(2,1)S(1)} %get-tuple-element.21), channel_id=1, source_target_pairs={{0,20},{4,16},{8,28},{12,24},{16,4},{20,0},{24,12},{28,8},{1,21},{... | collective-permute-start | bytes 589832 | tf_op jit(solution)/shard_map/ppermute | solution.py:582
  12.1 2.2 %collective-permute-done.refs_0_ = bf16[384,256]{1,0:T(8,128)(2,1)S(1)} collective-permute-done((bf16[384,256]{1,0:T(8,128)(2,1)S(1)}, bf16[384,256]{1,0:T(8,128)(2,1)S(1)}, u32[]{:S(2)}, u32[]{:S(2)}) %collective-permute-start) | collective-permute-done | bytes 196640 | tf_op jit(solution)/shard_map/ppermute | solution.py:582
  14.2 1.4 %collective-permute-start.5 = (bf16[384,256]{1,0:T(8,128)(2,1)S(1)}, bf16[384,256]{1,0:T(8,128)(2,1)S(1)}, u32[]{:S(2)}, u32[]{:S(2)}) collective-permute-start(bf16[384,256]{1,0:T(8,128)(2,1)S(1)} %get-tuple-element.22), channel_id=1, source_target_pairs={{0,24},{4,28},{8,16},{12,20},{16,8},{20,12},{24,0},{28,4},{1,25},{... | collective-permute-start | bytes 589832 | tf_op jit(solution)/shard_map/ppermute | solution.py:582
  15.7 5.2 %collective-permute-done.3.refs_3_.refs_0_ = bf16[544,256]{1,0:T(8,128)(2,1)S(1)} collective-permute-done((bf16[544,256]{1,0:T(8,128)(2,1)S(1)}, bf16[544,256]{1,0:T(8,128)(2,1)S(1)}, u32[]{:S(2)}, u32[]{:S(2)}) %collective-permute-start.3) | collective-permute-done | bytes 278560 | tf_op jit(solution)/shard_map/ppermute | solution.py:582
  20.8 3.8 %collective-permute-start.6 = (bf16[384,256]{1,0:T(8,128)(2,1)S(1)}, bf16[384,256]{1,0:T(8,128)(2,1)S(1)}, u32[]{:S(2)}, u32[]{:S(2)}) collective-permute-start(bf16[384,256]{1,0:T(8,128)(2,1)S(1)} %get-tuple-element.23), channel_id=1, source_target_pairs={{0,28},{4,24},{8,20},{12,16},{16,12},{20,8},{24,4},{28,0},{1,29},{... | collective-permute-start | bytes 589832 | tf_op jit(solution)/shard_map/ppermute | solution.py:582
  25.0 2.5 %collective-permute-done.2.refs_2_ = bf16[384,256]{1,0:T(8,128)(2,1)S(1)} collective-permute-done((bf16[384,256]{1,0:T(8,128)(2,1)S(1)}, bf16[384,256]{1,0:T(8,128)(2,1)S(1)}, u32[]{:S(2)}, u32[]{:S(2)}) %collective-permute-start.2) | collective-permute-done | bytes 196640 | tf_op jit(solution)/shard_map/ppermute | solution.py:582
  27.5 11.5 %collective-permute-done.4.refs_4_ = bf16[384,256]{1,0:T(8,128)(2,1)S(1)} collective-permute-done((bf16[384,256]{1,0:T(8,128)(2,1)S(1)}, bf16[384,256]{1,0:T(8,128)(2,1)S(1)}, u32[]{:S(2)}, u32[]{:S(2)}) %collective-permute-start.4) | collective-permute-done | bytes 196640 | tf_op jit(solution)/shard_map/ppermute | solution.py:582
  40.1 1.5 %collective-permute-start.10 = (bf16[4,320,128]{2,1,0:T(8,128)(2,1)S(1)}, bf16[4,320,128]{2,1,0:T(8,128)(2,1)S(1)}, u32[]{:S(2)}, u32[]{:S(2)}) collective-permute-start(bf16[4,320,128]{2,1,0:T(8,128)(2,1)S(1)} %shard_map.143.refs_0_), channel_id=1, source_target_pairs={{0,6},{1,7},{2,4},{3,5},{4,2},{5,3},{6,0},{7,1},{8,14},{9,15},{10,... | collective-permute-start | bytes 983048 | tf_op jit(solution)/shard_map/ppermute | solution.py:598
  42.2 1.5 %collective-permute-start.8 = (bf16[4,320,128]{2,1,0:T(8,128)(2,1)S(1)}, bf16[4,320,128]{2,1,0:T(8,128)(2,1)S(1)}, u32[]{:S(2)}, u32[]{:S(2)}) collective-permute-start(bf16[4,320,128]{2,1,0:T(8,128)(2,1)S(1)} %shard_map.143.refs_0_), channel_id=1, source_target_pairs={{0,4},{4,0},{8,12},{12,8},{16,20},{20,16},{24,28},{28,24},{1,5},{5... | collective-permute-start | bytes 983048 | tf_op jit(solution)/shard_map/ppermute | solution.py:582
  43.6 9.1 %shard_map.140 = (bf16[8,128,256]{2,1,0:T(8,128)(2,1)S(1)}, bf16[8,64,128]{2,1,0:T(8,128)(2,1)S(1)}, f32[8,128]{1,0:T(8,128)S(1)}) custom-call(s32[3]{0:T(128)S(1)} %pad_add_fusion.place_ref, bf16[384,256]{1,0:T(8,128)(2,1)S(1)} %collective-permute-done.refs_0_, bf16[384,256]{1,0:T(8,128)(2,1)S(1)} %collective-permute-done.1.refs_1_, ...), custom_call_target="tpu_custom_call" | custom-call | flops 1073741824 | bytes 2097152 | tf_op jit(solution)/shard_map/pallas_call | solution.py:306
  52.8 3.6 %collective-permute-done.9.refs_2_ = bf16[4,320,128]{2,1,0:T(8,128)(2,1)S(1)} collective-permute-done((bf16[4,320,128]{2,1,0:T(8,128)(2,1)S(1)}, bf16[4,320,128]{2,1,0:T(8,128)(2,1)S(1)}, u32[]{:S(2)}, u32[]{:S(2)}) %collective-permute-start.9) | collective-permute-done | bytes 327712 | tf_op jit(solution)/shard_map/ppermute | solution.py:582
  58.2 18.0 %all_to_all.15.refs_0_ = bf16[8,64,128]{2,1,0:T(8,128)(2,1)S(1)} all-to-all(bf16[8,64,128]{2,1,0:T(8,128)(2,1)S(1)} %get-tuple-element.25), channel_id=1, replica_groups=mesh['seq'=8,'dp'=4] {'seq'}, dimensions={0} | all-to-all | bytes 262144 | tf_op jit(solution)/shard_map/all_to_all | solution.py:586
  76.9 3.4 %all-to-all-start.1 = ((bf16[8,64,128]{2,1,0:T(8,128)(2,1)}), bf16[8,64,128]{2,1,0:T(8,128)(2,1)S(1)}, u32[]{:S(2)}, u32[]{:S(2)}) async-start(bf16[8,64,128]{2,1,0:T(8,128)(2,1)} %shard_map.141), calls=%async_computation.1 | async-start | bytes 262144 | tf_op jit(solution)/shard_map/all_to_all | solution.py:586
  80.9 6.6 %all-to-all-done.1 = bf16[8,64,128]{2,1,0:T(8,128)(2,1)S(1)} async-done(((bf16[8,64,128]{2,1,0:T(8,128)(2,1)}), bf16[8,64,128]{2,1,0:T(8,128)(2,1)S(1)}, u32[]{:S(2)}, u32[]{:S(2)}) %all-to-all-start.1) | async-done | bytes 131104 | tf_op jit(solution)/shard_map/all_to_all | solution.py:586
  87.6 5.0 %shard_map.145 = (f32[1,128]{1,0:T(1,128)}, bf16[512,128]{1,0:T(8,128)(2,1)S(1)}, bf16[64,256]{1,0:T(8,128)(2,1)S(1)}) custom-call(s32[3]{0:T(128)S(1)} %pad_add_fusion.place_ref, bf16[512,128]{1,0:T(8,128)(2,1)S(1)} %bitcast.7, bf16[2,256,1280]{2,1,0:T(8,128)(2,1)S(1)} %shard_map.144.refs_0_, bf16[2,256,1280]{2,1,0:T(8,128)(2,1)S(1)} %collective-permute-done.11.refs_1_, ...), custom_call_target="tpu_custom_call" | custom-call | flops 503316480 | bytes 2785280 | tf_op jit(solution)/shard_map/pallas_call | solution.py:471
  92.7 1.6 %collective-permute-start.13 = (bf16[64,256]{1,0:T(8,128)(2,1)S(1)}, bf16[64,256]{1,0:T(8,128)(2,1)S(1)}, u32[]{:S(2)}, u32[]{:S(2)}) collective-permute-start(bf16[64,256]{1,0:T(8,128)(2,1)S(1)} %get-tuple-element.30.refs_0_), channel_id=1, source_target_pairs={{0,2},{1,3},{2,0},{3,1},{4,6},{5,7},{6,4},{7,5},{8,10},{9,11},{10,... | collective-permute-start | bytes 98312 | tf_op jit(solution)/shard_map/ppermute | solution.py:582
  94.5 1.8 %collective-permute-done.14.refs_3_ = bf16[64,256]{1,0:T(8,128)(2,1)S(1)} collective-permute-done((bf16[64,256]{1,0:T(8,128)(2,1)S(1)}, bf16[64,256]{1,0:T(8,128)(2,1)S(1)}, u32[]{:S(2)}, u32[]{:S(2)}) %collective-permute-start.14) | collective-permute-done | bytes 32800 | tf_op jit(solution)/shard_map/ppermute | solution.py:582
  97.4 3.4 %all-to-all-start.2 = ((bf16[8,64,256]{2,1,0:T(8,128)(2,1)}), bf16[8,64,256]{2,1,0:T(8,128)(2,1)S(1)}, u32[]{:S(2)}, u32[]{:S(2)}) async-start(bf16[8,64,256]{2,1,0:T(8,128)(2,1)} %shard_map.147), calls=%async_computation.2 | async-start | bytes 524288 | tf_op jit(solution)/shard_map/all_to_all | solution.py:586
  100.9 2.4 %shard_map.146 = bf16[1,2,1024,128]{3,2,1,0:T(8,128)(2,1)} custom-call(s32[3]{0:T(128)S(1)} %pad_add_fusion.place_ref, bf16[512,128]{1,0:T(8,128)(2,1)S(1)} %get-tuple-element.29.grad_ref, f32[1,2048]{1,0:T(1,128)} %scale_ref.1, bf16[64,2048]{1,0:T(8,128)(2,1)} %bitcast.10), custom_call_target="tpu_custom_call" | custom-call | flops 67108864 | bytes 524288 | tf_op jit(solution)/shard_map/pallas_call | solution.py:531
  103.3 7.2 %all-to-all-done.2.in_ref = bf16[8,64,256]{2,1,0:T(8,128)(2,1)S(1)} async-done(((bf16[8,64,256]{2,1,0:T(8,128)(2,1)}), bf16[8,64,256]{2,1,0:T(8,128)(2,1)S(1)}, u32[]{:S(2)}, u32[]{:S(2)}) %all-to-all-start.2) | async-done | bytes 262176 | tf_op jit(solution)/shard_map/all_to_all | solution.py:586
  (22 shorter events, 7.3 us)
Async XLA Ops:
  3.2 17.7 %collective-permute-start.3 = (bf16[544,256]{1,0:T(8,128)(2,1)S(1)}, bf16[544,256]{1,0:T(8,128)(2,1)S(1)}, u32[]{:S(2)}, u32[]{:S(2)}) collective-permute-start(bf16[544,256]{1,0:T(8,128)(2,1)S(1)} %get-tuple-element.20), channel_id=1, source_target_pairs={{0,16},{4,20},{8,24},{12,28},{16,0},{20,4},{24,8},{28,12},{1,17},{... | collective-permute-start | bytes 835592 | tf_op jit(solution)/shard_map/ppermute | solution.py:582
  7.3 6.9 %collective-permute-start = (bf16[384,256]{1,0:T(8,128)(2,1)S(1)}, bf16[384,256]{1,0:T(8,128)(2,1)S(1)}, u32[]{:S(2)}, u32[]{:S(2)}) collective-permute-start(bf16[384,256]{1,0:T(8,128)(2,1)S(1)} %get-tuple-element.17), channel_id=1, source_target_pairs={{0,4},{4,0},{8,12},{12,8},{16,20},{20,16},{24,28},{28,24},{1,5},{5... | collective-permute-start | bytes 589832 | tf_op jit(solution)/shard_map/ppermute | solution.py:582
  8.8 16.1 %collective-permute-start.1 = (bf16[384,256]{1,0:T(8,128)(2,1)S(1)}, bf16[384,256]{1,0:T(8,128)(2,1)S(1)}, u32[]{:S(2)}, u32[]{:S(2)}) collective-permute-start(bf16[384,256]{1,0:T(8,128)(2,1)S(1)} %get-tuple-element.18), channel_id=1, source_target_pairs={{0,8},{4,12},{8,0},{12,4},{16,24},{20,28},{24,16},{28,20},{1,9},{5... | collective-permute-start | bytes 589832 | tf_op jit(solution)/shard_map/ppermute | solution.py:582
  10.4 17.1 %collective-permute-start.2 = (bf16[384,256]{1,0:T(8,128)(2,1)S(1)}, bf16[384,256]{1,0:T(8,128)(2,1)S(1)}, u32[]{:S(2)}, u32[]{:S(2)}) collective-permute-start(bf16[384,256]{1,0:T(8,128)(2,1)S(1)} %get-tuple-element.19), channel_id=1, source_target_pairs={{0,12},{4,8},{8,4},{12,0},{16,28},{20,24},{24,20},{28,16},{1,13},{... | collective-permute-start | bytes 589832 | tf_op jit(solution)/shard_map/ppermute | solution.py:582
  10.8 28.2 %collective-permute-start.4 = (bf16[384,256]{1,0:T(8,128)(2,1)S(1)}, bf16[384,256]{1,0:T(8,128)(2,1)S(1)}, u32[]{:S(2)}, u32[]{:S(2)}) collective-permute-start(bf16[384,256]{1,0:T(8,128)(2,1)S(1)} %get-tuple-element.21), channel_id=1, source_target_pairs={{0,20},{4,16},{8,28},{12,24},{16,4},{20,0},{24,12},{28,8},{1,21},{... | collective-permute-start | bytes 589832 | tf_op jit(solution)/shard_map/ppermute | solution.py:582
  14.2 24.8 %collective-permute-start.5 = (bf16[384,256]{1,0:T(8,128)(2,1)S(1)}, bf16[384,256]{1,0:T(8,128)(2,1)S(1)}, u32[]{:S(2)}, u32[]{:S(2)}) collective-permute-start(bf16[384,256]{1,0:T(8,128)(2,1)S(1)} %get-tuple-element.22), channel_id=1, source_target_pairs={{0,24},{4,28},{8,16},{12,20},{16,8},{20,12},{24,0},{28,4},{1,25},{... | collective-permute-start | bytes 589832 | tf_op jit(solution)/shard_map/ppermute | solution.py:582
  20.8 18.1 %collective-permute-start.6 = (bf16[384,256]{1,0:T(8,128)(2,1)S(1)}, bf16[384,256]{1,0:T(8,128)(2,1)S(1)}, u32[]{:S(2)}, u32[]{:S(2)}) collective-permute-start(bf16[384,256]{1,0:T(8,128)(2,1)S(1)} %get-tuple-element.23), channel_id=1, source_target_pairs={{0,28},{4,24},{8,20},{12,16},{16,12},{20,8},{24,4},{28,0},{1,29},{... | collective-permute-start | bytes 589832 | tf_op jit(solution)/shard_map/ppermute | solution.py:582
  25.0 15.1 %collective-permute-start.7 = (bf16[2,320,128]{2,1,0:T(8,128)(2,1)S(1)}, bf16[2,320,128]{2,1,0:T(8,128)(2,1)S(1)}, u32[]{:S(2)}, u32[]{:S(2)}) collective-permute-start(bf16[2,320,128]{2,1,0:T(8,128)(2,1)S(1)} %shard_map.142.first_ref), channel_id=1, source_target_pairs={{0,8},{4,12},{8,0},{12,4},{16,24},{20,28},{24,16},{28,20},{1,9},{5... | collective-permute-start | bytes 491528 | tf_op jit(solution)/shard_map/ppermute | solution.py:582
  40.1 12.7 %collective-permute-start.10 = (bf16[4,320,128]{2,1,0:T(8,128)(2,1)S(1)}, bf16[4,320,128]{2,1,0:T(8,128)(2,1)S(1)}, u32[]{:S(2)}, u32[]{:S(2)}) collective-permute-start(bf16[4,320,128]{2,1,0:T(8,128)(2,1)S(1)} %shard_map.143.refs_0_), channel_id=1, source_target_pairs={{0,6},{1,7},{2,4},{3,5},{4,2},{5,3},{6,0},{7,1},{8,14},{9,15},{10,... | collective-permute-start | bytes 983048 | tf_op jit(solution)/shard_map/ppermute | solution.py:598
  41.6 14.7 %collective-permute-start.9 = (bf16[4,320,128]{2,1,0:T(8,128)(2,1)S(1)}, bf16[4,320,128]{2,1,0:T(8,128)(2,1)S(1)}, u32[]{:S(2)}, u32[]{:S(2)}) collective-permute-start(bf16[4,320,128]{2,1,0:T(8,128)(2,1)S(1)} %shard_map.143.refs_0_), channel_id=1, source_target_pairs={{0,2},{1,3},{2,0},{3,1},{4,6},{5,7},{6,4},{7,5},{8,10},{9,11},{10,... | collective-permute-start | bytes 983048 | tf_op jit(solution)/shard_map/ppermute | solution.py:582
  42.2 15.1 %collective-permute-start.8 = (bf16[4,320,128]{2,1,0:T(8,128)(2,1)S(1)}, bf16[4,320,128]{2,1,0:T(8,128)(2,1)S(1)}, u32[]{:S(2)}, u32[]{:S(2)}) collective-permute-start(bf16[4,320,128]{2,1,0:T(8,128)(2,1)S(1)} %shard_map.143.refs_0_), channel_id=1, source_target_pairs={{0,4},{4,0},{8,12},{12,8},{16,20},{20,16},{24,28},{28,24},{1,5},{5... | collective-permute-start | bytes 983048 | tf_op jit(solution)/shard_map/ppermute | solution.py:582
  58.1 29.4 %collective-permute-start.11 = (bf16[2,256,1280]{2,1,0:T(8,128)(2,1)S(1)}, bf16[2,256,1280]{2,1,0:T(8,128)(2,1)S(1)}, u32[]{:S(2)}, u32[]{:S(2)}) collective-permute-start(bf16[2,256,1280]{2,1,0:T(8,128)(2,1)S(1)} %shard_map.144.refs_0_), channel_id=1, source_target_pairs={{0,1},{1,0},{2,3},{3,2},{4,5},{5,4},{6,7},{7,6},{8,9},{9,8},{10,11... | collective-permute-start | bytes 3932168 | tf_op jit(solution)/shard_map/ppermute | solution.py:582
  76.9 10.7 %all-to-all-start.1 = ((bf16[8,64,128]{2,1,0:T(8,128)(2,1)}), bf16[8,64,128]{2,1,0:T(8,128)(2,1)S(1)}, u32[]{:S(2)}, u32[]{:S(2)}) async-start(bf16[8,64,128]{2,1,0:T(8,128)(2,1)} %shard_map.141), calls=%async_computation.1 | async-start | bytes 262144 | tf_op jit(solution)/shard_map/all_to_all | solution.py:586
  92.6 3.7 %collective-permute-start.14 = (bf16[64,256]{1,0:T(8,128)(2,1)S(1)}, bf16[64,256]{1,0:T(8,128)(2,1)S(1)}, u32[]{:S(2)}, u32[]{:S(2)}) collective-permute-start(bf16[64,256]{1,0:T(8,128)(2,1)S(1)} %get-tuple-element.30.refs_0_), channel_id=1, source_target_pairs={{0,3},{1,2},{2,1},{3,0},{4,7},{5,6},{6,5},{7,4},{8,11},{9,10},{10,... | collective-permute-start | bytes 98312 | tf_op jit(solution)/shard_map/ppermute | solution.py:582
  92.7 4.0 %collective-permute-start.13 = (bf16[64,256]{1,0:T(8,128)(2,1)S(1)}, bf16[64,256]{1,0:T(8,128)(2,1)S(1)}, u32[]{:S(2)}, u32[]{:S(2)}) collective-permute-start(bf16[64,256]{1,0:T(8,128)(2,1)S(1)} %get-tuple-element.30.refs_0_), channel_id=1, source_target_pairs={{0,2},{1,3},{2,0},{3,1},{4,6},{5,7},{6,4},{7,5},{8,10},{9,11},{10,... | collective-permute-start | bytes 98312 | tf_op jit(solution)/shard_map/ppermute | solution.py:582
  94.2 2.5 %collective-permute-start.12 = (bf16[64,256]{1,0:T(8,128)(2,1)S(1)}, bf16[64,256]{1,0:T(8,128)(2,1)S(1)}, u32[]{:S(2)}, u32[]{:S(2)}) collective-permute-start(bf16[64,256]{1,0:T(8,128)(2,1)S(1)} %get-tuple-element.30.refs_0_), channel_id=1, source_target_pairs={{0,1},{1,0},{2,3},{3,2},{4,5},{5,4},{6,7},{7,6},{8,9},{9,8},{10,11... | collective-permute-start | bytes 98312 | tf_op jit(solution)/shard_map/ppermute | solution.py:582
  97.4 13.1 %all-to-all-start.2 = ((bf16[8,64,256]{2,1,0:T(8,128)(2,1)}), bf16[8,64,256]{2,1,0:T(8,128)(2,1)S(1)}, u32[]{:S(2)}, u32[]{:S(2)}) async-start(bf16[8,64,256]{2,1,0:T(8,128)(2,1)} %shard_map.147), calls=%async_computation.2 | async-start | bytes 524288 | tf_op jit(solution)/shard_map/all_to_all | solution.py:586

commit v9 on v8

--- a/solution.py
+++ b/solution.py
@@ -78,13 +78,13 @@
         ]
 
 
-def pack_kernel(sizes, place_ref, q_ref, k_ref, v_ref, embed_ref, *refs):
+def pack_kernel(sizes, q_ref, k_ref, v_ref, embed_ref, *refs):
     pieces = sizes.pieces()
     out_refs = refs[: len(pieces)]
     q_scr, k_scr, v_scr, embed_scr, share_scr, in_sems, out_sems = refs[len(pieces) :]
-    me = place_ref[0]
+    me = lax.axis_index("seq")
     tok_rows, part_rows, width = sizes.tok_rows, sizes.part_rows, sizes.width
-    share = pl.ds(place_ref[1] * sizes.share, sizes.share)
+    share = pl.ds(lax.axis_index("dp") * sizes.share, sizes.share)
     loads = [
         pltpu.make_async_copy(embed_ref.at[share], embed_scr, in_sems.at[3]),
         pltpu.make_async_copy(q_ref.at[0], q_scr, in_sems.at[0]),
@@ -130,13 +130,13 @@
             store.wait()
 
 
-def pack(sizes, place, queries, keys, values, patch_embed):
+def pack(sizes, queries, keys, values, patch_embed):
     tok_rows, full = queries.shape[1:]
     pieces = sizes.pieces()
     return pl.pallas_call(
         functools.partial(pack_kernel, sizes),
         out_shape=[jax.ShapeDtypeStruct(sizes.piece_shape(mask), BF16) for mask in pieces],
-        in_specs=[SMEM_SPEC] + [HBM_SPEC] * 4,
+        in_specs=[HBM_SPEC] * 4,
         out_specs=[HBM_SPEC] * len(pieces),
         scratch_shapes=[pltpu.VMEM((tok_rows, full), BF16)] * 3
         + [
@@ -149,7 +149,7 @@
         cost_estimate=pl.CostEstimate(
             flops=0, bytes_accessed=12 * tok_rows * full, transcendentals=0
         ),
-    )(place, queries, keys, values, patch_embed)
+    )(queries, keys, values, patch_embed)
 
 
 def collect_kernel(sizes, *refs):
@@ -234,7 +234,7 @@
     count, heads, width = sizes.count, sizes.heads, sizes.width
     tok_rows, part_rows = sizes.tok_rows, sizes.part_rows
     in_refs, refs = refs[:count], refs[count:]
-    scale_ref, shift_ref, proj_ref, mod_ref, lat_ref, token_ref, *refs = refs
+    scale_ref, shift_ref, proj_ref, mod_ref, lat_ref, *refs = refs
     query_scr, key_scr, value_scr, scale_scr, shift_scr, proj_scr, sems, side_sems = refs
     half = part_rows // 2
     factor = HD ** (-0.5) * math.log2(math.e)
@@ -264,7 +264,6 @@
     ]
     for copy in logit_copies + value_copies:
         copy.start()
-    token_ref[...] = jnp.zeros_like(token_ref)
     ones = jnp.ones((count * tok_rows, HD), BF16)
     for head in range(heads):
         value_scr[:, pl.ds((2 * head + 1) * HD, HD)] = ones
@@ -308,10 +307,9 @@
         out_shape=(
             jax.ShapeDtypeStruct((count, sizes.part_rows, width), BF16),
             jax.ShapeDtypeStruct((count, sizes.part_rows // 2, 2 * CH), BF16),
-            jax.ShapeDtypeStruct((8, 128), F32),
         ),
         in_specs=[SMEM_SPEC] + [ANY_SPEC] * count + [HBM_SPEC] * 3,
-        out_specs=(VMEM_SPEC, VMEM_SPEC, VMEM_SPEC),
+        out_specs=(VMEM_SPEC, VMEM_SPEC),
         scratch_shapes=[
             pltpu.VMEM((count, sizes.part_rows, width), BF16),
             pltpu.VMEM((lat_rows, width), BF16),
@@ -362,28 +360,25 @@
     sides, refs = refs[:4], refs[4:]
     cot_ref, refs = refs[0], refs[1:]
     mod_ref, refs = refs[0], refs[1:]
-    reward_ref, grad_ref, weight_ref, lat_scr, grad_scr, embed_ref, *refs = refs
-    pos_ref, pre_ref, post_ref, prompt_ref, sems, side_sems = refs
+    reward_ref, grad_ref, weight_ref, lat_scr, grad_scr, block_scr, back_scr, *refs = refs
+    pos_ref, pre_ref, post_ref, prompt_ref, side_sems = refs
     patch_rows = grid_rows // 4
     patch_cols = GW // 4
     patches = patch_rows * patch_cols
     copies = []
-    for ref, masks in zip(embed_refs, embed_masks):
-        for slot, mask in enumerate(masks):
-            rows = ref.shape[1]
-            first = pl.multiple_of(jnp.bitwise_xor(place_ref[1], mask) * rows, rows)
-            to = embed_ref.at[pl.ds(first, rows)]
-            copies.append(pltpu.make_async_copy(ref.at[slot], to, sems.at[len(copies)]))
     for slot, (side, scr) in enumerate(zip(sides, (pos_ref, pre_ref, post_ref, prompt_ref))):
         copies.append(pltpu.make_async_copy(side, scr, side_sems.at[slot]))
     for copy in copies:
         copy.start()
     lat_scr[...] = lat_ref[...].astype(F32)
 
-    def position_rows(ty):
-        return embed_ref[pl.ds(4 * ty * CH, 4 * CH), :]
-
-    blocks = []
+    data = place_ref[1]
+    shares = [
+        (jnp.bitwise_xor(data, mask), ref, slot)
+        for ref, masks in zip(embed_refs, embed_masks)
+        for slot, mask in enumerate(masks)
+    ]
+    share_rows = embed_refs[0].shape[1]
     for hi in range(2):
         wide = []
         for tx in range(4):
@@ -394,12 +389,19 @@
             wide.append(jnp.concatenate(rows, axis=0))
         for side in range(2):
             lanes = slice(side * CH, (side + 1) * CH)
-            blocks.append(jnp.concatenate([x[:, lanes] for x in wide], axis=1).astype(BF16))
+            line = jnp.concatenate([x[:, lanes] for x in wide], axis=1).astype(BF16)
+            first = (2 * hi + side) * 4 * CH
+            if share_rows >= 4 * CH:
+                at = first % share_rows
+                block_scr[first // share_rows, :, pl.ds(at, 4 * CH)] = line
+            else:
+                for at in range(0, 4 * CH, share_rows):
+                    block_scr[(first + at) // share_rows] = line[:, at : at + share_rows]
     for copy in copies:
         copy.wait()
     embedded = pos_ref[...].astype(F32)
-    for ty in range(4):
-        embedded = embedded + mm(blocks[ty], position_rows(ty))
+    for number, ref, slot in shares:
+        embedded = embedded + mm(block_scr[number], ref[slot])
     pre = pre_ref[...].reshape(1, VW)
     post = post_ref[...].reshape(1, VW)
     prompt = prompt_ref[...]
@@ -431,14 +433,17 @@
     high = embed_grad.astype(BF16)
     low = (embed_grad - high.astype(F32)).astype(BF16)
     stacked = jnp.concatenate([high, low], axis=0)
+    for number, ref, slot in shares:
+        both = mm_nt(stacked, ref[slot])
+        back_scr[number] = both[:patches] + both[patches:]
+    back = jnp.concatenate([back_scr[i] for i in range(16 * CH // share_rows)], axis=1)
     for hi in range(2):
-        sides = []
-        for side in range(2):
-            both = mm_nt(stacked, position_rows(2 * hi + side))
-            sides.append(both[:patches] + both[patches:])
         for tx in range(4):
-            lanes = slice(tx * CH, (tx + 1) * CH)
-            piece = jnp.concatenate([sides[0][:, lanes], sides[1][:, lanes]], axis=1)
+            first = (4 * (2 * hi) + tx) * CH
+            second = (4 * (2 * hi + 1) + tx) * CH
+            piece = jnp.concatenate(
+                [back[:, first : first + CH], back[:, second : second + CH]], axis=1
+            )
             for pr in range(patch_rows):
                 grad_scr[pl.ds((2 * pr + hi) * GW + tx, patch_cols, stride=4), :] = piece[
                     pr * patch_cols : (pr + 1) * patch_cols
@@ -468,6 +473,7 @@
     rows = grid_rows * GW // 2
     width = modulated.shape[2]
     embed_arrays, embed_masks = [x for x, _ in embed], [masks for _, masks in embed]
+    share_rows = embed_arrays[0].shape[1]
     return pl.pallas_call(
         functools.partial(head_kernel, grid_rows, fused, embed_masks, out_factor),
         out_shape=(
@@ -476,19 +482,19 @@
             jax.ShapeDtypeStruct((CH, width), BF16),
         ),
         in_specs=[SMEM_SPEC, VMEM_SPEC]
-        + [ANY_SPEC] * len(embed_arrays)
+        + [VMEM_SPEC] * len(embed_arrays)
         + [HBM_SPEC] * 4
         + [SMEM_SPEC, VMEM_SPEC],
         out_specs=(VMEM_SPEC, VMEM_SPEC, VMEM_SPEC),
         scratch_shapes=[
             pltpu.VMEM((rows, 2 * CH), F32),
             pltpu.VMEM((rows, 2 * CH), F32),
-            pltpu.VMEM((16 * CH, VW), BF16),
+            pltpu.VMEM((16 * CH // share_rows, patches, share_rows), BF16),
+            pltpu.VMEM((16 * CH // share_rows, patches, share_rows), F32),
             pltpu.VMEM((patches, VW), BF16),
             pltpu.VMEM((VW,), F32),
             pltpu.VMEM((VW,), F32),
             pltpu.VMEM((1, VW), F32),
-            pltpu.SemaphoreType.DMA((sum(len(masks) for masks in embed_masks),)),
             pltpu.SemaphoreType.DMA((4,)),
         ],
         compiler_params=limits(16),
@@ -631,7 +637,7 @@
 
     masks = sizes.pieces()
     packed = pack(
-        sizes, place, in_hbm(queries), in_hbm(keys), in_hbm(values), in_hbm(patch_embed)
+        sizes, in_hbm(queries), in_hbm(keys), in_hbm(values), in_hbm(patch_embed)
     )
     received = [swap(x, "seq", mask) if mask else x for mask, x in zip(masks, packed)]
     bits = [1 << b for b in reversed(range(data_count.bit_length() - 1))]
@@ -647,13 +653,11 @@
             (swap(held, "dp", bits[0]), swap_both(held, 1, bits[0])),
         ]
 
-    modulated, latent_part, token = attend(
+    modulated, latent_part = attend(
         sizes, masks, place, received, in_hbm(scales), in_hbm(shifts), in_hbm(proj_turned)
     )
 
-    if sizes.riding:
-        embed = [(arrange(sizes, ride_masks, place, pairs, token), [0, bits[0]])]
-    else:
+    if not sizes.riding:
         mine = patch_embed
         if shared:
             mine = lax.dynamic_slice_in_dim(
@@ -669,9 +673,12 @@
         groups = [[g * query_parts + r for g in range(group_count)] for r in range(query_parts)]
     per_share = seq_count // group_count
     parts = all_to_all(latent_part.reshape(group_count, per_share * half, 2 * CH), groups)
+    summed = total_copies([parts], seq_count)
+    if sizes.riding:
+        embed = [(arrange(sizes, ride_masks, place, pairs, summed), [0, bits[0]])]
     for bit in bits[1:] if shared else []:
         embed = embed + [(swap(x, "dp", bit), [m ^ bit for m in some]) for x, some in embed]
-    latent = all_to_all(total_copies([parts], seq_count))
+    latent = all_to_all(summed)
     if canonical:
         latent = latent.reshape(lat_rows // 2, 2 * CH)
     else:

time: 112 us -> 106 us (0.946)
  waiting for transfers between devices: 43.2 us -> 39.3 us
    ppermute x14, waiting for transfers between devices: 29.4 us -> 25 us  [swap(): return lax.ppermute(x, axis, [(i, i ^ mask) for i in range(count)])]
  transfers between devices with their start and end apart: 17 -> 17, of which waited for: 12 -> 10; matrix products, arithmetic and copies ran while one was open for 0% -> 0% of each run, Pallas kernels for 11% -> 12%
where the time goes in v9:
time: 106 us
  waiting for transfers between devices  39.3 us (37%)
  starting transfers between devices  26.4 us (25%)
  Pallas kernels  21.2 us (20%)
  blocking collectives  17.2 us (16%)
  between operations  1.37 us (1%)
    ppermute x14, waiting for transfers between devices, swap(): return lax.ppermute(x, axis, [(i, i ^ mask) for i in range(count)])  25 us
    ppermute x14, starting transfers between devices, swap(): return lax.ppermute(x, axis, [(i, i ^ mask) for i in range(count)])  18.1 us
    all_to_all x1, blocking collectives, all_to_all(): lax.all_to_all(x, 'seq', split_axis=0, concat_axis=0, tiled=True, axis_in...  17.2 us
    all_to_all x2, waiting for transfers between devices, all_to_all(): lax.all_to_all(x, 'seq', split_axis=0, concat_axis=0, tiled=True, axis_in...  14.2 us
    pallas_call x1, Pallas kernels, attend(): pl.pallas_call(functools.partial(attend_kernel, sizes, masks), out_shape=...  9.13 us
    all_to_all x2, starting transfers between devices, all_to_all(): lax.all_to_all(x, 'seq', split_axis=0, concat_axis=0, tiled=True, axis_in...  6.8 us
    pallas_call x1, Pallas kernels, reward_head(): pl.pallas_call(functools.partial(head_kernel, grid_rows, fused, embed_mas...  4.19 us
    pallas_call x1, Pallas kernels, spread(): pl.pallas_call(functools.partial(spread_kernel, count, half, heads), out_...  2.41 us
  transfers between devices with their start and end apart: 17, of which 10 were waited for; matrix products, arithmetic and copies ran while one was open for 0% of the time, Pallas kernels for 12%

profile of v9, /device:TPU:0, one launch (start us, length us, event | category | flops | bytes accessed | tf_op | source)
XLA Modules:
  0.0 105.6 jit_solution(8133993579971413171)
XLA Ops:
  0.6 1.9 %shard_map.139 = (bf16[384,256]{1,0:T(8,128)(2,1)S(1)}, bf16[384,256]{1,0:T(8,128)(2,1)S(1)}, bf16[384,256]{1,0:T(8,128)(2,1)S(1)}, bf16[544,256]{1,0:T(8,128)(2...) custom-call(bf16[1,128,2048]{2,1,0:T(8,128)(2,1)} %q_ref.1, ...), custom_call_target="tpu_custom_call" | custom-call | bytes 3145728 | tf_op jit(solution)/shard_map/pallas_call | solution.py:136
  2.6 4.1 %collective-permute-start.3 = (bf16[544,256]{1,0:T(8,128)(2,1)S(1)}, bf16[544,256]{1,0:T(8,128)(2,1)S(1)}, u32[]{:S(2)}, u32[]{:S(2)}) collective-permute-start(bf16[544,256]{1,0:T(8,128)(2,1)S(1)} %get-tuple-element.19), channel_id=1, source_target_pairs={{0,16},{4,20},{8,24},{12,28},{16,0},{20,4},{24,8},{28,12},{1,17},{... | collective-permute-start | bytes 835592 | tf_op jit(solution)/shard_map/ppermute | solution.py:588
  6.7 1.5 %collective-permute-start = (bf16[384,256]{1,0:T(8,128)(2,1)S(1)}, bf16[384,256]{1,0:T(8,128)(2,1)S(1)}, u32[]{:S(2)}, u32[]{:S(2)}) collective-permute-start(bf16[384,256]{1,0:T(8,128)(2,1)S(1)} %get-tuple-element.16), channel_id=1, source_target_pairs={{0,4},{4,0},{8,12},{12,8},{16,20},{20,16},{24,28},{28,24},{1,5},{5... | collective-permute-start | bytes 589832 | tf_op jit(solution)/shard_map/ppermute | solution.py:588
  8.2 1.6 %collective-permute-start.1 = (bf16[384,256]{1,0:T(8,128)(2,1)S(1)}, bf16[384,256]{1,0:T(8,128)(2,1)S(1)}, u32[]{:S(2)}, u32[]{:S(2)}) collective-permute-start(bf16[384,256]{1,0:T(8,128)(2,1)S(1)} %get-tuple-element.17), channel_id=1, source_target_pairs={{0,8},{4,12},{8,0},{12,4},{16,24},{20,28},{24,16},{28,20},{1,9},{5... | collective-permute-start | bytes 589832 | tf_op jit(solution)/shard_map/ppermute | solution.py:588
  10.2 1.3 %collective-permute-start.4 = (bf16[384,256]{1,0:T(8,128)(2,1)S(1)}, bf16[384,256]{1,0:T(8,128)(2,1)S(1)}, u32[]{:S(2)}, u32[]{:S(2)}) collective-permute-start(bf16[384,256]{1,0:T(8,128)(2,1)S(1)} %get-tuple-element.20), channel_id=1, source_target_pairs={{0,20},{4,16},{8,28},{12,24},{16,4},{20,0},{24,12},{28,8},{1,21},{... | collective-permute-start | bytes 589832 | tf_op jit(solution)/shard_map/ppermute | solution.py:588
  11.5 2.2 %collective-permute-done.refs_0_ = bf16[384,256]{1,0:T(8,128)(2,1)S(1)} collective-permute-done((bf16[384,256]{1,0:T(8,128)(2,1)S(1)}, bf16[384,256]{1,0:T(8,128)(2,1)S(1)}, u32[]{:S(2)}, u32[]{:S(2)}) %collective-permute-start) | collective-permute-done | bytes 196640 | tf_op jit(solution)/shard_map/ppermute | solution.py:588
  13.6 1.4 %collective-permute-start.5 = (bf16[384,256]{1,0:T(8,128)(2,1)S(1)}, bf16[384,256]{1,0:T(8,128)(2,1)S(1)}, u32[]{:S(2)}, u32[]{:S(2)}) collective-permute-start(bf16[384,256]{1,0:T(8,128)(2,1)S(1)} %get-tuple-element.21), channel_id=1, source_target_pairs={{0,24},{4,28},{8,16},{12,20},{16,8},{20,12},{24,0},{28,4},{1,25},{... | collective-permute-start | bytes 589832 | tf_op jit(solution)/shard_map/ppermute | solution.py:588
  15.1 5.2 %collective-permute-done.3.refs_3_.refs_0_ = bf16[544,256]{1,0:T(8,128)(2,1)S(1)} collective-permute-done((bf16[544,256]{1,0:T(8,128)(2,1)S(1)}, bf16[544,256]{1,0:T(8,128)(2,1)S(1)}, u32[]{:S(2)}, u32[]{:S(2)}) %collective-permute-start.3) | collective-permute-done | bytes 278560 | tf_op jit(solution)/shard_map/ppermute | solution.py:588
  20.2 3.8 %collective-permute-start.6 = (bf16[384,256]{1,0:T(8,128)(2,1)S(1)}, bf16[384,256]{1,0:T(8,128)(2,1)S(1)}, u32[]{:S(2)}, u32[]{:S(2)}) collective-permute-start(bf16[384,256]{1,0:T(8,128)(2,1)S(1)} %get-tuple-element.22), channel_id=1, source_target_pairs={{0,28},{4,24},{8,20},{12,16},{16,12},{20,8},{24,4},{28,0},{1,29},{... | collective-permute-start | bytes 589832 | tf_op jit(solution)/shard_map/ppermute | solution.py:588
  24.4 2.5 %collective-permute-done.2.refs_2_ = bf16[384,256]{1,0:T(8,128)(2,1)S(1)} collective-permute-done((bf16[384,256]{1,0:T(8,128)(2,1)S(1)}, bf16[384,256]{1,0:T(8,128)(2,1)S(1)}, u32[]{:S(2)}, u32[]{:S(2)}) %collective-permute-start.2) | collective-permute-done | bytes 196640 | tf_op jit(solution)/shard_map/ppermute | solution.py:588
  26.9 11.5 %collective-permute-done.4.refs_4_ = bf16[384,256]{1,0:T(8,128)(2,1)S(1)} collective-permute-done((bf16[384,256]{1,0:T(8,128)(2,1)S(1)}, bf16[384,256]{1,0:T(8,128)(2,1)S(1)}, u32[]{:S(2)}, u32[]{:S(2)}) %collective-permute-start.4) | collective-permute-done | bytes 196640 | tf_op jit(solution)/shard_map/ppermute | solution.py:588
  39.5 1.5 %collective-permute-start.10 = (bf16[4,320,128]{2,1,0:T(8,128)(2,1)S(1)}, bf16[4,320,128]{2,1,0:T(8,128)(2,1)S(1)}, u32[]{:S(2)}, u32[]{:S(2)}) collective-permute-start(bf16[4,320,128]{2,1,0:T(8,128)(2,1)S(1)} %shard_map.143.refs_0_), channel_id=1, source_target_pairs={{0,6},{1,7},{2,4},{3,5},{4,2},{5,3},{6,0},{7,1},{8,14},{9,15},{10,... | collective-permute-start | bytes 983048 | tf_op jit(solution)/shard_map/ppermute | solution.py:604
  41.6 1.5 %collective-permute-start.8 = (bf16[4,320,128]{2,1,0:T(8,128)(2,1)S(1)}, bf16[4,320,128]{2,1,0:T(8,128)(2,1)S(1)}, u32[]{:S(2)}, u32[]{:S(2)}) collective-permute-start(bf16[4,320,128]{2,1,0:T(8,128)(2,1)S(1)} %shard_map.143.refs_0_), channel_id=1, source_target_pairs={{0,4},{4,0},{8,12},{12,8},{16,20},{20,16},{24,28},{28,24},{1,5},{5... | collective-permute-start | bytes 983048 | tf_op jit(solution)/shard_map/ppermute | solution.py:588
  43.0 9.1 %shard_map.140 = (bf16[8,128,256]{2,1,0:T(8,128)(2,1)S(1)}, bf16[8,64,128]{2,1,0:T(8,128)(2,1)S(1)}) custom-call(s32[3]{0:T(128)S(1)} %pad_add_fusion.place_ref, bf16[384,256]{1,0:T(8,128)(2,1)S(1)} %collective-permute-done.refs_0_, bf16[384,256]{1,0:T(8,128)(2,1)S(1)} %collective-permute-done.1.refs_1_, ...), custom_call_target="tpu_custom_call" | custom-call | flops 1073741824 | bytes 2097152 | tf_op jit(solution)/shard_map/pallas_call | solution.py:305
  52.2 17.2 %all_to_all.15.refs_0_ = bf16[8,64,128]{2,1,0:T(8,128)(2,1)S(1)} all-to-all(bf16[8,64,128]{2,1,0:T(8,128)(2,1)S(1)} %get-tuple-element.24), channel_id=1, replica_groups=mesh['seq'=8,'dp'=4] {'seq'}, dimensions={0} | all-to-all | bytes 262144 | tf_op jit(solution)/shard_map/all_to_all | solution.py:592
  70.1 1.2 %shard_map.144.refs_0_ = bf16[2,256,1280]{2,1,0:T(8,128)(2,1)S(1)} custom-call(s32[3]{0:T(128)S(1)} %pad_add_fusion.place_ref, bf16[4,320,128]{2,1,0:T(8,128)(2,1)S(1)} %shard_map.143.refs_0_, bf16[4,320,128]{2,1,0:T(8,128)(2,1)S(1)} %collective-permute-done.8.refs_1_, bf16[4,320,128]{2,1,0:T(8,128)(2,1)S(1)} %collective-permute-done.9.refs_2_, ...), custom_call_target="tpu_custom_call" | custom-call | tf_op jit(solution)/shard_map/pallas_call | solution.py:224
  71.4 3.4 %all-to-all-start.1 = ((bf16[8,64,128]{2,1,0:T(8,128)(2,1)}), bf16[8,64,128]{2,1,0:T(8,128)(2,1)S(1)}, u32[]{:S(2)}, u32[]{:S(2)}) async-start(bf16[8,64,128]{2,1,0:T(8,128)(2,1)} %shard_map.141.refs_4_), calls=%async_computation.1 | async-start | bytes 262144 | tf_op jit(solution)/shard_map/all_to_all | solution.py:592
  75.4 7.2 %all-to-all-done.1 = bf16[8,64,128]{2,1,0:T(8,128)(2,1)S(1)} async-done(((bf16[8,64,128]{2,1,0:T(8,128)(2,1)}), bf16[8,64,128]{2,1,0:T(8,128)(2,1)S(1)}, u32[]{:S(2)}, u32[]{:S(2)}) %all-to-all-start.1) | async-done | bytes 131104 | tf_op jit(solution)/shard_map/all_to_all | solution.py:592
  82.7 4.2 %shard_map.145 = (f32[1,128]{1,0:T(1,128)}, bf16[512,128]{1,0:T(8,128)(2,1)S(1)}, bf16[64,256]{1,0:T(8,128)(2,1)S(1)}) custom-call(s32[3]{0:T(128)S(1)} %pad_add_fusion.place_ref, bf16[512,128]{1,0:T(8,128)(2,1)S(1)} %bitcast.7, bf16[2,256,1280]{2,1,0:T(8,128)(2,1)S(1)} %shard_map.144.refs_0_, bf16[2,256,1280]{2,1,0:T(8,128)(2,1)S(1)} %collective-permute-done.11.refs_1_, ...), custom_call_target="tpu_custom_call" | custom-call | flops 503316480 | bytes 2785280 | tf_op jit(solution)/shard_map/pallas_call | solution.py:477
  87.2 1.2 %collective-permute-start.13 = (bf16[64,256]{1,0:T(8,128)(2,1)S(1)}, bf16[64,256]{1,0:T(8,128)(2,1)S(1)}, u32[]{:S(2)}, u32[]{:S(2)}) collective-permute-start(bf16[64,256]{1,0:T(8,128)(2,1)S(1)} %get-tuple-element.28.refs_0_), channel_id=1, source_target_pairs={{0,2},{1,3},{2,0},{3,1},{4,6},{5,7},{6,4},{7,5},{8,10},{9,11},{10,... | collective-permute-start | bytes 98312 | tf_op jit(solution)/shard_map/ppermute | solution.py:588
  88.8 1.8 %collective-permute-done.14.refs_3_ = bf16[64,256]{1,0:T(8,128)(2,1)S(1)} collective-permute-done((bf16[64,256]{1,0:T(8,128)(2,1)S(1)}, bf16[64,256]{1,0:T(8,128)(2,1)S(1)}, u32[]{:S(2)}, u32[]{:S(2)}) %collective-permute-start.14) | collective-permute-done | bytes 32800 | tf_op jit(solution)/shard_map/ppermute | solution.py:588
  91.9 3.4 %all-to-all-start.2 = ((bf16[8,64,256]{2,1,0:T(8,128)(2,1)}), bf16[8,64,256]{2,1,0:T(8,128)(2,1)S(1)}, u32[]{:S(2)}, u32[]{:S(2)}) async-start(bf16[8,64,256]{2,1,0:T(8,128)(2,1)} %shard_map.147), calls=%async_computation.2 | async-start | bytes 524288 | tf_op jit(solution)/shard_map/all_to_all | solution.py:592
  95.3 2.4 %shard_map.146 = bf16[1,2,1024,128]{3,2,1,0:T(8,128)(2,1)} custom-call(s32[3]{0:T(128)S(1)} %pad_add_fusion.place_ref, bf16[512,128]{1,0:T(8,128)(2,1)S(1)} %get-tuple-element.27.grad_ref, f32[1,2048]{1,0:T(1,128)} %scale_ref.1, bf16[64,2048]{1,0:T(8,128)(2,1)} %bitcast.10), custom_call_target="tpu_custom_call" | custom-call | flops 67108864 | bytes 524288 | tf_op jit(solution)/shard_map/pallas_call | solution.py:537
  97.8 7.0 %all-to-all-done.2.in_ref = bf16[8,64,256]{2,1,0:T(8,128)(2,1)S(1)} async-done(((bf16[8,64,256]{2,1,0:T(8,128)(2,1)}), bf16[8,64,256]{2,1,0:T(8,128)(2,1)S(1)}, u32[]{:S(2)}, u32[]{:S(2)}) %all-to-all-start.2) | async-done | bytes 262176 | tf_op jit(solution)/shard_map/all_to_all | solution.py:592
  (22 shorter events, 6.1 us)
Async XLA Ops:
  2.6 17.7 %collective-permute-start.3 = (bf16[544,256]{1,0:T(8,128)(2,1)S(1)}, bf16[544,256]{1,0:T(8,128)(2,1)S(1)}, u32[]{:S(2)}, u32[]{:S(2)}) collective-permute-start(bf16[544,256]{1,0:T(8,128)(2,1)S(1)} %get-tuple-element.19), channel_id=1, source_target_pairs={{0,16},{4,20},{8,24},{12,28},{16,0},{20,4},{24,8},{28,12},{1,17},{... | collective-permute-start | bytes 835592 | tf_op jit(solution)/shard_map/ppermute | solution.py:588
  6.7 6.9 %collective-permute-start = (bf16[384,256]{1,0:T(8,128)(2,1)S(1)}, bf16[384,256]{1,0:T(8,128)(2,1)S(1)}, u32[]{:S(2)}, u32[]{:S(2)}) collective-permute-start(bf16[384,256]{1,0:T(8,128)(2,1)S(1)} %get-tuple-element.16), channel_id=1, source_target_pairs={{0,4},{4,0},{8,12},{12,8},{16,20},{20,16},{24,28},{28,24},{1,5},{5... | collective-permute-start | bytes 589832 | tf_op jit(solution)/shard_map/ppermute | solution.py:588
  8.2 16.1 %collective-permute-start.1 = (bf16[384,256]{1,0:T(8,128)(2,1)S(1)}, bf16[384,256]{1,0:T(8,128)(2,1)S(1)}, u32[]{:S(2)}, u32[]{:S(2)}) collective-permute-start(bf16[384,256]{1,0:T(8,128)(2,1)S(1)} %get-tuple-element.17), channel_id=1, source_target_pairs={{0,8},{4,12},{8,0},{12,4},{16,24},{20,28},{24,16},{28,20},{1,9},{5... | collective-permute-start | bytes 589832 | tf_op jit(solution)/shard_map/ppermute | solution.py:588
  9.8 17.1 %collective-permute-start.2 = (bf16[384,256]{1,0:T(8,128)(2,1)S(1)}, bf16[384,256]{1,0:T(8,128)(2,1)S(1)}, u32[]{:S(2)}, u32[]{:S(2)}) collective-permute-start(bf16[384,256]{1,0:T(8,128)(2,1)S(1)} %get-tuple-element.18), channel_id=1, source_target_pairs={{0,12},{4,8},{8,4},{12,0},{16,28},{20,24},{24,20},{28,16},{1,13},{... | collective-permute-start | bytes 589832 | tf_op jit(solution)/shard_map/ppermute | solution.py:588
  10.2 28.2 %collective-permute-start.4 = (bf16[384,256]{1,0:T(8,128)(2,1)S(1)}, bf16[384,256]{1,0:T(8,128)(2,1)S(1)}, u32[]{:S(2)}, u32[]{:S(2)}) collective-permute-start(bf16[384,256]{1,0:T(8,128)(2,1)S(1)} %get-tuple-element.20), channel_id=1, source_target_pairs={{0,20},{4,16},{8,28},{12,24},{16,4},{20,0},{24,12},{28,8},{1,21},{... | collective-permute-start | bytes 589832 | tf_op jit(solution)/shard_map/ppermute | solution.py:588
  13.6 24.8 %collective-permute-start.5 = (bf16[384,256]{1,0:T(8,128)(2,1)S(1)}, bf16[384,256]{1,0:T(8,128)(2,1)S(1)}, u32[]{:S(2)}, u32[]{:S(2)}) collective-permute-start(bf16[384,256]{1,0:T(8,128)(2,1)S(1)} %get-tuple-element.21), channel_id=1, source_target_pairs={{0,24},{4,28},{8,16},{12,20},{16,8},{20,12},{24,0},{28,4},{1,25},{... | collective-permute-start | bytes 589832 | tf_op jit(solution)/shard_map/ppermute | solution.py:588
  20.2 18.1 %collective-permute-start.6 = (bf16[384,256]{1,0:T(8,128)(2,1)S(1)}, bf16[384,256]{1,0:T(8,128)(2,1)S(1)}, u32[]{:S(2)}, u32[]{:S(2)}) collective-permute-start(bf16[384,256]{1,0:T(8,128)(2,1)S(1)} %get-tuple-element.22), channel_id=1, source_target_pairs={{0,28},{4,24},{8,20},{12,16},{16,12},{20,8},{24,4},{28,0},{1,29},{... | collective-permute-start | bytes 589832 | tf_op jit(solution)/shard_map/ppermute | solution.py:588
  24.3 15.1 %collective-permute-start.7 = (bf16[2,320,128]{2,1,0:T(8,128)(2,1)S(1)}, bf16[2,320,128]{2,1,0:T(8,128)(2,1)S(1)}, u32[]{:S(2)}, u32[]{:S(2)}) collective-permute-start(bf16[2,320,128]{2,1,0:T(8,128)(2,1)S(1)} %shard_map.142.first_ref), channel_id=1, source_target_pairs={{0,8},{4,12},{8,0},{12,4},{16,24},{20,28},{24,16},{28,20},{1,9},{5... | collective-permute-start | bytes 491528 | tf_op jit(solution)/shard_map/ppermute | solution.py:588
  39.5 30.6 %collective-permute-start.10 = (bf16[4,320,128]{2,1,0:T(8,128)(2,1)S(1)}, bf16[4,320,128]{2,1,0:T(8,128)(2,1)S(1)}, u32[]{:S(2)}, u32[]{:S(2)}) collective-permute-start(bf16[4,320,128]{2,1,0:T(8,128)(2,1)S(1)} %shard_map.143.refs_0_), channel_id=1, source_target_pairs={{0,6},{1,7},{2,4},{3,5},{4,2},{5,3},{6,0},{7,1},{8,14},{9,15},{10,... | collective-permute-start | bytes 983048 | tf_op jit(solution)/shard_map/ppermute | solution.py:604
  41.0 29.1 %collective-permute-start.9 = (bf16[4,320,128]{2,1,0:T(8,128)(2,1)S(1)}, bf16[4,320,128]{2,1,0:T(8,128)(2,1)S(1)}, u32[]{:S(2)}, u32[]{:S(2)}) collective-permute-start(bf16[4,320,128]{2,1,0:T(8,128)(2,1)S(1)} %shard_map.143.refs_0_), channel_id=1, source_target_pairs={{0,2},{1,3},{2,0},{3,1},{4,6},{5,7},{6,4},{7,5},{8,10},{9,11},{10,... | collective-permute-start | bytes 983048 | tf_op jit(solution)/shard_map/ppermute | solution.py:588
  41.6 28.5 %collective-permute-start.8 = (bf16[4,320,128]{2,1,0:T(8,128)(2,1)S(1)}, bf16[4,320,128]{2,1,0:T(8,128)(2,1)S(1)}, u32[]{:S(2)}, u32[]{:S(2)}) collective-permute-start(bf16[4,320,128]{2,1,0:T(8,128)(2,1)S(1)} %shard_map.143.refs_0_), channel_id=1, source_target_pairs={{0,4},{4,0},{8,12},{12,8},{16,20},{20,16},{24,28},{28,24},{1,5},{5... | collective-permute-start | bytes 983048 | tf_op jit(solution)/shard_map/ppermute | solution.py:588
  71.3 11.3 %collective-permute-start.11 = (bf16[2,256,1280]{2,1,0:T(8,128)(2,1)S(1)}, bf16[2,256,1280]{2,1,0:T(8,128)(2,1)S(1)}, u32[]{:S(2)}, u32[]{:S(2)}) collective-permute-start(bf16[2,256,1280]{2,1,0:T(8,128)(2,1)S(1)} %shard_map.144.refs_0_), channel_id=1, source_target_pairs={{0,1},{1,0},{2,3},{3,2},{4,5},{5,4},{6,7},{7,6},{8,9},{9,8},{10,11... | collective-permute-start | bytes 3932168 | tf_op jit(solution)/shard_map/ppermute | solution.py:588
  71.4 11.2 %all-to-all-start.1 = ((bf16[8,64,128]{2,1,0:T(8,128)(2,1)}), bf16[8,64,128]{2,1,0:T(8,128)(2,1)S(1)}, u32[]{:S(2)}, u32[]{:S(2)}) async-start(bf16[8,64,128]{2,1,0:T(8,128)(2,1)} %shard_map.141.refs_4_), calls=%async_computation.1 | async-start | bytes 262144 | tf_op jit(solution)/shard_map/all_to_all | solution.py:592
  86.9 3.7 %collective-permute-start.14 = (bf16[64,256]{1,0:T(8,128)(2,1)S(1)}, bf16[64,256]{1,0:T(8,128)(2,1)S(1)}, u32[]{:S(2)}, u32[]{:S(2)}) collective-permute-start(bf16[64,256]{1,0:T(8,128)(2,1)S(1)} %get-tuple-element.28.refs_0_), channel_id=1, source_target_pairs={{0,3},{1,2},{2,1},{3,0},{4,7},{5,6},{6,5},{7,4},{8,11},{9,10},{10,... | collective-permute-start | bytes 98312 | tf_op jit(solution)/shard_map/ppermute | solution.py:588
  87.2 4.0 %collective-permute-start.13 = (bf16[64,256]{1,0:T(8,128)(2,1)S(1)}, bf16[64,256]{1,0:T(8,128)(2,1)S(1)}, u32[]{:S(2)}, u32[]{:S(2)}) collective-permute-start(bf16[64,256]{1,0:T(8,128)(2,1)S(1)} %get-tuple-element.28.refs_0_), channel_id=1, source_target_pairs={{0,2},{1,3},{2,0},{3,1},{4,6},{5,7},{6,4},{7,5},{8,10},{9,11},{10,... | collective-permute-start | bytes 98312 | tf_op jit(solution)/shard_map/ppermute | solution.py:588
  88.5 2.7 %collective-permute-start.12 = (bf16[64,256]{1,0:T(8,128)(2,1)S(1)}, bf16[64,256]{1,0:T(8,128)(2,1)S(1)}, u32[]{:S(2)}, u32[]{:S(2)}) collective-permute-start(bf16[64,256]{1,0:T(8,128)(2,1)S(1)} %get-tuple-element.28.refs_0_), channel_id=1, source_target_pairs={{0,1},{1,0},{2,3},{3,2},{4,5},{5,4},{6,7},{7,6},{8,9},{9,8},{10,11... | collective-permute-start | bytes 98312 | tf_op jit(solution)/shard_map/ppermute | solution.py:588
  91.9 12.9 %all-to-all-start.2 = ((bf16[8,64,256]{2,1,0:T(8,128)(2,1)}), bf16[8,64,256]{2,1,0:T(8,128)(2,1)S(1)}, u32[]{:S(2)}, u32[]{:S(2)}) async-start(bf16[8,64,256]{2,1,0:T(8,128)(2,1)} %shard_map.147), calls=%async_computation.2 | async-start | bytes 524288 | tf_op jit(solution)/shard_map/all_to_all | solution.py:592

commit v10 on v9

--- a/solution.py
+++ b/solution.py
@@ -230,44 +230,114 @@
     )(place, *flat, wait)
 
 
-def attend_kernel(sizes, masks, place_ref, *refs):
-    count, heads, width = sizes.count, sizes.heads, sizes.width
+FACTOR = HD ** (-0.5) * math.log2(math.e)
+
+
+def load_pieces(sizes, in_refs, query_scr, key_scr, value_scr, sems):
     tok_rows, part_rows = sizes.tok_rows, sizes.part_rows
-    in_refs, refs = refs[:count], refs[count:]
-    scale_ref, shift_ref, proj_ref, mod_ref, lat_ref, *refs = refs
-    query_scr, key_scr, value_scr, scale_scr, shift_scr, proj_scr, sems, side_sems = refs
-    half = part_rows // 2
-    factor = HD ** (-0.5) * math.log2(math.e)
-    me = place_ref[0]
-    mine = pl.ds(pl.multiple_of(place_ref[2] * width, HD), width)
-    logit_copies, value_copies = [], []
+    copies = []
     for src, ref in enumerate(in_refs):
         rows = pl.ds(src * tok_rows, tok_rows)
-        logit_copies += [
+        copies += [
             pltpu.make_async_copy(ref.at[pl.ds(0, part_rows)], query_scr.at[src], sems.at[0, src]),
             pltpu.make_async_copy(
                 ref.at[pl.ds(part_rows, tok_rows)], key_scr.at[rows], sems.at[1, src]
             ),
         ]
-        for head in range(heads):
-            value_copies.append(
+        for head in range(sizes.heads):
+            copies.append(
                 pltpu.make_async_copy(
                     ref.at[pl.ds(part_rows + tok_rows, tok_rows), pl.ds(head * HD, HD)],
                     value_scr.at[rows, pl.ds(2 * head * HD, HD)],
                     sems.at[2 + head, src],
                 )
             )
-    value_copies += [
+    for copy in copies:
+        copy.start()
+    ones = jnp.ones((len(in_refs) * tok_rows, HD), BF16)
+    for head in range(sizes.heads):
+        value_scr[:, pl.ds((2 * head + 1) * HD, HD)] = ones
+    return copies
+
+
+def soft_part(query, key_scr, value_scr, rows, head, before):
+    logits = mm_nt(query, key_scr[rows, pl.ds(head * HD, HD)])
+    top = jnp.max(logits, axis=-1, keepdims=True)
+    if before:
+        top = jnp.maximum(top, before[2])
+    weights = jnp.exp2((logits - top) * FACTOR).astype(BF16)
+    both = mm(weights, value_scr[rows, pl.ds(2 * head * HD, 2 * HD)])
+    mixed, total = both[:, :HD], both[:, HD:]
+    if before:
+        shrink = jnp.exp2((before[2] - top) * FACTOR)
+        mixed, total = mixed + before[0] * shrink, total + before[1] * shrink
+    return mixed, total, top
+
+
+def piece_scratch(sizes, count):
+    lat_rows = count * sizes.tok_rows
+    return [
+        pltpu.VMEM((count, sizes.part_rows, sizes.width), BF16),
+        pltpu.VMEM((lat_rows, sizes.width), BF16),
+        pltpu.VMEM((lat_rows, 2 * sizes.width), BF16),
+        pltpu.SemaphoreType.DMA((2 + sizes.heads, count)),
+    ]
+
+
+def early_kernel(sizes, count, *refs):
+    in_refs, refs = refs[:count], refs[count:]
+    sum_ref, stat_ref, query_scr, key_scr, value_scr, sems = refs
+    for copy in load_pieces(sizes, in_refs, query_scr, key_scr, value_scr, sems):
+        copy.wait()
+    left = lax.broadcasted_iota(jnp.int32, (sizes.part_rows, HD), 1) < HD // 2
+    rows = pl.ds(0, count * sizes.tok_rows)
+    for src in range(count):
+        results = [
+            soft_part(
+                query_scr[src, :, pl.ds(head * HD, HD)], key_scr, value_scr, rows, head, None
+            )
+            for head in range(sizes.heads)
+        ]
+        for head, (mixed, total, top) in enumerate(results):
+            sum_ref[src, head] = mixed
+            stat_ref[src, head] = jnp.where(left, top, total)
+
+
+def attend_early(sizes, received):
+    count = len(received)
+    shape = jax.ShapeDtypeStruct((count, sizes.heads, sizes.part_rows, HD), F32)
+    return pl.pallas_call(
+        functools.partial(early_kernel, sizes, count),
+        out_shape=(shape, shape),
+        in_specs=[ANY_SPEC] * count,
+        out_specs=(VMEM_SPEC, VMEM_SPEC),
+        scratch_shapes=piece_scratch(sizes, count),
+        compiler_params=limits(12),
+        cost_estimate=pl.CostEstimate(flops=1, bytes_accessed=1, transcendentals=0),
+    )(*received)
+
+
+def attend_kernel(sizes, masks, early, place_ref, *refs):
+    count, heads, width = sizes.count, sizes.heads, sizes.width
+    tok_rows, part_rows = sizes.tok_rows, sizes.part_rows
+    in_refs, refs = refs[:count], refs[count:]
+    kept_refs, refs = refs[: 2 if early else 0], refs[2 if early else 0 :]
+    scale_ref, shift_ref, proj_ref, mod_ref, lat_ref, *refs = refs
+    query_scr, key_scr, value_scr, sems, scale_scr, shift_scr, proj_scr, side_sems, *kept_scr = refs
+    half = part_rows // 2
+    me = place_ref[0]
+    mine = pl.ds(pl.multiple_of(place_ref[2] * width, HD), width)
+    copies = load_pieces(sizes, in_refs, query_scr, key_scr, value_scr, sems)
+    others = [
         pltpu.make_async_copy(scale_ref.at[:, mine], scale_scr, side_sems.at[0]),
         pltpu.make_async_copy(shift_ref.at[:, mine], shift_scr, side_sems.at[1]),
         pltpu.make_async_copy(proj_ref.at[:, mine], proj_scr, side_sems.at[2]),
     ]
-    for copy in logit_copies + value_copies:
+    for slot, (ref, scr) in enumerate(zip(kept_refs, kept_scr)):
+        others.append(pltpu.make_async_copy(ref, scr, side_sems.at[3 + slot]))
+    for copy in others:
         copy.start()
-    ones = jnp.ones((count * tok_rows, HD), BF16)
-    for head in range(heads):
-        value_scr[:, pl.ds((2 * head + 1) * HD, HD)] = ones
-    for copy in logit_copies + value_copies:
+    for copy in copies + others:
         copy.wait()
     gain = 1.0 + scale_scr[...]
     shift = shift_scr[...]
@@ -282,12 +352,15 @@
         for src in range(first, first + together):
             mixed = []
             for head in range(heads):
-                cols = pl.ds(head * HD, HD)
-                logits = mm_nt(query_scr[src, :, cols], key_scr[:, cols])
-                top = jnp.max(logits, axis=-1, keepdims=True)
-                weights = jnp.exp2((logits - top) * factor).astype(BF16)
-                both = mm(weights, value_scr[:, pl.ds(2 * head * HD, 2 * HD)])
-                mixed.append(both[:, :HD] / both[:, HD:])
+                before = None
+                rows = pl.ds(0, count * tok_rows)
+                if src < early:
+                    rows = pl.ds(early * tok_rows, (count - early) * tok_rows)
+                    stat = kept_scr[1][src, head]
+                    before = (kept_scr[0][src, head], stat[:, HD - 1 :], stat[:, :1])
+                query = query_scr[src, :, pl.ds(head * HD, HD)]
+                value, total, _ = soft_part(query, key_scr, value_scr, rows, head, before)
+                mixed.append(value / total)
             attended = jnp.concatenate(mixed, axis=1) if heads > 1 else mixed[0]
             modulated = (attended * gain + shift).astype(BF16)
             pair = jnp.concatenate([modulated[:half], modulated[half:]], axis=1)
@@ -298,35 +371,34 @@
             lat_ref[place] = latent
 
 
-def attend(sizes, masks, place, received, scales, shifts, proj):
+def attend(sizes, masks, place, received, kept, scales, shifts, proj):
     count, width, heads = sizes.count, sizes.width, sizes.heads
     lat_rows = count * sizes.tok_rows
     query_rows = count * sizes.part_rows
-    return pl.pallas_call(
-        functools.partial(attend_kernel, sizes, masks),
+    early = kept[0].shape[0] if kept else 0
+    return pl.pallas_call(
+        functools.partial(attend_kernel, sizes, masks, early),
         out_shape=(
             jax.ShapeDtypeStruct((count, sizes.part_rows, width), BF16),
             jax.ShapeDtypeStruct((count, sizes.part_rows // 2, 2 * CH), BF16),
         ),
-        in_specs=[SMEM_SPEC] + [ANY_SPEC] * count + [HBM_SPEC] * 3,
+        in_specs=[SMEM_SPEC] + [ANY_SPEC] * (count + len(kept)) + [HBM_SPEC] * 3,
         out_specs=(VMEM_SPEC, VMEM_SPEC),
-        scratch_shapes=[
-            pltpu.VMEM((count, sizes.part_rows, width), BF16),
-            pltpu.VMEM((lat_rows, width), BF16),
-            pltpu.VMEM((lat_rows, 2 * width), BF16),
+        scratch_shapes=piece_scratch(sizes, count)
+        + [
             pltpu.VMEM((1, width), F32),
             pltpu.VMEM((1, width), F32),
             pltpu.VMEM((CH, width), BF16),
-            pltpu.SemaphoreType.DMA((2 + heads, count)),
-            pltpu.SemaphoreType.DMA((3,)),
-        ],
+            pltpu.SemaphoreType.DMA((5,)),
+        ]
+        + [pltpu.VMEM(x.shape, F32) for x in kept],
         compiler_params=limits(16),
         cost_estimate=pl.CostEstimate(
             flops=4 * query_rows * lat_rows * width,
             bytes_accessed=2 * (query_rows * 2 + lat_rows * 2) * width,
             transcendentals=query_rows * lat_rows * heads,
         ),
-    )(place, *received, scales, shifts, proj)
+    )(place, *received, *kept, scales, shifts, proj)
 
 
 def total_kernel(copies, *refs):
@@ -653,8 +725,15 @@
             (swap(held, "dp", bits[0]), swap_both(held, 1, bits[0])),
         ]
 
+    kept, order = [], list(range(seq_count))
+    if seq_count == 8:
+        late = [slot for slot, mask in enumerate(masks) if mask in (6, 7)]
+        order = [slot for slot in order if slot not in late]
+        kept = attend_early(sizes, [received[slot] for slot in order])
+        order = order + late
     modulated, latent_part = attend(
-        sizes, masks, place, received, in_hbm(scales), in_hbm(shifts), in_hbm(proj_turned)
+        sizes, [masks[slot] for slot in order], place, [received[slot] for slot in order], kept,
+        in_hbm(scales), in_hbm(shifts), in_hbm(proj_turned)
     )
 
     if not sizes.riding:

time: 106 us -> 106 us (level)
  Pallas kernels: 21.2 us -> 23.5 us
  blocking collectives: 17.2 us -> 15.1 us
    pallas_call x1 -> x2, Pallas kernels: 9.13 us -> 11.4 us  [the longest x1 8.28 us: attend(): pl.pallas_call(functools.partial(attend_kernel, sizes, masks, early), out...]
    all_to_all x1, blocking collectives: 17.2 us -> 15.1 us  [all_to_all(): lax.all_to_all(x, 'seq', split_axis=0, concat_axis=0, tiled=True, axis_in...]
  transfers between devices with their start and end apart: 17 -> 17, of which waited for: 10 -> 9; matrix products, arithmetic and copies ran while one was open for 0% -> 0% of each run, Pallas kernels for 12% -> 14%
where the time goes in v10:
time: 106 us; the launch traced here: 105 us
  waiting for transfers between devices  38.8 us (37%)
  starting transfers between devices  26.4 us (25%)
  Pallas kernels  23.5 us (22%)
  blocking collectives  15.1 us (14%)
  between operations  1.41 us (1%)
    ppermute x14, waiting for transfers between devices, swap(): return lax.ppermute(x, axis, [(i, i ^ mask) for i in range(count)])  24.6 us
    ppermute x14, starting transfers between devices, swap(): return lax.ppermute(x, axis, [(i, i ^ mask) for i in range(count)])  18.2 us
    all_to_all x1, blocking collectives, all_to_all(): lax.all_to_all(x, 'seq', split_axis=0, concat_axis=0, tiled=True, axis_in...  15.1 us
    all_to_all x2, waiting for transfers between devices, all_to_all(): lax.all_to_all(x, 'seq', split_axis=0, concat_axis=0, tiled=True, axis_in...  14.2 us
    pallas_call x1, Pallas kernels, attend(): pl.pallas_call(functools.partial(attend_kernel, sizes, masks, early), out...  8.28 us
    all_to_all x2, starting transfers between devices, all_to_all(): lax.all_to_all(x, 'seq', split_axis=0, concat_axis=0, tiled=True, axis_in...  6.8 us
    pallas_call x1, Pallas kernels, reward_head(): pl.pallas_call(functools.partial(head_kernel, grid_rows, fused, embed_mas...  4.19 us
    pallas_call x1, Pallas kernels, attend_early(): pl.pallas_call(functools.partial(early_kernel, sizes, count), out_shape=(...  3.16 us
  transfers between devices with their start and end apart: 17, of which 9 were waited for; matrix products, arithmetic and copies ran while one was open for 0% of the time, Pallas kernels for 14%

profile of v10, /device:TPU:0, one launch (start us, length us, event | category | flops | bytes accessed | tf_op | source)
XLA Modules:
  0.0 105.4 jit_solution(3778782163764657132)
XLA Ops:
  0.6 1.9 %shard_map.139 = (bf16[384,256]{1,0:T(8,128)(2,1)S(1)}, bf16[384,256]{1,0:T(8,128)(2,1)S(1)}, bf16[384,256]{1,0:T(8,128)(2,1)S(1)}, bf16[544,256]{1,0:T(8,128)(2...) custom-call(bf16[1,128,2048]{2,1,0:T(8,128)(2,1)} %q_ref.1, ...), custom_call_target="tpu_custom_call" | custom-call | bytes 3145728 | tf_op jit(solution)/shard_map/pallas_call | solution.py:136
  2.6 4.1 %collective-permute-start.3 = (bf16[544,256]{1,0:T(8,128)(2,1)S(1)}, bf16[544,256]{1,0:T(8,128)(2,1)S(1)}, u32[]{:S(2)}, u32[]{:S(2)}) collective-permute-start(bf16[544,256]{1,0:T(8,128)(2,1)S(1)} %get-tuple-element.21), channel_id=1, source_target_pairs={{0,16},{4,20},{8,24},{12,28},{16,0},{20,4},{24,8},{28,12},{1,17},{... | collective-permute-start | bytes 835592 | tf_op jit(solution)/shard_map/ppermute | solution.py:660
  6.7 1.5 %collective-permute-start = (bf16[384,256]{1,0:T(8,128)(2,1)S(1)}, bf16[384,256]{1,0:T(8,128)(2,1)S(1)}, u32[]{:S(2)}, u32[]{:S(2)}) collective-permute-start(bf16[384,256]{1,0:T(8,128)(2,1)S(1)} %get-tuple-element.18), channel_id=1, source_target_pairs={{0,4},{4,0},{8,12},{12,8},{16,20},{20,16},{24,28},{28,24},{1,5},{5... | collective-permute-start | bytes 589832 | tf_op jit(solution)/shard_map/ppermute | solution.py:660
  8.2 1.6 %collective-permute-start.1 = (bf16[384,256]{1,0:T(8,128)(2,1)S(1)}, bf16[384,256]{1,0:T(8,128)(2,1)S(1)}, u32[]{:S(2)}, u32[]{:S(2)}) collective-permute-start(bf16[384,256]{1,0:T(8,128)(2,1)S(1)} %get-tuple-element.19), channel_id=1, source_target_pairs={{0,8},{4,12},{8,0},{12,4},{16,24},{20,28},{24,16},{28,20},{1,9},{5... | collective-permute-start | bytes 589832 | tf_op jit(solution)/shard_map/ppermute | solution.py:660
  10.2 1.3 %collective-permute-start.4 = (bf16[384,256]{1,0:T(8,128)(2,1)S(1)}, bf16[384,256]{1,0:T(8,128)(2,1)S(1)}, u32[]{:S(2)}, u32[]{:S(2)}) collective-permute-start(bf16[384,256]{1,0:T(8,128)(2,1)S(1)} %get-tuple-element.22), channel_id=1, source_target_pairs={{0,20},{4,16},{8,28},{12,24},{16,4},{20,0},{24,12},{28,8},{1,21},{... | collective-permute-start | bytes 589832 | tf_op jit(solution)/shard_map/ppermute | solution.py:660
  11.5 2.2 %collective-permute-done.refs_0_ = bf16[384,256]{1,0:T(8,128)(2,1)S(1)} collective-permute-done((bf16[384,256]{1,0:T(8,128)(2,1)S(1)}, bf16[384,256]{1,0:T(8,128)(2,1)S(1)}, u32[]{:S(2)}, u32[]{:S(2)}) %collective-permute-start) | collective-permute-done | bytes 196640 | tf_op jit(solution)/shard_map/ppermute | solution.py:660
  13.6 1.4 %collective-permute-start.5 = (bf16[384,256]{1,0:T(8,128)(2,1)S(1)}, bf16[384,256]{1,0:T(8,128)(2,1)S(1)}, u32[]{:S(2)}, u32[]{:S(2)}) collective-permute-start(bf16[384,256]{1,0:T(8,128)(2,1)S(1)} %get-tuple-element.24), channel_id=1, source_target_pairs={{0,24},{4,28},{8,16},{12,20},{16,8},{20,12},{24,0},{28,4},{1,25},{... | collective-permute-start | bytes 589832 | tf_op jit(solution)/shard_map/ppermute | solution.py:660
  15.1 5.2 %collective-permute-done.3.refs_3_.refs_0_ = bf16[544,256]{1,0:T(8,128)(2,1)S(1)} collective-permute-done((bf16[544,256]{1,0:T(8,128)(2,1)S(1)}, bf16[544,256]{1,0:T(8,128)(2,1)S(1)}, u32[]{:S(2)}, u32[]{:S(2)}) %collective-permute-start.3) | collective-permute-done | bytes 278560 | tf_op jit(solution)/shard_map/ppermute | solution.py:660
  20.2 3.8 %collective-permute-start.6 = (bf16[384,256]{1,0:T(8,128)(2,1)S(1)}, bf16[384,256]{1,0:T(8,128)(2,1)S(1)}, u32[]{:S(2)}, u32[]{:S(2)}) collective-permute-start(bf16[384,256]{1,0:T(8,128)(2,1)S(1)} %get-tuple-element.25), channel_id=1, source_target_pairs={{0,28},{4,24},{8,20},{12,16},{16,12},{20,8},{24,4},{28,0},{1,29},{... | collective-permute-start | bytes 589832 | tf_op jit(solution)/shard_map/ppermute | solution.py:660
  24.4 2.5 %collective-permute-done.2.refs_2_ = bf16[384,256]{1,0:T(8,128)(2,1)S(1)} collective-permute-done((bf16[384,256]{1,0:T(8,128)(2,1)S(1)}, bf16[384,256]{1,0:T(8,128)(2,1)S(1)}, u32[]{:S(2)}, u32[]{:S(2)}) %collective-permute-start.2) | collective-permute-done | bytes 196640 | tf_op jit(solution)/shard_map/ppermute | solution.py:660
  26.9 11.5 %collective-permute-done.4.refs_4_ = bf16[384,256]{1,0:T(8,128)(2,1)S(1)} collective-permute-done((bf16[384,256]{1,0:T(8,128)(2,1)S(1)}, bf16[384,256]{1,0:T(8,128)(2,1)S(1)}, u32[]{:S(2)}, u32[]{:S(2)}) %collective-permute-start.4) | collective-permute-done | bytes 196640 | tf_op jit(solution)/shard_map/ppermute | solution.py:660
  38.4 3.2 %shard_map.140 = (f32[6,2,128,128]{3,2,1,0:T(8,128)S(1)}, f32[6,2,128,128]{3,2,1,0:T(8,128)S(1)}) custom-call(bf16[384,256]{1,0:T(8,128)(2,1)S(1)} %collective-permute-done.refs_0_, bf16[384,256]{1,0:T(8,128)(2,1)S(1)} %collective-permute-done.1.refs_1_, bf16[384,256]{1,0:T(8,128)(2,1)S(1)} %collective-permute-done.2.refs_2_, ...), custom_call_target="tpu_custom_call" | custom-call | flops 1 | bytes 1 | tf_op jit(solution)/shard_map/pallas_call | solution.py:309
  41.8 1.8 %collective-permute-start.9 = (bf16[4,320,128]{2,1,0:T(8,128)(2,1)S(1)}, bf16[4,320,128]{2,1,0:T(8,128)(2,1)S(1)}, u32[]{:S(2)}, u32[]{:S(2)}) collective-permute-start(bf16[4,320,128]{2,1,0:T(8,128)(2,1)S(1)} %shard_map.144.refs_0_), channel_id=1, source_target_pairs={{0,2},{1,3},{2,0},{3,1},{4,6},{5,7},{6,4},{7,5},{8,10},{9,11},{10,... | collective-permute-start | bytes 983048 | tf_op jit(solution)/shard_map/ppermute | solution.py:660
  43.7 1.5 %collective-permute-start.10 = (bf16[4,320,128]{2,1,0:T(8,128)(2,1)S(1)}, bf16[4,320,128]{2,1,0:T(8,128)(2,1)S(1)}, u32[]{:S(2)}, u32[]{:S(2)}) collective-permute-start(bf16[4,320,128]{2,1,0:T(8,128)(2,1)S(1)} %shard_map.144.refs_0_), channel_id=1, source_target_pairs={{0,6},{1,7},{2,4},{3,5},{4,2},{5,3},{6,0},{7,1},{8,14},{9,15},{10,... | collective-permute-start | bytes 983048 | tf_op jit(solution)/shard_map/ppermute | solution.py:676
  45.2 8.3 %shard_map.141 = (bf16[8,128,256]{2,1,0:T(8,128)(2,1)S(1)}, bf16[8,64,128]{2,1,0:T(8,128)(2,1)S(1)}) custom-call(s32[3]{0:T(128)S(1)} %pad_add_fusion.place_ref, bf16[384,256]{1,0:T(8,128)(2,1)S(1)} %collective-permute-done.refs_0_, bf16[384,256]{1,0:T(8,128)(2,1)S(1)} %collective-permute-done.1.refs_1_, ...), custom_call_target="tpu_custom_call" | custom-call | flops 1073741824 | bytes 2097152 | tf_op jit(solution)/shard_map/pallas_call | solution.py:379
  53.4 15.1 %all_to_all.15.refs_0_ = bf16[8,64,128]{2,1,0:T(8,128)(2,1)S(1)} all-to-all(bf16[8,64,128]{2,1,0:T(8,128)(2,1)S(1)} %get-tuple-element.28), channel_id=1, replica_groups=mesh['seq'=8,'dp'=4] {'seq'}, dimensions={0} | all-to-all | bytes 262144 | tf_op jit(solution)/shard_map/all_to_all | solution.py:664
  70.5 3.4 %all-to-all-start.1 = ((bf16[8,64,128]{2,1,0:T(8,128)(2,1)}), bf16[8,64,128]{2,1,0:T(8,128)(2,1)S(1)}, u32[]{:S(2)}, u32[]{:S(2)}) async-start(bf16[8,64,128]{2,1,0:T(8,128)(2,1)} %shard_map.142.refs_4_), calls=%async_computation.1 | async-start | bytes 262144 | tf_op jit(solution)/shard_map/all_to_all | solution.py:664
  74.6 7.2 %all-to-all-done.1 = bf16[8,64,128]{2,1,0:T(8,128)(2,1)S(1)} async-done(((bf16[8,64,128]{2,1,0:T(8,128)(2,1)}), bf16[8,64,128]{2,1,0:T(8,128)(2,1)S(1)}, u32[]{:S(2)}, u32[]{:S(2)}) %all-to-all-start.1) | async-done | bytes 131104 | tf_op jit(solution)/shard_map/all_to_all | solution.py:664
  81.8 4.2 %shard_map.146 = (f32[1,128]{1,0:T(1,128)}, bf16[512,128]{1,0:T(8,128)(2,1)S(1)}, bf16[64,256]{1,0:T(8,128)(2,1)S(1)}) custom-call(s32[3]{0:T(128)S(1)} %pad_add_fusion.place_ref, bf16[512,128]{1,0:T(8,128)(2,1)S(1)} %bitcast.7, bf16[2,256,1280]{2,1,0:T(8,128)(2,1)S(1)} %shard_map.145.refs_0_, bf16[2,256,1280]{2,1,0:T(8,128)(2,1)S(1)} %collective-permute-done.11.refs_1_, ...), custom_call_target="tpu_custom_call" | custom-call | flops 503316480 | bytes 2785280 | tf_op jit(solution)/shard_map/pallas_call | solution.py:549
  86.1 1.6 %collective-permute-start.13 = (bf16[64,256]{1,0:T(8,128)(2,1)S(1)}, bf16[64,256]{1,0:T(8,128)(2,1)S(1)}, u32[]{:S(2)}, u32[]{:S(2)}) collective-permute-start(bf16[64,256]{1,0:T(8,128)(2,1)S(1)} %get-tuple-element.32.refs_0_), channel_id=1, source_target_pairs={{0,2},{1,3},{2,0},{3,1},{4,6},{5,7},{6,4},{7,5},{8,10},{9,11},{10,... | collective-permute-start | bytes 98312 | tf_op jit(solution)/shard_map/ppermute | solution.py:660
  87.9 2.1 %collective-permute-done.13.refs_2_ = bf16[64,256]{1,0:T(8,128)(2,1)S(1)} collective-permute-done((bf16[64,256]{1,0:T(8,128)(2,1)S(1)}, bf16[64,256]{1,0:T(8,128)(2,1)S(1)}, u32[]{:S(2)}, u32[]{:S(2)}) %collective-permute-start.13) | collective-permute-done | bytes 32800 | tf_op jit(solution)/shard_map/ppermute | solution.py:660
  91.7 3.4 %all-to-all-start.2 = ((bf16[8,64,256]{2,1,0:T(8,128)(2,1)}), bf16[8,64,256]{2,1,0:T(8,128)(2,1)S(1)}, u32[]{:S(2)}, u32[]{:S(2)}) async-start(bf16[8,64,256]{2,1,0:T(8,128)(2,1)} %shard_map.148), calls=%async_computation.2 | async-start | bytes 524288 | tf_op jit(solution)/shard_map/all_to_all | solution.py:664
  95.1 2.4 %shard_map.147 = bf16[1,2,1024,128]{3,2,1,0:T(8,128)(2,1)} custom-call(s32[3]{0:T(128)S(1)} %pad_add_fusion.place_ref, bf16[512,128]{1,0:T(8,128)(2,1)S(1)} %get-tuple-element.31.grad_ref, f32[1,2048]{1,0:T(1,128)} %scale_ref.1, bf16[64,2048]{1,0:T(8,128)(2,1)} %bitcast.10), custom_call_target="tpu_custom_call" | custom-call | flops 67108864 | bytes 524288 | tf_op jit(solution)/shard_map/pallas_call | solution.py:609
  97.5 7.0 %all-to-all-done.2.in_ref = bf16[8,64,256]{2,1,0:T(8,128)(2,1)S(1)} async-done(((bf16[8,64,256]{2,1,0:T(8,128)(2,1)}), bf16[8,64,256]{2,1,0:T(8,128)(2,1)S(1)}, u32[]{:S(2)}, u32[]{:S(2)}) %all-to-all-start.2) | async-done | bytes 262176 | tf_op jit(solution)/shard_map/all_to_all | solution.py:664
  (23 shorter events, 5.9 us)
Async XLA Ops:
  2.6 17.7 %collective-permute-start.3 = (bf16[544,256]{1,0:T(8,128)(2,1)S(1)}, bf16[544,256]{1,0:T(8,128)(2,1)S(1)}, u32[]{:S(2)}, u32[]{:S(2)}) collective-permute-start(bf16[544,256]{1,0:T(8,128)(2,1)S(1)} %get-tuple-element.21), channel_id=1, source_target_pairs={{0,16},{4,20},{8,24},{12,28},{16,0},{20,4},{24,8},{28,12},{1,17},{... | collective-permute-start | bytes 835592 | tf_op jit(solution)/shard_map/ppermute | solution.py:660
  6.7 6.9 %collective-permute-start = (bf16[384,256]{1,0:T(8,128)(2,1)S(1)}, bf16[384,256]{1,0:T(8,128)(2,1)S(1)}, u32[]{:S(2)}, u32[]{:S(2)}) collective-permute-start(bf16[384,256]{1,0:T(8,128)(2,1)S(1)} %get-tuple-element.18), channel_id=1, source_target_pairs={{0,4},{4,0},{8,12},{12,8},{16,20},{20,16},{24,28},{28,24},{1,5},{5... | collective-permute-start | bytes 589832 | tf_op jit(solution)/shard_map/ppermute | solution.py:660
  8.2 16.1 %collective-permute-start.1 = (bf16[384,256]{1,0:T(8,128)(2,1)S(1)}, bf16[384,256]{1,0:T(8,128)(2,1)S(1)}, u32[]{:S(2)}, u32[]{:S(2)}) collective-permute-start(bf16[384,256]{1,0:T(8,128)(2,1)S(1)} %get-tuple-element.19), channel_id=1, source_target_pairs={{0,8},{4,12},{8,0},{12,4},{16,24},{20,28},{24,16},{28,20},{1,9},{5... | collective-permute-start | bytes 589832 | tf_op jit(solution)/shard_map/ppermute | solution.py:660
  9.8 17.1 %collective-permute-start.2 = (bf16[384,256]{1,0:T(8,128)(2,1)S(1)}, bf16[384,256]{1,0:T(8,128)(2,1)S(1)}, u32[]{:S(2)}, u32[]{:S(2)}) collective-permute-start(bf16[384,256]{1,0:T(8,128)(2,1)S(1)} %get-tuple-element.20), channel_id=1, source_target_pairs={{0,12},{4,8},{8,4},{12,0},{16,28},{20,24},{24,20},{28,16},{1,13},{... | collective-permute-start | bytes 589832 | tf_op jit(solution)/shard_map/ppermute | solution.py:660
  10.2 28.2 %collective-permute-start.4 = (bf16[384,256]{1,0:T(8,128)(2,1)S(1)}, bf16[384,256]{1,0:T(8,128)(2,1)S(1)}, u32[]{:S(2)}, u32[]{:S(2)}) collective-permute-start(bf16[384,256]{1,0:T(8,128)(2,1)S(1)} %get-tuple-element.22), channel_id=1, source_target_pairs={{0,20},{4,16},{8,28},{12,24},{16,4},{20,0},{24,12},{28,8},{1,21},{... | collective-permute-start | bytes 589832 | tf_op jit(solution)/shard_map/ppermute | solution.py:660
  13.6 27.9 %collective-permute-start.5 = (bf16[384,256]{1,0:T(8,128)(2,1)S(1)}, bf16[384,256]{1,0:T(8,128)(2,1)S(1)}, u32[]{:S(2)}, u32[]{:S(2)}) collective-permute-start(bf16[384,256]{1,0:T(8,128)(2,1)S(1)} %get-tuple-element.24), channel_id=1, source_target_pairs={{0,24},{4,28},{8,16},{12,20},{16,8},{20,12},{24,0},{28,4},{1,25},{... | collective-permute-start | bytes 589832 | tf_op jit(solution)/shard_map/ppermute | solution.py:660
  20.2 21.3 %collective-permute-start.6 = (bf16[384,256]{1,0:T(8,128)(2,1)S(1)}, bf16[384,256]{1,0:T(8,128)(2,1)S(1)}, u32[]{:S(2)}, u32[]{:S(2)}) collective-permute-start(bf16[384,256]{1,0:T(8,128)(2,1)S(1)} %get-tuple-element.25), channel_id=1, source_target_pairs={{0,28},{4,24},{8,20},{12,16},{16,12},{20,8},{24,4},{28,0},{1,29},{... | collective-permute-start | bytes 589832 | tf_op jit(solution)/shard_map/ppermute | solution.py:660
  24.3 17.2 %collective-permute-start.7 = (bf16[2,320,128]{2,1,0:T(8,128)(2,1)S(1)}, bf16[2,320,128]{2,1,0:T(8,128)(2,1)S(1)}, u32[]{:S(2)}, u32[]{:S(2)}) collective-permute-start(bf16[2,320,128]{2,1,0:T(8,128)(2,1)S(1)} %shard_map.143.first_ref), channel_id=1, source_target_pairs={{0,8},{4,12},{8,0},{12,4},{16,24},{20,28},{24,16},{28,20},{1,9},{5... | collective-permute-start | bytes 491528 | tf_op jit(solution)/shard_map/ppermute | solution.py:660
  41.6 27.6 %collective-permute-start.8 = (bf16[4,320,128]{2,1,0:T(8,128)(2,1)S(1)}, bf16[4,320,128]{2,1,0:T(8,128)(2,1)S(1)}, u32[]{:S(2)}, u32[]{:S(2)}) collective-permute-start(bf16[4,320,128]{2,1,0:T(8,128)(2,1)S(1)} %shard_map.144.refs_0_), channel_id=1, source_target_pairs={{0,4},{4,0},{8,12},{12,8},{16,20},{20,16},{24,28},{28,24},{1,5},{5... | collective-permute-start | bytes 983048 | tf_op jit(solution)/shard_map/ppermute | solution.py:660
  41.8 27.4 %collective-permute-start.9 = (bf16[4,320,128]{2,1,0:T(8,128)(2,1)S(1)}, bf16[4,320,128]{2,1,0:T(8,128)(2,1)S(1)}, u32[]{:S(2)}, u32[]{:S(2)}) collective-permute-start(bf16[4,320,128]{2,1,0:T(8,128)(2,1)S(1)} %shard_map.144.refs_0_), channel_id=1, source_target_pairs={{0,2},{1,3},{2,0},{3,1},{4,6},{5,7},{6,4},{7,5},{8,10},{9,11},{10,... | collective-permute-start | bytes 983048 | tf_op jit(solution)/shard_map/ppermute | solution.py:660
  43.7 25.6 %collective-permute-start.10 = (bf16[4,320,128]{2,1,0:T(8,128)(2,1)S(1)}, bf16[4,320,128]{2,1,0:T(8,128)(2,1)S(1)}, u32[]{:S(2)}, u32[]{:S(2)}) collective-permute-start(bf16[4,320,128]{2,1,0:T(8,128)(2,1)S(1)} %shard_map.144.refs_0_), channel_id=1, source_target_pairs={{0,6},{1,7},{2,4},{3,5},{4,2},{5,3},{6,0},{7,1},{8,14},{9,15},{10,... | collective-permute-start | bytes 983048 | tf_op jit(solution)/shard_map/ppermute | solution.py:676
  70.5 11.3 %collective-permute-start.11 = (bf16[2,256,1280]{2,1,0:T(8,128)(2,1)S(1)}, bf16[2,256,1280]{2,1,0:T(8,128)(2,1)S(1)}, u32[]{:S(2)}, u32[]{:S(2)}) collective-permute-start(bf16[2,256,1280]{2,1,0:T(8,128)(2,1)S(1)} %shard_map.145.refs_0_), channel_id=1, source_target_pairs={{0,1},{1,0},{2,3},{3,2},{4,5},{5,4},{6,7},{7,6},{8,9},{9,8},{10,11... | collective-permute-start | bytes 3932168 | tf_op jit(solution)/shard_map/ppermute | solution.py:660
  70.5 11.2 %all-to-all-start.1 = ((bf16[8,64,128]{2,1,0:T(8,128)(2,1)}), bf16[8,64,128]{2,1,0:T(8,128)(2,1)S(1)}, u32[]{:S(2)}, u32[]{:S(2)}) async-start(bf16[8,64,128]{2,1,0:T(8,128)(2,1)} %shard_map.142.refs_4_), calls=%async_computation.1 | async-start | bytes 262144 | tf_op jit(solution)/shard_map/all_to_all | solution.py:664
  86.0 1.9 %collective-permute-start.12 = (bf16[64,256]{1,0:T(8,128)(2,1)S(1)}, bf16[64,256]{1,0:T(8,128)(2,1)S(1)}, u32[]{:S(2)}, u32[]{:S(2)}) collective-permute-start(bf16[64,256]{1,0:T(8,128)(2,1)S(1)} %get-tuple-element.32.refs_0_), channel_id=1, source_target_pairs={{0,1},{1,0},{2,3},{3,2},{4,5},{5,4},{6,7},{7,6},{8,9},{9,8},{10,11... | collective-permute-start | bytes 98312 | tf_op jit(solution)/shard_map/ppermute | solution.py:660
  86.1 4.0 %collective-permute-start.13 = (bf16[64,256]{1,0:T(8,128)(2,1)S(1)}, bf16[64,256]{1,0:T(8,128)(2,1)S(1)}, u32[]{:S(2)}, u32[]{:S(2)}) collective-permute-start(bf16[64,256]{1,0:T(8,128)(2,1)S(1)} %get-tuple-element.32.refs_0_), channel_id=1, source_target_pairs={{0,2},{1,3},{2,0},{3,1},{4,6},{5,7},{6,4},{7,5},{8,10},{9,11},{10,... | collective-permute-start | bytes 98312 | tf_op jit(solution)/shard_map/ppermute | solution.py:660
  87.6 3.3 %collective-permute-start.14 = (bf16[64,256]{1,0:T(8,128)(2,1)S(1)}, bf16[64,256]{1,0:T(8,128)(2,1)S(1)}, u32[]{:S(2)}, u32[]{:S(2)}) collective-permute-start(bf16[64,256]{1,0:T(8,128)(2,1)S(1)} %get-tuple-element.32.refs_0_), channel_id=1, source_target_pairs={{0,3},{1,2},{2,1},{3,0},{4,7},{5,6},{6,5},{7,4},{8,11},{9,10},{10,... | collective-permute-start | bytes 98312 | tf_op jit(solution)/shard_map/ppermute | solution.py:660
  91.7 12.9 %all-to-all-start.2 = ((bf16[8,64,256]{2,1,0:T(8,128)(2,1)}), bf16[8,64,256]{2,1,0:T(8,128)(2,1)S(1)}, u32[]{:S(2)}, u32[]{:S(2)}) async-start(bf16[8,64,256]{2,1,0:T(8,128)(2,1)} %shard_map.148), calls=%async_computation.2 | async-start | bytes 524288 | tf_op jit(solution)/shard_map/all_to_all | solution.py:664

commit v11 on v10

--- a/solution.py
+++ b/solution.py
@@ -341,11 +341,6 @@
         copy.wait()
     gain = 1.0 + scale_scr[...]
     shift = shift_scr[...]
-    proj = proj_scr[...]
-    zero = jnp.zeros_like(proj)
-    proj_pair = jnp.concatenate(
-        [jnp.concatenate([proj, zero], axis=1), jnp.concatenate([zero, proj], axis=1)], axis=0
-    )
     together = 2
     for first in range(0, count, together):
         results = []
@@ -362,13 +357,15 @@
                 value, total, _ = soft_part(query, key_scr, value_scr, rows, head, before)
                 mixed.append(value / total)
             attended = jnp.concatenate(mixed, axis=1) if heads > 1 else mixed[0]
-            modulated = (attended * gain + shift).astype(BF16)
-            pair = jnp.concatenate([modulated[:half], modulated[half:]], axis=1)
-            results.append((modulated, mm_nt(pair, proj_pair).astype(BF16)))
-        for at, (modulated, latent) in enumerate(results):
-            place = jnp.bitwise_xor(me, masks[first + at])
-            mod_ref[place] = modulated
-            lat_ref[place] = latent
+            results.append((attended * gain + shift).astype(BF16))
+        for at, modulated in enumerate(results):
+            mod_ref[jnp.bitwise_xor(me, masks[first + at])] = modulated
+    sides = [
+        mm_nt(mod_ref[:, rows, :].reshape(count * half, width), proj_scr[...])
+        for rows in (slice(0, half), slice(half, part_rows))
+    ]
+    latent = jnp.concatenate(sides, axis=1).astype(BF16)
+    lat_ref[...] = latent.reshape(count, half, 2 * CH)
 
 
 def attend(sizes, masks, place, received, kept, scales, shifts, proj):
@@ -714,10 +711,16 @@
     received = [swap(x, "seq", mask) if mask else x for mask, x in zip(masks, packed)]
     bits = [1 << b for b in reversed(range(data_count.bit_length() - 1))]
     shared = sizes.share < patch_embed.shape[0]
+    kept, order = [], list(range(seq_count))
+    if seq_count == 8:
+        late = [slot for slot, mask in enumerate(masks) if mask in (6, 7)]
+        order = [slot for slot in order if slot not in late]
+        kept = attend_early(sizes, [received[slot] for slot in order])
+        order = order + late
     if sizes.riding:
         ride = [slot for slot, mask in enumerate(masks) if sizes.rides(mask)]
         two = collect(sizes, [received[slot] for slot in ride])
-        held = join(two, swap(two, "seq", 2), received[:-1])
+        held = join(two, swap(two, "seq", 2), kept)
         ride_masks = [masks[slot] for slot in ride]
         ride_masks = ride_masks + [mask ^ 2 for mask in ride_masks]
         pairs = [
@@ -725,12 +728,6 @@
             (swap(held, "dp", bits[0]), swap_both(held, 1, bits[0])),
         ]
 
-    kept, order = [], list(range(seq_count))
-    if seq_count == 8:
-        late = [slot for slot, mask in enumerate(masks) if mask in (6, 7)]
-        order = [slot for slot in order if slot not in late]
-        kept = attend_early(sizes, [received[slot] for slot in order])
-        order = order + late
     modulated, latent_part = attend(
         sizes, [masks[slot] for slot in order], place, [received[slot] for slot in order], kept,
         in_hbm(scales), in_hbm(shifts), in_hbm(proj_turned)

time: 106 us -> 101 us (0.953)
  blocking collectives: 15.1 us -> 12.5 us
  Pallas kernels: 23.5 us -> 21.4 us
    all_to_all x1, blocking collectives: 15.1 us -> 12.5 us  [all_to_all(): lax.all_to_all(x, 'seq', split_axis=0, concat_axis=0, tiled=True, axis_in...]
    pallas_call x1, Pallas kernels: 8.28 us -> 6.2 us  [attend(): pl.pallas_call(functools.partial(attend_kernel, sizes, masks, early), out...]
  transfers between devices with their start and end apart: 17 -> 17, of which waited for: 9 -> 9; matrix products, arithmetic and copies ran while one was open for 0% -> 0% of each run, Pallas kernels for 14% -> 12%
where the time goes in v11:
time: 101 us
  waiting for transfers between devices  38.8 us (38%)
  starting transfers between devices  26.4 us (26%)
  Pallas kernels  21.4 us (21%)
  blocking collectives  12.5 us (12%)
  between operations  1.4 us (1%)
    ppermute x14, waiting for transfers between devices, swap(): return lax.ppermute(x, axis, [(i, i ^ mask) for i in range(count)])  24.6 us
    ppermute x14, starting transfers between devices, swap(): return lax.ppermute(x, axis, [(i, i ^ mask) for i in range(count)])  18.2 us
    all_to_all x2, waiting for transfers between devices, all_to_all(): lax.all_to_all(x, 'seq', split_axis=0, concat_axis=0, tiled=True, axis_in...  14.2 us
    all_to_all x1, blocking collectives, all_to_all(): lax.all_to_all(x, 'seq', split_axis=0, concat_axis=0, tiled=True, axis_in...  12.5 us
    all_to_all x2, starting transfers between devices, all_to_all(): lax.all_to_all(x, 'seq', split_axis=0, concat_axis=0, tiled=True, axis_in...  6.8 us
    pallas_call x1, Pallas kernels, attend(): pl.pallas_call(functools.partial(attend_kernel, sizes, masks, early), out...  6.2 us
    pallas_call x1, Pallas kernels, reward_head(): pl.pallas_call(functools.partial(head_kernel, grid_rows, fused, embed_mas...  4.19 us
    pallas_call x1, Pallas kernels, attend_early(): pl.pallas_call(functools.partial(early_kernel, sizes, count), out_shape=(...  3.16 us
  transfers between devices with their start and end apart: 17, of which 9 were waited for; matrix products, arithmetic and copies ran while one was open for 0% of the time, Pallas kernels for 12%

profile of v11, /device:TPU:0, one launch (start us, length us, event | category | flops | bytes accessed | tf_op | source)
XLA Modules:
  0.0 100.7 jit_solution(12722392492223216471)
XLA Ops:
  0.6 1.9 %shard_map.139 = (bf16[384,256]{1,0:T(8,128)(2,1)S(1)}, bf16[384,256]{1,0:T(8,128)(2,1)S(1)}, bf16[384,256]{1,0:T(8,128)(2,1)S(1)}, bf16[544,256]{1,0:T(8,128)(2...) custom-call(bf16[1,128,2048]{2,1,0:T(8,128)(2,1)} %q_ref.1, ...), custom_call_target="tpu_custom_call" | custom-call | bytes 3145728 | tf_op jit(solution)/shard_map/pallas_call | solution.py:136
  2.6 4.1 %collective-permute-start.3 = (bf16[544,256]{1,0:T(8,128)(2,1)S(1)}, bf16[544,256]{1,0:T(8,128)(2,1)S(1)}, u32[]{:S(2)}, u32[]{:S(2)}) collective-permute-start(bf16[544,256]{1,0:T(8,128)(2,1)S(1)} %get-tuple-element.21), channel_id=1, source_target_pairs={{0,16},{4,20},{8,24},{12,28},{16,0},{20,4},{24,8},{28,12},{1,17},{... | collective-permute-start | bytes 835592 | tf_op jit(solution)/shard_map/ppermute | solution.py:657
  6.7 1.5 %collective-permute-start = (bf16[384,256]{1,0:T(8,128)(2,1)S(1)}, bf16[384,256]{1,0:T(8,128)(2,1)S(1)}, u32[]{:S(2)}, u32[]{:S(2)}) collective-permute-start(bf16[384,256]{1,0:T(8,128)(2,1)S(1)} %get-tuple-element.18), channel_id=1, source_target_pairs={{0,4},{4,0},{8,12},{12,8},{16,20},{20,16},{24,28},{28,24},{1,5},{5... | collective-permute-start | bytes 589832 | tf_op jit(solution)/shard_map/ppermute | solution.py:657
  8.2 1.6 %collective-permute-start.1 = (bf16[384,256]{1,0:T(8,128)(2,1)S(1)}, bf16[384,256]{1,0:T(8,128)(2,1)S(1)}, u32[]{:S(2)}, u32[]{:S(2)}) collective-permute-start(bf16[384,256]{1,0:T(8,128)(2,1)S(1)} %get-tuple-element.19), channel_id=1, source_target_pairs={{0,8},{4,12},{8,0},{12,4},{16,24},{20,28},{24,16},{28,20},{1,9},{5... | collective-permute-start | bytes 589832 | tf_op jit(solution)/shard_map/ppermute | solution.py:657
  10.2 1.3 %collective-permute-start.4 = (bf16[384,256]{1,0:T(8,128)(2,1)S(1)}, bf16[384,256]{1,0:T(8,128)(2,1)S(1)}, u32[]{:S(2)}, u32[]{:S(2)}) collective-permute-start(bf16[384,256]{1,0:T(8,128)(2,1)S(1)} %get-tuple-element.22), channel_id=1, source_target_pairs={{0,20},{4,16},{8,28},{12,24},{16,4},{20,0},{24,12},{28,8},{1,21},{... | collective-permute-start | bytes 589832 | tf_op jit(solution)/shard_map/ppermute | solution.py:657
  11.5 2.2 %collective-permute-done.refs_0_ = bf16[384,256]{1,0:T(8,128)(2,1)S(1)} collective-permute-done((bf16[384,256]{1,0:T(8,128)(2,1)S(1)}, bf16[384,256]{1,0:T(8,128)(2,1)S(1)}, u32[]{:S(2)}, u32[]{:S(2)}) %collective-permute-start) | collective-permute-done | bytes 196640 | tf_op jit(solution)/shard_map/ppermute | solution.py:657
  13.6 1.4 %collective-permute-start.5 = (bf16[384,256]{1,0:T(8,128)(2,1)S(1)}, bf16[384,256]{1,0:T(8,128)(2,1)S(1)}, u32[]{:S(2)}, u32[]{:S(2)}) collective-permute-start(bf16[384,256]{1,0:T(8,128)(2,1)S(1)} %get-tuple-element.24), channel_id=1, source_target_pairs={{0,24},{4,28},{8,16},{12,20},{16,8},{20,12},{24,0},{28,4},{1,25},{... | collective-permute-start | bytes 589832 | tf_op jit(solution)/shard_map/ppermute | solution.py:657
  15.1 5.2 %collective-permute-done.3.refs_3_.refs_0_ = bf16[544,256]{1,0:T(8,128)(2,1)S(1)} collective-permute-done((bf16[544,256]{1,0:T(8,128)(2,1)S(1)}, bf16[544,256]{1,0:T(8,128)(2,1)S(1)}, u32[]{:S(2)}, u32[]{:S(2)}) %collective-permute-start.3) | collective-permute-done | bytes 278560 | tf_op jit(solution)/shard_map/ppermute | solution.py:657
  20.2 3.8 %collective-permute-start.6 = (bf16[384,256]{1,0:T(8,128)(2,1)S(1)}, bf16[384,256]{1,0:T(8,128)(2,1)S(1)}, u32[]{:S(2)}, u32[]{:S(2)}) collective-permute-start(bf16[384,256]{1,0:T(8,128)(2,1)S(1)} %get-tuple-element.25), channel_id=1, source_target_pairs={{0,28},{4,24},{8,20},{12,16},{16,12},{20,8},{24,4},{28,0},{1,29},{... | collective-permute-start | bytes 589832 | tf_op jit(solution)/shard_map/ppermute | solution.py:657
  24.4 2.5 %collective-permute-done.2.refs_2_ = bf16[384,256]{1,0:T(8,128)(2,1)S(1)} collective-permute-done((bf16[384,256]{1,0:T(8,128)(2,1)S(1)}, bf16[384,256]{1,0:T(8,128)(2,1)S(1)}, u32[]{:S(2)}, u32[]{:S(2)}) %collective-permute-start.2) | collective-permute-done | bytes 196640 | tf_op jit(solution)/shard_map/ppermute | solution.py:657
  26.9 11.5 %collective-permute-done.4.refs_4_ = bf16[384,256]{1,0:T(8,128)(2,1)S(1)} collective-permute-done((bf16[384,256]{1,0:T(8,128)(2,1)S(1)}, bf16[384,256]{1,0:T(8,128)(2,1)S(1)}, u32[]{:S(2)}, u32[]{:S(2)}) %collective-permute-start.4) | collective-permute-done | bytes 196640 | tf_op jit(solution)/shard_map/ppermute | solution.py:657
  38.4 3.2 %shard_map.140 = (f32[6,2,128,128]{3,2,1,0:T(8,128)S(1)}, f32[6,2,128,128]{3,2,1,0:T(8,128)S(1)}) custom-call(bf16[384,256]{1,0:T(8,128)(2,1)S(1)} %collective-permute-done.refs_0_, bf16[384,256]{1,0:T(8,128)(2,1)S(1)} %collective-permute-done.1.refs_1_, bf16[384,256]{1,0:T(8,128)(2,1)S(1)} %collective-permute-done.2.refs_2_, ...), custom_call_target="tpu_custom_call" | custom-call | flops 1 | bytes 1 | tf_op jit(solution)/shard_map/pallas_call | solution.py:309
  41.8 1.8 %collective-permute-start.9 = (bf16[4,320,128]{2,1,0:T(8,128)(2,1)S(1)}, bf16[4,320,128]{2,1,0:T(8,128)(2,1)S(1)}, u32[]{:S(2)}, u32[]{:S(2)}) collective-permute-start(bf16[4,320,128]{2,1,0:T(8,128)(2,1)S(1)} %shard_map.144.refs_0_), channel_id=1, source_target_pairs={{0,2},{1,3},{2,0},{3,1},{4,6},{5,7},{6,4},{7,5},{8,10},{9,11},{10,... | collective-permute-start | bytes 983048 | tf_op jit(solution)/shard_map/ppermute | solution.py:657
  43.6 1.5 %collective-permute-start.10 = (bf16[4,320,128]{2,1,0:T(8,128)(2,1)S(1)}, bf16[4,320,128]{2,1,0:T(8,128)(2,1)S(1)}, u32[]{:S(2)}, u32[]{:S(2)}) collective-permute-start(bf16[4,320,128]{2,1,0:T(8,128)(2,1)S(1)} %shard_map.144.refs_0_), channel_id=1, source_target_pairs={{0,6},{1,7},{2,4},{3,5},{4,2},{5,3},{6,0},{7,1},{8,14},{9,15},{10,... | collective-permute-start | bytes 983048 | tf_op jit(solution)/shard_map/ppermute | solution.py:673
  45.1 6.2 %shard_map.141 = (bf16[8,128,256]{2,1,0:T(8,128)(2,1)S(1)}, bf16[8,64,128]{2,1,0:T(8,128)(2,1)S(1)}) custom-call(s32[3]{0:T(128)S(1)} %pad_add_fusion.place_ref, bf16[384,256]{1,0:T(8,128)(2,1)S(1)} %collective-permute-done.refs_0_, bf16[384,256]{1,0:T(8,128)(2,1)S(1)} %collective-permute-done.1.refs_1_, ...), custom_call_target="tpu_custom_call" | custom-call | flops 1073741824 | bytes 2097152 | tf_op jit(solution)/shard_map/pallas_call | solution.py:376
  51.3 12.5 %all_to_all.15.refs_0_ = bf16[8,64,128]{2,1,0:T(8,128)(2,1)S(1)} all-to-all(bf16[8,64,128]{2,1,0:T(8,128)(2,1)S(1)} %get-tuple-element.28), channel_id=1, replica_groups=mesh['seq'=8,'dp'=4] {'seq'}, dimensions={0} | all-to-all | bytes 262144 | tf_op jit(solution)/shard_map/all_to_all | solution.py:661
  65.8 3.4 %all-to-all-start.1 = ((bf16[8,64,128]{2,1,0:T(8,128)(2,1)}), bf16[8,64,128]{2,1,0:T(8,128)(2,1)S(1)}, u32[]{:S(2)}, u32[]{:S(2)}) async-start(bf16[8,64,128]{2,1,0:T(8,128)(2,1)} %shard_map.142.refs_4_), calls=%async_computation.1 | async-start | bytes 262144 | tf_op jit(solution)/shard_map/all_to_all | solution.py:661
  69.8 7.2 %all-to-all-done.1 = bf16[8,64,128]{2,1,0:T(8,128)(2,1)S(1)} async-done(((bf16[8,64,128]{2,1,0:T(8,128)(2,1)}), bf16[8,64,128]{2,1,0:T(8,128)(2,1)S(1)}, u32[]{:S(2)}, u32[]{:S(2)}) %all-to-all-start.1) | async-done | bytes 131104 | tf_op jit(solution)/shard_map/all_to_all | solution.py:661
  77.0 4.2 %shard_map.146 = (f32[1,128]{1,0:T(1,128)}, bf16[512,128]{1,0:T(8,128)(2,1)S(1)}, bf16[64,256]{1,0:T(8,128)(2,1)S(1)}) custom-call(s32[3]{0:T(128)S(1)} %pad_add_fusion.place_ref, bf16[512,128]{1,0:T(8,128)(2,1)S(1)} %bitcast.7, bf16[2,256,1280]{2,1,0:T(8,128)(2,1)S(1)} %shard_map.145.refs_0_, bf16[2,256,1280]{2,1,0:T(8,128)(2,1)S(1)} %collective-permute-done.11.refs_1_, ...), custom_call_target="tpu_custom_call" | custom-call | flops 503316480 | bytes 2785280 | tf_op jit(solution)/shard_map/pallas_call | solution.py:546
  81.3 1.6 %collective-permute-start.13 = (bf16[64,256]{1,0:T(8,128)(2,1)S(1)}, bf16[64,256]{1,0:T(8,128)(2,1)S(1)}, u32[]{:S(2)}, u32[]{:S(2)}) collective-permute-start(bf16[64,256]{1,0:T(8,128)(2,1)S(1)} %get-tuple-element.32.refs_0_), channel_id=1, source_target_pairs={{0,2},{1,3},{2,0},{3,1},{4,6},{5,7},{6,4},{7,5},{8,10},{9,11},{10,... | collective-permute-start | bytes 98312 | tf_op jit(solution)/shard_map/ppermute | solution.py:657
  83.2 2.1 %collective-permute-done.13.refs_2_ = bf16[64,256]{1,0:T(8,128)(2,1)S(1)} collective-permute-done((bf16[64,256]{1,0:T(8,128)(2,1)S(1)}, bf16[64,256]{1,0:T(8,128)(2,1)S(1)}, u32[]{:S(2)}, u32[]{:S(2)}) %collective-permute-start.13) | collective-permute-done | bytes 32800 | tf_op jit(solution)/shard_map/ppermute | solution.py:657
  86.9 3.4 %all-to-all-start.2 = ((bf16[8,64,256]{2,1,0:T(8,128)(2,1)}), bf16[8,64,256]{2,1,0:T(8,128)(2,1)S(1)}, u32[]{:S(2)}, u32[]{:S(2)}) async-start(bf16[8,64,256]{2,1,0:T(8,128)(2,1)} %shard_map.148), calls=%async_computation.2 | async-start | bytes 524288 | tf_op jit(solution)/shard_map/all_to_all | solution.py:661
  90.4 2.4 %shard_map.147 = bf16[1,2,1024,128]{3,2,1,0:T(8,128)(2,1)} custom-call(s32[3]{0:T(128)S(1)} %pad_add_fusion.place_ref, bf16[512,128]{1,0:T(8,128)(2,1)S(1)} %get-tuple-element.31.grad_ref, f32[1,2048]{1,0:T(1,128)} %scale_ref.1, bf16[64,2048]{1,0:T(8,128)(2,1)} %bitcast.10), custom_call_target="tpu_custom_call" | custom-call | flops 67108864 | bytes 524288 | tf_op jit(solution)/shard_map/pallas_call | solution.py:606
  92.8 7.0 %all-to-all-done.2.in_ref = bf16[8,64,256]{2,1,0:T(8,128)(2,1)S(1)} async-done(((bf16[8,64,256]{2,1,0:T(8,128)(2,1)}), bf16[8,64,256]{2,1,0:T(8,128)(2,1)S(1)}, u32[]{:S(2)}, u32[]{:S(2)}) %all-to-all-start.2) | async-done | bytes 262176 | tf_op jit(solution)/shard_map/all_to_all | solution.py:661
  (23 shorter events, 5.9 us)
Async XLA Ops:
  2.6 17.7 %collective-permute-start.3 = (bf16[544,256]{1,0:T(8,128)(2,1)S(1)}, bf16[544,256]{1,0:T(8,128)(2,1)S(1)}, u32[]{:S(2)}, u32[]{:S(2)}) collective-permute-start(bf16[544,256]{1,0:T(8,128)(2,1)S(1)} %get-tuple-element.21), channel_id=1, source_target_pairs={{0,16},{4,20},{8,24},{12,28},{16,0},{20,4},{24,8},{28,12},{1,17},{... | collective-permute-start | bytes 835592 | tf_op jit(solution)/shard_map/ppermute | solution.py:657
  6.7 6.9 %collective-permute-start = (bf16[384,256]{1,0:T(8,128)(2,1)S(1)}, bf16[384,256]{1,0:T(8,128)(2,1)S(1)}, u32[]{:S(2)}, u32[]{:S(2)}) collective-permute-start(bf16[384,256]{1,0:T(8,128)(2,1)S(1)} %get-tuple-element.18), channel_id=1, source_target_pairs={{0,4},{4,0},{8,12},{12,8},{16,20},{20,16},{24,28},{28,24},{1,5},{5... | collective-permute-start | bytes 589832 | tf_op jit(solution)/shard_map/ppermute | solution.py:657
  8.2 16.1 %collective-permute-start.1 = (bf16[384,256]{1,0:T(8,128)(2,1)S(1)}, bf16[384,256]{1,0:T(8,128)(2,1)S(1)}, u32[]{:S(2)}, u32[]{:S(2)}) collective-permute-start(bf16[384,256]{1,0:T(8,128)(2,1)S(1)} %get-tuple-element.19), channel_id=1, source_target_pairs={{0,8},{4,12},{8,0},{12,4},{16,24},{20,28},{24,16},{28,20},{1,9},{5... | collective-permute-start | bytes 589832 | tf_op jit(solution)/shard_map/ppermute | solution.py:657
  9.8 17.1 %collective-permute-start.2 = (bf16[384,256]{1,0:T(8,128)(2,1)S(1)}, bf16[384,256]{1,0:T(8,128)(2,1)S(1)}, u32[]{:S(2)}, u32[]{:S(2)}) collective-permute-start(bf16[384,256]{1,0:T(8,128)(2,1)S(1)} %get-tuple-element.20), channel_id=1, source_target_pairs={{0,12},{4,8},{8,4},{12,0},{16,28},{20,24},{24,20},{28,16},{1,13},{... | collective-permute-start | bytes 589832 | tf_op jit(solution)/shard_map/ppermute | solution.py:657
  10.2 28.2 %collective-permute-start.4 = (bf16[384,256]{1,0:T(8,128)(2,1)S(1)}, bf16[384,256]{1,0:T(8,128)(2,1)S(1)}, u32[]{:S(2)}, u32[]{:S(2)}) collective-permute-start(bf16[384,256]{1,0:T(8,128)(2,1)S(1)} %get-tuple-element.22), channel_id=1, source_target_pairs={{0,20},{4,16},{8,28},{12,24},{16,4},{20,0},{24,12},{28,8},{1,21},{... | collective-permute-start | bytes 589832 | tf_op jit(solution)/shard_map/ppermute | solution.py:657
  13.6 31.5 %collective-permute-start.5 = (bf16[384,256]{1,0:T(8,128)(2,1)S(1)}, bf16[384,256]{1,0:T(8,128)(2,1)S(1)}, u32[]{:S(2)}, u32[]{:S(2)}) collective-permute-start(bf16[384,256]{1,0:T(8,128)(2,1)S(1)} %get-tuple-element.24), channel_id=1, source_target_pairs={{0,24},{4,28},{8,16},{12,20},{16,8},{20,12},{24,0},{28,4},{1,25},{... | collective-permute-start | bytes 589832 | tf_op jit(solution)/shard_map/ppermute | solution.py:657
  20.2 24.9 %collective-permute-start.6 = (bf16[384,256]{1,0:T(8,128)(2,1)S(1)}, bf16[384,256]{1,0:T(8,128)(2,1)S(1)}, u32[]{:S(2)}, u32[]{:S(2)}) collective-permute-start(bf16[384,256]{1,0:T(8,128)(2,1)S(1)} %get-tuple-element.25), channel_id=1, source_target_pairs={{0,28},{4,24},{8,20},{12,16},{16,12},{20,8},{24,4},{28,0},{1,29},{... | collective-permute-start | bytes 589832 | tf_op jit(solution)/shard_map/ppermute | solution.py:657
  24.3 17.2 %collective-permute-start.7 = (bf16[2,320,128]{2,1,0:T(8,128)(2,1)S(1)}, bf16[2,320,128]{2,1,0:T(8,128)(2,1)S(1)}, u32[]{:S(2)}, u32[]{:S(2)}) collective-permute-start(bf16[2,320,128]{2,1,0:T(8,128)(2,1)S(1)} %shard_map.143.first_ref), channel_id=1, source_target_pairs={{0,8},{4,12},{8,0},{12,4},{16,24},{20,28},{24,16},{28,20},{1,9},{5... | collective-permute-start | bytes 491528 | tf_op jit(solution)/shard_map/ppermute | solution.py:657
  41.6 22.9 %collective-permute-start.8 = (bf16[4,320,128]{2,1,0:T(8,128)(2,1)S(1)}, bf16[4,320,128]{2,1,0:T(8,128)(2,1)S(1)}, u32[]{:S(2)}, u32[]{:S(2)}) collective-permute-start(bf16[4,320,128]{2,1,0:T(8,128)(2,1)S(1)} %shard_map.144.refs_0_), channel_id=1, source_target_pairs={{0,4},{4,0},{8,12},{12,8},{16,20},{20,16},{24,28},{28,24},{1,5},{5... | collective-permute-start | bytes 983048 | tf_op jit(solution)/shard_map/ppermute | solution.py:657
  41.8 22.7 %collective-permute-start.9 = (bf16[4,320,128]{2,1,0:T(8,128)(2,1)S(1)}, bf16[4,320,128]{2,1,0:T(8,128)(2,1)S(1)}, u32[]{:S(2)}, u32[]{:S(2)}) collective-permute-start(bf16[4,320,128]{2,1,0:T(8,128)(2,1)S(1)} %shard_map.144.refs_0_), channel_id=1, source_target_pairs={{0,2},{1,3},{2,0},{3,1},{4,6},{5,7},{6,4},{7,5},{8,10},{9,11},{10,... | collective-permute-start | bytes 983048 | tf_op jit(solution)/shard_map/ppermute | solution.py:657
  43.6 20.9 %collective-permute-start.10 = (bf16[4,320,128]{2,1,0:T(8,128)(2,1)S(1)}, bf16[4,320,128]{2,1,0:T(8,128)(2,1)S(1)}, u32[]{:S(2)}, u32[]{:S(2)}) collective-permute-start(bf16[4,320,128]{2,1,0:T(8,128)(2,1)S(1)} %shard_map.144.refs_0_), channel_id=1, source_target_pairs={{0,6},{1,7},{2,4},{3,5},{4,2},{5,3},{6,0},{7,1},{8,14},{9,15},{10,... | collective-permute-start | bytes 983048 | tf_op jit(solution)/shard_map/ppermute | solution.py:673
  65.7 11.3 %collective-permute-start.11 = (bf16[2,256,1280]{2,1,0:T(8,128)(2,1)S(1)}, bf16[2,256,1280]{2,1,0:T(8,128)(2,1)S(1)}, u32[]{:S(2)}, u32[]{:S(2)}) collective-permute-start(bf16[2,256,1280]{2,1,0:T(8,128)(2,1)S(1)} %shard_map.145.refs_0_), channel_id=1, source_target_pairs={{0,1},{1,0},{2,3},{3,2},{4,5},{5,4},{6,7},{7,6},{8,9},{9,8},{10,11... | collective-permute-start | bytes 3932168 | tf_op jit(solution)/shard_map/ppermute | solution.py:657
  65.8 11.2 %all-to-all-start.1 = ((bf16[8,64,128]{2,1,0:T(8,128)(2,1)}), bf16[8,64,128]{2,1,0:T(8,128)(2,1)S(1)}, u32[]{:S(2)}, u32[]{:S(2)}) async-start(bf16[8,64,128]{2,1,0:T(8,128)(2,1)} %shard_map.142.refs_4_), calls=%async_computation.1 | async-start | bytes 262144 | tf_op jit(solution)/shard_map/all_to_all | solution.py:661
  81.2 1.9 %collective-permute-start.12 = (bf16[64,256]{1,0:T(8,128)(2,1)S(1)}, bf16[64,256]{1,0:T(8,128)(2,1)S(1)}, u32[]{:S(2)}, u32[]{:S(2)}) collective-permute-start(bf16[64,256]{1,0:T(8,128)(2,1)S(1)} %get-tuple-element.32.refs_0_), channel_id=1, source_target_pairs={{0,1},{1,0},{2,3},{3,2},{4,5},{5,4},{6,7},{7,6},{8,9},{9,8},{10,11... | collective-permute-start | bytes 98312 | tf_op jit(solution)/shard_map/ppermute | solution.py:657
  81.3 4.0 %collective-permute-start.13 = (bf16[64,256]{1,0:T(8,128)(2,1)S(1)}, bf16[64,256]{1,0:T(8,128)(2,1)S(1)}, u32[]{:S(2)}, u32[]{:S(2)}) collective-permute-start(bf16[64,256]{1,0:T(8,128)(2,1)S(1)} %get-tuple-element.32.refs_0_), channel_id=1, source_target_pairs={{0,2},{1,3},{2,0},{3,1},{4,6},{5,7},{6,4},{7,5},{8,10},{9,11},{10,... | collective-permute-start | bytes 98312 | tf_op jit(solution)/shard_map/ppermute | solution.py:657
  82.9 3.3 %collective-permute-start.14 = (bf16[64,256]{1,0:T(8,128)(2,1)S(1)}, bf16[64,256]{1,0:T(8,128)(2,1)S(1)}, u32[]{:S(2)}, u32[]{:S(2)}) collective-permute-start(bf16[64,256]{1,0:T(8,128)(2,1)S(1)} %get-tuple-element.32.refs_0_), channel_id=1, source_target_pairs={{0,3},{1,2},{2,1},{3,0},{4,7},{5,6},{6,5},{7,4},{8,11},{9,10},{10,... | collective-permute-start | bytes 98312 | tf_op jit(solution)/shard_map/ppermute | solution.py:657
  86.9 12.9 %all-to-all-start.2 = ((bf16[8,64,256]{2,1,0:T(8,128)(2,1)}), bf16[8,64,256]{2,1,0:T(8,128)(2,1)S(1)}, u32[]{:S(2)}, u32[]{:S(2)}) async-start(bf16[8,64,256]{2,1,0:T(8,128)(2,1)} %shard_map.148), calls=%async_computation.2 | async-start | bytes 524288 | tf_op jit(solution)/shard_map/all_to_all | solution.py:661

commit v12 on v11

--- a/solution.py
+++ b/solution.py
@@ -233,31 +233,18 @@
 FACTOR = HD ** (-0.5) * math.log2(math.e)
 
 
-def load_pieces(sizes, in_refs, query_scr, key_scr, value_scr, sems):
+def load_pieces(sizes, in_refs, key_scr, value_scr):
     tok_rows, part_rows = sizes.tok_rows, sizes.part_rows
-    copies = []
     for src, ref in enumerate(in_refs):
         rows = pl.ds(src * tok_rows, tok_rows)
-        copies += [
-            pltpu.make_async_copy(ref.at[pl.ds(0, part_rows)], query_scr.at[src], sems.at[0, src]),
-            pltpu.make_async_copy(
-                ref.at[pl.ds(part_rows, tok_rows)], key_scr.at[rows], sems.at[1, src]
-            ),
-        ]
+        key_scr[rows, :] = ref[pl.ds(part_rows, tok_rows), :]
         for head in range(sizes.heads):
-            copies.append(
-                pltpu.make_async_copy(
-                    ref.at[pl.ds(part_rows + tok_rows, tok_rows), pl.ds(head * HD, HD)],
-                    value_scr.at[rows, pl.ds(2 * head * HD, HD)],
-                    sems.at[2 + head, src],
-                )
-            )
-    for copy in copies:
-        copy.start()
+            value_scr[rows, pl.ds(2 * head * HD, HD)] = ref[
+                pl.ds(part_rows + tok_rows, tok_rows), pl.ds(head * HD, HD)
+            ]
     ones = jnp.ones((len(in_refs) * tok_rows, HD), BF16)
     for head in range(sizes.heads):
         value_scr[:, pl.ds((2 * head + 1) * HD, HD)] = ones
-    return copies
 
 
 def soft_part(query, key_scr, value_scr, rows, head, before):
@@ -277,24 +264,22 @@
 def piece_scratch(sizes, count):
     lat_rows = count * sizes.tok_rows
     return [
-        pltpu.VMEM((count, sizes.part_rows, sizes.width), BF16),
         pltpu.VMEM((lat_rows, sizes.width), BF16),
         pltpu.VMEM((lat_rows, 2 * sizes.width), BF16),
-        pltpu.SemaphoreType.DMA((2 + sizes.heads, count)),
     ]
 
 
 def early_kernel(sizes, count, *refs):
     in_refs, refs = refs[:count], refs[count:]
-    sum_ref, stat_ref, query_scr, key_scr, value_scr, sems = refs
-    for copy in load_pieces(sizes, in_refs, query_scr, key_scr, value_scr, sems):
-        copy.wait()
+    sum_ref, stat_ref, key_scr, value_scr = refs
+    load_pieces(sizes, in_refs, key_scr, value_scr)
     left = lax.broadcasted_iota(jnp.int32, (sizes.part_rows, HD), 1) < HD // 2
     rows = pl.ds(0, count * sizes.tok_rows)
     for src in range(count):
         results = [
             soft_part(
-                query_scr[src, :, pl.ds(head * HD, HD)], key_scr, value_scr, rows, head, None
+                in_refs[src][pl.ds(0, sizes.part_rows), pl.ds(head * HD, HD)],
+                key_scr, value_scr, rows, head, None,
             )
             for head in range(sizes.heads)
         ]
@@ -309,7 +294,7 @@
     return pl.pallas_call(
         functools.partial(early_kernel, sizes, count),
         out_shape=(shape, shape),
-        in_specs=[ANY_SPEC] * count,
+        in_specs=[VMEM_SPEC] * count,
         out_specs=(VMEM_SPEC, VMEM_SPEC),
         scratch_shapes=piece_scratch(sizes, count),
         compiler_params=limits(12),
@@ -323,24 +308,18 @@
     in_refs, refs = refs[:count], refs[count:]
     kept_refs, refs = refs[: 2 if early else 0], refs[2 if early else 0 :]
     scale_ref, shift_ref, proj_ref, mod_ref, lat_ref, *refs = refs
-    query_scr, key_scr, value_scr, sems, scale_scr, shift_scr, proj_scr, side_sems, *kept_scr = refs
+    key_scr, value_scr, scale_scr, shift_scr, proj_scr, side_sems = refs
     half = part_rows // 2
     me = place_ref[0]
     mine = pl.ds(pl.multiple_of(place_ref[2] * width, HD), width)
-    copies = load_pieces(sizes, in_refs, query_scr, key_scr, value_scr, sems)
-    others = [
+    copies = [
         pltpu.make_async_copy(scale_ref.at[:, mine], scale_scr, side_sems.at[0]),
         pltpu.make_async_copy(shift_ref.at[:, mine], shift_scr, side_sems.at[1]),
         pltpu.make_async_copy(proj_ref.at[:, mine], proj_scr, side_sems.at[2]),
     ]
-    for slot, (ref, scr) in enumerate(zip(kept_refs, kept_scr)):
-        others.append(pltpu.make_async_copy(ref, scr, side_sems.at[3 + slot]))
-    for copy in others:
+    for copy in copies:
         copy.start()
-    for copy in copies + others:
-        copy.wait()
-    gain = 1.0 + scale_scr[...]
-    shift = shift_scr[...]
+    load_pieces(sizes, in_refs, key_scr, value_scr)
     together = 2
     for first in range(0, count, together):
         results = []
@@ -351,14 +330,19 @@
                 rows = pl.ds(0, count * tok_rows)
                 if src < early:
                     rows = pl.ds(early * tok_rows, (count - early) * tok_rows)
-                    stat = kept_scr[1][src, head]
-                    before = (kept_scr[0][src, head], stat[:, HD - 1 :], stat[:, :1])
-                query = query_scr[src, :, pl.ds(head * HD, HD)]
+                    stat = kept_refs[1][src, head]
+                    before = (kept_refs[0][src, head], stat[:, HD - 1 :], stat[:, :1])
+                query = in_refs[src][pl.ds(0, part_rows), pl.ds(head * HD, HD)]
                 value, total, _ = soft_part(query, key_scr, value_scr, rows, head, before)
                 mixed.append(value / total)
-            attended = jnp.concatenate(mixed, axis=1) if heads > 1 else mixed[0]
-            results.append((attended * gain + shift).astype(BF16))
-        for at, modulated in enumerate(results):
+            results.append(jnp.concatenate(mixed, axis=1) if heads > 1 else mixed[0])
+        if first == 0:
+            for copy in copies:
+                copy.wait()
+            gain = 1.0 + scale_scr[...]
+            shift = shift_scr[...]
+        for at, attended in enumerate(results):
+            modulated = (attended * gain + shift).astype(BF16)
             mod_ref[jnp.bitwise_xor(me, masks[first + at])] = modulated
     sides = [
         mm_nt(mod_ref[:, rows, :].reshape(count * half, width), proj_scr[...])
@@ -379,16 +363,15 @@
             jax.ShapeDtypeStruct((count, sizes.part_rows, width), BF16),
             jax.ShapeDtypeStruct((count, sizes.part_rows // 2, 2 * CH), BF16),
         ),
-        in_specs=[SMEM_SPEC] + [ANY_SPEC] * (count + len(kept)) + [HBM_SPEC] * 3,
+        in_specs=[SMEM_SPEC] + [VMEM_SPEC] * (count + len(kept)) + [HBM_SPEC] * 3,
         out_specs=(VMEM_SPEC, VMEM_SPEC),
         scratch_shapes=piece_scratch(sizes, count)
         + [
             pltpu.VMEM((1, width), F32),
             pltpu.VMEM((1, width), F32),
             pltpu.VMEM((CH, width), BF16),
-            pltpu.SemaphoreType.DMA((5,)),
-        ]
-        + [pltpu.VMEM(x.shape, F32) for x in kept],
+            pltpu.SemaphoreType.DMA((3,)),
+        ],
         compiler_params=limits(16),
         cost_estimate=pl.CostEstimate(
             flops=4 * query_rows * lat_rows * width,

time: 101 us -> 99.9 us (0.989)
  Pallas kernels: 21.4 us -> 18.8 us
  blocking collectives: 12.5 us -> 13.8 us
    pallas_call x1, Pallas kernels: 3.16 us -> 1.84 us  [attend_early(): pl.pallas_call(functools.partial(early_kernel, sizes, count), out_shape=(...]
    all_to_all x1, blocking collectives: 12.5 us -> 13.8 us  [all_to_all(): lax.all_to_all(x, 'seq', split_axis=0, concat_axis=0, tiled=True, axis_in...]
    pallas_call x1, Pallas kernels: 6.2 us -> 4.88 us  [attend(): pl.pallas_call(functools.partial(attend_kernel, sizes, masks, early), out...]
  transfers between devices with their start and end apart: 17 -> 17, of which waited for: 9 -> 9; matrix products, arithmetic and copies ran while one was open for 0% -> 0% of each run, Pallas kernels for 12% -> 10%
where the time goes in v12:
time: 99.9 us; the launch traced here: 99.3 us
  waiting for transfers between devices  38.8 us (39%)
  starting transfers between devices  26.4 us (26%)
  Pallas kernels  18.8 us (19%)
  blocking collectives  13.8 us (14%)
  between operations  1.39 us (1%)
    ppermute x14, waiting for transfers between devices, swap(): return lax.ppermute(x, axis, [(i, i ^ mask) for i in range(count)])  24.6 us
    ppermute x14, starting transfers between devices, swap(): return lax.ppermute(x, axis, [(i, i ^ mask) for i in range(count)])  18.2 us
    all_to_all x2, waiting for transfers between devices, all_to_all(): lax.all_to_all(x, 'seq', split_axis=0, concat_axis=0, tiled=True, axis_in...  14.2 us
    all_to_all x1, blocking collectives, all_to_all(): lax.all_to_all(x, 'seq', split_axis=0, concat_axis=0, tiled=True, axis_in...  13.8 us
    all_to_all x2, starting transfers between devices, all_to_all(): lax.all_to_all(x, 'seq', split_axis=0, concat_axis=0, tiled=True, axis_in...  6.8 us
    pallas_call x1, Pallas kernels, attend(): pl.pallas_call(functools.partial(attend_kernel, sizes, masks, early), out...  4.88 us
    pallas_call x1, Pallas kernels, reward_head(): pl.pallas_call(functools.partial(head_kernel, grid_rows, fused, embed_mas...  4.19 us
    pallas_call x1, Pallas kernels, spread(): pl.pallas_call(functools.partial(spread_kernel, count, half, heads), out_...  2.41 us
  transfers between devices with their start and end apart: 17, of which 9 were waited for; matrix products, arithmetic and copies ran while one was open for 0% of the time, Pallas kernels for 10%

profile of v12, /device:TPU:0, one launch (start us, length us, event | category | flops | bytes accessed | tf_op | source)
XLA Modules:
  0.0 99.3 jit_solution(5378087218004465260)
XLA Ops:
  0.6 1.9 %shard_map.139 = (bf16[384,256]{1,0:T(8,128)(2,1)S(1)}, bf16[384,256]{1,0:T(8,128)(2,1)S(1)}, bf16[384,256]{1,0:T(8,128)(2,1)S(1)}, bf16[544,256]{1,0:T(8,128)(2...) custom-call(bf16[1,128,2048]{2,1,0:T(8,128)(2,1)} %q_ref.1, ...), custom_call_target="tpu_custom_call" | custom-call | bytes 3145728 | tf_op jit(solution)/shard_map/pallas_call | solution.py:136
  2.6 4.1 %collective-permute-start.3 = (bf16[544,256]{1,0:T(8,128)(2,1)S(1)}, bf16[544,256]{1,0:T(8,128)(2,1)S(1)}, u32[]{:S(2)}, u32[]{:S(2)}) collective-permute-start(bf16[544,256]{1,0:T(8,128)(2,1)S(1)} %get-tuple-element.21), channel_id=1, source_target_pairs={{0,16},{4,20},{8,24},{12,28},{16,0},{20,4},{24,8},{28,12},{1,17},{... | collective-permute-start | bytes 835592 | tf_op jit(solution)/shard_map/ppermute | solution.py:640
  6.7 1.5 %collective-permute-start = (bf16[384,256]{1,0:T(8,128)(2,1)S(1)}, bf16[384,256]{1,0:T(8,128)(2,1)S(1)}, u32[]{:S(2)}, u32[]{:S(2)}) collective-permute-start(bf16[384,256]{1,0:T(8,128)(2,1)S(1)} %get-tuple-element.18), channel_id=1, source_target_pairs={{0,4},{4,0},{8,12},{12,8},{16,20},{20,16},{24,28},{28,24},{1,5},{5... | collective-permute-start | bytes 589832 | tf_op jit(solution)/shard_map/ppermute | solution.py:640
  8.2 1.6 %collective-permute-start.1 = (bf16[384,256]{1,0:T(8,128)(2,1)S(1)}, bf16[384,256]{1,0:T(8,128)(2,1)S(1)}, u32[]{:S(2)}, u32[]{:S(2)}) collective-permute-start(bf16[384,256]{1,0:T(8,128)(2,1)S(1)} %get-tuple-element.19), channel_id=1, source_target_pairs={{0,8},{4,12},{8,0},{12,4},{16,24},{20,28},{24,16},{28,20},{1,9},{5... | collective-permute-start | bytes 589832 | tf_op jit(solution)/shard_map/ppermute | solution.py:640
  10.2 1.3 %collective-permute-start.4 = (bf16[384,256]{1,0:T(8,128)(2,1)S(1)}, bf16[384,256]{1,0:T(8,128)(2,1)S(1)}, u32[]{:S(2)}, u32[]{:S(2)}) collective-permute-start(bf16[384,256]{1,0:T(8,128)(2,1)S(1)} %get-tuple-element.22), channel_id=1, source_target_pairs={{0,20},{4,16},{8,28},{12,24},{16,4},{20,0},{24,12},{28,8},{1,21},{... | collective-permute-start | bytes 589832 | tf_op jit(solution)/shard_map/ppermute | solution.py:640
  11.5 2.2 %collective-permute-done.refs_0_ = bf16[384,256]{1,0:T(8,128)(2,1)S(1)} collective-permute-done((bf16[384,256]{1,0:T(8,128)(2,1)S(1)}, bf16[384,256]{1,0:T(8,128)(2,1)S(1)}, u32[]{:S(2)}, u32[]{:S(2)}) %collective-permute-start) | collective-permute-done | bytes 196640 | tf_op jit(solution)/shard_map/ppermute | solution.py:640
  13.6 1.4 %collective-permute-start.5 = (bf16[384,256]{1,0:T(8,128)(2,1)S(1)}, bf16[384,256]{1,0:T(8,128)(2,1)S(1)}, u32[]{:S(2)}, u32[]{:S(2)}) collective-permute-start(bf16[384,256]{1,0:T(8,128)(2,1)S(1)} %get-tuple-element.24), channel_id=1, source_target_pairs={{0,24},{4,28},{8,16},{12,20},{16,8},{20,12},{24,0},{28,4},{1,25},{... | collective-permute-start | bytes 589832 | tf_op jit(solution)/shard_map/ppermute | solution.py:640
  15.1 5.2 %collective-permute-done.3.refs_3_.refs_0_ = bf16[544,256]{1,0:T(8,128)(2,1)S(1)} collective-permute-done((bf16[544,256]{1,0:T(8,128)(2,1)S(1)}, bf16[544,256]{1,0:T(8,128)(2,1)S(1)}, u32[]{:S(2)}, u32[]{:S(2)}) %collective-permute-start.3) | collective-permute-done | bytes 278560 | tf_op jit(solution)/shard_map/ppermute | solution.py:640
  20.2 3.8 %collective-permute-start.6 = (bf16[384,256]{1,0:T(8,128)(2,1)S(1)}, bf16[384,256]{1,0:T(8,128)(2,1)S(1)}, u32[]{:S(2)}, u32[]{:S(2)}) collective-permute-start(bf16[384,256]{1,0:T(8,128)(2,1)S(1)} %get-tuple-element.25), channel_id=1, source_target_pairs={{0,28},{4,24},{8,20},{12,16},{16,12},{20,8},{24,4},{28,0},{1,29},{... | collective-permute-start | bytes 589832 | tf_op jit(solution)/shard_map/ppermute | solution.py:640
  24.4 2.5 %collective-permute-done.2.refs_2_ = bf16[384,256]{1,0:T(8,128)(2,1)S(1)} collective-permute-done((bf16[384,256]{1,0:T(8,128)(2,1)S(1)}, bf16[384,256]{1,0:T(8,128)(2,1)S(1)}, u32[]{:S(2)}, u32[]{:S(2)}) %collective-permute-start.2) | collective-permute-done | bytes 196640 | tf_op jit(solution)/shard_map/ppermute | solution.py:640
  26.9 11.5 %collective-permute-done.4.refs_4_ = bf16[384,256]{1,0:T(8,128)(2,1)S(1)} collective-permute-done((bf16[384,256]{1,0:T(8,128)(2,1)S(1)}, bf16[384,256]{1,0:T(8,128)(2,1)S(1)}, u32[]{:S(2)}, u32[]{:S(2)}) %collective-permute-start.4) | collective-permute-done | bytes 196640 | tf_op jit(solution)/shard_map/ppermute | solution.py:640
  38.4 1.8 %shard_map.140 = (f32[6,2,128,128]{3,2,1,0:T(8,128)S(1)}, f32[6,2,128,128]{3,2,1,0:T(8,128)S(1)}) custom-call(bf16[384,256]{1,0:T(8,128)(2,1)S(1)} %collective-permute-done.refs_0_, bf16[384,256]{1,0:T(8,128)(2,1)S(1)} %collective-permute-done.1.refs_1_, bf16[384,256]{1,0:T(8,128)(2,1)S(1)} %collective-permute-done.2.refs_2_, ...), custom_call_target="tpu_custom_call" | custom-call | flops 1 | bytes 1 | tf_op jit(solution)/shard_map/pallas_call | solution.py:294
  40.5 1.8 %collective-permute-start.9 = (bf16[4,320,128]{2,1,0:T(8,128)(2,1)S(1)}, bf16[4,320,128]{2,1,0:T(8,128)(2,1)S(1)}, u32[]{:S(2)}, u32[]{:S(2)}) collective-permute-start(bf16[4,320,128]{2,1,0:T(8,128)(2,1)S(1)} %shard_map.144.refs_0_), channel_id=1, source_target_pairs={{0,2},{1,3},{2,0},{3,1},{4,6},{5,7},{6,4},{7,5},{8,10},{9,11},{10,... | collective-permute-start | bytes 983048 | tf_op jit(solution)/shard_map/ppermute | solution.py:640
  42.3 1.5 %collective-permute-start.10 = (bf16[4,320,128]{2,1,0:T(8,128)(2,1)S(1)}, bf16[4,320,128]{2,1,0:T(8,128)(2,1)S(1)}, u32[]{:S(2)}, u32[]{:S(2)}) collective-permute-start(bf16[4,320,128]{2,1,0:T(8,128)(2,1)S(1)} %shard_map.144.refs_0_), channel_id=1, source_target_pairs={{0,6},{1,7},{2,4},{3,5},{4,2},{5,3},{6,0},{7,1},{8,14},{9,15},{10,... | collective-permute-start | bytes 983048 | tf_op jit(solution)/shard_map/ppermute | solution.py:656
  43.8 4.9 %shard_map.141 = (bf16[8,128,256]{2,1,0:T(8,128)(2,1)S(1)}, bf16[8,64,128]{2,1,0:T(8,128)(2,1)S(1)}) custom-call(s32[3]{0:T(128)S(1)} %pad_add_fusion.place_ref, bf16[384,256]{1,0:T(8,128)(2,1)S(1)} %collective-permute-done.refs_0_, bf16[384,256]{1,0:T(8,128)(2,1)S(1)} %collective-permute-done.1.refs_1_, ...), custom_call_target="tpu_custom_call" | custom-call | flops 1073741824 | bytes 2097152 | tf_op jit(solution)/shard_map/pallas_call | solution.py:360
  48.7 13.8 %all_to_all.15.refs_0_ = bf16[8,64,128]{2,1,0:T(8,128)(2,1)S(1)} all-to-all(bf16[8,64,128]{2,1,0:T(8,128)(2,1)S(1)} %get-tuple-element.28), channel_id=1, replica_groups=mesh['seq'=8,'dp'=4] {'seq'}, dimensions={0} | all-to-all | bytes 262144 | tf_op jit(solution)/shard_map/all_to_all | solution.py:644
  64.5 3.4 %all-to-all-start.1 = ((bf16[8,64,128]{2,1,0:T(8,128)(2,1)}), bf16[8,64,128]{2,1,0:T(8,128)(2,1)S(1)}, u32[]{:S(2)}, u32[]{:S(2)}) async-start(bf16[8,64,128]{2,1,0:T(8,128)(2,1)} %shard_map.142.refs_4_), calls=%async_computation.1 | async-start | bytes 262144 | tf_op jit(solution)/shard_map/all_to_all | solution.py:644
  68.5 7.2 %all-to-all-done.1 = bf16[8,64,128]{2,1,0:T(8,128)(2,1)S(1)} async-done(((bf16[8,64,128]{2,1,0:T(8,128)(2,1)}), bf16[8,64,128]{2,1,0:T(8,128)(2,1)S(1)}, u32[]{:S(2)}, u32[]{:S(2)}) %all-to-all-start.1) | async-done | bytes 131104 | tf_op jit(solution)/shard_map/all_to_all | solution.py:644
  75.7 4.2 %shard_map.146 = (f32[1,128]{1,0:T(1,128)}, bf16[512,128]{1,0:T(8,128)(2,1)S(1)}, bf16[64,256]{1,0:T(8,128)(2,1)S(1)}) custom-call(s32[3]{0:T(128)S(1)} %pad_add_fusion.place_ref, bf16[512,128]{1,0:T(8,128)(2,1)S(1)} %bitcast.7, bf16[2,256,1280]{2,1,0:T(8,128)(2,1)S(1)} %shard_map.145.refs_0_, bf16[2,256,1280]{2,1,0:T(8,128)(2,1)S(1)} %collective-permute-done.11.refs_1_, ...), custom_call_target="tpu_custom_call" | custom-call | flops 503316480 | bytes 2785280 | tf_op jit(solution)/shard_map/pallas_call | solution.py:529
  80.0 1.6 %collective-permute-start.13 = (bf16[64,256]{1,0:T(8,128)(2,1)S(1)}, bf16[64,256]{1,0:T(8,128)(2,1)S(1)}, u32[]{:S(2)}, u32[]{:S(2)}) collective-permute-start(bf16[64,256]{1,0:T(8,128)(2,1)S(1)} %get-tuple-element.32.refs_0_), channel_id=1, source_target_pairs={{0,2},{1,3},{2,0},{3,1},{4,6},{5,7},{6,4},{7,5},{8,10},{9,11},{10,... | collective-permute-start | bytes 98312 | tf_op jit(solution)/shard_map/ppermute | solution.py:640
  81.9 2.1 %collective-permute-done.13.refs_2_ = bf16[64,256]{1,0:T(8,128)(2,1)S(1)} collective-permute-done((bf16[64,256]{1,0:T(8,128)(2,1)S(1)}, bf16[64,256]{1,0:T(8,128)(2,1)S(1)}, u32[]{:S(2)}, u32[]{:S(2)}) %collective-permute-start.13) | collective-permute-done | bytes 32800 | tf_op jit(solution)/shard_map/ppermute | solution.py:640
  85.6 3.4 %all-to-all-start.2 = ((bf16[8,64,256]{2,1,0:T(8,128)(2,1)}), bf16[8,64,256]{2,1,0:T(8,128)(2,1)S(1)}, u32[]{:S(2)}, u32[]{:S(2)}) async-start(bf16[8,64,256]{2,1,0:T(8,128)(2,1)} %shard_map.148), calls=%async_computation.2 | async-start | bytes 524288 | tf_op jit(solution)/shard_map/all_to_all | solution.py:644
  89.1 2.4 %shard_map.147 = bf16[1,2,1024,128]{3,2,1,0:T(8,128)(2,1)} custom-call(s32[3]{0:T(128)S(1)} %pad_add_fusion.place_ref, bf16[512,128]{1,0:T(8,128)(2,1)S(1)} %get-tuple-element.31.grad_ref, f32[1,2048]{1,0:T(1,128)} %scale_ref.1, bf16[64,2048]{1,0:T(8,128)(2,1)} %bitcast.10), custom_call_target="tpu_custom_call" | custom-call | flops 67108864 | bytes 524288 | tf_op jit(solution)/shard_map/pallas_call | solution.py:589
  91.5 7.0 %all-to-all-done.2.in_ref = bf16[8,64,256]{2,1,0:T(8,128)(2,1)S(1)} async-done(((bf16[8,64,256]{2,1,0:T(8,128)(2,1)}), bf16[8,64,256]{2,1,0:T(8,128)(2,1)S(1)}, u32[]{:S(2)}, u32[]{:S(2)}) %all-to-all-start.2) | async-done | bytes 262176 | tf_op jit(solution)/shard_map/all_to_all | solution.py:644
  (23 shorter events, 5.9 us)
Async XLA Ops:
  2.6 17.7 %collective-permute-start.3 = (bf16[544,256]{1,0:T(8,128)(2,1)S(1)}, bf16[544,256]{1,0:T(8,128)(2,1)S(1)}, u32[]{:S(2)}, u32[]{:S(2)}) collective-permute-start(bf16[544,256]{1,0:T(8,128)(2,1)S(1)} %get-tuple-element.21), channel_id=1, source_target_pairs={{0,16},{4,20},{8,24},{12,28},{16,0},{20,4},{24,8},{28,12},{1,17},{... | collective-permute-start | bytes 835592 | tf_op jit(solution)/shard_map/ppermute | solution.py:640
  6.7 6.9 %collective-permute-start = (bf16[384,256]{1,0:T(8,128)(2,1)S(1)}, bf16[384,256]{1,0:T(8,128)(2,1)S(1)}, u32[]{:S(2)}, u32[]{:S(2)}) collective-permute-start(bf16[384,256]{1,0:T(8,128)(2,1)S(1)} %get-tuple-element.18), channel_id=1, source_target_pairs={{0,4},{4,0},{8,12},{12,8},{16,20},{20,16},{24,28},{28,24},{1,5},{5... | collective-permute-start | bytes 589832 | tf_op jit(solution)/shard_map/ppermute | solution.py:640
  8.2 16.1 %collective-permute-start.1 = (bf16[384,256]{1,0:T(8,128)(2,1)S(1)}, bf16[384,256]{1,0:T(8,128)(2,1)S(1)}, u32[]{:S(2)}, u32[]{:S(2)}) collective-permute-start(bf16[384,256]{1,0:T(8,128)(2,1)S(1)} %get-tuple-element.19), channel_id=1, source_target_pairs={{0,8},{4,12},{8,0},{12,4},{16,24},{20,28},{24,16},{28,20},{1,9},{5... | collective-permute-start | bytes 589832 | tf_op jit(solution)/shard_map/ppermute | solution.py:640
  9.8 17.1 %collective-permute-start.2 = (bf16[384,256]{1,0:T(8,128)(2,1)S(1)}, bf16[384,256]{1,0:T(8,128)(2,1)S(1)}, u32[]{:S(2)}, u32[]{:S(2)}) collective-permute-start(bf16[384,256]{1,0:T(8,128)(2,1)S(1)} %get-tuple-element.20), channel_id=1, source_target_pairs={{0,12},{4,8},{8,4},{12,0},{16,28},{20,24},{24,20},{28,16},{1,13},{... | collective-permute-start | bytes 589832 | tf_op jit(solution)/shard_map/ppermute | solution.py:640
  10.2 28.2 %collective-permute-start.4 = (bf16[384,256]{1,0:T(8,128)(2,1)S(1)}, bf16[384,256]{1,0:T(8,128)(2,1)S(1)}, u32[]{:S(2)}, u32[]{:S(2)}) collective-permute-start(bf16[384,256]{1,0:T(8,128)(2,1)S(1)} %get-tuple-element.22), channel_id=1, source_target_pairs={{0,20},{4,16},{8,28},{12,24},{16,4},{20,0},{24,12},{28,8},{1,21},{... | collective-permute-start | bytes 589832 | tf_op jit(solution)/shard_map/ppermute | solution.py:640
  13.6 30.2 %collective-permute-start.5 = (bf16[384,256]{1,0:T(8,128)(2,1)S(1)}, bf16[384,256]{1,0:T(8,128)(2,1)S(1)}, u32[]{:S(2)}, u32[]{:S(2)}) collective-permute-start(bf16[384,256]{1,0:T(8,128)(2,1)S(1)} %get-tuple-element.24), channel_id=1, source_target_pairs={{0,24},{4,28},{8,16},{12,20},{16,8},{20,12},{24,0},{28,4},{1,25},{... | collective-permute-start | bytes 589832 | tf_op jit(solution)/shard_map/ppermute | solution.py:640
  20.2 23.6 %collective-permute-start.6 = (bf16[384,256]{1,0:T(8,128)(2,1)S(1)}, bf16[384,256]{1,0:T(8,128)(2,1)S(1)}, u32[]{:S(2)}, u32[]{:S(2)}) collective-permute-start(bf16[384,256]{1,0:T(8,128)(2,1)S(1)} %get-tuple-element.25), channel_id=1, source_target_pairs={{0,28},{4,24},{8,20},{12,16},{16,12},{20,8},{24,4},{28,0},{1,29},{... | collective-permute-start | bytes 589832 | tf_op jit(solution)/shard_map/ppermute | solution.py:640
  24.3 15.9 %collective-permute-start.7 = (bf16[2,320,128]{2,1,0:T(8,128)(2,1)S(1)}, bf16[2,320,128]{2,1,0:T(8,128)(2,1)S(1)}, u32[]{:S(2)}, u32[]{:S(2)}) collective-permute-start(bf16[2,320,128]{2,1,0:T(8,128)(2,1)S(1)} %shard_map.143.first_ref), channel_id=1, source_target_pairs={{0,8},{4,12},{8,0},{12,4},{16,24},{20,28},{24,16},{28,20},{1,9},{5... | collective-permute-start | bytes 491528 | tf_op jit(solution)/shard_map/ppermute | solution.py:640
  40.3 22.9 %collective-permute-start.8 = (bf16[4,320,128]{2,1,0:T(8,128)(2,1)S(1)}, bf16[4,320,128]{2,1,0:T(8,128)(2,1)S(1)}, u32[]{:S(2)}, u32[]{:S(2)}) collective-permute-start(bf16[4,320,128]{2,1,0:T(8,128)(2,1)S(1)} %shard_map.144.refs_0_), channel_id=1, source_target_pairs={{0,4},{4,0},{8,12},{12,8},{16,20},{20,16},{24,28},{28,24},{1,5},{5... | collective-permute-start | bytes 983048 | tf_op jit(solution)/shard_map/ppermute | solution.py:640
  40.5 22.7 %collective-permute-start.9 = (bf16[4,320,128]{2,1,0:T(8,128)(2,1)S(1)}, bf16[4,320,128]{2,1,0:T(8,128)(2,1)S(1)}, u32[]{:S(2)}, u32[]{:S(2)}) collective-permute-start(bf16[4,320,128]{2,1,0:T(8,128)(2,1)S(1)} %shard_map.144.refs_0_), channel_id=1, source_target_pairs={{0,2},{1,3},{2,0},{3,1},{4,6},{5,7},{6,4},{7,5},{8,10},{9,11},{10,... | collective-permute-start | bytes 983048 | tf_op jit(solution)/shard_map/ppermute | solution.py:640
  42.3 20.9 %collective-permute-start.10 = (bf16[4,320,128]{2,1,0:T(8,128)(2,1)S(1)}, bf16[4,320,128]{2,1,0:T(8,128)(2,1)S(1)}, u32[]{:S(2)}, u32[]{:S(2)}) collective-permute-start(bf16[4,320,128]{2,1,0:T(8,128)(2,1)S(1)} %shard_map.144.refs_0_), channel_id=1, source_target_pairs={{0,6},{1,7},{2,4},{3,5},{4,2},{5,3},{6,0},{7,1},{8,14},{9,15},{10,... | collective-permute-start | bytes 983048 | tf_op jit(solution)/shard_map/ppermute | solution.py:656
  64.4 11.3 %collective-permute-start.11 = (bf16[2,256,1280]{2,1,0:T(8,128)(2,1)S(1)}, bf16[2,256,1280]{2,1,0:T(8,128)(2,1)S(1)}, u32[]{:S(2)}, u32[]{:S(2)}) collective-permute-start(bf16[2,256,1280]{2,1,0:T(8,128)(2,1)S(1)} %shard_map.145.refs_0_), channel_id=1, source_target_pairs={{0,1},{1,0},{2,3},{3,2},{4,5},{5,4},{6,7},{7,6},{8,9},{9,8},{10,11... | collective-permute-start | bytes 3932168 | tf_op jit(solution)/shard_map/ppermute | solution.py:640
  64.5 11.2 %all-to-all-start.1 = ((bf16[8,64,128]{2,1,0:T(8,128)(2,1)}), bf16[8,64,128]{2,1,0:T(8,128)(2,1)S(1)}, u32[]{:S(2)}, u32[]{:S(2)}) async-start(bf16[8,64,128]{2,1,0:T(8,128)(2,1)} %shard_map.142.refs_4_), calls=%async_computation.1 | async-start | bytes 262144 | tf_op jit(solution)/shard_map/all_to_all | solution.py:644
  79.9 1.9 %collective-permute-start.12 = (bf16[64,256]{1,0:T(8,128)(2,1)S(1)}, bf16[64,256]{1,0:T(8,128)(2,1)S(1)}, u32[]{:S(2)}, u32[]{:S(2)}) collective-permute-start(bf16[64,256]{1,0:T(8,128)(2,1)S(1)} %get-tuple-element.32.refs_0_), channel_id=1, source_target_pairs={{0,1},{1,0},{2,3},{3,2},{4,5},{5,4},{6,7},{7,6},{8,9},{9,8},{10,11... | collective-permute-start | bytes 98312 | tf_op jit(solution)/shard_map/ppermute | solution.py:640
  80.0 4.0 %collective-permute-start.13 = (bf16[64,256]{1,0:T(8,128)(2,1)S(1)}, bf16[64,256]{1,0:T(8,128)(2,1)S(1)}, u32[]{:S(2)}, u32[]{:S(2)}) collective-permute-start(bf16[64,256]{1,0:T(8,128)(2,1)S(1)} %get-tuple-element.32.refs_0_), channel_id=1, source_target_pairs={{0,2},{1,3},{2,0},{3,1},{4,6},{5,7},{6,4},{7,5},{8,10},{9,11},{10,... | collective-permute-start | bytes 98312 | tf_op jit(solution)/shard_map/ppermute | solution.py:640
  81.6 3.3 %collective-permute-start.14 = (bf16[64,256]{1,0:T(8,128)(2,1)S(1)}, bf16[64,256]{1,0:T(8,128)(2,1)S(1)}, u32[]{:S(2)}, u32[]{:S(2)}) collective-permute-start(bf16[64,256]{1,0:T(8,128)(2,1)S(1)} %get-tuple-element.32.refs_0_), channel_id=1, source_target_pairs={{0,3},{1,2},{2,1},{3,0},{4,7},{5,6},{6,5},{7,4},{8,11},{9,10},{10,... | collective-permute-start | bytes 98312 | tf_op jit(solution)/shard_map/ppermute | solution.py:640
  85.6 12.9 %all-to-all-start.2 = ((bf16[8,64,256]{2,1,0:T(8,128)(2,1)}), bf16[8,64,256]{2,1,0:T(8,128)(2,1)S(1)}, u32[]{:S(2)}, u32[]{:S(2)}) async-start(bf16[8,64,256]{2,1,0:T(8,128)(2,1)} %shard_map.148), calls=%async_computation.2 | async-start | bytes 524288 | tf_op jit(solution)/shard_map/all_to_all | solution.py:644

commit v13 on v12

--- a/solution.py
+++ b/solution.py
@@ -230,6 +230,32 @@
     )(place, *flat, wait)
 
 
+def fetch_kernel(sizes, place_ref, *refs):
+    count = len(refs) // 2
+    sems = refs[-1]
+    mine = pl.ds(pl.multiple_of(place_ref[2] * sizes.width, HD), sizes.width)
+    copies = []
+    for slot in range(count):
+        source = refs[slot].at[:, mine] if slot < 3 else refs[slot]
+        copies.append(pltpu.make_async_copy(source, refs[count + slot], sems.at[slot]))
+        copies[-1].start()
+    for copy in copies:
+        copy.wait()
+
+
+def fetch(sizes, place, arrays):
+    shapes = [x.shape if slot >= 3 else (x.shape[0], sizes.width) for slot, x in enumerate(arrays)]
+    return pl.pallas_call(
+        functools.partial(fetch_kernel, sizes),
+        out_shape=[jax.ShapeDtypeStruct(shape, x.dtype) for shape, x in zip(shapes, arrays)],
+        in_specs=[SMEM_SPEC] + [HBM_SPEC] * len(arrays),
+        out_specs=[VMEM_SPEC] * len(arrays),
+        scratch_shapes=[pltpu.SemaphoreType.DMA((len(arrays),))],
+        compiler_params=limits(),
+        cost_estimate=pl.CostEstimate(flops=1, bytes_accessed=1, transcendentals=0),
+    )(place, *[in_hbm(x) for x in arrays])
+
+
 FACTOR = HD ** (-0.5) * math.log2(math.e)
 
 
@@ -270,7 +296,7 @@
 
 
 def early_kernel(sizes, count, *refs):
-    in_refs, refs = refs[:count], refs[count:]
+    in_refs, refs = refs[:count], refs[count + 1 :]
     sum_ref, stat_ref, key_scr, value_scr = refs
     load_pieces(sizes, in_refs, key_scr, value_scr)
     left = lax.broadcasted_iota(jnp.int32, (sizes.part_rows, HD), 1) < HD // 2
@@ -288,18 +314,18 @@
             stat_ref[src, head] = jnp.where(left, top, total)
 
 
-def attend_early(sizes, received):
+def attend_early(sizes, received, wait):
     count = len(received)
     shape = jax.ShapeDtypeStruct((count, sizes.heads, sizes.part_rows, HD), F32)
     return pl.pallas_call(
         functools.partial(early_kernel, sizes, count),
         out_shape=(shape, shape),
-        in_specs=[VMEM_SPEC] * count,
+        in_specs=[VMEM_SPEC] * (count + 1),
         out_specs=(VMEM_SPEC, VMEM_SPEC),
         scratch_shapes=piece_scratch(sizes, count),
         compiler_params=limits(12),
         cost_estimate=pl.CostEstimate(flops=1, bytes_accessed=1, transcendentals=0),
-    )(*received)
+    )(*received, wait)
 
 
 def attend_kernel(sizes, masks, early, place_ref, *refs):
@@ -308,17 +334,11 @@
     in_refs, refs = refs[:count], refs[count:]
     kept_refs, refs = refs[: 2 if early else 0], refs[2 if early else 0 :]
     scale_ref, shift_ref, proj_ref, mod_ref, lat_ref, *refs = refs
-    key_scr, value_scr, scale_scr, shift_scr, proj_scr, side_sems = refs
+    key_scr, value_scr = refs
     half = part_rows // 2
     me = place_ref[0]
-    mine = pl.ds(pl.multiple_of(place_ref[2] * width, HD), width)
-    copies = [
-        pltpu.make_async_copy(scale_ref.at[:, mine], scale_scr, side_sems.at[0]),
-        pltpu.make_async_copy(shift_ref.at[:, mine], shift_scr, side_sems.at[1]),
-        pltpu.make_async_copy(proj_ref.at[:, mine], proj_scr, side_sems.at[2]),
-    ]
-    for copy in copies:
-        copy.start()
+    gain = 1.0 + scale_ref[...]
+    shift = shift_ref[...]
     load_pieces(sizes, in_refs, key_scr, value_scr)
     together = 2
     for first in range(0, count, together):
@@ -336,16 +356,11 @@
                 value, total, _ = soft_part(query, key_scr, value_scr, rows, head, before)
                 mixed.append(value / total)
             results.append(jnp.concatenate(mixed, axis=1) if heads > 1 else mixed[0])
-        if first == 0:
-            for copy in copies:
-                copy.wait()
-            gain = 1.0 + scale_scr[...]
-            shift = shift_scr[...]
         for at, attended in enumerate(results):
             modulated = (attended * gain + shift).astype(BF16)
             mod_ref[jnp.bitwise_xor(me, masks[first + at])] = modulated
     sides = [
-        mm_nt(mod_ref[:, rows, :].reshape(count * half, width), proj_scr[...])
+        mm_nt(mod_ref[:, rows, :].reshape(count * half, width), proj_ref[...])
         for rows in (slice(0, half), slice(half, part_rows))
     ]
     latent = jnp.concatenate(sides, axis=1).astype(BF16)
@@ -363,15 +378,9 @@
             jax.ShapeDtypeStruct((count, sizes.part_rows, width), BF16),
             jax.ShapeDtypeStruct((count, sizes.part_rows // 2, 2 * CH), BF16),
         ),
-        in_specs=[SMEM_SPEC] + [VMEM_SPEC] * (count + len(kept)) + [HBM_SPEC] * 3,
+        in_specs=[SMEM_SPEC] + [VMEM_SPEC] * (count + len(kept) + 3),
         out_specs=(VMEM_SPEC, VMEM_SPEC),
-        scratch_shapes=piece_scratch(sizes, count)
-        + [
-            pltpu.VMEM((1, width), F32),
-            pltpu.VMEM((1, width), F32),
-            pltpu.VMEM((CH, width), BF16),
-            pltpu.SemaphoreType.DMA((3,)),
-        ],
+        scratch_shapes=piece_scratch(sizes, count),
         compiler_params=limits(16),
         cost_estimate=pl.CostEstimate(
             flops=4 * query_rows * lat_rows * width,
@@ -409,19 +418,11 @@
 
 def head_kernel(grid_rows, fused, embed_masks, out_factor, place_ref, lat_ref, *refs):
     embed_refs, refs = refs[: len(embed_masks)], refs[len(embed_masks) :]
-    sides, refs = refs[:4], refs[4:]
-    cot_ref, refs = refs[0], refs[1:]
-    mod_ref, refs = refs[0], refs[1:]
-    reward_ref, grad_ref, weight_ref, lat_scr, grad_scr, block_scr, back_scr, *refs = refs
-    pos_ref, pre_ref, post_ref, prompt_ref, side_sems = refs
+    pos_ref, pre_ref, post_ref, prompt_ref, cot_ref, mod_ref, *refs = refs
+    reward_ref, grad_ref, weight_ref, lat_scr, grad_scr, block_scr, back_scr = refs
     patch_rows = grid_rows // 4
     patch_cols = GW // 4
     patches = patch_rows * patch_cols
-    copies = []
-    for slot, (side, scr) in enumerate(zip(sides, (pos_ref, pre_ref, post_ref, prompt_ref))):
-        copies.append(pltpu.make_async_copy(side, scr, side_sems.at[slot]))
-    for copy in copies:
-        copy.start()
     lat_scr[...] = lat_ref[...].astype(F32)
 
     data = place_ref[1]
@@ -449,8 +450,6 @@
             else:
                 for at in range(0, 4 * CH, share_rows):
                     block_scr[(first + at) // share_rows] = line[:, at : at + share_rows]
-    for copy in copies:
-        copy.wait()
     embedded = pos_ref[...].astype(F32)
     for number, ref, slot in shares:
         embedded = embedded + mm(block_scr[number], ref[slot])
@@ -535,7 +534,7 @@
         ),
         in_specs=[SMEM_SPEC, VMEM_SPEC]
         + [VMEM_SPEC] * len(embed_arrays)
-        + [HBM_SPEC] * 4
+        + [VMEM_SPEC] * 4
         + [SMEM_SPEC, VMEM_SPEC],
         out_specs=(VMEM_SPEC, VMEM_SPEC, VMEM_SPEC),
         scratch_shapes=[
@@ -543,11 +542,6 @@
             pltpu.VMEM((rows, 2 * CH), F32),
             pltpu.VMEM((16 * CH // share_rows, patches, share_rows), BF16),
             pltpu.VMEM((16 * CH // share_rows, patches, share_rows), F32),
-            pltpu.VMEM((patches, VW), BF16),
-            pltpu.VMEM((VW,), F32),
-            pltpu.VMEM((VW,), F32),
-            pltpu.VMEM((1, VW), F32),
-            pltpu.SemaphoreType.DMA((4,)),
         ],
         compiler_params=limits(16),
         cost_estimate=pl.CostEstimate(
@@ -558,21 +552,9 @@
     )(place, latent, *embed_arrays, pos, pre, post, prompt, cot, modulated)
 
 
-def spread_kernel(
-    count, half, heads, place_ref, grad_ref, scale_ref, proj_ref, out_ref, scale_scr, proj_scr, sems
-):
-    width = heads * HD
-    mine = pl.ds(pl.multiple_of(place_ref[2] * width, HD), width)
-    copies = [
-        pltpu.make_async_copy(scale_ref.at[:, mine], scale_scr, sems.at[0]),
-        pltpu.make_async_copy(proj_ref.at[:, mine], proj_scr, sems.at[1]),
-    ]
-    for copy in copies:
-        copy.start()
-    for copy in copies:
-        copy.wait()
-    gain = 1.0 + scale_scr[...]
-    proj = proj_scr[...]
+def spread_kernel(count, half, heads, grad_ref, scale_ref, proj_ref, out_ref):
+    gain = 1.0 + scale_ref[...]
+    proj = proj_ref[...]
     zero = jnp.zeros_like(proj)
     sides = (jnp.concatenate([proj, zero], axis=0), jnp.concatenate([zero, proj], axis=0))
     for src in range(count):
@@ -585,24 +567,19 @@
                 ]
 
 
-def spread(place, grad, scales, proj, count, half, heads):
+def spread(grad, scales, proj, count, half, heads):
     return pl.pallas_call(
         functools.partial(spread_kernel, count, half, heads),
         out_shape=jax.ShapeDtypeStruct((1, heads, 2 * count * half, HD), BF16),
-        in_specs=[SMEM_SPEC, VMEM_SPEC, HBM_SPEC, HBM_SPEC],
+        in_specs=[VMEM_SPEC] * 3,
         out_specs=VMEM_SPEC,
-        scratch_shapes=[
-            pltpu.VMEM((1, heads * HD), F32),
-            pltpu.VMEM((CH, heads * HD), BF16),
-            pltpu.SemaphoreType.DMA((2,)),
-        ],
         compiler_params=limits(),
         cost_estimate=pl.CostEstimate(
             flops=8 * count * half * CH * heads * HD,
             bytes_accessed=4 * count * half * heads * HD,
             transcendentals=0,
         ),
-    )(place, grad, scales, proj)
+    )(grad, scales, proj)
 
 
 def weight_kernel(out_factor, grad_ref, *refs):
@@ -694,11 +671,15 @@
     received = [swap(x, "seq", mask) if mask else x for mask, x in zip(masks, packed)]
     bits = [1 << b for b in reversed(range(data_count.bit_length() - 1))]
     shared = sizes.share < patch_embed.shape[0]
+    scale, shift, proj, pos, pre, post, words = fetch(
+        sizes, place, [scales, shifts, proj_turned, pos_embed, pre_gain, post_gain, prompt]
+    )
+
     kept, order = [], list(range(seq_count))
     if seq_count == 8:
         late = [slot for slot, mask in enumerate(masks) if mask in (6, 7)]
         order = [slot for slot in order if slot not in late]
-        kept = attend_early(sizes, [received[slot] for slot in order])
+        kept = attend_early(sizes, [received[slot] for slot in order], scale)
         order = order + late
     if sizes.riding:
         ride = [slot for slot, mask in enumerate(masks) if sizes.rides(mask)]
@@ -713,7 +694,7 @@
 
     modulated, latent_part = attend(
         sizes, [masks[slot] for slot in order], place, [received[slot] for slot in order], kept,
-        in_hbm(scales), in_hbm(shifts), in_hbm(proj_turned)
+        scale, shift, proj,
     )
 
     if not sizes.riding:
@@ -746,7 +727,7 @@
         latent = latent.transpose(0, 2, 1, 3).reshape(lat_rows // 2, 2 * CH)
 
     reward, grad, weight = reward_head(
-        place, latent, embed, in_hbm(pos_embed), in_hbm(pre_gain), in_hbm(post_gain), in_hbm(prompt),
+        place, latent, embed, pos, pre, post, words,
         cotangent, modulated, grid_rows, canonical, out_factor,
     )
     if not canonical:
@@ -757,7 +738,7 @@
         weight = weight_call(grad, modulated, out_factor)
 
     parts = [weight] + [swap(weight, "dp", mask) for mask in range(1, data_count)]
-    attn_grad = spread(place, grad, in_hbm(scales), in_hbm(proj_turned), seq_count, half, head_count)
+    attn_grad = spread(grad, scale, proj, seq_count, half, head_count)
     if query_parts > 1:
         total = total_copies(parts, 1)[0]
         parts = [total] + [swap(total, "seq", mask) for mask in range(1, query_parts)]

time: 99.9 us -> 98.4 us (0.985)
  Pallas kernels: 18.8 us -> 17.1 us
  local copies, waits for them, and re-layouts: 0 us -> 1.55 us
  waiting for transfers between devices: 38.8 us -> 37.7 us
    ppermute x14, waiting for transfers between devices: 24.6 us -> 22.9 us  [swap(): return lax.ppermute(x, axis, [(i, i ^ mask) for i in range(count)])]
    pallas_call x0 -> x1, Pallas kernels: none -> 1.58 us  [fetch(): pl.pallas_call(functools.partial(fetch_kernel, sizes), out_shape=[jax.Sha...]
    unnamed x0 -> x4, local copies, waits for them, and re-layouts: none -> 1.55 us
    pallas_call x1, Pallas kernels: 2.41 us -> 1.08 us  [spread(): pl.pallas_call(functools.partial(spread_kernel, count, half, heads), out_...]
    pallas_call x1, Pallas kernels: 4.88 us -> 3.83 us  [attend(): pl.pallas_call(functools.partial(attend_kernel, sizes, masks, early), out...]
  transfers between devices with their start and end apart: 17 -> 17, of which waited for: 9 -> 9; matrix products, arithmetic and copies ran while one was open for 0% -> 0% of each run, Pallas kernels for 10% -> 9%
where the time goes in v13:
time: 98.4 us; the launch traced here: 98 us
  waiting for transfers between devices  37.7 us (38%)
  starting transfers between devices  26.4 us (27%)
  Pallas kernels  17.1 us (17%)
  blocking collectives  13.8 us (14%)
  local copies, waits for them, and re-layouts  1.55 us (2%)
  between operations  1.4 us (1%)
    ppermute x14, waiting for transfers between devices, swap(): return lax.ppermute(x, axis, [(i, i ^ mask) for i in range(count)])  22.9 us
    ppermute x14, starting transfers between devices, swap(): return lax.ppermute(x, axis, [(i, i ^ mask) for i in range(count)])  18.1 us
    all_to_all x2, waiting for transfers between devices, all_to_all(): lax.all_to_all(x, 'seq', split_axis=0, concat_axis=0, tiled=True, axis_in...  14.7 us
    all_to_all x1, blocking collectives, all_to_all(): lax.all_to_all(x, 'seq', split_axis=0, concat_axis=0, tiled=True, axis_in...  13.8 us
    all_to_all x2, starting transfers between devices, all_to_all(): lax.all_to_all(x, 'seq', split_axis=0, concat_axis=0, tiled=True, axis_in...  6.8 us
    pallas_call x1, Pallas kernels, attend(): pl.pallas_call(functools.partial(attend_kernel, sizes, masks, early), out...  3.83 us
    pallas_call x1, Pallas kernels, reward_head(): pl.pallas_call(functools.partial(head_kernel, grid_rows, fused, embed_mas...  3.32 us
  transfers between devices with their start and end apart: 17, of which 9 were waited for; matrix products, arithmetic and copies ran while one was open for 0% of the time, Pallas kernels for 9%

profile of v13, /device:TPU:0, one launch (start us, length us, event | category | flops | bytes accessed | tf_op | source)
XLA Modules:
  0.0 98.0 jit_solution(7915435710607199509)
XLA Ops:
  0.6 1.9 %shard_map.139 = (bf16[384,256]{1,0:T(8,128)(2,1)S(1)}, bf16[384,256]{1,0:T(8,128)(2,1)S(1)}, bf16[384,256]{1,0:T(8,128)(2,1)S(1)}, bf16[544,256]{1,0:T(8,128)(2...) custom-call(bf16[1,128,2048]{2,1,0:T(8,128)(2,1)} %q_ref.1, ...), custom_call_target="tpu_custom_call" | custom-call | bytes 3145728 | tf_op jit(solution)/shard_map/pallas_call | solution.py:136
  2.6 4.1 %collective-permute-start.3 = (bf16[544,256]{1,0:T(8,128)(2,1)S(1)}, bf16[544,256]{1,0:T(8,128)(2,1)S(1)}, u32[]{:S(2)}, u32[]{:S(2)}) collective-permute-start(bf16[544,256]{1,0:T(8,128)(2,1)S(1)} %get-tuple-element.28), channel_id=1, source_target_pairs={{0,16},{4,20},{8,24},{12,28},{16,0},{20,4},{24,8},{28,12},{1,17},{... | collective-permute-start | bytes 835592 | tf_op jit(solution)/shard_map/ppermute | solution.py:617
  6.7 1.5 %collective-permute-start = (bf16[384,256]{1,0:T(8,128)(2,1)S(1)}, bf16[384,256]{1,0:T(8,128)(2,1)S(1)}, u32[]{:S(2)}, u32[]{:S(2)}) collective-permute-start(bf16[384,256]{1,0:T(8,128)(2,1)S(1)} %get-tuple-element.25), channel_id=1, source_target_pairs={{0,4},{4,0},{8,12},{12,8},{16,20},{20,16},{24,28},{28,24},{1,5},{5... | collective-permute-start | bytes 589832 | tf_op jit(solution)/shard_map/ppermute | solution.py:617
  8.2 1.6 %collective-permute-start.1 = (bf16[384,256]{1,0:T(8,128)(2,1)S(1)}, bf16[384,256]{1,0:T(8,128)(2,1)S(1)}, u32[]{:S(2)}, u32[]{:S(2)}) collective-permute-start(bf16[384,256]{1,0:T(8,128)(2,1)S(1)} %get-tuple-element.26), channel_id=1, source_target_pairs={{0,8},{4,12},{8,0},{12,4},{16,24},{20,28},{24,16},{28,20},{1,9},{5... | collective-permute-start | bytes 589832 | tf_op jit(solution)/shard_map/ppermute | solution.py:617
  10.2 1.3 %collective-permute-start.4 = (bf16[384,256]{1,0:T(8,128)(2,1)S(1)}, bf16[384,256]{1,0:T(8,128)(2,1)S(1)}, u32[]{:S(2)}, u32[]{:S(2)}) collective-permute-start(bf16[384,256]{1,0:T(8,128)(2,1)S(1)} %get-tuple-element.29), channel_id=1, source_target_pairs={{0,20},{4,16},{8,28},{12,24},{16,4},{20,0},{24,12},{28,8},{1,21},{... | collective-permute-start | bytes 589832 | tf_op jit(solution)/shard_map/ppermute | solution.py:617
  11.5 2.2 %collective-permute-done.refs_0_ = bf16[384,256]{1,0:T(8,128)(2,1)S(1)} collective-permute-done((bf16[384,256]{1,0:T(8,128)(2,1)S(1)}, bf16[384,256]{1,0:T(8,128)(2,1)S(1)}, u32[]{:S(2)}, u32[]{:S(2)}) %collective-permute-start) | collective-permute-done | bytes 196640 | tf_op jit(solution)/shard_map/ppermute | solution.py:617
  13.6 1.4 %collective-permute-start.5 = (bf16[384,256]{1,0:T(8,128)(2,1)S(1)}, bf16[384,256]{1,0:T(8,128)(2,1)S(1)}, u32[]{:S(2)}, u32[]{:S(2)}) collective-permute-start(bf16[384,256]{1,0:T(8,128)(2,1)S(1)} %get-tuple-element.31), channel_id=1, source_target_pairs={{0,24},{4,28},{8,16},{12,20},{16,8},{20,12},{24,0},{28,4},{1,25},{... | collective-permute-start | bytes 589832 | tf_op jit(solution)/shard_map/ppermute | solution.py:617
  15.1 5.2 %collective-permute-done.3.refs_3_.refs_0_ = bf16[544,256]{1,0:T(8,128)(2,1)S(1)} collective-permute-done((bf16[544,256]{1,0:T(8,128)(2,1)S(1)}, bf16[544,256]{1,0:T(8,128)(2,1)S(1)}, u32[]{:S(2)}, u32[]{:S(2)}) %collective-permute-start.3) | collective-permute-done | bytes 278560 | tf_op jit(solution)/shard_map/ppermute | solution.py:617
  20.2 3.8 %collective-permute-start.6 = (bf16[384,256]{1,0:T(8,128)(2,1)S(1)}, bf16[384,256]{1,0:T(8,128)(2,1)S(1)}, u32[]{:S(2)}, u32[]{:S(2)}) collective-permute-start(bf16[384,256]{1,0:T(8,128)(2,1)S(1)} %get-tuple-element.32), channel_id=1, source_target_pairs={{0,28},{4,24},{8,20},{12,16},{16,12},{20,8},{24,4},{28,0},{1,29},{... | collective-permute-start | bytes 589832 | tf_op jit(solution)/shard_map/ppermute | solution.py:617
  24.4 1.6 %shard_map.140 = (f32[1,256]{1,0:T(1,128)S(1)}, f32[1,256]{1,0:T(1,128)S(1)}, bf16[64,256]{1,0:T(8,128)(2,1)S(1)}, bf16[64,1280]{1,0:T(8,128)(2,1)S(1)}, f32[128...) custom-call(s32[3]{0:T(128)S(1)} %pad_add_fusion.place_ref, f32[1,2048]{1,0:T(1,128)} %refs_0_.1, ...), custom_call_target="tpu_custom_call" | custom-call | flops 1 | bytes 1 | tf_op jit(solution)/shard_map/pallas_call | solution.py:248
  26.9 11.5 %collective-permute-done.4.refs_4_ = bf16[384,256]{1,0:T(8,128)(2,1)S(1)} collective-permute-done((bf16[384,256]{1,0:T(8,128)(2,1)S(1)}, bf16[384,256]{1,0:T(8,128)(2,1)S(1)}, u32[]{:S(2)}, u32[]{:S(2)}) %collective-permute-start.4) | collective-permute-done | bytes 196640 | tf_op jit(solution)/shard_map/ppermute | solution.py:617
  38.4 1.8 %shard_map.141 = (f32[6,2,128,128]{3,2,1,0:T(8,128)S(1)}, f32[6,2,128,128]{3,2,1,0:T(8,128)S(1)}) custom-call(bf16[384,256]{1,0:T(8,128)(2,1)S(1)} %collective-permute-done.refs_0_, bf16[384,256]{1,0:T(8,128)(2,1)S(1)} %collective-permute-done.1.refs_1_, bf16[384,256]{1,0:T(8,128)(2,1)S(1)} %collective-permute-done.2.refs_2_, ...), custom_call_target="tpu_custom_call" | custom-call | flops 1 | bytes 1 | tf_op jit(solution)/shard_map/pallas_call | solution.py:320
  40.5 1.8 %collective-permute-start.9 = (bf16[4,320,128]{2,1,0:T(8,128)(2,1)S(1)}, bf16[4,320,128]{2,1,0:T(8,128)(2,1)S(1)}, u32[]{:S(2)}, u32[]{:S(2)}) collective-permute-start(bf16[4,320,128]{2,1,0:T(8,128)(2,1)S(1)} %shard_map.145.refs_0_), channel_id=1, source_target_pairs={{0,2},{1,3},{2,0},{3,1},{4,6},{5,7},{6,4},{7,5},{8,10},{9,11},{10,... | collective-permute-start | bytes 983048 | tf_op jit(solution)/shard_map/ppermute | solution.py:617
  42.3 1.5 %collective-permute-start.10 = (bf16[4,320,128]{2,1,0:T(8,128)(2,1)S(1)}, bf16[4,320,128]{2,1,0:T(8,128)(2,1)S(1)}, u32[]{:S(2)}, u32[]{:S(2)}) collective-permute-start(bf16[4,320,128]{2,1,0:T(8,128)(2,1)S(1)} %shard_map.145.refs_0_), channel_id=1, source_target_pairs={{0,6},{1,7},{2,4},{3,5},{4,2},{5,3},{6,0},{7,1},{8,14},{9,15},{10,... | collective-permute-start | bytes 983048 | tf_op jit(solution)/shard_map/ppermute | solution.py:633
  43.8 3.8 %shard_map.142 = (bf16[8,128,256]{2,1,0:T(8,128)(2,1)S(1)}, bf16[8,64,128]{2,1,0:T(8,128)(2,1)S(1)}) custom-call(s32[3]{0:T(128)S(1)} %pad_add_fusion.place_ref, bf16[384,256]{1,0:T(8,128)(2,1)S(1)} %collective-permute-done.refs_0_, bf16[384,256]{1,0:T(8,128)(2,1)S(1)} %collective-permute-done.1.refs_1_, ...), custom_call_target="tpu_custom_call" | custom-call | flops 1073741824 | bytes 2097152 | tf_op jit(solution)/shard_map/pallas_call | solution.py:375
  47.7 13.8 %all_to_all.15.refs_0_ = bf16[8,64,128]{2,1,0:T(8,128)(2,1)S(1)} all-to-all(bf16[8,64,128]{2,1,0:T(8,128)(2,1)S(1)} %get-tuple-element.38), channel_id=1, replica_groups=mesh['seq'=8,'dp'=4] {'seq'}, dimensions={0} | all-to-all | bytes 262144 | tf_op jit(solution)/shard_map/all_to_all | solution.py:621
  62.1 1.2 %shard_map.146.refs_0_ = bf16[2,256,1280]{2,1,0:T(8,128)(2,1)S(1)} custom-call(s32[3]{0:T(128)S(1)} %pad_add_fusion.place_ref, bf16[4,320,128]{2,1,0:T(8,128)(2,1)S(1)} %shard_map.145.refs_0_, bf16[4,320,128]{2,1,0:T(8,128)(2,1)S(1)} %collective-permute-done.8.refs_1_, bf16[4,320,128]{2,1,0:T(8,128)(2,1)S(1)} %collective-permute-done.9.refs_2_, ...), custom_call_target="tpu_custom_call" | custom-call | tf_op jit(solution)/shard_map/pallas_call | solution.py:224
  63.4 3.4 %all-to-all-start.1 = ((bf16[8,64,128]{2,1,0:T(8,128)(2,1)}), bf16[8,64,128]{2,1,0:T(8,128)(2,1)S(1)}, u32[]{:S(2)}, u32[]{:S(2)}) async-start(bf16[8,64,128]{2,1,0:T(8,128)(2,1)} %shard_map.143.refs_4_), calls=%async_computation.1 | async-start | bytes 262144 | tf_op jit(solution)/shard_map/all_to_all | solution.py:621
  67.5 7.2 %all-to-all-done.1 = bf16[8,64,128]{2,1,0:T(8,128)(2,1)S(1)} async-done(((bf16[8,64,128]{2,1,0:T(8,128)(2,1)}), bf16[8,64,128]{2,1,0:T(8,128)(2,1)S(1)}, u32[]{:S(2)}, u32[]{:S(2)}) %all-to-all-start.1) | async-done | bytes 131104 | tf_op jit(solution)/shard_map/all_to_all | solution.py:621
  74.7 3.3 %shard_map.147 = (f32[1,128]{1,0:T(1,128)}, bf16[512,128]{1,0:T(8,128)(2,1)S(1)}, bf16[64,256]{1,0:T(8,128)(2,1)S(1)}) custom-call(s32[3]{0:T(128)S(1)} %pad_add_fusion.place_ref, bf16[512,128]{1,0:T(8,128)(2,1)S(1)} %bitcast.7, bf16[2,256,1280]{2,1,0:T(8,128)(2,1)S(1)} %shard_map.146.refs_0_, bf16[2,256,1280]{2,1,0:T(8,128)(2,1)S(1)} %collective-permute-done.11.refs_1_, ...), custom_call_target="tpu_custom_call" | custom-call | flops 503316480 | bytes 2785280 | tf_op jit(solution)/shard_map/pallas_call | solution.py:528
  78.7 1.5 %collective-permute-start.13 = (bf16[64,256]{1,0:T(8,128)(2,1)S(1)}, bf16[64,256]{1,0:T(8,128)(2,1)S(1)}, u32[]{:S(2)}, u32[]{:S(2)}) collective-permute-start(bf16[64,256]{1,0:T(8,128)(2,1)S(1)} %get-tuple-element.46.refs_0_), channel_id=1, source_target_pairs={{0,2},{1,3},{2,0},{3,1},{4,6},{5,7},{6,4},{7,5},{8,10},{9,11},{10,... | collective-permute-start | bytes 98312 | tf_op jit(solution)/shard_map/ppermute | solution.py:617
  80.5 2.1 %collective-permute-done.13.refs_2_ = bf16[64,256]{1,0:T(8,128)(2,1)S(1)} collective-permute-done((bf16[64,256]{1,0:T(8,128)(2,1)S(1)}, bf16[64,256]{1,0:T(8,128)(2,1)S(1)}, u32[]{:S(2)}, u32[]{:S(2)}) %collective-permute-start.13) | collective-permute-done | bytes 32800 | tf_op jit(solution)/shard_map/ppermute | solution.py:617
  84.2 3.4 %all-to-all-start.2 = ((bf16[8,64,256]{2,1,0:T(8,128)(2,1)}), bf16[8,64,256]{2,1,0:T(8,128)(2,1)S(1)}, u32[]{:S(2)}, u32[]{:S(2)}) async-start(bf16[8,64,256]{2,1,0:T(8,128)(2,1)} %shard_map.149), calls=%async_computation.2 | async-start | bytes 524288 | tf_op jit(solution)/shard_map/all_to_all | solution.py:621
  89.6 7.5 %all-to-all-done.2.in_ref = bf16[8,64,256]{2,1,0:T(8,128)(2,1)S(1)} async-done(((bf16[8,64,256]{2,1,0:T(8,128)(2,1)}), bf16[8,64,256]{2,1,0:T(8,128)(2,1)S(1)}, u32[]{:S(2)}, u32[]{:S(2)}) %all-to-all-start.2) | async-done | bytes 262176 | tf_op jit(solution)/shard_map/all_to_all | solution.py:621
  (28 shorter events, 8.2 us)
Async XLA Ops:
  2.6 17.7 %collective-permute-start.3 = (bf16[544,256]{1,0:T(8,128)(2,1)S(1)}, bf16[544,256]{1,0:T(8,128)(2,1)S(1)}, u32[]{:S(2)}, u32[]{:S(2)}) collective-permute-start(bf16[544,256]{1,0:T(8,128)(2,1)S(1)} %get-tuple-element.28), channel_id=1, source_target_pairs={{0,16},{4,20},{8,24},{12,28},{16,0},{20,4},{24,8},{28,12},{1,17},{... | collective-permute-start | bytes 835592 | tf_op jit(solution)/shard_map/ppermute | solution.py:617
  6.7 6.9 %collective-permute-start = (bf16[384,256]{1,0:T(8,128)(2,1)S(1)}, bf16[384,256]{1,0:T(8,128)(2,1)S(1)}, u32[]{:S(2)}, u32[]{:S(2)}) collective-permute-start(bf16[384,256]{1,0:T(8,128)(2,1)S(1)} %get-tuple-element.25), channel_id=1, source_target_pairs={{0,4},{4,0},{8,12},{12,8},{16,20},{20,16},{24,28},{28,24},{1,5},{5... | collective-permute-start | bytes 589832 | tf_op jit(solution)/shard_map/ppermute | solution.py:617
  8.2 16.1 %collective-permute-start.1 = (bf16[384,256]{1,0:T(8,128)(2,1)S(1)}, bf16[384,256]{1,0:T(8,128)(2,1)S(1)}, u32[]{:S(2)}, u32[]{:S(2)}) collective-permute-start(bf16[384,256]{1,0:T(8,128)(2,1)S(1)} %get-tuple-element.26), channel_id=1, source_target_pairs={{0,8},{4,12},{8,0},{12,4},{16,24},{20,28},{24,16},{28,20},{1,9},{5... | collective-permute-start | bytes 589832 | tf_op jit(solution)/shard_map/ppermute | solution.py:617
  9.8 17.1 %collective-permute-start.2 = (bf16[384,256]{1,0:T(8,128)(2,1)S(1)}, bf16[384,256]{1,0:T(8,128)(2,1)S(1)}, u32[]{:S(2)}, u32[]{:S(2)}) collective-permute-start(bf16[384,256]{1,0:T(8,128)(2,1)S(1)} %get-tuple-element.27), channel_id=1, source_target_pairs={{0,12},{4,8},{8,4},{12,0},{16,28},{20,24},{24,20},{28,16},{1,13},{... | collective-permute-start | bytes 589832 | tf_op jit(solution)/shard_map/ppermute | solution.py:617
  10.2 28.2 %collective-permute-start.4 = (bf16[384,256]{1,0:T(8,128)(2,1)S(1)}, bf16[384,256]{1,0:T(8,128)(2,1)S(1)}, u32[]{:S(2)}, u32[]{:S(2)}) collective-permute-start(bf16[384,256]{1,0:T(8,128)(2,1)S(1)} %get-tuple-element.29), channel_id=1, source_target_pairs={{0,20},{4,16},{8,28},{12,24},{16,4},{20,0},{24,12},{28,8},{1,21},{... | collective-permute-start | bytes 589832 | tf_op jit(solution)/shard_map/ppermute | solution.py:617
  13.6 30.2 %collective-permute-start.5 = (bf16[384,256]{1,0:T(8,128)(2,1)S(1)}, bf16[384,256]{1,0:T(8,128)(2,1)S(1)}, u32[]{:S(2)}, u32[]{:S(2)}) collective-permute-start(bf16[384,256]{1,0:T(8,128)(2,1)S(1)} %get-tuple-element.31), channel_id=1, source_target_pairs={{0,24},{4,28},{8,16},{12,20},{16,8},{20,12},{24,0},{28,4},{1,25},{... | collective-permute-start | bytes 589832 | tf_op jit(solution)/shard_map/ppermute | solution.py:617
  20.2 23.6 %collective-permute-start.6 = (bf16[384,256]{1,0:T(8,128)(2,1)S(1)}, bf16[384,256]{1,0:T(8,128)(2,1)S(1)}, u32[]{:S(2)}, u32[]{:S(2)}) collective-permute-start(bf16[384,256]{1,0:T(8,128)(2,1)S(1)} %get-tuple-element.32), channel_id=1, source_target_pairs={{0,28},{4,24},{8,20},{12,16},{16,12},{20,8},{24,4},{28,0},{1,29},{... | collective-permute-start | bytes 589832 | tf_op jit(solution)/shard_map/ppermute | solution.py:617
  24.3 15.9 %collective-permute-start.7 = (bf16[2,320,128]{2,1,0:T(8,128)(2,1)S(1)}, bf16[2,320,128]{2,1,0:T(8,128)(2,1)S(1)}, u32[]{:S(2)}, u32[]{:S(2)}) collective-permute-start(bf16[2,320,128]{2,1,0:T(8,128)(2,1)S(1)} %shard_map.144.first_ref), channel_id=1, source_target_pairs={{0,8},{4,12},{8,0},{12,4},{16,24},{20,28},{24,16},{28,20},{1,9},{5... | collective-permute-start | bytes 491528 | tf_op jit(solution)/shard_map/ppermute | solution.py:617
  40.3 21.9 %collective-permute-start.8 = (bf16[4,320,128]{2,1,0:T(8,128)(2,1)S(1)}, bf16[4,320,128]{2,1,0:T(8,128)(2,1)S(1)}, u32[]{:S(2)}, u32[]{:S(2)}) collective-permute-start(bf16[4,320,128]{2,1,0:T(8,128)(2,1)S(1)} %shard_map.145.refs_0_), channel_id=1, source_target_pairs={{0,4},{4,0},{8,12},{12,8},{16,20},{20,16},{24,28},{28,24},{1,5},{5... | collective-permute-start | bytes 983048 | tf_op jit(solution)/shard_map/ppermute | solution.py:617
  40.5 21.6 %collective-permute-start.9 = (bf16[4,320,128]{2,1,0:T(8,128)(2,1)S(1)}, bf16[4,320,128]{2,1,0:T(8,128)(2,1)S(1)}, u32[]{:S(2)}, u32[]{:S(2)}) collective-permute-start(bf16[4,320,128]{2,1,0:T(8,128)(2,1)S(1)} %shard_map.145.refs_0_), channel_id=1, source_target_pairs={{0,2},{1,3},{2,0},{3,1},{4,6},{5,7},{6,4},{7,5},{8,10},{9,11},{10,... | collective-permute-start | bytes 983048 | tf_op jit(solution)/shard_map/ppermute | solution.py:617
  42.3 19.8 %collective-permute-start.10 = (bf16[4,320,128]{2,1,0:T(8,128)(2,1)S(1)}, bf16[4,320,128]{2,1,0:T(8,128)(2,1)S(1)}, u32[]{:S(2)}, u32[]{:S(2)}) collective-permute-start(bf16[4,320,128]{2,1,0:T(8,128)(2,1)S(1)} %shard_map.145.refs_0_), channel_id=1, source_target_pairs={{0,6},{1,7},{2,4},{3,5},{4,2},{5,3},{6,0},{7,1},{8,14},{9,15},{10,... | collective-permute-start | bytes 983048 | tf_op jit(solution)/shard_map/ppermute | solution.py:633
  63.3 11.3 %collective-permute-start.11 = (bf16[2,256,1280]{2,1,0:T(8,128)(2,1)S(1)}, bf16[2,256,1280]{2,1,0:T(8,128)(2,1)S(1)}, u32[]{:S(2)}, u32[]{:S(2)}) collective-permute-start(bf16[2,256,1280]{2,1,0:T(8,128)(2,1)S(1)} %shard_map.146.refs_0_), channel_id=1, source_target_pairs={{0,1},{1,0},{2,3},{3,2},{4,5},{5,4},{6,7},{7,6},{8,9},{9,8},{10,11... | collective-permute-start | bytes 3932168 | tf_op jit(solution)/shard_map/ppermute | solution.py:617
  63.4 11.2 %all-to-all-start.1 = ((bf16[8,64,128]{2,1,0:T(8,128)(2,1)}), bf16[8,64,128]{2,1,0:T(8,128)(2,1)S(1)}, u32[]{:S(2)}, u32[]{:S(2)}) async-start(bf16[8,64,128]{2,1,0:T(8,128)(2,1)} %shard_map.143.refs_4_), calls=%async_computation.1 | async-start | bytes 262144 | tf_op jit(solution)/shard_map/all_to_all | solution.py:621
  78.0 0.7 copy-start
  78.6 1.9 %collective-permute-start.12 = (bf16[64,256]{1,0:T(8,128)(2,1)S(1)}, bf16[64,256]{1,0:T(8,128)(2,1)S(1)}, u32[]{:S(2)}, u32[]{:S(2)}) collective-permute-start(bf16[64,256]{1,0:T(8,128)(2,1)S(1)} %get-tuple-element.46.refs_0_), channel_id=1, source_target_pairs={{0,1},{1,0},{2,3},{3,2},{4,5},{5,4},{6,7},{7,6},{8,9},{9,8},{10,11... | collective-permute-start | bytes 98312 | tf_op jit(solution)/shard_map/ppermute | solution.py:617
  78.7 3.9 %collective-permute-start.13 = (bf16[64,256]{1,0:T(8,128)(2,1)S(1)}, bf16[64,256]{1,0:T(8,128)(2,1)S(1)}, u32[]{:S(2)}, u32[]{:S(2)}) collective-permute-start(bf16[64,256]{1,0:T(8,128)(2,1)S(1)} %get-tuple-element.46.refs_0_), channel_id=1, source_target_pairs={{0,2},{1,3},{2,0},{3,1},{4,6},{5,7},{6,4},{7,5},{8,10},{9,11},{10,... | collective-permute-start | bytes 98312 | tf_op jit(solution)/shard_map/ppermute | solution.py:617
  80.1 3.3 %collective-permute-start.14 = (bf16[64,256]{1,0:T(8,128)(2,1)S(1)}, bf16[64,256]{1,0:T(8,128)(2,1)S(1)}, u32[]{:S(2)}, u32[]{:S(2)}) collective-permute-start(bf16[64,256]{1,0:T(8,128)(2,1)S(1)} %get-tuple-element.46.refs_0_), channel_id=1, source_target_pairs={{0,3},{1,2},{2,1},{3,0},{4,7},{5,6},{6,5},{7,4},{8,11},{9,10},{10,... | collective-permute-start | bytes 98312 | tf_op jit(solution)/shard_map/ppermute | solution.py:617
  84.2 12.9 %all-to-all-start.2 = ((bf16[8,64,256]{2,1,0:T(8,128)(2,1)}), bf16[8,64,256]{2,1,0:T(8,128)(2,1)S(1)}, u32[]{:S(2)}, u32[]{:S(2)}) async-start(bf16[8,64,256]{2,1,0:T(8,128)(2,1)} %shard_map.149), calls=%async_computation.2 | async-start | bytes 524288 | tf_op jit(solution)/shard_map/all_to_all | solution.py:621
  87.6 0.9 copy-start.1

commit v14 on v13

--- a/solution.py
+++ b/solution.py
@@ -334,37 +334,35 @@
     in_refs, refs = refs[:count], refs[count:]
     kept_refs, refs = refs[: 2 if early else 0], refs[2 if early else 0 :]
     scale_ref, shift_ref, proj_ref, mod_ref, lat_ref, *refs = refs
-    key_scr, value_scr = refs
+    key_scr, value_scr, mod_scr = refs
     half = part_rows // 2
     me = place_ref[0]
     gain = 1.0 + scale_ref[...]
     shift = shift_ref[...]
     load_pieces(sizes, in_refs, key_scr, value_scr)
-    together = 2
-    for first in range(0, count, together):
-        results = []
-        for src in range(first, first + together):
-            mixed = []
-            for head in range(heads):
-                before = None
-                rows = pl.ds(0, count * tok_rows)
-                if src < early:
-                    rows = pl.ds(early * tok_rows, (count - early) * tok_rows)
-                    stat = kept_refs[1][src, head]
-                    before = (kept_refs[0][src, head], stat[:, HD - 1 :], stat[:, :1])
-                query = in_refs[src][pl.ds(0, part_rows), pl.ds(head * HD, HD)]
-                value, total, _ = soft_part(query, key_scr, value_scr, rows, head, before)
-                mixed.append(value / total)
-            results.append(jnp.concatenate(mixed, axis=1) if heads > 1 else mixed[0])
-        for at, attended in enumerate(results):
-            modulated = (attended * gain + shift).astype(BF16)
-            mod_ref[jnp.bitwise_xor(me, masks[first + at])] = modulated
+    for src in range(count):
+        mixed = []
+        for head in range(heads):
+            before = None
+            rows = pl.ds(0, count * tok_rows)
+            if src < early:
+                rows = pl.ds(early * tok_rows, (count - early) * tok_rows)
+                stat = kept_refs[1][src, head]
+                before = (kept_refs[0][src, head], stat[:, HD - 1 :], stat[:, :1])
+            query = in_refs[src][pl.ds(0, part_rows), pl.ds(head * HD, HD)]
+            value, total, _ = soft_part(query, key_scr, value_scr, rows, head, before)
+            mixed.append(value / total)
+        attended = jnp.concatenate(mixed, axis=1) if heads > 1 else mixed[0]
+        mod_scr[src] = (attended * gain + shift).astype(BF16)
     sides = [
-        mm_nt(mod_ref[:, rows, :].reshape(count * half, width), proj_ref[...])
+        mm_nt(mod_scr[:, rows, :].reshape(count * half, width), proj_ref[...])
         for rows in (slice(0, half), slice(half, part_rows))
     ]
     latent = jnp.concatenate(sides, axis=1).astype(BF16)
-    lat_ref[...] = latent.reshape(count, half, 2 * CH)
+    for src in range(count):
+        place = jnp.bitwise_xor(me, masks[src])
+        mod_ref[place] = mod_scr[src]
+        lat_ref[place] = latent[src * half : (src + 1) * half]
 
 
 def attend(sizes, masks, place, received, kept, scales, shifts, proj):
@@ -380,7 +378,8 @@
         ),
         in_specs=[SMEM_SPEC] + [VMEM_SPEC] * (count + len(kept) + 3),
         out_specs=(VMEM_SPEC, VMEM_SPEC),
-        scratch_shapes=piece_scratch(sizes, count),
+        scratch_shapes=piece_scratch(sizes, count)
+        + [pltpu.VMEM((count, sizes.part_rows, width), BF16)],
         compiler_params=limits(16),
         cost_estimate=pl.CostEstimate(
             flops=4 * query_rows * lat_rows * width,
@@ -552,9 +551,21 @@
     )(place, latent, *embed_arrays, pos, pre, post, prompt, cot, modulated)
 
 
-def spread_kernel(count, half, heads, grad_ref, scale_ref, proj_ref, out_ref):
-    gain = 1.0 + scale_ref[...]
-    proj = proj_ref[...]
+def spread_kernel(
+    count, half, heads, place_ref, grad_ref, scale_ref, proj_ref, out_ref, scale_scr, proj_scr, sems
+):
+    width = heads * HD
+    mine = pl.ds(pl.multiple_of(place_ref[2] * width, HD), width)
+    copies = [
+        pltpu.make_async_copy(scale_ref.at[:, mine], scale_scr, sems.at[0]),
+        pltpu.make_async_copy(proj_ref.at[:, mine], proj_scr, sems.at[1]),
+    ]
+    for copy in copies:
+        copy.start()
+    for copy in copies:
+        copy.wait()
+    gain = 1.0 + scale_scr[...]
+    proj = proj_scr[...]
     zero = jnp.zeros_like(proj)
     sides = (jnp.concatenate([proj, zero], axis=0), jnp.concatenate([zero, proj], axis=0))
     for src in range(count):
@@ -567,19 +578,24 @@
                 ]
 
 
-def spread(grad, scales, proj, count, half, heads):
+def spread(place, grad, scales, proj, count, half, heads):
     return pl.pallas_call(
         functools.partial(spread_kernel, count, half, heads),
         out_shape=jax.ShapeDtypeStruct((1, heads, 2 * count * half, HD), BF16),
-        in_specs=[VMEM_SPEC] * 3,
+        in_specs=[SMEM_SPEC, VMEM_SPEC, HBM_SPEC, HBM_SPEC],
         out_specs=VMEM_SPEC,
+        scratch_shapes=[
+            pltpu.VMEM((1, heads * HD), F32),
+            pltpu.VMEM((CH, heads * HD), BF16),
+            pltpu.SemaphoreType.DMA((2,)),
+        ],
         compiler_params=limits(),
         cost_estimate=pl.CostEstimate(
             flops=8 * count * half * CH * heads * HD,
             bytes_accessed=4 * count * half * heads * HD,
             transcendentals=0,
         ),
-    )(grad, scales, proj)
+    )(place, grad, scales, proj)
 
 
 def weight_kernel(out_factor, grad_ref, *refs):
@@ -738,7 +754,7 @@
         weight = weight_call(grad, modulated, out_factor)
 
     parts = [weight] + [swap(weight, "dp", mask) for mask in range(1, data_count)]
-    attn_grad = spread(grad, scale, proj, seq_count, half, head_count)
+    attn_grad = spread(place, grad, in_hbm(scales), in_hbm(proj_turned), seq_count, half, head_count)
     if query_parts > 1:
         total = total_copies(parts, 1)[0]
         parts = [total] + [swap(total, "seq", mask) for mask in range(1, query_parts)]

time: 98.4 us -> 98.6 us (level)
  Pallas kernels: 17.1 us -> 18.6 us
  waiting for transfers between devices: 37.7 us -> 36.4 us
    all_to_all x2, waiting for transfers between devices: 14.7 us -> 13.4 us  [all_to_all(): lax.all_to_all(x, 'seq', split_axis=0, concat_axis=0, tiled=True, axis_in...]
    pallas_call x1, Pallas kernels: 1.08 us -> 2.41 us  [spread(): pl.pallas_call(functools.partial(spread_kernel, count, half, heads), out_...]
  transfers between devices with their start and end apart: 17 -> 17, of which waited for: 9 -> 9; matrix products, arithmetic and copies ran while one was open for 0% -> 0% of each run, Pallas kernels for 9% -> 11%
where the time goes in v14:
time: 98.6 us; the launch traced here: 98.1 us
  waiting for transfers between devices  36.4 us (37%)
  starting transfers between devices  26.4 us (27%)
  Pallas kernels  18.6 us (19%)
  blocking collectives  13.8 us (14%)
  local copies, waits for them, and re-layouts  1.55 us (2%)
  between operations  1.41 us (1%)
    ppermute x14, waiting for transfers between devices, swap(): return lax.ppermute(x, axis, [(i, i ^ mask) for i in range(count)])  22.9 us
    ppermute x14, starting transfers between devices, swap(): return lax.ppermute(x, axis, [(i, i ^ mask) for i in range(count)])  18.1 us
    all_to_all x1, blocking collectives, all_to_all(): lax.all_to_all(x, 'seq', split_axis=0, concat_axis=0, tiled=True, axis_in...  13.8 us
    all_to_all x2, waiting for transfers between devices, all_to_all(): lax.all_to_all(x, 'seq', split_axis=0, concat_axis=0, tiled=True, axis_in...  13.4 us
    all_to_all x2, starting transfers between devices, all_to_all(): lax.all_to_all(x, 'seq', split_axis=0, concat_axis=0, tiled=True, axis_in...  6.8 us
    pallas_call x1, Pallas kernels, attend(): pl.pallas_call(functools.partial(attend_kernel, sizes, masks, early), out...  3.96 us
    pallas_call x1, Pallas kernels, reward_head(): pl.pallas_call(functools.partial(head_kernel, grid_rows, fused, embed_mas...  3.31 us
    pallas_call x1, Pallas kernels, spread(): pl.pallas_call(functools.partial(spread_kernel, count, half, heads), out_...  2.41 us
  transfers between devices with their start and end apart: 17, of which 9 were waited for; matrix products, arithmetic and copies ran while one was open for 0% of the time, Pallas kernels for 11%

profile of v14, /device:TPU:0, one launch (start us, length us, event | category | flops | bytes accessed | tf_op | source)
XLA Modules:
  0.0 98.1 jit_solution(14586562753561769147)
XLA Ops:
  0.6 1.9 %shard_map.139 = (bf16[384,256]{1,0:T(8,128)(2,1)S(1)}, bf16[384,256]{1,0:T(8,128)(2,1)S(1)}, bf16[384,256]{1,0:T(8,128)(2,1)S(1)}, bf16[544,256]{1,0:T(8,128)(2...) custom-call(bf16[1,128,2048]{2,1,0:T(8,128)(2,1)} %q_ref.1, ...), custom_call_target="tpu_custom_call" | custom-call | bytes 3145728 | tf_op jit(solution)/shard_map/pallas_call | solution.py:136
  2.6 4.1 %collective-permute-start.3 = (bf16[544,256]{1,0:T(8,128)(2,1)S(1)}, bf16[544,256]{1,0:T(8,128)(2,1)S(1)}, u32[]{:S(2)}, u32[]{:S(2)}) collective-permute-start(bf16[544,256]{1,0:T(8,128)(2,1)S(1)} %get-tuple-element.28), channel_id=1, source_target_pairs={{0,16},{4,20},{8,24},{12,28},{16,0},{20,4},{24,8},{28,12},{1,17},{... | collective-permute-start | bytes 835592 | tf_op jit(solution)/shard_map/ppermute | solution.py:633
  6.7 1.5 %collective-permute-start = (bf16[384,256]{1,0:T(8,128)(2,1)S(1)}, bf16[384,256]{1,0:T(8,128)(2,1)S(1)}, u32[]{:S(2)}, u32[]{:S(2)}) collective-permute-start(bf16[384,256]{1,0:T(8,128)(2,1)S(1)} %get-tuple-element.25), channel_id=1, source_target_pairs={{0,4},{4,0},{8,12},{12,8},{16,20},{20,16},{24,28},{28,24},{1,5},{5... | collective-permute-start | bytes 589832 | tf_op jit(solution)/shard_map/ppermute | solution.py:633
  8.2 1.6 %collective-permute-start.1 = (bf16[384,256]{1,0:T(8,128)(2,1)S(1)}, bf16[384,256]{1,0:T(8,128)(2,1)S(1)}, u32[]{:S(2)}, u32[]{:S(2)}) collective-permute-start(bf16[384,256]{1,0:T(8,128)(2,1)S(1)} %get-tuple-element.26), channel_id=1, source_target_pairs={{0,8},{4,12},{8,0},{12,4},{16,24},{20,28},{24,16},{28,20},{1,9},{5... | collective-permute-start | bytes 589832 | tf_op jit(solution)/shard_map/ppermute | solution.py:633
  10.2 1.3 %collective-permute-start.4 = (bf16[384,256]{1,0:T(8,128)(2,1)S(1)}, bf16[384,256]{1,0:T(8,128)(2,1)S(1)}, u32[]{:S(2)}, u32[]{:S(2)}) collective-permute-start(bf16[384,256]{1,0:T(8,128)(2,1)S(1)} %get-tuple-element.29), channel_id=1, source_target_pairs={{0,20},{4,16},{8,28},{12,24},{16,4},{20,0},{24,12},{28,8},{1,21},{... | collective-permute-start | bytes 589832 | tf_op jit(solution)/shard_map/ppermute | solution.py:633
  11.5 2.2 %collective-permute-done.refs_0_ = bf16[384,256]{1,0:T(8,128)(2,1)S(1)} collective-permute-done((bf16[384,256]{1,0:T(8,128)(2,1)S(1)}, bf16[384,256]{1,0:T(8,128)(2,1)S(1)}, u32[]{:S(2)}, u32[]{:S(2)}) %collective-permute-start) | collective-permute-done | bytes 196640 | tf_op jit(solution)/shard_map/ppermute | solution.py:633
  13.6 1.4 %collective-permute-start.5 = (bf16[384,256]{1,0:T(8,128)(2,1)S(1)}, bf16[384,256]{1,0:T(8,128)(2,1)S(1)}, u32[]{:S(2)}, u32[]{:S(2)}) collective-permute-start(bf16[384,256]{1,0:T(8,128)(2,1)S(1)} %get-tuple-element.31), channel_id=1, source_target_pairs={{0,24},{4,28},{8,16},{12,20},{16,8},{20,12},{24,0},{28,4},{1,25},{... | collective-permute-start | bytes 589832 | tf_op jit(solution)/shard_map/ppermute | solution.py:633
  15.1 5.2 %collective-permute-done.3.refs_3_.refs_0_ = bf16[544,256]{1,0:T(8,128)(2,1)S(1)} collective-permute-done((bf16[544,256]{1,0:T(8,128)(2,1)S(1)}, bf16[544,256]{1,0:T(8,128)(2,1)S(1)}, u32[]{:S(2)}, u32[]{:S(2)}) %collective-permute-start.3) | collective-permute-done | bytes 278560 | tf_op jit(solution)/shard_map/ppermute | solution.py:633
  20.2 3.8 %collective-permute-start.6 = (bf16[384,256]{1,0:T(8,128)(2,1)S(1)}, bf16[384,256]{1,0:T(8,128)(2,1)S(1)}, u32[]{:S(2)}, u32[]{:S(2)}) collective-permute-start(bf16[384,256]{1,0:T(8,128)(2,1)S(1)} %get-tuple-element.32), channel_id=1, source_target_pairs={{0,28},{4,24},{8,20},{12,16},{16,12},{20,8},{24,4},{28,0},{1,29},{... | collective-permute-start | bytes 589832 | tf_op jit(solution)/shard_map/ppermute | solution.py:633
  24.4 1.6 %shard_map.140 = (f32[1,256]{1,0:T(1,128)S(1)}, f32[1,256]{1,0:T(1,128)S(1)}, bf16[64,256]{1,0:T(8,128)(2,1)S(1)}, bf16[64,1280]{1,0:T(8,128)(2,1)S(1)}, f32[128...) custom-call(s32[3]{0:T(128)S(1)} %pad_add_fusion.place_ref, f32[1,2048]{1,0:T(1,128)} %scale_ref.1, ...), custom_call_target="tpu_custom_call" | custom-call | flops 1 | bytes 1 | tf_op jit(solution)/shard_map/pallas_call | solution.py:248
  26.9 11.5 %collective-permute-done.4.refs_4_ = bf16[384,256]{1,0:T(8,128)(2,1)S(1)} collective-permute-done((bf16[384,256]{1,0:T(8,128)(2,1)S(1)}, bf16[384,256]{1,0:T(8,128)(2,1)S(1)}, u32[]{:S(2)}, u32[]{:S(2)}) %collective-permute-start.4) | collective-permute-done | bytes 196640 | tf_op jit(solution)/shard_map/ppermute | solution.py:633
  38.4 1.8 %shard_map.141 = (f32[6,2,128,128]{3,2,1,0:T(8,128)S(1)}, f32[6,2,128,128]{3,2,1,0:T(8,128)S(1)}) custom-call(bf16[384,256]{1,0:T(8,128)(2,1)S(1)} %collective-permute-done.refs_0_, bf16[384,256]{1,0:T(8,128)(2,1)S(1)} %collective-permute-done.1.refs_1_, bf16[384,256]{1,0:T(8,128)(2,1)S(1)} %collective-permute-done.2.refs_2_, ...), custom_call_target="tpu_custom_call" | custom-call | flops 1 | bytes 1 | tf_op jit(solution)/shard_map/pallas_call | solution.py:320
  40.5 1.8 %collective-permute-start.9 = (bf16[4,320,128]{2,1,0:T(8,128)(2,1)S(1)}, bf16[4,320,128]{2,1,0:T(8,128)(2,1)S(1)}, u32[]{:S(2)}, u32[]{:S(2)}) collective-permute-start(bf16[4,320,128]{2,1,0:T(8,128)(2,1)S(1)} %shard_map.145.refs_0_), channel_id=1, source_target_pairs={{0,2},{1,3},{2,0},{3,1},{4,6},{5,7},{6,4},{7,5},{8,10},{9,11},{10,... | collective-permute-start | bytes 983048 | tf_op jit(solution)/shard_map/ppermute | solution.py:633
  42.3 1.5 %collective-permute-start.10 = (bf16[4,320,128]{2,1,0:T(8,128)(2,1)S(1)}, bf16[4,320,128]{2,1,0:T(8,128)(2,1)S(1)}, u32[]{:S(2)}, u32[]{:S(2)}) collective-permute-start(bf16[4,320,128]{2,1,0:T(8,128)(2,1)S(1)} %shard_map.145.refs_0_), channel_id=1, source_target_pairs={{0,6},{1,7},{2,4},{3,5},{4,2},{5,3},{6,0},{7,1},{8,14},{9,15},{10,... | collective-permute-start | bytes 983048 | tf_op jit(solution)/shard_map/ppermute | solution.py:649
  43.8 4.0 %shard_map.142 = (bf16[8,128,256]{2,1,0:T(8,128)(2,1)S(1)}, bf16[8,64,128]{2,1,0:T(8,128)(2,1)S(1)}) custom-call(s32[3]{0:T(128)S(1)} %pad_add_fusion.place_ref, bf16[384,256]{1,0:T(8,128)(2,1)S(1)} %collective-permute-done.refs_0_, bf16[384,256]{1,0:T(8,128)(2,1)S(1)} %collective-permute-done.1.refs_1_, ...), custom_call_target="tpu_custom_call" | custom-call | flops 1073741824 | bytes 2097152 | tf_op jit(solution)/shard_map/pallas_call | solution.py:373
  47.8 13.8 %all_to_all.15.refs_0_ = bf16[8,64,128]{2,1,0:T(8,128)(2,1)S(1)} all-to-all(bf16[8,64,128]{2,1,0:T(8,128)(2,1)S(1)} %get-tuple-element.38), channel_id=1, replica_groups=mesh['seq'=8,'dp'=4] {'seq'}, dimensions={0} | all-to-all | bytes 262144 | tf_op jit(solution)/shard_map/all_to_all | solution.py:637
  63.6 3.4 %all-to-all-start.1 = ((bf16[8,64,128]{2,1,0:T(8,128)(2,1)}), bf16[8,64,128]{2,1,0:T(8,128)(2,1)S(1)}, u32[]{:S(2)}, u32[]{:S(2)}) async-start(bf16[8,64,128]{2,1,0:T(8,128)(2,1)} %shard_map.143.refs_4_), calls=%async_computation.1 | async-start | bytes 262144 | tf_op jit(solution)/shard_map/all_to_all | solution.py:637
  67.6 7.2 %all-to-all-done.1 = bf16[8,64,128]{2,1,0:T(8,128)(2,1)S(1)} async-done(((bf16[8,64,128]{2,1,0:T(8,128)(2,1)}), bf16[8,64,128]{2,1,0:T(8,128)(2,1)S(1)}, u32[]{:S(2)}, u32[]{:S(2)}) %all-to-all-start.1) | async-done | bytes 131104 | tf_op jit(solution)/shard_map/all_to_all | solution.py:637
  74.8 3.3 %shard_map.147 = (f32[1,128]{1,0:T(1,128)}, bf16[512,128]{1,0:T(8,128)(2,1)S(1)}, bf16[64,256]{1,0:T(8,128)(2,1)S(1)}) custom-call(s32[3]{0:T(128)S(1)} %pad_add_fusion.place_ref, bf16[512,128]{1,0:T(8,128)(2,1)S(1)} %bitcast.7, bf16[2,256,1280]{2,1,0:T(8,128)(2,1)S(1)} %shard_map.146.refs_0_, bf16[2,256,1280]{2,1,0:T(8,128)(2,1)S(1)} %collective-permute-done.11.refs_1_, ...), custom_call_target="tpu_custom_call" | custom-call | flops 503316480 | bytes 2785280 | tf_op jit(solution)/shard_map/pallas_call | solution.py:527
  78.8 1.5 %collective-permute-start.13 = (bf16[64,256]{1,0:T(8,128)(2,1)S(1)}, bf16[64,256]{1,0:T(8,128)(2,1)S(1)}, u32[]{:S(2)}, u32[]{:S(2)}) collective-permute-start(bf16[64,256]{1,0:T(8,128)(2,1)S(1)} %get-tuple-element.46.refs_0_), channel_id=1, source_target_pairs={{0,2},{1,3},{2,0},{3,1},{4,6},{5,7},{6,4},{7,5},{8,10},{9,11},{10,... | collective-permute-start | bytes 98312 | tf_op jit(solution)/shard_map/ppermute | solution.py:633
  80.6 2.1 %collective-permute-done.13.refs_2_ = bf16[64,256]{1,0:T(8,128)(2,1)S(1)} collective-permute-done((bf16[64,256]{1,0:T(8,128)(2,1)S(1)}, bf16[64,256]{1,0:T(8,128)(2,1)S(1)}, u32[]{:S(2)}, u32[]{:S(2)}) %collective-permute-start.13) | collective-permute-done | bytes 32800 | tf_op jit(solution)/shard_map/ppermute | solution.py:633
  84.3 3.4 %all-to-all-start.2 = ((bf16[8,64,256]{2,1,0:T(8,128)(2,1)}), bf16[8,64,256]{2,1,0:T(8,128)(2,1)S(1)}, u32[]{:S(2)}, u32[]{:S(2)}) async-start(bf16[8,64,256]{2,1,0:T(8,128)(2,1)} %shard_map.149), calls=%async_computation.2 | async-start | bytes 524288 | tf_op jit(solution)/shard_map/all_to_all | solution.py:637
  88.7 2.4 %shard_map.148 = bf16[1,2,1024,128]{3,2,1,0:T(8,128)(2,1)} custom-call(s32[3]{0:T(128)S(1)} %pad_add_fusion.place_ref, bf16[512,128]{1,0:T(8,128)(2,1)S(1)} %copy-done.1, f32[1,2048]{1,0:T(1,128)} %scale_ref.1, bf16[64,2048]{1,0:T(8,128)(2,1)} %bitcast.9), custom_call_target="tpu_custom_call" | custom-call | flops 67108864 | bytes 524288 | tf_op jit(solution)/shard_map/pallas_call | solution.py:582
  91.1 6.2 %all-to-all-done.2.in_ref = bf16[8,64,256]{2,1,0:T(8,128)(2,1)S(1)} async-done(((bf16[8,64,256]{2,1,0:T(8,128)(2,1)}), bf16[8,64,256]{2,1,0:T(8,128)(2,1)S(1)}, u32[]{:S(2)}, u32[]{:S(2)}) %all-to-all-start.2) | async-done | bytes 262176 | tf_op jit(solution)/shard_map/all_to_all | solution.py:637
  (28 shorter events, 8.3 us)
Async XLA Ops:
  2.6 17.7 %collective-permute-start.3 = (bf16[544,256]{1,0:T(8,128)(2,1)S(1)}, bf16[544,256]{1,0:T(8,128)(2,1)S(1)}, u32[]{:S(2)}, u32[]{:S(2)}) collective-permute-start(bf16[544,256]{1,0:T(8,128)(2,1)S(1)} %get-tuple-element.28), channel_id=1, source_target_pairs={{0,16},{4,20},{8,24},{12,28},{16,0},{20,4},{24,8},{28,12},{1,17},{... | collective-permute-start | bytes 835592 | tf_op jit(solution)/shard_map/ppermute | solution.py:633
  6.7 6.9 %collective-permute-start = (bf16[384,256]{1,0:T(8,128)(2,1)S(1)}, bf16[384,256]{1,0:T(8,128)(2,1)S(1)}, u32[]{:S(2)}, u32[]{:S(2)}) collective-permute-start(bf16[384,256]{1,0:T(8,128)(2,1)S(1)} %get-tuple-element.25), channel_id=1, source_target_pairs={{0,4},{4,0},{8,12},{12,8},{16,20},{20,16},{24,28},{28,24},{1,5},{5... | collective-permute-start | bytes 589832 | tf_op jit(solution)/shard_map/ppermute | solution.py:633
  8.2 16.1 %collective-permute-start.1 = (bf16[384,256]{1,0:T(8,128)(2,1)S(1)}, bf16[384,256]{1,0:T(8,128)(2,1)S(1)}, u32[]{:S(2)}, u32[]{:S(2)}) collective-permute-start(bf16[384,256]{1,0:T(8,128)(2,1)S(1)} %get-tuple-element.26), channel_id=1, source_target_pairs={{0,8},{4,12},{8,0},{12,4},{16,24},{20,28},{24,16},{28,20},{1,9},{5... | collective-permute-start | bytes 589832 | tf_op jit(solution)/shard_map/ppermute | solution.py:633
  9.8 17.1 %collective-permute-start.2 = (bf16[384,256]{1,0:T(8,128)(2,1)S(1)}, bf16[384,256]{1,0:T(8,128)(2,1)S(1)}, u32[]{:S(2)}, u32[]{:S(2)}) collective-permute-start(bf16[384,256]{1,0:T(8,128)(2,1)S(1)} %get-tuple-element.27), channel_id=1, source_target_pairs={{0,12},{4,8},{8,4},{12,0},{16,28},{20,24},{24,20},{28,16},{1,13},{... | collective-permute-start | bytes 589832 | tf_op jit(solution)/shard_map/ppermute | solution.py:633
  10.2 28.2 %collective-permute-start.4 = (bf16[384,256]{1,0:T(8,128)(2,1)S(1)}, bf16[384,256]{1,0:T(8,128)(2,1)S(1)}, u32[]{:S(2)}, u32[]{:S(2)}) collective-permute-start(bf16[384,256]{1,0:T(8,128)(2,1)S(1)} %get-tuple-element.29), channel_id=1, source_target_pairs={{0,20},{4,16},{8,28},{12,24},{16,4},{20,0},{24,12},{28,8},{1,21},{... | collective-permute-start | bytes 589832 | tf_op jit(solution)/shard_map/ppermute | solution.py:633
  13.6 30.2 %collective-permute-start.5 = (bf16[384,256]{1,0:T(8,128)(2,1)S(1)}, bf16[384,256]{1,0:T(8,128)(2,1)S(1)}, u32[]{:S(2)}, u32[]{:S(2)}) collective-permute-start(bf16[384,256]{1,0:T(8,128)(2,1)S(1)} %get-tuple-element.31), channel_id=1, source_target_pairs={{0,24},{4,28},{8,16},{12,20},{16,8},{20,12},{24,0},{28,4},{1,25},{... | collective-permute-start | bytes 589832 | tf_op jit(solution)/shard_map/ppermute | solution.py:633
  20.2 23.6 %collective-permute-start.6 = (bf16[384,256]{1,0:T(8,128)(2,1)S(1)}, bf16[384,256]{1,0:T(8,128)(2,1)S(1)}, u32[]{:S(2)}, u32[]{:S(2)}) collective-permute-start(bf16[384,256]{1,0:T(8,128)(2,1)S(1)} %get-tuple-element.32), channel_id=1, source_target_pairs={{0,28},{4,24},{8,20},{12,16},{16,12},{20,8},{24,4},{28,0},{1,29},{... | collective-permute-start | bytes 589832 | tf_op jit(solution)/shard_map/ppermute | solution.py:633
  24.3 15.9 %collective-permute-start.7 = (bf16[2,320,128]{2,1,0:T(8,128)(2,1)S(1)}, bf16[2,320,128]{2,1,0:T(8,128)(2,1)S(1)}, u32[]{:S(2)}, u32[]{:S(2)}) collective-permute-start(bf16[2,320,128]{2,1,0:T(8,128)(2,1)S(1)} %shard_map.144.first_ref), channel_id=1, source_target_pairs={{0,8},{4,12},{8,0},{12,4},{16,24},{20,28},{24,16},{28,20},{1,9},{5... | collective-permute-start | bytes 491528 | tf_op jit(solution)/shard_map/ppermute | solution.py:633
  40.3 22.0 %collective-permute-start.8 = (bf16[4,320,128]{2,1,0:T(8,128)(2,1)S(1)}, bf16[4,320,128]{2,1,0:T(8,128)(2,1)S(1)}, u32[]{:S(2)}, u32[]{:S(2)}) collective-permute-start(bf16[4,320,128]{2,1,0:T(8,128)(2,1)S(1)} %shard_map.145.refs_0_), channel_id=1, source_target_pairs={{0,4},{4,0},{8,12},{12,8},{16,20},{20,16},{24,28},{28,24},{1,5},{5... | collective-permute-start | bytes 983048 | tf_op jit(solution)/shard_map/ppermute | solution.py:633
  40.5 21.8 %collective-permute-start.9 = (bf16[4,320,128]{2,1,0:T(8,128)(2,1)S(1)}, bf16[4,320,128]{2,1,0:T(8,128)(2,1)S(1)}, u32[]{:S(2)}, u32[]{:S(2)}) collective-permute-start(bf16[4,320,128]{2,1,0:T(8,128)(2,1)S(1)} %shard_map.145.refs_0_), channel_id=1, source_target_pairs={{0,2},{1,3},{2,0},{3,1},{4,6},{5,7},{6,4},{7,5},{8,10},{9,11},{10,... | collective-permute-start | bytes 983048 | tf_op jit(solution)/shard_map/ppermute | solution.py:633
  42.3 19.9 %collective-permute-start.10 = (bf16[4,320,128]{2,1,0:T(8,128)(2,1)S(1)}, bf16[4,320,128]{2,1,0:T(8,128)(2,1)S(1)}, u32[]{:S(2)}, u32[]{:S(2)}) collective-permute-start(bf16[4,320,128]{2,1,0:T(8,128)(2,1)S(1)} %shard_map.145.refs_0_), channel_id=1, source_target_pairs={{0,6},{1,7},{2,4},{3,5},{4,2},{5,3},{6,0},{7,1},{8,14},{9,15},{10,... | collective-permute-start | bytes 983048 | tf_op jit(solution)/shard_map/ppermute | solution.py:649
  63.5 11.3 %collective-permute-start.11 = (bf16[2,256,1280]{2,1,0:T(8,128)(2,1)S(1)}, bf16[2,256,1280]{2,1,0:T(8,128)(2,1)S(1)}, u32[]{:S(2)}, u32[]{:S(2)}) collective-permute-start(bf16[2,256,1280]{2,1,0:T(8,128)(2,1)S(1)} %shard_map.146.refs_0_), channel_id=1, source_target_pairs={{0,1},{1,0},{2,3},{3,2},{4,5},{5,4},{6,7},{7,6},{8,9},{9,8},{10,11... | collective-permute-start | bytes 3932168 | tf_op jit(solution)/shard_map/ppermute | solution.py:633
  63.6 11.2 %all-to-all-start.1 = ((bf16[8,64,128]{2,1,0:T(8,128)(2,1)}), bf16[8,64,128]{2,1,0:T(8,128)(2,1)S(1)}, u32[]{:S(2)}, u32[]{:S(2)}) async-start(bf16[8,64,128]{2,1,0:T(8,128)(2,1)} %shard_map.143.refs_4_), calls=%async_computation.1 | async-start | bytes 262144 | tf_op jit(solution)/shard_map/all_to_all | solution.py:637
  78.1 0.7 copy-start
  78.8 1.9 %collective-permute-start.12 = (bf16[64,256]{1,0:T(8,128)(2,1)S(1)}, bf16[64,256]{1,0:T(8,128)(2,1)S(1)}, u32[]{:S(2)}, u32[]{:S(2)}) collective-permute-start(bf16[64,256]{1,0:T(8,128)(2,1)S(1)} %get-tuple-element.46.refs_0_), channel_id=1, source_target_pairs={{0,1},{1,0},{2,3},{3,2},{4,5},{5,4},{6,7},{7,6},{8,9},{9,8},{10,11... | collective-permute-start | bytes 98312 | tf_op jit(solution)/shard_map/ppermute | solution.py:633
  78.8 3.9 %collective-permute-start.13 = (bf16[64,256]{1,0:T(8,128)(2,1)S(1)}, bf16[64,256]{1,0:T(8,128)(2,1)S(1)}, u32[]{:S(2)}, u32[]{:S(2)}) collective-permute-start(bf16[64,256]{1,0:T(8,128)(2,1)S(1)} %get-tuple-element.46.refs_0_), channel_id=1, source_target_pairs={{0,2},{1,3},{2,0},{3,1},{4,6},{5,7},{6,4},{7,5},{8,10},{9,11},{10,... | collective-permute-start | bytes 98312 | tf_op jit(solution)/shard_map/ppermute | solution.py:633
  80.3 3.3 %collective-permute-start.14 = (bf16[64,256]{1,0:T(8,128)(2,1)S(1)}, bf16[64,256]{1,0:T(8,128)(2,1)S(1)}, u32[]{:S(2)}, u32[]{:S(2)}) collective-permute-start(bf16[64,256]{1,0:T(8,128)(2,1)S(1)} %get-tuple-element.46.refs_0_), channel_id=1, source_target_pairs={{0,3},{1,2},{2,1},{3,0},{4,7},{5,6},{6,5},{7,4},{8,11},{9,10},{10,... | collective-permute-start | bytes 98312 | tf_op jit(solution)/shard_map/ppermute | solution.py:633
  84.3 12.9 %all-to-all-start.2 = ((bf16[8,64,256]{2,1,0:T(8,128)(2,1)}), bf16[8,64,256]{2,1,0:T(8,128)(2,1)S(1)}, u32[]{:S(2)}, u32[]{:S(2)}) async-start(bf16[8,64,256]{2,1,0:T(8,128)(2,1)} %shard_map.149), calls=%async_computation.2 | async-start | bytes 524288 | tf_op jit(solution)/shard_map/all_to_all | solution.py:637
  87.8 0.9 copy-start.1

commit v15 on v13

--- a/solution.py
+++ b/solution.py
@@ -230,9 +230,10 @@
     )(place, *flat, wait)
 
 
-def fetch_kernel(sizes, place_ref, *refs):
+def fetch_kernel(sizes, place_ref, cot_ref, *refs):
+    *refs, row_ref, sems = refs
     count = len(refs) // 2
-    sems = refs[-1]
+    row_ref[...] = jnp.full(row_ref.shape, cot_ref[0], F32)
     mine = pl.ds(pl.multiple_of(place_ref[2] * sizes.width, HD), sizes.width)
     copies = []
     for slot in range(count):
@@ -243,17 +244,18 @@
         copy.wait()
 
 
-def fetch(sizes, place, arrays):
+def fetch(sizes, place, cotangent, arrays):
     shapes = [x.shape if slot >= 3 else (x.shape[0], sizes.width) for slot, x in enumerate(arrays)]
     return pl.pallas_call(
         functools.partial(fetch_kernel, sizes),
-        out_shape=[jax.ShapeDtypeStruct(shape, x.dtype) for shape, x in zip(shapes, arrays)],
-        in_specs=[SMEM_SPEC] + [HBM_SPEC] * len(arrays),
-        out_specs=[VMEM_SPEC] * len(arrays),
+        out_shape=[jax.ShapeDtypeStruct(shape, x.dtype) for shape, x in zip(shapes, arrays)]
+        + [jax.ShapeDtypeStruct((1, 128), F32)],
+        in_specs=[SMEM_SPEC] * 2 + [HBM_SPEC] * len(arrays),
+        out_specs=[VMEM_SPEC] * (len(arrays) + 1),
         scratch_shapes=[pltpu.SemaphoreType.DMA((len(arrays),))],
         compiler_params=limits(),
         cost_estimate=pl.CostEstimate(flops=1, bytes_accessed=1, transcendentals=0),
-    )(place, *[in_hbm(x) for x in arrays])
+    )(place, cotangent, *[in_hbm(x) for x in arrays])
 
 
 FACTOR = HD ** (-0.5) * math.log2(math.e)
@@ -390,26 +392,26 @@
     )(place, *received, *kept, scales, shifts, proj)
 
 
-def total_kernel(copies, *refs):
+def total_kernel(copies, count, *refs):
     out_ref = refs[-1]
-    if len(refs) == 2:
+    if count == 1:
         parts = [refs[0][i].astype(F32) for i in range(refs[0].shape[0])]
     else:
-        parts = [ref[...].astype(F32) for ref in refs[:-1]]
+        parts = [ref[...].astype(F32) for ref in refs[:count]]
     while len(parts) > 1:
         parts = [parts[i] + parts[i + 1] for i in range(0, len(parts), 2)]
     for copy in range(copies):
         out_ref[copy] = parts[0].astype(BF16)
 
 
-def total_copies(arrays, copies):
-    return pl.pallas_call(
-        functools.partial(total_kernel, copies),
+def total_copies(arrays, copies, others=()):
+    return pl.pallas_call(
+        functools.partial(total_kernel, copies, len(arrays)),
         out_shape=jax.ShapeDtypeStruct((copies,) + arrays[0].shape[-2:], BF16),
-        in_specs=[VMEM_SPEC] * len(arrays),
+        in_specs=[VMEM_SPEC] * len(arrays) + [ANY_SPEC] * len(others),
         out_specs=VMEM_SPEC,
         compiler_params=limits(),
-    )(*arrays)
+    )(*arrays, *others)
 
 
 def lane_mean(x, count):
@@ -471,7 +473,7 @@
     prompt_len = jnp.sqrt(prompt_sq)
     cosine = dot / (final_len * prompt_len)
     reward_ref[...] = jnp.broadcast_to(100.0 * cosine, reward_ref.shape)
-    cot = cot_ref[0]
+    cot = cot_ref[:, :1]
     final_grad = (100.0 * cot) * (prompt / (final_len * prompt_len) - final * (cosine / final_sq))
     unit_grad = final_grad * post
     pooled_grad = pooled_rstd * (
@@ -534,8 +536,7 @@
         ),
         in_specs=[SMEM_SPEC, VMEM_SPEC]
         + [VMEM_SPEC] * len(embed_arrays)
-        + [VMEM_SPEC] * 4
-        + [SMEM_SPEC, VMEM_SPEC],
+        + [VMEM_SPEC] * 6,
         out_specs=(VMEM_SPEC, VMEM_SPEC, VMEM_SPEC),
         scratch_shapes=[
             pltpu.VMEM((rows, 2 * CH), F32),
@@ -671,8 +672,8 @@
     received = [swap(x, "seq", mask) if mask else x for mask, x in zip(masks, packed)]
     bits = [1 << b for b in reversed(range(data_count.bit_length() - 1))]
     shared = sizes.share < patch_embed.shape[0]
-    scale, shift, proj, pos, pre, post, words = fetch(
-        sizes, place, [scales, shifts, proj_turned, pos_embed, pre_gain, post_gain, prompt]
+    scale, shift, proj, pos, pre, post, words, cot = fetch(
+        sizes, place, cotangent, [scales, shifts, proj_turned, pos_embed, pre_gain, post_gain, prompt]
     )
 
     kept, order = [], list(range(seq_count))
@@ -728,7 +729,7 @@
 
     reward, grad, weight = reward_head(
         place, latent, embed, pos, pre, post, words,
-        cotangent, modulated, grid_rows, canonical, out_factor,
+        cot, modulated, grid_rows, canonical, out_factor,
     )
     if not canonical:
         tokens = grad.reshape(grid_rows // 2, GW, 2, CH).transpose(0, 2, 1, 3)
@@ -742,7 +743,7 @@
     if query_parts > 1:
         total = total_copies(parts, 1)[0]
         parts = [total] + [swap(total, "seq", mask) for mask in range(1, query_parts)]
-    blocks = all_to_all(total_copies(parts, group_count), groups)
+    blocks = all_to_all(total_copies(parts, group_count, [attn_grad]), groups)
     return (reward[0, :1], attn_grad, finish(blocks).T)
 
 

time: 98.4 us -> 95.2 us (0.967)
  blocking collectives: 13.8 us -> 36 us
  waiting for transfers between devices: 37.7 us -> 21.3 us
  starting transfers between devices: 26.4 us -> 19.7 us
  Pallas kernels: 17.1 us -> 15.4 us
    all_to_all x1 -> x3, blocking collectives: 13.8 us -> 36 us  [all_to_all(): lax.all_to_all(x, 'seq', split_axis=0, concat_axis=0, tiled=True, axis_in...]
    all_to_all x2 -> x0, waiting for transfers between devices: 14.7 us -> none  [all_to_all(): lax.all_to_all(x, 'seq', split_axis=0, concat_axis=0, tiled=True, axis_in...]
    all_to_all x2 -> x0, starting transfers between devices: 6.8 us -> none  [all_to_all(): lax.all_to_all(x, 'seq', split_axis=0, concat_axis=0, tiled=True, axis_in...]
    ppermute x14, waiting for transfers between devices: 22.9 us -> 21.3 us  [swap(): return lax.ppermute(x, axis, [(i, i ^ mask) for i in range(count)])]
    pallas_call x2, Pallas kernels: 1.41 us -> 0.05 us  [total_copies(): pl.pallas_call(functools.partial(total_kernel, copies, len(arrays)), out_...]
  transfers between devices with their start and end apart: 17 -> 15, of which waited for: 9 -> 7; matrix products, arithmetic and copies ran while one was open for 0% -> 0% of each run, Pallas kernels for 9% -> 9%
where the time goes in v15:
time: 95.2 us; the launch traced here: 94.9 us
  blocking collectives  36 us (38%)
  waiting for transfers between devices  21.3 us (22%)
  starting transfers between devices  19.7 us (21%)
  Pallas kernels  15.4 us (16%)
  between operations  1.41 us (1%)
  local copies, waits for them, and re-layouts  1.04 us (1%)
    all_to_all x3, blocking collectives, all_to_all(): lax.all_to_all(x, 'seq', split_axis=0, concat_axis=0, tiled=True, axis_in...  36 us
    ppermute x14, waiting for transfers between devices, swap(): return lax.ppermute(x, axis, [(i, i ^ mask) for i in range(count)])  21.3 us
    ppermute x14, starting transfers between devices, swap(): return lax.ppermute(x, axis, [(i, i ^ mask) for i in range(count)])  18.2 us
    pallas_call x1, Pallas kernels, attend(): pl.pallas_call(functools.partial(attend_kernel, sizes, masks, early), out...  3.83 us
    pallas_call x1, Pallas kernels, reward_head(): pl.pallas_call(functools.partial(head_kernel, grid_rows, fused, embed_mas...  3.33 us
    pallas_call x1, Pallas kernels, pack(): pl.pallas_call(functools.partial(pack_kernel, sizes), out_shape=[jax.Shap...  1.93 us
  transfers between devices with their start and end apart: 15, of which 7 were waited for; matrix products, arithmetic and copies ran while one was open for 0% of the time, Pallas kernels for 9%

profile of v15, /device:TPU:0, one launch (start us, length us, event | category | flops | bytes accessed | tf_op | source)
XLA Modules:
  0.0 94.9 jit_solution(11698363095290195608)
XLA Ops:
  0.6 1.9 %shard_map.139 = (bf16[384,256]{1,0:T(8,128)(2,1)S(1)}, bf16[384,256]{1,0:T(8,128)(2,1)S(1)}, bf16[384,256]{1,0:T(8,128)(2,1)S(1)}, bf16[544,256]{1,0:T(8,128)(2...) custom-call(bf16[1,128,2048]{2,1,0:T(8,128)(2,1)} %q_ref.1, ...), custom_call_target="tpu_custom_call" | custom-call | bytes 3145728 | tf_op jit(solution)/shard_map/pallas_call | solution.py:136
  2.6 4.1 %collective-permute-start.3 = (bf16[544,256]{1,0:T(8,128)(2,1)S(1)}, bf16[544,256]{1,0:T(8,128)(2,1)S(1)}, u32[]{:S(2)}, u32[]{:S(2)}) collective-permute-start(bf16[544,256]{1,0:T(8,128)(2,1)S(1)} %get-tuple-element.29), channel_id=1, source_target_pairs={{0,16},{4,20},{8,24},{12,28},{16,0},{20,4},{24,8},{28,12},{1,17},{... | collective-permute-start | bytes 835592 | tf_op jit(solution)/shard_map/ppermute | solution.py:618
  6.7 1.5 %collective-permute-start = (bf16[384,256]{1,0:T(8,128)(2,1)S(1)}, bf16[384,256]{1,0:T(8,128)(2,1)S(1)}, u32[]{:S(2)}, u32[]{:S(2)}) collective-permute-start(bf16[384,256]{1,0:T(8,128)(2,1)S(1)} %get-tuple-element.26), channel_id=1, source_target_pairs={{0,4},{4,0},{8,12},{12,8},{16,20},{20,16},{24,28},{28,24},{1,5},{5... | collective-permute-start | bytes 589832 | tf_op jit(solution)/shard_map/ppermute | solution.py:618
  8.2 1.6 %collective-permute-start.1 = (bf16[384,256]{1,0:T(8,128)(2,1)S(1)}, bf16[384,256]{1,0:T(8,128)(2,1)S(1)}, u32[]{:S(2)}, u32[]{:S(2)}) collective-permute-start(bf16[384,256]{1,0:T(8,128)(2,1)S(1)} %get-tuple-element.27), channel_id=1, source_target_pairs={{0,8},{4,12},{8,0},{12,4},{16,24},{20,28},{24,16},{28,20},{1,9},{5... | collective-permute-start | bytes 589832 | tf_op jit(solution)/shard_map/ppermute | solution.py:618
  10.2 1.3 %collective-permute-start.4 = (bf16[384,256]{1,0:T(8,128)(2,1)S(1)}, bf16[384,256]{1,0:T(8,128)(2,1)S(1)}, u32[]{:S(2)}, u32[]{:S(2)}) collective-permute-start(bf16[384,256]{1,0:T(8,128)(2,1)S(1)} %get-tuple-element.30), channel_id=1, source_target_pairs={{0,20},{4,16},{8,28},{12,24},{16,4},{20,0},{24,12},{28,8},{1,21},{... | collective-permute-start | bytes 589832 | tf_op jit(solution)/shard_map/ppermute | solution.py:618
  11.5 2.2 %collective-permute-done.refs_0_ = bf16[384,256]{1,0:T(8,128)(2,1)S(1)} collective-permute-done((bf16[384,256]{1,0:T(8,128)(2,1)S(1)}, bf16[384,256]{1,0:T(8,128)(2,1)S(1)}, u32[]{:S(2)}, u32[]{:S(2)}) %collective-permute-start) | collective-permute-done | bytes 196640 | tf_op jit(solution)/shard_map/ppermute | solution.py:618
  13.6 1.4 %collective-permute-start.5 = (bf16[384,256]{1,0:T(8,128)(2,1)S(1)}, bf16[384,256]{1,0:T(8,128)(2,1)S(1)}, u32[]{:S(2)}, u32[]{:S(2)}) collective-permute-start(bf16[384,256]{1,0:T(8,128)(2,1)S(1)} %get-tuple-element.32), channel_id=1, source_target_pairs={{0,24},{4,28},{8,16},{12,20},{16,8},{20,12},{24,0},{28,4},{1,25},{... | collective-permute-start | bytes 589832 | tf_op jit(solution)/shard_map/ppermute | solution.py:618
  15.1 5.2 %collective-permute-done.3.refs_3_.refs_0_ = bf16[544,256]{1,0:T(8,128)(2,1)S(1)} collective-permute-done((bf16[544,256]{1,0:T(8,128)(2,1)S(1)}, bf16[544,256]{1,0:T(8,128)(2,1)S(1)}, u32[]{:S(2)}, u32[]{:S(2)}) %collective-permute-start.3) | collective-permute-done | bytes 278560 | tf_op jit(solution)/shard_map/ppermute | solution.py:618
  20.2 3.8 %collective-permute-start.6 = (bf16[384,256]{1,0:T(8,128)(2,1)S(1)}, bf16[384,256]{1,0:T(8,128)(2,1)S(1)}, u32[]{:S(2)}, u32[]{:S(2)}) collective-permute-start(bf16[384,256]{1,0:T(8,128)(2,1)S(1)} %get-tuple-element.33), channel_id=1, source_target_pairs={{0,28},{4,24},{8,20},{12,16},{16,12},{20,8},{24,4},{28,0},{1,29},{... | collective-permute-start | bytes 589832 | tf_op jit(solution)/shard_map/ppermute | solution.py:618
  25.1 1.6 %shard_map.140 = (f32[1,256]{1,0:T(1,128)S(1)}, f32[1,256]{1,0:T(1,128)S(1)}, bf16[64,256]{1,0:T(8,128)(2,1)S(1)}, bf16[64,1280]{1,0:T(8,128)(2,1)S(1)}, f32[128...) custom-call(s32[3]{0:T(128)S(1)} %pad_add_fusion.place_ref, f32[1]{0:T(128)S(6)} %copy.15.cot_ref, ...), custom_call_target="tpu_custom_call" | custom-call | flops 1 | bytes 1 | tf_op jit(solution)/shard_map/pallas_call | solution.py:249
  26.9 11.5 %collective-permute-done.4.refs_4_ = bf16[384,256]{1,0:T(8,128)(2,1)S(1)} collective-permute-done((bf16[384,256]{1,0:T(8,128)(2,1)S(1)}, bf16[384,256]{1,0:T(8,128)(2,1)S(1)}, u32[]{:S(2)}, u32[]{:S(2)}) %collective-permute-start.4) | collective-permute-done | bytes 196640 | tf_op jit(solution)/shard_map/ppermute | solution.py:618
  38.4 1.8 %shard_map.141 = (f32[6,2,128,128]{3,2,1,0:T(8,128)S(1)}, f32[6,2,128,128]{3,2,1,0:T(8,128)S(1)}) custom-call(bf16[384,256]{1,0:T(8,128)(2,1)S(1)} %collective-permute-done.refs_0_, bf16[384,256]{1,0:T(8,128)(2,1)S(1)} %collective-permute-done.1.refs_1_, bf16[384,256]{1,0:T(8,128)(2,1)S(1)} %collective-permute-done.2.refs_2_, ...), custom_call_target="tpu_custom_call" | custom-call | flops 1 | bytes 1 | tf_op jit(solution)/shard_map/pallas_call | solution.py:322
  40.5 1.8 %collective-permute-start.9 = (bf16[4,320,128]{2,1,0:T(8,128)(2,1)S(1)}, bf16[4,320,128]{2,1,0:T(8,128)(2,1)S(1)}, u32[]{:S(2)}, u32[]{:S(2)}) collective-permute-start(bf16[4,320,128]{2,1,0:T(8,128)(2,1)S(1)} %shard_map.145.refs_0_), channel_id=1, source_target_pairs={{0,2},{1,3},{2,0},{3,1},{4,6},{5,7},{6,4},{7,5},{8,10},{9,11},{10,... | collective-permute-start | bytes 983048 | tf_op jit(solution)/shard_map/ppermute | solution.py:618
  42.3 1.5 %collective-permute-start.10 = (bf16[4,320,128]{2,1,0:T(8,128)(2,1)S(1)}, bf16[4,320,128]{2,1,0:T(8,128)(2,1)S(1)}, u32[]{:S(2)}, u32[]{:S(2)}) collective-permute-start(bf16[4,320,128]{2,1,0:T(8,128)(2,1)S(1)} %shard_map.145.refs_0_), channel_id=1, source_target_pairs={{0,6},{1,7},{2,4},{3,5},{4,2},{5,3},{6,0},{7,1},{8,14},{9,15},{10,... | collective-permute-start | bytes 983048 | tf_op jit(solution)/shard_map/ppermute | solution.py:634
  43.8 3.8 %shard_map.142 = (bf16[8,128,256]{2,1,0:T(8,128)(2,1)S(1)}, bf16[8,64,128]{2,1,0:T(8,128)(2,1)S(1)}) custom-call(s32[3]{0:T(128)S(1)} %pad_add_fusion.place_ref, bf16[384,256]{1,0:T(8,128)(2,1)S(1)} %collective-permute-done.refs_0_, bf16[384,256]{1,0:T(8,128)(2,1)S(1)} %collective-permute-done.1.refs_1_, ...), custom_call_target="tpu_custom_call" | custom-call | flops 1073741824 | bytes 2097152 | tf_op jit(solution)/shard_map/pallas_call | solution.py:377
  47.7 13.8 %all_to_all.15.refs_0_ = bf16[8,64,128]{2,1,0:T(8,128)(2,1)S(1)} all-to-all(bf16[8,64,128]{2,1,0:T(8,128)(2,1)S(1)} %get-tuple-element.39), channel_id=1, replica_groups=mesh['seq'=8,'dp'=4] {'seq'}, dimensions={0} | all-to-all | bytes 262144 | tf_op jit(solution)/shard_map/all_to_all | solution.py:622
  62.4 10.3 %all_to_all.16 = bf16[8,64,128]{2,1,0:T(8,128)(2,1)S(1)} all-to-all(bf16[8,64,128]{2,1,0:T(8,128)(2,1)S(1)} %shard_map.143.refs_4_), channel_id=1, replica_groups=mesh['seq'=8,'dp'=4] {'seq'}, dimensions={0} | all-to-all | bytes 262144 | tf_op jit(solution)/shard_map/all_to_all | solution.py:622
  72.7 3.3 %shard_map.147 = (f32[1,128]{1,0:T(1,128)}, bf16[512,128]{1,0:T(8,128)(2,1)S(1)}, bf16[64,256]{1,0:T(8,128)(2,1)S(1)}) custom-call(s32[3]{0:T(128)S(1)} %pad_add_fusion.place_ref, bf16[512,128]{1,0:T(8,128)(2,1)S(1)} %bitcast.7, bf16[2,256,1280]{2,1,0:T(8,128)(2,1)S(1)} %shard_map.146.refs_0_, bf16[2,256,1280]{2,1,0:T(8,128)(2,1)S(1)} %collective-permute-done.11.refs_1_, ...), custom_call_target="tpu_custom_call" | custom-call | flops 503316480 | bytes 2785280 | tf_op jit(solution)/shard_map/pallas_call | solution.py:530
  76.1 1.6 %collective-permute-start.13 = (bf16[64,256]{1,0:T(8,128)(2,1)S(1)}, bf16[64,256]{1,0:T(8,128)(2,1)S(1)}, u32[]{:S(2)}, u32[]{:S(2)}) collective-permute-start(bf16[64,256]{1,0:T(8,128)(2,1)S(1)} %get-tuple-element.48.refs_0_), channel_id=1, source_target_pairs={{0,2},{1,3},{2,0},{3,1},{4,6},{5,7},{6,4},{7,5},{8,10},{9,11},{10,... | collective-permute-start | bytes 98312 | tf_op jit(solution)/shard_map/ppermute | solution.py:618
  78.0 1.1 %shard_map.148.refs_4_ = bf16[1,2,1024,128]{3,2,1,0:T(8,128)(2,1)} custom-call(bf16[512,128]{1,0:T(8,128)(2,1)S(1)} %get-tuple-element.47.grad_ref, f32[1,256]{1,0:T(1,128)S(1)} %get-tuple-element.34.refs_6_.refs_10_.scale_ref, bf16[64,256]{1,0:T(8,128)(2,1)S(1)} %get-tuple-element.38.refs_12_.proj_ref), custom_call_target="tpu_custom_call" | custom-call | flops 67108864 | bytes 524288 | tf_op jit(solution)/shard_map/pallas_call | solution.py:572
  79.1 1.0 %collective-permute-done.13.refs_2_ = bf16[64,256]{1,0:T(8,128)(2,1)S(1)} collective-permute-done((bf16[64,256]{1,0:T(8,128)(2,1)S(1)}, bf16[64,256]{1,0:T(8,128)(2,1)S(1)}, u32[]{:S(2)}, u32[]{:S(2)}) %collective-permute-start.13) | collective-permute-done | bytes 32800 | tf_op jit(solution)/shard_map/ppermute | solution.py:618
  80.1 0.9 collective-permute-done.14.refs_3_
  81.0 1.0 %copy-done = bf16[1,2,1024,128]{3,2,1,0:T(8,128)(2,1)S(1)} copy-done((bf16[1,2,1024,128]{3,2,1,0:T(8,128)(2,1)S(1)}, bf16[1,2,1024,128]{3,2,1,0:T(8,128)(2,1)}, u32[]{:S(2)}) %copy-start) | copy-done | bytes 524312
  82.1 11.9 %all_to_all.17.in_ref = bf16[8,64,256]{2,1,0:T(8,128)(2,1)S(1)} all-to-all(bf16[8,64,256]{2,1,0:T(8,128)(2,1)S(1)} %shard_map.149), channel_id=1, replica_groups=mesh['seq'=8,'dp'=4] {'seq'}, dimensions={0} | all-to-all | bytes 524288 | tf_op jit(solution)/shard_map/all_to_all | solution.py:622
  (24 shorter events, 3.5 us)
Async XLA Ops:
  2.6 17.7 %collective-permute-start.3 = (bf16[544,256]{1,0:T(8,128)(2,1)S(1)}, bf16[544,256]{1,0:T(8,128)(2,1)S(1)}, u32[]{:S(2)}, u32[]{:S(2)}) collective-permute-start(bf16[544,256]{1,0:T(8,128)(2,1)S(1)} %get-tuple-element.29), channel_id=1, source_target_pairs={{0,16},{4,20},{8,24},{12,28},{16,0},{20,4},{24,8},{28,12},{1,17},{... | collective-permute-start | bytes 835592 | tf_op jit(solution)/shard_map/ppermute | solution.py:618
  6.7 6.9 %collective-permute-start = (bf16[384,256]{1,0:T(8,128)(2,1)S(1)}, bf16[384,256]{1,0:T(8,128)(2,1)S(1)}, u32[]{:S(2)}, u32[]{:S(2)}) collective-permute-start(bf16[384,256]{1,0:T(8,128)(2,1)S(1)} %get-tuple-element.26), channel_id=1, source_target_pairs={{0,4},{4,0},{8,12},{12,8},{16,20},{20,16},{24,28},{28,24},{1,5},{5... | collective-permute-start | bytes 589832 | tf_op jit(solution)/shard_map/ppermute | solution.py:618
  8.2 16.1 %collective-permute-start.1 = (bf16[384,256]{1,0:T(8,128)(2,1)S(1)}, bf16[384,256]{1,0:T(8,128)(2,1)S(1)}, u32[]{:S(2)}, u32[]{:S(2)}) collective-permute-start(bf16[384,256]{1,0:T(8,128)(2,1)S(1)} %get-tuple-element.27), channel_id=1, source_target_pairs={{0,8},{4,12},{8,0},{12,4},{16,24},{20,28},{24,16},{28,20},{1,9},{5... | collective-permute-start | bytes 589832 | tf_op jit(solution)/shard_map/ppermute | solution.py:618
  9.8 17.1 %collective-permute-start.2 = (bf16[384,256]{1,0:T(8,128)(2,1)S(1)}, bf16[384,256]{1,0:T(8,128)(2,1)S(1)}, u32[]{:S(2)}, u32[]{:S(2)}) collective-permute-start(bf16[384,256]{1,0:T(8,128)(2,1)S(1)} %get-tuple-element.28), channel_id=1, source_target_pairs={{0,12},{4,8},{8,4},{12,0},{16,28},{20,24},{24,20},{28,16},{1,13},{... | collective-permute-start | bytes 589832 | tf_op jit(solution)/shard_map/ppermute | solution.py:618
  10.2 28.2 %collective-permute-start.4 = (bf16[384,256]{1,0:T(8,128)(2,1)S(1)}, bf16[384,256]{1,0:T(8,128)(2,1)S(1)}, u32[]{:S(2)}, u32[]{:S(2)}) collective-permute-start(bf16[384,256]{1,0:T(8,128)(2,1)S(1)} %get-tuple-element.30), channel_id=1, source_target_pairs={{0,20},{4,16},{8,28},{12,24},{16,4},{20,0},{24,12},{28,8},{1,21},{... | collective-permute-start | bytes 589832 | tf_op jit(solution)/shard_map/ppermute | solution.py:618
  13.6 30.2 %collective-permute-start.5 = (bf16[384,256]{1,0:T(8,128)(2,1)S(1)}, bf16[384,256]{1,0:T(8,128)(2,1)S(1)}, u32[]{:S(2)}, u32[]{:S(2)}) collective-permute-start(bf16[384,256]{1,0:T(8,128)(2,1)S(1)} %get-tuple-element.32), channel_id=1, source_target_pairs={{0,24},{4,28},{8,16},{12,20},{16,8},{20,12},{24,0},{28,4},{1,25},{... | collective-permute-start | bytes 589832 | tf_op jit(solution)/shard_map/ppermute | solution.py:618
  20.2 23.6 %collective-permute-start.6 = (bf16[384,256]{1,0:T(8,128)(2,1)S(1)}, bf16[384,256]{1,0:T(8,128)(2,1)S(1)}, u32[]{:S(2)}, u32[]{:S(2)}) collective-permute-start(bf16[384,256]{1,0:T(8,128)(2,1)S(1)} %get-tuple-element.33), channel_id=1, source_target_pairs={{0,28},{4,24},{8,20},{12,16},{16,12},{20,8},{24,4},{28,0},{1,29},{... | collective-permute-start | bytes 589832 | tf_op jit(solution)/shard_map/ppermute | solution.py:618
  24.3 15.9 %collective-permute-start.7 = (bf16[2,320,128]{2,1,0:T(8,128)(2,1)S(1)}, bf16[2,320,128]{2,1,0:T(8,128)(2,1)S(1)}, u32[]{:S(2)}, u32[]{:S(2)}) collective-permute-start(bf16[2,320,128]{2,1,0:T(8,128)(2,1)S(1)} %shard_map.144.first_ref), channel_id=1, source_target_pairs={{0,8},{4,12},{8,0},{12,4},{16,24},{20,28},{24,16},{28,20},{1,9},{5... | collective-permute-start | bytes 491528 | tf_op jit(solution)/shard_map/ppermute | solution.py:618
  40.3 21.2 %collective-permute-start.8 = (bf16[4,320,128]{2,1,0:T(8,128)(2,1)S(1)}, bf16[4,320,128]{2,1,0:T(8,128)(2,1)S(1)}, u32[]{:S(2)}, u32[]{:S(2)}) collective-permute-start(bf16[4,320,128]{2,1,0:T(8,128)(2,1)S(1)} %shard_map.145.refs_0_), channel_id=1, source_target_pairs={{0,4},{4,0},{8,12},{12,8},{16,20},{20,16},{24,28},{28,24},{1,5},{5... | collective-permute-start | bytes 983048 | tf_op jit(solution)/shard_map/ppermute | solution.py:618
  40.5 21.0 %collective-permute-start.9 = (bf16[4,320,128]{2,1,0:T(8,128)(2,1)S(1)}, bf16[4,320,128]{2,1,0:T(8,128)(2,1)S(1)}, u32[]{:S(2)}, u32[]{:S(2)}) collective-permute-start(bf16[4,320,128]{2,1,0:T(8,128)(2,1)S(1)} %shard_map.145.refs_0_), channel_id=1, source_target_pairs={{0,2},{1,3},{2,0},{3,1},{4,6},{5,7},{6,4},{7,5},{8,10},{9,11},{10,... | collective-permute-start | bytes 983048 | tf_op jit(solution)/shard_map/ppermute | solution.py:618
  42.3 19.2 %collective-permute-start.10 = (bf16[4,320,128]{2,1,0:T(8,128)(2,1)S(1)}, bf16[4,320,128]{2,1,0:T(8,128)(2,1)S(1)}, u32[]{:S(2)}, u32[]{:S(2)}) collective-permute-start(bf16[4,320,128]{2,1,0:T(8,128)(2,1)S(1)} %shard_map.145.refs_0_), channel_id=1, source_target_pairs={{0,6},{1,7},{2,4},{3,5},{4,2},{5,3},{6,0},{7,1},{8,14},{9,15},{10,... | collective-permute-start | bytes 983048 | tf_op jit(solution)/shard_map/ppermute | solution.py:634
  62.3 10.4 %collective-permute-start.11 = (bf16[2,256,1280]{2,1,0:T(8,128)(2,1)S(1)}, bf16[2,256,1280]{2,1,0:T(8,128)(2,1)S(1)}, u32[]{:S(2)}, u32[]{:S(2)}) collective-permute-start(bf16[2,256,1280]{2,1,0:T(8,128)(2,1)S(1)} %shard_map.146.refs_0_), channel_id=1, source_target_pairs={{0,1},{1,0},{2,3},{3,2},{4,5},{5,4},{6,7},{7,6},{8,9},{9,8},{10,11... | collective-permute-start | bytes 3932168 | tf_op jit(solution)/shard_map/ppermute | solution.py:618
  76.1 3.0 %collective-permute-start.12 = (bf16[64,256]{1,0:T(8,128)(2,1)S(1)}, bf16[64,256]{1,0:T(8,128)(2,1)S(1)}, u32[]{:S(2)}, u32[]{:S(2)}) collective-permute-start(bf16[64,256]{1,0:T(8,128)(2,1)S(1)} %get-tuple-element.48.refs_0_), channel_id=1, source_target_pairs={{0,1},{1,0},{2,3},{3,2},{4,5},{5,4},{6,7},{7,6},{8,9},{9,8},{10,11... | collective-permute-start | bytes 98312 | tf_op jit(solution)/shard_map/ppermute | solution.py:618
  76.1 4.0 %collective-permute-start.13 = (bf16[64,256]{1,0:T(8,128)(2,1)S(1)}, bf16[64,256]{1,0:T(8,128)(2,1)S(1)}, u32[]{:S(2)}, u32[]{:S(2)}) collective-permute-start(bf16[64,256]{1,0:T(8,128)(2,1)S(1)} %get-tuple-element.48.refs_0_), channel_id=1, source_target_pairs={{0,2},{1,3},{2,0},{3,1},{4,6},{5,7},{6,4},{7,5},{8,10},{9,11},{10,... | collective-permute-start | bytes 98312 | tf_op jit(solution)/shard_map/ppermute | solution.py:618
  77.7 3.3 %collective-permute-start.14 = (bf16[64,256]{1,0:T(8,128)(2,1)S(1)}, bf16[64,256]{1,0:T(8,128)(2,1)S(1)}, u32[]{:S(2)}, u32[]{:S(2)}) collective-permute-start(bf16[64,256]{1,0:T(8,128)(2,1)S(1)} %get-tuple-element.48.refs_0_), channel_id=1, source_target_pairs={{0,3},{1,2},{2,1},{3,0},{4,7},{5,6},{6,5},{7,4},{8,11},{9,10},{10,... | collective-permute-start | bytes 98312 | tf_op jit(solution)/shard_map/ppermute | solution.py:618
  81.0 1.0 %copy-start = (bf16[1,2,1024,128]{3,2,1,0:T(8,128)(2,1)S(1)}, bf16[1,2,1024,128]{3,2,1,0:T(8,128)(2,1)}, u32[]{:S(2)}) copy-start(bf16[1,2,1024,128]{3,2,1,0:T(8,128)(2,1)} %shard_map.148.refs_4_) | copy-start | bytes 1572868

commit v16 on v15

--- a/solution.py
+++ b/solution.py
@@ -408,7 +408,7 @@
     return pl.pallas_call(
         functools.partial(total_kernel, copies, len(arrays)),
         out_shape=jax.ShapeDtypeStruct((copies,) + arrays[0].shape[-2:], BF16),
-        in_specs=[VMEM_SPEC] * len(arrays) + [ANY_SPEC] * len(others),
+        in_specs=[VMEM_SPEC] * (len(arrays) + len(others)),
         out_specs=VMEM_SPEC,
         compiler_params=limits(),
     )(*arrays, *others)
@@ -553,7 +553,8 @@
     )(place, latent, *embed_arrays, pos, pre, post, prompt, cot, modulated)
 
 
-def spread_kernel(count, half, heads, grad_ref, scale_ref, proj_ref, out_ref):
+def spread_kernel(count, half, heads, grad_ref, scale_ref, proj_ref, out_ref, token_ref):
+    token_ref[...] = jnp.zeros_like(token_ref)
     gain = 1.0 + scale_ref[...]
     proj = proj_ref[...]
     zero = jnp.zeros_like(proj)
@@ -571,9 +572,12 @@
 def spread(grad, scales, proj, count, half, heads):
     return pl.pallas_call(
         functools.partial(spread_kernel, count, half, heads),
-        out_shape=jax.ShapeDtypeStruct((1, heads, 2 * count * half, HD), BF16),
+        out_shape=(
+            jax.ShapeDtypeStruct((1, heads, 2 * count * half, HD), BF16),
+            jax.ShapeDtypeStruct((8, 128), F32),
+        ),
         in_specs=[VMEM_SPEC] * 3,
-        out_specs=VMEM_SPEC,
+        out_specs=(VMEM_SPEC, VMEM_SPEC),
         compiler_params=limits(),
         cost_estimate=pl.CostEstimate(
             flops=8 * count * half * CH * heads * HD,
@@ -739,11 +743,11 @@
         weight = weight_call(grad, modulated, out_factor)
 
     parts = [weight] + [swap(weight, "dp", mask) for mask in range(1, data_count)]
-    attn_grad = spread(grad, scale, proj, seq_count, half, head_count)
+    attn_grad, token = spread(grad, scale, proj, seq_count, half, head_count)
     if query_parts > 1:
         total = total_copies(parts, 1)[0]
         parts = [total] + [swap(total, "seq", mask) for mask in range(1, query_parts)]
-    blocks = all_to_all(total_copies(parts, group_count, [attn_grad]), groups)
+    blocks = all_to_all(total_copies(parts, group_count, [token]), groups)
     return (reward[0, :1], attn_grad, finish(blocks).T)
 
 

time: 95.2 us -> 94.1 us (0.988)
  local copies, waits for them, and re-layouts: 1.04 us -> 0 us
    unnamed x2 -> x0, local copies, waits for them, and re-layouts: 1.04 us -> none
where the time goes in v16:
time: 94.1 us; the launch traced here: 93.8 us
  blocking collectives  36 us (38%)
  waiting for transfers between devices  21.3 us (23%)
  starting transfers between devices  19.7 us (21%)
  Pallas kernels  15.4 us (16%)
  between operations  1.41 us (1%)
    all_to_all x3, blocking collectives, all_to_all(): lax.all_to_all(x, 'seq', split_axis=0, concat_axis=0, tiled=True, axis_in...  36 us
    ppermute x14, waiting for transfers between devices, swap(): return lax.ppermute(x, axis, [(i, i ^ mask) for i in range(count)])  21.3 us
    ppermute x14, starting transfers between devices, swap(): return lax.ppermute(x, axis, [(i, i ^ mask) for i in range(count)])  18.2 us
    pallas_call x1, Pallas kernels, attend(): pl.pallas_call(functools.partial(attend_kernel, sizes, masks, early), out...  3.83 us
    pallas_call x1, Pallas kernels, reward_head(): pl.pallas_call(functools.partial(head_kernel, grid_rows, fused, embed_mas...  3.33 us
    pallas_call x1, Pallas kernels, pack(): pl.pallas_call(functools.partial(pack_kernel, sizes), out_shape=[jax.Shap...  1.93 us
  transfers between devices with their start and end apart: 15, of which 7 were waited for; matrix products, arithmetic and copies ran while one was open for 0% of the time, Pallas kernels for 9%

profile of v16, /device:TPU:0, one launch (start us, length us, event | category | flops | bytes accessed | tf_op | source)
XLA Modules:
  0.0 93.8 jit_solution(5655877872018903147)
XLA Ops:
  0.6 1.9 %shard_map.139 = (bf16[384,256]{1,0:T(8,128)(2,1)S(1)}, bf16[384,256]{1,0:T(8,128)(2,1)S(1)}, bf16[384,256]{1,0:T(8,128)(2,1)S(1)}, bf16[544,256]{1,0:T(8,128)(2...) custom-call(bf16[1,128,2048]{2,1,0:T(8,128)(2,1)} %q_ref.1, ...), custom_call_target="tpu_custom_call" | custom-call | bytes 3145728 | tf_op jit(solution)/shard_map/pallas_call | solution.py:136
  2.6 4.1 %collective-permute-start.3 = (bf16[544,256]{1,0:T(8,128)(2,1)S(1)}, bf16[544,256]{1,0:T(8,128)(2,1)S(1)}, u32[]{:S(2)}, u32[]{:S(2)}) collective-permute-start(bf16[544,256]{1,0:T(8,128)(2,1)S(1)} %get-tuple-element.31), channel_id=1, source_target_pairs={{0,16},{4,20},{8,24},{12,28},{16,0},{20,4},{24,8},{28,12},{1,17},{... | collective-permute-start | bytes 835592 | tf_op jit(solution)/shard_map/ppermute | solution.py:622
  6.7 1.5 %collective-permute-start = (bf16[384,256]{1,0:T(8,128)(2,1)S(1)}, bf16[384,256]{1,0:T(8,128)(2,1)S(1)}, u32[]{:S(2)}, u32[]{:S(2)}) collective-permute-start(bf16[384,256]{1,0:T(8,128)(2,1)S(1)} %get-tuple-element.28), channel_id=1, source_target_pairs={{0,4},{4,0},{8,12},{12,8},{16,20},{20,16},{24,28},{28,24},{1,5},{5... | collective-permute-start | bytes 589832 | tf_op jit(solution)/shard_map/ppermute | solution.py:622
  8.2 1.6 %collective-permute-start.1 = (bf16[384,256]{1,0:T(8,128)(2,1)S(1)}, bf16[384,256]{1,0:T(8,128)(2,1)S(1)}, u32[]{:S(2)}, u32[]{:S(2)}) collective-permute-start(bf16[384,256]{1,0:T(8,128)(2,1)S(1)} %get-tuple-element.29), channel_id=1, source_target_pairs={{0,8},{4,12},{8,0},{12,4},{16,24},{20,28},{24,16},{28,20},{1,9},{5... | collective-permute-start | bytes 589832 | tf_op jit(solution)/shard_map/ppermute | solution.py:622
  10.2 1.3 %collective-permute-start.4 = (bf16[384,256]{1,0:T(8,128)(2,1)S(1)}, bf16[384,256]{1,0:T(8,128)(2,1)S(1)}, u32[]{:S(2)}, u32[]{:S(2)}) collective-permute-start(bf16[384,256]{1,0:T(8,128)(2,1)S(1)} %get-tuple-element.32), channel_id=1, source_target_pairs={{0,20},{4,16},{8,28},{12,24},{16,4},{20,0},{24,12},{28,8},{1,21},{... | collective-permute-start | bytes 589832 | tf_op jit(solution)/shard_map/ppermute | solution.py:622
  11.5 2.2 %collective-permute-done.refs_0_ = bf16[384,256]{1,0:T(8,128)(2,1)S(1)} collective-permute-done((bf16[384,256]{1,0:T(8,128)(2,1)S(1)}, bf16[384,256]{1,0:T(8,128)(2,1)S(1)}, u32[]{:S(2)}, u32[]{:S(2)}) %collective-permute-start) | collective-permute-done | bytes 196640 | tf_op jit(solution)/shard_map/ppermute | solution.py:622
  13.6 1.4 %collective-permute-start.5 = (bf16[384,256]{1,0:T(8,128)(2,1)S(1)}, bf16[384,256]{1,0:T(8,128)(2,1)S(1)}, u32[]{:S(2)}, u32[]{:S(2)}) collective-permute-start(bf16[384,256]{1,0:T(8,128)(2,1)S(1)} %get-tuple-element.34), channel_id=1, source_target_pairs={{0,24},{4,28},{8,16},{12,20},{16,8},{20,12},{24,0},{28,4},{1,25},{... | collective-permute-start | bytes 589832 | tf_op jit(solution)/shard_map/ppermute | solution.py:622
  15.1 5.2 %collective-permute-done.3.refs_3_.refs_0_ = bf16[544,256]{1,0:T(8,128)(2,1)S(1)} collective-permute-done((bf16[544,256]{1,0:T(8,128)(2,1)S(1)}, bf16[544,256]{1,0:T(8,128)(2,1)S(1)}, u32[]{:S(2)}, u32[]{:S(2)}) %collective-permute-start.3) | collective-permute-done | bytes 278560 | tf_op jit(solution)/shard_map/ppermute | solution.py:622
  20.2 3.8 %collective-permute-start.6 = (bf16[384,256]{1,0:T(8,128)(2,1)S(1)}, bf16[384,256]{1,0:T(8,128)(2,1)S(1)}, u32[]{:S(2)}, u32[]{:S(2)}) collective-permute-start(bf16[384,256]{1,0:T(8,128)(2,1)S(1)} %get-tuple-element.35), channel_id=1, source_target_pairs={{0,28},{4,24},{8,20},{12,16},{16,12},{20,8},{24,4},{28,0},{1,29},{... | collective-permute-start | bytes 589832 | tf_op jit(solution)/shard_map/ppermute | solution.py:622
  25.1 1.6 %shard_map.140 = (f32[1,256]{1,0:T(1,128)S(1)}, f32[1,256]{1,0:T(1,128)S(1)}, bf16[64,256]{1,0:T(8,128)(2,1)S(1)}, bf16[64,1280]{1,0:T(8,128)(2,1)S(1)}, f32[128...) custom-call(s32[3]{0:T(128)S(1)} %pad_add_fusion.place_ref, f32[1]{0:T(128)S(6)} %copy.15.cot_ref, ...), custom_call_target="tpu_custom_call" | custom-call | flops 1 | bytes 1 | tf_op jit(solution)/shard_map/pallas_call | solution.py:249
  26.9 11.5 %collective-permute-done.4.refs_4_ = bf16[384,256]{1,0:T(8,128)(2,1)S(1)} collective-permute-done((bf16[384,256]{1,0:T(8,128)(2,1)S(1)}, bf16[384,256]{1,0:T(8,128)(2,1)S(1)}, u32[]{:S(2)}, u32[]{:S(2)}) %collective-permute-start.4) | collective-permute-done | bytes 196640 | tf_op jit(solution)/shard_map/ppermute | solution.py:622
  38.4 1.8 %shard_map.141 = (f32[6,2,128,128]{3,2,1,0:T(8,128)S(1)}, f32[6,2,128,128]{3,2,1,0:T(8,128)S(1)}) custom-call(bf16[384,256]{1,0:T(8,128)(2,1)S(1)} %collective-permute-done.refs_0_, bf16[384,256]{1,0:T(8,128)(2,1)S(1)} %collective-permute-done.1.refs_1_, bf16[384,256]{1,0:T(8,128)(2,1)S(1)} %collective-permute-done.2.refs_2_, ...), custom_call_target="tpu_custom_call" | custom-call | flops 1 | bytes 1 | tf_op jit(solution)/shard_map/pallas_call | solution.py:322
  40.5 1.8 %collective-permute-start.9 = (bf16[4,320,128]{2,1,0:T(8,128)(2,1)S(1)}, bf16[4,320,128]{2,1,0:T(8,128)(2,1)S(1)}, u32[]{:S(2)}, u32[]{:S(2)}) collective-permute-start(bf16[4,320,128]{2,1,0:T(8,128)(2,1)S(1)} %shard_map.145.refs_0_), channel_id=1, source_target_pairs={{0,2},{1,3},{2,0},{3,1},{4,6},{5,7},{6,4},{7,5},{8,10},{9,11},{10,... | collective-permute-start | bytes 983048 | tf_op jit(solution)/shard_map/ppermute | solution.py:622
  42.3 1.5 %collective-permute-start.10 = (bf16[4,320,128]{2,1,0:T(8,128)(2,1)S(1)}, bf16[4,320,128]{2,1,0:T(8,128)(2,1)S(1)}, u32[]{:S(2)}, u32[]{:S(2)}) collective-permute-start(bf16[4,320,128]{2,1,0:T(8,128)(2,1)S(1)} %shard_map.145.refs_0_), channel_id=1, source_target_pairs={{0,6},{1,7},{2,4},{3,5},{4,2},{5,3},{6,0},{7,1},{8,14},{9,15},{10,... | collective-permute-start | bytes 983048 | tf_op jit(solution)/shard_map/ppermute | solution.py:638
  43.8 3.8 %shard_map.142 = (bf16[8,128,256]{2,1,0:T(8,128)(2,1)S(1)}, bf16[8,64,128]{2,1,0:T(8,128)(2,1)S(1)}) custom-call(s32[3]{0:T(128)S(1)} %pad_add_fusion.place_ref, bf16[384,256]{1,0:T(8,128)(2,1)S(1)} %collective-permute-done.refs_0_, bf16[384,256]{1,0:T(8,128)(2,1)S(1)} %collective-permute-done.1.refs_1_, ...), custom_call_target="tpu_custom_call" | custom-call | flops 1073741824 | bytes 2097152 | tf_op jit(solution)/shard_map/pallas_call | solution.py:377
  47.7 13.8 %all_to_all.15.refs_0_ = bf16[8,64,128]{2,1,0:T(8,128)(2,1)S(1)} all-to-all(bf16[8,64,128]{2,1,0:T(8,128)(2,1)S(1)} %get-tuple-element.41), channel_id=1, replica_groups=mesh['seq'=8,'dp'=4] {'seq'}, dimensions={0} | all-to-all | bytes 262144 | tf_op jit(solution)/shard_map/all_to_all | solution.py:626
  61.5 0.8 shard_map.146.refs_0_
  62.4 10.3 %all_to_all.16 = bf16[8,64,128]{2,1,0:T(8,128)(2,1)S(1)} all-to-all(bf16[8,64,128]{2,1,0:T(8,128)(2,1)S(1)} %shard_map.143.refs_4_), channel_id=1, replica_groups=mesh['seq'=8,'dp'=4] {'seq'}, dimensions={0} | all-to-all | bytes 262144 | tf_op jit(solution)/shard_map/all_to_all | solution.py:626
  72.7 3.3 %shard_map.147 = (f32[1,128]{1,0:T(1,128)}, bf16[512,128]{1,0:T(8,128)(2,1)S(1)}, bf16[64,256]{1,0:T(8,128)(2,1)S(1)}) custom-call(s32[3]{0:T(128)S(1)} %pad_add_fusion.place_ref, bf16[512,128]{1,0:T(8,128)(2,1)S(1)} %bitcast.7, bf16[2,256,1280]{2,1,0:T(8,128)(2,1)S(1)} %shard_map.146.refs_0_, bf16[2,256,1280]{2,1,0:T(8,128)(2,1)S(1)} %collective-permute-done.11.refs_1_, ...), custom_call_target="tpu_custom_call" | custom-call | flops 503316480 | bytes 2785280 | tf_op jit(solution)/shard_map/pallas_call | solution.py:530
  76.1 1.6 %collective-permute-start.13 = (bf16[64,256]{1,0:T(8,128)(2,1)S(1)}, bf16[64,256]{1,0:T(8,128)(2,1)S(1)}, u32[]{:S(2)}, u32[]{:S(2)}) collective-permute-start(bf16[64,256]{1,0:T(8,128)(2,1)S(1)} %get-tuple-element.51.refs_0_), channel_id=1, source_target_pairs={{0,2},{1,3},{2,0},{3,1},{4,6},{5,7},{6,4},{7,5},{8,10},{9,11},{10,... | collective-permute-start | bytes 98312 | tf_op jit(solution)/shard_map/ppermute | solution.py:622
  78.0 1.1 %shard_map.148 = (bf16[1,2,1024,128]{3,2,1,0:T(8,128)(2,1)}, f32[8,128]{1,0:T(8,128)S(1)}) custom-call(bf16[512,128]{1,0:T(8,128)(2,1)S(1)} %get-tuple-element.49.grad_ref, f32[1,256]{1,0:T(1,128)S(1)} %get-tuple-element.36.refs_6_.refs_10_.scale_ref, bf16[64,256]{1,0:T(8,128)(2,1)S(1)} %get-tuple-element.40.refs_12_.proj_ref), custom_call_target="tpu_custom_call" | custom-call | flops 67108864 | bytes 524288 | tf_op jit(solution)/shard_map/pallas_call | solution.py:573
  79.1 1.0 %collective-permute-done.13.refs_2_ = bf16[64,256]{1,0:T(8,128)(2,1)S(1)} collective-permute-done((bf16[64,256]{1,0:T(8,128)(2,1)S(1)}, bf16[64,256]{1,0:T(8,128)(2,1)S(1)}, u32[]{:S(2)}, u32[]{:S(2)}) %collective-permute-start.13) | collective-permute-done | bytes 32800 | tf_op jit(solution)/shard_map/ppermute | solution.py:622
  80.1 0.9 collective-permute-done.14.refs_3_
  81.1 11.9 %all_to_all.17.in_ref = bf16[8,64,256]{2,1,0:T(8,128)(2,1)S(1)} all-to-all(bf16[8,64,256]{2,1,0:T(8,128)(2,1)S(1)} %shard_map.149), channel_id=1, replica_groups=mesh['seq'=8,'dp'=4] {'seq'}, dimensions={0} | all-to-all | bytes 524288 | tf_op jit(solution)/shard_map/all_to_all | solution.py:626
  (22 shorter events, 2.6 us)
Async XLA Ops:
  2.6 17.7 %collective-permute-start.3 = (bf16[544,256]{1,0:T(8,128)(2,1)S(1)}, bf16[544,256]{1,0:T(8,128)(2,1)S(1)}, u32[]{:S(2)}, u32[]{:S(2)}) collective-permute-start(bf16[544,256]{1,0:T(8,128)(2,1)S(1)} %get-tuple-element.31), channel_id=1, source_target_pairs={{0,16},{4,20},{8,24},{12,28},{16,0},{20,4},{24,8},{28,12},{1,17},{... | collective-permute-start | bytes 835592 | tf_op jit(solution)/shard_map/ppermute | solution.py:622
  6.7 6.9 %collective-permute-start = (bf16[384,256]{1,0:T(8,128)(2,1)S(1)}, bf16[384,256]{1,0:T(8,128)(2,1)S(1)}, u32[]{:S(2)}, u32[]{:S(2)}) collective-permute-start(bf16[384,256]{1,0:T(8,128)(2,1)S(1)} %get-tuple-element.28), channel_id=1, source_target_pairs={{0,4},{4,0},{8,12},{12,8},{16,20},{20,16},{24,28},{28,24},{1,5},{5... | collective-permute-start | bytes 589832 | tf_op jit(solution)/shard_map/ppermute | solution.py:622
  8.2 16.1 %collective-permute-start.1 = (bf16[384,256]{1,0:T(8,128)(2,1)S(1)}, bf16[384,256]{1,0:T(8,128)(2,1)S(1)}, u32[]{:S(2)}, u32[]{:S(2)}) collective-permute-start(bf16[384,256]{1,0:T(8,128)(2,1)S(1)} %get-tuple-element.29), channel_id=1, source_target_pairs={{0,8},{4,12},{8,0},{12,4},{16,24},{20,28},{24,16},{28,20},{1,9},{5... | collective-permute-start | bytes 589832 | tf_op jit(solution)/shard_map/ppermute | solution.py:622
  9.8 17.1 %collective-permute-start.2 = (bf16[384,256]{1,0:T(8,128)(2,1)S(1)}, bf16[384,256]{1,0:T(8,128)(2,1)S(1)}, u32[]{:S(2)}, u32[]{:S(2)}) collective-permute-start(bf16[384,256]{1,0:T(8,128)(2,1)S(1)} %get-tuple-element.30), channel_id=1, source_target_pairs={{0,12},{4,8},{8,4},{12,0},{16,28},{20,24},{24,20},{28,16},{1,13},{... | collective-permute-start | bytes 589832 | tf_op jit(solution)/shard_map/ppermute | solution.py:622
  10.2 28.2 %collective-permute-start.4 = (bf16[384,256]{1,0:T(8,128)(2,1)S(1)}, bf16[384,256]{1,0:T(8,128)(2,1)S(1)}, u32[]{:S(2)}, u32[]{:S(2)}) collective-permute-start(bf16[384,256]{1,0:T(8,128)(2,1)S(1)} %get-tuple-element.32), channel_id=1, source_target_pairs={{0,20},{4,16},{8,28},{12,24},{16,4},{20,0},{24,12},{28,8},{1,21},{... | collective-permute-start | bytes 589832 | tf_op jit(solution)/shard_map/ppermute | solution.py:622
  13.6 30.2 %collective-permute-start.5 = (bf16[384,256]{1,0:T(8,128)(2,1)S(1)}, bf16[384,256]{1,0:T(8,128)(2,1)S(1)}, u32[]{:S(2)}, u32[]{:S(2)}) collective-permute-start(bf16[384,256]{1,0:T(8,128)(2,1)S(1)} %get-tuple-element.34), channel_id=1, source_target_pairs={{0,24},{4,28},{8,16},{12,20},{16,8},{20,12},{24,0},{28,4},{1,25},{... | collective-permute-start | bytes 589832 | tf_op jit(solution)/shard_map/ppermute | solution.py:622
  20.2 23.6 %collective-permute-start.6 = (bf16[384,256]{1,0:T(8,128)(2,1)S(1)}, bf16[384,256]{1,0:T(8,128)(2,1)S(1)}, u32[]{:S(2)}, u32[]{:S(2)}) collective-permute-start(bf16[384,256]{1,0:T(8,128)(2,1)S(1)} %get-tuple-element.35), channel_id=1, source_target_pairs={{0,28},{4,24},{8,20},{12,16},{16,12},{20,8},{24,4},{28,0},{1,29},{... | collective-permute-start | bytes 589832 | tf_op jit(solution)/shard_map/ppermute | solution.py:622
  24.3 15.9 %collective-permute-start.7 = (bf16[2,320,128]{2,1,0:T(8,128)(2,1)S(1)}, bf16[2,320,128]{2,1,0:T(8,128)(2,1)S(1)}, u32[]{:S(2)}, u32[]{:S(2)}) collective-permute-start(bf16[2,320,128]{2,1,0:T(8,128)(2,1)S(1)} %shard_map.144.first_ref), channel_id=1, source_target_pairs={{0,8},{4,12},{8,0},{12,4},{16,24},{20,28},{24,16},{28,20},{1,9},{5... | collective-permute-start | bytes 491528 | tf_op jit(solution)/shard_map/ppermute | solution.py:622
  40.3 21.2 %collective-permute-start.8 = (bf16[4,320,128]{2,1,0:T(8,128)(2,1)S(1)}, bf16[4,320,128]{2,1,0:T(8,128)(2,1)S(1)}, u32[]{:S(2)}, u32[]{:S(2)}) collective-permute-start(bf16[4,320,128]{2,1,0:T(8,128)(2,1)S(1)} %shard_map.145.refs_0_), channel_id=1, source_target_pairs={{0,4},{4,0},{8,12},{12,8},{16,20},{20,16},{24,28},{28,24},{1,5},{5... | collective-permute-start | bytes 983048 | tf_op jit(solution)/shard_map/ppermute | solution.py:622
  40.5 21.0 %collective-permute-start.9 = (bf16[4,320,128]{2,1,0:T(8,128)(2,1)S(1)}, bf16[4,320,128]{2,1,0:T(8,128)(2,1)S(1)}, u32[]{:S(2)}, u32[]{:S(2)}) collective-permute-start(bf16[4,320,128]{2,1,0:T(8,128)(2,1)S(1)} %shard_map.145.refs_0_), channel_id=1, source_target_pairs={{0,2},{1,3},{2,0},{3,1},{4,6},{5,7},{6,4},{7,5},{8,10},{9,11},{10,... | collective-permute-start | bytes 983048 | tf_op jit(solution)/shard_map/ppermute | solution.py:622
  42.3 19.2 %collective-permute-start.10 = (bf16[4,320,128]{2,1,0:T(8,128)(2,1)S(1)}, bf16[4,320,128]{2,1,0:T(8,128)(2,1)S(1)}, u32[]{:S(2)}, u32[]{:S(2)}) collective-permute-start(bf16[4,320,128]{2,1,0:T(8,128)(2,1)S(1)} %shard_map.145.refs_0_), channel_id=1, source_target_pairs={{0,6},{1,7},{2,4},{3,5},{4,2},{5,3},{6,0},{7,1},{8,14},{9,15},{10,... | collective-permute-start | bytes 983048 | tf_op jit(solution)/shard_map/ppermute | solution.py:638
  62.3 10.4 %collective-permute-start.11 = (bf16[2,256,1280]{2,1,0:T(8,128)(2,1)S(1)}, bf16[2,256,1280]{2,1,0:T(8,128)(2,1)S(1)}, u32[]{:S(2)}, u32[]{:S(2)}) collective-permute-start(bf16[2,256,1280]{2,1,0:T(8,128)(2,1)S(1)} %shard_map.146.refs_0_), channel_id=1, source_target_pairs={{0,1},{1,0},{2,3},{3,2},{4,5},{5,4},{6,7},{7,6},{8,9},{9,8},{10,11... | collective-permute-start | bytes 3932168 | tf_op jit(solution)/shard_map/ppermute | solution.py:622
  76.1 3.0 %collective-permute-start.12 = (bf16[64,256]{1,0:T(8,128)(2,1)S(1)}, bf16[64,256]{1,0:T(8,128)(2,1)S(1)}, u32[]{:S(2)}, u32[]{:S(2)}) collective-permute-start(bf16[64,256]{1,0:T(8,128)(2,1)S(1)} %get-tuple-element.51.refs_0_), channel_id=1, source_target_pairs={{0,1},{1,0},{2,3},{3,2},{4,5},{5,4},{6,7},{7,6},{8,9},{9,8},{10,11... | collective-permute-start | bytes 98312 | tf_op jit(solution)/shard_map/ppermute | solution.py:622
  76.1 4.0 %collective-permute-start.13 = (bf16[64,256]{1,0:T(8,128)(2,1)S(1)}, bf16[64,256]{1,0:T(8,128)(2,1)S(1)}, u32[]{:S(2)}, u32[]{:S(2)}) collective-permute-start(bf16[64,256]{1,0:T(8,128)(2,1)S(1)} %get-tuple-element.51.refs_0_), channel_id=1, source_target_pairs={{0,2},{1,3},{2,0},{3,1},{4,6},{5,7},{6,4},{7,5},{8,10},{9,11},{10,... | collective-permute-start | bytes 98312 | tf_op jit(solution)/shard_map/ppermute | solution.py:622
  77.7 3.3 %collective-permute-start.14 = (bf16[64,256]{1,0:T(8,128)(2,1)S(1)}, bf16[64,256]{1,0:T(8,128)(2,1)S(1)}, u32[]{:S(2)}, u32[]{:S(2)}) collective-permute-start(bf16[64,256]{1,0:T(8,128)(2,1)S(1)} %get-tuple-element.51.refs_0_), channel_id=1, source_target_pairs={{0,3},{1,2},{2,1},{3,0},{4,7},{5,6},{6,5},{7,4},{8,11},{9,10},{10,... | collective-permute-start | bytes 98312 | tf_op jit(solution)/shard_map/ppermute | solution.py:622

commit v17 on v16

--- a/solution.py
+++ b/solution.py
@@ -60,6 +60,9 @@
         self.riding = self.local % 8 == 0 and self.share_rows % 16 == 0 and seq_count == 8
         self.riding = self.riding and 1 < data_count <= positions
         self.ride_rows = self.chunks * self.share_rows if self.riding else 0
+
+    def order(self):
+        return [2, 3, 4, 5, 0, 1, 6, 7] if self.count == 8 else list(range(self.count))
 
     def pieces(self):
         return list(range(1, self.count)) + [0]
@@ -366,7 +369,8 @@
         for rows in (slice(0, half), slice(half, part_rows))
     ]
     latent = jnp.concatenate(sides, axis=1).astype(BF16)
-    lat_ref[...] = latent.reshape(count, half, 2 * CH)
+    for spot, place in enumerate(sizes.order()):
+        lat_ref[spot] = latent[place * half : (place + 1) * half]
 
 
 def attend(sizes, masks, place, received, kept, scales, shifts, proj):
@@ -418,14 +422,15 @@
     return jnp.sum(x, axis=-1, keepdims=True) * (1.0 / count)
 
 
-def head_kernel(grid_rows, fused, embed_masks, out_factor, place_ref, lat_ref, *refs):
+def head_kernel(grid_rows, fused, order, embed_masks, out_factor, place_ref, lat_ref, *refs):
     embed_refs, refs = refs[: len(embed_masks)], refs[len(embed_masks) :]
     pos_ref, pre_ref, post_ref, prompt_ref, cot_ref, mod_ref, *refs = refs
     reward_ref, grad_ref, weight_ref, lat_scr, grad_scr, block_scr, back_scr = refs
     patch_rows = grid_rows // 4
     patch_cols = GW // 4
     patches = patch_rows * patch_cols
-    lat_scr[...] = lat_ref[...].astype(F32)
+    for spot, place in enumerate(order):
+        lat_scr[pl.ds(place * GW, GW), :] = lat_ref[pl.ds(spot * GW, GW), :].astype(F32)
 
     data = place_ref[1]
     shares = [
@@ -520,7 +525,7 @@
 
 
 def reward_head(
-    place, latent, embed, pos, pre, post, prompt, cot, modulated, grid_rows, fused, out_factor
+    place, order, latent, embed, pos, pre, post, prompt, cot, modulated, grid_rows, fused, out_factor
 ):
     patches = grid_rows * GW // 16
     rows = grid_rows * GW // 2
@@ -528,7 +533,7 @@
     embed_arrays, embed_masks = [x for x, _ in embed], [masks for _, masks in embed]
     share_rows = embed_arrays[0].shape[1]
     return pl.pallas_call(
-        functools.partial(head_kernel, grid_rows, fused, embed_masks, out_factor),
+        functools.partial(head_kernel, grid_rows, fused, order, embed_masks, out_factor),
         out_shape=(
             jax.ShapeDtypeStruct((1, 128), F32),
             jax.ShapeDtypeStruct((rows, 2 * CH), BF16),
@@ -601,15 +606,15 @@
     )(grad, modulated)
 
 
-def finish_kernel(in_ref, out_ref):
-    count, _, width = in_ref.shape
-    for group in range(count):
-        out_ref[:, pl.ds(group * width, width)] = in_ref[group].astype(F32)
-
-
-def finish(blocks):
-    return pl.pallas_call(
-        finish_kernel,
+def finish_kernel(order, in_ref, out_ref):
+    width = in_ref.shape[2]
+    for spot, group in enumerate(order):
+        out_ref[:, pl.ds(group * width, width)] = in_ref[spot].astype(F32)
+
+
+def finish(blocks, order):
+    return pl.pallas_call(
+        functools.partial(finish_kernel, order),
         out_shape=jax.ShapeDtypeStruct((CH, HEADS * HD), F32),
         in_specs=[VMEM_SPEC],
         out_specs=VMEM_SPEC,
@@ -713,8 +718,9 @@
         if shared:
             embed = embed + [(swap(mine[None], "dp", bits[0]), [bits[0]])]
 
-    groups = None
+    groups, order = [sizes.order()], sizes.order()
     if query_parts > 1:
+        order = list(range(group_count))
         groups = [[g * query_parts + r for g in range(group_count)] for r in range(query_parts)]
     per_share = seq_count // group_count
     parts = all_to_all(latent_part.reshape(group_count, per_share * half, 2 * CH), groups)
@@ -723,7 +729,7 @@
         embed = [(arrange(sizes, ride_masks, place, pairs, summed), [0, bits[0]])]
     for bit in bits[1:] if shared else []:
         embed = embed + [(swap(x, "dp", bit), [m ^ bit for m in some]) for x, some in embed]
-    latent = all_to_all(summed)
+    latent = all_to_all(summed, [sizes.order()])
     if canonical:
         latent = latent.reshape(lat_rows // 2, 2 * CH)
     else:
@@ -732,7 +738,8 @@
         latent = latent.transpose(0, 2, 1, 3).reshape(lat_rows // 2, 2 * CH)
 
     reward, grad, weight = reward_head(
-        place, latent, embed, pos, pre, post, words,
+        place, sizes.order() if canonical else list(range(grid_rows // 2)),
+        latent, embed, pos, pre, post, words,
         cot, modulated, grid_rows, canonical, out_factor,
     )
     if not canonical:
@@ -748,7 +755,7 @@
         total = total_copies(parts, 1)[0]
         parts = [total] + [swap(total, "seq", mask) for mask in range(1, query_parts)]
     blocks = all_to_all(total_copies(parts, group_count, [token]), groups)
-    return (reward[0, :1], attn_grad, finish(blocks).T)
+    return (reward[0, :1], attn_grad, finish(blocks, order).T)
 
 
 def solution(mesh):

time: 94.1 us -> 92.3 us (0.981)
  blocking collectives: 36 us -> 34.2 us
    all_to_all x3, blocking collectives: 36 us -> 34.2 us  [all_to_all(): lax.all_to_all(x, 'seq', split_axis=0, concat_axis=0, tiled=True, axis_in...]
where the time goes in v17:
time: 92.3 us; the launch traced here: 92 us
  blocking collectives  34.2 us (37%)
  waiting for transfers between devices  21.3 us (23%)
  starting transfers between devices  19.7 us (21%)
  Pallas kernels  15.4 us (17%)
  between operations  1.41 us (2%)
    all_to_all x3, blocking collectives, all_to_all(): lax.all_to_all(x, 'seq', split_axis=0, concat_axis=0, tiled=True, axis_in...  34.2 us
    ppermute x14, waiting for transfers between devices, swap(): return lax.ppermute(x, axis, [(i, i ^ mask) for i in range(count)])  21.3 us
    ppermute x14, starting transfers between devices, swap(): return lax.ppermute(x, axis, [(i, i ^ mask) for i in range(count)])  18.2 us
    pallas_call x1, Pallas kernels, attend(): pl.pallas_call(functools.partial(attend_kernel, sizes, masks, early), out...  3.83 us
    pallas_call x1, Pallas kernels, reward_head(): pl.pallas_call(functools.partial(head_kernel, grid_rows, fused, order, em...  3.33 us
    pallas_call x1, Pallas kernels, pack(): pl.pallas_call(functools.partial(pack_kernel, sizes), out_shape=[jax.Shap...  1.93 us
  transfers between devices with their start and end apart: 15, of which 7 were waited for; matrix products, arithmetic and copies ran while one was open for 0% of the time, Pallas kernels for 9%

profile of v17, /device:TPU:0, one launch (start us, length us, event | category | flops | bytes accessed | tf_op | source)
XLA Modules:
  0.0 92.0 jit_solution(16976169902535919899)
XLA Ops:
  0.6 1.9 %shard_map.139 = (bf16[384,256]{1,0:T(8,128)(2,1)S(1)}, bf16[384,256]{1,0:T(8,128)(2,1)S(1)}, bf16[384,256]{1,0:T(8,128)(2,1)S(1)}, bf16[544,256]{1,0:T(8,128)(2...) custom-call(bf16[1,128,2048]{2,1,0:T(8,128)(2,1)} %q_ref.1, ...), custom_call_target="tpu_custom_call" | custom-call | bytes 3145728 | tf_op jit(solution)/shard_map/pallas_call | solution.py:139
  2.6 4.1 %collective-permute-start.3 = (bf16[544,256]{1,0:T(8,128)(2,1)S(1)}, bf16[544,256]{1,0:T(8,128)(2,1)S(1)}, u32[]{:S(2)}, u32[]{:S(2)}) collective-permute-start(bf16[544,256]{1,0:T(8,128)(2,1)S(1)} %get-tuple-element.31), channel_id=1, source_target_pairs={{0,16},{4,20},{8,24},{12,28},{16,0},{20,4},{24,8},{28,12},{1,17},{... | collective-permute-start | bytes 835592 | tf_op jit(solution)/shard_map/ppermute | solution.py:627
  6.7 1.5 %collective-permute-start = (bf16[384,256]{1,0:T(8,128)(2,1)S(1)}, bf16[384,256]{1,0:T(8,128)(2,1)S(1)}, u32[]{:S(2)}, u32[]{:S(2)}) collective-permute-start(bf16[384,256]{1,0:T(8,128)(2,1)S(1)} %get-tuple-element.28), channel_id=1, source_target_pairs={{0,4},{4,0},{8,12},{12,8},{16,20},{20,16},{24,28},{28,24},{1,5},{5... | collective-permute-start | bytes 589832 | tf_op jit(solution)/shard_map/ppermute | solution.py:627
  8.2 1.6 %collective-permute-start.1 = (bf16[384,256]{1,0:T(8,128)(2,1)S(1)}, bf16[384,256]{1,0:T(8,128)(2,1)S(1)}, u32[]{:S(2)}, u32[]{:S(2)}) collective-permute-start(bf16[384,256]{1,0:T(8,128)(2,1)S(1)} %get-tuple-element.29), channel_id=1, source_target_pairs={{0,8},{4,12},{8,0},{12,4},{16,24},{20,28},{24,16},{28,20},{1,9},{5... | collective-permute-start | bytes 589832 | tf_op jit(solution)/shard_map/ppermute | solution.py:627
  10.2 1.3 %collective-permute-start.4 = (bf16[384,256]{1,0:T(8,128)(2,1)S(1)}, bf16[384,256]{1,0:T(8,128)(2,1)S(1)}, u32[]{:S(2)}, u32[]{:S(2)}) collective-permute-start(bf16[384,256]{1,0:T(8,128)(2,1)S(1)} %get-tuple-element.32), channel_id=1, source_target_pairs={{0,20},{4,16},{8,28},{12,24},{16,4},{20,0},{24,12},{28,8},{1,21},{... | collective-permute-start | bytes 589832 | tf_op jit(solution)/shard_map/ppermute | solution.py:627
  11.5 2.2 %collective-permute-done.refs_0_ = bf16[384,256]{1,0:T(8,128)(2,1)S(1)} collective-permute-done((bf16[384,256]{1,0:T(8,128)(2,1)S(1)}, bf16[384,256]{1,0:T(8,128)(2,1)S(1)}, u32[]{:S(2)}, u32[]{:S(2)}) %collective-permute-start) | collective-permute-done | bytes 196640 | tf_op jit(solution)/shard_map/ppermute | solution.py:627
  13.6 1.4 %collective-permute-start.5 = (bf16[384,256]{1,0:T(8,128)(2,1)S(1)}, bf16[384,256]{1,0:T(8,128)(2,1)S(1)}, u32[]{:S(2)}, u32[]{:S(2)}) collective-permute-start(bf16[384,256]{1,0:T(8,128)(2,1)S(1)} %get-tuple-element.34), channel_id=1, source_target_pairs={{0,24},{4,28},{8,16},{12,20},{16,8},{20,12},{24,0},{28,4},{1,25},{... | collective-permute-start | bytes 589832 | tf_op jit(solution)/shard_map/ppermute | solution.py:627
  15.1 5.2 %collective-permute-done.3.refs_3_.refs_0_ = bf16[544,256]{1,0:T(8,128)(2,1)S(1)} collective-permute-done((bf16[544,256]{1,0:T(8,128)(2,1)S(1)}, bf16[544,256]{1,0:T(8,128)(2,1)S(1)}, u32[]{:S(2)}, u32[]{:S(2)}) %collective-permute-start.3) | collective-permute-done | bytes 278560 | tf_op jit(solution)/shard_map/ppermute | solution.py:627
  20.2 3.8 %collective-permute-start.6 = (bf16[384,256]{1,0:T(8,128)(2,1)S(1)}, bf16[384,256]{1,0:T(8,128)(2,1)S(1)}, u32[]{:S(2)}, u32[]{:S(2)}) collective-permute-start(bf16[384,256]{1,0:T(8,128)(2,1)S(1)} %get-tuple-element.35), channel_id=1, source_target_pairs={{0,28},{4,24},{8,20},{12,16},{16,12},{20,8},{24,4},{28,0},{1,29},{... | collective-permute-start | bytes 589832 | tf_op jit(solution)/shard_map/ppermute | solution.py:627
  25.1 1.6 %shard_map.140 = (f32[1,256]{1,0:T(1,128)S(1)}, f32[1,256]{1,0:T(1,128)S(1)}, bf16[64,256]{1,0:T(8,128)(2,1)S(1)}, bf16[64,1280]{1,0:T(8,128)(2,1)S(1)}, f32[128...) custom-call(s32[3]{0:T(128)S(1)} %pad_add_fusion.place_ref, f32[1]{0:T(128)S(6)} %copy.15.cot_ref, ...), custom_call_target="tpu_custom_call" | custom-call | flops 1 | bytes 1 | tf_op jit(solution)/shard_map/pallas_call | solution.py:252
  26.9 11.5 %collective-permute-done.4.refs_4_ = bf16[384,256]{1,0:T(8,128)(2,1)S(1)} collective-permute-done((bf16[384,256]{1,0:T(8,128)(2,1)S(1)}, bf16[384,256]{1,0:T(8,128)(2,1)S(1)}, u32[]{:S(2)}, u32[]{:S(2)}) %collective-permute-start.4) | collective-permute-done | bytes 196640 | tf_op jit(solution)/shard_map/ppermute | solution.py:627
  38.4 1.8 %shard_map.141 = (f32[6,2,128,128]{3,2,1,0:T(8,128)S(1)}, f32[6,2,128,128]{3,2,1,0:T(8,128)S(1)}) custom-call(bf16[384,256]{1,0:T(8,128)(2,1)S(1)} %collective-permute-done.refs_0_, bf16[384,256]{1,0:T(8,128)(2,1)S(1)} %collective-permute-done.1.refs_1_, bf16[384,256]{1,0:T(8,128)(2,1)S(1)} %collective-permute-done.2.refs_2_, ...), custom_call_target="tpu_custom_call" | custom-call | flops 1 | bytes 1 | tf_op jit(solution)/shard_map/pallas_call | solution.py:325
  40.5 1.8 %collective-permute-start.9 = (bf16[4,320,128]{2,1,0:T(8,128)(2,1)S(1)}, bf16[4,320,128]{2,1,0:T(8,128)(2,1)S(1)}, u32[]{:S(2)}, u32[]{:S(2)}) collective-permute-start(bf16[4,320,128]{2,1,0:T(8,128)(2,1)S(1)} %shard_map.145.refs_0_), channel_id=1, source_target_pairs={{0,2},{1,3},{2,0},{3,1},{4,6},{5,7},{6,4},{7,5},{8,10},{9,11},{10,... | collective-permute-start | bytes 983048 | tf_op jit(solution)/shard_map/ppermute | solution.py:627
  42.3 1.5 %collective-permute-start.10 = (bf16[4,320,128]{2,1,0:T(8,128)(2,1)S(1)}, bf16[4,320,128]{2,1,0:T(8,128)(2,1)S(1)}, u32[]{:S(2)}, u32[]{:S(2)}) collective-permute-start(bf16[4,320,128]{2,1,0:T(8,128)(2,1)S(1)} %shard_map.145.refs_0_), channel_id=1, source_target_pairs={{0,6},{1,7},{2,4},{3,5},{4,2},{5,3},{6,0},{7,1},{8,14},{9,15},{10,... | collective-permute-start | bytes 983048 | tf_op jit(solution)/shard_map/ppermute | solution.py:643
  43.8 3.8 %shard_map.142 = (bf16[8,128,256]{2,1,0:T(8,128)(2,1)S(1)}, bf16[8,64,128]{2,1,0:T(8,128)(2,1)S(1)}) custom-call(s32[3]{0:T(128)S(1)} %pad_add_fusion.place_ref, bf16[384,256]{1,0:T(8,128)(2,1)S(1)} %collective-permute-done.refs_0_, bf16[384,256]{1,0:T(8,128)(2,1)S(1)} %collective-permute-done.1.refs_1_, ...), custom_call_target="tpu_custom_call" | custom-call | flops 1073741824 | bytes 2097152 | tf_op jit(solution)/shard_map/pallas_call | solution.py:381
  47.7 12.7 %all_to_all.15.refs_0_ = bf16[8,64,128]{2,1,0:T(8,128)(2,1)S(1)} all-to-all(bf16[8,64,128]{2,1,0:T(8,128)(2,1)S(1)} %get-tuple-element.41), channel_id=1, replica_groups={{8,12,16,20,0,4,24,28},{9,13,17,21,1,5,25,29},{10,14,18,22,2,6,26,30},{..., dimensions={0} | all-to-all | bytes 262144 | tf_op jit(solution)/shard_map/all_to_all | solution.py:631
  60.4 0.8 shard_map.146.refs_0_
  61.3 9.4 %all_to_all.16 = bf16[8,64,128]{2,1,0:T(8,128)(2,1)S(1)} all-to-all(bf16[8,64,128]{2,1,0:T(8,128)(2,1)S(1)} %shard_map.143.refs_4_), channel_id=1, replica_groups={{8,12,16,20,0,4,24,28},{9,13,17,21,1,5,25,29},{10,14,18,22,2,6,26,30},{..., dimensions={0} | all-to-all | bytes 262144 | tf_op jit(solution)/shard_map/all_to_all | solution.py:631
  70.7 3.3 %shard_map.147 = (f32[1,128]{1,0:T(1,128)}, bf16[512,128]{1,0:T(8,128)(2,1)S(1)}, bf16[64,256]{1,0:T(8,128)(2,1)S(1)}) custom-call(s32[3]{0:T(128)S(1)} %pad_add_fusion.place_ref, bf16[512,128]{1,0:T(8,128)(2,1)S(1)} %bitcast.7, bf16[2,256,1280]{2,1,0:T(8,128)(2,1)S(1)} %shard_map.146.refs_0_, bf16[2,256,1280]{2,1,0:T(8,128)(2,1)S(1)} %collective-permute-done.11.refs_1_, ...), custom_call_target="tpu_custom_call" | custom-call | flops 503316480 | bytes 2785280 | tf_op jit(solution)/shard_map/pallas_call | solution.py:535
  74.2 1.6 %collective-permute-start.13 = (bf16[64,256]{1,0:T(8,128)(2,1)S(1)}, bf16[64,256]{1,0:T(8,128)(2,1)S(1)}, u32[]{:S(2)}, u32[]{:S(2)}) collective-permute-start(bf16[64,256]{1,0:T(8,128)(2,1)S(1)} %get-tuple-element.51.refs_0_), channel_id=1, source_target_pairs={{0,2},{1,3},{2,0},{3,1},{4,6},{5,7},{6,4},{7,5},{8,10},{9,11},{10,... | collective-permute-start | bytes 98312 | tf_op jit(solution)/shard_map/ppermute | solution.py:627
  76.0 1.1 %shard_map.148 = (bf16[1,2,1024,128]{3,2,1,0:T(8,128)(2,1)}, f32[8,128]{1,0:T(8,128)S(1)}) custom-call(bf16[512,128]{1,0:T(8,128)(2,1)S(1)} %get-tuple-element.49.grad_ref, f32[1,256]{1,0:T(1,128)S(1)} %get-tuple-element.36.refs_6_.refs_10_.scale_ref, bf16[64,256]{1,0:T(8,128)(2,1)S(1)} %get-tuple-element.40.refs_12_.proj_ref), custom_call_target="tpu_custom_call" | custom-call | flops 67108864 | bytes 524288 | tf_op jit(solution)/shard_map/pallas_call | solution.py:578
  77.1 1.0 %collective-permute-done.13.refs_2_ = bf16[64,256]{1,0:T(8,128)(2,1)S(1)} collective-permute-done((bf16[64,256]{1,0:T(8,128)(2,1)S(1)}, bf16[64,256]{1,0:T(8,128)(2,1)S(1)}, u32[]{:S(2)}, u32[]{:S(2)}) %collective-permute-start.13) | collective-permute-done | bytes 32800 | tf_op jit(solution)/shard_map/ppermute | solution.py:627
  78.1 0.9 %collective-permute-done.14.refs_3_ = bf16[64,256]{1,0:T(8,128)(2,1)S(1)} collective-permute-done((bf16[64,256]{1,0:T(8,128)(2,1)S(1)}, bf16[64,256]{1,0:T(8,128)(2,1)S(1)}, u32[]{:S(2)}, u32[]{:S(2)}) %collective-permute-start.14) | collective-permute-done | bytes 32800 | tf_op jit(solution)/shard_map/ppermute | solution.py:627
  79.1 12.1 %all_to_all.17.in_ref = bf16[8,64,256]{2,1,0:T(8,128)(2,1)S(1)} all-to-all(bf16[8,64,256]{2,1,0:T(8,128)(2,1)S(1)} %shard_map.149), channel_id=1, replica_groups={{8,12,16,20,0,4,24,28},{9,13,17,21,1,5,25,29},{10,14,18,22,2,6,26,30},{..., dimensions={0} | all-to-all | bytes 524288 | tf_op jit(solution)/shard_map/all_to_all | solution.py:631
  (22 shorter events, 2.6 us)
Async XLA Ops:
  2.6 17.7 %collective-permute-start.3 = (bf16[544,256]{1,0:T(8,128)(2,1)S(1)}, bf16[544,256]{1,0:T(8,128)(2,1)S(1)}, u32[]{:S(2)}, u32[]{:S(2)}) collective-permute-start(bf16[544,256]{1,0:T(8,128)(2,1)S(1)} %get-tuple-element.31), channel_id=1, source_target_pairs={{0,16},{4,20},{8,24},{12,28},{16,0},{20,4},{24,8},{28,12},{1,17},{... | collective-permute-start | bytes 835592 | tf_op jit(solution)/shard_map/ppermute | solution.py:627
  6.7 6.9 %collective-permute-start = (bf16[384,256]{1,0:T(8,128)(2,1)S(1)}, bf16[384,256]{1,0:T(8,128)(2,1)S(1)}, u32[]{:S(2)}, u32[]{:S(2)}) collective-permute-start(bf16[384,256]{1,0:T(8,128)(2,1)S(1)} %get-tuple-element.28), channel_id=1, source_target_pairs={{0,4},{4,0},{8,12},{12,8},{16,20},{20,16},{24,28},{28,24},{1,5},{5... | collective-permute-start | bytes 589832 | tf_op jit(solution)/shard_map/ppermute | solution.py:627
  8.2 16.1 %collective-permute-start.1 = (bf16[384,256]{1,0:T(8,128)(2,1)S(1)}, bf16[384,256]{1,0:T(8,128)(2,1)S(1)}, u32[]{:S(2)}, u32[]{:S(2)}) collective-permute-start(bf16[384,256]{1,0:T(8,128)(2,1)S(1)} %get-tuple-element.29), channel_id=1, source_target_pairs={{0,8},{4,12},{8,0},{12,4},{16,24},{20,28},{24,16},{28,20},{1,9},{5... | collective-permute-start | bytes 589832 | tf_op jit(solution)/shard_map/ppermute | solution.py:627
  9.8 17.1 %collective-permute-start.2 = (bf16[384,256]{1,0:T(8,128)(2,1)S(1)}, bf16[384,256]{1,0:T(8,128)(2,1)S(1)}, u32[]{:S(2)}, u32[]{:S(2)}) collective-permute-start(bf16[384,256]{1,0:T(8,128)(2,1)S(1)} %get-tuple-element.30), channel_id=1, source_target_pairs={{0,12},{4,8},{8,4},{12,0},{16,28},{20,24},{24,20},{28,16},{1,13},{... | collective-permute-start | bytes 589832 | tf_op jit(solution)/shard_map/ppermute | solution.py:627
  10.2 28.2 %collective-permute-start.4 = (bf16[384,256]{1,0:T(8,128)(2,1)S(1)}, bf16[384,256]{1,0:T(8,128)(2,1)S(1)}, u32[]{:S(2)}, u32[]{:S(2)}) collective-permute-start(bf16[384,256]{1,0:T(8,128)(2,1)S(1)} %get-tuple-element.32), channel_id=1, source_target_pairs={{0,20},{4,16},{8,28},{12,24},{16,4},{20,0},{24,12},{28,8},{1,21},{... | collective-permute-start | bytes 589832 | tf_op jit(solution)/shard_map/ppermute | solution.py:627
  13.6 30.2 %collective-permute-start.5 = (bf16[384,256]{1,0:T(8,128)(2,1)S(1)}, bf16[384,256]{1,0:T(8,128)(2,1)S(1)}, u32[]{:S(2)}, u32[]{:S(2)}) collective-permute-start(bf16[384,256]{1,0:T(8,128)(2,1)S(1)} %get-tuple-element.34), channel_id=1, source_target_pairs={{0,24},{4,28},{8,16},{12,20},{16,8},{20,12},{24,0},{28,4},{1,25},{... | collective-permute-start | bytes 589832 | tf_op jit(solution)/shard_map/ppermute | solution.py:627
  20.2 23.6 %collective-permute-start.6 = (bf16[384,256]{1,0:T(8,128)(2,1)S(1)}, bf16[384,256]{1,0:T(8,128)(2,1)S(1)}, u32[]{:S(2)}, u32[]{:S(2)}) collective-permute-start(bf16[384,256]{1,0:T(8,128)(2,1)S(1)} %get-tuple-element.35), channel_id=1, source_target_pairs={{0,28},{4,24},{8,20},{12,16},{16,12},{20,8},{24,4},{28,0},{1,29},{... | collective-permute-start | bytes 589832 | tf_op jit(solution)/shard_map/ppermute | solution.py:627
  24.3 15.9 %collective-permute-start.7 = (bf16[2,320,128]{2,1,0:T(8,128)(2,1)S(1)}, bf16[2,320,128]{2,1,0:T(8,128)(2,1)S(1)}, u32[]{:S(2)}, u32[]{:S(2)}) collective-permute-start(bf16[2,320,128]{2,1,0:T(8,128)(2,1)S(1)} %shard_map.144.first_ref), channel_id=1, source_target_pairs={{0,8},{4,12},{8,0},{12,4},{16,24},{20,28},{24,16},{28,20},{1,9},{5... | collective-permute-start | bytes 491528 | tf_op jit(solution)/shard_map/ppermute | solution.py:627
  40.3 20.1 %collective-permute-start.8 = (bf16[4,320,128]{2,1,0:T(8,128)(2,1)S(1)}, bf16[4,320,128]{2,1,0:T(8,128)(2,1)S(1)}, u32[]{:S(2)}, u32[]{:S(2)}) collective-permute-start(bf16[4,320,128]{2,1,0:T(8,128)(2,1)S(1)} %shard_map.145.refs_0_), channel_id=1, source_target_pairs={{0,4},{4,0},{8,12},{12,8},{16,20},{20,16},{24,28},{28,24},{1,5},{5... | collective-permute-start | bytes 983048 | tf_op jit(solution)/shard_map/ppermute | solution.py:627
  40.5 19.9 %collective-permute-start.9 = (bf16[4,320,128]{2,1,0:T(8,128)(2,1)S(1)}, bf16[4,320,128]{2,1,0:T(8,128)(2,1)S(1)}, u32[]{:S(2)}, u32[]{:S(2)}) collective-permute-start(bf16[4,320,128]{2,1,0:T(8,128)(2,1)S(1)} %shard_map.145.refs_0_), channel_id=1, source_target_pairs={{0,2},{1,3},{2,0},{3,1},{4,6},{5,7},{6,4},{7,5},{8,10},{9,11},{10,... | collective-permute-start | bytes 983048 | tf_op jit(solution)/shard_map/ppermute | solution.py:627
  42.3 18.1 %collective-permute-start.10 = (bf16[4,320,128]{2,1,0:T(8,128)(2,1)S(1)}, bf16[4,320,128]{2,1,0:T(8,128)(2,1)S(1)}, u32[]{:S(2)}, u32[]{:S(2)}) collective-permute-start(bf16[4,320,128]{2,1,0:T(8,128)(2,1)S(1)} %shard_map.145.refs_0_), channel_id=1, source_target_pairs={{0,6},{1,7},{2,4},{3,5},{4,2},{5,3},{6,0},{7,1},{8,14},{9,15},{10,... | collective-permute-start | bytes 983048 | tf_op jit(solution)/shard_map/ppermute | solution.py:643
  61.3 9.5 %collective-permute-start.11 = (bf16[2,256,1280]{2,1,0:T(8,128)(2,1)S(1)}, bf16[2,256,1280]{2,1,0:T(8,128)(2,1)S(1)}, u32[]{:S(2)}, u32[]{:S(2)}) collective-permute-start(bf16[2,256,1280]{2,1,0:T(8,128)(2,1)S(1)} %shard_map.146.refs_0_), channel_id=1, source_target_pairs={{0,1},{1,0},{2,3},{3,2},{4,5},{5,4},{6,7},{7,6},{8,9},{9,8},{10,11... | collective-permute-start | bytes 3932168 | tf_op jit(solution)/shard_map/ppermute | solution.py:627
  74.1 3.0 %collective-permute-start.12 = (bf16[64,256]{1,0:T(8,128)(2,1)S(1)}, bf16[64,256]{1,0:T(8,128)(2,1)S(1)}, u32[]{:S(2)}, u32[]{:S(2)}) collective-permute-start(bf16[64,256]{1,0:T(8,128)(2,1)S(1)} %get-tuple-element.51.refs_0_), channel_id=1, source_target_pairs={{0,1},{1,0},{2,3},{3,2},{4,5},{5,4},{6,7},{7,6},{8,9},{9,8},{10,11... | collective-permute-start | bytes 98312 | tf_op jit(solution)/shard_map/ppermute | solution.py:627
  74.2 4.0 %collective-permute-start.13 = (bf16[64,256]{1,0:T(8,128)(2,1)S(1)}, bf16[64,256]{1,0:T(8,128)(2,1)S(1)}, u32[]{:S(2)}, u32[]{:S(2)}) collective-permute-start(bf16[64,256]{1,0:T(8,128)(2,1)S(1)} %get-tuple-element.51.refs_0_), channel_id=1, source_target_pairs={{0,2},{1,3},{2,0},{3,1},{4,6},{5,7},{6,4},{7,5},{8,10},{9,11},{10,... | collective-permute-start | bytes 98312 | tf_op jit(solution)/shard_map/ppermute | solution.py:627
  75.7 3.3 %collective-permute-start.14 = (bf16[64,256]{1,0:T(8,128)(2,1)S(1)}, bf16[64,256]{1,0:T(8,128)(2,1)S(1)}, u32[]{:S(2)}, u32[]{:S(2)}) collective-permute-start(bf16[64,256]{1,0:T(8,128)(2,1)S(1)} %get-tuple-element.51.refs_0_), channel_id=1, source_target_pairs={{0,3},{1,2},{2,1},{3,0},{4,7},{5,6},{6,5},{7,4},{8,11},{9,10},{10,... | collective-permute-start | bytes 98312 | tf_op jit(solution)/shard_map/ppermute | solution.py:627

commit v18 on v17

--- a/solution.py
+++ b/solution.py
@@ -62,7 +62,7 @@
         self.ride_rows = self.chunks * self.share_rows if self.riding else 0
 
     def order(self):
-        return [2, 3, 4, 5, 0, 1, 6, 7] if self.count == 8 else list(range(self.count))
+        return [4, 5, 2, 3, 6, 7, 0, 1] if self.count == 8 else list(range(self.count))
 
     def pieces(self):
         return list(range(1, self.count)) + [0]
@@ -82,73 +82,58 @@
 
 
 def pack_kernel(sizes, q_ref, k_ref, v_ref, embed_ref, *refs):
-    pieces = sizes.pieces()
-    out_refs = refs[: len(pieces)]
-    q_scr, k_scr, v_scr, embed_scr, share_scr, in_sems, out_sems = refs[len(pieces) :]
+    masks = sizes.pieces()
+    out_refs = refs[: len(masks)]
+    embed_scr, share_scr, embed_sem, sems = refs[len(masks) :]
     me = lax.axis_index("seq")
     tok_rows, part_rows, width = sizes.tok_rows, sizes.part_rows, sizes.width
     share = pl.ds(lax.axis_index("dp") * sizes.share, sizes.share)
-    loads = [
-        pltpu.make_async_copy(embed_ref.at[share], embed_scr, in_sems.at[3]),
-        pltpu.make_async_copy(q_ref.at[0], q_scr, in_sems.at[0]),
-        pltpu.make_async_copy(k_ref.at[0], k_scr, in_sems.at[1]),
-        pltpu.make_async_copy(v_ref.at[0], v_scr, in_sems.at[2]),
-    ]
-    for load in loads:
-        load.start()
-    sent = [[], [], [], []]
-    for slot, (mask, out) in enumerate(zip(pieces, out_refs)):
+    load = pltpu.make_async_copy(embed_ref.at[share], embed_scr, embed_sem.at[0])
+    load.start()
+    copies = []
+    for slot, (mask, out) in enumerate(zip(masks, out_refs)):
         dest = jnp.bitwise_xor(me, mask)
         group, part = dest // sizes.query_parts, dest % sizes.query_parts
         cols = pl.ds(pl.multiple_of(group * width, HD), width)
         first = pl.ds(pl.multiple_of(part * part_rows, part_rows), part_rows)
         for kind, source, rows in (
-            (0, q_scr.at[first, cols], pl.ds(0, part_rows)),
-            (1, k_scr.at[:, cols], pl.ds(part_rows, tok_rows)),
-            (2, v_scr.at[:, cols], pl.ds(part_rows + tok_rows, tok_rows)),
+            (0, q_ref.at[0, first, cols], pl.ds(0, part_rows)),
+            (1, k_ref.at[0, :, cols], pl.ds(part_rows, tok_rows)),
+            (2, v_ref.at[0, :, cols], pl.ds(part_rows + tok_rows, tok_rows)),
         ):
-            sent[kind].append(pltpu.make_async_copy(source, out.at[rows], out_sems.at[kind, slot]))
-        if sizes.rides(mask):
-            for at, (rows, place, from_rows) in enumerate(sizes.ride_slices()):
-                sent[3].append(
-                    pltpu.make_async_copy(
-                        share_scr.at[from_rows], out.at[rows, place], out_sems.at[3 + at, slot]
-                    )
-                )
-    loads[0].wait()
+            copies.append(pltpu.make_async_copy(source, out.at[rows], sems.at[kind, slot]))
+    for copy in copies:
+        copy.start()
+    load.wait()
     if sizes.riding:
         for chunk in range(sizes.chunks):
             cols = embed_scr[:, :, pl.ds(chunk * HD, HD)].astype(F32)
             share_scr[pl.ds(chunk * sizes.share_rows, sizes.share_rows), :] = cols.reshape(
                 sizes.share_rows, HD
             ).astype(BF16)
-    for store in sent[3]:
-        store.start()
-    for kind in range(3):
-        loads[kind + 1].wait()
-        for store in sent[kind]:
-            store.start()
-    for stores in sent:
-        for store in stores:
-            store.wait()
+        for mask, out in zip(masks, out_refs):
+            if sizes.rides(mask):
+                for rows, place, from_rows in sizes.ride_slices():
+                    out[rows, place] = share_scr[from_rows, :]
+    for copy in copies:
+        copy.wait()
 
 
 def pack(sizes, queries, keys, values, patch_embed):
     tok_rows, full = queries.shape[1:]
-    pieces = sizes.pieces()
+    masks = sizes.pieces()
     return pl.pallas_call(
         functools.partial(pack_kernel, sizes),
-        out_shape=[jax.ShapeDtypeStruct(sizes.piece_shape(mask), BF16) for mask in pieces],
+        out_shape=[jax.ShapeDtypeStruct(sizes.piece_shape(mask), BF16) for mask in masks],
         in_specs=[HBM_SPEC] * 4,
-        out_specs=[HBM_SPEC] * len(pieces),
-        scratch_shapes=[pltpu.VMEM((tok_rows, full), BF16)] * 3
-        + [
+        out_specs=[VMEM_SPEC] * len(masks),
+        scratch_shapes=[
             pltpu.VMEM((sizes.share,) + patch_embed.shape[1:], BF16),
             pltpu.VMEM((max(16, sizes.ride_rows), HD), BF16),
-            pltpu.SemaphoreType.DMA((4,)),
-            pltpu.SemaphoreType.DMA((3 + sizes.heads, len(pieces))),
+            pltpu.SemaphoreType.DMA((1,)),
+            pltpu.SemaphoreType.DMA((3, len(masks))),
         ],
-        compiler_params=limits(),
+        compiler_params=limits(8),
         cost_estimate=pl.CostEstimate(
             flops=0, bytes_accessed=12 * tok_rows * full, transcendentals=0
         ),

time: 92.3 us -> 91.7 us (level)
  no operation moved by 1% of the time
where the time goes in v18:
time: 91.7 us; the launch traced here: 91.4 us
  blocking collectives  33.7 us (37%)
  waiting for transfers between devices  21.3 us (23%)
  starting transfers between devices  19.7 us (21%)
  Pallas kernels  15.3 us (17%)
  between operations  1.41 us (2%)
    all_to_all x3, blocking collectives, all_to_all(): lax.all_to_all(x, 'seq', split_axis=0, concat_axis=0, tiled=True, axis_in...  33.7 us
    ppermute x14, waiting for transfers between devices, swap(): return lax.ppermute(x, axis, [(i, i ^ mask) for i in range(count)])  21.3 us
    ppermute x14, starting transfers between devices, swap(): return lax.ppermute(x, axis, [(i, i ^ mask) for i in range(count)])  18.2 us
    pallas_call x1, Pallas kernels, attend(): pl.pallas_call(functools.partial(attend_kernel, sizes, masks, early), out...  3.83 us
    pallas_call x1, Pallas kernels, reward_head(): pl.pallas_call(functools.partial(head_kernel, grid_rows, fused, order, em...  3.33 us
    pallas_call x1, Pallas kernels, attend_early(): pl.pallas_call(functools.partial(early_kernel, sizes, count), out_shape=(...  1.84 us
  transfers between devices with their start and end apart: 15, of which 7 were waited for; matrix products, arithmetic and copies ran while one was open for 0% of the time, Pallas kernels for 9%

profile of v18, /device:TPU:0, one launch (start us, length us, event | category | flops | bytes accessed | tf_op | source)
XLA Modules:
  0.0 91.4 jit_solution(10645765498724593749)
XLA Ops:
  0.6 1.8 %shard_map.139 = (bf16[384,256]{1,0:T(8,128)(2,1)S(1)}, bf16[384,256]{1,0:T(8,128)(2,1)S(1)}, bf16[384,256]{1,0:T(8,128)(2,1)S(1)}, bf16[544,256]{1,0:T(8,128)(2...) custom-call(bf16[1,128,2048]{2,1,0:T(8,128)(2,1)} %q_ref.1, ...), custom_call_target="tpu_custom_call" | custom-call | bytes 3145728 | tf_op jit(solution)/shard_map/pallas_call | solution.py:125
  2.4 4.1 %collective-permute-start.3 = (bf16[544,256]{1,0:T(8,128)(2,1)S(1)}, bf16[544,256]{1,0:T(8,128)(2,1)S(1)}, u32[]{:S(2)}, u32[]{:S(2)}) collective-permute-start(bf16[544,256]{1,0:T(8,128)(2,1)S(1)} %get-tuple-element.31), channel_id=1, source_target_pairs={{0,16},{4,20},{8,24},{12,28},{16,0},{20,4},{24,8},{28,12},{1,17},{... | collective-permute-start | bytes 835592 | tf_op jit(solution)/shard_map/ppermute | solution.py:612
  6.5 1.5 %collective-permute-start = (bf16[384,256]{1,0:T(8,128)(2,1)S(1)}, bf16[384,256]{1,0:T(8,128)(2,1)S(1)}, u32[]{:S(2)}, u32[]{:S(2)}) collective-permute-start(bf16[384,256]{1,0:T(8,128)(2,1)S(1)} %get-tuple-element.28), channel_id=1, source_target_pairs={{0,4},{4,0},{8,12},{12,8},{16,20},{20,16},{24,28},{28,24},{1,5},{5... | collective-permute-start | bytes 589832 | tf_op jit(solution)/shard_map/ppermute | solution.py:612
  8.0 1.6 %collective-permute-start.1 = (bf16[384,256]{1,0:T(8,128)(2,1)S(1)}, bf16[384,256]{1,0:T(8,128)(2,1)S(1)}, u32[]{:S(2)}, u32[]{:S(2)}) collective-permute-start(bf16[384,256]{1,0:T(8,128)(2,1)S(1)} %get-tuple-element.29), channel_id=1, source_target_pairs={{0,8},{4,12},{8,0},{12,4},{16,24},{20,28},{24,16},{28,20},{1,9},{5... | collective-permute-start | bytes 589832 | tf_op jit(solution)/shard_map/ppermute | solution.py:612
  10.0 1.3 %collective-permute-start.4 = (bf16[384,256]{1,0:T(8,128)(2,1)S(1)}, bf16[384,256]{1,0:T(8,128)(2,1)S(1)}, u32[]{:S(2)}, u32[]{:S(2)}) collective-permute-start(bf16[384,256]{1,0:T(8,128)(2,1)S(1)} %get-tuple-element.32), channel_id=1, source_target_pairs={{0,20},{4,16},{8,28},{12,24},{16,4},{20,0},{24,12},{28,8},{1,21},{... | collective-permute-start | bytes 589832 | tf_op jit(solution)/shard_map/ppermute | solution.py:612
  11.3 2.2 %collective-permute-done.refs_0_ = bf16[384,256]{1,0:T(8,128)(2,1)S(1)} collective-permute-done((bf16[384,256]{1,0:T(8,128)(2,1)S(1)}, bf16[384,256]{1,0:T(8,128)(2,1)S(1)}, u32[]{:S(2)}, u32[]{:S(2)}) %collective-permute-start) | collective-permute-done | bytes 196640 | tf_op jit(solution)/shard_map/ppermute | solution.py:612
  13.5 1.4 %collective-permute-start.5 = (bf16[384,256]{1,0:T(8,128)(2,1)S(1)}, bf16[384,256]{1,0:T(8,128)(2,1)S(1)}, u32[]{:S(2)}, u32[]{:S(2)}) collective-permute-start(bf16[384,256]{1,0:T(8,128)(2,1)S(1)} %get-tuple-element.34), channel_id=1, source_target_pairs={{0,24},{4,28},{8,16},{12,20},{16,8},{20,12},{24,0},{28,4},{1,25},{... | collective-permute-start | bytes 589832 | tf_op jit(solution)/shard_map/ppermute | solution.py:612
  14.9 5.2 %collective-permute-done.3.refs_3_.refs_0_ = bf16[544,256]{1,0:T(8,128)(2,1)S(1)} collective-permute-done((bf16[544,256]{1,0:T(8,128)(2,1)S(1)}, bf16[544,256]{1,0:T(8,128)(2,1)S(1)}, u32[]{:S(2)}, u32[]{:S(2)}) %collective-permute-start.3) | collective-permute-done | bytes 278560 | tf_op jit(solution)/shard_map/ppermute | solution.py:612
  20.1 3.8 %collective-permute-start.6 = (bf16[384,256]{1,0:T(8,128)(2,1)S(1)}, bf16[384,256]{1,0:T(8,128)(2,1)S(1)}, u32[]{:S(2)}, u32[]{:S(2)}) collective-permute-start(bf16[384,256]{1,0:T(8,128)(2,1)S(1)} %get-tuple-element.35), channel_id=1, source_target_pairs={{0,28},{4,24},{8,20},{12,16},{16,12},{20,8},{24,4},{28,0},{1,29},{... | collective-permute-start | bytes 589832 | tf_op jit(solution)/shard_map/ppermute | solution.py:612
  24.9 1.6 %shard_map.140 = (f32[1,256]{1,0:T(1,128)S(1)}, f32[1,256]{1,0:T(1,128)S(1)}, bf16[64,256]{1,0:T(8,128)(2,1)S(1)}, bf16[64,1280]{1,0:T(8,128)(2,1)S(1)}, f32[128...) custom-call(s32[3]{0:T(128)S(1)} %pad_add_fusion.place_ref, f32[1]{0:T(128)S(6)} %copy.15.cot_ref, ...), custom_call_target="tpu_custom_call" | custom-call | flops 1 | bytes 1 | tf_op jit(solution)/shard_map/pallas_call | solution.py:237
  26.7 11.5 %collective-permute-done.4.refs_4_ = bf16[384,256]{1,0:T(8,128)(2,1)S(1)} collective-permute-done((bf16[384,256]{1,0:T(8,128)(2,1)S(1)}, bf16[384,256]{1,0:T(8,128)(2,1)S(1)}, u32[]{:S(2)}, u32[]{:S(2)}) %collective-permute-start.4) | collective-permute-done | bytes 196640 | tf_op jit(solution)/shard_map/ppermute | solution.py:612
  38.2 1.8 %shard_map.141 = (f32[6,2,128,128]{3,2,1,0:T(8,128)S(1)}, f32[6,2,128,128]{3,2,1,0:T(8,128)S(1)}) custom-call(bf16[384,256]{1,0:T(8,128)(2,1)S(1)} %collective-permute-done.refs_0_, bf16[384,256]{1,0:T(8,128)(2,1)S(1)} %collective-permute-done.1.refs_1_, bf16[384,256]{1,0:T(8,128)(2,1)S(1)} %collective-permute-done.2.refs_2_, ...), custom_call_target="tpu_custom_call" | custom-call | flops 1 | bytes 1 | tf_op jit(solution)/shard_map/pallas_call | solution.py:310
  40.3 1.8 %collective-permute-start.9 = (bf16[4,320,128]{2,1,0:T(8,128)(2,1)S(1)}, bf16[4,320,128]{2,1,0:T(8,128)(2,1)S(1)}, u32[]{:S(2)}, u32[]{:S(2)}) collective-permute-start(bf16[4,320,128]{2,1,0:T(8,128)(2,1)S(1)} %shard_map.145.refs_0_), channel_id=1, source_target_pairs={{0,2},{1,3},{2,0},{3,1},{4,6},{5,7},{6,4},{7,5},{8,10},{9,11},{10,... | collective-permute-start | bytes 983048 | tf_op jit(solution)/shard_map/ppermute | solution.py:612
  42.2 1.5 %collective-permute-start.10 = (bf16[4,320,128]{2,1,0:T(8,128)(2,1)S(1)}, bf16[4,320,128]{2,1,0:T(8,128)(2,1)S(1)}, u32[]{:S(2)}, u32[]{:S(2)}) collective-permute-start(bf16[4,320,128]{2,1,0:T(8,128)(2,1)S(1)} %shard_map.145.refs_0_), channel_id=1, source_target_pairs={{0,6},{1,7},{2,4},{3,5},{4,2},{5,3},{6,0},{7,1},{8,14},{9,15},{10,... | collective-permute-start | bytes 983048 | tf_op jit(solution)/shard_map/ppermute | solution.py:628
  43.7 3.8 %shard_map.142 = (bf16[8,128,256]{2,1,0:T(8,128)(2,1)S(1)}, bf16[8,64,128]{2,1,0:T(8,128)(2,1)S(1)}) custom-call(s32[3]{0:T(128)S(1)} %pad_add_fusion.place_ref, bf16[384,256]{1,0:T(8,128)(2,1)S(1)} %collective-permute-done.refs_0_, bf16[384,256]{1,0:T(8,128)(2,1)S(1)} %collective-permute-done.1.refs_1_, ...), custom_call_target="tpu_custom_call" | custom-call | flops 1073741824 | bytes 2097152 | tf_op jit(solution)/shard_map/pallas_call | solution.py:366
  47.5 12.8 %all_to_all.15.refs_0_ = bf16[8,64,128]{2,1,0:T(8,128)(2,1)S(1)} all-to-all(bf16[8,64,128]{2,1,0:T(8,128)(2,1)S(1)} %get-tuple-element.41), channel_id=1, replica_groups={{16,20,8,12,24,28,0,4},{17,21,9,13,25,29,1,5},{18,22,10,14,26,30,2,6},{..., dimensions={0} | all-to-all | bytes 262144 | tf_op jit(solution)/shard_map/all_to_all | solution.py:616
  60.4 0.8 shard_map.146.refs_0_
  61.3 9.4 %all_to_all.16 = bf16[8,64,128]{2,1,0:T(8,128)(2,1)S(1)} all-to-all(bf16[8,64,128]{2,1,0:T(8,128)(2,1)S(1)} %shard_map.143.refs_4_), channel_id=1, replica_groups={{16,20,8,12,24,28,0,4},{17,21,9,13,25,29,1,5},{18,22,10,14,26,30,2,6},{..., dimensions={0} | all-to-all | bytes 262144 | tf_op jit(solution)/shard_map/all_to_all | solution.py:616
  70.7 3.3 %shard_map.147 = (f32[1,128]{1,0:T(1,128)}, bf16[512,128]{1,0:T(8,128)(2,1)S(1)}, bf16[64,256]{1,0:T(8,128)(2,1)S(1)}) custom-call(s32[3]{0:T(128)S(1)} %pad_add_fusion.place_ref, bf16[512,128]{1,0:T(8,128)(2,1)S(1)} %bitcast.7, bf16[2,256,1280]{2,1,0:T(8,128)(2,1)S(1)} %shard_map.146.refs_0_, bf16[2,256,1280]{2,1,0:T(8,128)(2,1)S(1)} %collective-permute-done.11.refs_1_, ...), custom_call_target="tpu_custom_call" | custom-call | flops 503316480 | bytes 2785280 | tf_op jit(solution)/shard_map/pallas_call | solution.py:520
  74.1 1.6 %collective-permute-start.13 = (bf16[64,256]{1,0:T(8,128)(2,1)S(1)}, bf16[64,256]{1,0:T(8,128)(2,1)S(1)}, u32[]{:S(2)}, u32[]{:S(2)}) collective-permute-start(bf16[64,256]{1,0:T(8,128)(2,1)S(1)} %get-tuple-element.51.refs_0_), channel_id=1, source_target_pairs={{0,2},{1,3},{2,0},{3,1},{4,6},{5,7},{6,4},{7,5},{8,10},{9,11},{10,... | collective-permute-start | bytes 98312 | tf_op jit(solution)/shard_map/ppermute | solution.py:612
  76.0 1.1 %shard_map.148 = (bf16[1,2,1024,128]{3,2,1,0:T(8,128)(2,1)}, f32[8,128]{1,0:T(8,128)S(1)}) custom-call(bf16[512,128]{1,0:T(8,128)(2,1)S(1)} %get-tuple-element.49.grad_ref, f32[1,256]{1,0:T(1,128)S(1)} %get-tuple-element.36.refs_6_.refs_10_.scale_ref, bf16[64,256]{1,0:T(8,128)(2,1)S(1)} %get-tuple-element.40.refs_12_.proj_ref), custom_call_target="tpu_custom_call" | custom-call | flops 67108864 | bytes 524288 | tf_op jit(solution)/shard_map/pallas_call | solution.py:563
  77.1 1.0 %collective-permute-done.13.refs_2_ = bf16[64,256]{1,0:T(8,128)(2,1)S(1)} collective-permute-done((bf16[64,256]{1,0:T(8,128)(2,1)S(1)}, bf16[64,256]{1,0:T(8,128)(2,1)S(1)}, u32[]{:S(2)}, u32[]{:S(2)}) %collective-permute-start.13) | collective-permute-done | bytes 32800 | tf_op jit(solution)/shard_map/ppermute | solution.py:612
  78.1 0.9 %collective-permute-done.14.refs_3_ = bf16[64,256]{1,0:T(8,128)(2,1)S(1)} collective-permute-done((bf16[64,256]{1,0:T(8,128)(2,1)S(1)}, bf16[64,256]{1,0:T(8,128)(2,1)S(1)}, u32[]{:S(2)}, u32[]{:S(2)}) %collective-permute-start.14) | collective-permute-done | bytes 32800 | tf_op jit(solution)/shard_map/ppermute | solution.py:612
  79.1 11.5 %all_to_all.17.in_ref = bf16[8,64,256]{2,1,0:T(8,128)(2,1)S(1)} all-to-all(bf16[8,64,256]{2,1,0:T(8,128)(2,1)S(1)} %shard_map.149), channel_id=1, replica_groups={{16,20,8,12,24,28,0,4},{17,21,9,13,25,29,1,5},{18,22,10,14,26,30,2,6},{..., dimensions={0} | all-to-all | bytes 524288 | tf_op jit(solution)/shard_map/all_to_all | solution.py:616
  (22 shorter events, 2.6 us)
Async XLA Ops:
  2.4 17.7 %collective-permute-start.3 = (bf16[544,256]{1,0:T(8,128)(2,1)S(1)}, bf16[544,256]{1,0:T(8,128)(2,1)S(1)}, u32[]{:S(2)}, u32[]{:S(2)}) collective-permute-start(bf16[544,256]{1,0:T(8,128)(2,1)S(1)} %get-tuple-element.31), channel_id=1, source_target_pairs={{0,16},{4,20},{8,24},{12,28},{16,0},{20,4},{24,8},{28,12},{1,17},{... | collective-permute-start | bytes 835592 | tf_op jit(solution)/shard_map/ppermute | solution.py:612
  6.5 6.9 %collective-permute-start = (bf16[384,256]{1,0:T(8,128)(2,1)S(1)}, bf16[384,256]{1,0:T(8,128)(2,1)S(1)}, u32[]{:S(2)}, u32[]{:S(2)}) collective-permute-start(bf16[384,256]{1,0:T(8,128)(2,1)S(1)} %get-tuple-element.28), channel_id=1, source_target_pairs={{0,4},{4,0},{8,12},{12,8},{16,20},{20,16},{24,28},{28,24},{1,5},{5... | collective-permute-start | bytes 589832 | tf_op jit(solution)/shard_map/ppermute | solution.py:612
  8.0 16.1 %collective-permute-start.1 = (bf16[384,256]{1,0:T(8,128)(2,1)S(1)}, bf16[384,256]{1,0:T(8,128)(2,1)S(1)}, u32[]{:S(2)}, u32[]{:S(2)}) collective-permute-start(bf16[384,256]{1,0:T(8,128)(2,1)S(1)} %get-tuple-element.29), channel_id=1, source_target_pairs={{0,8},{4,12},{8,0},{12,4},{16,24},{20,28},{24,16},{28,20},{1,9},{5... | collective-permute-start | bytes 589832 | tf_op jit(solution)/shard_map/ppermute | solution.py:612
  9.6 17.1 %collective-permute-start.2 = (bf16[384,256]{1,0:T(8,128)(2,1)S(1)}, bf16[384,256]{1,0:T(8,128)(2,1)S(1)}, u32[]{:S(2)}, u32[]{:S(2)}) collective-permute-start(bf16[384,256]{1,0:T(8,128)(2,1)S(1)} %get-tuple-element.30), channel_id=1, source_target_pairs={{0,12},{4,8},{8,4},{12,0},{16,28},{20,24},{24,20},{28,16},{1,13},{... | collective-permute-start | bytes 589832 | tf_op jit(solution)/shard_map/ppermute | solution.py:612
  10.0 28.2 %collective-permute-start.4 = (bf16[384,256]{1,0:T(8,128)(2,1)S(1)}, bf16[384,256]{1,0:T(8,128)(2,1)S(1)}, u32[]{:S(2)}, u32[]{:S(2)}) collective-permute-start(bf16[384,256]{1,0:T(8,128)(2,1)S(1)} %get-tuple-element.32), channel_id=1, source_target_pairs={{0,20},{4,16},{8,28},{12,24},{16,4},{20,0},{24,12},{28,8},{1,21},{... | collective-permute-start | bytes 589832 | tf_op jit(solution)/shard_map/ppermute | solution.py:612
  13.5 30.2 %collective-permute-start.5 = (bf16[384,256]{1,0:T(8,128)(2,1)S(1)}, bf16[384,256]{1,0:T(8,128)(2,1)S(1)}, u32[]{:S(2)}, u32[]{:S(2)}) collective-permute-start(bf16[384,256]{1,0:T(8,128)(2,1)S(1)} %get-tuple-element.34), channel_id=1, source_target_pairs={{0,24},{4,28},{8,16},{12,20},{16,8},{20,12},{24,0},{28,4},{1,25},{... | collective-permute-start | bytes 589832 | tf_op jit(solution)/shard_map/ppermute | solution.py:612
  20.1 23.6 %collective-permute-start.6 = (bf16[384,256]{1,0:T(8,128)(2,1)S(1)}, bf16[384,256]{1,0:T(8,128)(2,1)S(1)}, u32[]{:S(2)}, u32[]{:S(2)}) collective-permute-start(bf16[384,256]{1,0:T(8,128)(2,1)S(1)} %get-tuple-element.35), channel_id=1, source_target_pairs={{0,28},{4,24},{8,20},{12,16},{16,12},{20,8},{24,4},{28,0},{1,29},{... | collective-permute-start | bytes 589832 | tf_op jit(solution)/shard_map/ppermute | solution.py:612
  24.2 15.9 %collective-permute-start.7 = (bf16[2,320,128]{2,1,0:T(8,128)(2,1)S(1)}, bf16[2,320,128]{2,1,0:T(8,128)(2,1)S(1)}, u32[]{:S(2)}, u32[]{:S(2)}) collective-permute-start(bf16[2,320,128]{2,1,0:T(8,128)(2,1)S(1)} %shard_map.144.first_ref), channel_id=1, source_target_pairs={{0,8},{4,12},{8,0},{12,4},{16,24},{20,28},{24,16},{28,20},{1,9},{5... | collective-permute-start | bytes 491528 | tf_op jit(solution)/shard_map/ppermute | solution.py:612
  40.1 20.2 %collective-permute-start.8 = (bf16[4,320,128]{2,1,0:T(8,128)(2,1)S(1)}, bf16[4,320,128]{2,1,0:T(8,128)(2,1)S(1)}, u32[]{:S(2)}, u32[]{:S(2)}) collective-permute-start(bf16[4,320,128]{2,1,0:T(8,128)(2,1)S(1)} %shard_map.145.refs_0_), channel_id=1, source_target_pairs={{0,4},{4,0},{8,12},{12,8},{16,20},{20,16},{24,28},{28,24},{1,5},{5... | collective-permute-start | bytes 983048 | tf_op jit(solution)/shard_map/ppermute | solution.py:612
  40.3 20.0 %collective-permute-start.9 = (bf16[4,320,128]{2,1,0:T(8,128)(2,1)S(1)}, bf16[4,320,128]{2,1,0:T(8,128)(2,1)S(1)}, u32[]{:S(2)}, u32[]{:S(2)}) collective-permute-start(bf16[4,320,128]{2,1,0:T(8,128)(2,1)S(1)} %shard_map.145.refs_0_), channel_id=1, source_target_pairs={{0,2},{1,3},{2,0},{3,1},{4,6},{5,7},{6,4},{7,5},{8,10},{9,11},{10,... | collective-permute-start | bytes 983048 | tf_op jit(solution)/shard_map/ppermute | solution.py:612
  42.2 18.2 %collective-permute-start.10 = (bf16[4,320,128]{2,1,0:T(8,128)(2,1)S(1)}, bf16[4,320,128]{2,1,0:T(8,128)(2,1)S(1)}, u32[]{:S(2)}, u32[]{:S(2)}) collective-permute-start(bf16[4,320,128]{2,1,0:T(8,128)(2,1)S(1)} %shard_map.145.refs_0_), channel_id=1, source_target_pairs={{0,6},{1,7},{2,4},{3,5},{4,2},{5,3},{6,0},{7,1},{8,14},{9,15},{10,... | collective-permute-start | bytes 983048 | tf_op jit(solution)/shard_map/ppermute | solution.py:628
  61.2 9.5 %collective-permute-start.11 = (bf16[2,256,1280]{2,1,0:T(8,128)(2,1)S(1)}, bf16[2,256,1280]{2,1,0:T(8,128)(2,1)S(1)}, u32[]{:S(2)}, u32[]{:S(2)}) collective-permute-start(bf16[2,256,1280]{2,1,0:T(8,128)(2,1)S(1)} %shard_map.146.refs_0_), channel_id=1, source_target_pairs={{0,1},{1,0},{2,3},{3,2},{4,5},{5,4},{6,7},{7,6},{8,9},{9,8},{10,11... | collective-permute-start | bytes 3932168 | tf_op jit(solution)/shard_map/ppermute | solution.py:612
  74.0 3.0 %collective-permute-start.12 = (bf16[64,256]{1,0:T(8,128)(2,1)S(1)}, bf16[64,256]{1,0:T(8,128)(2,1)S(1)}, u32[]{:S(2)}, u32[]{:S(2)}) collective-permute-start(bf16[64,256]{1,0:T(8,128)(2,1)S(1)} %get-tuple-element.51.refs_0_), channel_id=1, source_target_pairs={{0,1},{1,0},{2,3},{3,2},{4,5},{5,4},{6,7},{7,6},{8,9},{9,8},{10,11... | collective-permute-start | bytes 98312 | tf_op jit(solution)/shard_map/ppermute | solution.py:612
  74.1 4.0 %collective-permute-start.13 = (bf16[64,256]{1,0:T(8,128)(2,1)S(1)}, bf16[64,256]{1,0:T(8,128)(2,1)S(1)}, u32[]{:S(2)}, u32[]{:S(2)}) collective-permute-start(bf16[64,256]{1,0:T(8,128)(2,1)S(1)} %get-tuple-element.51.refs_0_), channel_id=1, source_target_pairs={{0,2},{1,3},{2,0},{3,1},{4,6},{5,7},{6,4},{7,5},{8,10},{9,11},{10,... | collective-permute-start | bytes 98312 | tf_op jit(solution)/shard_map/ppermute | solution.py:612
  75.7 3.3 %collective-permute-start.14 = (bf16[64,256]{1,0:T(8,128)(2,1)S(1)}, bf16[64,256]{1,0:T(8,128)(2,1)S(1)}, u32[]{:S(2)}, u32[]{:S(2)}) collective-permute-start(bf16[64,256]{1,0:T(8,128)(2,1)S(1)} %get-tuple-element.51.refs_0_), channel_id=1, source_target_pairs={{0,3},{1,2},{2,1},{3,0},{4,7},{5,6},{6,5},{7,4},{8,11},{9,10},{10,... | collective-permute-start | bytes 98312 | tf_op jit(solution)/shard_map/ppermute | solution.py:612

commit v19 on v18

--- a/solution.py
+++ b/solution.py
@@ -383,7 +383,7 @@
 
 def total_kernel(copies, count, *refs):
     out_ref = refs[-1]
-    if count == 1:
+    if len(refs[0].shape) == 3:
         parts = [refs[0][i].astype(F32) for i in range(refs[0].shape[0])]
     else:
         parts = [ref[...].astype(F32) for ref in refs[:count]]
@@ -672,7 +672,7 @@
 
     kept, order = [], list(range(seq_count))
     if seq_count == 8:
-        late = [slot for slot, mask in enumerate(masks) if mask in (6, 7)]
+        late = [slot for slot, mask in enumerate(masks) if mask in (5, 6, 7)]
         order = [slot for slot in order if slot not in late]
         kept = attend_early(sizes, [received[slot] for slot in order], scale)
         order = order + late

time: 91.7 us -> 92.1 us (level)
  no operation moved by 1% of the time
where the time goes in v19:
time: 92.1 us; the launch traced here: 91.8 us
  blocking collectives  34.5 us (37%)
  waiting for transfers between devices  20.7 us (22%)
  starting transfers between devices  19.7 us (21%)
  Pallas kernels  15.5 us (17%)
  between operations  1.4 us (2%)
    all_to_all x3, blocking collectives, all_to_all(): lax.all_to_all(x, 'seq', split_axis=0, concat_axis=0, tiled=True, axis_in...  34.5 us
    ppermute x14, waiting for transfers between devices, swap(): return lax.ppermute(x, axis, [(i, i ^ mask) for i in range(count)])  20.7 us
    ppermute x14, starting transfers between devices, swap(): return lax.ppermute(x, axis, [(i, i ^ mask) for i in range(count)])  18.2 us
    pallas_call x1, Pallas kernels, attend(): pl.pallas_call(functools.partial(attend_kernel, sizes, masks, early), out...  4.22 us
    pallas_call x1, Pallas kernels, reward_head(): pl.pallas_call(functools.partial(head_kernel, grid_rows, fused, order, em...  3.33 us
  transfers between devices with their start and end apart: 15, of which 7 were waited for; matrix products, arithmetic and copies ran while one was open for 0% of the time, Pallas kernels for 9%

profile of v19, /device:TPU:0, one launch (start us, length us, event | category | flops | bytes accessed | tf_op | source)
XLA Modules:
  0.0 91.8 jit_solution(15478672726135462175)
XLA Ops:
  0.6 1.8 %shard_map.139 = (bf16[384,256]{1,0:T(8,128)(2,1)S(1)}, bf16[384,256]{1,0:T(8,128)(2,1)S(1)}, bf16[384,256]{1,0:T(8,128)(2,1)S(1)}, bf16[544,256]{1,0:T(8,128)(2...) custom-call(bf16[1,128,2048]{2,1,0:T(8,128)(2,1)} %q_ref.1, ...), custom_call_target="tpu_custom_call" | custom-call | bytes 3145728 | tf_op jit(solution)/shard_map/pallas_call | solution.py:125
  2.4 4.1 %collective-permute-start.3 = (bf16[544,256]{1,0:T(8,128)(2,1)S(1)}, bf16[544,256]{1,0:T(8,128)(2,1)S(1)}, u32[]{:S(2)}, u32[]{:S(2)}) collective-permute-start(bf16[544,256]{1,0:T(8,128)(2,1)S(1)} %get-tuple-element.31), channel_id=1, source_target_pairs={{0,16},{4,20},{8,24},{12,28},{16,0},{20,4},{24,8},{28,12},{1,17},{... | collective-permute-start | bytes 835592 | tf_op jit(solution)/shard_map/ppermute | solution.py:612
  6.5 1.5 %collective-permute-start = (bf16[384,256]{1,0:T(8,128)(2,1)S(1)}, bf16[384,256]{1,0:T(8,128)(2,1)S(1)}, u32[]{:S(2)}, u32[]{:S(2)}) collective-permute-start(bf16[384,256]{1,0:T(8,128)(2,1)S(1)} %get-tuple-element.28), channel_id=1, source_target_pairs={{0,4},{4,0},{8,12},{12,8},{16,20},{20,16},{24,28},{28,24},{1,5},{5... | collective-permute-start | bytes 589832 | tf_op jit(solution)/shard_map/ppermute | solution.py:612
  8.0 1.6 %collective-permute-start.1 = (bf16[384,256]{1,0:T(8,128)(2,1)S(1)}, bf16[384,256]{1,0:T(8,128)(2,1)S(1)}, u32[]{:S(2)}, u32[]{:S(2)}) collective-permute-start(bf16[384,256]{1,0:T(8,128)(2,1)S(1)} %get-tuple-element.29), channel_id=1, source_target_pairs={{0,8},{4,12},{8,0},{12,4},{16,24},{20,28},{24,16},{28,20},{1,9},{5... | collective-permute-start | bytes 589832 | tf_op jit(solution)/shard_map/ppermute | solution.py:612
  10.0 1.3 %collective-permute-start.4 = (bf16[384,256]{1,0:T(8,128)(2,1)S(1)}, bf16[384,256]{1,0:T(8,128)(2,1)S(1)}, u32[]{:S(2)}, u32[]{:S(2)}) collective-permute-start(bf16[384,256]{1,0:T(8,128)(2,1)S(1)} %get-tuple-element.33), channel_id=1, source_target_pairs={{0,20},{4,16},{8,28},{12,24},{16,4},{20,0},{24,12},{28,8},{1,21},{... | collective-permute-start | bytes 589832 | tf_op jit(solution)/shard_map/ppermute | solution.py:612
  11.3 2.2 %collective-permute-done.refs_0_ = bf16[384,256]{1,0:T(8,128)(2,1)S(1)} collective-permute-done((bf16[384,256]{1,0:T(8,128)(2,1)S(1)}, bf16[384,256]{1,0:T(8,128)(2,1)S(1)}, u32[]{:S(2)}, u32[]{:S(2)}) %collective-permute-start) | collective-permute-done | bytes 196640 | tf_op jit(solution)/shard_map/ppermute | solution.py:612
  13.5 1.4 %collective-permute-start.5 = (bf16[384,256]{1,0:T(8,128)(2,1)S(1)}, bf16[384,256]{1,0:T(8,128)(2,1)S(1)}, u32[]{:S(2)}, u32[]{:S(2)}) collective-permute-start(bf16[384,256]{1,0:T(8,128)(2,1)S(1)} %get-tuple-element.34), channel_id=1, source_target_pairs={{0,24},{4,28},{8,16},{12,20},{16,8},{20,12},{24,0},{28,4},{1,25},{... | collective-permute-start | bytes 589832 | tf_op jit(solution)/shard_map/ppermute | solution.py:612
  14.9 5.2 %collective-permute-done.3.refs_3_.refs_0_ = bf16[544,256]{1,0:T(8,128)(2,1)S(1)} collective-permute-done((bf16[544,256]{1,0:T(8,128)(2,1)S(1)}, bf16[544,256]{1,0:T(8,128)(2,1)S(1)}, u32[]{:S(2)}, u32[]{:S(2)}) %collective-permute-start.3) | collective-permute-done | bytes 278560 | tf_op jit(solution)/shard_map/ppermute | solution.py:612
  20.1 3.8 %collective-permute-start.6 = (bf16[384,256]{1,0:T(8,128)(2,1)S(1)}, bf16[384,256]{1,0:T(8,128)(2,1)S(1)}, u32[]{:S(2)}, u32[]{:S(2)}) collective-permute-start(bf16[384,256]{1,0:T(8,128)(2,1)S(1)} %get-tuple-element.35), channel_id=1, source_target_pairs={{0,28},{4,24},{8,20},{12,16},{16,12},{20,8},{24,4},{28,0},{1,29},{... | collective-permute-start | bytes 589832 | tf_op jit(solution)/shard_map/ppermute | solution.py:612
  24.9 1.6 %shard_map.140 = (f32[1,256]{1,0:T(1,128)S(1)}, f32[1,256]{1,0:T(1,128)S(1)}, bf16[64,256]{1,0:T(8,128)(2,1)S(1)}, bf16[64,1280]{1,0:T(8,128)(2,1)S(1)}, f32[128...) custom-call(s32[3]{0:T(128)S(1)} %pad_add_fusion.place_ref, f32[1]{0:T(128)S(6)} %copy.15.cot_ref, ...), custom_call_target="tpu_custom_call" | custom-call | flops 1 | bytes 1 | tf_op jit(solution)/shard_map/pallas_call | solution.py:237
  26.7 1.7 %shard_map.141 = (f32[5,2,128,128]{3,2,1,0:T(8,128)S(1)}, f32[5,2,128,128]{3,2,1,0:T(8,128)S(1)}) custom-call(bf16[384,256]{1,0:T(8,128)(2,1)S(1)} %collective-permute-done.refs_0_, bf16[384,256]{1,0:T(8,128)(2,1)S(1)} %collective-permute-done.1.refs_1_, bf16[384,256]{1,0:T(8,128)(2,1)S(1)} %collective-permute-done.2.refs_2_, ...), custom_call_target="tpu_custom_call" | custom-call | flops 1 | bytes 1 | tf_op jit(solution)/shard_map/pallas_call | solution.py:310
  28.4 10.9 %collective-permute-done.7.second_ref = bf16[2,320,128]{2,1,0:T(8,128)(2,1)S(1)} collective-permute-done((bf16[2,320,128]{2,1,0:T(8,128)(2,1)S(1)}, bf16[2,320,128]{2,1,0:T(8,128)(2,1)S(1)}, u32[]{:S(2)}, u32[]{:S(2)}) %collective-permute-start.7) | collective-permute-done | bytes 163872 | tf_op jit(solution)/shard_map/ppermute | solution.py:612
  39.9 1.5 %collective-permute-start.9 = (bf16[4,320,128]{2,1,0:T(8,128)(2,1)S(1)}, bf16[4,320,128]{2,1,0:T(8,128)(2,1)S(1)}, u32[]{:S(2)}, u32[]{:S(2)}) collective-permute-start(bf16[4,320,128]{2,1,0:T(8,128)(2,1)S(1)} %shard_map.145.refs_0_), channel_id=1, source_target_pairs={{0,2},{1,3},{2,0},{3,1},{4,6},{5,7},{6,4},{7,5},{8,10},{9,11},{10,... | collective-permute-start | bytes 983048 | tf_op jit(solution)/shard_map/ppermute | solution.py:612
  41.4 1.4 %collective-permute-start.10 = (bf16[4,320,128]{2,1,0:T(8,128)(2,1)S(1)}, bf16[4,320,128]{2,1,0:T(8,128)(2,1)S(1)}, u32[]{:S(2)}, u32[]{:S(2)}) collective-permute-start(bf16[4,320,128]{2,1,0:T(8,128)(2,1)S(1)} %shard_map.145.refs_0_), channel_id=1, source_target_pairs={{0,6},{1,7},{2,4},{3,5},{4,2},{5,3},{6,0},{7,1},{8,14},{9,15},{10,... | collective-permute-start | bytes 983048 | tf_op jit(solution)/shard_map/ppermute | solution.py:628
  42.9 4.2 %shard_map.142 = (bf16[8,128,256]{2,1,0:T(8,128)(2,1)S(1)}, bf16[8,64,128]{2,1,0:T(8,128)(2,1)S(1)}) custom-call(s32[3]{0:T(128)S(1)} %pad_add_fusion.place_ref, bf16[384,256]{1,0:T(8,128)(2,1)S(1)} %collective-permute-done.refs_0_, bf16[384,256]{1,0:T(8,128)(2,1)S(1)} %collective-permute-done.1.refs_1_, ...), custom_call_target="tpu_custom_call" | custom-call | flops 1073741824 | bytes 2097152 | tf_op jit(solution)/shard_map/pallas_call | solution.py:366
  47.1 13.6 %all_to_all.15.refs_0_ = bf16[8,64,128]{2,1,0:T(8,128)(2,1)S(1)} all-to-all(bf16[8,64,128]{2,1,0:T(8,128)(2,1)S(1)} %get-tuple-element.41), channel_id=1, replica_groups={{16,20,8,12,24,28,0,4},{17,21,9,13,25,29,1,5},{18,22,10,14,26,30,2,6},{..., dimensions={0} | all-to-all | bytes 262144 | tf_op jit(solution)/shard_map/all_to_all | solution.py:616
  60.8 0.8 shard_map.146.refs_0_
  61.7 9.4 %all_to_all.16 = bf16[8,64,128]{2,1,0:T(8,128)(2,1)S(1)} all-to-all(bf16[8,64,128]{2,1,0:T(8,128)(2,1)S(1)} %shard_map.143.refs_4_), channel_id=1, replica_groups={{16,20,8,12,24,28,0,4},{17,21,9,13,25,29,1,5},{18,22,10,14,26,30,2,6},{..., dimensions={0} | all-to-all | bytes 262144 | tf_op jit(solution)/shard_map/all_to_all | solution.py:616
  71.1 3.3 %shard_map.147 = (f32[1,128]{1,0:T(1,128)}, bf16[512,128]{1,0:T(8,128)(2,1)S(1)}, bf16[64,256]{1,0:T(8,128)(2,1)S(1)}) custom-call(s32[3]{0:T(128)S(1)} %pad_add_fusion.place_ref, bf16[512,128]{1,0:T(8,128)(2,1)S(1)} %bitcast.7, bf16[2,256,1280]{2,1,0:T(8,128)(2,1)S(1)} %shard_map.146.refs_0_, bf16[2,256,1280]{2,1,0:T(8,128)(2,1)S(1)} %collective-permute-done.11.refs_1_, ...), custom_call_target="tpu_custom_call" | custom-call | flops 503316480 | bytes 2785280 | tf_op jit(solution)/shard_map/pallas_call | solution.py:520
  74.5 1.6 %collective-permute-start.13 = (bf16[64,256]{1,0:T(8,128)(2,1)S(1)}, bf16[64,256]{1,0:T(8,128)(2,1)S(1)}, u32[]{:S(2)}, u32[]{:S(2)}) collective-permute-start(bf16[64,256]{1,0:T(8,128)(2,1)S(1)} %get-tuple-element.51.refs_0_), channel_id=1, source_target_pairs={{0,2},{1,3},{2,0},{3,1},{4,6},{5,7},{6,4},{7,5},{8,10},{9,11},{10,... | collective-permute-start | bytes 98312 | tf_op jit(solution)/shard_map/ppermute | solution.py:612
  76.4 1.1 %shard_map.148 = (bf16[1,2,1024,128]{3,2,1,0:T(8,128)(2,1)}, f32[8,128]{1,0:T(8,128)S(1)}) custom-call(bf16[512,128]{1,0:T(8,128)(2,1)S(1)} %get-tuple-element.49.grad_ref, f32[1,256]{1,0:T(1,128)S(1)} %get-tuple-element.36.refs_5_.refs_10_.scale_ref, bf16[64,256]{1,0:T(8,128)(2,1)S(1)} %get-tuple-element.40.refs_12_.proj_ref), custom_call_target="tpu_custom_call" | custom-call | flops 67108864 | bytes 524288 | tf_op jit(solution)/shard_map/pallas_call | solution.py:563
  77.5 1.0 %collective-permute-done.13.refs_2_ = bf16[64,256]{1,0:T(8,128)(2,1)S(1)} collective-permute-done((bf16[64,256]{1,0:T(8,128)(2,1)S(1)}, bf16[64,256]{1,0:T(8,128)(2,1)S(1)}, u32[]{:S(2)}, u32[]{:S(2)}) %collective-permute-start.13) | collective-permute-done | bytes 32800 | tf_op jit(solution)/shard_map/ppermute | solution.py:612
  78.5 0.9 %collective-permute-done.14.refs_3_ = bf16[64,256]{1,0:T(8,128)(2,1)S(1)} collective-permute-done((bf16[64,256]{1,0:T(8,128)(2,1)S(1)}, bf16[64,256]{1,0:T(8,128)(2,1)S(1)}, u32[]{:S(2)}, u32[]{:S(2)}) %collective-permute-start.14) | collective-permute-done | bytes 32800 | tf_op jit(solution)/shard_map/ppermute | solution.py:612
  79.4 11.5 %all_to_all.17.in_ref = bf16[8,64,256]{2,1,0:T(8,128)(2,1)S(1)} all-to-all(bf16[8,64,256]{2,1,0:T(8,128)(2,1)S(1)} %shard_map.149), channel_id=1, replica_groups={{16,20,8,12,24,28,0,4},{17,21,9,13,25,29,1,5},{18,22,10,14,26,30,2,6},{..., dimensions={0} | all-to-all | bytes 524288 | tf_op jit(solution)/shard_map/all_to_all | solution.py:616
  (22 shorter events, 3.0 us)
Async XLA Ops:
  2.4 17.7 %collective-permute-start.3 = (bf16[544,256]{1,0:T(8,128)(2,1)S(1)}, bf16[544,256]{1,0:T(8,128)(2,1)S(1)}, u32[]{:S(2)}, u32[]{:S(2)}) collective-permute-start(bf16[544,256]{1,0:T(8,128)(2,1)S(1)} %get-tuple-element.31), channel_id=1, source_target_pairs={{0,16},{4,20},{8,24},{12,28},{16,0},{20,4},{24,8},{28,12},{1,17},{... | collective-permute-start | bytes 835592 | tf_op jit(solution)/shard_map/ppermute | solution.py:612
  6.5 6.9 %collective-permute-start = (bf16[384,256]{1,0:T(8,128)(2,1)S(1)}, bf16[384,256]{1,0:T(8,128)(2,1)S(1)}, u32[]{:S(2)}, u32[]{:S(2)}) collective-permute-start(bf16[384,256]{1,0:T(8,128)(2,1)S(1)} %get-tuple-element.28), channel_id=1, source_target_pairs={{0,4},{4,0},{8,12},{12,8},{16,20},{20,16},{24,28},{28,24},{1,5},{5... | collective-permute-start | bytes 589832 | tf_op jit(solution)/shard_map/ppermute | solution.py:612
  8.0 16.1 %collective-permute-start.1 = (bf16[384,256]{1,0:T(8,128)(2,1)S(1)}, bf16[384,256]{1,0:T(8,128)(2,1)S(1)}, u32[]{:S(2)}, u32[]{:S(2)}) collective-permute-start(bf16[384,256]{1,0:T(8,128)(2,1)S(1)} %get-tuple-element.29), channel_id=1, source_target_pairs={{0,8},{4,12},{8,0},{12,4},{16,24},{20,28},{24,16},{28,20},{1,9},{5... | collective-permute-start | bytes 589832 | tf_op jit(solution)/shard_map/ppermute | solution.py:612
  9.6 17.1 %collective-permute-start.2 = (bf16[384,256]{1,0:T(8,128)(2,1)S(1)}, bf16[384,256]{1,0:T(8,128)(2,1)S(1)}, u32[]{:S(2)}, u32[]{:S(2)}) collective-permute-start(bf16[384,256]{1,0:T(8,128)(2,1)S(1)} %get-tuple-element.30), channel_id=1, source_target_pairs={{0,12},{4,8},{8,4},{12,0},{16,28},{20,24},{24,20},{28,16},{1,13},{... | collective-permute-start | bytes 589832 | tf_op jit(solution)/shard_map/ppermute | solution.py:612
  10.0 31.4 %collective-permute-start.4 = (bf16[384,256]{1,0:T(8,128)(2,1)S(1)}, bf16[384,256]{1,0:T(8,128)(2,1)S(1)}, u32[]{:S(2)}, u32[]{:S(2)}) collective-permute-start(bf16[384,256]{1,0:T(8,128)(2,1)S(1)} %get-tuple-element.33), channel_id=1, source_target_pairs={{0,20},{4,16},{8,28},{12,24},{16,4},{20,0},{24,12},{28,8},{1,21},{... | collective-permute-start | bytes 589832 | tf_op jit(solution)/shard_map/ppermute | solution.py:612
  13.5 29.4 %collective-permute-start.5 = (bf16[384,256]{1,0:T(8,128)(2,1)S(1)}, bf16[384,256]{1,0:T(8,128)(2,1)S(1)}, u32[]{:S(2)}, u32[]{:S(2)}) collective-permute-start(bf16[384,256]{1,0:T(8,128)(2,1)S(1)} %get-tuple-element.34), channel_id=1, source_target_pairs={{0,24},{4,28},{8,16},{12,20},{16,8},{20,12},{24,0},{28,4},{1,25},{... | collective-permute-start | bytes 589832 | tf_op jit(solution)/shard_map/ppermute | solution.py:612
  20.1 22.8 %collective-permute-start.6 = (bf16[384,256]{1,0:T(8,128)(2,1)S(1)}, bf16[384,256]{1,0:T(8,128)(2,1)S(1)}, u32[]{:S(2)}, u32[]{:S(2)}) collective-permute-start(bf16[384,256]{1,0:T(8,128)(2,1)S(1)} %get-tuple-element.35), channel_id=1, source_target_pairs={{0,28},{4,24},{8,20},{12,16},{16,12},{20,8},{24,4},{28,0},{1,29},{... | collective-permute-start | bytes 589832 | tf_op jit(solution)/shard_map/ppermute | solution.py:612
  24.2 15.1 %collective-permute-start.7 = (bf16[2,320,128]{2,1,0:T(8,128)(2,1)S(1)}, bf16[2,320,128]{2,1,0:T(8,128)(2,1)S(1)}, u32[]{:S(2)}, u32[]{:S(2)}) collective-permute-start(bf16[2,320,128]{2,1,0:T(8,128)(2,1)S(1)} %shard_map.144.first_ref), channel_id=1, source_target_pairs={{0,8},{4,12},{8,0},{12,4},{16,24},{20,28},{24,16},{28,20},{1,9},{5... | collective-permute-start | bytes 491528 | tf_op jit(solution)/shard_map/ppermute | solution.py:612
  39.3 21.4 %collective-permute-start.8 = (bf16[4,320,128]{2,1,0:T(8,128)(2,1)S(1)}, bf16[4,320,128]{2,1,0:T(8,128)(2,1)S(1)}, u32[]{:S(2)}, u32[]{:S(2)}) collective-permute-start(bf16[4,320,128]{2,1,0:T(8,128)(2,1)S(1)} %shard_map.145.refs_0_), channel_id=1, source_target_pairs={{0,4},{4,0},{8,12},{12,8},{16,20},{20,16},{24,28},{28,24},{1,5},{5... | collective-permute-start | bytes 983048 | tf_op jit(solution)/shard_map/ppermute | solution.py:612
  39.9 20.8 %collective-permute-start.9 = (bf16[4,320,128]{2,1,0:T(8,128)(2,1)S(1)}, bf16[4,320,128]{2,1,0:T(8,128)(2,1)S(1)}, u32[]{:S(2)}, u32[]{:S(2)}) collective-permute-start(bf16[4,320,128]{2,1,0:T(8,128)(2,1)S(1)} %shard_map.145.refs_0_), channel_id=1, source_target_pairs={{0,2},{1,3},{2,0},{3,1},{4,6},{5,7},{6,4},{7,5},{8,10},{9,11},{10,... | collective-permute-start | bytes 983048 | tf_op jit(solution)/shard_map/ppermute | solution.py:612
  41.4 19.3 %collective-permute-start.10 = (bf16[4,320,128]{2,1,0:T(8,128)(2,1)S(1)}, bf16[4,320,128]{2,1,0:T(8,128)(2,1)S(1)}, u32[]{:S(2)}, u32[]{:S(2)}) collective-permute-start(bf16[4,320,128]{2,1,0:T(8,128)(2,1)S(1)} %shard_map.145.refs_0_), channel_id=1, source_target_pairs={{0,6},{1,7},{2,4},{3,5},{4,2},{5,3},{6,0},{7,1},{8,14},{9,15},{10,... | collective-permute-start | bytes 983048 | tf_op jit(solution)/shard_map/ppermute | solution.py:628
  61.6 9.5 %collective-permute-start.11 = (bf16[2,256,1280]{2,1,0:T(8,128)(2,1)S(1)}, bf16[2,256,1280]{2,1,0:T(8,128)(2,1)S(1)}, u32[]{:S(2)}, u32[]{:S(2)}) collective-permute-start(bf16[2,256,1280]{2,1,0:T(8,128)(2,1)S(1)} %shard_map.146.refs_0_), channel_id=1, source_target_pairs={{0,1},{1,0},{2,3},{3,2},{4,5},{5,4},{6,7},{7,6},{8,9},{9,8},{10,11... | collective-permute-start | bytes 3932168 | tf_op jit(solution)/shard_map/ppermute | solution.py:612
  74.4 3.0 %collective-permute-start.12 = (bf16[64,256]{1,0:T(8,128)(2,1)S(1)}, bf16[64,256]{1,0:T(8,128)(2,1)S(1)}, u32[]{:S(2)}, u32[]{:S(2)}) collective-permute-start(bf16[64,256]{1,0:T(8,128)(2,1)S(1)} %get-tuple-element.51.refs_0_), channel_id=1, source_target_pairs={{0,1},{1,0},{2,3},{3,2},{4,5},{5,4},{6,7},{7,6},{8,9},{9,8},{10,11... | collective-permute-start | bytes 98312 | tf_op jit(solution)/shard_map/ppermute | solution.py:612
  74.5 4.0 %collective-permute-start.13 = (bf16[64,256]{1,0:T(8,128)(2,1)S(1)}, bf16[64,256]{1,0:T(8,128)(2,1)S(1)}, u32[]{:S(2)}, u32[]{:S(2)}) collective-permute-start(bf16[64,256]{1,0:T(8,128)(2,1)S(1)} %get-tuple-element.51.refs_0_), channel_id=1, source_target_pairs={{0,2},{1,3},{2,0},{3,1},{4,6},{5,7},{6,4},{7,5},{8,10},{9,11},{10,... | collective-permute-start | bytes 98312 | tf_op jit(solution)/shard_map/ppermute | solution.py:612
  76.1 3.3 %collective-permute-start.14 = (bf16[64,256]{1,0:T(8,128)(2,1)S(1)}, bf16[64,256]{1,0:T(8,128)(2,1)S(1)}, u32[]{:S(2)}, u32[]{:S(2)}) collective-permute-start(bf16[64,256]{1,0:T(8,128)(2,1)S(1)} %get-tuple-element.51.refs_0_), channel_id=1, source_target_pairs={{0,3},{1,2},{2,1},{3,0},{4,7},{5,6},{6,5},{7,4},{8,11},{9,10},{10,... | collective-permute-start | bytes 98312 | tf_op jit(solution)/shard_map/ppermute | solution.py:612

commit v20 on v19

--- a/solution.py
+++ b/solution.py
@@ -672,7 +672,7 @@
 
     kept, order = [], list(range(seq_count))
     if seq_count == 8:
-        late = [slot for slot, mask in enumerate(masks) if mask in (5, 6, 7)]
+        late = [slot for slot, mask in enumerate(masks) if mask in (6, 7)]
         order = [slot for slot in order if slot not in late]
         kept = attend_early(sizes, [received[slot] for slot in order], scale)
         order = order + late

time: 92.1 us -> 91.7 us (level)
  no operation moved by 1% of the time
where the time goes in v20:
time: 91.7 us; the launch traced here: 91.4 us
  blocking collectives  33.7 us (37%)
  waiting for transfers between devices  21.3 us (23%)
  starting transfers between devices  19.7 us (21%)
  Pallas kernels  15.3 us (17%)
  between operations  1.41 us (2%)
    all_to_all x3, blocking collectives, all_to_all(): lax.all_to_all(x, 'seq', split_axis=0, concat_axis=0, tiled=True, axis_in...  33.7 us
    ppermute x14, waiting for transfers between devices, swap(): return lax.ppermute(x, axis, [(i, i ^ mask) for i in range(count)])  21.3 us
    ppermute x14, starting transfers between devices, swap(): return lax.ppermute(x, axis, [(i, i ^ mask) for i in range(count)])  18.2 us
    pallas_call x1, Pallas kernels, attend(): pl.pallas_call(functools.partial(attend_kernel, sizes, masks, early), out...  3.83 us
    pallas_call x1, Pallas kernels, reward_head(): pl.pallas_call(functools.partial(head_kernel, grid_rows, fused, order, em...  3.33 us
    pallas_call x1, Pallas kernels, attend_early(): pl.pallas_call(functools.partial(early_kernel, sizes, count), out_shape=(...  1.84 us
  transfers between devices with their start and end apart: 15, of which 7 were waited for; matrix products, arithmetic and copies ran while one was open for 0% of the time, Pallas kernels for 9%

profile of v20, /device:TPU:0, one launch (start us, length us, event | category | flops | bytes accessed | tf_op | source)
XLA Modules:
  0.0 91.4 jit_solution(10645765498724593749)
XLA Ops:
  0.6 1.8 %shard_map.139 = (bf16[384,256]{1,0:T(8,128)(2,1)S(1)}, bf16[384,256]{1,0:T(8,128)(2,1)S(1)}, bf16[384,256]{1,0:T(8,128)(2,1)S(1)}, bf16[544,256]{1,0:T(8,128)(2...) custom-call(bf16[1,128,2048]{2,1,0:T(8,128)(2,1)} %q_ref.1, ...), custom_call_target="tpu_custom_call" | custom-call | bytes 3145728 | tf_op jit(solution)/shard_map/pallas_call | solution.py:125
  2.4 4.1 %collective-permute-start.3 = (bf16[544,256]{1,0:T(8,128)(2,1)S(1)}, bf16[544,256]{1,0:T(8,128)(2,1)S(1)}, u32[]{:S(2)}, u32[]{:S(2)}) collective-permute-start(bf16[544,256]{1,0:T(8,128)(2,1)S(1)} %get-tuple-element.31), channel_id=1, source_target_pairs={{0,16},{4,20},{8,24},{12,28},{16,0},{20,4},{24,8},{28,12},{1,17},{... | collective-permute-start | bytes 835592 | tf_op jit(solution)/shard_map/ppermute | solution.py:612
  6.5 1.5 %collective-permute-start = (bf16[384,256]{1,0:T(8,128)(2,1)S(1)}, bf16[384,256]{1,0:T(8,128)(2,1)S(1)}, u32[]{:S(2)}, u32[]{:S(2)}) collective-permute-start(bf16[384,256]{1,0:T(8,128)(2,1)S(1)} %get-tuple-element.28), channel_id=1, source_target_pairs={{0,4},{4,0},{8,12},{12,8},{16,20},{20,16},{24,28},{28,24},{1,5},{5... | collective-permute-start | bytes 589832 | tf_op jit(solution)/shard_map/ppermute | solution.py:612
  8.0 1.6 %collective-permute-start.1 = (bf16[384,256]{1,0:T(8,128)(2,1)S(1)}, bf16[384,256]{1,0:T(8,128)(2,1)S(1)}, u32[]{:S(2)}, u32[]{:S(2)}) collective-permute-start(bf16[384,256]{1,0:T(8,128)(2,1)S(1)} %get-tuple-element.29), channel_id=1, source_target_pairs={{0,8},{4,12},{8,0},{12,4},{16,24},{20,28},{24,16},{28,20},{1,9},{5... | collective-permute-start | bytes 589832 | tf_op jit(solution)/shard_map/ppermute | solution.py:612
  10.0 1.3 %collective-permute-start.4 = (bf16[384,256]{1,0:T(8,128)(2,1)S(1)}, bf16[384,256]{1,0:T(8,128)(2,1)S(1)}, u32[]{:S(2)}, u32[]{:S(2)}) collective-permute-start(bf16[384,256]{1,0:T(8,128)(2,1)S(1)} %get-tuple-element.32), channel_id=1, source_target_pairs={{0,20},{4,16},{8,28},{12,24},{16,4},{20,0},{24,12},{28,8},{1,21},{... | collective-permute-start | bytes 589832 | tf_op jit(solution)/shard_map/ppermute | solution.py:612
  11.3 2.2 %collective-permute-done.refs_0_ = bf16[384,256]{1,0:T(8,128)(2,1)S(1)} collective-permute-done((bf16[384,256]{1,0:T(8,128)(2,1)S(1)}, bf16[384,256]{1,0:T(8,128)(2,1)S(1)}, u32[]{:S(2)}, u32[]{:S(2)}) %collective-permute-start) | collective-permute-done | bytes 196640 | tf_op jit(solution)/shard_map/ppermute | solution.py:612
  13.5 1.4 %collective-permute-start.5 = (bf16[384,256]{1,0:T(8,128)(2,1)S(1)}, bf16[384,256]{1,0:T(8,128)(2,1)S(1)}, u32[]{:S(2)}, u32[]{:S(2)}) collective-permute-start(bf16[384,256]{1,0:T(8,128)(2,1)S(1)} %get-tuple-element.34), channel_id=1, source_target_pairs={{0,24},{4,28},{8,16},{12,20},{16,8},{20,12},{24,0},{28,4},{1,25},{... | collective-permute-start | bytes 589832 | tf_op jit(solution)/shard_map/ppermute | solution.py:612
  14.9 5.2 %collective-permute-done.3.refs_3_.refs_0_ = bf16[544,256]{1,0:T(8,128)(2,1)S(1)} collective-permute-done((bf16[544,256]{1,0:T(8,128)(2,1)S(1)}, bf16[544,256]{1,0:T(8,128)(2,1)S(1)}, u32[]{:S(2)}, u32[]{:S(2)}) %collective-permute-start.3) | collective-permute-done | bytes 278560 | tf_op jit(solution)/shard_map/ppermute | solution.py:612
  20.1 3.8 %collective-permute-start.6 = (bf16[384,256]{1,0:T(8,128)(2,1)S(1)}, bf16[384,256]{1,0:T(8,128)(2,1)S(1)}, u32[]{:S(2)}, u32[]{:S(2)}) collective-permute-start(bf16[384,256]{1,0:T(8,128)(2,1)S(1)} %get-tuple-element.35), channel_id=1, source_target_pairs={{0,28},{4,24},{8,20},{12,16},{16,12},{20,8},{24,4},{28,0},{1,29},{... | collective-permute-start | bytes 589832 | tf_op jit(solution)/shard_map/ppermute | solution.py:612
  24.9 1.6 %shard_map.140 = (f32[1,256]{1,0:T(1,128)S(1)}, f32[1,256]{1,0:T(1,128)S(1)}, bf16[64,256]{1,0:T(8,128)(2,1)S(1)}, bf16[64,1280]{1,0:T(8,128)(2,1)S(1)}, f32[128...) custom-call(s32[3]{0:T(128)S(1)} %pad_add_fusion.place_ref, f32[1]{0:T(128)S(6)} %copy.15.cot_ref, ...), custom_call_target="tpu_custom_call" | custom-call | flops 1 | bytes 1 | tf_op jit(solution)/shard_map/pallas_call | solution.py:237
  26.7 11.5 %collective-permute-done.4.refs_4_ = bf16[384,256]{1,0:T(8,128)(2,1)S(1)} collective-permute-done((bf16[384,256]{1,0:T(8,128)(2,1)S(1)}, bf16[384,256]{1,0:T(8,128)(2,1)S(1)}, u32[]{:S(2)}, u32[]{:S(2)}) %collective-permute-start.4) | collective-permute-done | bytes 196640 | tf_op jit(solution)/shard_map/ppermute | solution.py:612
  38.2 1.8 %shard_map.141 = (f32[6,2,128,128]{3,2,1,0:T(8,128)S(1)}, f32[6,2,128,128]{3,2,1,0:T(8,128)S(1)}) custom-call(bf16[384,256]{1,0:T(8,128)(2,1)S(1)} %collective-permute-done.refs_0_, bf16[384,256]{1,0:T(8,128)(2,1)S(1)} %collective-permute-done.1.refs_1_, bf16[384,256]{1,0:T(8,128)(2,1)S(1)} %collective-permute-done.2.refs_2_, ...), custom_call_target="tpu_custom_call" | custom-call | flops 1 | bytes 1 | tf_op jit(solution)/shard_map/pallas_call | solution.py:310
  40.3 1.8 %collective-permute-start.9 = (bf16[4,320,128]{2,1,0:T(8,128)(2,1)S(1)}, bf16[4,320,128]{2,1,0:T(8,128)(2,1)S(1)}, u32[]{:S(2)}, u32[]{:S(2)}) collective-permute-start(bf16[4,320,128]{2,1,0:T(8,128)(2,1)S(1)} %shard_map.145.refs_0_), channel_id=1, source_target_pairs={{0,2},{1,3},{2,0},{3,1},{4,6},{5,7},{6,4},{7,5},{8,10},{9,11},{10,... | collective-permute-start | bytes 983048 | tf_op jit(solution)/shard_map/ppermute | solution.py:612
  42.2 1.5 %collective-permute-start.10 = (bf16[4,320,128]{2,1,0:T(8,128)(2,1)S(1)}, bf16[4,320,128]{2,1,0:T(8,128)(2,1)S(1)}, u32[]{:S(2)}, u32[]{:S(2)}) collective-permute-start(bf16[4,320,128]{2,1,0:T(8,128)(2,1)S(1)} %shard_map.145.refs_0_), channel_id=1, source_target_pairs={{0,6},{1,7},{2,4},{3,5},{4,2},{5,3},{6,0},{7,1},{8,14},{9,15},{10,... | collective-permute-start | bytes 983048 | tf_op jit(solution)/shard_map/ppermute | solution.py:628
  43.7 3.8 %shard_map.142 = (bf16[8,128,256]{2,1,0:T(8,128)(2,1)S(1)}, bf16[8,64,128]{2,1,0:T(8,128)(2,1)S(1)}) custom-call(s32[3]{0:T(128)S(1)} %pad_add_fusion.place_ref, bf16[384,256]{1,0:T(8,128)(2,1)S(1)} %collective-permute-done.refs_0_, bf16[384,256]{1,0:T(8,128)(2,1)S(1)} %collective-permute-done.1.refs_1_, ...), custom_call_target="tpu_custom_call" | custom-call | flops 1073741824 | bytes 2097152 | tf_op jit(solution)/shard_map/pallas_call | solution.py:366
  47.5 12.8 %all_to_all.15.refs_0_ = bf16[8,64,128]{2,1,0:T(8,128)(2,1)S(1)} all-to-all(bf16[8,64,128]{2,1,0:T(8,128)(2,1)S(1)} %get-tuple-element.41), channel_id=1, replica_groups={{16,20,8,12,24,28,0,4},{17,21,9,13,25,29,1,5},{18,22,10,14,26,30,2,6},{..., dimensions={0} | all-to-all | bytes 262144 | tf_op jit(solution)/shard_map/all_to_all | solution.py:616
  60.4 0.8 shard_map.146.refs_0_
  61.3 9.4 %all_to_all.16 = bf16[8,64,128]{2,1,0:T(8,128)(2,1)S(1)} all-to-all(bf16[8,64,128]{2,1,0:T(8,128)(2,1)S(1)} %shard_map.143.refs_4_), channel_id=1, replica_groups={{16,20,8,12,24,28,0,4},{17,21,9,13,25,29,1,5},{18,22,10,14,26,30,2,6},{..., dimensions={0} | all-to-all | bytes 262144 | tf_op jit(solution)/shard_map/all_to_all | solution.py:616
  70.7 3.3 %shard_map.147 = (f32[1,128]{1,0:T(1,128)}, bf16[512,128]{1,0:T(8,128)(2,1)S(1)}, bf16[64,256]{1,0:T(8,128)(2,1)S(1)}) custom-call(s32[3]{0:T(128)S(1)} %pad_add_fusion.place_ref, bf16[512,128]{1,0:T(8,128)(2,1)S(1)} %bitcast.7, bf16[2,256,1280]{2,1,0:T(8,128)(2,1)S(1)} %shard_map.146.refs_0_, bf16[2,256,1280]{2,1,0:T(8,128)(2,1)S(1)} %collective-permute-done.11.refs_1_, ...), custom_call_target="tpu_custom_call" | custom-call | flops 503316480 | bytes 2785280 | tf_op jit(solution)/shard_map/pallas_call | solution.py:520
  74.1 1.6 %collective-permute-start.13 = (bf16[64,256]{1,0:T(8,128)(2,1)S(1)}, bf16[64,256]{1,0:T(8,128)(2,1)S(1)}, u32[]{:S(2)}, u32[]{:S(2)}) collective-permute-start(bf16[64,256]{1,0:T(8,128)(2,1)S(1)} %get-tuple-element.51.refs_0_), channel_id=1, source_target_pairs={{0,2},{1,3},{2,0},{3,1},{4,6},{5,7},{6,4},{7,5},{8,10},{9,11},{10,... | collective-permute-start | bytes 98312 | tf_op jit(solution)/shard_map/ppermute | solution.py:612
  76.0 1.1 %shard_map.148 = (bf16[1,2,1024,128]{3,2,1,0:T(8,128)(2,1)}, f32[8,128]{1,0:T(8,128)S(1)}) custom-call(bf16[512,128]{1,0:T(8,128)(2,1)S(1)} %get-tuple-element.49.grad_ref, f32[1,256]{1,0:T(1,128)S(1)} %get-tuple-element.36.refs_6_.refs_10_.scale_ref, bf16[64,256]{1,0:T(8,128)(2,1)S(1)} %get-tuple-element.40.refs_12_.proj_ref), custom_call_target="tpu_custom_call" | custom-call | flops 67108864 | bytes 524288 | tf_op jit(solution)/shard_map/pallas_call | solution.py:563
  77.1 1.0 %collective-permute-done.13.refs_2_ = bf16[64,256]{1,0:T(8,128)(2,1)S(1)} collective-permute-done((bf16[64,256]{1,0:T(8,128)(2,1)S(1)}, bf16[64,256]{1,0:T(8,128)(2,1)S(1)}, u32[]{:S(2)}, u32[]{:S(2)}) %collective-permute-start.13) | collective-permute-done | bytes 32800 | tf_op jit(solution)/shard_map/ppermute | solution.py:612
  78.1 0.9 %collective-permute-done.14.refs_3_ = bf16[64,256]{1,0:T(8,128)(2,1)S(1)} collective-permute-done((bf16[64,256]{1,0:T(8,128)(2,1)S(1)}, bf16[64,256]{1,0:T(8,128)(2,1)S(1)}, u32[]{:S(2)}, u32[]{:S(2)}) %collective-permute-start.14) | collective-permute-done | bytes 32800 | tf_op jit(solution)/shard_map/ppermute | solution.py:612
  79.1 11.5 %all_to_all.17.in_ref = bf16[8,64,256]{2,1,0:T(8,128)(2,1)S(1)} all-to-all(bf16[8,64,256]{2,1,0:T(8,128)(2,1)S(1)} %shard_map.149), channel_id=1, replica_groups={{16,20,8,12,24,28,0,4},{17,21,9,13,25,29,1,5},{18,22,10,14,26,30,2,6},{..., dimensions={0} | all-to-all | bytes 524288 | tf_op jit(solution)/shard_map/all_to_all | solution.py:616
  (22 shorter events, 2.6 us)
Async XLA Ops:
  2.4 17.7 %collective-permute-start.3 = (bf16[544,256]{1,0:T(8,128)(2,1)S(1)}, bf16[544,256]{1,0:T(8,128)(2,1)S(1)}, u32[]{:S(2)}, u32[]{:S(2)}) collective-permute-start(bf16[544,256]{1,0:T(8,128)(2,1)S(1)} %get-tuple-element.31), channel_id=1, source_target_pairs={{0,16},{4,20},{8,24},{12,28},{16,0},{20,4},{24,8},{28,12},{1,17},{... | collective-permute-start | bytes 835592 | tf_op jit(solution)/shard_map/ppermute | solution.py:612
  6.5 6.9 %collective-permute-start = (bf16[384,256]{1,0:T(8,128)(2,1)S(1)}, bf16[384,256]{1,0:T(8,128)(2,1)S(1)}, u32[]{:S(2)}, u32[]{:S(2)}) collective-permute-start(bf16[384,256]{1,0:T(8,128)(2,1)S(1)} %get-tuple-element.28), channel_id=1, source_target_pairs={{0,4},{4,0},{8,12},{12,8},{16,20},{20,16},{24,28},{28,24},{1,5},{5... | collective-permute-start | bytes 589832 | tf_op jit(solution)/shard_map/ppermute | solution.py:612
  8.0 16.1 %collective-permute-start.1 = (bf16[384,256]{1,0:T(8,128)(2,1)S(1)}, bf16[384,256]{1,0:T(8,128)(2,1)S(1)}, u32[]{:S(2)}, u32[]{:S(2)}) collective-permute-start(bf16[384,256]{1,0:T(8,128)(2,1)S(1)} %get-tuple-element.29), channel_id=1, source_target_pairs={{0,8},{4,12},{8,0},{12,4},{16,24},{20,28},{24,16},{28,20},{1,9},{5... | collective-permute-start | bytes 589832 | tf_op jit(solution)/shard_map/ppermute | solution.py:612
  9.6 17.1 %collective-permute-start.2 = (bf16[384,256]{1,0:T(8,128)(2,1)S(1)}, bf16[384,256]{1,0:T(8,128)(2,1)S(1)}, u32[]{:S(2)}, u32[]{:S(2)}) collective-permute-start(bf16[384,256]{1,0:T(8,128)(2,1)S(1)} %get-tuple-element.30), channel_id=1, source_target_pairs={{0,12},{4,8},{8,4},{12,0},{16,28},{20,24},{24,20},{28,16},{1,13},{... | collective-permute-start | bytes 589832 | tf_op jit(solution)/shard_map/ppermute | solution.py:612
  10.0 28.2 %collective-permute-start.4 = (bf16[384,256]{1,0:T(8,128)(2,1)S(1)}, bf16[384,256]{1,0:T(8,128)(2,1)S(1)}, u32[]{:S(2)}, u32[]{:S(2)}) collective-permute-start(bf16[384,256]{1,0:T(8,128)(2,1)S(1)} %get-tuple-element.32), channel_id=1, source_target_pairs={{0,20},{4,16},{8,28},{12,24},{16,4},{20,0},{24,12},{28,8},{1,21},{... | collective-permute-start | bytes 589832 | tf_op jit(solution)/shard_map/ppermute | solution.py:612
  13.5 30.2 %collective-permute-start.5 = (bf16[384,256]{1,0:T(8,128)(2,1)S(1)}, bf16[384,256]{1,0:T(8,128)(2,1)S(1)}, u32[]{:S(2)}, u32[]{:S(2)}) collective-permute-start(bf16[384,256]{1,0:T(8,128)(2,1)S(1)} %get-tuple-element.34), channel_id=1, source_target_pairs={{0,24},{4,28},{8,16},{12,20},{16,8},{20,12},{24,0},{28,4},{1,25},{... | collective-permute-start | bytes 589832 | tf_op jit(solution)/shard_map/ppermute | solution.py:612
  20.1 23.6 %collective-permute-start.6 = (bf16[384,256]{1,0:T(8,128)(2,1)S(1)}, bf16[384,256]{1,0:T(8,128)(2,1)S(1)}, u32[]{:S(2)}, u32[]{:S(2)}) collective-permute-start(bf16[384,256]{1,0:T(8,128)(2,1)S(1)} %get-tuple-element.35), channel_id=1, source_target_pairs={{0,28},{4,24},{8,20},{12,16},{16,12},{20,8},{24,4},{28,0},{1,29},{... | collective-permute-start | bytes 589832 | tf_op jit(solution)/shard_map/ppermute | solution.py:612
  24.2 15.9 %collective-permute-start.7 = (bf16[2,320,128]{2,1,0:T(8,128)(2,1)S(1)}, bf16[2,320,128]{2,1,0:T(8,128)(2,1)S(1)}, u32[]{:S(2)}, u32[]{:S(2)}) collective-permute-start(bf16[2,320,128]{2,1,0:T(8,128)(2,1)S(1)} %shard_map.144.first_ref), channel_id=1, source_target_pairs={{0,8},{4,12},{8,0},{12,4},{16,24},{20,28},{24,16},{28,20},{1,9},{5... | collective-permute-start | bytes 491528 | tf_op jit(solution)/shard_map/ppermute | solution.py:612
  40.1 20.2 %collective-permute-start.8 = (bf16[4,320,128]{2,1,0:T(8,128)(2,1)S(1)}, bf16[4,320,128]{2,1,0:T(8,128)(2,1)S(1)}, u32[]{:S(2)}, u32[]{:S(2)}) collective-permute-start(bf16[4,320,128]{2,1,0:T(8,128)(2,1)S(1)} %shard_map.145.refs_0_), channel_id=1, source_target_pairs={{0,4},{4,0},{8,12},{12,8},{16,20},{20,16},{24,28},{28,24},{1,5},{5... | collective-permute-start | bytes 983048 | tf_op jit(solution)/shard_map/ppermute | solution.py:612
  40.3 20.0 %collective-permute-start.9 = (bf16[4,320,128]{2,1,0:T(8,128)(2,1)S(1)}, bf16[4,320,128]{2,1,0:T(8,128)(2,1)S(1)}, u32[]{:S(2)}, u32[]{:S(2)}) collective-permute-start(bf16[4,320,128]{2,1,0:T(8,128)(2,1)S(1)} %shard_map.145.refs_0_), channel_id=1, source_target_pairs={{0,2},{1,3},{2,0},{3,1},{4,6},{5,7},{6,4},{7,5},{8,10},{9,11},{10,... | collective-permute-start | bytes 983048 | tf_op jit(solution)/shard_map/ppermute | solution.py:612
  42.2 18.2 %collective-permute-start.10 = (bf16[4,320,128]{2,1,0:T(8,128)(2,1)S(1)}, bf16[4,320,128]{2,1,0:T(8,128)(2,1)S(1)}, u32[]{:S(2)}, u32[]{:S(2)}) collective-permute-start(bf16[4,320,128]{2,1,0:T(8,128)(2,1)S(1)} %shard_map.145.refs_0_), channel_id=1, source_target_pairs={{0,6},{1,7},{2,4},{3,5},{4,2},{5,3},{6,0},{7,1},{8,14},{9,15},{10,... | collective-permute-start | bytes 983048 | tf_op jit(solution)/shard_map/ppermute | solution.py:628
  61.2 9.5 %collective-permute-start.11 = (bf16[2,256,1280]{2,1,0:T(8,128)(2,1)S(1)}, bf16[2,256,1280]{2,1,0:T(8,128)(2,1)S(1)}, u32[]{:S(2)}, u32[]{:S(2)}) collective-permute-start(bf16[2,256,1280]{2,1,0:T(8,128)(2,1)S(1)} %shard_map.146.refs_0_), channel_id=1, source_target_pairs={{0,1},{1,0},{2,3},{3,2},{4,5},{5,4},{6,7},{7,6},{8,9},{9,8},{10,11... | collective-permute-start | bytes 3932168 | tf_op jit(solution)/shard_map/ppermute | solution.py:612
  74.0 3.0 %collective-permute-start.12 = (bf16[64,256]{1,0:T(8,128)(2,1)S(1)}, bf16[64,256]{1,0:T(8,128)(2,1)S(1)}, u32[]{:S(2)}, u32[]{:S(2)}) collective-permute-start(bf16[64,256]{1,0:T(8,128)(2,1)S(1)} %get-tuple-element.51.refs_0_), channel_id=1, source_target_pairs={{0,1},{1,0},{2,3},{3,2},{4,5},{5,4},{6,7},{7,6},{8,9},{9,8},{10,11... | collective-permute-start | bytes 98312 | tf_op jit(solution)/shard_map/ppermute | solution.py:612
  74.1 4.0 %collective-permute-start.13 = (bf16[64,256]{1,0:T(8,128)(2,1)S(1)}, bf16[64,256]{1,0:T(8,128)(2,1)S(1)}, u32[]{:S(2)}, u32[]{:S(2)}) collective-permute-start(bf16[64,256]{1,0:T(8,128)(2,1)S(1)} %get-tuple-element.51.refs_0_), channel_id=1, source_target_pairs={{0,2},{1,3},{2,0},{3,1},{4,6},{5,7},{6,4},{7,5},{8,10},{9,11},{10,... | collective-permute-start | bytes 98312 | tf_op jit(solution)/shard_map/ppermute | solution.py:612
  75.7 3.3 %collective-permute-start.14 = (bf16[64,256]{1,0:T(8,128)(2,1)S(1)}, bf16[64,256]{1,0:T(8,128)(2,1)S(1)}, u32[]{:S(2)}, u32[]{:S(2)}) collective-permute-start(bf16[64,256]{1,0:T(8,128)(2,1)S(1)} %get-tuple-element.51.refs_0_), channel_id=1, source_target_pairs={{0,3},{1,2},{2,1},{3,0},{4,7},{5,6},{6,5},{7,4},{8,11},{9,10},{10,... | collective-permute-start | bytes 98312 | tf_op jit(solution)/shard_map/ppermute | solution.py:612

commit v21 on v20

--- a/solution.py
+++ b/solution.py
@@ -330,25 +330,25 @@
     gain = 1.0 + scale_ref[...]
     shift = shift_ref[...]
     load_pieces(sizes, in_refs, key_scr, value_scr)
-    together = 2
-    for first in range(0, count, together):
-        results = []
-        for src in range(first, first + together):
-            mixed = []
-            for head in range(heads):
-                before = None
-                rows = pl.ds(0, count * tok_rows)
-                if src < early:
-                    rows = pl.ds(early * tok_rows, (count - early) * tok_rows)
-                    stat = kept_refs[1][src, head]
-                    before = (kept_refs[0][src, head], stat[:, HD - 1 :], stat[:, :1])
-                query = in_refs[src][pl.ds(0, part_rows), pl.ds(head * HD, HD)]
-                value, total, _ = soft_part(query, key_scr, value_scr, rows, head, before)
-                mixed.append(value / total)
-            results.append(jnp.concatenate(mixed, axis=1) if heads > 1 else mixed[0])
-        for at, attended in enumerate(results):
-            modulated = (attended * gain + shift).astype(BF16)
-            mod_ref[jnp.bitwise_xor(me, masks[first + at])] = modulated
+    groups = [range(early), range(early, count)] if early else [[src] for src in range(count)]
+    for group in groups:
+        mixed = []
+        for head in range(heads):
+            before = None
+            rows = pl.ds(0, count * tok_rows)
+            if group[0] < early:
+                rows = pl.ds(early * tok_rows, (count - early) * tok_rows)
+                sums = kept_refs[0][:, head].reshape(early * part_rows, HD)
+                stat = kept_refs[1][:, head].reshape(early * part_rows, HD)
+                before = (sums, stat[:, HD - 1 :], stat[:, :1])
+            cols = pl.ds(head * HD, HD)
+            query = jnp.concatenate([in_refs[src][pl.ds(0, part_rows), cols] for src in group], axis=0)
+            value, total, _ = soft_part(query, key_scr, value_scr, rows, head, before)
+            mixed.append(value / total)
+        attended = jnp.concatenate(mixed, axis=1) if heads > 1 else mixed[0]
+        modulated = (attended * gain + shift).astype(BF16)
+        for at, src in enumerate(group):
+            mod_ref[jnp.bitwise_xor(me, masks[src])] = modulated[at * part_rows : (at + 1) * part_rows]
     sides = [
         mm_nt(mod_ref[:, rows, :].reshape(count * half, width), proj_ref[...])
         for rows in (slice(0, half), slice(half, part_rows))

time: 91.7 us -> 91.5 us (level)
  no operation moved by 1% of the time
where the time goes in v21:
time: 91.5 us; the launch traced here: 91.2 us
  blocking collectives  33.7 us (37%)
  waiting for transfers between devices  21.3 us (23%)
  starting transfers between devices  19.7 us (22%)
  Pallas kernels  15 us (16%)
  between operations  1.41 us (2%)
    all_to_all x3, blocking collectives, all_to_all(): lax.all_to_all(x, 'seq', split_axis=0, concat_axis=0, tiled=True, axis_in...  33.7 us
    ppermute x14, waiting for transfers between devices, swap(): return lax.ppermute(x, axis, [(i, i ^ mask) for i in range(count)])  21.3 us
    ppermute x14, starting transfers between devices, swap(): return lax.ppermute(x, axis, [(i, i ^ mask) for i in range(count)])  18.2 us
    pallas_call x1, Pallas kernels, attend(): pl.pallas_call(functools.partial(attend_kernel, sizes, masks, early), out...  3.58 us
    pallas_call x1, Pallas kernels, reward_head(): pl.pallas_call(functools.partial(head_kernel, grid_rows, fused, order, em...  3.33 us
    pallas_call x1, Pallas kernels, attend_early(): pl.pallas_call(functools.partial(early_kernel, sizes, count), out_shape=(...  1.84 us
  transfers between devices with their start and end apart: 15, of which 7 were waited for; matrix products, arithmetic and copies ran while one was open for 0% of the time, Pallas kernels for 9%

profile of v21, /device:TPU:0, one launch (start us, length us, event | category | flops | bytes accessed | tf_op | source)
XLA Modules:
  0.0 91.2 jit_solution(5852938785181061660)
XLA Ops:
  0.6 1.8 %shard_map.139 = (bf16[384,256]{1,0:T(8,128)(2,1)S(1)}, bf16[384,256]{1,0:T(8,128)(2,1)S(1)}, bf16[384,256]{1,0:T(8,128)(2,1)S(1)}, bf16[544,256]{1,0:T(8,128)(2...) custom-call(bf16[1,128,2048]{2,1,0:T(8,128)(2,1)} %q_ref.1, ...), custom_call_target="tpu_custom_call" | custom-call | bytes 3145728 | tf_op jit(solution)/shard_map/pallas_call | solution.py:125
  2.4 4.1 %collective-permute-start.3 = (bf16[544,256]{1,0:T(8,128)(2,1)S(1)}, bf16[544,256]{1,0:T(8,128)(2,1)S(1)}, u32[]{:S(2)}, u32[]{:S(2)}) collective-permute-start(bf16[544,256]{1,0:T(8,128)(2,1)S(1)} %get-tuple-element.31), channel_id=1, source_target_pairs={{0,16},{4,20},{8,24},{12,28},{16,0},{20,4},{24,8},{28,12},{1,17},{... | collective-permute-start | bytes 835592 | tf_op jit(solution)/shard_map/ppermute | solution.py:612
  6.5 1.5 %collective-permute-start = (bf16[384,256]{1,0:T(8,128)(2,1)S(1)}, bf16[384,256]{1,0:T(8,128)(2,1)S(1)}, u32[]{:S(2)}, u32[]{:S(2)}) collective-permute-start(bf16[384,256]{1,0:T(8,128)(2,1)S(1)} %get-tuple-element.28), channel_id=1, source_target_pairs={{0,4},{4,0},{8,12},{12,8},{16,20},{20,16},{24,28},{28,24},{1,5},{5... | collective-permute-start | bytes 589832 | tf_op jit(solution)/shard_map/ppermute | solution.py:612
  8.0 1.6 %collective-permute-start.1 = (bf16[384,256]{1,0:T(8,128)(2,1)S(1)}, bf16[384,256]{1,0:T(8,128)(2,1)S(1)}, u32[]{:S(2)}, u32[]{:S(2)}) collective-permute-start(bf16[384,256]{1,0:T(8,128)(2,1)S(1)} %get-tuple-element.29), channel_id=1, source_target_pairs={{0,8},{4,12},{8,0},{12,4},{16,24},{20,28},{24,16},{28,20},{1,9},{5... | collective-permute-start | bytes 589832 | tf_op jit(solution)/shard_map/ppermute | solution.py:612
  10.0 1.3 %collective-permute-start.4 = (bf16[384,256]{1,0:T(8,128)(2,1)S(1)}, bf16[384,256]{1,0:T(8,128)(2,1)S(1)}, u32[]{:S(2)}, u32[]{:S(2)}) collective-permute-start(bf16[384,256]{1,0:T(8,128)(2,1)S(1)} %get-tuple-element.32), channel_id=1, source_target_pairs={{0,20},{4,16},{8,28},{12,24},{16,4},{20,0},{24,12},{28,8},{1,21},{... | collective-permute-start | bytes 589832 | tf_op jit(solution)/shard_map/ppermute | solution.py:612
  11.3 2.2 %collective-permute-done.refs_0_ = bf16[384,256]{1,0:T(8,128)(2,1)S(1)} collective-permute-done((bf16[384,256]{1,0:T(8,128)(2,1)S(1)}, bf16[384,256]{1,0:T(8,128)(2,1)S(1)}, u32[]{:S(2)}, u32[]{:S(2)}) %collective-permute-start) | collective-permute-done | bytes 196640 | tf_op jit(solution)/shard_map/ppermute | solution.py:612
  13.5 1.4 %collective-permute-start.5 = (bf16[384,256]{1,0:T(8,128)(2,1)S(1)}, bf16[384,256]{1,0:T(8,128)(2,1)S(1)}, u32[]{:S(2)}, u32[]{:S(2)}) collective-permute-start(bf16[384,256]{1,0:T(8,128)(2,1)S(1)} %get-tuple-element.34), channel_id=1, source_target_pairs={{0,24},{4,28},{8,16},{12,20},{16,8},{20,12},{24,0},{28,4},{1,25},{... | collective-permute-start | bytes 589832 | tf_op jit(solution)/shard_map/ppermute | solution.py:612
  14.9 5.2 %collective-permute-done.3.refs_3_.refs_0_ = bf16[544,256]{1,0:T(8,128)(2,1)S(1)} collective-permute-done((bf16[544,256]{1,0:T(8,128)(2,1)S(1)}, bf16[544,256]{1,0:T(8,128)(2,1)S(1)}, u32[]{:S(2)}, u32[]{:S(2)}) %collective-permute-start.3) | collective-permute-done | bytes 278560 | tf_op jit(solution)/shard_map/ppermute | solution.py:612
  20.1 3.8 %collective-permute-start.6 = (bf16[384,256]{1,0:T(8,128)(2,1)S(1)}, bf16[384,256]{1,0:T(8,128)(2,1)S(1)}, u32[]{:S(2)}, u32[]{:S(2)}) collective-permute-start(bf16[384,256]{1,0:T(8,128)(2,1)S(1)} %get-tuple-element.35), channel_id=1, source_target_pairs={{0,28},{4,24},{8,20},{12,16},{16,12},{20,8},{24,4},{28,0},{1,29},{... | collective-permute-start | bytes 589832 | tf_op jit(solution)/shard_map/ppermute | solution.py:612
  24.9 1.6 %shard_map.140 = (f32[1,256]{1,0:T(1,128)S(1)}, f32[1,256]{1,0:T(1,128)S(1)}, bf16[64,256]{1,0:T(8,128)(2,1)S(1)}, bf16[64,1280]{1,0:T(8,128)(2,1)S(1)}, f32[128...) custom-call(s32[3]{0:T(128)S(1)} %pad_add_fusion.place_ref, f32[1]{0:T(128)S(6)} %copy.15.cot_ref, ...), custom_call_target="tpu_custom_call" | custom-call | flops 1 | bytes 1 | tf_op jit(solution)/shard_map/pallas_call | solution.py:237
  26.7 11.5 %collective-permute-done.4.refs_4_ = bf16[384,256]{1,0:T(8,128)(2,1)S(1)} collective-permute-done((bf16[384,256]{1,0:T(8,128)(2,1)S(1)}, bf16[384,256]{1,0:T(8,128)(2,1)S(1)}, u32[]{:S(2)}, u32[]{:S(2)}) %collective-permute-start.4) | collective-permute-done | bytes 196640 | tf_op jit(solution)/shard_map/ppermute | solution.py:612
  38.2 1.8 %shard_map.141 = (f32[6,2,128,128]{3,2,1,0:T(8,128)S(1)}, f32[6,2,128,128]{3,2,1,0:T(8,128)S(1)}) custom-call(bf16[384,256]{1,0:T(8,128)(2,1)S(1)} %collective-permute-done.refs_0_, bf16[384,256]{1,0:T(8,128)(2,1)S(1)} %collective-permute-done.1.refs_1_, bf16[384,256]{1,0:T(8,128)(2,1)S(1)} %collective-permute-done.2.refs_2_, ...), custom_call_target="tpu_custom_call" | custom-call | flops 1 | bytes 1 | tf_op jit(solution)/shard_map/pallas_call | solution.py:310
  40.3 1.8 %collective-permute-start.9 = (bf16[4,320,128]{2,1,0:T(8,128)(2,1)S(1)}, bf16[4,320,128]{2,1,0:T(8,128)(2,1)S(1)}, u32[]{:S(2)}, u32[]{:S(2)}) collective-permute-start(bf16[4,320,128]{2,1,0:T(8,128)(2,1)S(1)} %shard_map.145.refs_0_), channel_id=1, source_target_pairs={{0,2},{1,3},{2,0},{3,1},{4,6},{5,7},{6,4},{7,5},{8,10},{9,11},{10,... | collective-permute-start | bytes 983048 | tf_op jit(solution)/shard_map/ppermute | solution.py:612
  42.2 1.5 %collective-permute-start.10 = (bf16[4,320,128]{2,1,0:T(8,128)(2,1)S(1)}, bf16[4,320,128]{2,1,0:T(8,128)(2,1)S(1)}, u32[]{:S(2)}, u32[]{:S(2)}) collective-permute-start(bf16[4,320,128]{2,1,0:T(8,128)(2,1)S(1)} %shard_map.145.refs_0_), channel_id=1, source_target_pairs={{0,6},{1,7},{2,4},{3,5},{4,2},{5,3},{6,0},{7,1},{8,14},{9,15},{10,... | collective-permute-start | bytes 983048 | tf_op jit(solution)/shard_map/ppermute | solution.py:628
  43.7 3.6 %shard_map.142 = (bf16[8,128,256]{2,1,0:T(8,128)(2,1)S(1)}, bf16[8,64,128]{2,1,0:T(8,128)(2,1)S(1)}) custom-call(s32[3]{0:T(128)S(1)} %pad_add_fusion.place_ref, bf16[384,256]{1,0:T(8,128)(2,1)S(1)} %collective-permute-done.refs_0_, bf16[384,256]{1,0:T(8,128)(2,1)S(1)} %collective-permute-done.1.refs_1_, ...), custom_call_target="tpu_custom_call" | custom-call | flops 1073741824 | bytes 2097152 | tf_op jit(solution)/shard_map/pallas_call | solution.py:366
  47.3 12.8 %all_to_all.15.refs_0_ = bf16[8,64,128]{2,1,0:T(8,128)(2,1)S(1)} all-to-all(bf16[8,64,128]{2,1,0:T(8,128)(2,1)S(1)} %get-tuple-element.41), channel_id=1, replica_groups={{16,20,8,12,24,28,0,4},{17,21,9,13,25,29,1,5},{18,22,10,14,26,30,2,6},{..., dimensions={0} | all-to-all | bytes 262144 | tf_op jit(solution)/shard_map/all_to_all | solution.py:616
  60.1 0.8 shard_map.146.refs_0_
  61.0 9.4 %all_to_all.16 = bf16[8,64,128]{2,1,0:T(8,128)(2,1)S(1)} all-to-all(bf16[8,64,128]{2,1,0:T(8,128)(2,1)S(1)} %shard_map.143.refs_4_), channel_id=1, replica_groups={{16,20,8,12,24,28,0,4},{17,21,9,13,25,29,1,5},{18,22,10,14,26,30,2,6},{..., dimensions={0} | all-to-all | bytes 262144 | tf_op jit(solution)/shard_map/all_to_all | solution.py:616
  70.5 3.3 %shard_map.147 = (f32[1,128]{1,0:T(1,128)}, bf16[512,128]{1,0:T(8,128)(2,1)S(1)}, bf16[64,256]{1,0:T(8,128)(2,1)S(1)}) custom-call(s32[3]{0:T(128)S(1)} %pad_add_fusion.place_ref, bf16[512,128]{1,0:T(8,128)(2,1)S(1)} %bitcast.7, bf16[2,256,1280]{2,1,0:T(8,128)(2,1)S(1)} %shard_map.146.refs_0_, bf16[2,256,1280]{2,1,0:T(8,128)(2,1)S(1)} %collective-permute-done.11.refs_1_, ...), custom_call_target="tpu_custom_call" | custom-call | flops 503316480 | bytes 2785280 | tf_op jit(solution)/shard_map/pallas_call | solution.py:520
  73.9 1.6 %collective-permute-start.13 = (bf16[64,256]{1,0:T(8,128)(2,1)S(1)}, bf16[64,256]{1,0:T(8,128)(2,1)S(1)}, u32[]{:S(2)}, u32[]{:S(2)}) collective-permute-start(bf16[64,256]{1,0:T(8,128)(2,1)S(1)} %get-tuple-element.51.refs_0_), channel_id=1, source_target_pairs={{0,2},{1,3},{2,0},{3,1},{4,6},{5,7},{6,4},{7,5},{8,10},{9,11},{10,... | collective-permute-start | bytes 98312 | tf_op jit(solution)/shard_map/ppermute | solution.py:612
  75.7 1.1 %shard_map.148 = (bf16[1,2,1024,128]{3,2,1,0:T(8,128)(2,1)}, f32[8,128]{1,0:T(8,128)S(1)}) custom-call(bf16[512,128]{1,0:T(8,128)(2,1)S(1)} %get-tuple-element.49.grad_ref, f32[1,256]{1,0:T(1,128)S(1)} %get-tuple-element.36.refs_6_.refs_10_.scale_ref, bf16[64,256]{1,0:T(8,128)(2,1)S(1)} %get-tuple-element.40.refs_12_.proj_ref), custom_call_target="tpu_custom_call" | custom-call | flops 67108864 | bytes 524288 | tf_op jit(solution)/shard_map/pallas_call | solution.py:563
  76.8 1.0 %collective-permute-done.13.refs_2_ = bf16[64,256]{1,0:T(8,128)(2,1)S(1)} collective-permute-done((bf16[64,256]{1,0:T(8,128)(2,1)S(1)}, bf16[64,256]{1,0:T(8,128)(2,1)S(1)}, u32[]{:S(2)}, u32[]{:S(2)}) %collective-permute-start.13) | collective-permute-done | bytes 32800 | tf_op jit(solution)/shard_map/ppermute | solution.py:612
  77.9 0.9 %collective-permute-done.14.refs_3_ = bf16[64,256]{1,0:T(8,128)(2,1)S(1)} collective-permute-done((bf16[64,256]{1,0:T(8,128)(2,1)S(1)}, bf16[64,256]{1,0:T(8,128)(2,1)S(1)}, u32[]{:S(2)}, u32[]{:S(2)}) %collective-permute-start.14) | collective-permute-done | bytes 32800 | tf_op jit(solution)/shard_map/ppermute | solution.py:612
  78.8 11.5 %all_to_all.17.in_ref = bf16[8,64,256]{2,1,0:T(8,128)(2,1)S(1)} all-to-all(bf16[8,64,256]{2,1,0:T(8,128)(2,1)S(1)} %shard_map.149), channel_id=1, replica_groups={{16,20,8,12,24,28,0,4},{17,21,9,13,25,29,1,5},{18,22,10,14,26,30,2,6},{..., dimensions={0} | all-to-all | bytes 524288 | tf_op jit(solution)/shard_map/all_to_all | solution.py:616
  (22 shorter events, 2.6 us)
Async XLA Ops:
  2.4 17.7 %collective-permute-start.3 = (bf16[544,256]{1,0:T(8,128)(2,1)S(1)}, bf16[544,256]{1,0:T(8,128)(2,1)S(1)}, u32[]{:S(2)}, u32[]{:S(2)}) collective-permute-start(bf16[544,256]{1,0:T(8,128)(2,1)S(1)} %get-tuple-element.31), channel_id=1, source_target_pairs={{0,16},{4,20},{8,24},{12,28},{16,0},{20,4},{24,8},{28,12},{1,17},{... | collective-permute-start | bytes 835592 | tf_op jit(solution)/shard_map/ppermute | solution.py:612
  6.5 6.9 %collective-permute-start = (bf16[384,256]{1,0:T(8,128)(2,1)S(1)}, bf16[384,256]{1,0:T(8,128)(2,1)S(1)}, u32[]{:S(2)}, u32[]{:S(2)}) collective-permute-start(bf16[384,256]{1,0:T(8,128)(2,1)S(1)} %get-tuple-element.28), channel_id=1, source_target_pairs={{0,4},{4,0},{8,12},{12,8},{16,20},{20,16},{24,28},{28,24},{1,5},{5... | collective-permute-start | bytes 589832 | tf_op jit(solution)/shard_map/ppermute | solution.py:612
  8.0 16.1 %collective-permute-start.1 = (bf16[384,256]{1,0:T(8,128)(2,1)S(1)}, bf16[384,256]{1,0:T(8,128)(2,1)S(1)}, u32[]{:S(2)}, u32[]{:S(2)}) collective-permute-start(bf16[384,256]{1,0:T(8,128)(2,1)S(1)} %get-tuple-element.29), channel_id=1, source_target_pairs={{0,8},{4,12},{8,0},{12,4},{16,24},{20,28},{24,16},{28,20},{1,9},{5... | collective-permute-start | bytes 589832 | tf_op jit(solution)/shard_map/ppermute | solution.py:612
  9.6 17.1 %collective-permute-start.2 = (bf16[384,256]{1,0:T(8,128)(2,1)S(1)}, bf16[384,256]{1,0:T(8,128)(2,1)S(1)}, u32[]{:S(2)}, u32[]{:S(2)}) collective-permute-start(bf16[384,256]{1,0:T(8,128)(2,1)S(1)} %get-tuple-element.30), channel_id=1, source_target_pairs={{0,12},{4,8},{8,4},{12,0},{16,28},{20,24},{24,20},{28,16},{1,13},{... | collective-permute-start | bytes 589832 | tf_op jit(solution)/shard_map/ppermute | solution.py:612
  10.0 28.2 %collective-permute-start.4 = (bf16[384,256]{1,0:T(8,128)(2,1)S(1)}, bf16[384,256]{1,0:T(8,128)(2,1)S(1)}, u32[]{:S(2)}, u32[]{:S(2)}) collective-permute-start(bf16[384,256]{1,0:T(8,128)(2,1)S(1)} %get-tuple-element.32), channel_id=1, source_target_pairs={{0,20},{4,16},{8,28},{12,24},{16,4},{20,0},{24,12},{28,8},{1,21},{... | collective-permute-start | bytes 589832 | tf_op jit(solution)/shard_map/ppermute | solution.py:612
  13.5 30.2 %collective-permute-start.5 = (bf16[384,256]{1,0:T(8,128)(2,1)S(1)}, bf16[384,256]{1,0:T(8,128)(2,1)S(1)}, u32[]{:S(2)}, u32[]{:S(2)}) collective-permute-start(bf16[384,256]{1,0:T(8,128)(2,1)S(1)} %get-tuple-element.34), channel_id=1, source_target_pairs={{0,24},{4,28},{8,16},{12,20},{16,8},{20,12},{24,0},{28,4},{1,25},{... | collective-permute-start | bytes 589832 | tf_op jit(solution)/shard_map/ppermute | solution.py:612
  20.1 23.6 %collective-permute-start.6 = (bf16[384,256]{1,0:T(8,128)(2,1)S(1)}, bf16[384,256]{1,0:T(8,128)(2,1)S(1)}, u32[]{:S(2)}, u32[]{:S(2)}) collective-permute-start(bf16[384,256]{1,0:T(8,128)(2,1)S(1)} %get-tuple-element.35), channel_id=1, source_target_pairs={{0,28},{4,24},{8,20},{12,16},{16,12},{20,8},{24,4},{28,0},{1,29},{... | collective-permute-start | bytes 589832 | tf_op jit(solution)/shard_map/ppermute | solution.py:612
  24.2 15.9 %collective-permute-start.7 = (bf16[2,320,128]{2,1,0:T(8,128)(2,1)S(1)}, bf16[2,320,128]{2,1,0:T(8,128)(2,1)S(1)}, u32[]{:S(2)}, u32[]{:S(2)}) collective-permute-start(bf16[2,320,128]{2,1,0:T(8,128)(2,1)S(1)} %shard_map.144.first_ref), channel_id=1, source_target_pairs={{0,8},{4,12},{8,0},{12,4},{16,24},{20,28},{24,16},{28,20},{1,9},{5... | collective-permute-start | bytes 491528 | tf_op jit(solution)/shard_map/ppermute | solution.py:612
  40.1 20.0 %collective-permute-start.8 = (bf16[4,320,128]{2,1,0:T(8,128)(2,1)S(1)}, bf16[4,320,128]{2,1,0:T(8,128)(2,1)S(1)}, u32[]{:S(2)}, u32[]{:S(2)}) collective-permute-start(bf16[4,320,128]{2,1,0:T(8,128)(2,1)S(1)} %shard_map.145.refs_0_), channel_id=1, source_target_pairs={{0,4},{4,0},{8,12},{12,8},{16,20},{20,16},{24,28},{28,24},{1,5},{5... | collective-permute-start | bytes 983048 | tf_op jit(solution)/shard_map/ppermute | solution.py:612
  40.3 19.8 %collective-permute-start.9 = (bf16[4,320,128]{2,1,0:T(8,128)(2,1)S(1)}, bf16[4,320,128]{2,1,0:T(8,128)(2,1)S(1)}, u32[]{:S(2)}, u32[]{:S(2)}) collective-permute-start(bf16[4,320,128]{2,1,0:T(8,128)(2,1)S(1)} %shard_map.145.refs_0_), channel_id=1, source_target_pairs={{0,2},{1,3},{2,0},{3,1},{4,6},{5,7},{6,4},{7,5},{8,10},{9,11},{10,... | collective-permute-start | bytes 983048 | tf_op jit(solution)/shard_map/ppermute | solution.py:612
  42.2 17.9 %collective-permute-start.10 = (bf16[4,320,128]{2,1,0:T(8,128)(2,1)S(1)}, bf16[4,320,128]{2,1,0:T(8,128)(2,1)S(1)}, u32[]{:S(2)}, u32[]{:S(2)}) collective-permute-start(bf16[4,320,128]{2,1,0:T(8,128)(2,1)S(1)} %shard_map.145.refs_0_), channel_id=1, source_target_pairs={{0,6},{1,7},{2,4},{3,5},{4,2},{5,3},{6,0},{7,1},{8,14},{9,15},{10,... | collective-permute-start | bytes 983048 | tf_op jit(solution)/shard_map/ppermute | solution.py:628
  61.0 9.5 %collective-permute-start.11 = (bf16[2,256,1280]{2,1,0:T(8,128)(2,1)S(1)}, bf16[2,256,1280]{2,1,0:T(8,128)(2,1)S(1)}, u32[]{:S(2)}, u32[]{:S(2)}) collective-permute-start(bf16[2,256,1280]{2,1,0:T(8,128)(2,1)S(1)} %shard_map.146.refs_0_), channel_id=1, source_target_pairs={{0,1},{1,0},{2,3},{3,2},{4,5},{5,4},{6,7},{7,6},{8,9},{9,8},{10,11... | collective-permute-start | bytes 3932168 | tf_op jit(solution)/shard_map/ppermute | solution.py:612
  73.8 3.0 %collective-permute-start.12 = (bf16[64,256]{1,0:T(8,128)(2,1)S(1)}, bf16[64,256]{1,0:T(8,128)(2,1)S(1)}, u32[]{:S(2)}, u32[]{:S(2)}) collective-permute-start(bf16[64,256]{1,0:T(8,128)(2,1)S(1)} %get-tuple-element.51.refs_0_), channel_id=1, source_target_pairs={{0,1},{1,0},{2,3},{3,2},{4,5},{5,4},{6,7},{7,6},{8,9},{9,8},{10,11... | collective-permute-start | bytes 98312 | tf_op jit(solution)/shard_map/ppermute | solution.py:612
  73.9 4.0 %collective-permute-start.13 = (bf16[64,256]{1,0:T(8,128)(2,1)S(1)}, bf16[64,256]{1,0:T(8,128)(2,1)S(1)}, u32[]{:S(2)}, u32[]{:S(2)}) collective-permute-start(bf16[64,256]{1,0:T(8,128)(2,1)S(1)} %get-tuple-element.51.refs_0_), channel_id=1, source_target_pairs={{0,2},{1,3},{2,0},{3,1},{4,6},{5,7},{6,4},{7,5},{8,10},{9,11},{10,... | collective-permute-start | bytes 98312 | tf_op jit(solution)/shard_map/ppermute | solution.py:612
  75.4 3.3 %collective-permute-start.14 = (bf16[64,256]{1,0:T(8,128)(2,1)S(1)}, bf16[64,256]{1,0:T(8,128)(2,1)S(1)}, u32[]{:S(2)}, u32[]{:S(2)}) collective-permute-start(bf16[64,256]{1,0:T(8,128)(2,1)S(1)} %get-tuple-element.51.refs_0_), channel_id=1, source_target_pairs={{0,3},{1,2},{2,1},{3,0},{4,7},{5,6},{6,5},{7,4},{8,11},{9,10},{10,... | collective-permute-start | bytes 98312 | tf_op jit(solution)/shard_map/ppermute | solution.py:612
